TPU v7x, 32 devices: a whole 2x2x4 slice. The times are simulated.
32 devices in a mesh: seq: 8 (over z, y), head: 4 (over x, core).
Axes of the slice: x: 2, y: 2, z: 4, core: 2. Of those that a mesh axis runs over, the one named last changes fastest.
Arguments:
- queries: bfloat16 [2048, 4096], P('seq', 'head'), may hold values from -6 to 6
- key_vectors: bfloat16 [2048, 4096], P('seq', 'head'), may hold values from -6 to 6
- value_vectors: bfloat16 [2048, 4096], P('seq', 'head'), may hold values from -6 to 6
- norm_gain: float32 [4096], P('head'), may hold values from 0.1 to 1.9
- out_weight: bfloat16 [4096, 4096], P('head', 'seq'), may hold values from -0.09375 to 0.09375
Outputs:
- projected: bfloat16 [2048, 4096], P('seq', 'head')
All inputs are finite; a program needn't handle non-finite values.
Results may differ from a plain program's by a relative error of at most 0.022.
Values may be sent and summed in bfloat16 or wider, within the bound.
No kernel may reach another device: no remote copies, remote signals or barrier semaphores. Data moves between devices by JAX's collectives and lax.ppermute only.
A program may use at most 192 MiB of HBM per device.

v0:
```python
import jax
import jax.numpy as jnp
from jax import lax
from jax.sharding import PartitionSpec as P

HD = 128
BLOCK = 256


epsilon = 1e-06


def carried_in(shard, axis, join, neutral):
    place = lax.axis_index(axis)
    gathered = lax.all_gather(shard.astype(jnp.bfloat16), axis)
    state = jnp.zeros_like(shard) + jnp.asarray(neutral, shard.dtype)

    def one(hop, state):
        return join(state, lax.dynamic_index_in_dim(gathered, hop, 0, False).astype(shard.dtype))

    return lax.fori_loop(0, place, one, state)


def add_states(earlier, later):
    return earlier + later


def body(queries, key_vectors, value_vectors, norm_gain, out_weight):
    row_count = queries.shape[0]
    feature_count = queries.shape[1]
    head_count = feature_count // HD
    block_count = row_count // BLOCK
    shape_four = (block_count, BLOCK, head_count, HD)
    query_blocks = queries.reshape(shape_four)
    key_blocks = key_vectors.reshape(shape_four)
    value_blocks = value_vectors.reshape(shape_four)
    block_terms = jnp.einsum(
        "bshd,bshe->bhde", key_blocks, value_blocks, preferred_element_type=jnp.float32
    )
    inclusive = jnp.cumsum(block_terms, axis=0)
    device_total = inclusive[-1]
    empty_state = jnp.zeros((1, head_count, HD, HD), jnp.float32)
    earlier_blocks = jnp.concatenate([empty_state, inclusive[:-1]], axis=0)
    incoming = carried_in(device_total, "seq", add_states, jnp.zeros_like(device_total))
    state_in = (incoming[None] + earlier_blocks).astype(jnp.bfloat16)
    positions = jnp.arange(BLOCK, dtype=jnp.int32)
    causal = positions[:, None] >= positions[None, :]
    scores = jnp.einsum(
        "bthd,bshd->bhts", query_blocks, key_blocks, preferred_element_type=jnp.float32
    )
    scores = jnp.where(causal[None, None], scores, jnp.float32(0.0)).astype(jnp.bfloat16)
    within = jnp.einsum("bhts,bshd->bthd", scores, value_blocks, preferred_element_type=jnp.float32)
    carried = jnp.einsum(
        "bthd,bhde->bthe", query_blocks, state_in, preferred_element_type=jnp.float32
    )
    combined = within + carried
    root_mean = jnp.sqrt(jnp.mean(combined * combined, axis=-1, keepdims=True) + epsilon)
    gain_table = norm_gain.reshape(head_count, HD)
    attended = (combined / root_mean * gain_table[None, None]).astype(jnp.bfloat16)
    attended = attended.reshape(row_count, feature_count)
    full_weight = lax.all_gather(out_weight, "seq", axis=1, tiled=True)
    partial_sums = jnp.dot(attended, full_weight, preferred_element_type=jnp.float32)
    projected = lax.psum_scatter(
        partial_sums.astype(jnp.bfloat16), "head", scatter_dimension=1, tiled=True
    )
    return projected


def solution(mesh):
    in_specs = (P("seq", "head"), P("seq", "head"), P("seq", "head"), P("head"), P("head", "seq"))
    out_specs = P("seq", "head")
    return jax.shard_map(body, mesh=mesh, in_specs=in_specs, out_specs=out_specs, check_vma=False)
```

profile of v0, /device:TPU:1, one launch (start us, length us, event | category | flops | bytes accessed | tf_op | source)
XLA Modules:
  0.0 230.8 jit_solution(10708775713017219536)
XLA Ops:
  6.5 0.0 copy-start
  6.5 0.0 all-gather.6.cloned.1.call-start
  6.5 1.3 copy.17
  7.8 2.0 convolution_convert_fusion.1
  9.9 0.0 all-gather.6.cloned.1.call-update
  9.9 0.0 all-gather.4.cloned.1.call-start
  10.0 0.7 all-gather.4.cloned.1.call-update
  10.7 0.0 reduce-scatter.2.cloned.1.call-start
  10.7 49.6 %all-gather.6.cloned.1.call-done = bf16[64,128,128]{2,1,0:T(8,128)(2,1)} async-done(((bf16[8,128,128]{2,1,0:T(8,128)(2,1)}), bf16[64,128,128]{2,1,0:T(8,128)(2,1)}) %all-gather.6.cloned.1.call-update) | async-done | bytes 2097168 | tf_op jit(solution)/shard_map/all_gather | solution.py:15
  60.4 0.0 copy-done
  60.4 0.3 fusion.10
  60.7 0.0 copy-start.1
  60.8 1.8 multiply_reduce_fusion
  62.5 0.0 copy-done.1
  62.6 0.2 multiply_convert_fusion
  62.8 124.2 %all-gather.4.cloned.1.call-done = bf16[1024,4096]{1,0:T(8,128)(2,1)} async-done(((bf16[1024,512]{1,0:T(8,128)(2,1)}), bf16[1024,4096]{1,0:T(8,128)(2,1)}) %all-gather.4.cloned.1.call-update) | async-done | bytes 8388624 | tf_op jit(solution)/shard_map/all_gather | solution.py:61
  186.9 7.1 %convolution_convert_fusion = bf16[256,4096]{1,0:T(8,128)(2,1)} fusion(bf16[256,1024]{0,1:T(8,128)(2,1)S(1)} %bitcast.53, bf16[1024,4096]{1,0:T(8,128)(2,1)} %all-gather.4.cloned.1.call-done), kind=kOutput, calls=%fused_computation.1 | convolution fusion | flops 2148532224 | bytes 11010048 | tf_op jit(solution)/shard_map/dot_general | solution.py:62
  194.0 0.0 reduce-scatter.2.cloned.1.call-update
  194.1 30.2 %reduce-scatter.2.cloned.1.call-done = bf16[256,1024]{1,0:T(8,128)(2,1)} async-done(((bf16[256,4096]{1,0:T(8,128)(2,1)}), bf16[256,1024]{1,0:T(8,128)(2,1)}) %reduce-scatter.2.cloned.1.call-update) | async-done | bytes 524304 | tf_op jit(solution)/shard_map/reduce_scatter | solution.py:63
  (4 shorter events, 0.1 us)
Async XLA Ops:
  6.5 53.8 %copy-start = (bf16[256,1024]{1,0:T(8,128)(2,1)S(1)}, bf16[256,1024]{1,0:T(8,128)(2,1)}, u32[]{:S(2)}) copy-start(bf16[256,1024]{1,0:T(8,128)(2,1)} %param.7) | copy-start | bytes 1572868
  6.5 53.8 %all-gather.6.cloned.1.call-start = ((), (), s32[]{:S(2)}) async-start(), calls=%async_computation.3 | async-start | bytes 2359296 | tf_op jit(solution)/shard_map/all_gather | solution.py:15
  9.9 177.0 %all-gather.4.cloned.1.call-start = ((), (), s32[]{:S(2)}) async-start(), calls=%async_computation.1 | async-start | bytes 9437184 | tf_op jit(solution)/shard_map/all_gather | solution.py:61
  10.7 213.6 %reduce-scatter.2.cloned.1.call-start = ((), (), s32[]{:S(2)}) async-start(), calls=%async_computation.2 | async-start | bytes 2621440 | tf_op jit(solution)/shard_map/reduce_scatter | solution.py:63
  60.7 1.8 copy-start.1
Sparse Core Ops, SparseCore 0:
  10.0 50.2 all-gather.5
  62.4 124.5 all-gather.3
  194.2 30.0 reduce-scatter.1
where the time goes:
time: 232 us; the launch traced here: 231 us
  waiting for transfers between devices  205 us (88%)
  between operations  13.2 us (6%)
  matrix products  11.3 us (5%)
    all_gather x1, waiting for transfers between devices, body(): full_weight = lax.all_gather(out_weight, 'seq', axis=1, tiled=True)  124 us
    all_gather x1, waiting for transfers between devices, carried_in(): gathered = lax.all_gather(shard.astype(jnp.bfloat16), axis)  49.6 us
    reduce_scatter x1, waiting for transfers between devices, body(): lax.psum_scatter(partial_sums.astype(jnp.bfloat16), 'head', scatter_dimen...  30.2 us
    dot_general x1, matrix products, body(): jnp.dot(attended, full_weight, preferred_element_type=jnp.float32)  7.11 us
  transfers between devices with their start and end apart: 3, of which 3 were waited for; matrix products, arithmetic and copies ran while one was open for 1% of the time, Pallas kernels for 0%

commit v1 on v0

v1 whole, which is shorter than its diff:
```python
import jax
import jax.numpy as jnp
from jax import lax
from jax.experimental import pallas as pl
from jax.experimental.pallas import tpu as pltpu
from jax.sharding import PartitionSpec as P

HD = 128
BLOCK = 256
F32 = jnp.float32
BF16 = jnp.bfloat16

epsilon = 1e-06


def general_body(queries, key_vectors, value_vectors, norm_gain, out_weight):
    row_count, feature_count = queries.shape
    head_count = feature_count // HD
    block_count = row_count // BLOCK
    shape_four = (block_count, BLOCK, head_count, HD)
    query_blocks = queries.reshape(shape_four)
    key_blocks = key_vectors.reshape(shape_four)
    value_blocks = value_vectors.reshape(shape_four)
    block_terms = jnp.einsum("bshd,bshe->bhde", key_blocks, value_blocks, preferred_element_type=F32)
    inclusive = jnp.cumsum(block_terms, axis=0)
    empty_state = jnp.zeros((1, head_count, HD, HD), F32)
    earlier_blocks = jnp.concatenate([empty_state, inclusive[:-1]], axis=0)
    gathered = lax.all_gather(inclusive[-1].astype(BF16), "seq")
    incoming = lax.fori_loop(
        0,
        lax.axis_index("seq"),
        lambda hop, state: state + lax.dynamic_index_in_dim(gathered, hop, 0, False).astype(F32),
        jnp.zeros((head_count, HD, HD), F32),
    )
    state_in = (incoming[None] + earlier_blocks).astype(BF16)
    positions = jnp.arange(BLOCK, dtype=jnp.int32)
    causal = positions[:, None] >= positions[None, :]
    scores = jnp.einsum("bthd,bshd->bhts", query_blocks, key_blocks, preferred_element_type=F32)
    scores = jnp.where(causal[None, None], scores, 0.0).astype(BF16)
    combined = jnp.einsum("bhts,bshd->bthd", scores, value_blocks, preferred_element_type=F32)
    combined += jnp.einsum("bthd,bhde->bthe", query_blocks, state_in, preferred_element_type=F32)
    root_mean = jnp.sqrt(jnp.mean(combined * combined, axis=-1, keepdims=True) + epsilon)
    gain_table = norm_gain.reshape(head_count, HD)
    attended = (combined / root_mean * gain_table[None, None]).astype(BF16)
    full_weight = lax.all_gather(out_weight, "seq", axis=1, tiled=True)
    partial_sums = jnp.dot(attended.reshape(row_count, feature_count), full_weight, preferred_element_type=F32)
    return lax.psum_scatter(partial_sums.astype(BF16), "head", scatter_dimension=1, tiled=True)


def head_slice(head):
    return slice(head * HD, (head + 1) * HD)


def state_kernel(k_ref, v_ref, wide_ref, narrow_ref):
    for head in range(wide_ref.shape[0]):
        cols = head_slice(head)
        state = lax.dot_general(
            k_ref[:, cols], v_ref[:, cols], (((0,), (0,)), ((), ())), preferred_element_type=F32
        )
        wide_ref[head] = state
        narrow_ref[head] = state.astype(BF16)


def within_kernel(q_ref, k_ref, v_ref, out_ref):
    rows = lax.broadcasted_iota(jnp.int32, (BLOCK, BLOCK), 0)
    cols_at = lax.broadcasted_iota(jnp.int32, (BLOCK, BLOCK), 1)
    causal = rows >= cols_at
    for head in range(q_ref.shape[1] // HD):
        cols = head_slice(head)
        scores = lax.dot_general(
            q_ref[:, cols], k_ref[:, cols], (((1,), (1,)), ((), ())), preferred_element_type=F32
        )
        scores = jnp.where(causal, scores, 0.0).astype(BF16)
        out_ref[:, cols] = jnp.dot(scores, v_ref[:, cols], preferred_element_type=F32)


def attend_kernel(q_ref, within_ref, state_ref, gain_ref, out_ref):
    for head in range(q_ref.shape[1] // HD):
        cols = head_slice(head)
        carried = jnp.dot(q_ref[:, cols], state_ref[head].astype(BF16), preferred_element_type=F32)
        combined = within_ref[:, cols] + carried
        mean_square = jnp.mean(combined * combined, axis=-1, keepdims=True)
        scaled = combined / jnp.sqrt(mean_square + epsilon) * gain_ref[:, cols]
        out_ref[:, cols] = scaled.astype(BF16)


def call(kernel, out_shape, flops, moved):
    return pl.pallas_call(
        kernel,
        out_shape=out_shape,
        compiler_params=pltpu.CompilerParams(vmem_limit_bytes=24 * 1024 * 1024),
        cost_estimate=pl.CostEstimate(flops=flops, bytes_accessed=moved, transcendentals=0),
    )


def planes_body(seq_count, head_groups):
    planes = head_groups
    inner = seq_count // planes

    def seq_perm(step):
        return [
            (z * inner + y, (z + step) * inner + y)
            for z in range(planes - step)
            for y in range(inner)
        ]

    def flat(z, y, h):
        return (z * inner + y) * head_groups + h

    everywhere = [
        (z, y, h) for z in range(planes) for y in range(inner) for h in range(head_groups)
    ]

    def prefix_over_seq(wide, narrow):
        place = lax.axis_index("seq")
        excl = jnp.zeros_like(wide)
        incl = wide
        if inner == 2:
            swap = [(s, s ^ 1) for s in range(seq_count)]
            mate = lax.ppermute(narrow, "seq", swap).astype(F32)
            excl = jnp.where(place % 2 == 1, mate, 0.0)
            incl = wide + mate
            before = jnp.zeros_like(wide)
            step = 1
            while step < planes:
                got = lax.ppermute(incl.astype(BF16), "seq", seq_perm(step)).astype(F32)
                before += got
                incl += got
                step *= 2
            return (excl + before).astype(BF16)
        step = 1
        while step < seq_count:
            pairs = [(s, s + step) for s in range(seq_count - step)]
            got = lax.ppermute(incl.astype(BF16), "seq", pairs).astype(F32)
            excl += got
            incl += got
            step *= 2
        return excl.astype(BF16)

    def gather_weight(out_weight):
        if inner == 2:
            swap = [(s, s ^ 1) for s in range(seq_count)]
            mate = lax.ppermute(out_weight, "seq", swap)
            first = lax.axis_index("seq") % 2 == 0
            return jnp.concatenate(
                [jnp.where(first, out_weight, mate), jnp.where(first, mate, out_weight)], axis=1
            )
        groups = [[z * inner + y for y in range(inner)] for z in range(planes)]
        return lax.all_gather(out_weight, "seq", axis=1, tiled=True, axis_index_groups=groups)

    def body(queries, key_vectors, value_vectors, norm_gain, out_weight):
        rows, features = queries.shape
        heads = features // HD
        size = rows * features
        weight = gather_weight(out_weight)
        wide, narrow = call(
            state_kernel,
            (
                jax.ShapeDtypeStruct((heads, HD, HD), F32),
                jax.ShapeDtypeStruct((heads, HD, HD), BF16),
            ),
            2 * size * HD,
            4 * size + 6 * heads * HD * HD,
        )(key_vectors, value_vectors)
        within = call(
            within_kernel, jax.ShapeDtypeStruct((rows, features), F32), 4 * size * BLOCK, 10 * size
        )(queries, key_vectors, value_vectors)
        state_in = prefix_over_seq(wide, narrow)
        attended = call(
            attend_kernel, jax.ShapeDtypeStruct((rows, features), BF16), 2 * size * HD, 8 * size
        )(queries, within, state_in, norm_gain[None])

        parts = [None] * head_groups
        for j in (3, 2, 1, 0):
            pairs = [
                (flat(z, y, h), flat((z + (h ^ j)) % planes, y, h)) for z, y, h in everywhere
            ]
            parts[j] = lax.ppermute(attended, ("seq", "head"), pairs)
        parts = [
            jnp.dot(part, weight, preferred_element_type=F32).astype(BF16) for part in parts
        ]
        core = [(h, h ^ 1) for h in range(head_groups)]
        chip = [(h, h ^ 2) for h in range(head_groups)]
        far = parts[2].astype(F32) + lax.ppermute(parts[3], "head", core).astype(F32)
        near = parts[0].astype(F32) + lax.ppermute(parts[1], "head", core).astype(F32)
        near += lax.ppermute(far.astype(BF16), "head", chip).astype(F32)
        home = [
            (flat(z, y, h), flat((z - h) % planes, y, z)) for z, y, h in everywhere
        ]
        return lax.ppermute(near.astype(BF16), ("seq", "head"), home)

    return body


def solution(mesh):
    seq_count, head_groups = mesh.shape["seq"], mesh.shape["head"]

    def run(queries, key_vectors, value_vectors, norm_gain, out_weight):
        one_block = queries.shape[0] == BLOCK * seq_count
        body = general_body
        if one_block and head_groups == 4 and seq_count % head_groups == 0:
            body = planes_body(seq_count, head_groups)
        return jax.shard_map(
            body,
            mesh=mesh,
            in_specs=(P("seq", "head"), P("seq", "head"), P("seq", "head"), P("head"), P("head", "seq")),
            out_specs=P("seq", "head"),
            check_vma=False,
        )(queries, key_vectors, value_vectors, norm_gain, out_weight)

    return run
```

time: 232 us -> 114 us (0.49)
  the two profiles are of different devices: /device:TPU:1 before, /device:TPU:6 now
where the time goes in v1:
time: 114 us; the launch traced here: 113 us
  starting transfers between devices  59.6 us (52%)
  waiting for transfers between devices  43.2 us (38%)
  local copies, waits for them, and re-layouts  2.9 us (3%)
  matrix products  2.86 us (3%)
  other arithmetic  2.59 us (2%)
  Pallas kernels  2.01 us (2%)
    ppermute x4, starting transfers between devices, body(): parts[j] = lax.ppermute(attended, ('seq', 'head'), pairs)  31.9 us
    ppermute x1, waiting for transfers between devices, body(): return lax.ppermute(near.astype(BF16), ('seq', 'head'), home)  13.4 us
    ppermute x4, waiting for transfers between devices, body(): parts[j] = lax.ppermute(attended, ('seq', 'head'), pairs)  11.9 us
    ppermute x1, starting transfers between devices, body(): near += lax.ppermute(far.astype(BF16), 'head', chip).astype(F32)  11.5 us
    ppermute x2, starting transfers between devices, prefix_over_seq(): got = lax.ppermute(incl.astype(BF16), 'seq', seq_perm(step)).astype(F32)  9.76 us
    ppermute x1, waiting for transfers between devices, prefix_over_seq(): mate = lax.ppermute(narrow, 'seq', swap).astype(F32)  7.54 us
    ppermute x2, waiting for transfers between devices, prefix_over_seq(): got = lax.ppermute(incl.astype(BF16), 'seq', seq_perm(step)).astype(F32)  6.27 us
    ppermute x1, waiting for transfers between devices, body(): near += lax.ppermute(far.astype(BF16), 'head', chip).astype(F32)  4.13 us
  transfers between devices with their start and end apart: 12, of which 7 were waited for; matrix products, arithmetic and copies ran while one was open for 4% of the time, Pallas kernels for 1%

profile of v1, /device:TPU:6, one launch (start us, length us, event | category | flops | bytes accessed | tf_op | source)
XLA Modules:
  0.0 113.3 jit_solution(9483868470788825340)
XLA Ops:
  0.0 0.0 copy-start
  0.0 1.0 copy-done
  1.0 0.0 copy-start.2
  1.0 1.0 copy-done.2
  2.1 0.0 copy-start.6
  2.1 0.4 shard_map.56
  2.4 0.6 collective-permute-start
  3.0 7.5 %collective-permute-done = bf16[8,128,128]{2,1,0:T(8,128)(2,1)S(1)} collective-permute-done((bf16[8,128,128]{2,1,0:T(8,128)(2,1)S(1)}, bf16[8,128,128]{2,1,0:T(8,128)(2,1)S(1)}, u32[]{:S(2)}, u32[]{:S(2)}) %collective-permute-start) | collective-permute-done | bytes 262176 | tf_op jit(solution)/shard_map/ppermute | solution.py:120
  10.6 0.0 copy-start.1
  10.6 0.0 copy-start.3
  10.6 0.0 copy-start.4
  10.6 0.1 fusion.10
  10.6 3.6 %collective-permute-start.1 = (bf16[8,128,128]{2,1,0:T(8,128)(2,1)S(1)}, bf16[8,128,128]{2,1,0:T(8,128)(2,1)S(1)}, u32[]{:S(2)}, u32[]{:S(2)}) collective-permute-start(bf16[8,128,128]{2,1,0:T(8,128)(2,1)S(1)} %fusion.10), channel_id=1, source_target_pairs={{0,8},{4,12},{8,16},{12,20},{16,24},{20,28},{1,9},{5,13},{9,17},{1... | collective-permute-start | bytes 786440 | tf_op jit(solution)/shard_map/ppermute | solution.py:126
  14.3 0.0 copy-done.6
  14.3 0.6 collective-permute-start.4
  14.8 4.1 %collective-permute-done.1 = bf16[8,128,128]{2,1,0:T(8,128)(2,1)S(1)} collective-permute-done((bf16[8,128,128]{2,1,0:T(8,128)(2,1)S(1)}, bf16[8,128,128]{2,1,0:T(8,128)(2,1)S(1)}, u32[]{:S(2)}, u32[]{:S(2)}) %collective-permute-start.1) | collective-permute-done | bytes 262176 | tf_op jit(solution)/shard_map/ppermute | solution.py:126
  18.9 0.1 fusion.9
  19.0 6.1 %collective-permute-start.2 = (bf16[8,128,128]{2,1,0:T(8,128)(2,1)S(1)}, bf16[8,128,128]{2,1,0:T(8,128)(2,1)}, u32[]{:S(2)}, u32[]{:S(2)}) collective-permute-start(bf16[8,128,128]{2,1,0:T(8,128)(2,1)S(1)} %fusion.9), channel_id=1, source_target_pairs={{0,16},{4,20},{8,24},{12,28},{1,17},{5,21},{9,25},{13,29},{2,18},{... | collective-permute-start | bytes 786440 | tf_op jit(solution)/shard_map/ppermute | solution.py:126
  25.1 0.0 copy-done.1
  25.1 0.0 copy-done.3
  25.1 0.0 copy-done.4
  25.1 0.9 shard_map.55.within_ref
  26.1 0.0 copy-start.5
  26.1 2.2 %collective-permute-done.2 = bf16[8,128,128]{2,1,0:T(8,128)(2,1)} collective-permute-done((bf16[8,128,128]{2,1,0:T(8,128)(2,1)S(1)}, bf16[8,128,128]{2,1,0:T(8,128)(2,1)}, u32[]{:S(2)}, u32[]{:S(2)}) %collective-permute-start.2) | collective-permute-done | bytes 262176 | tf_op jit(solution)/shard_map/ppermute | solution.py:126
  28.3 1.1 fusion.8.state_ref
  29.4 0.0 copy-done.5
  29.4 0.7 shard_map.57
  30.1 14.5 %collective-permute-start.8 = (bf16[256,1024]{1,0:T(8,128)(2,1)S(1)}, bf16[256,1024]{1,0:T(8,128)(2,1)S(1)}, u32[]{:S(2)}, u32[]{:S(2)}) collective-permute-start(bf16[256,1024]{1,0:T(8,128)(2,1)S(1)} %shard_map.57), channel_id=1, source_target_pairs={{0,24},{1,17},{2,10},{3,3},{4,28},{5,21},{6,14},{7,7},{8,0},{9,25}... | collective-permute-start | bytes 1572872 | tf_op jit(solution)/shard_map/ppermute | solution.py:178
  44.6 4.8 %collective-permute-start.5 = (bf16[256,1024]{1,0:T(8,128)(2,1)S(1)}, bf16[256,1024]{1,0:T(8,128)(2,1)S(1)}, u32[]{:S(2)}, u32[]{:S(2)}) collective-permute-start(bf16[256,1024]{1,0:T(8,128)(2,1)S(1)} %shard_map.57), channel_id=1, source_target_pairs={{0,8},{1,1},{2,26},{3,19},{4,12},{5,5},{6,30},{7,23},{8,16},{9,9},... | collective-permute-start | bytes 1572872 | tf_op jit(solution)/shard_map/ppermute | solution.py:178
  49.5 0.7 collective-permute-start.7
  50.2 0.0 collective-permute-done.4
  50.2 1.4 %broadcast_select_fusion.1 = (bf16[1024,512]{1,0:T(8,128)(2,1)S(1)}, bf16[1024,512]{1,0:T(8,128)(2,1)S(1)}) fusion(bf16[1024,512]{1,0:T(8,128)(2,1)S(1)} %copy-done.6, bf16[1024,512]{1,0:T(8,128)(2,1)} %collective-permute-done.4, pred[]{:T(512)S(6)} %eq.10), kind=kLoop, calls=%fused_computation.13 | loop fusion | flops 1048576 | bytes 4194305 | tf_op jit(solution)/shard_map/jit(_where)/select_n | solution.py:146
  51.5 8.8 %collective-permute-done.8 = bf16[256,1024]{1,0:T(8,128)(2,1)S(1)} collective-permute-done((bf16[256,1024]{1,0:T(8,128)(2,1)S(1)}, bf16[256,1024]{1,0:T(8,128)(2,1)S(1)}, u32[]{:S(2)}, u32[]{:S(2)}) %collective-permute-start.8) | collective-permute-done | bytes 524320 | tf_op jit(solution)/shard_map/ppermute | solution.py:178
  60.4 0.7 convolution_convert_fusion
  61.1 0.1 collective-permute-start.9
  61.2 11.9 %collective-permute-start.3 = (bf16[256,1024]{1,0:T(8,128)(2,1)S(1)}, bf16[256,1024]{1,0:T(8,128)(2,1)S(1)}, u32[]{:S(2)}, u32[]{:S(2)}) collective-permute-start(bf16[256,1024]{1,0:T(8,128)(2,1)S(1)} %shard_map.57), channel_id=1, source_target_pairs={{0,0},{1,9},{2,18},{3,27},{4,4},{5,13},{6,22},{7,31},{8,8},{9,17},... | collective-permute-start | bytes 1572872 | tf_op jit(solution)/shard_map/ppermute | solution.py:178
  73.1 0.0 collective-permute-done.5
  73.1 0.7 convolution_convert_fusion.2
  73.8 2.2 %collective-permute-start.6 = (bf16[256,1024]{1,0:T(8,128)(2,1)S(1)}, bf16[256,1024]{1,0:T(8,128)(2,1)S(1)}, u32[]{:S(2)}, u32[]{:S(2)}) collective-permute-start(bf16[256,1024]{1,0:T(8,128)(2,1)S(1)} %convolution_convert_fusion.2), channel_id=1, source_target_pairs={{0,1},{1,0},{2,3},{3,2},{4,5},{5,4},{6,7},{7,6},{8,9},{9,8},{10,11... | collective-permute-start | bytes 1572872 | tf_op jit(solution)/shard_map/ppermute | solution.py:185
  76.0 0.0 collective-permute-done.7
  76.0 0.0 collective-permute-done.9
  76.0 0.7 fusion.6
  76.7 11.5 %collective-permute-start.10 = (bf16[256,1024]{1,0:T(8,128)(2,1)S(1)}, bf16[256,1024]{1,0:T(8,128)(2,1)S(1)}, u32[]{:S(2)}, u32[]{:S(2)}) collective-permute-start(bf16[256,1024]{1,0:T(8,128)(2,1)S(1)} %fusion.6), channel_id=1, source_target_pairs={{0,2},{1,3},{2,0},{3,1},{4,6},{5,7},{6,4},{7,5},{8,10},{9,11},{10,... | collective-permute-start | bytes 1572872 | tf_op jit(solution)/shard_map/ppermute | solution.py:186
  88.2 3.0 %collective-permute-done.3 = bf16[256,1024]{1,0:T(8,128)(2,1)S(1)} collective-permute-done((bf16[256,1024]{1,0:T(8,128)(2,1)S(1)}, bf16[256,1024]{1,0:T(8,128)(2,1)S(1)}, u32[]{:S(2)}, u32[]{:S(2)}) %collective-permute-start.3) | collective-permute-done | bytes 524320 | tf_op jit(solution)/shard_map/ppermute | solution.py:178
  91.3 0.0 collective-permute-done.6
  91.3 4.1 %collective-permute-done.10 = bf16[256,1024]{1,0:T(8,128)(2,1)S(1)} collective-permute-done((bf16[256,1024]{1,0:T(8,128)(2,1)S(1)}, bf16[256,1024]{1,0:T(8,128)(2,1)S(1)}, u32[]{:S(2)}, u32[]{:S(2)}) %collective-permute-start.10) | collective-permute-done | bytes 524320 | tf_op jit(solution)/shard_map/ppermute | solution.py:186
  95.4 0.8 fusion.3
  96.1 2.9 %collective-permute-start.11 = (bf16[256,1024]{1,0:T(8,128)(2,1)S(1)}, bf16[256,1024]{1,0:T(8,128)(2,1)S(1)}, u32[]{:S(2)}, u32[]{:S(2)}) collective-permute-start(bf16[256,1024]{1,0:T(8,128)(2,1)S(1)} %fusion.3), channel_id=1, source_target_pairs={{0,0},{1,24},{2,16},{3,8},{4,4},{5,28},{6,20},{7,12},{8,9},{9,1},{... | collective-permute-start | bytes 1572872 | tf_op jit(solution)/shard_map/ppermute | solution.py:190
  99.1 13.4 %collective-permute-done.11 = bf16[256,1024]{1,0:T(8,128)(2,1)S(1)} collective-permute-done((bf16[256,1024]{1,0:T(8,128)(2,1)S(1)}, bf16[256,1024]{1,0:T(8,128)(2,1)S(1)}, u32[]{:S(2)}, u32[]{:S(2)}) %collective-permute-start.11) | collective-permute-done | bytes 524320 | tf_op jit(solution)/shard_map/ppermute | solution.py:190
  112.5 0.8 copy.7
Async XLA Ops:
  0.0 1.0 copy-start
  1.0 1.0 copy-start.2
  2.1 12.2 %copy-start.6 = (bf16[1024,512]{1,0:T(8,128)(2,1)S(1)}, bf16[1024,512]{1,0:T(8,128)(2,1)}, u32[]{:S(2)}) copy-start(bf16[1024,512]{1,0:T(8,128)(2,1)} %param.9) | copy-start | bytes 3145732
  2.4 8.1 %collective-permute-start = (bf16[8,128,128]{2,1,0:T(8,128)(2,1)S(1)}, bf16[8,128,128]{2,1,0:T(8,128)(2,1)S(1)}, u32[]{:S(2)}, u32[]{:S(2)}) collective-permute-start(bf16[8,128,128]{2,1,0:T(8,128)(2,1)S(1)} %get-tuple-element.7), channel_id=1, source_target_pairs={{0,4},{4,0},{8,12},{12,8},{16,20},{20,16},{24,28},{28,24},{1,5},{5... | collective-permute-start | bytes 786440 | tf_op jit(solution)/shard_map/ppermute | solution.py:120
  10.6 14.6 %copy-start.1 = (bf16[256,1024]{1,0:T(8,128)(2,1)S(1)}, bf16[256,1024]{1,0:T(8,128)(2,1)}, u32[]{:S(2)}) copy-start(bf16[256,1024]{1,0:T(8,128)(2,1)} %k_ref.3) | copy-start | bytes 1572868
  10.6 14.6 %copy-start.3 = (bf16[256,1024]{1,0:T(8,128)(2,1)S(1)}, bf16[256,1024]{1,0:T(8,128)(2,1)}, u32[]{:S(2)}) copy-start(bf16[256,1024]{1,0:T(8,128)(2,1)} %v_ref.3) | copy-start | bytes 1572868
  10.6 14.6 %copy-start.4 = (bf16[256,1024]{1,0:T(8,128)(2,1)S(1)}, bf16[256,1024]{1,0:T(8,128)(2,1)}, u32[]{:S(2)}) copy-start(bf16[256,1024]{1,0:T(8,128)(2,1)} %q_ref.3) | copy-start | bytes 1572868
  10.6 8.3 %collective-permute-start.1 = (bf16[8,128,128]{2,1,0:T(8,128)(2,1)S(1)}, bf16[8,128,128]{2,1,0:T(8,128)(2,1)S(1)}, u32[]{:S(2)}, u32[]{:S(2)}) collective-permute-start(bf16[8,128,128]{2,1,0:T(8,128)(2,1)S(1)} %fusion.10), channel_id=1, source_target_pairs={{0,8},{4,12},{8,16},{12,20},{16,24},{20,28},{1,9},{5,13},{9,17},{1... | collective-permute-start | bytes 786440 | tf_op jit(solution)/shard_map/ppermute | solution.py:126
  14.3 35.9 %collective-permute-start.4 = (bf16[1024,512]{1,0:T(8,128)(2,1)S(1)}, bf16[1024,512]{1,0:T(8,128)(2,1)}, u32[]{:S(2)}, u32[]{:S(2)}) collective-permute-start(bf16[1024,512]{1,0:T(8,128)(2,1)S(1)} %copy-done.6), channel_id=1, source_target_pairs={{0,4},{4,0},{8,12},{12,8},{16,20},{20,16},{24,28},{28,24},{1,5},{5... | collective-permute-start | bytes 3145736 | tf_op jit(solution)/shard_map/ppermute | solution.py:143
  19.0 9.3 %collective-permute-start.2 = (bf16[8,128,128]{2,1,0:T(8,128)(2,1)S(1)}, bf16[8,128,128]{2,1,0:T(8,128)(2,1)}, u32[]{:S(2)}, u32[]{:S(2)}) collective-permute-start(bf16[8,128,128]{2,1,0:T(8,128)(2,1)S(1)} %fusion.9), channel_id=1, source_target_pairs={{0,16},{4,20},{8,24},{12,28},{1,17},{5,21},{9,25},{13,29},{2,18},{... | collective-permute-start | bytes 786440 | tf_op jit(solution)/shard_map/ppermute | solution.py:126
  26.1 3.3 %copy-start.5 = (f32[1024]{0:T(1024)S(1)}, f32[1024]{0:T(1024)}, u32[]{:S(2)}) copy-start(f32[1024]{0:T(1024)} %param.8) | copy-start | bytes 12292
  30.1 30.3 %collective-permute-start.8 = (bf16[256,1024]{1,0:T(8,128)(2,1)S(1)}, bf16[256,1024]{1,0:T(8,128)(2,1)S(1)}, u32[]{:S(2)}, u32[]{:S(2)}) collective-permute-start(bf16[256,1024]{1,0:T(8,128)(2,1)S(1)} %shard_map.57), channel_id=1, source_target_pairs={{0,24},{1,17},{2,10},{3,3},{4,28},{5,21},{6,14},{7,7},{8,0},{9,25}... | collective-permute-start | bytes 1572872 | tf_op jit(solution)/shard_map/ppermute | solution.py:178
  44.6 28.4 %collective-permute-start.5 = (bf16[256,1024]{1,0:T(8,128)(2,1)S(1)}, bf16[256,1024]{1,0:T(8,128)(2,1)S(1)}, u32[]{:S(2)}, u32[]{:S(2)}) collective-permute-start(bf16[256,1024]{1,0:T(8,128)(2,1)S(1)} %shard_map.57), channel_id=1, source_target_pairs={{0,8},{1,1},{2,26},{3,19},{4,12},{5,5},{6,30},{7,23},{8,16},{9,9},... | collective-permute-start | bytes 1572872 | tf_op jit(solution)/shard_map/ppermute | solution.py:178
  49.5 26.5 %collective-permute-start.7 = (bf16[256,1024]{1,0:T(8,128)(2,1)S(1)}, bf16[256,1024]{1,0:T(8,128)(2,1)S(1)}, u32[]{:S(2)}, u32[]{:S(2)}) collective-permute-start(bf16[256,1024]{1,0:T(8,128)(2,1)S(1)} %shard_map.57), channel_id=1, source_target_pairs={{0,16},{1,25},{2,2},{3,11},{4,20},{5,29},{6,6},{7,15},{8,24},{9,1}... | collective-permute-start | bytes 1572872 | tf_op jit(solution)/shard_map/ppermute | solution.py:178
  61.1 14.9 %collective-permute-start.9 = (bf16[256,1024]{1,0:T(8,128)(2,1)S(1)}, bf16[256,1024]{1,0:T(8,128)(2,1)S(1)}, u32[]{:S(2)}, u32[]{:S(2)}) collective-permute-start(bf16[256,1024]{1,0:T(8,128)(2,1)S(1)} %convolution_convert_fusion), channel_id=1, source_target_pairs={{0,1},{1,0},{2,3},{3,2},{4,5},{5,4},{6,7},{7,6},{8,9},{9,8},{10,11... | collective-permute-start | bytes 1572872 | tf_op jit(solution)/shard_map/ppermute | solution.py:184
  61.2 30.1 %collective-permute-start.3 = (bf16[256,1024]{1,0:T(8,128)(2,1)S(1)}, bf16[256,1024]{1,0:T(8,128)(2,1)S(1)}, u32[]{:S(2)}, u32[]{:S(2)}) collective-permute-start(bf16[256,1024]{1,0:T(8,128)(2,1)S(1)} %shard_map.57), channel_id=1, source_target_pairs={{0,0},{1,9},{2,18},{3,27},{4,4},{5,13},{6,22},{7,31},{8,8},{9,17},... | collective-permute-start | bytes 1572872 | tf_op jit(solution)/shard_map/ppermute | solution.py:178
  73.8 17.5 %collective-permute-start.6 = (bf16[256,1024]{1,0:T(8,128)(2,1)S(1)}, bf16[256,1024]{1,0:T(8,128)(2,1)S(1)}, u32[]{:S(2)}, u32[]{:S(2)}) collective-permute-start(bf16[256,1024]{1,0:T(8,128)(2,1)S(1)} %convolution_convert_fusion.2), channel_id=1, source_target_pairs={{0,1},{1,0},{2,3},{3,2},{4,5},{5,4},{6,7},{7,6},{8,9},{9,8},{10,11... | collective-permute-start | bytes 1572872 | tf_op jit(solution)/shard_map/ppermute | solution.py:185
  76.7 18.7 %collective-permute-start.10 = (bf16[256,1024]{1,0:T(8,128)(2,1)S(1)}, bf16[256,1024]{1,0:T(8,128)(2,1)S(1)}, u32[]{:S(2)}, u32[]{:S(2)}) collective-permute-start(bf16[256,1024]{1,0:T(8,128)(2,1)S(1)} %fusion.6), channel_id=1, source_target_pairs={{0,2},{1,3},{2,0},{3,1},{4,6},{5,7},{6,4},{7,5},{8,10},{9,11},{10,... | collective-permute-start | bytes 1572872 | tf_op jit(solution)/shard_map/ppermute | solution.py:186
  96.1 16.4 %collective-permute-start.11 = (bf16[256,1024]{1,0:T(8,128)(2,1)S(1)}, bf16[256,1024]{1,0:T(8,128)(2,1)S(1)}, u32[]{:S(2)}, u32[]{:S(2)}) collective-permute-start(bf16[256,1024]{1,0:T(8,128)(2,1)S(1)} %fusion.3), channel_id=1, source_target_pairs={{0,0},{1,24},{2,16},{3,8},{4,4},{5,28},{6,20},{7,12},{8,9},{9,1},{... | collective-permute-start | bytes 1572872 | tf_op jit(solution)/shard_map/ppermute | solution.py:190

commit v2 on v1

--- a/solution.py
+++ b/solution.py
@@ -138,13 +138,6 @@
         return excl.astype(BF16)
 
     def gather_weight(out_weight):
-        if inner == 2:
-            swap = [(s, s ^ 1) for s in range(seq_count)]
-            mate = lax.ppermute(out_weight, "seq", swap)
-            first = lax.axis_index("seq") % 2 == 0
-            return jnp.concatenate(
-                [jnp.where(first, out_weight, mate), jnp.where(first, mate, out_weight)], axis=1
-            )
         groups = [[z * inner + y for y in range(inner)] for z in range(planes)]
         return lax.all_gather(out_weight, "seq", axis=1, tiled=True, axis_index_groups=groups)
 

time: 114 us -> 136 us (1.19)
  the two profiles are of different devices: /device:TPU:6 before, /device:TPU:17 now
where the time goes in v2:
time: 136 us
  starting transfers between devices  61.7 us (45%)
  waiting for transfers between devices  50.4 us (37%)
  between operations  13.6 us (10%)
  matrix products  4.62 us (3%)
  local copies, waits for them, and re-layouts  2.89 us (2%)
  Pallas kernels  2 us (1%)
    ppermute x4, starting transfers between devices, body(): parts[j] = lax.ppermute(attended, ('seq', 'head'), pairs)  36.3 us
    ppermute x1, waiting for transfers between devices, body(): return lax.ppermute(near.astype(BF16), ('seq', 'head'), home)  19.3 us
    ppermute x1, waiting for transfers between devices, body(): near += lax.ppermute(far.astype(BF16), 'head', chip).astype(F32)  12.8 us
    ppermute x1, starting transfers between devices, body(): lax.ppermute(parts[3], 'head', core).astype(F32)  12.5 us
    ppermute x2, waiting for transfers between devices, prefix_over_seq(): got = lax.ppermute(incl.astype(BF16), 'seq', seq_perm(step)).astype(F32)  10.9 us
    ppermute x1, waiting for transfers between devices, prefix_over_seq(): mate = lax.ppermute(narrow, 'seq', swap).astype(F32)  5.93 us
    ppermute x1, starting transfers between devices, body(): lax.ppermute(parts[1], 'head', core).astype(F32)  5.06 us
    dot_general x4, matrix products, body(): jnp.dot(part, weight, preferred_element_type=F32).astype(BF16)  4.62 us
  transfers between devices with their start and end apart: 12, of which 6 were waited for; matrix products, arithmetic and copies ran while one was open for 3% of the time, Pallas kernels for 1%

profile of v2, /device:TPU:17, one launch (start us, length us, event | category | flops | bytes accessed | tf_op | source)
XLA Modules:
  0.0 135.5 jit_solution(2512281957053479694)
XLA Ops:
  6.5 0.0 copy-start.3
  6.5 0.0 copy-start.1
  6.5 0.0 all-gather.2.cloned.1.call-start
  6.5 0.7 all-gather.2.cloned.1.call-update
  7.3 0.0 copy-start
  7.3 1.0 copy-done
  8.3 0.0 copy-start.2
  8.3 1.0 copy-done.2
  9.3 0.0 copy-start.4
  9.3 0.4 shard_map.56
  9.7 1.3 collective-permute-start
  11.0 5.9 %collective-permute-done = bf16[8,128,128]{2,1,0:T(8,128)(2,1)S(1)} collective-permute-done((bf16[8,128,128]{2,1,0:T(8,128)(2,1)S(1)}, bf16[8,128,128]{2,1,0:T(8,128)(2,1)S(1)}, u32[]{:S(2)}, u32[]{:S(2)}) %collective-permute-start) | collective-permute-done | bytes 262176 | tf_op jit(solution)/shard_map/ppermute | solution.py:120
  16.9 0.1 fusion.10
  17.0 3.2 %collective-permute-start.1 = (bf16[8,128,128]{2,1,0:T(8,128)(2,1)S(1)}, bf16[8,128,128]{2,1,0:T(8,128)(2,1)S(1)}, u32[]{:S(2)}, u32[]{:S(2)}) collective-permute-start(bf16[8,128,128]{2,1,0:T(8,128)(2,1)S(1)} %fusion.10), channel_id=1, source_target_pairs={{0,8},{4,12},{8,16},{12,20},{16,24},{20,28},{1,9},{5,13},{9,17},{1... | collective-permute-start | bytes 786440 | tf_op jit(solution)/shard_map/ppermute | solution.py:126
  20.2 5.0 %collective-permute-done.1 = bf16[8,128,128]{2,1,0:T(8,128)(2,1)S(1)} collective-permute-done((bf16[8,128,128]{2,1,0:T(8,128)(2,1)S(1)}, bf16[8,128,128]{2,1,0:T(8,128)(2,1)S(1)}, u32[]{:S(2)}, u32[]{:S(2)}) %collective-permute-start.1) | collective-permute-done | bytes 262176 | tf_op jit(solution)/shard_map/ppermute | solution.py:126
  25.3 0.1 fusion.9
  25.4 0.0 copy-start.5
  25.4 1.3 collective-permute-start.2
  26.7 0.0 copy-done.3
  26.7 0.0 copy-done.1
  26.7 0.0 copy-done.4
  26.7 0.9 shard_map.55.within_ref
  27.6 5.8 %collective-permute-done.2 = bf16[8,128,128]{2,1,0:T(8,128)(2,1)S(1)} collective-permute-done((bf16[8,128,128]{2,1,0:T(8,128)(2,1)S(1)}, bf16[8,128,128]{2,1,0:T(8,128)(2,1)S(1)}, u32[]{:S(2)}, u32[]{:S(2)}) %collective-permute-start.2) | collective-permute-done | bytes 262176 | tf_op jit(solution)/shard_map/ppermute | solution.py:126
  33.5 0.1 fusion.8.state_ref
  33.6 0.0 copy-done.5
  33.6 0.7 shard_map.57
  34.3 1.9 %collective-permute-start.7 = (bf16[256,1024]{1,0:T(8,128)(2,1)S(1)}, bf16[256,1024]{1,0:T(8,128)(2,1)S(1)}, u32[]{:S(2)}, u32[]{:S(2)}) collective-permute-start(bf16[256,1024]{1,0:T(8,128)(2,1)S(1)} %shard_map.57), channel_id=1, source_target_pairs={{0,24},{1,17},{2,10},{3,3},{4,28},{5,21},{6,14},{7,7},{8,0},{9,25}... | collective-permute-start | bytes 1572872 | tf_op jit(solution)/shard_map/ppermute | solution.py:171
  36.3 18.4 %collective-permute-start.6 = (bf16[256,1024]{1,0:T(8,128)(2,1)S(1)}, bf16[256,1024]{1,0:T(8,128)(2,1)S(1)}, u32[]{:S(2)}, u32[]{:S(2)}) collective-permute-start(bf16[256,1024]{1,0:T(8,128)(2,1)S(1)} %shard_map.57), channel_id=1, source_target_pairs={{0,16},{1,25},{2,2},{3,11},{4,20},{5,29},{6,6},{7,15},{8,24},{9,1}... | collective-permute-start | bytes 1572872 | tf_op jit(solution)/shard_map/ppermute | solution.py:171
  54.7 0.7 collective-permute-start.4
  55.4 0.0 collective-permute-done.7
  55.4 0.0 all-gather.2.cloned.1.call-done
  55.4 0.0 copy-start.6
  55.4 2.4 %convolution_convert_fusion = bf16[256,1024]{1,0:T(8,128)(2,1)S(1)} fusion(bf16[256,1024]{1,0:T(8,128)(2,1)S(1)} %collective-permute-done.7, bf16[1024,1024]{1,0:T(8,128)(2,1)} %all-gather.2.cloned.1.call-done), kind=kOutput, calls=%fused_computation | convolution fusion | flops 537133056 | bytes 3145728 | tf_op jit(solution)/shard_map/dot_general | solution.py:173
  57.9 12.5 %collective-permute-start.8 = (bf16[256,1024]{1,0:T(8,128)(2,1)S(1)}, bf16[256,1024]{1,0:T(8,128)(2,1)S(1)}, u32[]{:S(2)}, u32[]{:S(2)}) collective-permute-start(bf16[256,1024]{1,0:T(8,128)(2,1)S(1)} %convolution_convert_fusion), channel_id=1, source_target_pairs={{0,1},{1,0},{2,3},{3,2},{4,5},{5,4},{6,7},{7,6},{8,9},{9,8},{10,11... | collective-permute-start | bytes 1572872 | tf_op jit(solution)/shard_map/ppermute | solution.py:177
  70.4 15.3 %collective-permute-start.3 = (bf16[256,1024]{1,0:T(8,128)(2,1)S(1)}, bf16[256,1024]{1,0:T(8,128)(2,1)S(1)}, u32[]{:S(2)}, u32[]{:S(2)}) collective-permute-start(bf16[256,1024]{1,0:T(8,128)(2,1)S(1)} %shard_map.57), channel_id=1, source_target_pairs={{0,0},{1,9},{2,18},{3,27},{4,4},{5,13},{6,22},{7,31},{8,8},{9,17},... | collective-permute-start | bytes 1572872 | tf_op jit(solution)/shard_map/ppermute | solution.py:171
  85.7 0.0 collective-permute-done.4
  85.8 0.0 copy-done.6
  85.8 0.7 convolution_convert_fusion.2
  86.5 5.1 %collective-permute-start.5 = (bf16[256,1024]{1,0:T(8,128)(2,1)S(1)}, bf16[256,1024]{1,0:T(8,128)(2,1)S(1)}, u32[]{:S(2)}, u32[]{:S(2)}) collective-permute-start(bf16[256,1024]{1,0:T(8,128)(2,1)S(1)} %convolution_convert_fusion.2), channel_id=1, source_target_pairs={{0,1},{1,0},{2,3},{3,2},{4,5},{5,4},{6,7},{7,6},{8,9},{9,8},{10,11... | collective-permute-start | bytes 1572872 | tf_op jit(solution)/shard_map/ppermute | solution.py:178
  91.5 0.0 collective-permute-done.6
  91.5 0.0 collective-permute-done.8
  91.5 0.7 fusion.6
  92.3 0.1 collective-permute-start.9
  92.3 0.7 collective-permute-done.3
  93.1 0.0 collective-permute-done.5
  93.1 12.8 %collective-permute-done.9 = bf16[256,1024]{1,0:T(8,128)(2,1)S(1)} collective-permute-done((bf16[256,1024]{1,0:T(8,128)(2,1)S(1)}, bf16[256,1024]{1,0:T(8,128)(2,1)S(1)}, u32[]{:S(2)}, u32[]{:S(2)}) %collective-permute-start.9) | collective-permute-done | bytes 524320 | tf_op jit(solution)/shard_map/ppermute | solution.py:179
  105.9 0.8 fusion.3
  106.6 1.9 %collective-permute-start.10 = (bf16[256,1024]{1,0:T(8,128)(2,1)S(1)}, bf16[256,1024]{1,0:T(8,128)(2,1)S(1)}, u32[]{:S(2)}, u32[]{:S(2)}) collective-permute-start(bf16[256,1024]{1,0:T(8,128)(2,1)S(1)} %fusion.3), channel_id=1, source_target_pairs={{0,0},{1,24},{2,16},{3,8},{4,4},{5,28},{6,20},{7,12},{8,9},{9,1},{... | collective-permute-start | bytes 1572872 | tf_op jit(solution)/shard_map/ppermute | solution.py:183
  108.5 19.3 %collective-permute-done.10 = bf16[256,1024]{1,0:T(8,128)(2,1)S(1)} collective-permute-done((bf16[256,1024]{1,0:T(8,128)(2,1)S(1)}, bf16[256,1024]{1,0:T(8,128)(2,1)S(1)}, u32[]{:S(2)}, u32[]{:S(2)}) %collective-permute-start.10) | collective-permute-done | bytes 524320 | tf_op jit(solution)/shard_map/ppermute | solution.py:183
  127.9 0.8 copy.7
Async XLA Ops:
  6.5 20.1 %copy-start.3 = (bf16[256,1024]{1,0:T(8,128)(2,1)S(1)}, bf16[256,1024]{1,0:T(8,128)(2,1)}, u32[]{:S(2)}) copy-start(bf16[256,1024]{1,0:T(8,128)(2,1)} %v_ref.3) | copy-start | bytes 1572868
  6.5 20.2 %copy-start.1 = (bf16[256,1024]{1,0:T(8,128)(2,1)S(1)}, bf16[256,1024]{1,0:T(8,128)(2,1)}, u32[]{:S(2)}) copy-start(bf16[256,1024]{1,0:T(8,128)(2,1)} %k_ref.3) | copy-start | bytes 1572868
  6.5 48.9 %all-gather.2.cloned.1.call-start = ((), (), s32[]{:S(2)}) async-start(), calls=%async_computation | async-start | bytes 3145728 | tf_op jit(solution)/shard_map/all_gather | solution.py:142
  7.3 1.0 copy-start
  8.3 1.0 copy-start.2
  9.3 17.4 %copy-start.4 = (bf16[256,1024]{1,0:T(8,128)(2,1)S(1)}, bf16[256,1024]{1,0:T(8,128)(2,1)}, u32[]{:S(2)}) copy-start(bf16[256,1024]{1,0:T(8,128)(2,1)} %q_ref.3) | copy-start | bytes 1572868
  9.7 7.2 %collective-permute-start = (bf16[8,128,128]{2,1,0:T(8,128)(2,1)S(1)}, bf16[8,128,128]{2,1,0:T(8,128)(2,1)S(1)}, u32[]{:S(2)}, u32[]{:S(2)}) collective-permute-start(bf16[8,128,128]{2,1,0:T(8,128)(2,1)S(1)} %get-tuple-element.7), channel_id=1, source_target_pairs={{0,4},{4,0},{8,12},{12,8},{16,20},{20,16},{24,28},{28,24},{1,5},{5... | collective-permute-start | bytes 786440 | tf_op jit(solution)/shard_map/ppermute | solution.py:120
  17.0 8.3 %collective-permute-start.1 = (bf16[8,128,128]{2,1,0:T(8,128)(2,1)S(1)}, bf16[8,128,128]{2,1,0:T(8,128)(2,1)S(1)}, u32[]{:S(2)}, u32[]{:S(2)}) collective-permute-start(bf16[8,128,128]{2,1,0:T(8,128)(2,1)S(1)} %fusion.10), channel_id=1, source_target_pairs={{0,8},{4,12},{8,16},{12,20},{16,24},{20,28},{1,9},{5,13},{9,17},{1... | collective-permute-start | bytes 786440 | tf_op jit(solution)/shard_map/ppermute | solution.py:126
  25.4 8.3 %copy-start.5 = (f32[1024]{0:T(1024)S(1)}, f32[1024]{0:T(1024)}, u32[]{:S(2)}) copy-start(f32[1024]{0:T(1024)} %param.8) | copy-start | bytes 12292
  25.4 8.1 %collective-permute-start.2 = (bf16[8,128,128]{2,1,0:T(8,128)(2,1)S(1)}, bf16[8,128,128]{2,1,0:T(8,128)(2,1)S(1)}, u32[]{:S(2)}, u32[]{:S(2)}) collective-permute-start(bf16[8,128,128]{2,1,0:T(8,128)(2,1)S(1)} %fusion.9), channel_id=1, source_target_pairs={{0,16},{4,20},{8,24},{12,28},{1,17},{5,21},{9,25},{13,29},{2,18},{... | collective-permute-start | bytes 786440 | tf_op jit(solution)/shard_map/ppermute | solution.py:126
  34.3 21.0 %collective-permute-start.7 = (bf16[256,1024]{1,0:T(8,128)(2,1)S(1)}, bf16[256,1024]{1,0:T(8,128)(2,1)S(1)}, u32[]{:S(2)}, u32[]{:S(2)}) collective-permute-start(bf16[256,1024]{1,0:T(8,128)(2,1)S(1)} %shard_map.57), channel_id=1, source_target_pairs={{0,24},{1,17},{2,10},{3,3},{4,28},{5,21},{6,14},{7,7},{8,0},{9,25}... | collective-permute-start | bytes 1572872 | tf_op jit(solution)/shard_map/ppermute | solution.py:171
  36.3 55.3 %collective-permute-start.6 = (bf16[256,1024]{1,0:T(8,128)(2,1)S(1)}, bf16[256,1024]{1,0:T(8,128)(2,1)S(1)}, u32[]{:S(2)}, u32[]{:S(2)}) collective-permute-start(bf16[256,1024]{1,0:T(8,128)(2,1)S(1)} %shard_map.57), channel_id=1, source_target_pairs={{0,16},{1,25},{2,2},{3,11},{4,20},{5,29},{6,6},{7,15},{8,24},{9,1}... | collective-permute-start | bytes 1572872 | tf_op jit(solution)/shard_map/ppermute | solution.py:171
  54.7 31.1 %collective-permute-start.4 = (bf16[256,1024]{1,0:T(8,128)(2,1)S(1)}, bf16[256,1024]{1,0:T(8,128)(2,1)S(1)}, u32[]{:S(2)}, u32[]{:S(2)}) collective-permute-start(bf16[256,1024]{1,0:T(8,128)(2,1)S(1)} %shard_map.57), channel_id=1, source_target_pairs={{0,8},{1,1},{2,26},{3,19},{4,12},{5,5},{6,30},{7,23},{8,16},{9,9},... | collective-permute-start | bytes 1572872 | tf_op jit(solution)/shard_map/ppermute | solution.py:171
  55.4 30.3 %copy-start.6 = (bf16[1024,1024]{1,0:T(8,128)(2,1)S(1)}, bf16[1024,1024]{1,0:T(8,128)(2,1)}, u32[]{:S(2)}) copy-start(bf16[1024,1024]{1,0:T(8,128)(2,1)} %all-gather.2.cloned.1.call-done) | copy-start | bytes 6291460
  57.9 33.6 %collective-permute-start.8 = (bf16[256,1024]{1,0:T(8,128)(2,1)S(1)}, bf16[256,1024]{1,0:T(8,128)(2,1)S(1)}, u32[]{:S(2)}, u32[]{:S(2)}) collective-permute-start(bf16[256,1024]{1,0:T(8,128)(2,1)S(1)} %convolution_convert_fusion), channel_id=1, source_target_pairs={{0,1},{1,0},{2,3},{3,2},{4,5},{5,4},{6,7},{7,6},{8,9},{9,8},{10,11... | collective-permute-start | bytes 1572872 | tf_op jit(solution)/shard_map/ppermute | solution.py:177
  70.4 22.6 %collective-permute-start.3 = (bf16[256,1024]{1,0:T(8,128)(2,1)S(1)}, bf16[256,1024]{1,0:T(8,128)(2,1)S(1)}, u32[]{:S(2)}, u32[]{:S(2)}) collective-permute-start(bf16[256,1024]{1,0:T(8,128)(2,1)S(1)} %shard_map.57), channel_id=1, source_target_pairs={{0,0},{1,9},{2,18},{3,27},{4,4},{5,13},{6,22},{7,31},{8,8},{9,17},... | collective-permute-start | bytes 1572872 | tf_op jit(solution)/shard_map/ppermute | solution.py:171
  86.5 6.6 %collective-permute-start.5 = (bf16[256,1024]{1,0:T(8,128)(2,1)S(1)}, bf16[256,1024]{1,0:T(8,128)(2,1)S(1)}, u32[]{:S(2)}, u32[]{:S(2)}) collective-permute-start(bf16[256,1024]{1,0:T(8,128)(2,1)S(1)} %convolution_convert_fusion.2), channel_id=1, source_target_pairs={{0,1},{1,0},{2,3},{3,2},{4,5},{5,4},{6,7},{7,6},{8,9},{9,8},{10,11... | collective-permute-start | bytes 1572872 | tf_op jit(solution)/shard_map/ppermute | solution.py:178
  92.3 13.6 %collective-permute-start.9 = (bf16[256,1024]{1,0:T(8,128)(2,1)S(1)}, bf16[256,1024]{1,0:T(8,128)(2,1)S(1)}, u32[]{:S(2)}, u32[]{:S(2)}) collective-permute-start(bf16[256,1024]{1,0:T(8,128)(2,1)S(1)} %fusion.6), channel_id=1, source_target_pairs={{0,2},{1,3},{2,0},{3,1},{4,6},{5,7},{6,4},{7,5},{8,10},{9,11},{10,... | collective-permute-start | bytes 1572872 | tf_op jit(solution)/shard_map/ppermute | solution.py:179
  106.6 21.3 %collective-permute-start.10 = (bf16[256,1024]{1,0:T(8,128)(2,1)S(1)}, bf16[256,1024]{1,0:T(8,128)(2,1)S(1)}, u32[]{:S(2)}, u32[]{:S(2)}) collective-permute-start(bf16[256,1024]{1,0:T(8,128)(2,1)S(1)} %fusion.3), channel_id=1, source_target_pairs={{0,0},{1,24},{2,16},{3,8},{4,4},{5,28},{6,20},{7,12},{8,9},{9,1},{... | collective-permute-start | bytes 1572872 | tf_op jit(solution)/shard_map/ppermute | solution.py:183
Sparse Core Ops, SparseCore 0:
  8.9 34.1 all-gather.1

commit v3 on v2

--- a/solution.py
+++ b/solution.py
@@ -185,13 +185,128 @@
     return body
 
 
+def project_kernel(pick_ref, here_ref, there_ref, low_ref, high_ref, keep_ref, send_ref):
+    own = pick_ref[0] == 1
+    here, there = here_ref[...], there_ref[...]
+    kept = jnp.where(own, here, there)
+    sent = jnp.where(own, there, here)
+    for half, weight_ref in enumerate((low_ref, high_ref)):
+        weight = weight_ref[...]
+        send_ref[half] = jnp.dot(sent, weight, preferred_element_type=F32).astype(BF16)
+        keep_ref[half] = jnp.dot(kept, weight, preferred_element_type=F32).astype(BF16)
+
+
+def pairs_body(queries, key_vectors, value_vectors, norm_gain, out_weight):
+    rows, features = queries.shape
+    heads = features // HD
+    size = rows * features
+    half_cols = out_weight.shape[1]
+    both = ("seq", "head")
+    place, group = lax.axis_index("seq"), lax.axis_index("head")
+    z, y, x, core = place // 2, place % 2, group // 2, group % 2
+    lower = z < 2
+    home_core = core == z % 2
+    devices = [(s // 2, s % 2, h // 2, h % 2) for s in range(8) for h in range(4)]
+
+    def at(z, y, x, c):
+        return (z * 2 + y) * 4 + x * 2 + c
+
+    def seq_swap(mask):
+        return [(s, s ^ mask) for s in range(8)]
+
+    def move(value, place_of, chosen=lambda z, y, x, c: True):
+        pairs = [(at(*d), at(*place_of(*d))) for d in devices if chosen(*d)]
+        return lax.ppermute(value, both, pairs)
+
+    wide, narrow = call(
+        state_kernel,
+        (
+            jax.ShapeDtypeStruct((heads, HD, HD), F32),
+            jax.ShapeDtypeStruct((heads, HD, HD), BF16),
+        ),
+        2 * size * HD,
+        4 * size + 6 * heads * HD * HD,
+    )(key_vectors, value_vectors)
+    within = call(
+        within_kernel, jax.ShapeDtypeStruct((rows, features), F32), 4 * size * BLOCK, 10 * size
+    )(queries, key_vectors, value_vectors)
+
+    cut = out_weight.shape[0] // 4
+    down = lax.ppermute(out_weight, "seq", [(s, s - 4) for s in range(4, 8)])
+    up_pairs = [(s, s + 4) for s in range(4)]
+    up_first = lax.ppermute(out_weight[:cut], "seq", up_pairs)
+
+    parts = 2
+    step = heads // parts
+    totals, firsts, before = [], [], []
+    for part in range(parts):
+        mine = slice(part * step, (part + 1) * step)
+        mate = lax.ppermute(narrow[mine], "seq", seq_swap(1)).astype(F32)
+        totals.append(wide[mine] + mate)
+        firsts.append(jnp.where(y == 1, mate, 0.0))
+        before.append(jnp.zeros((step, HD, HD), F32))
+    for plane in range(3):
+        pairs = [(2 * plane + i, 2 * plane + 2 + i) for i in range(2)]
+        for part in range(parts):
+            onward = (before[part] + totals[part]).astype(BF16)
+            before[part] += lax.ppermute(onward, "seq", pairs).astype(F32)
+        if plane == 1:
+            rest, before[0] = lax.optimization_barrier((out_weight[cut:], before[0]))
+    up_rest = lax.ppermute(rest, "seq", up_pairs)
+    state_in = jnp.concatenate(
+        [(before[part] + firsts[part]).astype(BF16) for part in range(parts)], axis=0
+    )
+    attended = call(
+        attend_kernel, jax.ShapeDtypeStruct((rows, features), BF16), 2 * size * HD, 8 * size
+    )(queries, within, state_in, norm_gain[None])
+
+    from_y = lax.ppermute(attended, "seq", seq_swap(1))
+    from_z = lax.ppermute(attended, "seq", seq_swap(2))
+    from_both = lax.ppermute(attended, "seq", seq_swap(3))
+
+    low = jnp.where(lower, out_weight, jnp.concatenate([up_first, up_rest], axis=0))
+    high = jnp.where(lower, down, out_weight)
+    pick = home_core.astype(jnp.int32)[None]
+
+    def reduced(here, there):
+        tile = jax.ShapeDtypeStruct((2, rows, half_cols), BF16)
+        vmem = pl.BlockSpec(memory_space=pltpu.VMEM)
+        keep, send = pl.pallas_call(
+            project_kernel,
+            out_shape=(tile, tile),
+            in_specs=[pl.BlockSpec(memory_space=pltpu.SMEM)] + [vmem] * 4,
+            out_specs=(vmem, vmem),
+            compiler_params=pltpu.CompilerParams(vmem_limit_bytes=24 * 1024 * 1024),
+            cost_estimate=pl.CostEstimate(
+                flops=8 * size * half_cols, bytes_accessed=12 * size, transcendentals=0
+            ),
+        )(pick, here, there, low, high)
+        got = move(send, lambda z, y, x, c: (z, y, x, 1 - c))
+        total = keep.astype(F32) + got.astype(F32)
+        own = jnp.where(x == 0, total[0], total[1])
+        other = jnp.where(x == 0, total[1], total[0]).astype(BF16)
+        return (own + move(other, lambda z, y, x, c: (z, y, 1 - x, c)).astype(F32)).astype(BF16)
+
+    first = reduced(attended, from_z)
+    second = reduced(from_y, from_both)
+    near = move(first, lambda z, y, x, c: (z ^ 1, y, x, 1 - c), lambda z, y, x, c: c != z % 2)
+    near = jnp.where(home_core, first, near)
+    far = move(
+        second,
+        lambda z, y, x, c: (z, y ^ 1, x, c) if c == z % 2 else (z ^ 1, y ^ 1, x, 1 - c),
+    )
+    return jnp.concatenate([jnp.where(y == 0, near, far), jnp.where(y == 0, far, near)], axis=1)
+
+
 def solution(mesh):
     seq_count, head_groups = mesh.shape["seq"], mesh.shape["head"]
 
     def run(queries, key_vectors, value_vectors, norm_gain, out_weight):
         one_block = queries.shape[0] == BLOCK * seq_count
         body = general_body
-        if one_block and head_groups == 4 and seq_count % head_groups == 0:
+        if one_block and head_groups == 4 and seq_count == 8:
+            body = pairs_body
+        elif one_block and head_groups == 4 and seq_count % head_groups == 0:
             body = planes_body(seq_count, head_groups)
         return jax.shard_map(
             body,

time: 136 us -> 116 us (0.85)
  the two profiles are of different devices: /device:TPU:17 before, /device:TPU:27 now
where the time goes in v3:
time: 116 us; the launch traced here: 115 us
  waiting for transfers between devices  69.6 us (60%)
  starting transfers between devices  29.7 us (26%)
  other arithmetic  7.16 us (6%)
  Pallas kernels  4.49 us (4%)
  local copies, waits for them, and re-layouts  3.81 us (3%)
    ppermute x6, waiting for transfers between devices, move(): return lax.ppermute(value, both, pairs)  19.7 us
    ppermute x1, waiting for transfers between devices, pairs_body(): up_first = lax.ppermute(out_weight[:cut], 'seq', up_pairs)  17.1 us
    ppermute x1, waiting for transfers between devices, pairs_body(): up_rest = lax.ppermute(rest, 'seq', up_pairs)  17.1 us
    ppermute x1, starting transfers between devices, pairs_body(): down = lax.ppermute(out_weight, 'seq', [(s, s - 4) for s in range(4, 8)])  12.1 us
    ppermute x1, waiting for transfers between devices, pairs_body(): from_both = lax.ppermute(attended, 'seq', seq_swap(3))  7.17 us
    ppermute x6, starting transfers between devices, move(): return lax.ppermute(value, both, pairs)  6.09 us
    ppermute x6, starting transfers between devices, pairs_body(): before[part] += lax.ppermute(onward, 'seq', pairs).astype(F32)  5.89 us
    ppermute x2, waiting for transfers between devices, pairs_body(): mate = lax.ppermute(narrow[mine], 'seq', seq_swap(1)).astype(F32)  4.99 us
  transfers between devices with their start and end apart: 20, of which 11 were waited for; matrix products, arithmetic and copies ran while one was open for 6% of the time, Pallas kernels for 4%

profile of v3, /device:TPU:27, one launch (start us, length us, event | category | flops | bytes accessed | tf_op | source)
XLA Modules:
  0.0 115.1 jit_solution(12403918383002473407)
XLA Ops:
  0.0 1.0 copy-done
  1.0 1.0 copy-done.2
  2.1 0.4 shard_map.56
  2.4 0.0 copy-start.6
  2.5 1.3 %collective-permute-start = (bf16[4,128,128]{2,1,0:T(8,128)(2,1)S(1)}, bf16[4,128,128]{2,1,0:T(8,128)(2,1)S(1)}, u32[]{:S(2)}, u32[]{:S(2)}) collective-permute-start(bf16[4,128,128]{2,1,0:T(8,128)(2,1)S(1)} %get-tuple-element.29), channel_id=1, source_target_pairs={{0,4},{4,0},{8,12},{12,8},{16,20},{20,16},{24,28},{28,24},{1,5},{5... | collective-permute-start | bytes 393224 | tf_op jit(solution)/shard_map/ppermute | solution.py:244
  3.8 0.2 collective-permute-start.4
  4.0 2.9 %collective-permute-done = bf16[4,128,128]{2,1,0:T(8,128)(2,1)S(1)} collective-permute-done((bf16[4,128,128]{2,1,0:T(8,128)(2,1)S(1)}, bf16[4,128,128]{2,1,0:T(8,128)(2,1)S(1)}, u32[]{:S(2)}, u32[]{:S(2)}) %collective-permute-start) | collective-permute-done | bytes 131104 | tf_op jit(solution)/shard_map/ppermute | solution.py:244
  7.0 0.7 collective-permute-start.1
  7.6 2.1 %collective-permute-done.4 = bf16[4,128,128]{2,1,0:T(8,128)(2,1)S(1)} collective-permute-done((bf16[4,128,128]{2,1,0:T(8,128)(2,1)S(1)}, bf16[4,128,128]{2,1,0:T(8,128)(2,1)S(1)}, u32[]{:S(2)}, u32[]{:S(2)}) %collective-permute-start.4) | collective-permute-done | bytes 131104 | tf_op jit(solution)/shard_map/ppermute | solution.py:244
  9.7 0.0 collective-permute-done.1
  9.7 0.1 fusion.4
  9.8 0.7 collective-permute-start.2
  10.5 0.9 slice.34
  11.4 0.7 collective-permute-start.5
  12.1 0.0 collective-permute-done.2
  12.2 0.0 copy-start.1
  12.2 0.0 copy-start.3
  12.2 0.0 copy-start.4
  12.2 0.0 collective-permute-done.5
  12.2 0.8 add_convert_fusion.1
  13.0 1.3 %collective-permute-start.6 = (bf16[4,128,128]{2,1,0:T(8,128)(2,1)}, bf16[4,128,128]{2,1,0:T(8,128)(2,1)}, u32[]{:S(2)}, u32[]{:S(2)}) collective-permute-start(bf16[4,128,128]{2,1,0:T(8,128)(2,1)} %get-tuple-element.26), channel_id=1, source_target_pairs={{8,16},{12,20},{9,17},{13,21},{10,18},{14,22},{11,19},{15,23}} | collective-permute-start | bytes 393224 | tf_op jit(solution)/shard_map/ppermute | solution.py:252
  14.3 12.1 %collective-permute-start.11 = (bf16[1024,512]{1,0:T(8,128)(2,1)S(1)}, bf16[1024,512]{1,0:T(8,128)(2,1)}, u32[]{:S(2)}, u32[]{:S(2)}) collective-permute-start(bf16[1024,512]{1,0:T(8,128)(2,1)S(1)} %copy-done.6), channel_id=1, source_target_pairs={{16,0},{20,4},{24,8},{28,12},{17,1},{21,5},{25,9},{29,13},{18,2},{... | collective-permute-start | bytes 3145736 | tf_op jit(solution)/shard_map/ppermute | solution.py:235
  26.4 0.7 slice.39
  27.1 1.3 %collective-permute-start.9 = (bf16[256,512]{1,0:T(8,128)(2,1)}, bf16[256,512]{1,0:T(8,128)(2,1)}, u32[]{:S(2)}, u32[]{:S(2)}) collective-permute-start(bf16[256,512]{1,0:T(8,128)(2,1)} %slice.39), channel_id=1, source_target_pairs={{0,16},{4,20},{8,24},{12,28},{1,17},{5,21},{9,25},{13,29},{2,18},{... | collective-permute-start | bytes 786440 | tf_op jit(solution)/shard_map/ppermute | solution.py:237
  28.4 0.9 shard_map.55.within_ref
  29.4 1.4 %collective-permute-start.10 = (bf16[768,512]{1,0:T(8,128)(2,1)}, bf16[768,512]{1,0:T(8,128)(2,1)}, u32[]{:S(2)}, u32[]{:S(2)}) collective-permute-start(bf16[768,512]{1,0:T(8,128)(2,1)} %slice.34), channel_id=1, source_target_pairs={{0,16},{4,20},{8,24},{12,28},{1,17},{5,21},{9,25},{13,29},{2,18},{... | collective-permute-start | bytes 2359304 | tf_op jit(solution)/shard_map/ppermute | solution.py:255
  30.8 1.3 %collective-permute-start.3 = (bf16[4,128,128]{2,1,0:T(8,128)(2,1)}, bf16[4,128,128]{2,1,0:T(8,128)(2,1)S(1)}, u32[]{:S(2)}, u32[]{:S(2)}) collective-permute-start(bf16[4,128,128]{2,1,0:T(8,128)(2,1)} %get-tuple-element.25), channel_id=1, source_target_pairs={{16,24},{20,28},{17,25},{21,29},{18,26},{22,30},{19,27},{23,31}} | collective-permute-start | bytes 393224 | tf_op jit(solution)/shard_map/ppermute | solution.py:252
  32.1 1.0 add_convert_fusion
  33.2 0.0 copy-start.5
  33.2 1.3 %collective-permute-start.7 = (bf16[4,128,128]{2,1,0:T(8,128)(2,1)S(1)}, bf16[4,128,128]{2,1,0:T(8,128)(2,1)S(1)}, u32[]{:S(2)}, u32[]{:S(2)}) collective-permute-start(bf16[4,128,128]{2,1,0:T(8,128)(2,1)S(1)} %add_convert_fusion), channel_id=1, source_target_pairs={{16,24},{20,28},{17,25},{21,29},{18,26},{22,30},{19,27},{23,31}} | collective-permute-start | bytes 393224 | tf_op jit(solution)/shard_map/ppermute | solution.py:252
  34.5 2.3 %collective-permute-done.3 = bf16[4,128,128]{2,1,0:T(8,128)(2,1)S(1)} collective-permute-done((bf16[4,128,128]{2,1,0:T(8,128)(2,1)}, bf16[4,128,128]{2,1,0:T(8,128)(2,1)S(1)}, u32[]{:S(2)}, u32[]{:S(2)}) %collective-permute-start.3) | collective-permute-done | bytes 131104 | tf_op jit(solution)/shard_map/ppermute | solution.py:252
  36.7 1.0 fusion.3
  37.7 1.2 %collective-permute-done.7 = bf16[4,128,128]{2,1,0:T(8,128)(2,1)S(1)} collective-permute-done((bf16[4,128,128]{2,1,0:T(8,128)(2,1)S(1)}, bf16[4,128,128]{2,1,0:T(8,128)(2,1)S(1)}, u32[]{:S(2)}, u32[]{:S(2)}) %collective-permute-start.7) | collective-permute-done | bytes 131104 | tf_op jit(solution)/shard_map/ppermute | solution.py:252
  38.9 1.0 fusion.6
  39.9 0.7 shard_map.57.here_ref
  40.7 0.1 collective-permute-start.8
  40.8 1.3 %collective-permute-start.15 = (bf16[256,1024]{1,0:T(8,128)(2,1)S(1)}, bf16[256,1024]{1,0:T(8,128)(2,1)S(1)}, u32[]{:S(2)}, u32[]{:S(2)}) collective-permute-start(bf16[256,1024]{1,0:T(8,128)(2,1)S(1)} %shard_map.57.here_ref), channel_id=1, source_target_pairs={{0,4},{4,0},{8,12},{12,8},{16,20},{20,16},{24,28},{28,24},{1,5},{5... | collective-permute-start | bytes 1572872 | tf_op jit(solution)/shard_map/ppermute | solution.py:263
  42.1 17.1 %collective-permute-done.9 = bf16[256,512]{1,0:T(8,128)(2,1)} collective-permute-done((bf16[256,512]{1,0:T(8,128)(2,1)}, bf16[256,512]{1,0:T(8,128)(2,1)}, u32[]{:S(2)}, u32[]{:S(2)}) %collective-permute-start.9) | collective-permute-done | bytes 262176 | tf_op jit(solution)/shard_map/ppermute | solution.py:237
  59.2 0.0 collective-permute-done.11
  59.2 17.1 %collective-permute-done.10 = bf16[768,512]{1,0:T(8,128)(2,1)} collective-permute-done((bf16[768,512]{1,0:T(8,128)(2,1)}, bf16[768,512]{1,0:T(8,128)(2,1)}, u32[]{:S(2)}, u32[]{:S(2)}) %collective-permute-start.10) | collective-permute-done | bytes 786464 | tf_op jit(solution)/shard_map/ppermute | solution.py:255
  76.3 1.7 %broadcast_select_fusion = (bf16[1024,512]{1,0:T(8,128)(2,1)S(1)}, bf16[1024,512]{1,0:T(8,128)(2,1)S(1)}) fusion(bf16[1024,512]{1,0:T(8,128)(2,1)} %collective-permute-done.11, bf16[1024,512]{1,0:T(8,128)(2,1)S(1)} %copy-done.6, pred[]{:T(512)S(6)} %lt.20, bf16[768,512]{1,0:T(8,128)(2,1)} %collective-permute-done.10, bf16[256,512]{1,0:T(8,128)(2,1)} %collective-permute-done.9), kind=kLoop, calls=%fused_computation.3 | loop fusion | flops 3145728 | bytes 5242881 | tf_op jit(solution)/shard_map/jit(_where)/select_n | solution.py:268
  78.0 0.0 collective-permute-done.8.there_ref
  78.0 1.2 %shard_map.58 = (bf16[2,256,512]{2,1,0:T(8,128)(2,1)S(1)}, bf16[2,256,512]{2,1,0:T(8,128)(2,1)S(1)}) custom-call(s32[1]{0:T(128)} %bitcast.pick_ref, bf16[256,1024]{1,0:T(8,128)(2,1)S(1)} %shard_map.57.here_ref, bf16[256,1024]{1,0:T(8,128)(2,1)S(1)} %collective-permute-done.8.there_ref, bf16[1024,512]{1,0:T(8,128)(2,1)S(1)} %get-tuple-element.22.low_ref, ...), custom_call_target="tpu_custom_call" | custom-call | flops 1073741824 | bytes 3145728 | tf_op jit(solution)/shard_map/pallas_call | solution.py:274
  79.2 2.4 %collective-permute-start.12 = (bf16[2,256,512]{2,1,0:T(8,128)(2,1)S(1)}, bf16[2,256,512]{2,1,0:T(8,128)(2,1)S(1)}, u32[]{:S(2)}, u32[]{:S(2)}) collective-permute-start(bf16[2,256,512]{2,1,0:T(8,128)(2,1)S(1)} %get-tuple-element.18), channel_id=1, source_target_pairs={{0,1},{1,0},{2,3},{3,2},{4,5},{5,4},{6,7},{7,6},{8,9},{9,8},{10,11... | collective-permute-start | bytes 1572872 | tf_op jit(solution)/shard_map/ppermute | solution.py:219
  81.6 0.0 collective-permute-done.15.here_ref
  81.6 7.2 %collective-permute-done.16.there_ref = bf16[256,1024]{1,0:T(8,128)(2,1)S(1)} collective-permute-done((bf16[256,1024]{1,0:T(8,128)(2,1)S(1)}, bf16[256,1024]{1,0:T(8,128)(2,1)S(1)}, u32[]{:S(2)}, u32[]{:S(2)}) %collective-permute-start.16) | collective-permute-done | bytes 524320 | tf_op jit(solution)/shard_map/ppermute | solution.py:265
  88.8 1.2 %shard_map.59 = (bf16[2,256,512]{2,1,0:T(8,128)(2,1)S(1)}, bf16[2,256,512]{2,1,0:T(8,128)(2,1)S(1)}) custom-call(s32[1]{0:T(128)} %bitcast.pick_ref, bf16[256,1024]{1,0:T(8,128)(2,1)S(1)} %collective-permute-done.15.here_ref, bf16[256,1024]{1,0:T(8,128)(2,1)S(1)} %collective-permute-done.16.there_ref, bf16[1024,512]{1,0:T(8,128)(2,1)S(1)} %get-tuple-element.22.low_ref, ...), custom_call_target="tpu_custom_call" | custom-call | flops 1073741824 | bytes 3145728 | tf_op jit(solution)/shard_map/pallas_call | solution.py:274
  90.0 2.1 %collective-permute-start.17 = (bf16[2,256,512]{2,1,0:T(8,128)(2,1)S(1)}, bf16[2,256,512]{2,1,0:T(8,128)(2,1)S(1)}, u32[]{:S(2)}, u32[]{:S(2)}) collective-permute-start(bf16[2,256,512]{2,1,0:T(8,128)(2,1)S(1)} %get-tuple-element.20), channel_id=1, source_target_pairs={{0,1},{1,0},{2,3},{3,2},{4,5},{5,4},{6,7},{7,6},{8,9},{9,8},{10,11... | collective-permute-start | bytes 1572872 | tf_op jit(solution)/shard_map/ppermute | solution.py:219
  92.2 0.0 collective-permute-done.12
  92.2 0.1 convert_add_fusion.1
  92.3 0.1 fusion.8
  92.4 0.3 collective-permute-start.13
  92.7 1.0 collective-permute-done.17
  93.7 0.1 convert_add_fusion
  93.8 0.1 fusion.9
  93.9 0.3 collective-permute-start.18
  94.2 6.1 %collective-permute-done.13 = bf16[256,512]{1,0:T(8,128)(2,1)S(1)} collective-permute-done((bf16[256,512]{1,0:T(8,128)(2,1)S(1)}, bf16[256,512]{1,0:T(8,128)(2,1)S(1)}, u32[]{:S(2)}, u32[]{:S(2)}) %collective-permute-start.13) | collective-permute-done | bytes 262176 | tf_op jit(solution)/shard_map/ppermute | solution.py:219
  100.3 0.1 fusion.1
  100.5 0.7 collective-permute-start.14
  101.2 4.8 %collective-permute-done.18 = bf16[256,512]{1,0:T(8,128)(2,1)S(1)} collective-permute-done((bf16[256,512]{1,0:T(8,128)(2,1)S(1)}, bf16[256,512]{1,0:T(8,128)(2,1)S(1)}, u32[]{:S(2)}, u32[]{:S(2)}) %collective-permute-start.18) | collective-permute-done | bytes 262176 | tf_op jit(solution)/shard_map/ppermute | solution.py:219
  105.9 0.1 fusion
  106.1 0.3 collective-permute-start.19
  106.4 7.8 %collective-permute-done.19 = bf16[256,512]{1,0:T(8,128)(2,1)S(1)} collective-permute-done((bf16[256,512]{1,0:T(8,128)(2,1)S(1)}, bf16[256,512]{1,0:T(8,128)(2,1)S(1)}, u32[]{:S(2)}, u32[]{:S(2)}) %collective-permute-start.19) | collective-permute-done | bytes 262176 | tf_op jit(solution)/shard_map/ppermute | solution.py:219
  114.2 0.9 pad_maximum_fusion
  (21 shorter events, 0.2 us)
Async XLA Ops:
  0.0 1.0 copy-start
  1.0 1.0 copy-start.2
  2.4 8.0 %copy-start.6 = (bf16[1024,512]{1,0:T(8,128)(2,1)S(1)}, bf16[1024,512]{1,0:T(8,128)(2,1)}, u32[]{:S(2)}) copy-start(bf16[1024,512]{1,0:T(8,128)(2,1)} %param.9) | copy-start | bytes 3145732
  2.5 4.4 %collective-permute-start = (bf16[4,128,128]{2,1,0:T(8,128)(2,1)S(1)}, bf16[4,128,128]{2,1,0:T(8,128)(2,1)S(1)}, u32[]{:S(2)}, u32[]{:S(2)}) collective-permute-start(bf16[4,128,128]{2,1,0:T(8,128)(2,1)S(1)} %get-tuple-element.29), channel_id=1, source_target_pairs={{0,4},{4,0},{8,12},{12,8},{16,20},{20,16},{24,28},{28,24},{1,5},{5... | collective-permute-start | bytes 393224 | tf_op jit(solution)/shard_map/ppermute | solution.py:244
  3.8 5.9 %collective-permute-start.4 = (bf16[4,128,128]{2,1,0:T(8,128)(2,1)S(1)}, bf16[4,128,128]{2,1,0:T(8,128)(2,1)S(1)}, u32[]{:S(2)}, u32[]{:S(2)}) collective-permute-start(bf16[4,128,128]{2,1,0:T(8,128)(2,1)S(1)} %get-tuple-element.30), channel_id=1, source_target_pairs={{0,4},{4,0},{8,12},{12,8},{16,20},{20,16},{24,28},{28,24},{1,5},{5... | collective-permute-start | bytes 393224 | tf_op jit(solution)/shard_map/ppermute | solution.py:244
  6.9 5.3 %copy-start.7 = (bf16[4,128,128]{2,1,0:T(8,128)(2,1)}, bf16[4,128,128]{2,1,0:T(8,128)(2,1)S(1)}, u32[]{:S(2)}) copy-start(bf16[4,128,128]{2,1,0:T(8,128)(2,1)S(1)} %collective-permute-done) | copy-start | bytes 393220
  7.0 2.8 %collective-permute-start.1 = (bf16[4,128,128]{2,1,0:T(8,128)(2,1)S(1)}, bf16[4,128,128]{2,1,0:T(8,128)(2,1)S(1)}, u32[]{:S(2)}, u32[]{:S(2)}) collective-permute-start(bf16[4,128,128]{2,1,0:T(8,128)(2,1)S(1)} %fusion.10), channel_id=1, source_target_pairs={{0,8},{4,12},{1,9},{5,13},{2,10},{6,14},{3,11},{7,15}} | collective-permute-start | bytes 393224 | tf_op jit(solution)/shard_map/ppermute | solution.py:252
  9.8 2.3 %collective-permute-start.2 = (bf16[4,128,128]{2,1,0:T(8,128)(2,1)S(1)}, bf16[4,128,128]{2,1,0:T(8,128)(2,1)S(1)}, u32[]{:S(2)}, u32[]{:S(2)}) collective-permute-start(bf16[4,128,128]{2,1,0:T(8,128)(2,1)S(1)} %get-tuple-element.27), channel_id=1, source_target_pairs={{8,16},{12,20},{9,17},{13,21},{10,18},{14,22},{11,19},{15,23}} | collective-permute-start | bytes 393224 | tf_op jit(solution)/shard_map/ppermute | solution.py:252
  11.4 0.8 collective-permute-start.5
  12.2 16.2 %copy-start.1 = (bf16[256,1024]{1,0:T(8,128)(2,1)S(1)}, bf16[256,1024]{1,0:T(8,128)(2,1)}, u32[]{:S(2)}) copy-start(bf16[256,1024]{1,0:T(8,128)(2,1)} %k_ref.3) | copy-start | bytes 1572868
  12.2 16.2 %copy-start.3 = (bf16[256,1024]{1,0:T(8,128)(2,1)S(1)}, bf16[256,1024]{1,0:T(8,128)(2,1)}, u32[]{:S(2)}) copy-start(bf16[256,1024]{1,0:T(8,128)(2,1)} %v_ref.3) | copy-start | bytes 1572868
  12.2 16.2 %copy-start.4 = (bf16[256,1024]{1,0:T(8,128)(2,1)S(1)}, bf16[256,1024]{1,0:T(8,128)(2,1)}, u32[]{:S(2)}) copy-start(bf16[256,1024]{1,0:T(8,128)(2,1)} %q_ref.3) | copy-start | bytes 1572868
  12.2 14.9 %copy-start.8 = (bf16[4,128,128]{2,1,0:T(8,128)(2,1)}, bf16[4,128,128]{2,1,0:T(8,128)(2,1)S(1)}, u32[]{:S(2)}) copy-start(bf16[4,128,128]{2,1,0:T(8,128)(2,1)S(1)} %collective-permute-done.5) | copy-start | bytes 393220
  13.0 19.1 %collective-permute-start.6 = (bf16[4,128,128]{2,1,0:T(8,128)(2,1)}, bf16[4,128,128]{2,1,0:T(8,128)(2,1)}, u32[]{:S(2)}, u32[]{:S(2)}) collective-permute-start(bf16[4,128,128]{2,1,0:T(8,128)(2,1)} %get-tuple-element.26), channel_id=1, source_target_pairs={{8,16},{12,20},{9,17},{13,21},{10,18},{14,22},{11,19},{15,23}} | collective-permute-start | bytes 393224 | tf_op jit(solution)/shard_map/ppermute | solution.py:252
  14.3 44.9 %collective-permute-start.11 = (bf16[1024,512]{1,0:T(8,128)(2,1)S(1)}, bf16[1024,512]{1,0:T(8,128)(2,1)}, u32[]{:S(2)}, u32[]{:S(2)}) collective-permute-start(bf16[1024,512]{1,0:T(8,128)(2,1)S(1)} %copy-done.6), channel_id=1, source_target_pairs={{16,0},{20,4},{24,8},{28,12},{17,1},{21,5},{25,9},{29,13},{18,2},{... | collective-permute-start | bytes 3145736 | tf_op jit(solution)/shard_map/ppermute | solution.py:235
  27.1 32.1 %collective-permute-start.9 = (bf16[256,512]{1,0:T(8,128)(2,1)}, bf16[256,512]{1,0:T(8,128)(2,1)}, u32[]{:S(2)}, u32[]{:S(2)}) collective-permute-start(bf16[256,512]{1,0:T(8,128)(2,1)} %slice.39), channel_id=1, source_target_pairs={{0,16},{4,20},{8,24},{12,28},{1,17},{5,21},{9,25},{13,29},{2,18},{... | collective-permute-start | bytes 786440 | tf_op jit(solution)/shard_map/ppermute | solution.py:237
  29.4 9.5 %copy-start.9 = (bf16[4,128,128]{2,1,0:T(8,128)(2,1)S(1)}, bf16[4,128,128]{2,1,0:T(8,128)(2,1)}, u32[]{:S(2)}) copy-start(bf16[4,128,128]{2,1,0:T(8,128)(2,1)} %copy-done.8) | copy-start | bytes 393220
  29.4 46.9 %collective-permute-start.10 = (bf16[768,512]{1,0:T(8,128)(2,1)}, bf16[768,512]{1,0:T(8,128)(2,1)}, u32[]{:S(2)}, u32[]{:S(2)}) collective-permute-start(bf16[768,512]{1,0:T(8,128)(2,1)} %slice.34), channel_id=1, source_target_pairs={{0,16},{4,20},{8,24},{12,28},{1,17},{5,21},{9,25},{13,29},{2,18},{... | collective-permute-start | bytes 2359304 | tf_op jit(solution)/shard_map/ppermute | solution.py:255
  30.8 5.9 %collective-permute-start.3 = (bf16[4,128,128]{2,1,0:T(8,128)(2,1)}, bf16[4,128,128]{2,1,0:T(8,128)(2,1)S(1)}, u32[]{:S(2)}, u32[]{:S(2)}) collective-permute-start(bf16[4,128,128]{2,1,0:T(8,128)(2,1)} %get-tuple-element.25), channel_id=1, source_target_pairs={{16,24},{20,28},{17,25},{21,29},{18,26},{22,30},{19,27},{23,31}} | collective-permute-start | bytes 393224 | tf_op jit(solution)/shard_map/ppermute | solution.py:252
  33.2 6.8 %copy-start.5 = (f32[1024]{0:T(1024)S(1)}, f32[1024]{0:T(1024)}, u32[]{:S(2)}) copy-start(f32[1024]{0:T(1024)} %param.8) | copy-start | bytes 12292
  33.2 5.7 %collective-permute-start.7 = (bf16[4,128,128]{2,1,0:T(8,128)(2,1)S(1)}, bf16[4,128,128]{2,1,0:T(8,128)(2,1)S(1)}, u32[]{:S(2)}, u32[]{:S(2)}) collective-permute-start(bf16[4,128,128]{2,1,0:T(8,128)(2,1)S(1)} %add_convert_fusion), channel_id=1, source_target_pairs={{16,24},{20,28},{17,25},{21,29},{18,26},{22,30},{19,27},{23,31}} | collective-permute-start | bytes 393224 | tf_op jit(solution)/shard_map/ppermute | solution.py:252
  40.7 37.3 %collective-permute-start.8 = (bf16[256,1024]{1,0:T(8,128)(2,1)S(1)}, bf16[256,1024]{1,0:T(8,128)(2,1)S(1)}, u32[]{:S(2)}, u32[]{:S(2)}) collective-permute-start(bf16[256,1024]{1,0:T(8,128)(2,1)S(1)} %shard_map.57.here_ref), channel_id=1, source_target_pairs={{0,8},{4,12},{8,0},{12,4},{16,24},{20,28},{24,16},{28,20},{1,9},{5... | collective-permute-start | bytes 1572872 | tf_op jit(solution)/shard_map/ppermute | solution.py:264
  40.8 40.8 %collective-permute-start.15 = (bf16[256,1024]{1,0:T(8,128)(2,1)S(1)}, bf16[256,1024]{1,0:T(8,128)(2,1)S(1)}, u32[]{:S(2)}, u32[]{:S(2)}) collective-permute-start(bf16[256,1024]{1,0:T(8,128)(2,1)S(1)} %shard_map.57.here_ref), channel_id=1, source_target_pairs={{0,4},{4,0},{8,12},{12,8},{16,20},{20,16},{24,28},{28,24},{1,5},{5... | collective-permute-start | bytes 1572872 | tf_op jit(solution)/shard_map/ppermute | solution.py:263
  59.2 29.6 %collective-permute-start.16 = (bf16[256,1024]{1,0:T(8,128)(2,1)S(1)}, bf16[256,1024]{1,0:T(8,128)(2,1)S(1)}, u32[]{:S(2)}, u32[]{:S(2)}) collective-permute-start(bf16[256,1024]{1,0:T(8,128)(2,1)S(1)} %shard_map.57.here_ref), channel_id=1, source_target_pairs={{0,12},{4,8},{8,4},{12,0},{16,28},{20,24},{24,20},{28,16},{1,13},{... | collective-permute-start | bytes 1572872 | tf_op jit(solution)/shard_map/ppermute | solution.py:265
  79.2 12.9 %collective-permute-start.12 = (bf16[2,256,512]{2,1,0:T(8,128)(2,1)S(1)}, bf16[2,256,512]{2,1,0:T(8,128)(2,1)S(1)}, u32[]{:S(2)}, u32[]{:S(2)}) collective-permute-start(bf16[2,256,512]{2,1,0:T(8,128)(2,1)S(1)} %get-tuple-element.18), channel_id=1, source_target_pairs={{0,1},{1,0},{2,3},{3,2},{4,5},{5,4},{6,7},{7,6},{8,9},{9,8},{10,11... | collective-permute-start | bytes 1572872 | tf_op jit(solution)/shard_map/ppermute | solution.py:219
  90.0 3.7 %collective-permute-start.17 = (bf16[2,256,512]{2,1,0:T(8,128)(2,1)S(1)}, bf16[2,256,512]{2,1,0:T(8,128)(2,1)S(1)}, u32[]{:S(2)}, u32[]{:S(2)}) collective-permute-start(bf16[2,256,512]{2,1,0:T(8,128)(2,1)S(1)} %get-tuple-element.20), channel_id=1, source_target_pairs={{0,1},{1,0},{2,3},{3,2},{4,5},{5,4},{6,7},{7,6},{8,9},{9,8},{10,11... | collective-permute-start | bytes 1572872 | tf_op jit(solution)/shard_map/ppermute | solution.py:219
  92.4 8.0 %collective-permute-start.13 = (bf16[256,512]{1,0:T(8,128)(2,1)S(1)}, bf16[256,512]{1,0:T(8,128)(2,1)S(1)}, u32[]{:S(2)}, u32[]{:S(2)}) collective-permute-start(bf16[256,512]{1,0:T(8,128)(2,1)S(1)} %fusion.8), channel_id=1, source_target_pairs={{0,2},{1,3},{2,0},{3,1},{4,6},{5,7},{6,4},{7,5},{8,10},{9,11},{10,... | collective-permute-start | bytes 786440 | tf_op jit(solution)/shard_map/ppermute | solution.py:219
  93.9 12.0 %collective-permute-start.18 = (bf16[256,512]{1,0:T(8,128)(2,1)S(1)}, bf16[256,512]{1,0:T(8,128)(2,1)S(1)}, u32[]{:S(2)}, u32[]{:S(2)}) collective-permute-start(bf16[256,512]{1,0:T(8,128)(2,1)S(1)} %fusion.9), channel_id=1, source_target_pairs={{0,2},{1,3},{2,0},{3,1},{4,6},{5,7},{6,4},{7,5},{8,10},{9,11},{10,... | collective-permute-start | bytes 786440 | tf_op jit(solution)/shard_map/ppermute | solution.py:219
  100.5 5.9 %collective-permute-start.14 = (bf16[256,512]{1,0:T(8,128)(2,1)S(1)}, bf16[256,512]{1,0:T(8,128)(2,1)S(1)}, u32[]{:S(2)}, u32[]{:S(2)}) collective-permute-start(bf16[256,512]{1,0:T(8,128)(2,1)S(1)} %fusion.1), channel_id=1, source_target_pairs={{1,8},{3,10},{5,12},{7,14},{8,1},{10,3},{12,5},{14,7},{17,24},{19,... | collective-permute-start | bytes 786440 | tf_op jit(solution)/shard_map/ppermute | solution.py:219
  106.1 8.1 %collective-permute-start.19 = (bf16[256,512]{1,0:T(8,128)(2,1)S(1)}, bf16[256,512]{1,0:T(8,128)(2,1)S(1)}, u32[]{:S(2)}, u32[]{:S(2)}) collective-permute-start(bf16[256,512]{1,0:T(8,128)(2,1)S(1)} %fusion), channel_id=1, source_target_pairs={{0,4},{1,12},{2,6},{3,14},{4,0},{5,8},{6,2},{7,10},{8,5},{9,13},{1... | collective-permute-start | bytes 786440 | tf_op jit(solution)/shard_map/ppermute | solution.py:219

commit v4 on v3

--- a/solution.py
+++ b/solution.py
@@ -231,12 +231,9 @@
         within_kernel, jax.ShapeDtypeStruct((rows, features), F32), 4 * size * BLOCK, 10 * size
     )(queries, key_vectors, value_vectors)
 
-    cut = out_weight.shape[0] // 4
-    down = lax.ppermute(out_weight, "seq", [(s, s - 4) for s in range(4, 8)])
-    up_pairs = [(s, s + 4) for s in range(4)]
-    up_first = lax.ppermute(out_weight[:cut], "seq", up_pairs)
-
-    parts = 2
+    far_weight = lax.ppermute(out_weight, "seq", seq_swap(4))
+
+    parts = 1
     step = heads // parts
     totals, firsts, before = [], [], []
     for part in range(parts):
@@ -250,9 +247,6 @@
         for part in range(parts):
             onward = (before[part] + totals[part]).astype(BF16)
             before[part] += lax.ppermute(onward, "seq", pairs).astype(F32)
-        if plane == 1:
-            rest, before[0] = lax.optimization_barrier((out_weight[cut:], before[0]))
-    up_rest = lax.ppermute(rest, "seq", up_pairs)
     state_in = jnp.concatenate(
         [(before[part] + firsts[part]).astype(BF16) for part in range(parts)], axis=0
     )
@@ -264,8 +258,8 @@
     from_z = lax.ppermute(attended, "seq", seq_swap(2))
     from_both = lax.ppermute(attended, "seq", seq_swap(3))
 
-    low = jnp.where(lower, out_weight, jnp.concatenate([up_first, up_rest], axis=0))
-    high = jnp.where(lower, down, out_weight)
+    low = jnp.where(lower, out_weight, far_weight)
+    high = jnp.where(lower, far_weight, out_weight)
     pick = home_core.astype(jnp.int32)[None]
 
     def reduced(here, there):

time: 116 us -> 132 us (1.14)
  the two profiles are of different devices: /device:TPU:27 before, /device:TPU:18 now
where the time goes in v4:
time: 132 us
  waiting for transfers between devices  99.4 us (75%)
  starting transfers between devices  20.2 us (15%)
  other arithmetic  5.05 us (4%)
  Pallas kernels  4.57 us (3%)
  local copies, waits for them, and re-layouts  2.11 us (2%)
    ppermute x3, waiting for transfers between devices, pairs_body(): before[part] += lax.ppermute(onward, 'seq', pairs).astype(F32)  50.5 us
    ppermute x6, waiting for transfers between devices, move(): return lax.ppermute(value, both, pairs)  20.8 us
    ppermute x1, waiting for transfers between devices, pairs_body(): from_both = lax.ppermute(attended, 'seq', seq_swap(3))  10.3 us
    ppermute x1, waiting for transfers between devices, pairs_body(): from_z = lax.ppermute(attended, 'seq', seq_swap(2))  9.77 us
    ppermute x1, starting transfers between devices, pairs_body(): far_weight = lax.ppermute(out_weight, 'seq', seq_swap(4))  7.72 us
    ppermute x1, waiting for transfers between devices, pairs_body(): mate = lax.ppermute(narrow[mine], 'seq', seq_swap(1)).astype(F32)  6.52 us
    ppermute x3, starting transfers between devices, pairs_body(): before[part] += lax.ppermute(onward, 'seq', pairs).astype(F32)  4.21 us
  transfers between devices with their start and end apart: 14, of which 10 were waited for; matrix products, arithmetic and copies ran while one was open for 3% of the time, Pallas kernels for 3%

profile of v4, /device:TPU:18, one launch (start us, length us, event | category | flops | bytes accessed | tf_op | source)
XLA Modules:
  0.0 131.6 jit_solution(464278001932778886)
XLA Ops:
  0.0 0.0 copy-start
  0.0 1.0 copy-done
  1.0 0.0 copy-start.2
  1.0 1.0 copy-done.2
  2.1 0.4 shard_map.56
  2.4 1.6 %collective-permute-start = (bf16[8,128,128]{2,1,0:T(8,128)(2,1)S(1)}, bf16[8,128,128]{2,1,0:T(8,128)(2,1)S(1)}, u32[]{:S(2)}, u32[]{:S(2)}) collective-permute-start(bf16[8,128,128]{2,1,0:T(8,128)(2,1)S(1)} %get-tuple-element.12), channel_id=1, source_target_pairs={{0,4},{4,0},{8,12},{12,8},{16,20},{20,16},{24,28},{28,24},{1,5},{5... | collective-permute-start | bytes 786440 | tf_op jit(solution)/shard_map/ppermute | solution.py:241
  4.0 6.5 %collective-permute-done = bf16[8,128,128]{2,1,0:T(8,128)(2,1)S(1)} collective-permute-done((bf16[8,128,128]{2,1,0:T(8,128)(2,1)S(1)}, bf16[8,128,128]{2,1,0:T(8,128)(2,1)S(1)}, u32[]{:S(2)}, u32[]{:S(2)}) %collective-permute-start) | collective-permute-done | bytes 262176 | tf_op jit(solution)/shard_map/ppermute | solution.py:241
  10.6 0.0 copy-start.6
  10.6 0.1 fusion.7
  10.6 0.8 collective-permute-start.1
  11.4 0.0 collective-permute-done.1
  11.4 0.1 fusion.2
  11.5 0.0 copy-start.1
  11.6 0.0 copy-start.3
  11.6 0.0 copy-start.4
  11.6 1.4 %collective-permute-start.2 = (bf16[8,128,128]{2,1,0:T(8,128)(2,1)S(1)}, bf16[8,128,128]{2,1,0:T(8,128)(2,1)S(1)}, u32[]{:S(2)}, u32[]{:S(2)}) collective-permute-start(bf16[8,128,128]{2,1,0:T(8,128)(2,1)S(1)} %fusion.2), channel_id=1, source_target_pairs={{8,16},{12,20},{9,17},{13,21},{10,18},{14,22},{11,19},{15,23}} | collective-permute-start | bytes 786440 | tf_op jit(solution)/shard_map/ppermute | solution.py:249
  13.0 0.0 copy-done.6
  13.0 7.7 %collective-permute-start.5 = (bf16[1024,512]{1,0:T(8,128)(2,1)S(1)}, bf16[1024,512]{1,0:T(8,128)(2,1)}, u32[]{:S(2)}, u32[]{:S(2)}) collective-permute-start(bf16[1024,512]{1,0:T(8,128)(2,1)S(1)} %copy-done.6), channel_id=1, source_target_pairs={{0,16},{4,20},{8,24},{12,28},{16,0},{20,4},{24,8},{28,12},{1,17},{... | collective-permute-start | bytes 3145736 | tf_op jit(solution)/shard_map/ppermute | solution.py:234
  20.7 27.1 %collective-permute-done.2 = bf16[8,128,128]{2,1,0:T(8,128)(2,1)S(1)} collective-permute-done((bf16[8,128,128]{2,1,0:T(8,128)(2,1)S(1)}, bf16[8,128,128]{2,1,0:T(8,128)(2,1)S(1)}, u32[]{:S(2)}, u32[]{:S(2)}) %collective-permute-start.2) | collective-permute-done | bytes 262176 | tf_op jit(solution)/shard_map/ppermute | solution.py:249
  47.9 0.8 add_convert_fusion
  48.7 2.0 %collective-permute-start.3 = (bf16[8,128,128]{2,1,0:T(8,128)(2,1)}, bf16[8,128,128]{2,1,0:T(8,128)(2,1)}, u32[]{:S(2)}, u32[]{:S(2)}) collective-permute-start(bf16[8,128,128]{2,1,0:T(8,128)(2,1)} %add_convert_fusion), channel_id=1, source_target_pairs={{16,24},{20,28},{17,25},{21,29},{18,26},{22,30},{19,27},{23,31}} | collective-permute-start | bytes 786440 | tf_op jit(solution)/shard_map/ppermute | solution.py:249
  50.7 0.0 copy-done.1
  50.7 0.0 copy-done.3
  50.7 0.0 copy-done.4
  50.7 0.9 shard_map.55.within_ref
  51.6 23.3 %collective-permute-done.3 = bf16[8,128,128]{2,1,0:T(8,128)(2,1)} collective-permute-done((bf16[8,128,128]{2,1,0:T(8,128)(2,1)}, bf16[8,128,128]{2,1,0:T(8,128)(2,1)}, u32[]{:S(2)}, u32[]{:S(2)}) %collective-permute-start.3) | collective-permute-done | bytes 262176 | tf_op jit(solution)/shard_map/ppermute | solution.py:249
  75.0 0.0 copy-start.5
  75.0 1.1 fusion.1.state_ref
  76.1 0.0 copy-done.5
  76.1 0.7 shard_map.57.here_ref
  76.8 2.5 %collective-permute-start.4 = (bf16[256,1024]{1,0:T(8,128)(2,1)S(1)}, bf16[256,1024]{1,0:T(8,128)(2,1)S(1)}, u32[]{:S(2)}, u32[]{:S(2)}) collective-permute-start(bf16[256,1024]{1,0:T(8,128)(2,1)S(1)} %shard_map.57.here_ref), channel_id=1, source_target_pairs={{0,8},{4,12},{8,0},{12,4},{16,24},{20,28},{24,16},{28,20},{1,9},{5... | collective-permute-start | bytes 1572872 | tf_op jit(solution)/shard_map/ppermute | solution.py:258
  79.4 1.1 collective-permute-start.10
  80.5 0.5 collective-permute-start.9
  81.0 0.0 collective-permute-done.5
  81.0 1.4 %broadcast_select_fusion = (bf16[1024,512]{1,0:T(8,128)(2,1)S(1)}, bf16[1024,512]{1,0:T(8,128)(2,1)S(1)}) fusion(bf16[1024,512]{1,0:T(8,128)(2,1)} %collective-permute-done.5, bf16[1024,512]{1,0:T(8,128)(2,1)S(1)} %copy-done.6, pred[]{:T(512)S(6)} %lt.20), kind=kLoop, calls=%fused_computation.2 | loop fusion | flops 1048576 | bytes 4194305 | tf_op jit(solution)/shard_map/jit(_where)/select_n | solution.py:262
  82.3 9.8 %collective-permute-done.4.there_ref = bf16[256,1024]{1,0:T(8,128)(2,1)S(1)} collective-permute-done((bf16[256,1024]{1,0:T(8,128)(2,1)S(1)}, bf16[256,1024]{1,0:T(8,128)(2,1)S(1)}, u32[]{:S(2)}, u32[]{:S(2)}) %collective-permute-start.4) | collective-permute-done | bytes 524320 | tf_op jit(solution)/shard_map/ppermute | solution.py:258
  92.1 1.3 shard_map.58
  93.4 0.1 collective-permute-start.6
  93.5 10.3 %collective-permute-done.10.there_ref = bf16[256,1024]{1,0:T(8,128)(2,1)S(1)} collective-permute-done((bf16[256,1024]{1,0:T(8,128)(2,1)S(1)}, bf16[256,1024]{1,0:T(8,128)(2,1)S(1)}, u32[]{:S(2)}, u32[]{:S(2)}) %collective-permute-start.10) | collective-permute-done | bytes 524320 | tf_op jit(solution)/shard_map/ppermute | solution.py:259
  103.8 1.5 %collective-permute-done.9.here_ref = bf16[256,1024]{1,0:T(8,128)(2,1)S(1)} collective-permute-done((bf16[256,1024]{1,0:T(8,128)(2,1)S(1)}, bf16[256,1024]{1,0:T(8,128)(2,1)S(1)}, u32[]{:S(2)}, u32[]{:S(2)}) %collective-permute-start.9) | collective-permute-done | bytes 524320 | tf_op jit(solution)/shard_map/ppermute | solution.py:257
  105.3 1.3 shard_map.59
  106.6 0.1 collective-permute-start.11
  106.7 0.0 collective-permute-done.6
  106.7 0.2 convert_add_fusion.1
  106.8 0.1 fusion.5
  106.9 0.6 collective-permute-start.7
  107.5 1.1 collective-permute-done.11
  108.5 0.2 convert_add_fusion
  108.7 0.1 fusion.6
  108.8 0.6 collective-permute-start.12
  109.3 6.7 %collective-permute-done.7 = bf16[256,512]{1,0:T(8,128)(2,1)S(1)} collective-permute-done((bf16[256,512]{1,0:T(8,128)(2,1)S(1)}, bf16[256,512]{1,0:T(8,128)(2,1)S(1)}, u32[]{:S(2)}, u32[]{:S(2)}) %collective-permute-start.7) | collective-permute-done | bytes 262176 | tf_op jit(solution)/shard_map/ppermute | solution.py:219
  116.1 0.1 fusion.4
  116.2 0.7 collective-permute-start.8
  116.9 4.4 %collective-permute-done.12 = bf16[256,512]{1,0:T(8,128)(2,1)S(1)} collective-permute-done((bf16[256,512]{1,0:T(8,128)(2,1)S(1)}, bf16[256,512]{1,0:T(8,128)(2,1)S(1)}, u32[]{:S(2)}, u32[]{:S(2)}) %collective-permute-start.12) | collective-permute-done | bytes 262176 | tf_op jit(solution)/shard_map/ppermute | solution.py:219
  121.3 0.1 fusion.3
  121.4 0.6 collective-permute-start.13
  122.0 0.0 collective-permute-done.8
  122.0 8.7 %collective-permute-done.13 = bf16[256,512]{1,0:T(8,128)(2,1)S(1)} collective-permute-done((bf16[256,512]{1,0:T(8,128)(2,1)S(1)}, bf16[256,512]{1,0:T(8,128)(2,1)S(1)}, u32[]{:S(2)}, u32[]{:S(2)}) %collective-permute-start.13) | collective-permute-done | bytes 262176 | tf_op jit(solution)/shard_map/ppermute | solution.py:219
  130.7 0.9 pad_maximum_fusion
  (1 shorter events, 0.0 us)
Async XLA Ops:
  0.0 1.0 copy-start
  1.0 1.0 copy-start.2
  2.4 8.1 %collective-permute-start = (bf16[8,128,128]{2,1,0:T(8,128)(2,1)S(1)}, bf16[8,128,128]{2,1,0:T(8,128)(2,1)S(1)}, u32[]{:S(2)}, u32[]{:S(2)}) collective-permute-start(bf16[8,128,128]{2,1,0:T(8,128)(2,1)S(1)} %get-tuple-element.12), channel_id=1, source_target_pairs={{0,4},{4,0},{8,12},{12,8},{16,20},{20,16},{24,28},{28,24},{1,5},{5... | collective-permute-start | bytes 786440 | tf_op jit(solution)/shard_map/ppermute | solution.py:241
  10.6 2.5 %copy-start.6 = (bf16[1024,512]{1,0:T(8,128)(2,1)S(1)}, bf16[1024,512]{1,0:T(8,128)(2,1)}, u32[]{:S(2)}) copy-start(bf16[1024,512]{1,0:T(8,128)(2,1)} %param.9) | copy-start | bytes 3145732
  10.6 0.8 collective-permute-start.1
  11.5 39.2 %copy-start.1 = (bf16[256,1024]{1,0:T(8,128)(2,1)S(1)}, bf16[256,1024]{1,0:T(8,128)(2,1)}, u32[]{:S(2)}) copy-start(bf16[256,1024]{1,0:T(8,128)(2,1)} %k_ref.3) | copy-start | bytes 1572868
  11.6 39.1 %copy-start.3 = (bf16[256,1024]{1,0:T(8,128)(2,1)S(1)}, bf16[256,1024]{1,0:T(8,128)(2,1)}, u32[]{:S(2)}) copy-start(bf16[256,1024]{1,0:T(8,128)(2,1)} %v_ref.3) | copy-start | bytes 1572868
  11.6 39.1 %copy-start.4 = (bf16[256,1024]{1,0:T(8,128)(2,1)S(1)}, bf16[256,1024]{1,0:T(8,128)(2,1)}, u32[]{:S(2)}) copy-start(bf16[256,1024]{1,0:T(8,128)(2,1)} %q_ref.3) | copy-start | bytes 1572868
  11.6 36.3 %collective-permute-start.2 = (bf16[8,128,128]{2,1,0:T(8,128)(2,1)S(1)}, bf16[8,128,128]{2,1,0:T(8,128)(2,1)S(1)}, u32[]{:S(2)}, u32[]{:S(2)}) collective-permute-start(bf16[8,128,128]{2,1,0:T(8,128)(2,1)S(1)} %fusion.2), channel_id=1, source_target_pairs={{8,16},{12,20},{9,17},{13,21},{10,18},{14,22},{11,19},{15,23}} | collective-permute-start | bytes 786440 | tf_op jit(solution)/shard_map/ppermute | solution.py:249
  13.0 68.0 %collective-permute-start.5 = (bf16[1024,512]{1,0:T(8,128)(2,1)S(1)}, bf16[1024,512]{1,0:T(8,128)(2,1)}, u32[]{:S(2)}, u32[]{:S(2)}) collective-permute-start(bf16[1024,512]{1,0:T(8,128)(2,1)S(1)} %copy-done.6), channel_id=1, source_target_pairs={{0,16},{4,20},{8,24},{12,28},{16,0},{20,4},{24,8},{28,12},{1,17},{... | collective-permute-start | bytes 3145736 | tf_op jit(solution)/shard_map/ppermute | solution.py:234
  48.7 26.3 %collective-permute-start.3 = (bf16[8,128,128]{2,1,0:T(8,128)(2,1)}, bf16[8,128,128]{2,1,0:T(8,128)(2,1)}, u32[]{:S(2)}, u32[]{:S(2)}) collective-permute-start(bf16[8,128,128]{2,1,0:T(8,128)(2,1)} %add_convert_fusion), channel_id=1, source_target_pairs={{16,24},{20,28},{17,25},{21,29},{18,26},{22,30},{19,27},{23,31}} | collective-permute-start | bytes 786440 | tf_op jit(solution)/shard_map/ppermute | solution.py:249
  75.0 1.1 copy-start.5
  76.8 15.3 %collective-permute-start.4 = (bf16[256,1024]{1,0:T(8,128)(2,1)S(1)}, bf16[256,1024]{1,0:T(8,128)(2,1)S(1)}, u32[]{:S(2)}, u32[]{:S(2)}) collective-permute-start(bf16[256,1024]{1,0:T(8,128)(2,1)S(1)} %shard_map.57.here_ref), channel_id=1, source_target_pairs={{0,8},{4,12},{8,0},{12,4},{16,24},{20,28},{24,16},{28,20},{1,9},{5... | collective-permute-start | bytes 1572872 | tf_op jit(solution)/shard_map/ppermute | solution.py:258
  79.4 24.4 %collective-permute-start.10 = (bf16[256,1024]{1,0:T(8,128)(2,1)S(1)}, bf16[256,1024]{1,0:T(8,128)(2,1)S(1)}, u32[]{:S(2)}, u32[]{:S(2)}) collective-permute-start(bf16[256,1024]{1,0:T(8,128)(2,1)S(1)} %shard_map.57.here_ref), channel_id=1, source_target_pairs={{0,12},{4,8},{8,4},{12,0},{16,28},{20,24},{24,20},{28,16},{1,13},{... | collective-permute-start | bytes 1572872 | tf_op jit(solution)/shard_map/ppermute | solution.py:259
  80.5 24.8 %collective-permute-start.9 = (bf16[256,1024]{1,0:T(8,128)(2,1)S(1)}, bf16[256,1024]{1,0:T(8,128)(2,1)S(1)}, u32[]{:S(2)}, u32[]{:S(2)}) collective-permute-start(bf16[256,1024]{1,0:T(8,128)(2,1)S(1)} %shard_map.57.here_ref), channel_id=1, source_target_pairs={{0,4},{4,0},{8,12},{12,8},{16,20},{20,16},{24,28},{28,24},{1,5},{5... | collective-permute-start | bytes 1572872 | tf_op jit(solution)/shard_map/ppermute | solution.py:257
  93.4 13.2 %collective-permute-start.6 = (bf16[2,256,512]{2,1,0:T(8,128)(2,1)S(1)}, bf16[2,256,512]{2,1,0:T(8,128)(2,1)S(1)}, u32[]{:S(2)}, u32[]{:S(2)}) collective-permute-start(bf16[2,256,512]{2,1,0:T(8,128)(2,1)S(1)} %get-tuple-element.14), channel_id=1, source_target_pairs={{0,1},{1,0},{2,3},{3,2},{4,5},{5,4},{6,7},{7,6},{8,9},{9,8},{10,11... | collective-permute-start | bytes 1572872 | tf_op jit(solution)/shard_map/ppermute | solution.py:219
  106.6 2.0 %collective-permute-start.11 = (bf16[2,256,512]{2,1,0:T(8,128)(2,1)S(1)}, bf16[2,256,512]{2,1,0:T(8,128)(2,1)S(1)}, u32[]{:S(2)}, u32[]{:S(2)}) collective-permute-start(bf16[2,256,512]{2,1,0:T(8,128)(2,1)S(1)} %get-tuple-element.16), channel_id=1, source_target_pairs={{0,1},{1,0},{2,3},{3,2},{4,5},{5,4},{6,7},{7,6},{8,9},{9,8},{10,11... | collective-permute-start | bytes 1572872 | tf_op jit(solution)/shard_map/ppermute | solution.py:219
  106.9 9.2 %collective-permute-start.7 = (bf16[256,512]{1,0:T(8,128)(2,1)S(1)}, bf16[256,512]{1,0:T(8,128)(2,1)S(1)}, u32[]{:S(2)}, u32[]{:S(2)}) collective-permute-start(bf16[256,512]{1,0:T(8,128)(2,1)S(1)} %fusion.5), channel_id=1, source_target_pairs={{0,2},{1,3},{2,0},{3,1},{4,6},{5,7},{6,4},{7,5},{8,10},{9,11},{10,... | collective-permute-start | bytes 786440 | tf_op jit(solution)/shard_map/ppermute | solution.py:219
  108.8 12.5 %collective-permute-start.12 = (bf16[256,512]{1,0:T(8,128)(2,1)S(1)}, bf16[256,512]{1,0:T(8,128)(2,1)S(1)}, u32[]{:S(2)}, u32[]{:S(2)}) collective-permute-start(bf16[256,512]{1,0:T(8,128)(2,1)S(1)} %fusion.6), channel_id=1, source_target_pairs={{0,2},{1,3},{2,0},{3,1},{4,6},{5,7},{6,4},{7,5},{8,10},{9,11},{10,... | collective-permute-start | bytes 786440 | tf_op jit(solution)/shard_map/ppermute | solution.py:219
  116.2 5.8 %collective-permute-start.8 = (bf16[256,512]{1,0:T(8,128)(2,1)S(1)}, bf16[256,512]{1,0:T(8,128)(2,1)S(1)}, u32[]{:S(2)}, u32[]{:S(2)}) collective-permute-start(bf16[256,512]{1,0:T(8,128)(2,1)S(1)} %fusion.4), channel_id=1, source_target_pairs={{1,8},{3,10},{5,12},{7,14},{8,1},{10,3},{12,5},{14,7},{17,24},{19,... | collective-permute-start | bytes 786440 | tf_op jit(solution)/shard_map/ppermute | solution.py:219
  121.4 9.2 %collective-permute-start.13 = (bf16[256,512]{1,0:T(8,128)(2,1)S(1)}, bf16[256,512]{1,0:T(8,128)(2,1)S(1)}, u32[]{:S(2)}, u32[]{:S(2)}) collective-permute-start(bf16[256,512]{1,0:T(8,128)(2,1)S(1)} %fusion.3), channel_id=1, source_target_pairs={{0,4},{1,12},{2,6},{3,14},{4,0},{5,8},{6,2},{7,10},{8,5},{9,13},{1... | collective-permute-start | bytes 786440 | tf_op jit(solution)/shard_map/ppermute | solution.py:219

commit v5 on v2

--- a/solution.py
+++ b/solution.py
@@ -185,13 +185,114 @@
     return body
 
 
+def project_kernel(pick_ref, tokens_ref, near_a, near_b, far_a, far_b, keep_ref, send_ref):
+    def multiply(out_ref, weights):
+        for half, weight_ref in enumerate(weights):
+            out_ref[half] = jnp.dot(
+                tokens_ref[...], weight_ref[...], preferred_element_type=F32
+            ).astype(BF16)
+
+    @pl.when(pick_ref[0] == 1)
+    def _():
+        multiply(keep_ref, (near_a, near_b))
+        multiply(send_ref, (far_a, far_b))
+
+    @pl.when(pick_ref[0] != 1)
+    def _():
+        multiply(keep_ref, (far_a, far_b))
+        multiply(send_ref, (near_a, near_b))
+
+
+def pairs_body(queries, key_vectors, value_vectors, norm_gain, out_weight):
+    rows, features = queries.shape
+    heads = features // HD
+    size = rows * features
+    half_cols = out_weight.shape[1]
+    both = ("seq", "head")
+    place, group = lax.axis_index("seq"), lax.axis_index("head")
+    z, y, x, core = place // 2, place % 2, group // 2, group % 2
+    devices = [(s // 2, s % 2, h // 2, h % 2) for s in range(8) for h in range(4)]
+
+    def at(z, y, x, c):
+        return (z * 2 + y) * 4 + x * 2 + c
+
+    def swap(value, mask):
+        return lax.ppermute(value, "seq", [(s, s ^ mask) for s in range(8)])
+
+    def move(value, place_of, chosen=lambda z, y, x, c: True):
+        pairs = [(at(*d), at(*place_of(*d))) for d in devices if chosen(*d)]
+        return lax.ppermute(value, both, pairs)
+
+    wide, narrow = call(
+        state_kernel,
+        (
+            jax.ShapeDtypeStruct((heads, HD, HD), F32),
+            jax.ShapeDtypeStruct((heads, HD, HD), BF16),
+        ),
+        2 * size * HD,
+        4 * size + 6 * heads * HD * HD,
+    )(key_vectors, value_vectors)
+    within = call(
+        within_kernel, jax.ShapeDtypeStruct((rows, features), F32), 4 * size * BLOCK, 10 * size
+    )(queries, key_vectors, value_vectors)
+
+    near_mate = swap(out_weight, 1)
+    far_own = swap(out_weight, 2)
+
+    mate = swap(narrow, 1).astype(F32)
+    total = wide + mate
+    before = jnp.zeros_like(wide)
+    for plane in range(3):
+        pairs = [(2 * plane + i, 2 * plane + 2 + i) for i in range(2)]
+        onward = (before + total).astype(BF16)
+        before += lax.ppermute(onward, "seq", pairs).astype(F32)
+    state_in = (before + jnp.where(y == 1, mate, 0.0)).astype(BF16)
+    attended = call(
+        attend_kernel, jax.ShapeDtypeStruct((rows, features), BF16), 2 * size * HD, 8 * size
+    )(queries, within, state_in, norm_gain[None])
+
+    remote = swap(attended, 4)
+    far_mate = swap(far_own, 1)
+    pick = (core == z % 2).astype(jnp.int32)[None]
+
+    def projected(tokens):
+        tile = jax.ShapeDtypeStruct((2, rows, half_cols), BF16)
+        vmem = pl.BlockSpec(memory_space=pltpu.VMEM)
+        keep, send = pl.pallas_call(
+            project_kernel,
+            out_shape=(tile, tile),
+            in_specs=[pl.BlockSpec(memory_space=pltpu.SMEM)] + [vmem] * 5,
+            out_specs=(vmem, vmem),
+            compiler_params=pltpu.CompilerParams(vmem_limit_bytes=24 * 1024 * 1024),
+            cost_estimate=pl.CostEstimate(
+                flops=8 * size * half_cols, bytes_accessed=12 * size, transcendentals=0
+            ),
+        )(pick, tokens, out_weight, near_mate, far_own, far_mate)
+        got = move(send, lambda z, y, x, c: (z, y, x, 1 - c))
+        return keep.astype(F32) + got.astype(F32)
+
+    at_home = lambda z, y, x, c: x == z // 2
+    away = lambda z, y, x, c: x != z // 2
+    own = projected(attended)
+    from_x = move(own.astype(BF16), lambda z, y, x, c: (z, y, 1 - x, c), away)
+    other = projected(remote).astype(BF16)
+    straight = move(other, lambda z, y, x, c: (z ^ 2, y, x, c), at_home)
+    across = move(other, lambda z, y, x, c: (z ^ 2, y, 1 - x, c), away)
+    result = jnp.where(x == z // 2, own, 0.0) + from_x.astype(F32)
+    result = (result + straight.astype(F32) + across.astype(F32)).astype(BF16)
+    first = jnp.where(y == 0, result[0], result[1])
+    return jnp.concatenate([first, jnp.where(y == 0, result[1], result[0])], axis=1)
+
+
 def solution(mesh):
     seq_count, head_groups = mesh.shape["seq"], mesh.shape["head"]
 
     def run(queries, key_vectors, value_vectors, norm_gain, out_weight):
         one_block = queries.shape[0] == BLOCK * seq_count
         body = general_body
-        if one_block and head_groups == 4 and seq_count % head_groups == 0:
+        if one_block and head_groups == 4 and seq_count == 8:
+            body = pairs_body
+        elif one_block and head_groups == 4 and seq_count % head_groups == 0:
             body = planes_body(seq_count, head_groups)
         return jax.shard_map(
             body,

time: 136 us -> 128 us (0.941)
  the two profiles are of different devices: /device:TPU:17 before, /device:TPU:3 now
where the time goes in v5:
time: 128 us
  waiting for transfers between devices  72.3 us (56%)
  starting transfers between devices  37 us (29%)
  Pallas kernels  8.06 us (6%)
  local copies, waits for them, and re-layouts  5.39 us (4%)
  other arithmetic  4.68 us (4%)
    ppermute x5, waiting for transfers between devices, swap(): return lax.ppermute(value, 'seq', [(s, s ^ mask) for s in range(8)])  32.4 us
    ppermute x5, waiting for transfers between devices, move(): return lax.ppermute(value, both, pairs)  20.7 us
    ppermute x3, waiting for transfers between devices, pairs_body(): before += lax.ppermute(onward, 'seq', pairs).astype(F32)  19.2 us
    ppermute x5, starting transfers between devices, move(): return lax.ppermute(value, both, pairs)  18.3 us
    ppermute x5, starting transfers between devices, swap(): return lax.ppermute(value, 'seq', [(s, s ^ mask) for s in range(8)])  13.4 us
    unnamed x24, local copies, waits for them, and re-layouts  5.39 us
    pallas_call x2, Pallas kernels, projected(): pl.pallas_call(project_kernel, out_shape=(tile, tile), in_specs=[pl.Block...  5.26 us
    ppermute x3, starting transfers between devices, pairs_body(): before += lax.ppermute(onward, 'seq', pairs).astype(F32)  5.25 us
  transfers between devices with their start and end apart: 13, of which 7 were waited for; matrix products, arithmetic and copies ran while one was open for 2% of the time, Pallas kernels for 4%

profile of v5, /device:TPU:3, one launch (start us, length us, event | category | flops | bytes accessed | tf_op | source)
XLA Modules:
  0.0 127.6 jit_solution(4562423292823686783)
XLA Ops:
  0.0 0.0 copy-start
  0.0 0.0 copy-start.1
  0.0 1.1 copy-done.1
  1.1 0.0 copy-start.3
  1.1 1.0 copy-done.3
  2.2 0.4 shard_map.56
  2.5 1.3 %collective-permute-start = (bf16[8,128,128]{2,1,0:T(8,128)(2,1)S(1)}, bf16[8,128,128]{2,1,0:T(8,128)(2,1)S(1)}, u32[]{:S(2)}, u32[]{:S(2)}) collective-permute-start(bf16[8,128,128]{2,1,0:T(8,128)(2,1)S(1)} %get-tuple-element.12), channel_id=1, source_target_pairs={{0,4},{4,0},{8,12},{12,8},{16,20},{20,16},{24,28},{28,24},{1,5},{5... | collective-permute-start | bytes 786440 | tf_op jit(solution)/shard_map/ppermute | solution.py:220
  3.8 0.0 copy-done
  3.8 1.3 %collective-permute-start.5 = (bf16[1024,512]{1,0:T(8,128)(2,1)S(1)}, bf16[1024,512]{1,0:T(8,128)(2,1)S(1)}, u32[]{:S(2)}, u32[]{:S(2)}) collective-permute-start(bf16[1024,512]{1,0:T(8,128)(2,1)S(1)} %copy-done), channel_id=1, source_target_pairs={{0,8},{4,12},{8,0},{12,4},{16,24},{20,28},{24,16},{28,20},{1,9},{5... | collective-permute-start | bytes 3145736 | tf_op jit(solution)/shard_map/ppermute | solution.py:220
  5.1 4.6 %collective-permute-done = bf16[8,128,128]{2,1,0:T(8,128)(2,1)S(1)} collective-permute-done((bf16[8,128,128]{2,1,0:T(8,128)(2,1)S(1)}, bf16[8,128,128]{2,1,0:T(8,128)(2,1)S(1)}, u32[]{:S(2)}, u32[]{:S(2)}) %collective-permute-start) | collective-permute-done | bytes 262176 | tf_op jit(solution)/shard_map/ppermute | solution.py:220
  9.8 0.1 fusion.4
  9.8 3.2 %collective-permute-start.1 = (bf16[8,128,128]{2,1,0:T(8,128)(2,1)S(1)}, bf16[8,128,128]{2,1,0:T(8,128)(2,1)S(1)}, u32[]{:S(2)}, u32[]{:S(2)}) collective-permute-start(bf16[8,128,128]{2,1,0:T(8,128)(2,1)S(1)} %fusion.4), channel_id=1, source_target_pairs={{0,8},{4,12},{1,9},{5,13},{2,10},{6,14},{3,11},{7,15}} | collective-permute-start | bytes 786440 | tf_op jit(solution)/shard_map/ppermute | solution.py:248
  13.1 19.2 %collective-permute-done.1 = bf16[8,128,128]{2,1,0:T(8,128)(2,1)S(1)} collective-permute-done((bf16[8,128,128]{2,1,0:T(8,128)(2,1)S(1)}, bf16[8,128,128]{2,1,0:T(8,128)(2,1)S(1)}, u32[]{:S(2)}, u32[]{:S(2)}) %collective-permute-start.1) | collective-permute-done | bytes 262176 | tf_op jit(solution)/shard_map/ppermute | solution.py:248
  32.3 0.0 copy-start.8
  32.3 0.1 fusion.3
  32.4 0.7 collective-permute-start.2
  33.0 0.0 collective-permute-done.2
  33.1 0.0 copy-done.8
  33.1 0.0 copy-start.10
  33.1 0.8 add_convert_fusion.2
  33.9 0.0 copy-done.10
  33.9 1.4 %collective-permute-start.3 = (bf16[8,128,128]{2,1,0:T(8,128)(2,1)}, bf16[8,128,128]{2,1,0:T(8,128)(2,1)}, u32[]{:S(2)}, u32[]{:S(2)}) collective-permute-start(bf16[8,128,128]{2,1,0:T(8,128)(2,1)} %add_convert_fusion.2), channel_id=1, source_target_pairs={{16,24},{20,28},{17,25},{21,29},{18,26},{22,30},{19,27},{23,31}} | collective-permute-start | bytes 786440 | tf_op jit(solution)/shard_map/ppermute | solution.py:248
  35.3 0.2 collective-permute-start.4
  35.5 0.0 collective-permute-done.5.far_a
  35.5 1.2 collective-permute-start.6
  36.7 0.0 copy-start.2
  36.7 1.0 copy-done.2
  37.8 0.0 copy-start.4
  37.8 1.0 copy-done.4
  38.8 0.0 copy-start.5
  38.8 1.0 copy-done.5
  39.9 0.0 copy-start.9
  39.9 0.0 copy-start.11
  39.9 0.9 shard_map.55.within_ref
  40.8 0.0 collective-permute-done.3
  40.8 0.0 copy-done.9
  40.8 0.1 copy-done.11
  40.9 0.0 copy-start.7
  40.9 1.1 fusion.2.state_ref
  42.0 0.0 copy-done.7
  42.0 1.5 %shard_map.57.tokens_ref = bf16[256,1024]{1,0:T(8,128)(2,1)} custom-call(bf16[256,1024]{1,0:T(8,128)(2,1)S(1)} %copy-done.5, f32[256,1024]{1,0:T(8,128)S(1)} %shard_map.55.within_ref, bf16[8,128,128]{2,1,0:T(8,128)(2,1)S(1)} %fusion.2.state_ref, f32[1,1024]{1,0:T(1,128)S(1)} %bitcast.6), custom_call_target="tpu_custom_call" | custom-call | flops 67108864 | bytes 2097152 | tf_op jit(solution)/shard_map/pallas_call | solution.py:250
  43.5 9.3 %collective-permute-start.9 = (bf16[256,1024]{1,0:T(8,128)(2,1)}, bf16[256,1024]{1,0:T(8,128)(2,1)}, u32[]{:S(2)}, u32[]{:S(2)}) collective-permute-start(bf16[256,1024]{1,0:T(8,128)(2,1)} %shard_map.57.tokens_ref), channel_id=1, source_target_pairs={{0,16},{4,20},{8,24},{12,28},{16,0},{20,4},{24,8},{28,12},{1,17},{... | collective-permute-start | bytes 1572872 | tf_op jit(solution)/shard_map/ppermute | solution.py:220
  52.9 5.2 %collective-permute-done.4.near_b = bf16[1024,512]{1,0:T(8,128)(2,1)S(1)} collective-permute-done((bf16[1024,512]{1,0:T(8,128)(2,1)S(1)}, bf16[1024,512]{1,0:T(8,128)(2,1)S(1)}, u32[]{:S(2)}, u32[]{:S(2)}) %collective-permute-start.4) | collective-permute-done | bytes 1048608 | tf_op jit(solution)/shard_map/ppermute | solution.py:220
  58.1 18.3 %collective-permute-done.9.tokens_ref = bf16[256,1024]{1,0:T(8,128)(2,1)} collective-permute-done((bf16[256,1024]{1,0:T(8,128)(2,1)}, bf16[256,1024]{1,0:T(8,128)(2,1)}, u32[]{:S(2)}, u32[]{:S(2)}) %collective-permute-start.9) | collective-permute-done | bytes 524320 | tf_op jit(solution)/shard_map/ppermute | solution.py:220
  76.3 4.3 %collective-permute-done.6.far_b = bf16[1024,512]{1,0:T(8,128)(2,1)} collective-permute-done((bf16[1024,512]{1,0:T(8,128)(2,1)S(1)}, bf16[1024,512]{1,0:T(8,128)(2,1)}, u32[]{:S(2)}, u32[]{:S(2)}) %collective-permute-start.6) | collective-permute-done | bytes 1048608 | tf_op jit(solution)/shard_map/ppermute | solution.py:220
  80.6 2.6 %shard_map.59 = (bf16[2,256,512]{2,1,0:T(8,128)(2,1)S(1)}, bf16[2,256,512]{2,1,0:T(8,128)(2,1)S(1)}) custom-call(s32[1]{0:T(128)} %bitcast.pick_ref, bf16[256,1024]{1,0:T(8,128)(2,1)} %collective-permute-done.9.tokens_ref, bf16[1024,512]{1,0:T(8,128)(2,1)S(1)} %copy-done, bf16[1024,512]{1,0:T(8,128)(2,1)S(1)} %collective-permute-done.4.near_b, ...), custom_call_target="tpu_custom_call" | custom-call | flops 1073741824 | bytes 3145728 | tf_op jit(solution)/shard_map/pallas_call | solution.py:261
  83.3 2.9 %collective-permute-start.10 = (bf16[2,256,512]{2,1,0:T(8,128)(2,1)S(1)}, bf16[2,256,512]{2,1,0:T(8,128)(2,1)S(1)}, u32[]{:S(2)}, u32[]{:S(2)}) collective-permute-start(bf16[2,256,512]{2,1,0:T(8,128)(2,1)S(1)} %get-tuple-element.16), channel_id=1, source_target_pairs={{0,1},{1,0},{2,3},{3,2},{4,5},{5,4},{6,7},{7,6},{8,9},{9,8},{10,11... | collective-permute-start | bytes 1572872 | tf_op jit(solution)/shard_map/ppermute | solution.py:224
  86.1 2.6 %shard_map.58 = (bf16[2,256,512]{2,1,0:T(8,128)(2,1)S(1)}, bf16[2,256,512]{2,1,0:T(8,128)(2,1)S(1)}) custom-call(s32[1]{0:T(128)} %bitcast.pick_ref, bf16[256,1024]{1,0:T(8,128)(2,1)} %shard_map.57.tokens_ref, bf16[1024,512]{1,0:T(8,128)(2,1)S(1)} %copy-done, bf16[1024,512]{1,0:T(8,128)(2,1)S(1)} %collective-permute-done.4.near_b, ...), custom_call_target="tpu_custom_call" | custom-call | flops 1073741824 | bytes 3145728 | tf_op jit(solution)/shard_map/pallas_call | solution.py:261
  88.8 0.0 copy-start.6
  88.8 0.1 collective-permute-start.7
  88.9 0.0 collective-permute-done.10
  88.9 0.1 add_convert_fusion.1
  89.0 11.2 %collective-permute-start.12 = (bf16[2,256,512]{2,1,0:T(8,128)(2,1)S(1)}, bf16[2,256,512]{2,1,0:T(8,128)(2,1)S(1)}, u32[]{:S(2)}, u32[]{:S(2)}) collective-permute-start(bf16[2,256,512]{2,1,0:T(8,128)(2,1)S(1)} %add_convert_fusion.1), channel_id=1, source_target_pairs={{2,16},{3,17},{6,20},{7,21},{10,24},{11,25},{14,28},{15,29},{16,2}... | collective-permute-start | bytes 1572872 | tf_op jit(solution)/shard_map/ppermute | solution.py:224
  100.2 1.3 %collective-permute-start.11 = (bf16[2,256,512]{2,1,0:T(8,128)(2,1)S(1)}, bf16[2,256,512]{2,1,0:T(8,128)(2,1)S(1)}, u32[]{:S(2)}, u32[]{:S(2)}) collective-permute-start(bf16[2,256,512]{2,1,0:T(8,128)(2,1)S(1)} %add_convert_fusion.1), channel_id=1, source_target_pairs={{0,16},{1,17},{4,20},{5,21},{8,24},{9,25},{12,28},{13,29},{18,2},{... | collective-permute-start | bytes 1572872 | tf_op jit(solution)/shard_map/ppermute | solution.py:224
  101.5 0.0 collective-permute-done.7
  101.6 0.0 copy-done.6
  101.6 0.1 fusion
  101.7 2.9 %collective-permute-start.8 = (bf16[2,256,512]{2,1,0:T(8,128)(2,1)S(1)}, bf16[2,256,512]{2,1,0:T(8,128)(2,1)S(1)}, u32[]{:S(2)}, u32[]{:S(2)}) collective-permute-start(bf16[2,256,512]{2,1,0:T(8,128)(2,1)S(1)} %fusion), channel_id=1, source_target_pairs={{2,0},{3,1},{6,4},{7,5},{10,8},{11,9},{14,12},{15,13},{16,18},{17,... | collective-permute-start | bytes 1572872 | tf_op jit(solution)/shard_map/ppermute | solution.py:224
  104.6 18.8 %collective-permute-done.12 = bf16[2,256,512]{2,1,0:T(8,128)(2,1)S(1)} collective-permute-done((bf16[2,256,512]{2,1,0:T(8,128)(2,1)S(1)}, bf16[2,256,512]{2,1,0:T(8,128)(2,1)S(1)}, u32[]{:S(2)}, u32[]{:S(2)}) %collective-permute-start.12) | collective-permute-done | bytes 524320 | tf_op jit(solution)/shard_map/ppermute | solution.py:224
  123.5 1.8 %collective-permute-done.11 = bf16[2,256,512]{2,1,0:T(8,128)(2,1)S(1)} collective-permute-done((bf16[2,256,512]{2,1,0:T(8,128)(2,1)S(1)}, bf16[2,256,512]{2,1,0:T(8,128)(2,1)S(1)}, u32[]{:S(2)}, u32[]{:S(2)}) %collective-permute-start.11) | collective-permute-done | bytes 524320 | tf_op jit(solution)/shard_map/ppermute | solution.py:224
  125.3 0.0 collective-permute-done.8
  125.3 1.4 %add_convert_fusion = bf16[2,256,512]{2,1,0:T(8,128)(2,1)S(1)} fusion(bf16[2,256,512]{2,1,0:T(8,128)(2,1)S(1)} %collective-permute-done.12, bf16[2,256,512]{2,1,0:T(8,128)(2,1)S(1)} %collective-permute-done.11, bf16[2,256,512]{2,1,0:T(8,128)(2,1)S(1)} %collective-permute-done.8, bf16[2,256,512]{2,1,0:T(8,128)(2,1)S(1)} %collective-permute-done.7, ...), kind=kLoop, calls=%fused_computation | loop fusion | flops 2883584 | bytes 3145729 | tf_op jit(solution)/shard_map/convert_element_type | solution.py:282
  126.8 0.9 pad_maximum_fusion
  (1 shorter events, 0.0 us)
Async XLA Ops:
  0.0 3.8 %copy-start = (bf16[1024,512]{1,0:T(8,128)(2,1)S(1)}, bf16[1024,512]{1,0:T(8,128)(2,1)}, u32[]{:S(2)}) copy-start(bf16[1024,512]{1,0:T(8,128)(2,1)} %near_a.3) | copy-start | bytes 3145732
  0.0 1.1 copy-start.1
  1.1 1.0 copy-start.3
  2.5 7.2 %collective-permute-start = (bf16[8,128,128]{2,1,0:T(8,128)(2,1)S(1)}, bf16[8,128,128]{2,1,0:T(8,128)(2,1)S(1)}, u32[]{:S(2)}, u32[]{:S(2)}) collective-permute-start(bf16[8,128,128]{2,1,0:T(8,128)(2,1)S(1)} %get-tuple-element.12), channel_id=1, source_target_pairs={{0,4},{4,0},{8,12},{12,8},{16,20},{20,16},{24,28},{28,24},{1,5},{5... | collective-permute-start | bytes 786440 | tf_op jit(solution)/shard_map/ppermute | solution.py:220
  3.8 31.7 %collective-permute-start.5 = (bf16[1024,512]{1,0:T(8,128)(2,1)S(1)}, bf16[1024,512]{1,0:T(8,128)(2,1)S(1)}, u32[]{:S(2)}, u32[]{:S(2)}) collective-permute-start(bf16[1024,512]{1,0:T(8,128)(2,1)S(1)} %copy-done), channel_id=1, source_target_pairs={{0,8},{4,12},{8,0},{12,4},{16,24},{20,28},{24,16},{28,20},{1,9},{5... | collective-permute-start | bytes 3145736 | tf_op jit(solution)/shard_map/ppermute | solution.py:220
  9.8 22.4 %collective-permute-start.1 = (bf16[8,128,128]{2,1,0:T(8,128)(2,1)S(1)}, bf16[8,128,128]{2,1,0:T(8,128)(2,1)S(1)}, u32[]{:S(2)}, u32[]{:S(2)}) collective-permute-start(bf16[8,128,128]{2,1,0:T(8,128)(2,1)S(1)} %fusion.4), channel_id=1, source_target_pairs={{0,8},{4,12},{1,9},{5,13},{2,10},{6,14},{3,11},{7,15}} | collective-permute-start | bytes 786440 | tf_op jit(solution)/shard_map/ppermute | solution.py:248
  32.3 0.8 copy-start.8
  32.4 0.7 collective-permute-start.2
  33.1 0.8 copy-start.10
  33.9 6.9 %collective-permute-start.3 = (bf16[8,128,128]{2,1,0:T(8,128)(2,1)}, bf16[8,128,128]{2,1,0:T(8,128)(2,1)}, u32[]{:S(2)}, u32[]{:S(2)}) collective-permute-start(bf16[8,128,128]{2,1,0:T(8,128)(2,1)} %add_convert_fusion.2), channel_id=1, source_target_pairs={{16,24},{20,28},{17,25},{21,29},{18,26},{22,30},{19,27},{23,31}} | collective-permute-start | bytes 786440 | tf_op jit(solution)/shard_map/ppermute | solution.py:248
  35.3 22.8 %collective-permute-start.4 = (bf16[1024,512]{1,0:T(8,128)(2,1)S(1)}, bf16[1024,512]{1,0:T(8,128)(2,1)S(1)}, u32[]{:S(2)}, u32[]{:S(2)}) collective-permute-start(bf16[1024,512]{1,0:T(8,128)(2,1)S(1)} %copy-done), channel_id=1, source_target_pairs={{0,4},{4,0},{8,12},{12,8},{16,20},{20,16},{24,28},{28,24},{1,5},{5... | collective-permute-start | bytes 3145736 | tf_op jit(solution)/shard_map/ppermute | solution.py:220
  35.5 45.1 %collective-permute-start.6 = (bf16[1024,512]{1,0:T(8,128)(2,1)S(1)}, bf16[1024,512]{1,0:T(8,128)(2,1)}, u32[]{:S(2)}, u32[]{:S(2)}) collective-permute-start(bf16[1024,512]{1,0:T(8,128)(2,1)S(1)} %collective-permute-done.5.far_a), channel_id=1, source_target_pairs={{0,4},{4,0},{8,12},{12,8},{16,20},{20,16},{24,28},{28,24},{1,5},{5... | collective-permute-start | bytes 3145736 | tf_op jit(solution)/shard_map/ppermute | solution.py:220
  36.7 1.0 copy-start.2
  37.8 1.0 copy-start.4
  38.8 1.0 copy-start.5
  39.9 0.9 copy-start.9
  39.9 1.0 copy-start.11
  40.9 1.1 copy-start.7
  43.5 32.8 %collective-permute-start.9 = (bf16[256,1024]{1,0:T(8,128)(2,1)}, bf16[256,1024]{1,0:T(8,128)(2,1)}, u32[]{:S(2)}, u32[]{:S(2)}) collective-permute-start(bf16[256,1024]{1,0:T(8,128)(2,1)} %shard_map.57.tokens_ref), channel_id=1, source_target_pairs={{0,16},{4,20},{8,24},{12,28},{16,0},{20,4},{24,8},{28,12},{1,17},{... | collective-permute-start | bytes 1572872 | tf_op jit(solution)/shard_map/ppermute | solution.py:220
  83.3 5.6 %collective-permute-start.10 = (bf16[2,256,512]{2,1,0:T(8,128)(2,1)S(1)}, bf16[2,256,512]{2,1,0:T(8,128)(2,1)S(1)}, u32[]{:S(2)}, u32[]{:S(2)}) collective-permute-start(bf16[2,256,512]{2,1,0:T(8,128)(2,1)S(1)} %get-tuple-element.16), channel_id=1, source_target_pairs={{0,1},{1,0},{2,3},{3,2},{4,5},{5,4},{6,7},{7,6},{8,9},{9,8},{10,11... | collective-permute-start | bytes 1572872 | tf_op jit(solution)/shard_map/ppermute | solution.py:224
  88.8 12.8 %copy-start.6 = (bf16[2,256,512]{2,1,0:T(8,128)(2,1)}, bf16[2,256,512]{2,1,0:T(8,128)(2,1)S(1)}, u32[]{:S(2)}) copy-start(bf16[2,256,512]{2,1,0:T(8,128)(2,1)S(1)} %get-tuple-element.13) | copy-start | bytes 1572868
  88.8 12.8 %collective-permute-start.7 = (bf16[2,256,512]{2,1,0:T(8,128)(2,1)S(1)}, bf16[2,256,512]{2,1,0:T(8,128)(2,1)S(1)}, u32[]{:S(2)}, u32[]{:S(2)}) collective-permute-start(bf16[2,256,512]{2,1,0:T(8,128)(2,1)S(1)} %get-tuple-element.14), channel_id=1, source_target_pairs={{0,1},{1,0},{2,3},{3,2},{4,5},{5,4},{6,7},{7,6},{8,9},{9,8},{10,11... | collective-permute-start | bytes 1572872 | tf_op jit(solution)/shard_map/ppermute | solution.py:224
  89.0 34.4 %collective-permute-start.12 = (bf16[2,256,512]{2,1,0:T(8,128)(2,1)S(1)}, bf16[2,256,512]{2,1,0:T(8,128)(2,1)S(1)}, u32[]{:S(2)}, u32[]{:S(2)}) collective-permute-start(bf16[2,256,512]{2,1,0:T(8,128)(2,1)S(1)} %add_convert_fusion.1), channel_id=1, source_target_pairs={{2,16},{3,17},{6,20},{7,21},{10,24},{11,25},{14,28},{15,29},{16,2}... | collective-permute-start | bytes 1572872 | tf_op jit(solution)/shard_map/ppermute | solution.py:224
  100.2 25.1 %collective-permute-start.11 = (bf16[2,256,512]{2,1,0:T(8,128)(2,1)S(1)}, bf16[2,256,512]{2,1,0:T(8,128)(2,1)S(1)}, u32[]{:S(2)}, u32[]{:S(2)}) collective-permute-start(bf16[2,256,512]{2,1,0:T(8,128)(2,1)S(1)} %add_convert_fusion.1), channel_id=1, source_target_pairs={{0,16},{1,17},{4,20},{5,21},{8,24},{9,25},{12,28},{13,29},{18,2},{... | collective-permute-start | bytes 1572872 | tf_op jit(solution)/shard_map/ppermute | solution.py:224
  101.7 23.6 %collective-permute-start.8 = (bf16[2,256,512]{2,1,0:T(8,128)(2,1)S(1)}, bf16[2,256,512]{2,1,0:T(8,128)(2,1)S(1)}, u32[]{:S(2)}, u32[]{:S(2)}) collective-permute-start(bf16[2,256,512]{2,1,0:T(8,128)(2,1)S(1)} %fusion), channel_id=1, source_target_pairs={{2,0},{3,1},{6,4},{7,5},{10,8},{11,9},{14,12},{15,13},{16,18},{17,... | collective-permute-start | bytes 1572872 | tf_op jit(solution)/shard_map/ppermute | solution.py:224

commit v6 on v2

--- a/solution.py
+++ b/solution.py
@@ -74,14 +74,18 @@
         out_ref[:, cols] = jnp.dot(scores, v_ref[:, cols], preferred_element_type=F32)
 
 
-def attend_kernel(q_ref, within_ref, state_ref, gain_ref, out_ref):
+def attend_kernel(q_ref, within_ref, state_ref, gain_ref, whole_ref, top_ref, bottom_ref):
+    half = q_ref.shape[0] // 2
     for head in range(q_ref.shape[1] // HD):
         cols = head_slice(head)
         carried = jnp.dot(q_ref[:, cols], state_ref[head].astype(BF16), preferred_element_type=F32)
         combined = within_ref[:, cols] + carried
         mean_square = jnp.mean(combined * combined, axis=-1, keepdims=True)
         scaled = combined / jnp.sqrt(mean_square + epsilon) * gain_ref[:, cols]
-        out_ref[:, cols] = scaled.astype(BF16)
+        scaled = scaled.astype(BF16)
+        whole_ref[:, cols] = scaled
+        top_ref[:, cols] = scaled[:half]
+        bottom_ref[:, cols] = scaled[half:]
 
 
 def call(kernel, out_shape, flops, moved):
@@ -91,6 +95,18 @@
         compiler_params=pltpu.CompilerParams(vmem_limit_bytes=24 * 1024 * 1024),
         cost_estimate=pl.CostEstimate(flops=flops, bytes_accessed=moved, transcendentals=0),
     )
+
+
+def attend(queries, within, state_in, norm_gain):
+    rows, features = queries.shape
+    size = rows * features
+    half = jax.ShapeDtypeStruct((rows // 2, features), BF16)
+    return call(
+        attend_kernel,
+        (jax.ShapeDtypeStruct((rows, features), BF16), half, half),
+        2 * size * HD,
+        10 * size,
+    )(queries, within, state_in, norm_gain[None])
 
 
 def planes_body(seq_count, head_groups):
@@ -159,9 +175,7 @@
             within_kernel, jax.ShapeDtypeStruct((rows, features), F32), 4 * size * BLOCK, 10 * size
         )(queries, key_vectors, value_vectors)
         state_in = prefix_over_seq(wide, narrow)
-        attended = call(
-            attend_kernel, jax.ShapeDtypeStruct((rows, features), BF16), 2 * size * HD, 8 * size
-        )(queries, within, state_in, norm_gain[None])
+        attended = attend(queries, within, state_in, norm_gain)[0]
 
         parts = [None] * head_groups
         for j in (3, 2, 1, 0):
@@ -185,13 +199,127 @@
     return body
 
 
+def project_pair_kernel(pick_ref, even_ref, odd_ref, own_ref, mate_ref, keep_ref, send_ref):
+    first = pick_ref[0] == 0
+    even, odd = even_ref[...], odd_ref[...]
+    kept = jnp.where(first, even, odd)
+    sent = jnp.where(first, odd, even)
+    for half, weight_ref in enumerate((own_ref, mate_ref)):
+        weight = weight_ref[...]
+        send_ref[half] = jnp.dot(sent, weight, preferred_element_type=F32).astype(BF16)
+        keep_ref[half] = jnp.dot(kept, weight, preferred_element_type=F32).astype(BF16)
+
+
+def project_split_kernel(top_ref, bottom_ref, own_ref, mate_ref, out_ref):
+    rows = top_ref.shape[0]
+    for half, weight_ref in enumerate((own_ref, mate_ref)):
+        weight = weight_ref[...]
+        for part, tokens_ref in enumerate((top_ref, bottom_ref)):
+            product = jnp.dot(tokens_ref[...], weight, preferred_element_type=F32)
+            out_ref[half, part * rows : (part + 1) * rows] = product.astype(BF16)
+
+
+def pairs_body(queries, key_vectors, value_vectors, norm_gain, out_weight):
+    rows, features = queries.shape
+    heads = features // HD
+    size = rows * features
+    half_cols = out_weight.shape[1]
+    both = ("seq", "head")
+    place, group = lax.axis_index("seq"), lax.axis_index("head")
+    y, core = place % 2, group % 2
+    devices = [(s // 2, s % 2, h // 2, h % 2) for s in range(8) for h in range(4)]
+
+    def at(z, y, x, c):
+        return (z * 2 + y) * 4 + x * 2 + c
+
+    def swap(value, mask):
+        return lax.ppermute(value, "seq", [(s, s ^ mask) for s in range(8)])
+
+    def move(value, place_of, chosen=lambda z, y, x, c: True):
+        pairs = [(at(*d), at(*place_of(*d))) for d in devices if chosen(*d)]
+        return lax.ppermute(value, both, pairs)
+
+    wide, narrow = call(
+        state_kernel,
+        (
+            jax.ShapeDtypeStruct((heads, HD, HD), F32),
+            jax.ShapeDtypeStruct((heads, HD, HD), BF16),
+        ),
+        2 * size * HD,
+        4 * size + 6 * heads * HD * HD,
+    )(key_vectors, value_vectors)
+    within = call(
+        within_kernel, jax.ShapeDtypeStruct((rows, features), F32), 4 * size * BLOCK, 10 * size
+    )(queries, key_vectors, value_vectors)
+
+    mate_weight = swap(out_weight, 1)
+
+    mate = swap(narrow, 1).astype(F32)
+    total = wide + mate
+    before = jnp.zeros_like(wide)
+    for plane in range(3):
+        pairs = [(2 * plane + i, 2 * plane + 2 + i) for i in range(2)]
+        onward = (before + total).astype(BF16)
+        before += lax.ppermute(onward, "seq", pairs).astype(F32)
+    state_in = (before + jnp.where(y == 1, mate, 0.0)).astype(BF16)
+    attended, top, bottom = attend(queries, within, state_in, norm_gain)
+
+    top_two, bottom_two = swap(top, 4), swap(bottom, 4)
+    attended_one = swap(attended, 2)
+    top_three, bottom_three = swap(top_two, 2), swap(bottom_two, 2)
+
+    tile = jax.ShapeDtypeStruct((2, rows, half_cols), BF16)
+    vmem = pl.BlockSpec(memory_space=pltpu.VMEM)
+    smem = pl.BlockSpec(memory_space=pltpu.SMEM)
+    flops = 4 * size * half_cols
+    keep, send = pl.pallas_call(
+        project_pair_kernel,
+        out_shape=(tile, tile),
+        in_specs=[smem] + [vmem] * 4,
+        out_specs=(vmem, vmem),
+        compiler_params=pltpu.CompilerParams(vmem_limit_bytes=24 * 1024 * 1024),
+        cost_estimate=pl.CostEstimate(flops=2 * flops, bytes_accessed=12 * size, transcendentals=0),
+    )(core.astype(jnp.int32)[None], attended, attended_one, out_weight, mate_weight)
+    split = call(project_split_kernel, tile, flops, 8 * size)
+    tile_two = split(top_two, bottom_two, out_weight, mate_weight)
+    tile_three = split(top_three, bottom_three, out_weight, mate_weight)
+
+    def other_core(value, chosen=lambda z, y, x, c: True):
+        return move(value, lambda z, y, x, c: (z, y, x, 1 - c), chosen)
+
+    def add(one, two):
+        return (one.astype(F32) + two.astype(F32)).astype(BF16)
+
+    near = add(keep, other_core(send))
+    tile_two = add(tile_two, other_core(tile_two, lambda z, y, x, c: c == 1))
+    tile_three = add(tile_three, other_core(tile_three, lambda z, y, x, c: c == 0))
+
+    def home(value, masks):
+        total = 0.0
+        for chip in range(2):
+            got = move(
+                value,
+                lambda z, y, x, c: (z ^ masks[c], y, z // 2, z % 2),
+                lambda z, y, x, c: x == chip and masks[c] is not None,
+            )
+            total += got.astype(F32)
+        return total
+
+    result = home(near, (0, 1)) + home(tile_two, (2, None)) + home(tile_three, (None, 3))
+    result = result.astype(BF16)
+    first = jnp.where(y == 0, result[0], result[1])
+    return jnp.concatenate([first, jnp.where(y == 0, result[1], result[0])], axis=1)
+
+
 def solution(mesh):
     seq_count, head_groups = mesh.shape["seq"], mesh.shape["head"]
 
     def run(queries, key_vectors, value_vectors, norm_gain, out_weight):
         one_block = queries.shape[0] == BLOCK * seq_count
         body = general_body
-        if one_block and head_groups == 4 and seq_count % head_groups == 0:
+        if one_block and head_groups == 4 and seq_count == 8:
+            body = pairs_body
+        elif one_block and head_groups == 4 and seq_count % head_groups == 0:
             body = planes_body(seq_count, head_groups)
         return jax.shard_map(
             body,

time: 136 us -> 124 us (0.912)
  the two profiles are of different devices: /device:TPU:17 before, /device:TPU:10 now
where the time goes in v6:
time: 124 us; the launch traced here: 123 us
  waiting for transfers between devices  76.2 us (61%)
  starting transfers between devices  29.7 us (24%)
  other arithmetic  6.85 us (6%)
  Pallas kernels  6.7 us (5%)
  local copies, waits for them, and re-layouts  3.23 us (3%)
    ppermute x7, waiting for transfers between devices, swap(): return lax.ppermute(value, 'seq', [(s, s ^ mask) for s in range(8)])  35 us
    ppermute x9, waiting for transfers between devices, move(): return lax.ppermute(value, both, pairs)  31 us
    ppermute x9, starting transfers between devices, move(): return lax.ppermute(value, both, pairs)  13.8 us
    ppermute x7, starting transfers between devices, swap(): return lax.ppermute(value, 'seq', [(s, s ^ mask) for s in range(8)])  11.8 us
    ppermute x3, waiting for transfers between devices, pairs_body(): before += lax.ppermute(onward, 'seq', pairs).astype(F32)  10.2 us
    ppermute x3, starting transfers between devices, pairs_body(): before += lax.ppermute(onward, 'seq', pairs).astype(F32)  4.21 us
    unnamed x22, local copies, waits for them, and re-layouts  3.23 us
  transfers between devices with their start and end apart: 19, of which 11 were waited for; matrix products, arithmetic and copies ran while one was open for 3% of the time, Pallas kernels for 5%

profile of v6, /device:TPU:10, one launch (start us, length us, event | category | flops | bytes accessed | tf_op | source)
XLA Modules:
  0.0 123.0 jit_solution(9517258015158487077)
XLA Ops:
  0.0 1.0 copy-done.2
  1.0 1.0 copy-done.4
  2.1 0.4 shard_map.56
  2.4 1.6 %collective-permute-start = (bf16[8,128,128]{2,1,0:T(8,128)(2,1)S(1)}, bf16[8,128,128]{2,1,0:T(8,128)(2,1)S(1)}, u32[]{:S(2)}, u32[]{:S(2)}) collective-permute-start(bf16[8,128,128]{2,1,0:T(8,128)(2,1)S(1)} %get-tuple-element.13), channel_id=1, source_target_pairs={{0,4},{4,0},{8,12},{12,8},{16,20},{20,16},{24,28},{28,24},{1,5},{5... | collective-permute-start | bytes 786440 | tf_op jit(solution)/shard_map/ppermute | solution.py:236
  4.0 6.5 %collective-permute-done = bf16[8,128,128]{2,1,0:T(8,128)(2,1)S(1)} collective-permute-done((bf16[8,128,128]{2,1,0:T(8,128)(2,1)S(1)}, bf16[8,128,128]{2,1,0:T(8,128)(2,1)S(1)}, u32[]{:S(2)}, u32[]{:S(2)}) %collective-permute-start) | collective-permute-done | bytes 262176 | tf_op jit(solution)/shard_map/ppermute | solution.py:236
  10.6 0.1 fusion.3
  10.6 1.4 %collective-permute-start.1 = (bf16[8,128,128]{2,1,0:T(8,128)(2,1)S(1)}, bf16[8,128,128]{2,1,0:T(8,128)(2,1)S(1)}, u32[]{:S(2)}, u32[]{:S(2)}) collective-permute-start(bf16[8,128,128]{2,1,0:T(8,128)(2,1)S(1)} %fusion.3), channel_id=1, source_target_pairs={{0,8},{4,12},{1,9},{5,13},{2,10},{6,14},{3,11},{7,15}} | collective-permute-start | bytes 786440 | tf_op jit(solution)/shard_map/ppermute | solution.py:263
  12.1 7.8 %collective-permute-done.1 = bf16[8,128,128]{2,1,0:T(8,128)(2,1)S(1)} collective-permute-done((bf16[8,128,128]{2,1,0:T(8,128)(2,1)S(1)}, bf16[8,128,128]{2,1,0:T(8,128)(2,1)S(1)}, u32[]{:S(2)}, u32[]{:S(2)}) %collective-permute-start.1) | collective-permute-done | bytes 262176 | tf_op jit(solution)/shard_map/ppermute | solution.py:263
  19.8 0.1 fusion.2
  19.9 0.0 copy-start.1
  19.9 0.0 copy-start.3
  19.9 1.4 %collective-permute-start.2 = (bf16[8,128,128]{2,1,0:T(8,128)(2,1)S(1)}, bf16[8,128,128]{2,1,0:T(8,128)(2,1)S(1)}, u32[]{:S(2)}, u32[]{:S(2)}) collective-permute-start(bf16[8,128,128]{2,1,0:T(8,128)(2,1)S(1)} %fusion.2), channel_id=1, source_target_pairs={{8,16},{12,20},{9,17},{13,21},{10,18},{14,22},{11,19},{15,23}} | collective-permute-start | bytes 786440 | tf_op jit(solution)/shard_map/ppermute | solution.py:263
  21.4 0.0 copy-done
  21.4 1.6 %collective-permute-start.5 = (bf16[1024,512]{1,0:T(8,128)(2,1)S(1)}, bf16[1024,512]{1,0:T(8,128)(2,1)S(1)}, u32[]{:S(2)}, u32[]{:S(2)}) collective-permute-start(bf16[1024,512]{1,0:T(8,128)(2,1)S(1)} %copy-done), channel_id=1, source_target_pairs={{0,4},{4,0},{8,12},{12,8},{16,20},{20,16},{24,28},{28,24},{1,5},{5... | collective-permute-start | bytes 3145736 | tf_op jit(solution)/shard_map/ppermute | solution.py:236
  23.0 2.4 %collective-permute-done.2 = bf16[8,128,128]{2,1,0:T(8,128)(2,1)S(1)} collective-permute-done((bf16[8,128,128]{2,1,0:T(8,128)(2,1)S(1)}, bf16[8,128,128]{2,1,0:T(8,128)(2,1)S(1)}, u32[]{:S(2)}, u32[]{:S(2)}) %collective-permute-start.2) | collective-permute-done | bytes 262176 | tf_op jit(solution)/shard_map/ppermute | solution.py:263
  25.4 0.0 copy-done.7
  25.4 0.8 add_convert_fusion.4
  26.2 0.0 copy-done.9
  26.2 1.3 %collective-permute-start.3 = (bf16[8,128,128]{2,1,0:T(8,128)(2,1)}, bf16[8,128,128]{2,1,0:T(8,128)(2,1)}, u32[]{:S(2)}, u32[]{:S(2)}) collective-permute-start(bf16[8,128,128]{2,1,0:T(8,128)(2,1)} %add_convert_fusion.4), channel_id=1, source_target_pairs={{16,24},{20,28},{17,25},{21,29},{18,26},{22,30},{19,27},{23,31}} | collective-permute-start | bytes 786440 | tf_op jit(solution)/shard_map/ppermute | solution.py:263
  27.6 0.0 copy-done.1
  27.6 0.0 copy-done.3
  27.6 1.0 copy-done.5
  28.6 0.9 shard_map.55.within_ref
  29.6 0.0 collective-permute-done.3
  29.6 0.1 copy-done.10
  29.7 1.1 fusion.1.state_ref
  30.8 1.5 %shard_map.57 = (bf16[256,1024]{1,0:T(8,128)(2,1)}, bf16[128,1024]{1,0:T(8,128)(2,1)S(1)}, bf16[128,1024]{1,0:T(8,128)(2,1)S(1)}) custom-call(bf16[256,1024]{1,0:T(8,128)(2,1)S(1)} %copy-done.1, f32[256,1024]{1,0:T(8,128)S(1)} %shard_map.55.within_ref, bf16[8,128,128]{2,1,0:T(8,128)(2,1)S(1)} %fusion.1.state_ref, f32[1,1024]{1,0:T(1,128)S(1)} %bitcast.6), custom_call_target="tpu_custom_call" | custom-call | flops 67108864 | bytes 2621440 | tf_op jit(solution)/shard_map/pallas_call | solution.py:104
  32.3 0.0 collective-permute-start.4
  32.3 6.5 %collective-permute-start.9 = (bf16[128,1024]{1,0:T(8,128)(2,1)S(1)}, bf16[128,1024]{1,0:T(8,128)(2,1)S(1)}, u32[]{:S(2)}, u32[]{:S(2)}) collective-permute-start(bf16[128,1024]{1,0:T(8,128)(2,1)S(1)} %get-tuple-element.17), channel_id=1, source_target_pairs={{0,16},{4,20},{8,24},{12,28},{16,0},{20,4},{24,8},{28,12},{1,17},{... | collective-permute-start | bytes 786440 | tf_op jit(solution)/shard_map/ppermute | solution.py:236
  38.8 0.0 collective-permute-start.10
  38.8 5.7 %collective-permute-done.5.mate_ref = bf16[1024,512]{1,0:T(8,128)(2,1)S(1)} collective-permute-done((bf16[1024,512]{1,0:T(8,128)(2,1)S(1)}, bf16[1024,512]{1,0:T(8,128)(2,1)S(1)}, u32[]{:S(2)}, u32[]{:S(2)}) %collective-permute-start.5) | collective-permute-done | bytes 1048608 | tf_op jit(solution)/shard_map/ppermute | solution.py:236
  44.6 11.8 %collective-permute-done.9.top_ref = bf16[128,1024]{1,0:T(8,128)(2,1)S(1)} collective-permute-done((bf16[128,1024]{1,0:T(8,128)(2,1)S(1)}, bf16[128,1024]{1,0:T(8,128)(2,1)S(1)}, u32[]{:S(2)}, u32[]{:S(2)}) %collective-permute-start.9) | collective-permute-done | bytes 262176 | tf_op jit(solution)/shard_map/ppermute | solution.py:236
  56.3 2.8 %collective-permute-done.10.bottom_ref = bf16[128,1024]{1,0:T(8,128)(2,1)S(1)} collective-permute-done((bf16[128,1024]{1,0:T(8,128)(2,1)S(1)}, bf16[128,1024]{1,0:T(8,128)(2,1)S(1)}, u32[]{:S(2)}, u32[]{:S(2)}) %collective-permute-start.10) | collective-permute-done | bytes 262176 | tf_op jit(solution)/shard_map/ppermute | solution.py:236
  59.1 0.7 shard_map.59
  59.9 1.3 %collective-permute-start.11 = (bf16[2,256,512]{2,1,0:T(8,128)(2,1)S(1)}, bf16[2,256,512]{2,1,0:T(8,128)(2,1)}, u32[]{:S(2)}, u32[]{:S(2)}) collective-permute-start(bf16[2,256,512]{2,1,0:T(8,128)(2,1)S(1)} %shard_map.59), channel_id=1, source_target_pairs={{1,0},{3,2},{5,4},{7,6},{9,8},{11,10},{13,12},{15,14},{17,16},{19,... | collective-permute-start | bytes 1572872 | tf_op jit(solution)/shard_map/ppermute | solution.py:240
  61.2 1.5 %collective-permute-start.14 = (bf16[128,1024]{1,0:T(8,128)(2,1)S(1)}, bf16[128,1024]{1,0:T(8,128)(2,1)S(1)}, u32[]{:S(2)}, u32[]{:S(2)}) collective-permute-start(bf16[128,1024]{1,0:T(8,128)(2,1)S(1)} %collective-permute-done.9.top_ref), channel_id=1, source_target_pairs={{0,8},{4,12},{8,0},{12,4},{16,24},{20,28},{24,16},{28,20},{1,9},{5... | collective-permute-start | bytes 786440 | tf_op jit(solution)/shard_map/ppermute | solution.py:236
  62.7 0.5 collective-permute-start.15
  63.3 0.0 collective-permute-done.4.odd_ref
  63.3 2.4 %shard_map.58 = (bf16[2,256,512]{2,1,0:T(8,128)(2,1)S(1)}, bf16[2,256,512]{2,1,0:T(8,128)(2,1)S(1)}) custom-call(s32[1]{0:T(128)} %bitcast.pick_ref, bf16[256,1024]{1,0:T(8,128)(2,1)} %get-tuple-element.14.even_ref, bf16[256,1024]{1,0:T(8,128)(2,1)} %collective-permute-done.4.odd_ref, bf16[1024,512]{1,0:T(8,128)(2,1)S(1)} %copy-done, ...), custom_call_target="tpu_custom_call" | custom-call | flops 1073741824 | bytes 3145728 | tf_op jit(solution)/shard_map/pallas_call | solution.py:275
  65.7 1.3 %collective-permute-start.6 = (bf16[2,256,512]{2,1,0:T(8,128)(2,1)S(1)}, bf16[2,256,512]{2,1,0:T(8,128)(2,1)S(1)}, u32[]{:S(2)}, u32[]{:S(2)}) collective-permute-start(bf16[2,256,512]{2,1,0:T(8,128)(2,1)S(1)} %get-tuple-element.16), channel_id=1, source_target_pairs={{0,1},{1,0},{2,3},{3,2},{4,5},{5,4},{6,7},{7,6},{8,9},{9,8},{10,11... | collective-permute-start | bytes 1572872 | tf_op jit(solution)/shard_map/ppermute | solution.py:240
  67.1 2.5 %collective-permute-done.14.top_ref = bf16[128,1024]{1,0:T(8,128)(2,1)S(1)} collective-permute-done((bf16[128,1024]{1,0:T(8,128)(2,1)S(1)}, bf16[128,1024]{1,0:T(8,128)(2,1)S(1)}, u32[]{:S(2)}, u32[]{:S(2)}) %collective-permute-start.14) | collective-permute-done | bytes 262176 | tf_op jit(solution)/shard_map/ppermute | solution.py:236
  69.6 5.6 %collective-permute-done.15.bottom_ref = bf16[128,1024]{1,0:T(8,128)(2,1)S(1)} collective-permute-done((bf16[128,1024]{1,0:T(8,128)(2,1)S(1)}, bf16[128,1024]{1,0:T(8,128)(2,1)S(1)}, u32[]{:S(2)}, u32[]{:S(2)}) %collective-permute-start.15) | collective-permute-done | bytes 262176 | tf_op jit(solution)/shard_map/ppermute | solution.py:236
  75.2 0.7 shard_map.60
  75.9 2.6 %collective-permute-start.16 = (bf16[2,256,512]{2,1,0:T(8,128)(2,1)S(1)}, bf16[2,256,512]{2,1,0:T(8,128)(2,1)S(1)}, u32[]{:S(2)}, u32[]{:S(2)}) collective-permute-start(bf16[2,256,512]{2,1,0:T(8,128)(2,1)S(1)} %shard_map.60), channel_id=1, source_target_pairs={{0,1},{2,3},{4,5},{6,7},{8,9},{10,11},{12,13},{14,15},{16,17},{18,... | collective-permute-start | bytes 1572872 | tf_op jit(solution)/shard_map/ppermute | solution.py:240
  78.5 0.0 collective-permute-done.11
  78.5 1.2 add_convert_fusion.2
  79.7 3.2 %collective-permute-start.13 = (bf16[2,256,512]{2,1,0:T(8,128)(2,1)S(1)}, bf16[2,256,512]{2,1,0:T(8,128)(2,1)S(1)}, u32[]{:S(2)}, u32[]{:S(2)}) collective-permute-start(bf16[2,256,512]{2,1,0:T(8,128)(2,1)S(1)} %add_convert_fusion.2), channel_id=1, source_target_pairs={{2,16},{6,20},{10,25},{14,29},{18,2},{22,6},{26,11},{30,15}} | collective-permute-start | bytes 1572872 | tf_op jit(solution)/shard_map/ppermute | solution.py:240
  83.0 0.7 collective-permute-start.12
  83.7 0.0 collective-permute-done.6
  83.7 0.1 add_convert_fusion.3
  83.8 1.3 %collective-permute-start.8 = (bf16[2,256,512]{2,1,0:T(8,128)(2,1)S(1)}, bf16[2,256,512]{2,1,0:T(8,128)(2,1)S(1)}, u32[]{:S(2)}, u32[]{:S(2)}) collective-permute-start(bf16[2,256,512]{2,1,0:T(8,128)(2,1)S(1)} %add_convert_fusion.3), channel_id=1, source_target_pairs={{2,0},{3,8},{6,4},{7,12},{10,9},{11,1},{14,13},{15,5},{18,18},{19,... | collective-permute-start | bytes 1572872 | tf_op jit(solution)/shard_map/ppermute | solution.py:240
  85.2 0.7 collective-permute-start.7
  85.9 0.0 collective-permute-done.16
  85.9 0.9 add_convert_fusion.1
  86.8 1.3 %collective-permute-start.18 = (bf16[2,256,512]{2,1,0:T(8,128)(2,1)}, bf16[2,256,512]{2,1,0:T(8,128)(2,1)}, u32[]{:S(2)}, u32[]{:S(2)}) collective-permute-start(bf16[2,256,512]{2,1,0:T(8,128)(2,1)} %add_convert_fusion.1), channel_id=1, source_target_pairs={{3,24},{7,28},{11,17},{15,21},{19,10},{23,14},{27,3},{31,7}} | collective-permute-start | bytes 1572872 | tf_op jit(solution)/shard_map/ppermute | solution.py:240
  88.1 15.0 %collective-permute-done.13 = bf16[2,256,512]{2,1,0:T(8,128)(2,1)S(1)} collective-permute-done((bf16[2,256,512]{2,1,0:T(8,128)(2,1)S(1)}, bf16[2,256,512]{2,1,0:T(8,128)(2,1)S(1)}, u32[]{:S(2)}, u32[]{:S(2)}) %collective-permute-start.13) | collective-permute-done | bytes 524320 | tf_op jit(solution)/shard_map/ppermute | solution.py:240
  103.1 1.3 %collective-permute-start.17 = (bf16[2,256,512]{2,1,0:T(8,128)(2,1)}, bf16[2,256,512]{2,1,0:T(8,128)(2,1)}, u32[]{:S(2)}, u32[]{:S(2)}) collective-permute-start(bf16[2,256,512]{2,1,0:T(8,128)(2,1)} %add_convert_fusion.1), channel_id=1, source_target_pairs={{1,24},{5,28},{9,17},{13,21},{17,10},{21,14},{25,3},{29,7}} | collective-permute-start | bytes 1572872 | tf_op jit(solution)/shard_map/ppermute | solution.py:240
  104.4 0.0 collective-permute-done.12
  104.4 0.0 collective-permute-done.8
  104.4 0.0 collective-permute-done.7
  104.5 3.3 %collective-permute-done.18 = bf16[2,256,512]{2,1,0:T(8,128)(2,1)} collective-permute-done((bf16[2,256,512]{2,1,0:T(8,128)(2,1)}, bf16[2,256,512]{2,1,0:T(8,128)(2,1)}, u32[]{:S(2)}, u32[]{:S(2)}) %collective-permute-start.18) | collective-permute-done | bytes 524320 | tf_op jit(solution)/shard_map/ppermute | solution.py:240
  107.8 12.7 %collective-permute-done.17 = bf16[2,256,512]{2,1,0:T(8,128)(2,1)} collective-permute-done((bf16[2,256,512]{2,1,0:T(8,128)(2,1)}, bf16[2,256,512]{2,1,0:T(8,128)(2,1)}, u32[]{:S(2)}, u32[]{:S(2)}) %collective-permute-start.17) | collective-permute-done | bytes 524320 | tf_op jit(solution)/shard_map/ppermute | solution.py:240
  120.5 1.6 %add_convert_fusion = bf16[2,256,512]{2,1,0:T(8,128)(2,1)S(1)} fusion(bf16[2,256,512]{2,1,0:T(8,128)(2,1)} %collective-permute-done.18, bf16[2,256,512]{2,1,0:T(8,128)(2,1)} %collective-permute-done.17, bf16[2,256,512]{2,1,0:T(8,128)(2,1)S(1)} %collective-permute-done.13, bf16[2,256,512]{2,1,0:T(8,128)(2,1)S(1)} %collective-permute-done.12, ...), kind=kLoop, calls=%fused_computation | loop fusion | flops 3145728 | bytes 3670016 | tf_op jit(solution)/shard_map/convert_element_type | solution.py:309
  122.1 0.9 pad_maximum_fusion
  (12 shorter events, 0.1 us)
Async XLA Ops:
  0.0 1.0 copy-start.2
  1.0 1.0 copy-start.4
  2.4 8.1 %collective-permute-start = (bf16[8,128,128]{2,1,0:T(8,128)(2,1)S(1)}, bf16[8,128,128]{2,1,0:T(8,128)(2,1)S(1)}, u32[]{:S(2)}, u32[]{:S(2)}) collective-permute-start(bf16[8,128,128]{2,1,0:T(8,128)(2,1)S(1)} %get-tuple-element.13), channel_id=1, source_target_pairs={{0,4},{4,0},{8,12},{12,8},{16,20},{20,16},{24,28},{28,24},{1,5},{5... | collective-permute-start | bytes 786440 | tf_op jit(solution)/shard_map/ppermute | solution.py:236
  10.6 10.8 %copy-start = (bf16[1024,512]{1,0:T(8,128)(2,1)S(1)}, bf16[1024,512]{1,0:T(8,128)(2,1)}, u32[]{:S(2)}) copy-start(bf16[1024,512]{1,0:T(8,128)(2,1)} %own_ref.5) | copy-start | bytes 3145732
  10.6 9.2 %collective-permute-start.1 = (bf16[8,128,128]{2,1,0:T(8,128)(2,1)S(1)}, bf16[8,128,128]{2,1,0:T(8,128)(2,1)S(1)}, u32[]{:S(2)}, u32[]{:S(2)}) collective-permute-start(bf16[8,128,128]{2,1,0:T(8,128)(2,1)S(1)} %fusion.3), channel_id=1, source_target_pairs={{0,8},{4,12},{1,9},{5,13},{2,10},{6,14},{3,11},{7,15}} | collective-permute-start | bytes 786440 | tf_op jit(solution)/shard_map/ppermute | solution.py:263
  19.8 5.6 %copy-start.7 = (bf16[8,128,128]{2,1,0:T(8,128)(2,1)}, bf16[8,128,128]{2,1,0:T(8,128)(2,1)S(1)}, u32[]{:S(2)}) copy-start(bf16[8,128,128]{2,1,0:T(8,128)(2,1)S(1)} %collective-permute-done.1) | copy-start | bytes 786436
  19.9 7.7 %copy-start.1 = (bf16[256,1024]{1,0:T(8,128)(2,1)S(1)}, bf16[256,1024]{1,0:T(8,128)(2,1)}, u32[]{:S(2)}) copy-start(bf16[256,1024]{1,0:T(8,128)(2,1)} %q_ref.3) | copy-start | bytes 1572868
  19.9 7.7 %copy-start.3 = (bf16[256,1024]{1,0:T(8,128)(2,1)S(1)}, bf16[256,1024]{1,0:T(8,128)(2,1)}, u32[]{:S(2)}) copy-start(bf16[256,1024]{1,0:T(8,128)(2,1)} %k_ref.3) | copy-start | bytes 1572868
  19.9 5.5 %collective-permute-start.2 = (bf16[8,128,128]{2,1,0:T(8,128)(2,1)S(1)}, bf16[8,128,128]{2,1,0:T(8,128)(2,1)S(1)}, u32[]{:S(2)}, u32[]{:S(2)}) collective-permute-start(bf16[8,128,128]{2,1,0:T(8,128)(2,1)S(1)} %fusion.2), channel_id=1, source_target_pairs={{8,16},{12,20},{9,17},{13,21},{10,18},{14,22},{11,19},{15,23}} | collective-permute-start | bytes 786440 | tf_op jit(solution)/shard_map/ppermute | solution.py:263
  21.4 23.2 %collective-permute-start.5 = (bf16[1024,512]{1,0:T(8,128)(2,1)S(1)}, bf16[1024,512]{1,0:T(8,128)(2,1)S(1)}, u32[]{:S(2)}, u32[]{:S(2)}) collective-permute-start(bf16[1024,512]{1,0:T(8,128)(2,1)S(1)} %copy-done), channel_id=1, source_target_pairs={{0,4},{4,0},{8,12},{12,8},{16,20},{20,16},{24,28},{28,24},{1,5},{5... | collective-permute-start | bytes 3145736 | tf_op jit(solution)/shard_map/ppermute | solution.py:236
  25.4 0.8 copy-start.9
  26.2 3.3 %collective-permute-start.3 = (bf16[8,128,128]{2,1,0:T(8,128)(2,1)}, bf16[8,128,128]{2,1,0:T(8,128)(2,1)}, u32[]{:S(2)}, u32[]{:S(2)}) collective-permute-start(bf16[8,128,128]{2,1,0:T(8,128)(2,1)} %add_convert_fusion.4), channel_id=1, source_target_pairs={{16,24},{20,28},{17,25},{21,29},{18,26},{22,30},{19,27},{23,31}} | collective-permute-start | bytes 786440 | tf_op jit(solution)/shard_map/ppermute | solution.py:263
  27.6 1.0 copy-start.5
  28.6 1.0 copy-start.8
  28.6 1.0 copy-start.10
  29.7 1.1 copy-start.6
  32.3 30.9 %collective-permute-start.4 = (bf16[256,1024]{1,0:T(8,128)(2,1)}, bf16[256,1024]{1,0:T(8,128)(2,1)}, u32[]{:S(2)}, u32[]{:S(2)}) collective-permute-start(bf16[256,1024]{1,0:T(8,128)(2,1)} %get-tuple-element.14.even_ref), channel_id=1, source_target_pairs={{0,8},{4,12},{8,0},{12,4},{16,24},{20,28},{24,16},{28,20},{1,9},{5... | collective-permute-start | bytes 1572872 | tf_op jit(solution)/shard_map/ppermute | solution.py:236
  32.3 24.0 %collective-permute-start.9 = (bf16[128,1024]{1,0:T(8,128)(2,1)S(1)}, bf16[128,1024]{1,0:T(8,128)(2,1)S(1)}, u32[]{:S(2)}, u32[]{:S(2)}) collective-permute-start(bf16[128,1024]{1,0:T(8,128)(2,1)S(1)} %get-tuple-element.17), channel_id=1, source_target_pairs={{0,16},{4,20},{8,24},{12,28},{16,0},{20,4},{24,8},{28,12},{1,17},{... | collective-permute-start | bytes 786440 | tf_op jit(solution)/shard_map/ppermute | solution.py:236
  38.8 20.4 %collective-permute-start.10 = (bf16[128,1024]{1,0:T(8,128)(2,1)S(1)}, bf16[128,1024]{1,0:T(8,128)(2,1)S(1)}, u32[]{:S(2)}, u32[]{:S(2)}) collective-permute-start(bf16[128,1024]{1,0:T(8,128)(2,1)S(1)} %get-tuple-element.18), channel_id=1, source_target_pairs={{0,16},{4,20},{8,24},{12,28},{16,0},{20,4},{24,8},{28,12},{1,17},{... | collective-permute-start | bytes 786440 | tf_op jit(solution)/shard_map/ppermute | solution.py:236
  59.9 18.7 %collective-permute-start.11 = (bf16[2,256,512]{2,1,0:T(8,128)(2,1)S(1)}, bf16[2,256,512]{2,1,0:T(8,128)(2,1)}, u32[]{:S(2)}, u32[]{:S(2)}) collective-permute-start(bf16[2,256,512]{2,1,0:T(8,128)(2,1)S(1)} %shard_map.59), channel_id=1, source_target_pairs={{1,0},{3,2},{5,4},{7,6},{9,8},{11,10},{13,12},{15,14},{17,16},{19,... | collective-permute-start | bytes 1572872 | tf_op jit(solution)/shard_map/ppermute | solution.py:240
  61.2 8.4 %collective-permute-start.14 = (bf16[128,1024]{1,0:T(8,128)(2,1)S(1)}, bf16[128,1024]{1,0:T(8,128)(2,1)S(1)}, u32[]{:S(2)}, u32[]{:S(2)}) collective-permute-start(bf16[128,1024]{1,0:T(8,128)(2,1)S(1)} %collective-permute-done.9.top_ref), channel_id=1, source_target_pairs={{0,8},{4,12},{8,0},{12,4},{16,24},{20,28},{24,16},{28,20},{1,9},{5... | collective-permute-start | bytes 786440 | tf_op jit(solution)/shard_map/ppermute | solution.py:236
  62.7 12.5 %collective-permute-start.15 = (bf16[128,1024]{1,0:T(8,128)(2,1)S(1)}, bf16[128,1024]{1,0:T(8,128)(2,1)S(1)}, u32[]{:S(2)}, u32[]{:S(2)}) collective-permute-start(bf16[128,1024]{1,0:T(8,128)(2,1)S(1)} %collective-permute-done.10.bottom_ref), channel_id=1, source_target_pairs={{0,8},{4,12},{8,0},{12,4},{16,24},{20,28},{24,16},{28,20},{1,9},{5... | collective-permute-start | bytes 786440 | tf_op jit(solution)/shard_map/ppermute | solution.py:236
  65.7 18.0 %collective-permute-start.6 = (bf16[2,256,512]{2,1,0:T(8,128)(2,1)S(1)}, bf16[2,256,512]{2,1,0:T(8,128)(2,1)S(1)}, u32[]{:S(2)}, u32[]{:S(2)}) collective-permute-start(bf16[2,256,512]{2,1,0:T(8,128)(2,1)S(1)} %get-tuple-element.16), channel_id=1, source_target_pairs={{0,1},{1,0},{2,3},{3,2},{4,5},{5,4},{6,7},{7,6},{8,9},{9,8},{10,11... | collective-permute-start | bytes 1572872 | tf_op jit(solution)/shard_map/ppermute | solution.py:240
  75.9 10.0 %collective-permute-start.16 = (bf16[2,256,512]{2,1,0:T(8,128)(2,1)S(1)}, bf16[2,256,512]{2,1,0:T(8,128)(2,1)S(1)}, u32[]{:S(2)}, u32[]{:S(2)}) collective-permute-start(bf16[2,256,512]{2,1,0:T(8,128)(2,1)S(1)} %shard_map.60), channel_id=1, source_target_pairs={{0,1},{2,3},{4,5},{6,7},{8,9},{10,11},{12,13},{14,15},{16,17},{18,... | collective-permute-start | bytes 1572872 | tf_op jit(solution)/shard_map/ppermute | solution.py:240
  79.7 23.4 %collective-permute-start.13 = (bf16[2,256,512]{2,1,0:T(8,128)(2,1)S(1)}, bf16[2,256,512]{2,1,0:T(8,128)(2,1)S(1)}, u32[]{:S(2)}, u32[]{:S(2)}) collective-permute-start(bf16[2,256,512]{2,1,0:T(8,128)(2,1)S(1)} %add_convert_fusion.2), channel_id=1, source_target_pairs={{2,16},{6,20},{10,25},{14,29},{18,2},{22,6},{26,11},{30,15}} | collective-permute-start | bytes 1572872 | tf_op jit(solution)/shard_map/ppermute | solution.py:240
  83.0 21.4 %collective-permute-start.12 = (bf16[2,256,512]{2,1,0:T(8,128)(2,1)S(1)}, bf16[2,256,512]{2,1,0:T(8,128)(2,1)S(1)}, u32[]{:S(2)}, u32[]{:S(2)}) collective-permute-start(bf16[2,256,512]{2,1,0:T(8,128)(2,1)S(1)} %add_convert_fusion.2), channel_id=1, source_target_pairs={{0,16},{4,20},{8,25},{12,29},{16,2},{20,6},{24,11},{28,15}} | collective-permute-start | bytes 1572872 | tf_op jit(solution)/shard_map/ppermute | solution.py:240
  83.8 20.6 %collective-permute-start.8 = (bf16[2,256,512]{2,1,0:T(8,128)(2,1)S(1)}, bf16[2,256,512]{2,1,0:T(8,128)(2,1)S(1)}, u32[]{:S(2)}, u32[]{:S(2)}) collective-permute-start(bf16[2,256,512]{2,1,0:T(8,128)(2,1)S(1)} %add_convert_fusion.3), channel_id=1, source_target_pairs={{2,0},{3,8},{6,4},{7,12},{10,9},{11,1},{14,13},{15,5},{18,18},{19,... | collective-permute-start | bytes 1572872 | tf_op jit(solution)/shard_map/ppermute | solution.py:240
  85.2 19.3 %collective-permute-start.7 = (bf16[2,256,512]{2,1,0:T(8,128)(2,1)S(1)}, bf16[2,256,512]{2,1,0:T(8,128)(2,1)S(1)}, u32[]{:S(2)}, u32[]{:S(2)}) collective-permute-start(bf16[2,256,512]{2,1,0:T(8,128)(2,1)S(1)} %add_convert_fusion.3), channel_id=1, source_target_pairs={{0,0},{1,8},{4,4},{5,12},{8,9},{9,1},{12,13},{13,5},{16,18},{17,26... | collective-permute-start | bytes 1572872 | tf_op jit(solution)/shard_map/ppermute | solution.py:240
  86.8 21.0 %collective-permute-start.18 = (bf16[2,256,512]{2,1,0:T(8,128)(2,1)}, bf16[2,256,512]{2,1,0:T(8,128)(2,1)}, u32[]{:S(2)}, u32[]{:S(2)}) collective-permute-start(bf16[2,256,512]{2,1,0:T(8,128)(2,1)} %add_convert_fusion.1), channel_id=1, source_target_pairs={{3,24},{7,28},{11,17},{15,21},{19,10},{23,14},{27,3},{31,7}} | collective-permute-start | bytes 1572872 | tf_op jit(solution)/shard_map/ppermute | solution.py:240
  103.1 17.3 %collective-permute-start.17 = (bf16[2,256,512]{2,1,0:T(8,128)(2,1)}, bf16[2,256,512]{2,1,0:T(8,128)(2,1)}, u32[]{:S(2)}, u32[]{:S(2)}) collective-permute-start(bf16[2,256,512]{2,1,0:T(8,128)(2,1)} %add_convert_fusion.1), channel_id=1, source_target_pairs={{1,24},{5,28},{9,17},{13,21},{17,10},{21,14},{25,3},{29,7}} | collective-permute-start | bytes 1572872 | tf_op jit(solution)/shard_map/ppermute | solution.py:240

commit v7 on v5

--- a/solution.py
+++ b/solution.py
@@ -1,3 +1,5 @@
+import functools
+
 import jax
 import jax.numpy as jnp
 from jax import lax
@@ -185,22 +187,28 @@
     return body
 
 
-def project_kernel(pick_ref, tokens_ref, near_a, near_b, far_a, far_b, keep_ref, send_ref):
-    def multiply(out_ref, weights):
-        for half, weight_ref in enumerate(weights):
-            out_ref[half] = jnp.dot(
-                tokens_ref[...], weight_ref[...], preferred_element_type=F32
-            ).astype(BF16)
-
-    @pl.when(pick_ref[0] == 1)
+def multiply_tile(first, second, weights, out_ref):
+    for half in range(2):
+        total = jnp.dot(first, weights[half][...], preferred_element_type=F32)
+        total += jnp.dot(second, weights[2 + half][...], preferred_element_type=F32)
+        out_ref[half] = total.astype(BF16)
+
+
+def project_both_kernel(core_ref, even_a, even_b, odd_a, odd_b, *refs):
+    even = core_ref[0] == 0
+    first = jnp.where(even, even_a[...], odd_a[...])
+    second = jnp.where(even, even_b[...], odd_b[...])
+    multiply_tile(first, second, refs[:4], refs[4])
+
+
+def project_one_kernel(wanted, core_ref, a_ref, b_ref, *refs):
+    @pl.when(core_ref[0] == wanted)
     def _():
-        multiply(keep_ref, (near_a, near_b))
-        multiply(send_ref, (far_a, far_b))
-
-    @pl.when(pick_ref[0] != 1)
+        multiply_tile(a_ref[...], b_ref[...], refs[:4], refs[4])
+
+    @pl.when(core_ref[0] != wanted)
     def _():
-        multiply(keep_ref, (far_a, far_b))
-        multiply(send_ref, (near_a, near_b))
+        refs[4][...] = jnp.zeros_like(refs[4])
 
 
 def pairs_body(queries, key_vectors, value_vectors, norm_gain, out_weight):
@@ -222,6 +230,9 @@
     def move(value, place_of, chosen=lambda z, y, x, c: True):
         pairs = [(at(*d), at(*place_of(*d))) for d in devices if chosen(*d)]
         return lax.ppermute(value, both, pairs)
+
+    def swap_cores(value):
+        return move(value, lambda z, y, x, c: (z, y, x, 1 - c))
 
     wide, narrow = call(
         state_kernel,
@@ -236,8 +247,8 @@
         within_kernel, jax.ShapeDtypeStruct((rows, features), F32), 4 * size * BLOCK, 10 * size
     )(queries, key_vectors, value_vectors)
 
-    near_mate = swap(out_weight, 1)
-    far_own = swap(out_weight, 2)
+    mate_weight = swap(out_weight, 1)
+    weights = (out_weight, mate_weight, swap_cores(out_weight), swap_cores(mate_weight))
 
     mate = swap(narrow, 1).astype(F32)
     total = wide + mate
@@ -251,35 +262,51 @@
         attend_kernel, jax.ShapeDtypeStruct((rows, features), BF16), 2 * size * HD, 8 * size
     )(queries, within, state_in, norm_gain[None])
 
-    remote = swap(attended, 4)
-    far_mate = swap(far_own, 1)
-    pick = (core == z % 2).astype(jnp.int32)[None]
-
-    def projected(tokens):
-        tile = jax.ShapeDtypeStruct((2, rows, half_cols), BF16)
-        vmem = pl.BlockSpec(memory_space=pltpu.VMEM)
-        keep, send = pl.pallas_call(
-            project_kernel,
-            out_shape=(tile, tile),
-            in_specs=[pl.BlockSpec(memory_space=pltpu.SMEM)] + [vmem] * 5,
-            out_specs=(vmem, vmem),
+    hops = (2, 1)
+    from_same = move(attended, lambda z, y, x, c: (z ^ hops[c], y, x, c))
+    from_other = move(attended, lambda z, y, x, c: (z ^ hops[1 - c], y, x, 1 - c))
+    beside = move(attended, lambda z, y, x, c: (z, y, x, 0), lambda z, y, x, c: c == 1)
+    on_core_one = lambda z, y, x, c: (z ^ 1, y, x, 1)
+    passed_a = move(from_same, on_core_one, lambda z, y, x, c: c == 0)
+    passed_b = move(from_other, on_core_one, lambda z, y, x, c: c == 0)
+
+    vmem = pl.BlockSpec(memory_space=pltpu.VMEM)
+    which = core.astype(jnp.int32)[None]
+
+    def project(kernel, *tokens):
+        return pl.pallas_call(
+            kernel,
+            out_shape=jax.ShapeDtypeStruct((2, rows, half_cols), BF16),
+            in_specs=[pl.BlockSpec(memory_space=pltpu.SMEM)] + [vmem] * (len(tokens) + 4),
+            out_specs=vmem,
             compiler_params=pltpu.CompilerParams(vmem_limit_bytes=24 * 1024 * 1024),
             cost_estimate=pl.CostEstimate(
-                flops=8 * size * half_cols, bytes_accessed=12 * size, transcendentals=0
+                flops=8 * size * half_cols, bytes_accessed=14 * size, transcendentals=0
             ),
-        )(pick, tokens, out_weight, near_mate, far_own, far_mate)
-        got = move(send, lambda z, y, x, c: (z, y, x, 1 - c))
-        return keep.astype(F32) + got.astype(F32)
-
-    at_home = lambda z, y, x, c: x == z // 2
-    away = lambda z, y, x, c: x != z // 2
-    own = projected(attended)
-    from_x = move(own.astype(BF16), lambda z, y, x, c: (z, y, 1 - x, c), away)
-    other = projected(remote).astype(BF16)
-    straight = move(other, lambda z, y, x, c: (z ^ 2, y, x, c), at_home)
-    across = move(other, lambda z, y, x, c: (z ^ 2, y, 1 - x, c), away)
-    result = jnp.where(x == z // 2, own, 0.0) + from_x.astype(F32)
-    result = (result + straight.astype(F32) + across.astype(F32)).astype(BF16)
+        )(which, *tokens, *weights)
+
+    two = project(functools.partial(project_one_kernel, 0), from_same, from_other)
+    near = project(project_both_kernel, attended, beside, from_same, from_other)
+    three = project(functools.partial(project_one_kernel, 1), passed_b, passed_a)
+
+    def along_z(value, masks):
+        return move(
+            value,
+            lambda z, y, x, c: (z ^ masks[c], y, x, z % 2),
+            lambda z, y, x, c: masks[c] is not None,
+        )
+
+    def across_x(value, chosen):
+        return move(value, lambda z, y, x, c: (z, y, 1 - x, c), chosen).astype(F32)
+
+    two = along_z(two, (2, None))
+    near = along_z(near, (0, 1))
+    three = along_z(three, (None, 3))
+    near_sum = near.astype(F32) + across_x(near, lambda z, y, x, c: x != z // 2)
+    far_sum = two.astype(F32) + across_x(two, lambda z, y, x, c: x == z // 2 and c == z % 2)
+    far_sum += three.astype(F32)
+    far_sum += across_x(three, lambda z, y, x, c: x == z // 2 and c != z % 2)
+    result = jnp.where(x == z // 2, near_sum, far_sum).astype(BF16)
     first = jnp.where(y == 0, result[0], result[1])
     return jnp.concatenate([first, jnp.where(y == 0, result[1], result[0])], axis=1)
 

time: 128 us -> 122 us (0.953)
  the two profiles are of different devices: /device:TPU:3 before, /device:TPU:10 now
where the time goes in v7:
time: 122 us; the launch traced here: 121 us
  waiting for transfers between devices  72.6 us (60%)
  starting transfers between devices  27.8 us (23%)
  Pallas kernels  10.3 us (8%)
  local copies, waits for them, and re-layouts  5.32 us (4%)
  other arithmetic  4.6 us (4%)
    ppermute x13, waiting for transfers between devices, move(): return lax.ppermute(value, both, pairs)  51.3 us
    ppermute x13, starting transfers between devices, move(): return lax.ppermute(value, both, pairs)  20.7 us
    ppermute x2, waiting for transfers between devices, swap(): return lax.ppermute(value, 'seq', [(s, s ^ mask) for s in range(8)])  11.2 us
    ppermute x3, waiting for transfers between devices, pairs_body(): before += lax.ppermute(onward, 'seq', pairs).astype(F32)  10.2 us
    pallas_call x3, Pallas kernels, project(): pl.pallas_call(kernel, out_shape=jax.ShapeDtypeStruct((2, rows, half_cols...  7.48 us
    unnamed x22, local copies, waits for them, and re-layouts  5.32 us
    ppermute x3, starting transfers between devices, pairs_body(): before += lax.ppermute(onward, 'seq', pairs).astype(F32)  3.97 us
    ppermute x2, starting transfers between devices, swap(): return lax.ppermute(value, 'seq', [(s, s ^ mask) for s in range(8)])  3.17 us
  transfers between devices with their start and end apart: 18, of which 8 were waited for; matrix products, arithmetic and copies ran while one was open for 2% of the time, Pallas kernels for 8%

profile of v7, /device:TPU:10, one launch (start us, length us, event | category | flops | bytes accessed | tf_op | source)
XLA Modules:
  0.0 121.0 jit_solution(10454567004246659205)
XLA Ops:
  0.0 0.0 copy-start
  0.0 0.0 copy-start.1
  0.0 1.1 copy-done.1
  1.1 0.0 copy-start.3
  1.1 1.0 copy-done.3
  2.2 0.4 shard_map.56
  2.5 1.6 %collective-permute-start = (bf16[8,128,128]{2,1,0:T(8,128)(2,1)S(1)}, bf16[8,128,128]{2,1,0:T(8,128)(2,1)S(1)}, u32[]{:S(2)}, u32[]{:S(2)}) collective-permute-start(bf16[8,128,128]{2,1,0:T(8,128)(2,1)S(1)} %get-tuple-element.8), channel_id=1, source_target_pairs={{0,4},{4,0},{8,12},{12,8},{16,20},{20,16},{24,28},{28,24},{1,5},{5... | collective-permute-start | bytes 786440 | tf_op jit(solution)/shard_map/ppermute | solution.py:228
  4.1 6.5 %collective-permute-done = bf16[8,128,128]{2,1,0:T(8,128)(2,1)S(1)} collective-permute-done((bf16[8,128,128]{2,1,0:T(8,128)(2,1)S(1)}, bf16[8,128,128]{2,1,0:T(8,128)(2,1)S(1)}, u32[]{:S(2)}, u32[]{:S(2)}) %collective-permute-start) | collective-permute-done | bytes 262176 | tf_op jit(solution)/shard_map/ppermute | solution.py:228
  10.6 0.1 fusion.3
  10.7 1.3 %collective-permute-start.1 = (bf16[8,128,128]{2,1,0:T(8,128)(2,1)S(1)}, bf16[8,128,128]{2,1,0:T(8,128)(2,1)S(1)}, u32[]{:S(2)}, u32[]{:S(2)}) collective-permute-start(bf16[8,128,128]{2,1,0:T(8,128)(2,1)S(1)} %fusion.3), channel_id=1, source_target_pairs={{0,8},{4,12},{1,9},{5,13},{2,10},{6,14},{3,11},{7,15}} | collective-permute-start | bytes 786440 | tf_op jit(solution)/shard_map/ppermute | solution.py:259
  12.0 0.0 copy-done
  12.0 1.6 %collective-permute-start.7 = (bf16[1024,512]{1,0:T(8,128)(2,1)S(1)}, bf16[1024,512]{1,0:T(8,128)(2,1)S(1)}, u32[]{:S(2)}, u32[]{:S(2)}) collective-permute-start(bf16[1024,512]{1,0:T(8,128)(2,1)S(1)} %copy-done), channel_id=1, source_target_pairs={{0,4},{4,0},{8,12},{12,8},{16,20},{20,16},{24,28},{28,24},{1,5},{5... | collective-permute-start | bytes 3145736 | tf_op jit(solution)/shard_map/ppermute | solution.py:228
  13.6 6.2 %collective-permute-done.1 = bf16[8,128,128]{2,1,0:T(8,128)(2,1)S(1)} collective-permute-done((bf16[8,128,128]{2,1,0:T(8,128)(2,1)S(1)}, bf16[8,128,128]{2,1,0:T(8,128)(2,1)S(1)}, u32[]{:S(2)}, u32[]{:S(2)}) %collective-permute-start.1) | collective-permute-done | bytes 262176 | tf_op jit(solution)/shard_map/ppermute | solution.py:259
  19.8 0.0 copy-start.7
  19.8 0.1 fusion.2
  19.9 1.3 %collective-permute-start.2 = (bf16[8,128,128]{2,1,0:T(8,128)(2,1)S(1)}, bf16[8,128,128]{2,1,0:T(8,128)(2,1)S(1)}, u32[]{:S(2)}, u32[]{:S(2)}) collective-permute-start(bf16[8,128,128]{2,1,0:T(8,128)(2,1)S(1)} %fusion.2), channel_id=1, source_target_pairs={{8,16},{12,20},{9,17},{13,21},{10,18},{14,22},{11,19},{15,23}} | collective-permute-start | bytes 786440 | tf_op jit(solution)/shard_map/ppermute | solution.py:259
  21.2 4.0 %collective-permute-done.2 = bf16[8,128,128]{2,1,0:T(8,128)(2,1)S(1)} collective-permute-done((bf16[8,128,128]{2,1,0:T(8,128)(2,1)S(1)}, bf16[8,128,128]{2,1,0:T(8,128)(2,1)S(1)}, u32[]{:S(2)}, u32[]{:S(2)}) %collective-permute-start.2) | collective-permute-done | bytes 262176 | tf_op jit(solution)/shard_map/ppermute | solution.py:259
  25.2 0.0 copy-done.7
  25.2 0.8 add_convert_fusion
  26.0 0.0 copy-done.9
  26.0 1.4 %collective-permute-start.3 = (bf16[8,128,128]{2,1,0:T(8,128)(2,1)}, bf16[8,128,128]{2,1,0:T(8,128)(2,1)}, u32[]{:S(2)}, u32[]{:S(2)}) collective-permute-start(bf16[8,128,128]{2,1,0:T(8,128)(2,1)} %add_convert_fusion), channel_id=1, source_target_pairs={{16,24},{20,28},{17,25},{21,29},{18,26},{22,30},{19,27},{23,31}} | collective-permute-start | bytes 786440 | tf_op jit(solution)/shard_map/ppermute | solution.py:259
  27.4 0.0 collective-permute-start.8
  27.4 1.0 copy-done.2
  28.4 1.0 copy-done.4
  29.5 1.0 copy-done.5
  30.5 0.9 shard_map.55.within_ref
  31.5 4.6 %collective-permute-done.7.refs_1_ = bf16[1024,512]{1,0:T(8,128)(2,1)S(1)} collective-permute-done((bf16[1024,512]{1,0:T(8,128)(2,1)S(1)}, bf16[1024,512]{1,0:T(8,128)(2,1)S(1)}, u32[]{:S(2)}, u32[]{:S(2)}) %collective-permute-start.7) | collective-permute-done | bytes 1048608 | tf_op jit(solution)/shard_map/ppermute | solution.py:228
  36.1 0.0 collective-permute-start.9
  36.1 0.0 collective-permute-done.3
  36.1 0.0 copy-done.8
  36.1 0.0 copy-done.10
  36.1 0.0 copy-start.6
  36.1 1.1 fusion.1.state_ref
  37.3 0.0 copy-done.6
  37.3 1.5 %shard_map.57.even_a = bf16[256,1024]{1,0:T(8,128)(2,1)} custom-call(bf16[256,1024]{1,0:T(8,128)(2,1)S(1)} %copy-done.5, f32[256,1024]{1,0:T(8,128)S(1)} %shard_map.55.within_ref, bf16[8,128,128]{2,1,0:T(8,128)(2,1)S(1)} %fusion.1.state_ref, f32[1,1024]{1,0:T(1,128)S(1)} %bitcast.6), custom_call_target="tpu_custom_call" | custom-call | flops 67108864 | bytes 2097152 | tf_op jit(solution)/shard_map/pallas_call | solution.py:261
  38.8 2.5 %collective-permute-start.6 = (bf16[256,1024]{1,0:T(8,128)(2,1)}, bf16[256,1024]{1,0:T(8,128)(2,1)}, u32[]{:S(2)}, u32[]{:S(2)}) collective-permute-start(bf16[256,1024]{1,0:T(8,128)(2,1)} %shard_map.57.even_a), channel_id=1, source_target_pairs={{0,9},{1,16},{2,11},{3,18},{4,13},{5,20},{6,15},{7,22},{8,1},{9,24... | collective-permute-start | bytes 1572872 | tf_op jit(solution)/shard_map/ppermute | solution.py:232
  41.3 0.1 collective-permute-start.5
  41.3 1.3 %collective-permute-start.4 = (bf16[256,1024]{1,0:T(8,128)(2,1)}, bf16[256,1024]{1,0:T(8,128)(2,1)}, u32[]{:S(2)}, u32[]{:S(2)}) collective-permute-start(bf16[256,1024]{1,0:T(8,128)(2,1)} %shard_map.57.even_a), channel_id=1, source_target_pairs={{1,0},{3,2},{5,4},{7,6},{9,8},{11,10},{13,12},{15,14},{17,16},{19,... | collective-permute-start | bytes 1572872 | tf_op jit(solution)/shard_map/ppermute | solution.py:232
  42.6 21.4 %collective-permute-done.6.odd_b.b_ref = bf16[256,1024]{1,0:T(8,128)(2,1)} collective-permute-done((bf16[256,1024]{1,0:T(8,128)(2,1)}, bf16[256,1024]{1,0:T(8,128)(2,1)}, u32[]{:S(2)}, u32[]{:S(2)}) %collective-permute-start.6) | collective-permute-done | bytes 524320 | tf_op jit(solution)/shard_map/ppermute | solution.py:232
  64.1 5.0 %collective-permute-start.14 = (bf16[256,1024]{1,0:T(8,128)(2,1)}, bf16[256,1024]{1,0:T(8,128)(2,1)}, u32[]{:S(2)}, u32[]{:S(2)}) collective-permute-start(bf16[256,1024]{1,0:T(8,128)(2,1)} %collective-permute-done.6.odd_b.b_ref), channel_id=1, source_target_pairs={{0,9},{2,11},{4,13},{6,15},{8,1},{10,3},{12,5},{14,7},{16,25},{18,... | collective-permute-start | bytes 1572872 | tf_op jit(solution)/shard_map/ppermute | solution.py:232
  69.1 0.0 collective-permute-done.5.odd_a.a_ref
  69.1 2.1 %collective-permute-start.15 = (bf16[256,1024]{1,0:T(8,128)(2,1)}, bf16[256,1024]{1,0:T(8,128)(2,1)}, u32[]{:S(2)}, u32[]{:S(2)}) collective-permute-start(bf16[256,1024]{1,0:T(8,128)(2,1)} %collective-permute-done.5.odd_a.a_ref), channel_id=1, source_target_pairs={{0,9},{2,11},{4,13},{6,15},{8,1},{10,3},{12,5},{14,7},{16,25},{18,... | collective-permute-start | bytes 1572872 | tf_op jit(solution)/shard_map/ppermute | solution.py:232
  71.2 0.0 collective-permute-done.8.refs_2_
  71.2 0.0 collective-permute-done.9.refs_3_
  71.2 2.8 %shard_map.59 = bf16[2,256,512]{2,1,0:T(8,128)(2,1)S(1)} custom-call(s32[1]{0:T(128)} %bitcast.core_ref, bf16[256,1024]{1,0:T(8,128)(2,1)} %collective-permute-done.5.odd_a.a_ref, bf16[256,1024]{1,0:T(8,128)(2,1)} %collective-permute-done.6.odd_b.b_ref, bf16[1024,512]{1,0:T(8,128)(2,1)S(1)} %copy-done, bf16[1024,512]{1,0:T(8,128)(2,1)S(1)} %collective-permute-done.7.refs_1_, ...), custom_call_target="tpu_custom_call" | custom-call | flops 1073741824 | bytes 3670016 | tf_op jit(solution)/shard_map/pallas_call | solution.py:277
  74.0 2.1 %collective-permute-start.12 = (bf16[2,256,512]{2,1,0:T(8,128)(2,1)S(1)}, bf16[2,256,512]{2,1,0:T(8,128)(2,1)}, u32[]{:S(2)}, u32[]{:S(2)}) collective-permute-start(bf16[2,256,512]{2,1,0:T(8,128)(2,1)S(1)} %shard_map.59), channel_id=1, source_target_pairs={{0,16},{2,18},{4,20},{6,22},{8,25},{10,27},{12,29},{14,31},{16,0},... | collective-permute-start | bytes 1572872 | tf_op jit(solution)/shard_map/ppermute | solution.py:232
  76.1 0.0 collective-permute-done.4.even_b
  76.1 3.1 %shard_map.58 = bf16[2,256,512]{2,1,0:T(8,128)(2,1)S(1)} custom-call(s32[1]{0:T(128)} %bitcast.core_ref, bf16[256,1024]{1,0:T(8,128)(2,1)} %shard_map.57.even_a, bf16[256,1024]{1,0:T(8,128)(2,1)} %collective-permute-done.4.even_b, bf16[256,1024]{1,0:T(8,128)(2,1)} %collective-permute-done.5.odd_a.a_ref, ...), custom_call_target="tpu_custom_call" | custom-call | flops 1073741824 | bytes 3670016 | tf_op jit(solution)/shard_map/pallas_call | solution.py:277
  79.2 1.9 %collective-permute-start.10 = (bf16[2,256,512]{2,1,0:T(8,128)(2,1)S(1)}, bf16[2,256,512]{2,1,0:T(8,128)(2,1)}, u32[]{:S(2)}, u32[]{:S(2)}) collective-permute-start(bf16[2,256,512]{2,1,0:T(8,128)(2,1)S(1)} %shard_map.58), channel_id=1, source_target_pairs={{0,0},{1,8},{2,2},{3,10},{4,4},{5,12},{6,6},{7,14},{8,9},{9,1},{10... | collective-permute-start | bytes 1572872 | tf_op jit(solution)/shard_map/ppermute | solution.py:232
  81.2 0.0 collective-permute-done.14.a_ref
  81.2 8.5 %collective-permute-done.15.b_ref = bf16[256,1024]{1,0:T(8,128)(2,1)} collective-permute-done((bf16[256,1024]{1,0:T(8,128)(2,1)}, bf16[256,1024]{1,0:T(8,128)(2,1)}, u32[]{:S(2)}, u32[]{:S(2)}) %collective-permute-start.15) | collective-permute-done | bytes 524320 | tf_op jit(solution)/shard_map/ppermute | solution.py:232
  89.7 1.6 %shard_map.60 = bf16[2,256,512]{2,1,0:T(8,128)(2,1)S(1)} custom-call(s32[1]{0:T(128)} %bitcast.core_ref, bf16[256,1024]{1,0:T(8,128)(2,1)} %collective-permute-done.14.a_ref, bf16[256,1024]{1,0:T(8,128)(2,1)} %collective-permute-done.15.b_ref, bf16[1024,512]{1,0:T(8,128)(2,1)S(1)} %copy-done, bf16[1024,512]{1,0:T(8,128)(2,1)S(1)} %collective-permute-done.7.refs_1_, ...), custom_call_target="tpu_custom_call" | custom-call | flops 1073741824 | bytes 3670016 | tf_op jit(solution)/shard_map/pallas_call | solution.py:277
  91.2 1.3 %collective-permute-start.16 = (bf16[2,256,512]{2,1,0:T(8,128)(2,1)S(1)}, bf16[2,256,512]{2,1,0:T(8,128)(2,1)S(1)}, u32[]{:S(2)}, u32[]{:S(2)}) collective-permute-start(bf16[2,256,512]{2,1,0:T(8,128)(2,1)S(1)} %shard_map.60), channel_id=1, source_target_pairs={{1,24},{3,26},{5,28},{7,30},{9,17},{11,19},{13,21},{15,23},{17,8},... | collective-permute-start | bytes 1572872 | tf_op jit(solution)/shard_map/ppermute | solution.py:232
  92.5 0.0 collective-permute-done.12
  92.6 0.7 collective-permute-start.13
  93.3 0.0 collective-permute-done.10
  93.3 2.5 %collective-permute-start.11 = (bf16[2,256,512]{2,1,0:T(8,128)(2,1)}, bf16[2,256,512]{2,1,0:T(8,128)(2,1)S(1)}, u32[]{:S(2)}, u32[]{:S(2)}) collective-permute-start(bf16[2,256,512]{2,1,0:T(8,128)(2,1)} %collective-permute-done.10), channel_id=1, source_target_pairs={{2,0},{3,1},{6,4},{7,5},{10,8},{11,9},{14,12},{15,13},{16,18},{17,... | collective-permute-start | bytes 1572872 | tf_op jit(solution)/shard_map/ppermute | solution.py:232
  95.7 11.6 %collective-permute-done.16 = bf16[2,256,512]{2,1,0:T(8,128)(2,1)S(1)} collective-permute-done((bf16[2,256,512]{2,1,0:T(8,128)(2,1)S(1)}, bf16[2,256,512]{2,1,0:T(8,128)(2,1)S(1)}, u32[]{:S(2)}, u32[]{:S(2)}) %collective-permute-start.16) | collective-permute-done | bytes 524320 | tf_op jit(solution)/shard_map/ppermute | solution.py:232
  107.4 1.3 %collective-permute-start.17 = (bf16[2,256,512]{2,1,0:T(8,128)(2,1)S(1)}, bf16[2,256,512]{2,1,0:T(8,128)(2,1)S(1)}, u32[]{:S(2)}, u32[]{:S(2)}) collective-permute-start(bf16[2,256,512]{2,1,0:T(8,128)(2,1)S(1)} %collective-permute-done.16), channel_id=1, source_target_pairs={{1,3},{5,7},{8,10},{12,14},{19,17},{23,21},{26,24},{30,28}} | collective-permute-start | bytes 1572872 | tf_op jit(solution)/shard_map/ppermute | solution.py:232
  108.7 0.0 collective-permute-done.13
  108.7 0.0 collective-permute-done.11
  108.7 9.7 %collective-permute-done.17 = bf16[2,256,512]{2,1,0:T(8,128)(2,1)S(1)} collective-permute-done((bf16[2,256,512]{2,1,0:T(8,128)(2,1)S(1)}, bf16[2,256,512]{2,1,0:T(8,128)(2,1)S(1)}, u32[]{:S(2)}, u32[]{:S(2)}) %collective-permute-start.17) | collective-permute-done | bytes 524320 | tf_op jit(solution)/shard_map/ppermute | solution.py:232
  118.4 1.6 %select_convert_fusion = bf16[2,256,512]{2,1,0:T(8,128)(2,1)S(1)} fusion(bf16[2,256,512]{2,1,0:T(8,128)(2,1)S(1)} %collective-permute-done.17, bf16[2,256,512]{2,1,0:T(8,128)(2,1)S(1)} %collective-permute-done.16, bf16[2,256,512]{2,1,0:T(8,128)(2,1)S(1)} %collective-permute-done.13, bf16[2,256,512]{2,1,0:T(8,128)(2,1)} %collective-permute-done.12, ...), kind=kLoop, calls=%fused_computation | loop fusion | flops 3145728 | bytes 3670017 | tf_op jit(solution)/shard_map/convert_element_type | solution.py:309
  120.1 0.9 pad_maximum_fusion
  (7 shorter events, 0.0 us)
Async XLA Ops:
  0.0 12.0 %copy-start = (bf16[1024,512]{1,0:T(8,128)(2,1)S(1)}, bf16[1024,512]{1,0:T(8,128)(2,1)}, u32[]{:S(2)}) copy-start(bf16[1024,512]{1,0:T(8,128)(2,1)} %refs_0_.5) | copy-start | bytes 3145732
  0.0 1.1 copy-start.1
  1.1 1.0 copy-start.3
  2.5 8.1 %collective-permute-start = (bf16[8,128,128]{2,1,0:T(8,128)(2,1)S(1)}, bf16[8,128,128]{2,1,0:T(8,128)(2,1)S(1)}, u32[]{:S(2)}, u32[]{:S(2)}) collective-permute-start(bf16[8,128,128]{2,1,0:T(8,128)(2,1)S(1)} %get-tuple-element.8), channel_id=1, source_target_pairs={{0,4},{4,0},{8,12},{12,8},{16,20},{20,16},{24,28},{28,24},{1,5},{5... | collective-permute-start | bytes 786440 | tf_op jit(solution)/shard_map/ppermute | solution.py:228
  10.7 9.1 %collective-permute-start.1 = (bf16[8,128,128]{2,1,0:T(8,128)(2,1)S(1)}, bf16[8,128,128]{2,1,0:T(8,128)(2,1)S(1)}, u32[]{:S(2)}, u32[]{:S(2)}) collective-permute-start(bf16[8,128,128]{2,1,0:T(8,128)(2,1)S(1)} %fusion.3), channel_id=1, source_target_pairs={{0,8},{4,12},{1,9},{5,13},{2,10},{6,14},{3,11},{7,15}} | collective-permute-start | bytes 786440 | tf_op jit(solution)/shard_map/ppermute | solution.py:259
  12.0 24.1 %collective-permute-start.7 = (bf16[1024,512]{1,0:T(8,128)(2,1)S(1)}, bf16[1024,512]{1,0:T(8,128)(2,1)S(1)}, u32[]{:S(2)}, u32[]{:S(2)}) collective-permute-start(bf16[1024,512]{1,0:T(8,128)(2,1)S(1)} %copy-done), channel_id=1, source_target_pairs={{0,4},{4,0},{8,12},{12,8},{16,20},{20,16},{24,28},{28,24},{1,5},{5... | collective-permute-start | bytes 3145736 | tf_op jit(solution)/shard_map/ppermute | solution.py:228
  19.8 5.4 %copy-start.7 = (bf16[8,128,128]{2,1,0:T(8,128)(2,1)}, bf16[8,128,128]{2,1,0:T(8,128)(2,1)S(1)}, u32[]{:S(2)}) copy-start(bf16[8,128,128]{2,1,0:T(8,128)(2,1)S(1)} %collective-permute-done.1) | copy-start | bytes 786436
  19.9 5.3 %collective-permute-start.2 = (bf16[8,128,128]{2,1,0:T(8,128)(2,1)S(1)}, bf16[8,128,128]{2,1,0:T(8,128)(2,1)S(1)}, u32[]{:S(2)}, u32[]{:S(2)}) collective-permute-start(bf16[8,128,128]{2,1,0:T(8,128)(2,1)S(1)} %fusion.2), channel_id=1, source_target_pairs={{8,16},{12,20},{9,17},{13,21},{10,18},{14,22},{11,19},{15,23}} | collective-permute-start | bytes 786440 | tf_op jit(solution)/shard_map/ppermute | solution.py:259
  25.2 0.8 copy-start.9
  26.0 10.1 %collective-permute-start.3 = (bf16[8,128,128]{2,1,0:T(8,128)(2,1)}, bf16[8,128,128]{2,1,0:T(8,128)(2,1)}, u32[]{:S(2)}, u32[]{:S(2)}) collective-permute-start(bf16[8,128,128]{2,1,0:T(8,128)(2,1)} %add_convert_fusion), channel_id=1, source_target_pairs={{16,24},{20,28},{17,25},{21,29},{18,26},{22,30},{19,27},{23,31}} | collective-permute-start | bytes 786440 | tf_op jit(solution)/shard_map/ppermute | solution.py:259
  27.4 43.8 %collective-permute-start.8 = (bf16[1024,512]{1,0:T(8,128)(2,1)S(1)}, bf16[1024,512]{1,0:T(8,128)(2,1)S(1)}, u32[]{:S(2)}, u32[]{:S(2)}) collective-permute-start(bf16[1024,512]{1,0:T(8,128)(2,1)S(1)} %copy-done), channel_id=1, source_target_pairs={{0,1},{1,0},{2,3},{3,2},{4,5},{5,4},{6,7},{7,6},{8,9},{9,8},{10,11... | collective-permute-start | bytes 3145736 | tf_op jit(solution)/shard_map/ppermute | solution.py:232
  27.4 1.0 copy-start.2
  28.4 1.0 copy-start.4
  29.5 1.0 copy-start.5
  30.5 5.6 %copy-start.8 = (bf16[8,128,128]{2,1,0:T(8,128)(2,1)S(1)}, bf16[8,128,128]{2,1,0:T(8,128)(2,1)}, u32[]{:S(2)}) copy-start(bf16[8,128,128]{2,1,0:T(8,128)(2,1)} %copy-done.7) | copy-start | bytes 786436
  30.5 5.6 %copy-start.10 = (bf16[8,128,128]{2,1,0:T(8,128)(2,1)S(1)}, bf16[8,128,128]{2,1,0:T(8,128)(2,1)}, u32[]{:S(2)}) copy-start(bf16[8,128,128]{2,1,0:T(8,128)(2,1)} %copy-done.9) | copy-start | bytes 786436
  36.1 35.1 %collective-permute-start.9 = (bf16[1024,512]{1,0:T(8,128)(2,1)S(1)}, bf16[1024,512]{1,0:T(8,128)(2,1)}, u32[]{:S(2)}, u32[]{:S(2)}) collective-permute-start(bf16[1024,512]{1,0:T(8,128)(2,1)S(1)} %collective-permute-done.7.refs_1_), channel_id=1, source_target_pairs={{0,1},{1,0},{2,3},{3,2},{4,5},{5,4},{6,7},{7,6},{8,9},{9,8},{10,11... | collective-permute-start | bytes 3145736 | tf_op jit(solution)/shard_map/ppermute | solution.py:232
  36.1 1.1 copy-start.6
  38.8 25.3 %collective-permute-start.6 = (bf16[256,1024]{1,0:T(8,128)(2,1)}, bf16[256,1024]{1,0:T(8,128)(2,1)}, u32[]{:S(2)}, u32[]{:S(2)}) collective-permute-start(bf16[256,1024]{1,0:T(8,128)(2,1)} %shard_map.57.even_a), channel_id=1, source_target_pairs={{0,9},{1,16},{2,11},{3,18},{4,13},{5,20},{6,15},{7,22},{8,1},{9,24... | collective-permute-start | bytes 1572872 | tf_op jit(solution)/shard_map/ppermute | solution.py:232
  41.3 27.8 %collective-permute-start.5 = (bf16[256,1024]{1,0:T(8,128)(2,1)}, bf16[256,1024]{1,0:T(8,128)(2,1)}, u32[]{:S(2)}, u32[]{:S(2)}) collective-permute-start(bf16[256,1024]{1,0:T(8,128)(2,1)} %shard_map.57.even_a), channel_id=1, source_target_pairs={{0,16},{1,9},{2,18},{3,11},{4,20},{5,13},{6,22},{7,15},{8,24},{9,1... | collective-permute-start | bytes 1572872 | tf_op jit(solution)/shard_map/ppermute | solution.py:232
  41.3 34.8 %collective-permute-start.4 = (bf16[256,1024]{1,0:T(8,128)(2,1)}, bf16[256,1024]{1,0:T(8,128)(2,1)}, u32[]{:S(2)}, u32[]{:S(2)}) collective-permute-start(bf16[256,1024]{1,0:T(8,128)(2,1)} %shard_map.57.even_a), channel_id=1, source_target_pairs={{1,0},{3,2},{5,4},{7,6},{9,8},{11,10},{13,12},{15,14},{17,16},{19,... | collective-permute-start | bytes 1572872 | tf_op jit(solution)/shard_map/ppermute | solution.py:232
  64.1 17.1 %collective-permute-start.14 = (bf16[256,1024]{1,0:T(8,128)(2,1)}, bf16[256,1024]{1,0:T(8,128)(2,1)}, u32[]{:S(2)}, u32[]{:S(2)}) collective-permute-start(bf16[256,1024]{1,0:T(8,128)(2,1)} %collective-permute-done.6.odd_b.b_ref), channel_id=1, source_target_pairs={{0,9},{2,11},{4,13},{6,15},{8,1},{10,3},{12,5},{14,7},{16,25},{18,... | collective-permute-start | bytes 1572872 | tf_op jit(solution)/shard_map/ppermute | solution.py:232
  69.1 20.6 %collective-permute-start.15 = (bf16[256,1024]{1,0:T(8,128)(2,1)}, bf16[256,1024]{1,0:T(8,128)(2,1)}, u32[]{:S(2)}, u32[]{:S(2)}) collective-permute-start(bf16[256,1024]{1,0:T(8,128)(2,1)} %collective-permute-done.5.odd_a.a_ref), channel_id=1, source_target_pairs={{0,9},{2,11},{4,13},{6,15},{8,1},{10,3},{12,5},{14,7},{16,25},{18,... | collective-permute-start | bytes 1572872 | tf_op jit(solution)/shard_map/ppermute | solution.py:232
  74.0 18.6 %collective-permute-start.12 = (bf16[2,256,512]{2,1,0:T(8,128)(2,1)S(1)}, bf16[2,256,512]{2,1,0:T(8,128)(2,1)}, u32[]{:S(2)}, u32[]{:S(2)}) collective-permute-start(bf16[2,256,512]{2,1,0:T(8,128)(2,1)S(1)} %shard_map.59), channel_id=1, source_target_pairs={{0,16},{2,18},{4,20},{6,22},{8,25},{10,27},{12,29},{14,31},{16,0},... | collective-permute-start | bytes 1572872 | tf_op jit(solution)/shard_map/ppermute | solution.py:232
  79.2 14.0 %collective-permute-start.10 = (bf16[2,256,512]{2,1,0:T(8,128)(2,1)S(1)}, bf16[2,256,512]{2,1,0:T(8,128)(2,1)}, u32[]{:S(2)}, u32[]{:S(2)}) collective-permute-start(bf16[2,256,512]{2,1,0:T(8,128)(2,1)S(1)} %shard_map.58), channel_id=1, source_target_pairs={{0,0},{1,8},{2,2},{3,10},{4,4},{5,12},{6,6},{7,14},{8,9},{9,1},{10... | collective-permute-start | bytes 1572872 | tf_op jit(solution)/shard_map/ppermute | solution.py:232
  91.2 16.1 %collective-permute-start.16 = (bf16[2,256,512]{2,1,0:T(8,128)(2,1)S(1)}, bf16[2,256,512]{2,1,0:T(8,128)(2,1)S(1)}, u32[]{:S(2)}, u32[]{:S(2)}) collective-permute-start(bf16[2,256,512]{2,1,0:T(8,128)(2,1)S(1)} %shard_map.60), channel_id=1, source_target_pairs={{1,24},{3,26},{5,28},{7,30},{9,17},{11,19},{13,21},{15,23},{17,8},... | collective-permute-start | bytes 1572872 | tf_op jit(solution)/shard_map/ppermute | solution.py:232
  92.6 16.2 %collective-permute-start.13 = (bf16[2,256,512]{2,1,0:T(8,128)(2,1)}, bf16[2,256,512]{2,1,0:T(8,128)(2,1)S(1)}, u32[]{:S(2)}, u32[]{:S(2)}) collective-permute-start(bf16[2,256,512]{2,1,0:T(8,128)(2,1)} %collective-permute-done.12), channel_id=1, source_target_pairs={{0,2},{4,6},{9,11},{13,15},{18,16},{22,20},{27,25},{31,29}} | collective-permute-start | bytes 1572872 | tf_op jit(solution)/shard_map/ppermute | solution.py:232
  93.3 15.5 %collective-permute-start.11 = (bf16[2,256,512]{2,1,0:T(8,128)(2,1)}, bf16[2,256,512]{2,1,0:T(8,128)(2,1)S(1)}, u32[]{:S(2)}, u32[]{:S(2)}) collective-permute-start(bf16[2,256,512]{2,1,0:T(8,128)(2,1)} %collective-permute-done.10), channel_id=1, source_target_pairs={{2,0},{3,1},{6,4},{7,5},{10,8},{11,9},{14,12},{15,13},{16,18},{17,... | collective-permute-start | bytes 1572872 | tf_op jit(solution)/shard_map/ppermute | solution.py:232
  107.4 11.1 %collective-permute-start.17 = (bf16[2,256,512]{2,1,0:T(8,128)(2,1)S(1)}, bf16[2,256,512]{2,1,0:T(8,128)(2,1)S(1)}, u32[]{:S(2)}, u32[]{:S(2)}) collective-permute-start(bf16[2,256,512]{2,1,0:T(8,128)(2,1)S(1)} %collective-permute-done.16), channel_id=1, source_target_pairs={{1,3},{5,7},{8,10},{12,14},{19,17},{23,21},{26,24},{30,28}} | collective-permute-start | bytes 1572872 | tf_op jit(solution)/shard_map/ppermute | solution.py:232

commit v8 on v2

--- a/solution.py
+++ b/solution.py
@@ -74,14 +74,23 @@
         out_ref[:, cols] = jnp.dot(scores, v_ref[:, cols], preferred_element_type=F32)
 
 
-def attend_kernel(q_ref, within_ref, state_ref, gain_ref, out_ref):
+def attend_kernel(second_ref, q_ref, within_ref, gain_ref, mate_ref, *refs):
+    *earlier_refs, whole_ref, top_ref, bottom_ref = refs
+    half = q_ref.shape[0] // 2
+    second = second_ref[0] == 1
     for head in range(q_ref.shape[1] // HD):
         cols = head_slice(head)
-        carried = jnp.dot(q_ref[:, cols], state_ref[head].astype(BF16), preferred_element_type=F32)
+        state = jnp.where(second, mate_ref[head].astype(F32), 0.0)
+        for earlier_ref in earlier_refs:
+            state += earlier_ref[head].astype(F32)
+        carried = jnp.dot(q_ref[:, cols], state.astype(BF16), preferred_element_type=F32)
         combined = within_ref[:, cols] + carried
         mean_square = jnp.mean(combined * combined, axis=-1, keepdims=True)
         scaled = combined / jnp.sqrt(mean_square + epsilon) * gain_ref[:, cols]
-        out_ref[:, cols] = scaled.astype(BF16)
+        scaled = scaled.astype(BF16)
+        whole_ref[:, cols] = scaled
+        top_ref[:, cols] = scaled[:half]
+        bottom_ref[:, cols] = scaled[half:]
 
 
 def call(kernel, out_shape, flops, moved):
@@ -91,6 +100,23 @@
         compiler_params=pltpu.CompilerParams(vmem_limit_bytes=24 * 1024 * 1024),
         cost_estimate=pl.CostEstimate(flops=flops, bytes_accessed=moved, transcendentals=0),
     )
+
+
+def attend(second, queries, within, norm_gain, mate, *earlier):
+    rows, features = queries.shape
+    size = rows * features
+    half = jax.ShapeDtypeStruct((rows // 2, features), BF16)
+    vmem = pl.BlockSpec(memory_space=pltpu.VMEM)
+    return pl.pallas_call(
+        attend_kernel,
+        out_shape=(jax.ShapeDtypeStruct((rows, features), BF16), half, half),
+        in_specs=[pl.BlockSpec(memory_space=pltpu.SMEM)] + [vmem] * (4 + len(earlier)),
+        out_specs=(vmem, vmem, vmem),
+        compiler_params=pltpu.CompilerParams(vmem_limit_bytes=24 * 1024 * 1024),
+        cost_estimate=pl.CostEstimate(
+            flops=2 * size * HD, bytes_accessed=10 * size, transcendentals=0
+        ),
+    )(second.astype(jnp.int32)[None], queries, within, norm_gain[None], mate, *earlier)
 
 
 def planes_body(seq_count, head_groups):
@@ -159,9 +185,8 @@
             within_kernel, jax.ShapeDtypeStruct((rows, features), F32), 4 * size * BLOCK, 10 * size
         )(queries, key_vectors, value_vectors)
         state_in = prefix_over_seq(wide, narrow)
-        attended = call(
-            attend_kernel, jax.ShapeDtypeStruct((rows, features), BF16), 2 * size * HD, 8 * size
-        )(queries, within, state_in, norm_gain[None])
+        nothing = jnp.zeros_like(state_in)
+        attended = attend(jnp.int32(0), queries, within, norm_gain, nothing, state_in)[0]
 
         parts = [None] * head_groups
         for j in (3, 2, 1, 0):
@@ -185,13 +210,122 @@
     return body
 
 
+def project_kernel(own_ref, mate_ref, *refs):
+    *parts, out_ref = refs
+    rows = parts[0].shape[0]
+    for half, weight_ref in enumerate((own_ref, mate_ref)):
+        weight = weight_ref[...]
+        for part, tokens_ref in enumerate(parts):
+            product = jnp.dot(tokens_ref[...], weight, preferred_element_type=F32)
+            out_ref[half, part * rows : (part + 1) * rows] = product.astype(BF16)
+
+
+def pairs_body(queries, key_vectors, value_vectors, norm_gain, out_weight):
+    rows, features = queries.shape
+    heads = features // HD
+    size = rows * features
+    half_cols = out_weight.shape[1]
+    both = ("seq", "head")
+    place, group = lax.axis_index("seq"), lax.axis_index("head")
+    z, y = place // 2, place % 2
+    devices = [(s // 2, s % 2, h // 2, h % 2) for s in range(8) for h in range(4)]
+
+    def at(z, y, x, c):
+        return (z * 2 + y) * 4 + x * 2 + c
+
+    def swap(value, mask):
+        return lax.ppermute(value, "seq", [(s, s ^ mask) for s in range(8)])
+
+    def move(value, place_of, chosen):
+        pairs = [(at(*d), at(*place_of(*d))) for d in devices if chosen(*d)]
+        return lax.ppermute(value, both, pairs)
+
+    def add(one, two):
+        return (one.astype(F32) + two.astype(F32)).astype(BF16)
+
+    wide, narrow = call(
+        state_kernel,
+        (
+            jax.ShapeDtypeStruct((heads, HD, HD), F32),
+            jax.ShapeDtypeStruct((heads, HD, HD), BF16),
+        ),
+        2 * size * HD,
+        4 * size + 6 * heads * HD * HD,
+    )(key_vectors, value_vectors)
+    within = call(
+        within_kernel, jax.ShapeDtypeStruct((rows, features), F32), 4 * size * BLOCK, 10 * size
+    )(queries, key_vectors, value_vectors)
+
+    mate_weight = swap(out_weight, 1)
+
+    mate = swap(narrow, 1)
+    onward = wide + mate.astype(F32)
+    earlier = []
+    for plane in range(3):
+        pairs = [(2 * plane + i, 2 * plane + 2 + i) for i in range(2)]
+        earlier.append(lax.ppermute(onward.astype(BF16), "seq", pairs))
+        onward += earlier[-1].astype(F32)
+    attended, top, bottom = attend(y, queries, within, norm_gain, mate, *earlier)
+
+    top_two, bottom_two = swap(top, 4), swap(bottom, 4)
+    attended_one = swap(attended, 2)
+    top_three, bottom_three = swap(top_two, 2), swap(bottom_two, 2)
+
+    def project(*parts):
+        count = sum(part.shape[0] for part in parts)
+        return call(
+            project_kernel,
+            jax.ShapeDtypeStruct((2, count, half_cols), BF16),
+            4 * count * features * half_cols,
+            2 * size + 4 * features * half_cols,
+        )(out_weight, mate_weight, *parts)
+
+    def summed(value, chip_of=lambda z: z // 2):
+        value = add(
+            value, move(value, lambda z, y, x, c: (z, y, x, 1 - c), lambda z, y, x, c: c != z % 2)
+        )
+        return add(
+            value,
+            move(
+                value,
+                lambda z, y, x, c: (z, y, 1 - x, c),
+                lambda z, y, x, c: c == z % 2 and x != chip_of(z),
+            ),
+        )
+
+    def along_z(value, mask, chip_of=lambda z: z // 2):
+        return move(
+            value,
+            lambda z, y, x, c: (z ^ mask, y, x, c),
+            lambda z, y, x, c: c == z % 2 and x == chip_of(z),
+        )
+
+    other_chip = lambda z: 1 - z // 2
+    zero = summed(project(attended))
+    two = along_z(summed(project(top_two, bottom_two), other_chip), 2, other_chip)
+    two = move(
+        two,
+        lambda z, y, x, c: (z, y, 1 - x, c),
+        lambda z, y, x, c: c == z % 2 and x == z // 2,
+    )
+    one = along_z(summed(project(attended_one)), 1)
+    three_top = along_z(summed(project(top_three)), 3)
+    three_bottom = along_z(summed(project(bottom_three)), 3)
+    result = jnp.where(group == z, zero, 0) + one + two
+    result += jnp.concatenate([three_top, three_bottom], axis=1)
+    first = jnp.where(y == 0, result[0], result[1])
+    return jnp.concatenate([first, jnp.where(y == 0, result[1], result[0])], axis=1)
+
+
 def solution(mesh):
     seq_count, head_groups = mesh.shape["seq"], mesh.shape["head"]
 
     def run(queries, key_vectors, value_vectors, norm_gain, out_weight):
         one_block = queries.shape[0] == BLOCK * seq_count
         body = general_body
-        if one_block and head_groups == 4 and seq_count % head_groups == 0:
+        if one_block and head_groups == 4 and seq_count == 8:
+            body = pairs_body
+        elif one_block and head_groups == 4 and seq_count % head_groups == 0:
             body = planes_body(seq_count, head_groups)
         return jax.shard_map(
             body,

time: 136 us -> 114 us (0.84)
  the two profiles are of different devices: /device:TPU:17 before, /device:TPU:10 now
where the time goes in v8:
time: 114 us; the launch traced here: 113 us
  waiting for transfers between devices  66.3 us (58%)
  starting transfers between devices  32.2 us (28%)
  Pallas kernels  6.02 us (5%)
  local copies, waits for them, and re-layouts  4.18 us (4%)
  other arithmetic  4.15 us (4%)
    ppermute x7, waiting for transfers between devices, swap(): return lax.ppermute(value, 'seq', [(s, s ^ mask) for s in range(8)])  30.3 us
    ppermute x15, waiting for transfers between devices, move(): return lax.ppermute(value, both, pairs)  25.7 us
    ppermute x15, starting transfers between devices, move(): return lax.ppermute(value, both, pairs)  17.1 us
    ppermute x7, starting transfers between devices, swap(): return lax.ppermute(value, 'seq', [(s, s ^ mask) for s in range(8)])  10.9 us
    ppermute x3, waiting for transfers between devices, pairs_body(): earlier.append(lax.ppermute(onward.astype(BF16), 'seq', pairs))  10.2 us
    ppermute x3, starting transfers between devices, pairs_body(): earlier.append(lax.ppermute(onward.astype(BF16), 'seq', pairs))  4.21 us
    unnamed x14, local copies, waits for them, and re-layouts  4.18 us
    pallas_call x5, Pallas kernels, project(): call(project_kernel, jax.ShapeDtypeStruct((2, count, half_cols), BF16), 4...  3.02 us
  transfers between devices with their start and end apart: 25, of which 10 were waited for; matrix products, arithmetic and copies ran while one was open for 2% of the time, Pallas kernels for 5%

profile of v8, /device:TPU:10, one launch (start us, length us, event | category | flops | bytes accessed | tf_op | source)
XLA Modules:
  0.0 113.3 jit_solution(13573006202697379294)
XLA Ops:
  0.0 1.0 copy-done.1
  1.0 1.0 copy-done.3
  2.1 0.4 shard_map.56
  2.4 1.6 %collective-permute-start.1 = (bf16[8,128,128]{2,1,0:T(8,128)(2,1)S(1)}, bf16[8,128,128]{2,1,0:T(8,128)(2,1)S(1)}, u32[]{:S(2)}, u32[]{:S(2)}) collective-permute-start(bf16[8,128,128]{2,1,0:T(8,128)(2,1)S(1)} %get-tuple-element.10), channel_id=1, source_target_pairs={{0,4},{4,0},{8,12},{12,8},{16,20},{20,16},{24,28},{28,24},{1,5},{5... | collective-permute-start | bytes 786440 | tf_op jit(solution)/shard_map/ppermute | solution.py:237
  4.0 6.5 %collective-permute-done.1.mate_ref = bf16[8,128,128]{2,1,0:T(8,128)(2,1)S(1)} collective-permute-done((bf16[8,128,128]{2,1,0:T(8,128)(2,1)S(1)}, bf16[8,128,128]{2,1,0:T(8,128)(2,1)S(1)}, u32[]{:S(2)}, u32[]{:S(2)}) %collective-permute-start.1) | collective-permute-done | bytes 262176 | tf_op jit(solution)/shard_map/ppermute | solution.py:237
  10.6 0.1 fusion.4
  10.6 1.4 %collective-permute-start.2 = (bf16[8,128,128]{2,1,0:T(8,128)(2,1)S(1)}, bf16[8,128,128]{2,1,0:T(8,128)(2,1)S(1)}, u32[]{:S(2)}, u32[]{:S(2)}) collective-permute-start(bf16[8,128,128]{2,1,0:T(8,128)(2,1)S(1)} %fusion.4), channel_id=1, source_target_pairs={{0,8},{4,12},{1,9},{5,13},{2,10},{6,14},{3,11},{7,15}} | collective-permute-start | bytes 786440 | tf_op jit(solution)/shard_map/ppermute | solution.py:266
  12.1 7.8 %collective-permute-done.2.refs_0_ = bf16[8,128,128]{2,1,0:T(8,128)(2,1)S(1)} collective-permute-done((bf16[8,128,128]{2,1,0:T(8,128)(2,1)S(1)}, bf16[8,128,128]{2,1,0:T(8,128)(2,1)S(1)}, u32[]{:S(2)}, u32[]{:S(2)}) %collective-permute-start.2) | collective-permute-done | bytes 262176 | tf_op jit(solution)/shard_map/ppermute | solution.py:266
  19.8 0.1 fusion.5
  19.9 0.0 copy-start.2
  19.9 1.4 %collective-permute-start.3 = (bf16[8,128,128]{2,1,0:T(8,128)(2,1)S(1)}, bf16[8,128,128]{2,1,0:T(8,128)(2,1)S(1)}, u32[]{:S(2)}, u32[]{:S(2)}) collective-permute-start(bf16[8,128,128]{2,1,0:T(8,128)(2,1)S(1)} %fusion.5), channel_id=1, source_target_pairs={{8,16},{12,20},{9,17},{13,21},{10,18},{14,22},{11,19},{15,23}} | collective-permute-start | bytes 786440 | tf_op jit(solution)/shard_map/ppermute | solution.py:266
  21.4 1.6 %collective-permute-start = (bf16[1024,512]{1,0:T(8,128)(2,1)S(1)}, bf16[1024,512]{1,0:T(8,128)(2,1)S(1)}, u32[]{:S(2)}, u32[]{:S(2)}) collective-permute-start(bf16[1024,512]{1,0:T(8,128)(2,1)S(1)} %copy-done), channel_id=1, source_target_pairs={{0,4},{4,0},{8,12},{12,8},{16,20},{20,16},{24,28},{28,24},{1,5},{5... | collective-permute-start | bytes 3145736 | tf_op jit(solution)/shard_map/ppermute | solution.py:237
  23.0 2.4 %collective-permute-done.3.refs_1_ = bf16[8,128,128]{2,1,0:T(8,128)(2,1)S(1)} collective-permute-done((bf16[8,128,128]{2,1,0:T(8,128)(2,1)S(1)}, bf16[8,128,128]{2,1,0:T(8,128)(2,1)S(1)}, u32[]{:S(2)}, u32[]{:S(2)}) %collective-permute-start.3) | collective-permute-done | bytes 262176 | tf_op jit(solution)/shard_map/ppermute | solution.py:266
  25.4 0.8 add_convert_fusion.10
  26.2 1.4 %collective-permute-start.4 = (bf16[8,128,128]{2,1,0:T(8,128)(2,1)}, bf16[8,128,128]{2,1,0:T(8,128)(2,1)}, u32[]{:S(2)}, u32[]{:S(2)}) collective-permute-start(bf16[8,128,128]{2,1,0:T(8,128)(2,1)} %add_convert_fusion.10), channel_id=1, source_target_pairs={{16,24},{20,28},{17,25},{21,29},{18,26},{22,30},{19,27},{23,31}} | collective-permute-start | bytes 786440 | tf_op jit(solution)/shard_map/ppermute | solution.py:266
  27.6 1.0 copy-done.4
  28.6 1.0 copy-done.5
  29.7 0.9 shard_map.55.within_ref
  30.6 1.7 %shard_map.57 = (bf16[256,1024]{1,0:T(8,128)(2,1)S(1)}, bf16[128,1024]{1,0:T(8,128)(2,1)S(1)}, bf16[128,1024]{1,0:T(8,128)(2,1)S(1)}) custom-call(s32[1]{0:T(128)} %bitcast.second_ref, bf16[256,1024]{1,0:T(8,128)(2,1)S(1)} %copy-done.5, f32[256,1024]{1,0:T(8,128)S(1)} %shard_map.55.within_ref, f32[1,1024]{1,0:T(1,128)S(1)} %bitcast.6, ...), custom_call_target="tpu_custom_call" | custom-call | flops 67108864 | bytes 2621440 | tf_op jit(solution)/shard_map/pallas_call | solution.py:110
  32.3 5.5 %collective-permute-start.11 = (bf16[128,1024]{1,0:T(8,128)(2,1)S(1)}, bf16[128,1024]{1,0:T(8,128)(2,1)S(1)}, u32[]{:S(2)}, u32[]{:S(2)}) collective-permute-start(bf16[128,1024]{1,0:T(8,128)(2,1)S(1)} %get-tuple-element.13), channel_id=1, source_target_pairs={{0,16},{4,20},{8,24},{12,28},{16,0},{20,4},{24,8},{28,12},{1,17},{... | collective-permute-start | bytes 786440 | tf_op jit(solution)/shard_map/ppermute | solution.py:237
  37.9 0.1 collective-permute-start.12
  38.0 0.0 collective-permute-start.7
  38.0 6.6 %collective-permute-done.mate_ref = bf16[1024,512]{1,0:T(8,128)(2,1)S(1)} collective-permute-done((bf16[1024,512]{1,0:T(8,128)(2,1)S(1)}, bf16[1024,512]{1,0:T(8,128)(2,1)S(1)}, u32[]{:S(2)}, u32[]{:S(2)}) %collective-permute-start) | collective-permute-done | bytes 1048608 | tf_op jit(solution)/shard_map/ppermute | solution.py:237
  44.6 6.4 %collective-permute-done.11.refs_0_ = bf16[128,1024]{1,0:T(8,128)(2,1)S(1)} collective-permute-done((bf16[128,1024]{1,0:T(8,128)(2,1)S(1)}, bf16[128,1024]{1,0:T(8,128)(2,1)S(1)}, u32[]{:S(2)}, u32[]{:S(2)}) %collective-permute-start.11) | collective-permute-done | bytes 262176 | tf_op jit(solution)/shard_map/ppermute | solution.py:237
  50.9 5.5 %collective-permute-done.12.refs_1_ = bf16[128,1024]{1,0:T(8,128)(2,1)S(1)} collective-permute-done((bf16[128,1024]{1,0:T(8,128)(2,1)S(1)}, bf16[128,1024]{1,0:T(8,128)(2,1)S(1)}, u32[]{:S(2)}, u32[]{:S(2)}) %collective-permute-start.12) | collective-permute-done | bytes 262176 | tf_op jit(solution)/shard_map/ppermute | solution.py:237
  56.4 0.7 shard_map.60
  57.2 2.0 %collective-permute-start.13 = (bf16[2,256,512]{2,1,0:T(8,128)(2,1)S(1)}, bf16[2,256,512]{2,1,0:T(8,128)(2,1)S(1)}, u32[]{:S(2)}, u32[]{:S(2)}) collective-permute-start(bf16[2,256,512]{2,1,0:T(8,128)(2,1)S(1)} %shard_map.60), channel_id=1, source_target_pairs={{1,0},{3,2},{5,4},{7,6},{8,9},{10,11},{12,13},{14,15},{17,16},{19,... | collective-permute-start | bytes 1572872 | tf_op jit(solution)/shard_map/ppermute | solution.py:241
  59.1 0.7 shard_map.58
  59.8 1.3 %collective-permute-start.5 = (bf16[2,256,512]{2,1,0:T(8,128)(2,1)S(1)}, bf16[2,256,512]{2,1,0:T(8,128)(2,1)S(1)}, u32[]{:S(2)}, u32[]{:S(2)}) collective-permute-start(bf16[2,256,512]{2,1,0:T(8,128)(2,1)S(1)} %shard_map.58), channel_id=1, source_target_pairs={{1,0},{3,2},{5,4},{7,6},{8,9},{10,11},{12,13},{14,15},{17,16},{19,... | collective-permute-start | bytes 1572872 | tf_op jit(solution)/shard_map/ppermute | solution.py:241
  61.2 0.7 collective-permute-start.17
  61.9 1.3 %collective-permute-start.21 = (bf16[128,1024]{1,0:T(8,128)(2,1)S(1)}, bf16[128,1024]{1,0:T(8,128)(2,1)S(1)}, u32[]{:S(2)}, u32[]{:S(2)}) collective-permute-start(bf16[128,1024]{1,0:T(8,128)(2,1)S(1)} %collective-permute-done.12.refs_1_), channel_id=1, source_target_pairs={{0,8},{4,12},{8,0},{12,4},{16,24},{20,28},{24,16},{28,20},{1,9},{5... | collective-permute-start | bytes 786440 | tf_op jit(solution)/shard_map/ppermute | solution.py:237
  63.3 0.7 shard_map.59
  64.0 1.6 %collective-permute-start.8 = (bf16[2,256,512]{2,1,0:T(8,128)(2,1)S(1)}, bf16[2,256,512]{2,1,0:T(8,128)(2,1)S(1)}, u32[]{:S(2)}, u32[]{:S(2)}) collective-permute-start(bf16[2,256,512]{2,1,0:T(8,128)(2,1)S(1)} %shard_map.59), channel_id=1, source_target_pairs={{1,0},{3,2},{5,4},{7,6},{8,9},{10,11},{12,13},{14,15},{17,16},{19,... | collective-permute-start | bytes 1572872 | tf_op jit(solution)/shard_map/ppermute | solution.py:241
  65.6 0.0 collective-permute-done.13
  65.6 0.1 add_convert_fusion.1
  65.7 0.7 collective-permute-start.14
  66.4 0.0 collective-permute-done.5
  66.4 0.1 add_convert_fusion.5
  66.6 0.7 collective-permute-start.6
  67.3 3.1 %collective-permute-done.17.refs_0_ = bf16[128,1024]{1,0:T(8,128)(2,1)S(1)} collective-permute-done((bf16[128,1024]{1,0:T(8,128)(2,1)S(1)}, bf16[128,1024]{1,0:T(8,128)(2,1)S(1)}, u32[]{:S(2)}, u32[]{:S(2)}) %collective-permute-start.17) | collective-permute-done | bytes 262176 | tf_op jit(solution)/shard_map/ppermute | solution.py:237
  70.4 0.4 shard_map.61
  70.8 2.1 %collective-permute-start.18 = (bf16[2,128,512]{2,1,0:T(8,128)(2,1)S(1)}, bf16[2,128,512]{2,1,0:T(8,128)(2,1)S(1)}, u32[]{:S(2)}, u32[]{:S(2)}) collective-permute-start(bf16[2,128,512]{2,1,0:T(8,128)(2,1)S(1)} %shard_map.61), channel_id=1, source_target_pairs={{1,0},{3,2},{5,4},{7,6},{8,9},{10,11},{12,13},{14,15},{17,16},{19,... | collective-permute-start | bytes 786440 | tf_op jit(solution)/shard_map/ppermute | solution.py:241
  73.0 2.2 %collective-permute-done.21.refs_0_ = bf16[128,1024]{1,0:T(8,128)(2,1)S(1)} collective-permute-done((bf16[128,1024]{1,0:T(8,128)(2,1)S(1)}, bf16[128,1024]{1,0:T(8,128)(2,1)S(1)}, u32[]{:S(2)}, u32[]{:S(2)}) %collective-permute-start.21) | collective-permute-done | bytes 262176 | tf_op jit(solution)/shard_map/ppermute | solution.py:237
  75.2 0.4 shard_map.62
  75.6 1.3 %collective-permute-start.22 = (bf16[2,128,512]{2,1,0:T(8,128)(2,1)S(1)}, bf16[2,128,512]{2,1,0:T(8,128)(2,1)S(1)}, u32[]{:S(2)}, u32[]{:S(2)}) collective-permute-start(bf16[2,128,512]{2,1,0:T(8,128)(2,1)S(1)} %shard_map.62), channel_id=1, source_target_pairs={{1,0},{3,2},{5,4},{7,6},{8,9},{10,11},{12,13},{14,15},{17,16},{19,... | collective-permute-start | bytes 786440 | tf_op jit(solution)/shard_map/ppermute | solution.py:241
  77.0 0.1 add_convert_fusion.3
  77.1 0.7 collective-permute-start.9
  77.8 0.1 add_convert_fusion
  78.0 1.5 %collective-permute-start.15 = (bf16[2,256,512]{2,1,0:T(8,128)(2,1)S(1)}, bf16[2,256,512]{2,1,0:T(8,128)(2,1)}, u32[]{:S(2)}, u32[]{:S(2)}) collective-permute-start(bf16[2,256,512]{2,1,0:T(8,128)(2,1)S(1)} %add_convert_fusion), channel_id=1, source_target_pairs={{2,18},{6,22},{11,27},{15,31},{16,0},{20,4},{25,9},{29,13}} | collective-permute-start | bytes 1572872 | tf_op jit(solution)/shard_map/ppermute | solution.py:241
  79.4 0.1 add_convert_fusion.9
  79.5 0.7 collective-permute-start.19
  80.2 0.1 add_convert_fusion.7
  80.3 0.7 collective-permute-start.23
  81.0 0.1 add_convert_fusion.2
  81.1 0.7 collective-permute-start.10
  81.8 0.7 collective-permute-start.16
  82.6 0.1 add_convert_fusion.8
  82.6 1.3 %collective-permute-start.20 = (bf16[2,128,512]{2,1,0:T(8,128)(2,1)S(1)}, bf16[2,128,512]{2,1,0:T(8,128)(2,1)S(1)}, u32[]{:S(2)}, u32[]{:S(2)}) collective-permute-start(bf16[2,128,512]{2,1,0:T(8,128)(2,1)S(1)} %add_convert_fusion.8), channel_id=1, source_target_pairs={{0,24},{4,28},{9,17},{13,21},{18,10},{22,14},{27,3},{31,7}} | collective-permute-start | bytes 786440 | tf_op jit(solution)/shard_map/ppermute | solution.py:241
  83.9 0.1 add_convert_fusion.6
  84.0 1.3 %collective-permute-start.24 = (bf16[2,128,512]{2,1,0:T(8,128)(2,1)S(1)}, bf16[2,128,512]{2,1,0:T(8,128)(2,1)}, u32[]{:S(2)}, u32[]{:S(2)}) collective-permute-start(bf16[2,128,512]{2,1,0:T(8,128)(2,1)S(1)} %add_convert_fusion.6), channel_id=1, source_target_pairs={{0,24},{4,28},{9,17},{13,21},{18,10},{22,14},{27,3},{31,7}} | collective-permute-start | bytes 786440 | tf_op jit(solution)/shard_map/ppermute | solution.py:241
  85.3 22.8 %collective-permute-done.20 = bf16[2,128,512]{2,1,0:T(8,128)(2,1)S(1)} collective-permute-done((bf16[2,128,512]{2,1,0:T(8,128)(2,1)S(1)}, bf16[2,128,512]{2,1,0:T(8,128)(2,1)S(1)}, u32[]{:S(2)}, u32[]{:S(2)}) %collective-permute-start.20) | collective-permute-done | bytes 262176 | tf_op jit(solution)/shard_map/ppermute | solution.py:241
  108.1 2.9 %collective-permute-done.24 = bf16[2,128,512]{2,1,0:T(8,128)(2,1)} collective-permute-done((bf16[2,128,512]{2,1,0:T(8,128)(2,1)S(1)}, bf16[2,128,512]{2,1,0:T(8,128)(2,1)}, u32[]{:S(2)}, u32[]{:S(2)}) %collective-permute-start.24) | collective-permute-done | bytes 262176 | tf_op jit(solution)/shard_map/ppermute | solution.py:241
  111.1 1.3 %fusion.3 = bf16[2,256,512]{2,1,0:T(8,128)(2,1)S(1)} fusion(bf16[2,256,512]{2,1,0:T(8,128)(2,1)S(1)} %collective-permute-done.16, bf16[2,256,512]{2,1,0:T(8,128)(2,1)S(1)} %collective-permute-done.10, bf16[2,256,512]{2,1,0:T(8,128)(2,1)S(1)} %collective-permute-done.6, bf16[2,256,512]{2,1,0:T(8,128)(2,1)S(1)} %add_convert_fusion.5, ...), kind=kLoop, calls=%fused_computation.9 | loop fusion | flops 3932160 | bytes 3145729 | tf_op jit(solution)/shard_map/add | solution.py:315
  112.4 0.9 pad_maximum_fusion
  (23 shorter events, 0.1 us)
Async XLA Ops:
  0.0 1.0 copy-start.1
  1.0 1.0 copy-start.3
  2.4 8.1 %collective-permute-start.1 = (bf16[8,128,128]{2,1,0:T(8,128)(2,1)S(1)}, bf16[8,128,128]{2,1,0:T(8,128)(2,1)S(1)}, u32[]{:S(2)}, u32[]{:S(2)}) collective-permute-start(bf16[8,128,128]{2,1,0:T(8,128)(2,1)S(1)} %get-tuple-element.10), channel_id=1, source_target_pairs={{0,4},{4,0},{8,12},{12,8},{16,20},{20,16},{24,28},{28,24},{1,5},{5... | collective-permute-start | bytes 786440 | tf_op jit(solution)/shard_map/ppermute | solution.py:237
  10.6 10.8 %copy-start = (bf16[1024,512]{1,0:T(8,128)(2,1)S(1)}, bf16[1024,512]{1,0:T(8,128)(2,1)}, u32[]{:S(2)}) copy-start(bf16[1024,512]{1,0:T(8,128)(2,1)} %own_ref.9) | copy-start | bytes 3145732
  10.6 9.2 %collective-permute-start.2 = (bf16[8,128,128]{2,1,0:T(8,128)(2,1)S(1)}, bf16[8,128,128]{2,1,0:T(8,128)(2,1)S(1)}, u32[]{:S(2)}, u32[]{:S(2)}) collective-permute-start(bf16[8,128,128]{2,1,0:T(8,128)(2,1)S(1)} %fusion.4), channel_id=1, source_target_pairs={{0,8},{4,12},{1,9},{5,13},{2,10},{6,14},{3,11},{7,15}} | collective-permute-start | bytes 786440 | tf_op jit(solution)/shard_map/ppermute | solution.py:266
  19.9 7.7 %copy-start.2 = (bf16[256,1024]{1,0:T(8,128)(2,1)S(1)}, bf16[256,1024]{1,0:T(8,128)(2,1)}, u32[]{:S(2)}) copy-start(bf16[256,1024]{1,0:T(8,128)(2,1)} %k_ref.3) | copy-start | bytes 1572868
  19.9 5.5 %collective-permute-start.3 = (bf16[8,128,128]{2,1,0:T(8,128)(2,1)S(1)}, bf16[8,128,128]{2,1,0:T(8,128)(2,1)S(1)}, u32[]{:S(2)}, u32[]{:S(2)}) collective-permute-start(bf16[8,128,128]{2,1,0:T(8,128)(2,1)S(1)} %fusion.5), channel_id=1, source_target_pairs={{8,16},{12,20},{9,17},{13,21},{10,18},{14,22},{11,19},{15,23}} | collective-permute-start | bytes 786440 | tf_op jit(solution)/shard_map/ppermute | solution.py:266
  21.4 23.2 %collective-permute-start = (bf16[1024,512]{1,0:T(8,128)(2,1)S(1)}, bf16[1024,512]{1,0:T(8,128)(2,1)S(1)}, u32[]{:S(2)}, u32[]{:S(2)}) collective-permute-start(bf16[1024,512]{1,0:T(8,128)(2,1)S(1)} %copy-done), channel_id=1, source_target_pairs={{0,4},{4,0},{8,12},{12,8},{16,20},{20,16},{24,28},{28,24},{1,5},{5... | collective-permute-start | bytes 3145736 | tf_op jit(solution)/shard_map/ppermute | solution.py:237
  26.2 4.4 %collective-permute-start.4 = (bf16[8,128,128]{2,1,0:T(8,128)(2,1)}, bf16[8,128,128]{2,1,0:T(8,128)(2,1)}, u32[]{:S(2)}, u32[]{:S(2)}) collective-permute-start(bf16[8,128,128]{2,1,0:T(8,128)(2,1)} %add_convert_fusion.10), channel_id=1, source_target_pairs={{16,24},{20,28},{17,25},{21,29},{18,26},{22,30},{19,27},{23,31}} | collective-permute-start | bytes 786440 | tf_op jit(solution)/shard_map/ppermute | solution.py:266
  27.6 1.0 copy-start.4
  28.6 1.0 copy-start.5
  29.7 0.9 copy-start.6
  32.3 18.6 %collective-permute-start.11 = (bf16[128,1024]{1,0:T(8,128)(2,1)S(1)}, bf16[128,1024]{1,0:T(8,128)(2,1)S(1)}, u32[]{:S(2)}, u32[]{:S(2)}) collective-permute-start(bf16[128,1024]{1,0:T(8,128)(2,1)S(1)} %get-tuple-element.13), channel_id=1, source_target_pairs={{0,16},{4,20},{8,24},{12,28},{16,0},{20,4},{24,8},{28,12},{1,17},{... | collective-permute-start | bytes 786440 | tf_op jit(solution)/shard_map/ppermute | solution.py:237
  37.9 18.6 %collective-permute-start.12 = (bf16[128,1024]{1,0:T(8,128)(2,1)S(1)}, bf16[128,1024]{1,0:T(8,128)(2,1)S(1)}, u32[]{:S(2)}, u32[]{:S(2)}) collective-permute-start(bf16[128,1024]{1,0:T(8,128)(2,1)S(1)} %get-tuple-element.14), channel_id=1, source_target_pairs={{0,16},{4,20},{8,24},{12,28},{16,0},{20,4},{24,8},{28,12},{1,17},{... | collective-permute-start | bytes 786440 | tf_op jit(solution)/shard_map/ppermute | solution.py:237
  38.0 25.3 %collective-permute-start.7 = (bf16[256,1024]{1,0:T(8,128)(2,1)S(1)}, bf16[256,1024]{1,0:T(8,128)(2,1)S(1)}, u32[]{:S(2)}, u32[]{:S(2)}) collective-permute-start(bf16[256,1024]{1,0:T(8,128)(2,1)S(1)} %get-tuple-element.12.refs_0_), channel_id=1, source_target_pairs={{0,8},{4,12},{8,0},{12,4},{16,24},{20,28},{24,16},{28,20},{1,9},{5... | collective-permute-start | bytes 1572872 | tf_op jit(solution)/shard_map/ppermute | solution.py:237
  57.2 8.4 %collective-permute-start.13 = (bf16[2,256,512]{2,1,0:T(8,128)(2,1)S(1)}, bf16[2,256,512]{2,1,0:T(8,128)(2,1)S(1)}, u32[]{:S(2)}, u32[]{:S(2)}) collective-permute-start(bf16[2,256,512]{2,1,0:T(8,128)(2,1)S(1)} %shard_map.60), channel_id=1, source_target_pairs={{1,0},{3,2},{5,4},{7,6},{8,9},{10,11},{12,13},{14,15},{17,16},{19,... | collective-permute-start | bytes 1572872 | tf_op jit(solution)/shard_map/ppermute | solution.py:241
  59.8 6.6 %collective-permute-start.5 = (bf16[2,256,512]{2,1,0:T(8,128)(2,1)S(1)}, bf16[2,256,512]{2,1,0:T(8,128)(2,1)S(1)}, u32[]{:S(2)}, u32[]{:S(2)}) collective-permute-start(bf16[2,256,512]{2,1,0:T(8,128)(2,1)S(1)} %shard_map.58), channel_id=1, source_target_pairs={{1,0},{3,2},{5,4},{7,6},{8,9},{10,11},{12,13},{14,15},{17,16},{19,... | collective-permute-start | bytes 1572872 | tf_op jit(solution)/shard_map/ppermute | solution.py:241
  61.2 9.2 %collective-permute-start.17 = (bf16[128,1024]{1,0:T(8,128)(2,1)S(1)}, bf16[128,1024]{1,0:T(8,128)(2,1)S(1)}, u32[]{:S(2)}, u32[]{:S(2)}) collective-permute-start(bf16[128,1024]{1,0:T(8,128)(2,1)S(1)} %collective-permute-done.11.refs_0_), channel_id=1, source_target_pairs={{0,8},{4,12},{8,0},{12,4},{16,24},{20,28},{24,16},{28,20},{1,9},{5... | collective-permute-start | bytes 786440 | tf_op jit(solution)/shard_map/ppermute | solution.py:237
  61.9 13.3 %collective-permute-start.21 = (bf16[128,1024]{1,0:T(8,128)(2,1)S(1)}, bf16[128,1024]{1,0:T(8,128)(2,1)S(1)}, u32[]{:S(2)}, u32[]{:S(2)}) collective-permute-start(bf16[128,1024]{1,0:T(8,128)(2,1)S(1)} %collective-permute-done.12.refs_1_), channel_id=1, source_target_pairs={{0,8},{4,12},{8,0},{12,4},{16,24},{20,28},{24,16},{28,20},{1,9},{5... | collective-permute-start | bytes 786440 | tf_op jit(solution)/shard_map/ppermute | solution.py:237
  64.0 13.0 %collective-permute-start.8 = (bf16[2,256,512]{2,1,0:T(8,128)(2,1)S(1)}, bf16[2,256,512]{2,1,0:T(8,128)(2,1)S(1)}, u32[]{:S(2)}, u32[]{:S(2)}) collective-permute-start(bf16[2,256,512]{2,1,0:T(8,128)(2,1)S(1)} %shard_map.59), channel_id=1, source_target_pairs={{1,0},{3,2},{5,4},{7,6},{8,9},{10,11},{12,13},{14,15},{17,16},{19,... | collective-permute-start | bytes 1572872 | tf_op jit(solution)/shard_map/ppermute | solution.py:241
  65.7 12.1 %collective-permute-start.14 = (bf16[2,256,512]{2,1,0:T(8,128)(2,1)S(1)}, bf16[2,256,512]{2,1,0:T(8,128)(2,1)S(1)}, u32[]{:S(2)}, u32[]{:S(2)}) collective-permute-start(bf16[2,256,512]{2,1,0:T(8,128)(2,1)S(1)} %add_convert_fusion.1), channel_id=1, source_target_pairs={{0,2},{4,6},{9,11},{13,15},{18,16},{22,20},{27,25},{31,29}} | collective-permute-start | bytes 1572872 | tf_op jit(solution)/shard_map/ppermute | solution.py:241
  66.6 18.8 %collective-permute-start.6 = (bf16[2,256,512]{2,1,0:T(8,128)(2,1)S(1)}, bf16[2,256,512]{2,1,0:T(8,128)(2,1)S(1)}, u32[]{:S(2)}, u32[]{:S(2)}) collective-permute-start(bf16[2,256,512]{2,1,0:T(8,128)(2,1)S(1)} %add_convert_fusion.5), channel_id=1, source_target_pairs={{2,0},{6,4},{11,9},{15,13},{16,18},{20,22},{25,27},{29,31}} | collective-permute-start | bytes 1572872 | tf_op jit(solution)/shard_map/ppermute | solution.py:241
  70.8 8.6 %collective-permute-start.18 = (bf16[2,128,512]{2,1,0:T(8,128)(2,1)S(1)}, bf16[2,128,512]{2,1,0:T(8,128)(2,1)S(1)}, u32[]{:S(2)}, u32[]{:S(2)}) collective-permute-start(bf16[2,128,512]{2,1,0:T(8,128)(2,1)S(1)} %shard_map.61), channel_id=1, source_target_pairs={{1,0},{3,2},{5,4},{7,6},{8,9},{10,11},{12,13},{14,15},{17,16},{19,... | collective-permute-start | bytes 786440 | tf_op jit(solution)/shard_map/ppermute | solution.py:241
  75.6 4.6 %collective-permute-start.22 = (bf16[2,128,512]{2,1,0:T(8,128)(2,1)S(1)}, bf16[2,128,512]{2,1,0:T(8,128)(2,1)S(1)}, u32[]{:S(2)}, u32[]{:S(2)}) collective-permute-start(bf16[2,128,512]{2,1,0:T(8,128)(2,1)S(1)} %shard_map.62), channel_id=1, source_target_pairs={{1,0},{3,2},{5,4},{7,6},{8,9},{10,11},{12,13},{14,15},{17,16},{19,... | collective-permute-start | bytes 786440 | tf_op jit(solution)/shard_map/ppermute | solution.py:241
  77.1 3.9 %collective-permute-start.9 = (bf16[2,256,512]{2,1,0:T(8,128)(2,1)S(1)}, bf16[2,256,512]{2,1,0:T(8,128)(2,1)S(1)}, u32[]{:S(2)}, u32[]{:S(2)}) collective-permute-start(bf16[2,256,512]{2,1,0:T(8,128)(2,1)S(1)} %add_convert_fusion.3), channel_id=1, source_target_pairs={{2,0},{6,4},{11,9},{15,13},{16,18},{20,22},{25,27},{29,31}} | collective-permute-start | bytes 1572872 | tf_op jit(solution)/shard_map/ppermute | solution.py:241
  78.0 3.9 %collective-permute-start.15 = (bf16[2,256,512]{2,1,0:T(8,128)(2,1)S(1)}, bf16[2,256,512]{2,1,0:T(8,128)(2,1)}, u32[]{:S(2)}, u32[]{:S(2)}) collective-permute-start(bf16[2,256,512]{2,1,0:T(8,128)(2,1)S(1)} %add_convert_fusion), channel_id=1, source_target_pairs={{2,18},{6,22},{11,27},{15,31},{16,0},{20,4},{25,9},{29,13}} | collective-permute-start | bytes 1572872 | tf_op jit(solution)/shard_map/ppermute | solution.py:241
  79.5 3.0 %collective-permute-start.19 = (bf16[2,128,512]{2,1,0:T(8,128)(2,1)S(1)}, bf16[2,128,512]{2,1,0:T(8,128)(2,1)S(1)}, u32[]{:S(2)}, u32[]{:S(2)}) collective-permute-start(bf16[2,128,512]{2,1,0:T(8,128)(2,1)S(1)} %add_convert_fusion.9), channel_id=1, source_target_pairs={{2,0},{6,4},{11,9},{15,13},{16,18},{20,22},{25,27},{29,31}} | collective-permute-start | bytes 786440 | tf_op jit(solution)/shard_map/ppermute | solution.py:241
  80.3 3.6 %collective-permute-start.23 = (bf16[2,128,512]{2,1,0:T(8,128)(2,1)S(1)}, bf16[2,128,512]{2,1,0:T(8,128)(2,1)S(1)}, u32[]{:S(2)}, u32[]{:S(2)}) collective-permute-start(bf16[2,128,512]{2,1,0:T(8,128)(2,1)S(1)} %add_convert_fusion.7), channel_id=1, source_target_pairs={{2,0},{6,4},{11,9},{15,13},{16,18},{20,22},{25,27},{29,31}} | collective-permute-start | bytes 786440 | tf_op jit(solution)/shard_map/ppermute | solution.py:241
  81.1 29.9 %collective-permute-start.10 = (bf16[2,256,512]{2,1,0:T(8,128)(2,1)S(1)}, bf16[2,256,512]{2,1,0:T(8,128)(2,1)S(1)}, u32[]{:S(2)}, u32[]{:S(2)}) collective-permute-start(bf16[2,256,512]{2,1,0:T(8,128)(2,1)S(1)} %add_convert_fusion.2), channel_id=1, source_target_pairs={{0,8},{4,12},{9,1},{13,5},{18,26},{22,30},{27,19},{31,23}} | collective-permute-start | bytes 1572872 | tf_op jit(solution)/shard_map/ppermute | solution.py:241
  81.8 29.2 %collective-permute-start.16 = (bf16[2,256,512]{2,1,0:T(8,128)(2,1)}, bf16[2,256,512]{2,1,0:T(8,128)(2,1)S(1)}, u32[]{:S(2)}, u32[]{:S(2)}) collective-permute-start(bf16[2,256,512]{2,1,0:T(8,128)(2,1)} %collective-permute-done.15), channel_id=1, source_target_pairs={{0,2},{4,6},{9,11},{13,15},{18,16},{22,20},{27,25},{31,29}} | collective-permute-start | bytes 1572872 | tf_op jit(solution)/shard_map/ppermute | solution.py:241
  82.6 25.5 %collective-permute-start.20 = (bf16[2,128,512]{2,1,0:T(8,128)(2,1)S(1)}, bf16[2,128,512]{2,1,0:T(8,128)(2,1)S(1)}, u32[]{:S(2)}, u32[]{:S(2)}) collective-permute-start(bf16[2,128,512]{2,1,0:T(8,128)(2,1)S(1)} %add_convert_fusion.8), channel_id=1, source_target_pairs={{0,24},{4,28},{9,17},{13,21},{18,10},{22,14},{27,3},{31,7}} | collective-permute-start | bytes 786440 | tf_op jit(solution)/shard_map/ppermute | solution.py:241
  84.0 27.1 %collective-permute-start.24 = (bf16[2,128,512]{2,1,0:T(8,128)(2,1)S(1)}, bf16[2,128,512]{2,1,0:T(8,128)(2,1)}, u32[]{:S(2)}, u32[]{:S(2)}) collective-permute-start(bf16[2,128,512]{2,1,0:T(8,128)(2,1)S(1)} %add_convert_fusion.6), channel_id=1, source_target_pairs={{0,24},{4,28},{9,17},{13,21},{18,10},{22,14},{27,3},{31,7}} | collective-permute-start | bytes 786440 | tf_op jit(solution)/shard_map/ppermute | solution.py:241

commit v9 on v1

--- a/solution.py
+++ b/solution.py
@@ -74,10 +74,15 @@
         out_ref[:, cols] = jnp.dot(scores, v_ref[:, cols], preferred_element_type=F32)
 
 
-def attend_kernel(q_ref, within_ref, state_ref, gain_ref, out_ref):
+def attend_kernel(second_ref, q_ref, within_ref, gain_ref, mate_ref, *refs):
+    *earlier_refs, out_ref = refs
+    second = second_ref[0] == 1
     for head in range(q_ref.shape[1] // HD):
         cols = head_slice(head)
-        carried = jnp.dot(q_ref[:, cols], state_ref[head].astype(BF16), preferred_element_type=F32)
+        state = jnp.where(second, mate_ref[head].astype(F32), 0.0)
+        for earlier_ref in earlier_refs:
+            state += earlier_ref[head].astype(F32)
+        carried = jnp.dot(q_ref[:, cols], state.astype(BF16), preferred_element_type=F32)
         combined = within_ref[:, cols] + carried
         mean_square = jnp.mean(combined * combined, axis=-1, keepdims=True)
         scaled = combined / jnp.sqrt(mean_square + epsilon) * gain_ref[:, cols]
@@ -93,17 +98,26 @@
     )
 
 
+def attend(second, queries, within, norm_gain, mate, *earlier):
+    rows, features = queries.shape
+    size = rows * features
+    vmem = pl.BlockSpec(memory_space=pltpu.VMEM)
+    return pl.pallas_call(
+        attend_kernel,
+        out_shape=jax.ShapeDtypeStruct((rows, features), BF16),
+        in_specs=[pl.BlockSpec(memory_space=pltpu.SMEM)] + [vmem] * (4 + len(earlier)),
+        out_specs=vmem,
+        compiler_params=pltpu.CompilerParams(vmem_limit_bytes=24 * 1024 * 1024),
+        cost_estimate=pl.CostEstimate(
+            flops=2 * size * HD, bytes_accessed=8 * size, transcendentals=0
+        ),
+    )(second.astype(jnp.int32)[None], queries, within, norm_gain[None], mate, *earlier)
+
+
 def planes_body(seq_count, head_groups):
     planes = head_groups
     inner = seq_count // planes
 
-    def seq_perm(step):
-        return [
-            (z * inner + y, (z + step) * inner + y)
-            for z in range(planes - step)
-            for y in range(inner)
-        ]
-
     def flat(z, y, h):
         return (z * inner + y) * head_groups + h
 
@@ -112,30 +126,24 @@
     ]
 
     def prefix_over_seq(wide, narrow):
-        place = lax.axis_index("seq")
-        excl = jnp.zeros_like(wide)
-        incl = wide
-        if inner == 2:
-            swap = [(s, s ^ 1) for s in range(seq_count)]
-            mate = lax.ppermute(narrow, "seq", swap).astype(F32)
-            excl = jnp.where(place % 2 == 1, mate, 0.0)
-            incl = wide + mate
-            before = jnp.zeros_like(wide)
-            step = 1
-            while step < planes:
-                got = lax.ppermute(incl.astype(BF16), "seq", seq_perm(step)).astype(F32)
-                before += got
-                incl += got
-                step *= 2
-            return (excl + before).astype(BF16)
-        step = 1
+        before, total, step = jnp.zeros_like(wide), wide, 1
         while step < seq_count:
             pairs = [(s, s + step) for s in range(seq_count - step)]
-            got = lax.ppermute(incl.astype(BF16), "seq", pairs).astype(F32)
-            excl += got
-            incl += got
+            got = lax.ppermute(total.astype(BF16), "seq", pairs).astype(F32)
+            before += got
+            total += got
             step *= 2
-        return excl.astype(BF16)
+        return jnp.zeros_like(narrow), [before.astype(BF16)]
+
+    def prefix_over_planes(wide, narrow):
+        mate = lax.ppermute(narrow, "seq", [(s, s ^ 1) for s in range(seq_count)])
+        onward = wide + mate.astype(F32)
+        earlier = []
+        for plane in range(planes - 1):
+            pairs = [(2 * plane + i, 2 * plane + 2 + i) for i in range(2)]
+            earlier.append(lax.ppermute(onward.astype(BF16), "seq", pairs))
+            onward += earlier[-1].astype(F32)
+        return mate, earlier
 
     def gather_weight(out_weight):
         if inner == 2:
@@ -165,10 +173,10 @@
         within = call(
             within_kernel, jax.ShapeDtypeStruct((rows, features), F32), 4 * size * BLOCK, 10 * size
         )(queries, key_vectors, value_vectors)
-        state_in = prefix_over_seq(wide, narrow)
-        attended = call(
-            attend_kernel, jax.ShapeDtypeStruct((rows, features), BF16), 2 * size * HD, 8 * size
-        )(queries, within, state_in, norm_gain[None])
+        prefix = prefix_over_planes if inner == 2 else prefix_over_seq
+        mate, earlier = prefix(wide, narrow)
+        second = lax.axis_index("seq") % 2
+        attended = attend(second, queries, within, norm_gain, mate, *earlier)
 
         parts = [None] * head_groups
         for j in (3, 2, 1, 0):

time: 114 us -> 109 us (0.956)
  the two profiles are of different devices: /device:TPU:6 before, /device:TPU:2 now
where the time goes in v9:
time: 109 us; the launch traced here: 108 us
  starting transfers between devices  54.9 us (50%)
  waiting for transfers between devices  43.4 us (40%)
  local copies, waits for them, and re-layouts  2.9 us (3%)
  matrix products  2.86 us (3%)
  Pallas kernels  2.05 us (2%)
  other arithmetic  1.96 us (2%)
    ppermute x4, starting transfers between devices, body(): parts[j] = lax.ppermute(attended, ('seq', 'head'), pairs)  31 us
    ppermute x4, waiting for transfers between devices, body(): parts[j] = lax.ppermute(attended, ('seq', 'head'), pairs)  15.9 us
    ppermute x1, waiting for transfers between devices, body(): return lax.ppermute(near.astype(BF16), ('seq', 'head'), home)  14.7 us
    ppermute x1, starting transfers between devices, body(): near += lax.ppermute(far.astype(BF16), 'head', chip).astype(F32)  7.91 us
    ppermute x1, waiting for transfers between devices, prefix_over_planes(): mate = lax.ppermute(narrow, 'seq', [(s, s ^ 1) for s in range(seq_count)])  6.53 us
    ppermute x1, starting transfers between devices, body(): return lax.ppermute(near.astype(BF16), ('seq', 'head'), home)  6.17 us
    ppermute x3, starting transfers between devices, prefix_over_planes(): earlier.append(lax.ppermute(onward.astype(BF16), 'seq', pairs))  4.98 us
    ppermute x1, waiting for transfers between devices, body(): near += lax.ppermute(far.astype(BF16), 'head', chip).astype(F32)  3.21 us
  transfers between devices with their start and end apart: 13, of which 6 were waited for; matrix products, arithmetic and copies ran while one was open for 4% of the time, Pallas kernels for 2%

profile of v9, /device:TPU:2, one launch (start us, length us, event | category | flops | bytes accessed | tf_op | source)
XLA Modules:
  0.0 108.3 jit_solution(1243379724497858218)
XLA Ops:
  0.0 0.0 copy-start
  0.0 1.0 copy-done
  1.0 0.0 copy-start.2
  1.0 1.0 copy-done.2
  2.1 0.4 shard_map.56
  2.4 1.6 %collective-permute-start = (bf16[8,128,128]{2,1,0:T(8,128)(2,1)S(1)}, bf16[8,128,128]{2,1,0:T(8,128)(2,1)S(1)}, u32[]{:S(2)}, u32[]{:S(2)}) collective-permute-start(bf16[8,128,128]{2,1,0:T(8,128)(2,1)S(1)} %get-tuple-element.7), channel_id=1, source_target_pairs={{0,4},{4,0},{8,12},{12,8},{16,20},{20,16},{24,28},{28,24},{1,5},{5... | collective-permute-start | bytes 786440 | tf_op jit(solution)/shard_map/ppermute | solution.py:139
  4.0 6.5 %collective-permute-done.mate_ref = bf16[8,128,128]{2,1,0:T(8,128)(2,1)S(1)} collective-permute-done((bf16[8,128,128]{2,1,0:T(8,128)(2,1)S(1)}, bf16[8,128,128]{2,1,0:T(8,128)(2,1)S(1)}, u32[]{:S(2)}, u32[]{:S(2)}) %collective-permute-start) | collective-permute-done | bytes 262176 | tf_op jit(solution)/shard_map/ppermute | solution.py:139
  10.6 0.1 fusion.7
  10.6 3.5 %collective-permute-start.1 = (bf16[8,128,128]{2,1,0:T(8,128)(2,1)S(1)}, bf16[8,128,128]{2,1,0:T(8,128)(2,1)S(1)}, u32[]{:S(2)}, u32[]{:S(2)}) collective-permute-start(bf16[8,128,128]{2,1,0:T(8,128)(2,1)S(1)} %fusion.7), channel_id=1, source_target_pairs={{0,8},{4,12},{1,9},{5,13},{2,10},{6,14},{3,11},{7,15}} | collective-permute-start | bytes 786440 | tf_op jit(solution)/shard_map/ppermute | solution.py:144
  14.1 1.6 %collective-permute-start.5 = (bf16[1024,512]{1,0:T(8,128)(2,1)}, bf16[1024,512]{1,0:T(8,128)(2,1)}, u32[]{:S(2)}, u32[]{:S(2)}) collective-permute-start(bf16[1024,512]{1,0:T(8,128)(2,1)} %param.9), channel_id=1, source_target_pairs={{0,4},{4,0},{8,12},{12,8},{16,20},{20,16},{24,28},{28,24},{1,5},{5... | collective-permute-start | bytes 3145736 | tf_op jit(solution)/shard_map/ppermute | solution.py:151
  15.7 3.1 %collective-permute-done.1.refs_0_ = bf16[8,128,128]{2,1,0:T(8,128)(2,1)S(1)} collective-permute-done((bf16[8,128,128]{2,1,0:T(8,128)(2,1)S(1)}, bf16[8,128,128]{2,1,0:T(8,128)(2,1)S(1)}, u32[]{:S(2)}, u32[]{:S(2)}) %collective-permute-start.1) | collective-permute-done | bytes 262176 | tf_op jit(solution)/shard_map/ppermute | solution.py:144
  18.8 0.1 fusion.8
  18.9 0.0 copy-start.1
  18.9 0.0 copy-start.3
  18.9 0.0 copy-start.4
  18.9 0.8 collective-permute-start.2
  19.7 0.0 collective-permute-done.2.refs_1_
  19.7 0.1 add_convert_fusion
  19.9 0.7 collective-permute-start.3
  20.6 0.0 copy-done.1
  20.6 0.0 copy-done.3
  20.6 0.0 copy-done.4
  20.6 0.0 copy-start.5
  20.6 0.9 shard_map.55.within_ref
  21.6 0.0 collective-permute-done.3.refs_2_
  21.6 0.0 copy-done.5
  21.6 0.8 shard_map.57
  22.3 9.1 %collective-permute-start.9 = (bf16[256,1024]{1,0:T(8,128)(2,1)S(1)}, bf16[256,1024]{1,0:T(8,128)(2,1)S(1)}, u32[]{:S(2)}, u32[]{:S(2)}) collective-permute-start(bf16[256,1024]{1,0:T(8,128)(2,1)S(1)} %shard_map.57), channel_id=1, source_target_pairs={{0,24},{1,17},{2,10},{3,3},{4,28},{5,21},{6,14},{7,7},{8,0},{9,25}... | collective-permute-start | bytes 1572872 | tf_op jit(solution)/shard_map/ppermute | solution.py:186
  31.5 9.2 %collective-permute-start.6 = (bf16[256,1024]{1,0:T(8,128)(2,1)S(1)}, bf16[256,1024]{1,0:T(8,128)(2,1)S(1)}, u32[]{:S(2)}, u32[]{:S(2)}) collective-permute-start(bf16[256,1024]{1,0:T(8,128)(2,1)S(1)} %shard_map.57), channel_id=1, source_target_pairs={{0,8},{1,1},{2,26},{3,19},{4,12},{5,5},{6,30},{7,23},{8,16},{9,9},... | collective-permute-start | bytes 1572872 | tf_op jit(solution)/shard_map/ppermute | solution.py:186
  40.7 0.7 collective-permute-start.8
  41.4 0.0 collective-permute-done.5
  41.4 1.7 %broadcast_select_fusion.1 = (bf16[1024,512]{1,0:T(8,128)(2,1)S(1)}, bf16[1024,512]{1,0:T(8,128)(2,1)S(1)}) fusion(bf16[1024,512]{1,0:T(8,128)(2,1)} %param.9, bf16[1024,512]{1,0:T(8,128)(2,1)} %collective-permute-done.5, pred[]{:T(512)S(6)} %eq.6), kind=kLoop, calls=%fused_computation.13 | loop fusion | flops 1048576 | bytes 4194305 | tf_op jit(solution)/shard_map/jit(_where)/select_n | solution.py:154
  43.1 8.6 %collective-permute-done.9 = bf16[256,1024]{1,0:T(8,128)(2,1)S(1)} collective-permute-done((bf16[256,1024]{1,0:T(8,128)(2,1)S(1)}, bf16[256,1024]{1,0:T(8,128)(2,1)S(1)}, u32[]{:S(2)}, u32[]{:S(2)}) %collective-permute-start.9) | collective-permute-done | bytes 524320 | tf_op jit(solution)/shard_map/ppermute | solution.py:186
  51.8 0.7 convolution_convert_fusion
  52.5 0.1 collective-permute-start.10
  52.6 11.9 %collective-permute-start.4 = (bf16[256,1024]{1,0:T(8,128)(2,1)S(1)}, bf16[256,1024]{1,0:T(8,128)(2,1)S(1)}, u32[]{:S(2)}, u32[]{:S(2)}) collective-permute-start(bf16[256,1024]{1,0:T(8,128)(2,1)S(1)} %shard_map.57), channel_id=1, source_target_pairs={{0,0},{1,9},{2,18},{3,27},{4,4},{5,13},{6,22},{7,31},{8,8},{9,17},... | collective-permute-start | bytes 1572872 | tf_op jit(solution)/shard_map/ppermute | solution.py:186
  64.5 0.0 collective-permute-done.6
  64.5 0.7 convolution_convert_fusion.2
  65.2 1.6 %collective-permute-start.7 = (bf16[256,1024]{1,0:T(8,128)(2,1)S(1)}, bf16[256,1024]{1,0:T(8,128)(2,1)S(1)}, u32[]{:S(2)}, u32[]{:S(2)}) collective-permute-start(bf16[256,1024]{1,0:T(8,128)(2,1)S(1)} %convolution_convert_fusion.2), channel_id=1, source_target_pairs={{0,1},{1,0},{2,3},{3,2},{4,5},{5,4},{6,7},{7,6},{8,9},{9,8},{10,11... | collective-permute-start | bytes 1572872 | tf_op jit(solution)/shard_map/ppermute | solution.py:193
  66.8 0.0 collective-permute-done.8
  66.8 0.0 collective-permute-done.10
  66.8 0.7 fusion.6
  67.5 7.9 %collective-permute-start.11 = (bf16[256,1024]{1,0:T(8,128)(2,1)S(1)}, bf16[256,1024]{1,0:T(8,128)(2,1)S(1)}, u32[]{:S(2)}, u32[]{:S(2)}) collective-permute-start(bf16[256,1024]{1,0:T(8,128)(2,1)S(1)} %fusion.6), channel_id=1, source_target_pairs={{0,2},{1,3},{2,0},{3,1},{4,6},{5,7},{6,4},{7,5},{8,10},{9,11},{10,... | collective-permute-start | bytes 1572872 | tf_op jit(solution)/shard_map/ppermute | solution.py:194
  75.4 7.2 %collective-permute-done.4 = bf16[256,1024]{1,0:T(8,128)(2,1)S(1)} collective-permute-done((bf16[256,1024]{1,0:T(8,128)(2,1)S(1)}, bf16[256,1024]{1,0:T(8,128)(2,1)S(1)}, u32[]{:S(2)}, u32[]{:S(2)}) %collective-permute-start.4) | collective-permute-done | bytes 524320 | tf_op jit(solution)/shard_map/ppermute | solution.py:186
  82.7 0.0 collective-permute-done.7
  82.7 3.2 %collective-permute-done.11 = bf16[256,1024]{1,0:T(8,128)(2,1)S(1)} collective-permute-done((bf16[256,1024]{1,0:T(8,128)(2,1)S(1)}, bf16[256,1024]{1,0:T(8,128)(2,1)S(1)}, u32[]{:S(2)}, u32[]{:S(2)}) %collective-permute-start.11) | collective-permute-done | bytes 524320 | tf_op jit(solution)/shard_map/ppermute | solution.py:194
  85.9 0.8 fusion.3
  86.6 6.2 %collective-permute-start.12 = (bf16[256,1024]{1,0:T(8,128)(2,1)S(1)}, bf16[256,1024]{1,0:T(8,128)(2,1)S(1)}, u32[]{:S(2)}, u32[]{:S(2)}) collective-permute-start(bf16[256,1024]{1,0:T(8,128)(2,1)S(1)} %fusion.3), channel_id=1, source_target_pairs={{0,0},{1,24},{2,16},{3,8},{4,4},{5,28},{6,20},{7,12},{8,9},{9,1},{... | collective-permute-start | bytes 1572872 | tf_op jit(solution)/shard_map/ppermute | solution.py:198
  92.8 14.7 %collective-permute-done.12 = bf16[256,1024]{1,0:T(8,128)(2,1)S(1)} collective-permute-done((bf16[256,1024]{1,0:T(8,128)(2,1)S(1)}, bf16[256,1024]{1,0:T(8,128)(2,1)S(1)}, u32[]{:S(2)}, u32[]{:S(2)}) %collective-permute-start.12) | collective-permute-done | bytes 524320 | tf_op jit(solution)/shard_map/ppermute | solution.py:198
  107.5 0.8 copy.7
Async XLA Ops:
  0.0 1.0 copy-start
  1.0 1.0 copy-start.2
  2.4 8.1 %collective-permute-start = (bf16[8,128,128]{2,1,0:T(8,128)(2,1)S(1)}, bf16[8,128,128]{2,1,0:T(8,128)(2,1)S(1)}, u32[]{:S(2)}, u32[]{:S(2)}) collective-permute-start(bf16[8,128,128]{2,1,0:T(8,128)(2,1)S(1)} %get-tuple-element.7), channel_id=1, source_target_pairs={{0,4},{4,0},{8,12},{12,8},{16,20},{20,16},{24,28},{28,24},{1,5},{5... | collective-permute-start | bytes 786440 | tf_op jit(solution)/shard_map/ppermute | solution.py:139
  10.6 8.2 %collective-permute-start.1 = (bf16[8,128,128]{2,1,0:T(8,128)(2,1)S(1)}, bf16[8,128,128]{2,1,0:T(8,128)(2,1)S(1)}, u32[]{:S(2)}, u32[]{:S(2)}) collective-permute-start(bf16[8,128,128]{2,1,0:T(8,128)(2,1)S(1)} %fusion.7), channel_id=1, source_target_pairs={{0,8},{4,12},{1,9},{5,13},{2,10},{6,14},{3,11},{7,15}} | collective-permute-start | bytes 786440 | tf_op jit(solution)/shard_map/ppermute | solution.py:144
  14.1 27.3 %collective-permute-start.5 = (bf16[1024,512]{1,0:T(8,128)(2,1)}, bf16[1024,512]{1,0:T(8,128)(2,1)}, u32[]{:S(2)}, u32[]{:S(2)}) collective-permute-start(bf16[1024,512]{1,0:T(8,128)(2,1)} %param.9), channel_id=1, source_target_pairs={{0,4},{4,0},{8,12},{12,8},{16,20},{20,16},{24,28},{28,24},{1,5},{5... | collective-permute-start | bytes 3145736 | tf_op jit(solution)/shard_map/ppermute | solution.py:151
  18.9 1.7 %copy-start.1 = (bf16[256,1024]{1,0:T(8,128)(2,1)S(1)}, bf16[256,1024]{1,0:T(8,128)(2,1)}, u32[]{:S(2)}) copy-start(bf16[256,1024]{1,0:T(8,128)(2,1)} %k_ref.3) | copy-start | bytes 1572868
  18.9 1.7 %copy-start.3 = (bf16[256,1024]{1,0:T(8,128)(2,1)S(1)}, bf16[256,1024]{1,0:T(8,128)(2,1)}, u32[]{:S(2)}) copy-start(bf16[256,1024]{1,0:T(8,128)(2,1)} %v_ref.3) | copy-start | bytes 1572868
  18.9 1.7 %copy-start.4 = (bf16[256,1024]{1,0:T(8,128)(2,1)S(1)}, bf16[256,1024]{1,0:T(8,128)(2,1)}, u32[]{:S(2)}) copy-start(bf16[256,1024]{1,0:T(8,128)(2,1)} %q_ref.3) | copy-start | bytes 1572868
  18.9 0.8 collective-permute-start.2
  19.9 1.7 %collective-permute-start.3 = (bf16[8,128,128]{2,1,0:T(8,128)(2,1)S(1)}, bf16[8,128,128]{2,1,0:T(8,128)(2,1)S(1)}, u32[]{:S(2)}, u32[]{:S(2)}) collective-permute-start(bf16[8,128,128]{2,1,0:T(8,128)(2,1)S(1)} %add_convert_fusion), channel_id=1, source_target_pairs={{16,24},{20,28},{17,25},{21,29},{18,26},{22,30},{19,27},{23,31}} | collective-permute-start | bytes 786440 | tf_op jit(solution)/shard_map/ppermute | solution.py:144
  20.6 1.0 copy-start.5
  22.3 29.4 %collective-permute-start.9 = (bf16[256,1024]{1,0:T(8,128)(2,1)S(1)}, bf16[256,1024]{1,0:T(8,128)(2,1)S(1)}, u32[]{:S(2)}, u32[]{:S(2)}) collective-permute-start(bf16[256,1024]{1,0:T(8,128)(2,1)S(1)} %shard_map.57), channel_id=1, source_target_pairs={{0,24},{1,17},{2,10},{3,3},{4,28},{5,21},{6,14},{7,7},{8,0},{9,25}... | collective-permute-start | bytes 1572872 | tf_op jit(solution)/shard_map/ppermute | solution.py:186
  31.5 33.0 %collective-permute-start.6 = (bf16[256,1024]{1,0:T(8,128)(2,1)S(1)}, bf16[256,1024]{1,0:T(8,128)(2,1)S(1)}, u32[]{:S(2)}, u32[]{:S(2)}) collective-permute-start(bf16[256,1024]{1,0:T(8,128)(2,1)S(1)} %shard_map.57), channel_id=1, source_target_pairs={{0,8},{1,1},{2,26},{3,19},{4,12},{5,5},{6,30},{7,23},{8,16},{9,9},... | collective-permute-start | bytes 1572872 | tf_op jit(solution)/shard_map/ppermute | solution.py:186
  40.7 26.1 %collective-permute-start.8 = (bf16[256,1024]{1,0:T(8,128)(2,1)S(1)}, bf16[256,1024]{1,0:T(8,128)(2,1)S(1)}, u32[]{:S(2)}, u32[]{:S(2)}) collective-permute-start(bf16[256,1024]{1,0:T(8,128)(2,1)S(1)} %shard_map.57), channel_id=1, source_target_pairs={{0,16},{1,25},{2,2},{3,11},{4,20},{5,29},{6,6},{7,15},{8,24},{9,1}... | collective-permute-start | bytes 1572872 | tf_op jit(solution)/shard_map/ppermute | solution.py:186
  52.5 14.3 %collective-permute-start.10 = (bf16[256,1024]{1,0:T(8,128)(2,1)S(1)}, bf16[256,1024]{1,0:T(8,128)(2,1)S(1)}, u32[]{:S(2)}, u32[]{:S(2)}) collective-permute-start(bf16[256,1024]{1,0:T(8,128)(2,1)S(1)} %convolution_convert_fusion), channel_id=1, source_target_pairs={{0,1},{1,0},{2,3},{3,2},{4,5},{5,4},{6,7},{7,6},{8,9},{9,8},{10,11... | collective-permute-start | bytes 1572872 | tf_op jit(solution)/shard_map/ppermute | solution.py:192
  52.6 30.1 %collective-permute-start.4 = (bf16[256,1024]{1,0:T(8,128)(2,1)S(1)}, bf16[256,1024]{1,0:T(8,128)(2,1)S(1)}, u32[]{:S(2)}, u32[]{:S(2)}) collective-permute-start(bf16[256,1024]{1,0:T(8,128)(2,1)S(1)} %shard_map.57), channel_id=1, source_target_pairs={{0,0},{1,9},{2,18},{3,27},{4,4},{5,13},{6,22},{7,31},{8,8},{9,17},... | collective-permute-start | bytes 1572872 | tf_op jit(solution)/shard_map/ppermute | solution.py:186
  65.2 17.5 %collective-permute-start.7 = (bf16[256,1024]{1,0:T(8,128)(2,1)S(1)}, bf16[256,1024]{1,0:T(8,128)(2,1)S(1)}, u32[]{:S(2)}, u32[]{:S(2)}) collective-permute-start(bf16[256,1024]{1,0:T(8,128)(2,1)S(1)} %convolution_convert_fusion.2), channel_id=1, source_target_pairs={{0,1},{1,0},{2,3},{3,2},{4,5},{5,4},{6,7},{7,6},{8,9},{9,8},{10,11... | collective-permute-start | bytes 1572872 | tf_op jit(solution)/shard_map/ppermute | solution.py:193
  67.5 18.4 %collective-permute-start.11 = (bf16[256,1024]{1,0:T(8,128)(2,1)S(1)}, bf16[256,1024]{1,0:T(8,128)(2,1)S(1)}, u32[]{:S(2)}, u32[]{:S(2)}) collective-permute-start(bf16[256,1024]{1,0:T(8,128)(2,1)S(1)} %fusion.6), channel_id=1, source_target_pairs={{0,2},{1,3},{2,0},{3,1},{4,6},{5,7},{6,4},{7,5},{8,10},{9,11},{10,... | collective-permute-start | bytes 1572872 | tf_op jit(solution)/shard_map/ppermute | solution.py:194
  86.6 20.8 %collective-permute-start.12 = (bf16[256,1024]{1,0:T(8,128)(2,1)S(1)}, bf16[256,1024]{1,0:T(8,128)(2,1)S(1)}, u32[]{:S(2)}, u32[]{:S(2)}) collective-permute-start(bf16[256,1024]{1,0:T(8,128)(2,1)S(1)} %fusion.3), channel_id=1, source_target_pairs={{0,0},{1,24},{2,16},{3,8},{4,4},{5,28},{6,20},{7,12},{8,9},{9,1},{... | collective-permute-start | bytes 1572872 | tf_op jit(solution)/shard_map/ppermute | solution.py:198

commit v10 on v9

--- a/solution.py
+++ b/solution.py
@@ -178,11 +178,12 @@
         second = lax.axis_index("seq") % 2
         attended = attend(second, queries, within, norm_gain, mate, *earlier)
 
+        def tile(h):
+            return (0, 3, 1, 2)[h]
+
         parts = [None] * head_groups
         for j in (3, 2, 1, 0):
-            pairs = [
-                (flat(z, y, h), flat((z + (h ^ j)) % planes, y, h)) for z, y, h in everywhere
-            ]
+            pairs = [(flat(z, y, h), flat(z ^ tile(h ^ j), y, h)) for z, y, h in everywhere]
             parts[j] = lax.ppermute(attended, ("seq", "head"), pairs)
         parts = [
             jnp.dot(part, weight, preferred_element_type=F32).astype(BF16) for part in parts
@@ -193,7 +194,7 @@
         near = parts[0].astype(F32) + lax.ppermute(parts[1], "head", core).astype(F32)
         near += lax.ppermute(far.astype(BF16), "head", chip).astype(F32)
         home = [
-            (flat(z, y, h), flat((z - h) % planes, y, z)) for z, y, h in everywhere
+            (flat(z, y, h), flat(z ^ tile(h), y, z)) for z, y, h in everywhere
         ]
         return lax.ppermute(near.astype(BF16), ("seq", "head"), home)
 

time: 109 us -> 111 us (1.018)
  the two profiles are of different devices: /device:TPU:2 before, /device:TPU:1 now
where the time goes in v10:
time: 111 us
  starting transfers between devices  69.8 us (63%)
  waiting for transfers between devices  31.2 us (28%)
  local copies, waits for them, and re-layouts  2.9 us (3%)
  matrix products  2.86 us (3%)
  Pallas kernels  2.05 us (2%)
  other arithmetic  1.96 us (2%)
    ppermute x1, starting transfers between devices, body(): lax.ppermute(parts[3], 'head', core).astype(F32)  25.5 us
    ppermute x4, starting transfers between devices, body(): parts[j] = lax.ppermute(attended, ('seq', 'head'), pairs)  24.8 us
    ppermute x1, waiting for transfers between devices, body(): near += lax.ppermute(far.astype(BF16), 'head', chip).astype(F32)  10.6 us
    ppermute x1, waiting for transfers between devices, body(): return lax.ppermute(near.astype(BF16), ('seq', 'head'), home)  10.1 us
    ppermute x1, starting transfers between devices, body(): return lax.ppermute(near.astype(BF16), ('seq', 'head'), home)  8 us
    ppermute x1, waiting for transfers between devices, prefix_over_planes(): mate = lax.ppermute(narrow, 'seq', [(s, s ^ 1) for s in range(seq_count)])  6.03 us
    ppermute x3, starting transfers between devices, prefix_over_planes(): earlier.append(lax.ppermute(onward.astype(BF16), 'seq', pairs))  4.6 us
    ppermute x1, starting transfers between devices, body(): near += lax.ppermute(far.astype(BF16), 'head', chip).astype(F32)  3.41 us
  transfers between devices with their start and end apart: 13, of which 5 were waited for; matrix products, arithmetic and copies ran while one was open for 4% of the time, Pallas kernels for 2%

profile of v10, /device:TPU:1, one launch (start us, length us, event | category | flops | bytes accessed | tf_op | source)
XLA Modules:
  0.0 111.0 jit_solution(16713549272522620809)
XLA Ops:
  0.0 0.0 copy-start
  0.0 1.0 copy-done
  1.0 0.0 copy-start.2
  1.0 1.0 copy-done.2
  2.1 0.4 shard_map.56
  2.4 2.1 %collective-permute-start = (bf16[8,128,128]{2,1,0:T(8,128)(2,1)S(1)}, bf16[8,128,128]{2,1,0:T(8,128)(2,1)S(1)}, u32[]{:S(2)}, u32[]{:S(2)}) collective-permute-start(bf16[8,128,128]{2,1,0:T(8,128)(2,1)S(1)} %get-tuple-element.7), channel_id=1, source_target_pairs={{0,4},{4,0},{8,12},{12,8},{16,20},{20,16},{24,28},{28,24},{1,5},{5... | collective-permute-start | bytes 786440 | tf_op jit(solution)/shard_map/ppermute | solution.py:139
  4.6 6.0 %collective-permute-done.mate_ref = bf16[8,128,128]{2,1,0:T(8,128)(2,1)S(1)} collective-permute-done((bf16[8,128,128]{2,1,0:T(8,128)(2,1)S(1)}, bf16[8,128,128]{2,1,0:T(8,128)(2,1)S(1)}, u32[]{:S(2)}, u32[]{:S(2)}) %collective-permute-start) | collective-permute-done | bytes 262176 | tf_op jit(solution)/shard_map/ppermute | solution.py:139
  10.6 0.1 fusion.7
  10.7 3.1 %collective-permute-start.1 = (bf16[8,128,128]{2,1,0:T(8,128)(2,1)S(1)}, bf16[8,128,128]{2,1,0:T(8,128)(2,1)S(1)}, u32[]{:S(2)}, u32[]{:S(2)}) collective-permute-start(bf16[8,128,128]{2,1,0:T(8,128)(2,1)S(1)} %fusion.7), channel_id=1, source_target_pairs={{0,8},{4,12},{1,9},{5,13},{2,10},{6,14},{3,11},{7,15}} | collective-permute-start | bytes 786440 | tf_op jit(solution)/shard_map/ppermute | solution.py:144
  13.8 1.3 %collective-permute-start.5 = (bf16[1024,512]{1,0:T(8,128)(2,1)}, bf16[1024,512]{1,0:T(8,128)(2,1)}, u32[]{:S(2)}, u32[]{:S(2)}) collective-permute-start(bf16[1024,512]{1,0:T(8,128)(2,1)} %param.9), channel_id=1, source_target_pairs={{0,4},{4,0},{8,12},{12,8},{16,20},{20,16},{24,28},{28,24},{1,5},{5... | collective-permute-start | bytes 3145736 | tf_op jit(solution)/shard_map/ppermute | solution.py:151
  15.1 2.7 %collective-permute-done.1.refs_0_ = bf16[8,128,128]{2,1,0:T(8,128)(2,1)S(1)} collective-permute-done((bf16[8,128,128]{2,1,0:T(8,128)(2,1)S(1)}, bf16[8,128,128]{2,1,0:T(8,128)(2,1)S(1)}, u32[]{:S(2)}, u32[]{:S(2)}) %collective-permute-start.1) | collective-permute-done | bytes 262176 | tf_op jit(solution)/shard_map/ppermute | solution.py:144
  17.8 0.1 fusion.8
  17.9 0.0 copy-start.1
  17.9 0.0 copy-start.3
  17.9 0.0 copy-start.4
  17.9 0.8 collective-permute-start.2
  18.8 0.0 collective-permute-done.2.refs_1_
  18.8 0.1 add_convert_fusion
  18.9 0.7 collective-permute-start.3
  19.6 0.0 copy-done.1
  19.6 0.0 copy-done.3
  19.6 0.0 copy-done.4
  19.6 0.0 copy-start.5
  19.7 0.9 shard_map.55.within_ref
  20.6 0.0 collective-permute-done.3.refs_2_
  20.6 0.0 copy-done.5
  20.6 0.8 shard_map.57
  21.4 8.1 %collective-permute-start.9 = (bf16[256,1024]{1,0:T(8,128)(2,1)S(1)}, bf16[256,1024]{1,0:T(8,128)(2,1)S(1)}, u32[]{:S(2)}, u32[]{:S(2)}) collective-permute-start(bf16[256,1024]{1,0:T(8,128)(2,1)S(1)} %shard_map.57), channel_id=1, source_target_pairs={{0,16},{1,9},{2,26},{3,3},{4,20},{5,13},{6,30},{7,7},{8,24},{9,1},... | collective-permute-start | bytes 1572872 | tf_op jit(solution)/shard_map/ppermute | solution.py:187
  29.5 0.7 collective-permute-start.6
  30.2 9.3 %collective-permute-start.8 = (bf16[256,1024]{1,0:T(8,128)(2,1)S(1)}, bf16[256,1024]{1,0:T(8,128)(2,1)S(1)}, u32[]{:S(2)}, u32[]{:S(2)}) collective-permute-start(bf16[256,1024]{1,0:T(8,128)(2,1)S(1)} %shard_map.57), channel_id=1, source_target_pairs={{0,8},{1,17},{2,2},{3,27},{4,12},{5,21},{6,6},{7,31},{8,0},{9,25},... | collective-permute-start | bytes 1572872 | tf_op jit(solution)/shard_map/ppermute | solution.py:187
  39.5 0.0 collective-permute-done.5
  39.6 1.7 %broadcast_select_fusion.1 = (bf16[1024,512]{1,0:T(8,128)(2,1)S(1)}, bf16[1024,512]{1,0:T(8,128)(2,1)S(1)}) fusion(bf16[1024,512]{1,0:T(8,128)(2,1)} %param.9, bf16[1024,512]{1,0:T(8,128)(2,1)} %collective-permute-done.5, pred[]{:T(512)S(6)} %eq.6), kind=kLoop, calls=%fused_computation.13 | loop fusion | flops 1048576 | bytes 4194305 | tf_op jit(solution)/shard_map/jit(_where)/select_n | solution.py:154
  41.2 0.0 collective-permute-done.9
  41.3 0.7 convolution_convert_fusion
  42.0 25.5 %collective-permute-start.10 = (bf16[256,1024]{1,0:T(8,128)(2,1)S(1)}, bf16[256,1024]{1,0:T(8,128)(2,1)S(1)}, u32[]{:S(2)}, u32[]{:S(2)}) collective-permute-start(bf16[256,1024]{1,0:T(8,128)(2,1)S(1)} %convolution_convert_fusion), channel_id=1, source_target_pairs={{0,1},{1,0},{2,3},{3,2},{4,5},{5,4},{6,7},{7,6},{8,9},{9,8},{10,11... | collective-permute-start | bytes 1572872 | tf_op jit(solution)/shard_map/ppermute | solution.py:193
  67.4 6.7 %collective-permute-start.4 = (bf16[256,1024]{1,0:T(8,128)(2,1)S(1)}, bf16[256,1024]{1,0:T(8,128)(2,1)S(1)}, u32[]{:S(2)}, u32[]{:S(2)}) collective-permute-start(bf16[256,1024]{1,0:T(8,128)(2,1)S(1)} %shard_map.57), channel_id=1, source_target_pairs={{0,0},{1,25},{2,10},{3,19},{4,4},{5,29},{6,14},{7,23},{8,8},{9,17}... | collective-permute-start | bytes 1572872 | tf_op jit(solution)/shard_map/ppermute | solution.py:187
  74.1 0.0 collective-permute-done.6
  74.1 0.7 convolution_convert_fusion.2
  74.9 0.1 collective-permute-start.7
  74.9 0.0 collective-permute-done.8
  74.9 0.0 collective-permute-done.10
  75.0 0.7 fusion.6
  75.7 3.4 %collective-permute-start.11 = (bf16[256,1024]{1,0:T(8,128)(2,1)S(1)}, bf16[256,1024]{1,0:T(8,128)(2,1)S(1)}, u32[]{:S(2)}, u32[]{:S(2)}) collective-permute-start(bf16[256,1024]{1,0:T(8,128)(2,1)S(1)} %fusion.6), channel_id=1, source_target_pairs={{0,2},{1,3},{2,0},{3,1},{4,6},{5,7},{6,4},{7,5},{8,10},{9,11},{10,... | collective-permute-start | bytes 1572872 | tf_op jit(solution)/shard_map/ppermute | solution.py:195
  79.1 1.7 %collective-permute-done.4 = bf16[256,1024]{1,0:T(8,128)(2,1)S(1)} collective-permute-done((bf16[256,1024]{1,0:T(8,128)(2,1)S(1)}, bf16[256,1024]{1,0:T(8,128)(2,1)S(1)}, u32[]{:S(2)}, u32[]{:S(2)}) %collective-permute-start.4) | collective-permute-done | bytes 524320 | tf_op jit(solution)/shard_map/ppermute | solution.py:187
  80.8 0.0 collective-permute-done.7
  80.8 10.6 %collective-permute-done.11 = bf16[256,1024]{1,0:T(8,128)(2,1)S(1)} collective-permute-done((bf16[256,1024]{1,0:T(8,128)(2,1)S(1)}, bf16[256,1024]{1,0:T(8,128)(2,1)S(1)}, u32[]{:S(2)}, u32[]{:S(2)}) %collective-permute-start.11) | collective-permute-done | bytes 524320 | tf_op jit(solution)/shard_map/ppermute | solution.py:195
  91.4 0.7 fusion.3
  92.1 8.0 %collective-permute-start.12 = (bf16[256,1024]{1,0:T(8,128)(2,1)S(1)}, bf16[256,1024]{1,0:T(8,128)(2,1)S(1)}, u32[]{:S(2)}, u32[]{:S(2)}) collective-permute-start(bf16[256,1024]{1,0:T(8,128)(2,1)S(1)} %fusion.3), channel_id=1, source_target_pairs={{0,0},{1,24},{2,8},{3,16},{4,4},{5,28},{6,12},{7,20},{8,9},{9,17},... | collective-permute-start | bytes 1572872 | tf_op jit(solution)/shard_map/ppermute | solution.py:199
  100.1 10.1 %collective-permute-done.12 = bf16[256,1024]{1,0:T(8,128)(2,1)S(1)} collective-permute-done((bf16[256,1024]{1,0:T(8,128)(2,1)S(1)}, bf16[256,1024]{1,0:T(8,128)(2,1)S(1)}, u32[]{:S(2)}, u32[]{:S(2)}) %collective-permute-start.12) | collective-permute-done | bytes 524320 | tf_op jit(solution)/shard_map/ppermute | solution.py:199
  110.2 0.8 copy.7
Async XLA Ops:
  0.0 1.0 copy-start
  1.0 1.0 copy-start.2
  2.4 8.2 %collective-permute-start = (bf16[8,128,128]{2,1,0:T(8,128)(2,1)S(1)}, bf16[8,128,128]{2,1,0:T(8,128)(2,1)S(1)}, u32[]{:S(2)}, u32[]{:S(2)}) collective-permute-start(bf16[8,128,128]{2,1,0:T(8,128)(2,1)S(1)} %get-tuple-element.7), channel_id=1, source_target_pairs={{0,4},{4,0},{8,12},{12,8},{16,20},{20,16},{24,28},{28,24},{1,5},{5... | collective-permute-start | bytes 786440 | tf_op jit(solution)/shard_map/ppermute | solution.py:139
  10.7 7.1 %collective-permute-start.1 = (bf16[8,128,128]{2,1,0:T(8,128)(2,1)S(1)}, bf16[8,128,128]{2,1,0:T(8,128)(2,1)S(1)}, u32[]{:S(2)}, u32[]{:S(2)}) collective-permute-start(bf16[8,128,128]{2,1,0:T(8,128)(2,1)S(1)} %fusion.7), channel_id=1, source_target_pairs={{0,8},{4,12},{1,9},{5,13},{2,10},{6,14},{3,11},{7,15}} | collective-permute-start | bytes 786440 | tf_op jit(solution)/shard_map/ppermute | solution.py:144
  13.8 25.8 %collective-permute-start.5 = (bf16[1024,512]{1,0:T(8,128)(2,1)}, bf16[1024,512]{1,0:T(8,128)(2,1)}, u32[]{:S(2)}, u32[]{:S(2)}) collective-permute-start(bf16[1024,512]{1,0:T(8,128)(2,1)} %param.9), channel_id=1, source_target_pairs={{0,4},{4,0},{8,12},{12,8},{16,20},{20,16},{24,28},{28,24},{1,5},{5... | collective-permute-start | bytes 3145736 | tf_op jit(solution)/shard_map/ppermute | solution.py:151
  17.9 1.7 %copy-start.1 = (bf16[256,1024]{1,0:T(8,128)(2,1)S(1)}, bf16[256,1024]{1,0:T(8,128)(2,1)}, u32[]{:S(2)}) copy-start(bf16[256,1024]{1,0:T(8,128)(2,1)} %k_ref.3) | copy-start | bytes 1572868
  17.9 1.7 %copy-start.3 = (bf16[256,1024]{1,0:T(8,128)(2,1)S(1)}, bf16[256,1024]{1,0:T(8,128)(2,1)}, u32[]{:S(2)}) copy-start(bf16[256,1024]{1,0:T(8,128)(2,1)} %v_ref.3) | copy-start | bytes 1572868
  17.9 1.7 %copy-start.4 = (bf16[256,1024]{1,0:T(8,128)(2,1)S(1)}, bf16[256,1024]{1,0:T(8,128)(2,1)}, u32[]{:S(2)}) copy-start(bf16[256,1024]{1,0:T(8,128)(2,1)} %q_ref.3) | copy-start | bytes 1572868
  17.9 0.8 collective-permute-start.2
  18.9 1.7 %collective-permute-start.3 = (bf16[8,128,128]{2,1,0:T(8,128)(2,1)S(1)}, bf16[8,128,128]{2,1,0:T(8,128)(2,1)S(1)}, u32[]{:S(2)}, u32[]{:S(2)}) collective-permute-start(bf16[8,128,128]{2,1,0:T(8,128)(2,1)S(1)} %add_convert_fusion), channel_id=1, source_target_pairs={{16,24},{20,28},{17,25},{21,29},{18,26},{22,30},{19,27},{23,31}} | collective-permute-start | bytes 786440 | tf_op jit(solution)/shard_map/ppermute | solution.py:144
  19.6 1.0 copy-start.5
  21.4 19.9 %collective-permute-start.9 = (bf16[256,1024]{1,0:T(8,128)(2,1)S(1)}, bf16[256,1024]{1,0:T(8,128)(2,1)S(1)}, u32[]{:S(2)}, u32[]{:S(2)}) collective-permute-start(bf16[256,1024]{1,0:T(8,128)(2,1)S(1)} %shard_map.57), channel_id=1, source_target_pairs={{0,16},{1,9},{2,26},{3,3},{4,20},{5,13},{6,30},{7,7},{8,24},{9,1},... | collective-permute-start | bytes 1572872 | tf_op jit(solution)/shard_map/ppermute | solution.py:187
  29.5 44.6 %collective-permute-start.6 = (bf16[256,1024]{1,0:T(8,128)(2,1)S(1)}, bf16[256,1024]{1,0:T(8,128)(2,1)S(1)}, u32[]{:S(2)}, u32[]{:S(2)}) collective-permute-start(bf16[256,1024]{1,0:T(8,128)(2,1)S(1)} %shard_map.57), channel_id=1, source_target_pairs={{0,24},{1,1},{2,18},{3,11},{4,28},{5,5},{6,22},{7,15},{8,16},{9,9}... | collective-permute-start | bytes 1572872 | tf_op jit(solution)/shard_map/ppermute | solution.py:187
  30.2 44.7 %collective-permute-start.8 = (bf16[256,1024]{1,0:T(8,128)(2,1)S(1)}, bf16[256,1024]{1,0:T(8,128)(2,1)S(1)}, u32[]{:S(2)}, u32[]{:S(2)}) collective-permute-start(bf16[256,1024]{1,0:T(8,128)(2,1)S(1)} %shard_map.57), channel_id=1, source_target_pairs={{0,8},{1,17},{2,2},{3,27},{4,12},{5,21},{6,6},{7,31},{8,0},{9,25},... | collective-permute-start | bytes 1572872 | tf_op jit(solution)/shard_map/ppermute | solution.py:187
  42.0 33.0 %collective-permute-start.10 = (bf16[256,1024]{1,0:T(8,128)(2,1)S(1)}, bf16[256,1024]{1,0:T(8,128)(2,1)S(1)}, u32[]{:S(2)}, u32[]{:S(2)}) collective-permute-start(bf16[256,1024]{1,0:T(8,128)(2,1)S(1)} %convolution_convert_fusion), channel_id=1, source_target_pairs={{0,1},{1,0},{2,3},{3,2},{4,5},{5,4},{6,7},{7,6},{8,9},{9,8},{10,11... | collective-permute-start | bytes 1572872 | tf_op jit(solution)/shard_map/ppermute | solution.py:193
  67.4 13.3 %collective-permute-start.4 = (bf16[256,1024]{1,0:T(8,128)(2,1)S(1)}, bf16[256,1024]{1,0:T(8,128)(2,1)S(1)}, u32[]{:S(2)}, u32[]{:S(2)}) collective-permute-start(bf16[256,1024]{1,0:T(8,128)(2,1)S(1)} %shard_map.57), channel_id=1, source_target_pairs={{0,0},{1,25},{2,10},{3,19},{4,4},{5,29},{6,14},{7,23},{8,8},{9,17}... | collective-permute-start | bytes 1572872 | tf_op jit(solution)/shard_map/ppermute | solution.py:187
  74.9 5.9 %collective-permute-start.7 = (bf16[256,1024]{1,0:T(8,128)(2,1)S(1)}, bf16[256,1024]{1,0:T(8,128)(2,1)S(1)}, u32[]{:S(2)}, u32[]{:S(2)}) collective-permute-start(bf16[256,1024]{1,0:T(8,128)(2,1)S(1)} %convolution_convert_fusion.2), channel_id=1, source_target_pairs={{0,1},{1,0},{2,3},{3,2},{4,5},{5,4},{6,7},{7,6},{8,9},{9,8},{10,11... | collective-permute-start | bytes 1572872 | tf_op jit(solution)/shard_map/ppermute | solution.py:194
  75.7 15.7 %collective-permute-start.11 = (bf16[256,1024]{1,0:T(8,128)(2,1)S(1)}, bf16[256,1024]{1,0:T(8,128)(2,1)S(1)}, u32[]{:S(2)}, u32[]{:S(2)}) collective-permute-start(bf16[256,1024]{1,0:T(8,128)(2,1)S(1)} %fusion.6), channel_id=1, source_target_pairs={{0,2},{1,3},{2,0},{3,1},{4,6},{5,7},{6,4},{7,5},{8,10},{9,11},{10,... | collective-permute-start | bytes 1572872 | tf_op jit(solution)/shard_map/ppermute | solution.py:195
  92.1 18.1 %collective-permute-start.12 = (bf16[256,1024]{1,0:T(8,128)(2,1)S(1)}, bf16[256,1024]{1,0:T(8,128)(2,1)S(1)}, u32[]{:S(2)}, u32[]{:S(2)}) collective-permute-start(bf16[256,1024]{1,0:T(8,128)(2,1)S(1)} %fusion.3), channel_id=1, source_target_pairs={{0,0},{1,24},{2,8},{3,16},{4,4},{5,28},{6,12},{7,20},{8,9},{9,17},... | collective-permute-start | bytes 1572872 | tf_op jit(solution)/shard_map/ppermute | solution.py:199

commit v11 on v10

--- a/solution.py
+++ b/solution.py
@@ -137,9 +137,10 @@
 
     def prefix_over_planes(wide, narrow):
         mate = lax.ppermute(narrow, "seq", [(s, s ^ 1) for s in range(seq_count)])
-        onward = wide + mate.astype(F32)
-        earlier = []
-        for plane in range(planes - 1):
+        hops = [lax.ppermute(narrow, "seq", [(i, 2 + (i ^ flip)) for i in range(2)]) for flip in (0, 1)]
+        earlier = list(hops)
+        onward = wide + mate.astype(F32) + hops[0].astype(F32) + hops[1].astype(F32)
+        for plane in range(1, planes - 1):
             pairs = [(2 * plane + i, 2 * plane + 2 + i) for i in range(2)]
             earlier.append(lax.ppermute(onward.astype(BF16), "seq", pairs))
             onward += earlier[-1].astype(F32)
@@ -183,16 +184,21 @@
 
         parts = [None] * head_groups
         for j in (3, 2, 1, 0):
+            if j == 1:
+                attended, parts[3] = lax.optimization_barrier((attended, parts[3]))
             pairs = [(flat(z, y, h), flat(z ^ tile(h ^ j), y, h)) for z, y, h in everywhere]
             parts[j] = lax.ppermute(attended, ("seq", "head"), pairs)
-        parts = [
-            jnp.dot(part, weight, preferred_element_type=F32).astype(BF16) for part in parts
-        ]
+        def project(part):
+            return jnp.dot(part, weight, preferred_element_type=F32).astype(BF16)
+
         core = [(h, h ^ 1) for h in range(head_groups)]
         chip = [(h, h ^ 2) for h in range(head_groups)]
-        far = parts[2].astype(F32) + lax.ppermute(parts[3], "head", core).astype(F32)
-        near = parts[0].astype(F32) + lax.ppermute(parts[1], "head", core).astype(F32)
-        near += lax.ppermute(far.astype(BF16), "head", chip).astype(F32)
+        far = lax.ppermute(project(parts[3]), "head", core).astype(F32)
+        far = (far + project(parts[2]).astype(F32)).astype(BF16)
+        crossed = lax.ppermute(far, "head", chip)
+        crossed, parts[1], parts[0] = lax.optimization_barrier((crossed, parts[1], parts[0]))
+        near = project(parts[0]).astype(F32) + crossed.astype(F32)
+        near += lax.ppermute(project(parts[1]), "head", core).astype(F32)
         home = [
             (flat(z, y, h), flat(z ^ tile(h), y, z)) for z, y, h in everywhere
         ]

time: 111 us -> 110 us (level); the launches traced: 111 us -> 108 us
  starting transfers between devices: 69.8 us -> 58.4 us
  waiting for transfers between devices: 31.2 us -> 39.9 us
    ppermute x4, waiting for transfers between devices: 1.72 us -> 11 us  [body(): parts[j] = lax.ppermute(attended, ('seq', 'head'), pairs)]
    ppermute x1, waiting for transfers between devices: 10.1 us -> 17.4 us  [body(): return lax.ppermute(near.astype(BF16), ('seq', 'head'), home)]
    ppermute x1, waiting for transfers between devices: 6.03 us -> 0.27 us  [prefix_over_planes(): mate = lax.ppermute(narrow, 'seq', [(s, s ^ 1) for s in range(seq_count)])]
    ppermute x1, starting transfers between devices: 8 us -> 2.81 us  [body(): return lax.ppermute(near.astype(BF16), ('seq', 'head'), home)]
    ppermute x3 -> x2, starting transfers between devices: 4.6 us -> 1.49 us  [prefix_over_planes(): earlier.append(lax.ppermute(onward.astype(BF16), 'seq', pairs))]
    ppermute x3 -> x2, waiting for transfers between devices: 2.73 us -> 0.01 us  [prefix_over_planes(): earlier.append(lax.ppermute(onward.astype(BF16), 'seq', pairs))]
    ppermute x3 -> x5, starting transfers between devices: 29 us -> 26.3 us  [the longest x1 20.6 us: body(): far = lax.ppermute(project(parts[3]), 'head', core).astype(F32)]
    ppermute x3 -> x5, waiting for transfers between devices: 10.6 us -> 11.2 us  [the longest x2 7.46 us: prefix_over_planes(): lax.ppermute(narrow, 'seq', [(i, 2 + (i ^ flip)) for i in range(2)])]
  transfers between devices with their start and end apart: 13 -> 14, of which waited for: 5 -> 7; matrix products, arithmetic and copies ran while one was open for 4% -> 3% of each run, Pallas kernels for 2% -> 2%
where the time goes in v11:
time: 110 us; the launch traced here: 108 us
  starting transfers between devices  58.4 us (53%)
  waiting for transfers between devices  39.9 us (36%)
  local copies, waits for them, and re-layouts  2.9 us (3%)
  matrix products  2.88 us (3%)
  Pallas kernels  2.06 us (2%)
  other arithmetic  1.97 us (2%)
    ppermute x4, starting transfers between devices, body(): parts[j] = lax.ppermute(attended, ('seq', 'head'), pairs)  24.4 us
    ppermute x1, starting transfers between devices, body(): far = lax.ppermute(project(parts[3]), 'head', core).astype(F32)  20.6 us
    ppermute x1, waiting for transfers between devices, body(): return lax.ppermute(near.astype(BF16), ('seq', 'head'), home)  17.4 us
    ppermute x4, waiting for transfers between devices, body(): parts[j] = lax.ppermute(attended, ('seq', 'head'), pairs)  11 us
    ppermute x2, waiting for transfers between devices, prefix_over_planes(): lax.ppermute(narrow, 'seq', [(i, 2 + (i ^ flip)) for i in range(2)])  7.46 us
    ppermute x2, starting transfers between devices, prefix_over_planes(): lax.ppermute(narrow, 'seq', [(i, 2 + (i ^ flip)) for i in range(2)])  4.51 us
    unnamed x13, local copies, waits for them, and re-layouts  2.9 us
    dot_general x4, matrix products, project(): return jnp.dot(part, weight, preferred_element_type=F32).astype(BF16)  2.88 us
  transfers between devices with their start and end apart: 14, of which 7 were waited for; matrix products, arithmetic and copies ran while one was open for 3% of the time, Pallas kernels for 2%

profile of v11, /device:TPU:1, one launch (start us, length us, event | category | flops | bytes accessed | tf_op | source)
XLA Modules:
  0.0 108.4 jit_solution(14676909780435121839)
XLA Ops:
  0.0 0.0 copy-start
  0.0 1.0 copy-done
  1.0 0.0 copy-start.2
  1.0 1.0 copy-done.2
  2.1 0.4 shard_map.56
  2.4 2.1 %collective-permute-start = (bf16[8,128,128]{2,1,0:T(8,128)(2,1)S(1)}, bf16[8,128,128]{2,1,0:T(8,128)(2,1)S(1)}, u32[]{:S(2)}, u32[]{:S(2)}) collective-permute-start(bf16[8,128,128]{2,1,0:T(8,128)(2,1)S(1)} %get-tuple-element.12), channel_id=1, source_target_pairs={{0,4},{4,0},{8,12},{12,8},{16,20},{20,16},{24,28},{28,24},{1,5},{5... | collective-permute-start | bytes 786440 | tf_op jit(solution)/shard_map/ppermute | solution.py:139
  4.6 3.2 %collective-permute-start.1 = (bf16[8,128,128]{2,1,0:T(8,128)(2,1)S(1)}, bf16[8,128,128]{2,1,0:T(8,128)(2,1)S(1)}, u32[]{:S(2)}, u32[]{:S(2)}) collective-permute-start(bf16[8,128,128]{2,1,0:T(8,128)(2,1)S(1)} %get-tuple-element.12), channel_id=1, source_target_pairs={{0,8},{4,12},{1,9},{5,13},{2,10},{6,14},{3,11},{7,15}} | collective-permute-start | bytes 786440 | tf_op jit(solution)/shard_map/ppermute | solution.py:140
  7.8 1.3 %collective-permute-start.2 = (bf16[8,128,128]{2,1,0:T(8,128)(2,1)S(1)}, bf16[8,128,128]{2,1,0:T(8,128)(2,1)S(1)}, u32[]{:S(2)}, u32[]{:S(2)}) collective-permute-start(bf16[8,128,128]{2,1,0:T(8,128)(2,1)S(1)} %get-tuple-element.12), channel_id=1, source_target_pairs={{0,12},{4,8},{1,13},{5,9},{2,14},{6,10},{3,15},{7,11}} | collective-permute-start | bytes 786440 | tf_op jit(solution)/shard_map/ppermute | solution.py:140
  9.1 1.2 %collective-permute-start.6 = (bf16[1024,512]{1,0:T(8,128)(2,1)}, bf16[1024,512]{1,0:T(8,128)(2,1)}, u32[]{:S(2)}, u32[]{:S(2)}) collective-permute-start(bf16[1024,512]{1,0:T(8,128)(2,1)} %param.9), channel_id=1, source_target_pairs={{0,4},{4,0},{8,12},{12,8},{16,20},{20,16},{24,28},{28,24},{1,5},{5... | collective-permute-start | bytes 3145736 | tf_op jit(solution)/shard_map/ppermute | solution.py:152
  10.3 0.3 collective-permute-done.mate_ref
  10.6 1.8 %collective-permute-done.1.refs_0_ = bf16[8,128,128]{2,1,0:T(8,128)(2,1)S(1)} collective-permute-done((bf16[8,128,128]{2,1,0:T(8,128)(2,1)S(1)}, bf16[8,128,128]{2,1,0:T(8,128)(2,1)S(1)}, u32[]{:S(2)}, u32[]{:S(2)}) %collective-permute-start.1) | collective-permute-done | bytes 262176 | tf_op jit(solution)/shard_map/ppermute | solution.py:140
  12.4 5.7 %collective-permute-done.2.refs_1_ = bf16[8,128,128]{2,1,0:T(8,128)(2,1)S(1)} collective-permute-done((bf16[8,128,128]{2,1,0:T(8,128)(2,1)S(1)}, bf16[8,128,128]{2,1,0:T(8,128)(2,1)S(1)}, u32[]{:S(2)}, u32[]{:S(2)}) %collective-permute-start.2) | collective-permute-done | bytes 262176 | tf_op jit(solution)/shard_map/ppermute | solution.py:140
  18.1 0.1 fusion.5
  18.2 0.0 copy-start.1
  18.2 0.0 copy-start.3
  18.2 0.0 copy-start.4
  18.2 0.8 collective-permute-start.3
  19.1 0.0 collective-permute-done.3.refs_2_
  19.1 0.2 add_convert_fusion.1
  19.2 0.7 collective-permute-start.4
  19.9 0.0 copy-done.1
  19.9 0.0 copy-done.3
  19.9 0.0 copy-done.4
  20.0 0.0 copy-start.5
  20.0 0.9 shard_map.55.within_ref
  20.9 0.0 collective-permute-done.4.refs_3_
  20.9 0.0 copy-done.5
  20.9 0.8 shard_map.57
  21.7 8.6 %collective-permute-start.5 = (bf16[256,1024]{1,0:T(8,128)(2,1)S(1)}, bf16[256,1024]{1,0:T(8,128)(2,1)S(1)}, u32[]{:S(2)}, u32[]{:S(2)}) collective-permute-start(bf16[256,1024]{1,0:T(8,128)(2,1)S(1)} %shard_map.57), channel_id=1, source_target_pairs={{0,16},{1,9},{2,26},{3,3},{4,20},{5,13},{6,30},{7,7},{8,24},{9,1},... | collective-permute-start | bytes 1572872 | tf_op jit(solution)/shard_map/ppermute | solution.py:190
  30.3 9.2 %collective-permute-start.8 = (bf16[256,1024]{1,0:T(8,128)(2,1)S(1)}, bf16[256,1024]{1,0:T(8,128)(2,1)S(1)}, u32[]{:S(2)}, u32[]{:S(2)}) collective-permute-start(bf16[256,1024]{1,0:T(8,128)(2,1)S(1)} %shard_map.57), channel_id=1, source_target_pairs={{0,8},{1,17},{2,2},{3,27},{4,12},{5,21},{6,6},{7,31},{8,0},{9,25},... | collective-permute-start | bytes 1572872 | tf_op jit(solution)/shard_map/ppermute | solution.py:190
  39.6 0.0 collective-permute-done.6
  39.6 1.7 %broadcast_select_fusion.1 = (bf16[1024,512]{1,0:T(8,128)(2,1)S(1)}, bf16[1024,512]{1,0:T(8,128)(2,1)S(1)}) fusion(bf16[1024,512]{1,0:T(8,128)(2,1)} %param.9, bf16[1024,512]{1,0:T(8,128)(2,1)} %collective-permute-done.6, pred[]{:T(512)S(6)} %eq.6), kind=kLoop, calls=%fused_computation.12 | loop fusion | flops 1048576 | bytes 4194305 | tf_op jit(solution)/shard_map/jit(_where)/select_n | solution.py:155
  41.3 0.0 collective-permute-done.5
  41.3 0.7 convolution_convert_fusion.3
  42.0 20.6 %collective-permute-start.7 = (bf16[256,1024]{1,0:T(8,128)(2,1)S(1)}, bf16[256,1024]{1,0:T(8,128)(2,1)S(1)}, u32[]{:S(2)}, u32[]{:S(2)}) collective-permute-start(bf16[256,1024]{1,0:T(8,128)(2,1)S(1)} %convolution_convert_fusion.3), channel_id=1, source_target_pairs={{0,1},{1,0},{2,3},{3,2},{4,5},{5,4},{6,7},{7,6},{8,9},{9,8},{10,11... | collective-permute-start | bytes 1572872 | tf_op jit(solution)/shard_map/ppermute | solution.py:196
  62.6 0.7 collective-permute-start.10
  63.2 5.9 %collective-permute-start.11 = (bf16[256,1024]{1,0:T(8,128)(2,1)S(1)}, bf16[256,1024]{1,0:T(8,128)(2,1)S(1)}, u32[]{:S(2)}, u32[]{:S(2)}) collective-permute-start(bf16[256,1024]{1,0:T(8,128)(2,1)S(1)} %shard_map.57), channel_id=1, source_target_pairs={{0,0},{1,25},{2,10},{3,19},{4,4},{5,29},{6,14},{7,23},{8,8},{9,17}... | collective-permute-start | bytes 1572872 | tf_op jit(solution)/shard_map/ppermute | solution.py:190
  69.1 0.0 collective-permute-done.8
  69.1 0.0 collective-permute-done.7
  69.1 0.7 add_convert_fusion
  69.9 0.1 collective-permute-start.9
  69.9 0.0 collective-permute-done.10
  70.0 11.0 %collective-permute-done.11 = bf16[256,1024]{1,0:T(8,128)(2,1)S(1)} collective-permute-done((bf16[256,1024]{1,0:T(8,128)(2,1)S(1)}, bf16[256,1024]{1,0:T(8,128)(2,1)S(1)}, u32[]{:S(2)}, u32[]{:S(2)}) %collective-permute-start.11) | collective-permute-done | bytes 524320 | tf_op jit(solution)/shard_map/ppermute | solution.py:190
  80.9 2.2 %collective-permute-done.9 = bf16[256,1024]{1,0:T(8,128)(2,1)S(1)} collective-permute-done((bf16[256,1024]{1,0:T(8,128)(2,1)S(1)}, bf16[256,1024]{1,0:T(8,128)(2,1)S(1)}, u32[]{:S(2)}, u32[]{:S(2)}) %collective-permute-start.9) | collective-permute-done | bytes 524320 | tf_op jit(solution)/shard_map/ppermute | solution.py:198
  83.1 0.7 convolution_convert_fusion
  83.9 1.2 %collective-permute-start.12 = (bf16[256,1024]{1,0:T(8,128)(2,1)S(1)}, bf16[256,1024]{1,0:T(8,128)(2,1)S(1)}, u32[]{:S(2)}, u32[]{:S(2)}) collective-permute-start(bf16[256,1024]{1,0:T(8,128)(2,1)S(1)} %convolution_convert_fusion), channel_id=1, source_target_pairs={{0,1},{1,0},{2,3},{3,2},{4,5},{5,4},{6,7},{7,6},{8,9},{9,8},{10,11... | collective-permute-start | bytes 1572872 | tf_op jit(solution)/shard_map/ppermute | solution.py:201
  85.1 1.5 %collective-permute-done.12 = bf16[256,1024]{1,0:T(8,128)(2,1)S(1)} collective-permute-done((bf16[256,1024]{1,0:T(8,128)(2,1)S(1)}, bf16[256,1024]{1,0:T(8,128)(2,1)S(1)}, u32[]{:S(2)}, u32[]{:S(2)}) %collective-permute-start.12) | collective-permute-done | bytes 524320 | tf_op jit(solution)/shard_map/ppermute | solution.py:201
  86.6 0.8 fusion.4
  87.4 2.8 %collective-permute-start.13 = (bf16[256,1024]{1,0:T(8,128)(2,1)S(1)}, bf16[256,1024]{1,0:T(8,128)(2,1)S(1)}, u32[]{:S(2)}, u32[]{:S(2)}) collective-permute-start(bf16[256,1024]{1,0:T(8,128)(2,1)S(1)} %fusion.4), channel_id=1, source_target_pairs={{0,0},{1,24},{2,8},{3,16},{4,4},{5,28},{6,12},{7,20},{8,9},{9,17},... | collective-permute-start | bytes 1572872 | tf_op jit(solution)/shard_map/ppermute | solution.py:205
  90.2 17.4 %collective-permute-done.13 = bf16[256,1024]{1,0:T(8,128)(2,1)S(1)} collective-permute-done((bf16[256,1024]{1,0:T(8,128)(2,1)S(1)}, bf16[256,1024]{1,0:T(8,128)(2,1)S(1)}, u32[]{:S(2)}, u32[]{:S(2)}) %collective-permute-start.13) | collective-permute-done | bytes 524320 | tf_op jit(solution)/shard_map/ppermute | solution.py:205
  107.6 0.8 copy.7
Async XLA Ops:
  0.0 1.0 copy-start
  1.0 1.0 copy-start.2
  2.4 8.2 %collective-permute-start = (bf16[8,128,128]{2,1,0:T(8,128)(2,1)S(1)}, bf16[8,128,128]{2,1,0:T(8,128)(2,1)S(1)}, u32[]{:S(2)}, u32[]{:S(2)}) collective-permute-start(bf16[8,128,128]{2,1,0:T(8,128)(2,1)S(1)} %get-tuple-element.12), channel_id=1, source_target_pairs={{0,4},{4,0},{8,12},{12,8},{16,20},{20,16},{24,28},{28,24},{1,5},{5... | collective-permute-start | bytes 786440 | tf_op jit(solution)/shard_map/ppermute | solution.py:139
  4.6 7.8 %collective-permute-start.1 = (bf16[8,128,128]{2,1,0:T(8,128)(2,1)S(1)}, bf16[8,128,128]{2,1,0:T(8,128)(2,1)S(1)}, u32[]{:S(2)}, u32[]{:S(2)}) collective-permute-start(bf16[8,128,128]{2,1,0:T(8,128)(2,1)S(1)} %get-tuple-element.12), channel_id=1, source_target_pairs={{0,8},{4,12},{1,9},{5,13},{2,10},{6,14},{3,11},{7,15}} | collective-permute-start | bytes 786440 | tf_op jit(solution)/shard_map/ppermute | solution.py:140
  7.8 10.3 %collective-permute-start.2 = (bf16[8,128,128]{2,1,0:T(8,128)(2,1)S(1)}, bf16[8,128,128]{2,1,0:T(8,128)(2,1)S(1)}, u32[]{:S(2)}, u32[]{:S(2)}) collective-permute-start(bf16[8,128,128]{2,1,0:T(8,128)(2,1)S(1)} %get-tuple-element.12), channel_id=1, source_target_pairs={{0,12},{4,8},{1,13},{5,9},{2,14},{6,10},{3,15},{7,11}} | collective-permute-start | bytes 786440 | tf_op jit(solution)/shard_map/ppermute | solution.py:140
  9.1 30.5 %collective-permute-start.6 = (bf16[1024,512]{1,0:T(8,128)(2,1)}, bf16[1024,512]{1,0:T(8,128)(2,1)}, u32[]{:S(2)}, u32[]{:S(2)}) collective-permute-start(bf16[1024,512]{1,0:T(8,128)(2,1)} %param.9), channel_id=1, source_target_pairs={{0,4},{4,0},{8,12},{12,8},{16,20},{20,16},{24,28},{28,24},{1,5},{5... | collective-permute-start | bytes 3145736 | tf_op jit(solution)/shard_map/ppermute | solution.py:152
  18.2 1.7 %copy-start.1 = (bf16[256,1024]{1,0:T(8,128)(2,1)S(1)}, bf16[256,1024]{1,0:T(8,128)(2,1)}, u32[]{:S(2)}) copy-start(bf16[256,1024]{1,0:T(8,128)(2,1)} %k_ref.3) | copy-start | bytes 1572868
  18.2 1.7 %copy-start.3 = (bf16[256,1024]{1,0:T(8,128)(2,1)S(1)}, bf16[256,1024]{1,0:T(8,128)(2,1)}, u32[]{:S(2)}) copy-start(bf16[256,1024]{1,0:T(8,128)(2,1)} %v_ref.3) | copy-start | bytes 1572868
  18.2 1.7 %copy-start.4 = (bf16[256,1024]{1,0:T(8,128)(2,1)S(1)}, bf16[256,1024]{1,0:T(8,128)(2,1)}, u32[]{:S(2)}) copy-start(bf16[256,1024]{1,0:T(8,128)(2,1)} %q_ref.3) | copy-start | bytes 1572868
  18.2 0.8 collective-permute-start.3
  19.2 1.7 %collective-permute-start.4 = (bf16[8,128,128]{2,1,0:T(8,128)(2,1)S(1)}, bf16[8,128,128]{2,1,0:T(8,128)(2,1)S(1)}, u32[]{:S(2)}, u32[]{:S(2)}) collective-permute-start(bf16[8,128,128]{2,1,0:T(8,128)(2,1)S(1)} %add_convert_fusion.1), channel_id=1, source_target_pairs={{16,24},{20,28},{17,25},{21,29},{18,26},{22,30},{19,27},{23,31}} | collective-permute-start | bytes 786440 | tf_op jit(solution)/shard_map/ppermute | solution.py:145
  20.0 1.0 copy-start.5
  21.7 19.5 %collective-permute-start.5 = (bf16[256,1024]{1,0:T(8,128)(2,1)S(1)}, bf16[256,1024]{1,0:T(8,128)(2,1)S(1)}, u32[]{:S(2)}, u32[]{:S(2)}) collective-permute-start(bf16[256,1024]{1,0:T(8,128)(2,1)S(1)} %shard_map.57), channel_id=1, source_target_pairs={{0,16},{1,9},{2,26},{3,3},{4,20},{5,13},{6,30},{7,7},{8,24},{9,1},... | collective-permute-start | bytes 1572872 | tf_op jit(solution)/shard_map/ppermute | solution.py:190
  30.3 38.8 %collective-permute-start.8 = (bf16[256,1024]{1,0:T(8,128)(2,1)S(1)}, bf16[256,1024]{1,0:T(8,128)(2,1)S(1)}, u32[]{:S(2)}, u32[]{:S(2)}) collective-permute-start(bf16[256,1024]{1,0:T(8,128)(2,1)S(1)} %shard_map.57), channel_id=1, source_target_pairs={{0,8},{1,17},{2,2},{3,27},{4,12},{5,21},{6,6},{7,31},{8,0},{9,25},... | collective-permute-start | bytes 1572872 | tf_op jit(solution)/shard_map/ppermute | solution.py:190
  42.0 27.2 %collective-permute-start.7 = (bf16[256,1024]{1,0:T(8,128)(2,1)S(1)}, bf16[256,1024]{1,0:T(8,128)(2,1)S(1)}, u32[]{:S(2)}, u32[]{:S(2)}) collective-permute-start(bf16[256,1024]{1,0:T(8,128)(2,1)S(1)} %convolution_convert_fusion.3), channel_id=1, source_target_pairs={{0,1},{1,0},{2,3},{3,2},{4,5},{5,4},{6,7},{7,6},{8,9},{9,8},{10,11... | collective-permute-start | bytes 1572872 | tf_op jit(solution)/shard_map/ppermute | solution.py:196
  62.6 7.4 %collective-permute-start.10 = (bf16[256,1024]{1,0:T(8,128)(2,1)S(1)}, bf16[256,1024]{1,0:T(8,128)(2,1)S(1)}, u32[]{:S(2)}, u32[]{:S(2)}) collective-permute-start(bf16[256,1024]{1,0:T(8,128)(2,1)S(1)} %shard_map.57), channel_id=1, source_target_pairs={{0,24},{1,1},{2,18},{3,11},{4,28},{5,5},{6,22},{7,15},{8,16},{9,9}... | collective-permute-start | bytes 1572872 | tf_op jit(solution)/shard_map/ppermute | solution.py:190
  63.2 17.7 %collective-permute-start.11 = (bf16[256,1024]{1,0:T(8,128)(2,1)S(1)}, bf16[256,1024]{1,0:T(8,128)(2,1)S(1)}, u32[]{:S(2)}, u32[]{:S(2)}) collective-permute-start(bf16[256,1024]{1,0:T(8,128)(2,1)S(1)} %shard_map.57), channel_id=1, source_target_pairs={{0,0},{1,25},{2,10},{3,19},{4,4},{5,29},{6,14},{7,23},{8,8},{9,17}... | collective-permute-start | bytes 1572872 | tf_op jit(solution)/shard_map/ppermute | solution.py:190
  69.9 13.3 %collective-permute-start.9 = (bf16[256,1024]{1,0:T(8,128)(2,1)S(1)}, bf16[256,1024]{1,0:T(8,128)(2,1)S(1)}, u32[]{:S(2)}, u32[]{:S(2)}) collective-permute-start(bf16[256,1024]{1,0:T(8,128)(2,1)S(1)} %add_convert_fusion), channel_id=1, source_target_pairs={{0,2},{1,3},{2,0},{3,1},{4,6},{5,7},{6,4},{7,5},{8,10},{9,11},{10,... | collective-permute-start | bytes 1572872 | tf_op jit(solution)/shard_map/ppermute | solution.py:198
  83.9 2.7 %collective-permute-start.12 = (bf16[256,1024]{1,0:T(8,128)(2,1)S(1)}, bf16[256,1024]{1,0:T(8,128)(2,1)S(1)}, u32[]{:S(2)}, u32[]{:S(2)}) collective-permute-start(bf16[256,1024]{1,0:T(8,128)(2,1)S(1)} %convolution_convert_fusion), channel_id=1, source_target_pairs={{0,1},{1,0},{2,3},{3,2},{4,5},{5,4},{6,7},{7,6},{8,9},{9,8},{10,11... | collective-permute-start | bytes 1572872 | tf_op jit(solution)/shard_map/ppermute | solution.py:201
  87.4 20.3 %collective-permute-start.13 = (bf16[256,1024]{1,0:T(8,128)(2,1)S(1)}, bf16[256,1024]{1,0:T(8,128)(2,1)S(1)}, u32[]{:S(2)}, u32[]{:S(2)}) collective-permute-start(bf16[256,1024]{1,0:T(8,128)(2,1)S(1)} %fusion.4), channel_id=1, source_target_pairs={{0,0},{1,24},{2,8},{3,16},{4,4},{5,28},{6,12},{7,20},{8,9},{9,17},... | collective-permute-start | bytes 1572872 | tf_op jit(solution)/shard_map/ppermute | solution.py:205

commit v12 on v9

--- a/solution.py
+++ b/solution.py
@@ -200,13 +200,108 @@
     return body
 
 
+def project_kernel(tokens_ref, own_ref, mate_ref, out_ref):
+    for half, weight_ref in enumerate((own_ref, mate_ref)):
+        product = jnp.dot(tokens_ref[...], weight_ref[...], preferred_element_type=F32)
+        out_ref[half] = product.astype(BF16)
+
+
+def project_pair_kernel(core_ref, light_ref, heavy_ref, own_ref, mate_ref, keep_ref, send_ref):
+    def multiply(out_ref, tokens_ref):
+        project_kernel(tokens_ref, own_ref, mate_ref, out_ref)
+
+    @pl.when(core_ref[0] == 0)
+    def _():
+        multiply(send_ref, heavy_ref)
+        multiply(keep_ref, light_ref)
+
+    @pl.when(core_ref[0] != 0)
+    def _():
+        multiply(send_ref, light_ref)
+        multiply(keep_ref, heavy_ref)
+
+
+def pairs_body(queries, key_vectors, value_vectors, norm_gain, out_weight):
+    rows, features = queries.shape
+    heads = features // HD
+    size = rows * features
+    half_cols = out_weight.shape[1]
+    both = ("seq", "head")
+    place, group = lax.axis_index("seq"), lax.axis_index("head")
+    z, y, x, core = place // 2, place % 2, group // 2, group % 2
+    devices = [(s // 2, s % 2, h // 2, h % 2) for s in range(8) for h in range(4)]
+
+    def at(z, y, x, c):
+        return (z * 2 + y) * 4 + x * 2 + c
+
+    def swap(value, mask):
+        return lax.ppermute(value, "seq", [(s, s ^ mask) for s in range(8)])
+
+    def move(value, place_of, chosen=lambda z, y, x, c: True):
+        pairs = [(at(*d), at(*place_of(*d))) for d in devices if chosen(*d)]
+        return lax.ppermute(value, both, pairs)
+
+    wide, narrow = call(
+        state_kernel,
+        (
+            jax.ShapeDtypeStruct((heads, HD, HD), F32),
+            jax.ShapeDtypeStruct((heads, HD, HD), BF16),
+        ),
+        2 * size * HD,
+        4 * size + 6 * heads * HD * HD,
+    )(key_vectors, value_vectors)
+    within = call(
+        within_kernel, jax.ShapeDtypeStruct((rows, features), F32), 4 * size * BLOCK, 10 * size
+    )(queries, key_vectors, value_vectors)
+    mate_weight = swap(out_weight, 1)
+
+    mate = swap(narrow, 1)
+    onward = wide + mate.astype(F32)
+    earlier = []
+    for plane in range(3):
+        pairs = [(2 * plane + i, 2 * plane + 2 + i) for i in range(2)]
+        earlier.append(lax.ppermute(onward.astype(BF16), "seq", pairs))
+        onward += earlier[-1].astype(F32)
+    attended = attend(y, queries, within, norm_gain, mate, *earlier)
+
+    straight = move(attended, lambda z, y, x, c: (z ^ (2 + x), y, x, c))
+    beside = swap(attended, 2)
+    onward = swap(straight, 2)
+
+    tile = jax.ShapeDtypeStruct((2, rows, half_cols), BF16)
+    flops, moved = 4 * size * half_cols, 8 * size
+    vmem = pl.BlockSpec(memory_space=pltpu.VMEM)
+
+    def projected(light, heavy):
+        keep, send = pl.pallas_call(
+            project_pair_kernel,
+            out_shape=(tile, tile),
+            in_specs=[pl.BlockSpec(memory_space=pltpu.SMEM)] + [vmem] * 4,
+            out_specs=(vmem, vmem),
+            compiler_params=pltpu.CompilerParams(vmem_limit_bytes=24 * 1024 * 1024),
+            cost_estimate=pl.CostEstimate(
+                flops=2 * flops, bytes_accessed=2 * moved, transcendentals=0
+            ),
+        )(core.astype(jnp.int32)[None], light, heavy, out_weight, mate_weight)
+        return keep.astype(F32) + move(send, lambda z, y, x, c: (z, y, x, 1 - c)).astype(F32)
+
+    far = projected(jnp.where(x == 0, beside, attended), straight).astype(BF16)
+    crossed = move(far, lambda z, y, x, c: (z, y, 1 - x, c))
+    near = projected(jnp.where(x == 0, attended, beside), onward) + crossed.astype(F32)
+    result = move(near.astype(BF16), lambda z, y, x, c: (z ^ 3 * c ^ x, y, z // 2, z % 2))
+    first = jnp.where(y == 0, result[0], result[1])
+    return jnp.concatenate([first, jnp.where(y == 0, result[1], result[0])], axis=1)
+
+
 def solution(mesh):
     seq_count, head_groups = mesh.shape["seq"], mesh.shape["head"]
 
     def run(queries, key_vectors, value_vectors, norm_gain, out_weight):
         one_block = queries.shape[0] == BLOCK * seq_count
         body = general_body
-        if one_block and head_groups == 4 and seq_count % head_groups == 0:
+        if one_block and head_groups == 4 and seq_count == 8:
+            body = pairs_body
+        elif one_block and head_groups == 4 and seq_count % head_groups == 0:
             body = planes_body(seq_count, head_groups)
         return jax.shard_map(
             body,

time: 109 us -> 97.9 us (0.90)
  the two profiles are of different devices: /device:TPU:2 before, /device:TPU:1 now
where the time goes in v12:
time: 97.9 us; the launch traced here: 97.6 us
  waiting for transfers between devices  48.3 us (49%)
  starting transfers between devices  37.7 us (39%)
  Pallas kernels  7.7 us (8%)
  local copies, waits for them, and re-layouts  2.1 us (2%)
  other arithmetic  1.6 us (2%)
    ppermute x4, waiting for transfers between devices, swap(): return lax.ppermute(value, 'seq', [(s, s ^ mask) for s in range(8)])  28.2 us
    ppermute x5, starting transfers between devices, move(): return lax.ppermute(value, both, pairs)  23.5 us
    ppermute x5, waiting for transfers between devices, move(): return lax.ppermute(value, both, pairs)  16.1 us
    ppermute x4, starting transfers between devices, swap(): return lax.ppermute(value, 'seq', [(s, s ^ mask) for s in range(8)])  9.66 us
    pallas_call x2, Pallas kernels, projected(): pl.pallas_call(project_pair_kernel, out_shape=(tile, tile), in_specs=[pl....  5.65 us
    ppermute x3, starting transfers between devices, pairs_body(): earlier.append(lax.ppermute(onward.astype(BF16), 'seq', pairs))  4.6 us
    ppermute x3, waiting for transfers between devices, pairs_body(): earlier.append(lax.ppermute(onward.astype(BF16), 'seq', pairs))  4.02 us
    unnamed x12, local copies, waits for them, and re-layouts  2.1 us
  transfers between devices with their start and end apart: 12, of which 8 were waited for; matrix products, arithmetic and copies ran while one was open for 0% of the time, Pallas kernels for 5%

profile of v12, /device:TPU:1, one launch (start us, length us, event | category | flops | bytes accessed | tf_op | source)
XLA Modules:
  0.0 97.6 jit_solution(8390661505661957081)
XLA Ops:
  0.0 0.0 copy-start
  0.0 1.0 %copy-done = bf16[256,1024]{1,0:T(8,128)(2,1)S(1)} copy-done((bf16[256,1024]{1,0:T(8,128)(2,1)S(1)}, bf16[256,1024]{1,0:T(8,128)(2,1)}, u32[]{:S(2)}) %copy-start) | copy-done | bytes 524312
  1.0 0.0 copy-start.2
  1.0 1.0 %copy-done.2 = bf16[256,1024]{1,0:T(8,128)(2,1)S(1)} copy-done((bf16[256,1024]{1,0:T(8,128)(2,1)S(1)}, bf16[256,1024]{1,0:T(8,128)(2,1)}, u32[]{:S(2)}) %copy-start.2) | copy-done | bytes 524312
  2.1 0.4 shard_map.56
  2.4 2.1 %collective-permute-start = (bf16[8,128,128]{2,1,0:T(8,128)(2,1)S(1)}, bf16[8,128,128]{2,1,0:T(8,128)(2,1)S(1)}, u32[]{:S(2)}, u32[]{:S(2)}) collective-permute-start(bf16[8,128,128]{2,1,0:T(8,128)(2,1)S(1)} %get-tuple-element.11), channel_id=1, source_target_pairs={{0,4},{4,0},{8,12},{12,8},{16,20},{20,16},{24,28},{28,24},{1,5},{5... | collective-permute-start | bytes 786440 | tf_op jit(solution)/shard_map/ppermute | solution.py:238
  4.6 6.0 %collective-permute-done.mate_ref = bf16[8,128,128]{2,1,0:T(8,128)(2,1)S(1)} collective-permute-done((bf16[8,128,128]{2,1,0:T(8,128)(2,1)S(1)}, bf16[8,128,128]{2,1,0:T(8,128)(2,1)S(1)}, u32[]{:S(2)}, u32[]{:S(2)}) %collective-permute-start) | collective-permute-done | bytes 262176 | tf_op jit(solution)/shard_map/ppermute | solution.py:238
  10.6 0.1 fusion
  10.7 3.1 %collective-permute-start.1 = (bf16[8,128,128]{2,1,0:T(8,128)(2,1)S(1)}, bf16[8,128,128]{2,1,0:T(8,128)(2,1)S(1)}, u32[]{:S(2)}, u32[]{:S(2)}) collective-permute-start(bf16[8,128,128]{2,1,0:T(8,128)(2,1)S(1)} %fusion), channel_id=1, source_target_pairs={{0,8},{4,12},{1,9},{5,13},{2,10},{6,14},{3,11},{7,15}} | collective-permute-start | bytes 786440 | tf_op jit(solution)/shard_map/ppermute | solution.py:263
  13.8 4.0 %collective-permute-done.1.refs_0_ = bf16[8,128,128]{2,1,0:T(8,128)(2,1)S(1)} collective-permute-done((bf16[8,128,128]{2,1,0:T(8,128)(2,1)S(1)}, bf16[8,128,128]{2,1,0:T(8,128)(2,1)S(1)}, u32[]{:S(2)}, u32[]{:S(2)}) %collective-permute-start.1) | collective-permute-done | bytes 262176 | tf_op jit(solution)/shard_map/ppermute | solution.py:263
  17.8 0.1 fusion.1
  17.9 0.0 copy-start.1
  17.9 0.0 copy-start.3
  17.9 0.0 copy-start.4
  17.9 0.8 collective-permute-start.2
  18.8 0.0 collective-permute-done.2.refs_1_
  18.8 0.1 add_convert_fusion.2
  18.9 0.7 collective-permute-start.3
  19.6 1.3 %collective-permute-start.7 = (bf16[1024,512]{1,0:T(8,128)(2,1)}, bf16[1024,512]{1,0:T(8,128)(2,1)}, u32[]{:S(2)}, u32[]{:S(2)}) collective-permute-start(bf16[1024,512]{1,0:T(8,128)(2,1)} %own_ref.3), channel_id=1, source_target_pairs={{0,4},{4,0},{8,12},{12,8},{16,20},{20,16},{24,28},{28,24},{1,5},{5... | collective-permute-start | bytes 3145736 | tf_op jit(solution)/shard_map/ppermute | solution.py:238
  20.9 0.0 copy-done.1
  20.9 0.0 copy-done.3
  20.9 0.0 copy-done.4
  20.9 0.0 copy-start.5
  20.9 0.9 shard_map.55.within_ref
  21.8 0.0 collective-permute-done.3.refs_2_
  21.9 0.0 copy-done.5
  21.9 0.8 shard_map.57
  22.6 6.2 %collective-permute-start.4 = (bf16[256,1024]{1,0:T(8,128)(2,1)S(1)}, bf16[256,1024]{1,0:T(8,128)(2,1)S(1)}, u32[]{:S(2)}, u32[]{:S(2)}) collective-permute-start(bf16[256,1024]{1,0:T(8,128)(2,1)S(1)} %shard_map.57), channel_id=1, source_target_pairs={{0,8},{4,12},{8,0},{12,4},{16,24},{20,28},{24,16},{28,20},{1,9},{5... | collective-permute-start | bytes 1572872 | tf_op jit(solution)/shard_map/ppermute | solution.py:238
  28.8 6.0 %collective-permute-start.5 = (bf16[256,1024]{1,0:T(8,128)(2,1)S(1)}, bf16[256,1024]{1,0:T(8,128)(2,1)S(1)}, u32[]{:S(2)}, u32[]{:S(2)}) collective-permute-start(bf16[256,1024]{1,0:T(8,128)(2,1)S(1)} %shard_map.57), channel_id=1, source_target_pairs={{0,16},{1,17},{2,26},{3,27},{4,20},{5,21},{6,30},{7,31},{8,24},{9,... | collective-permute-start | bytes 1572872 | tf_op jit(solution)/shard_map/ppermute | solution.py:242
  34.8 11.4 %collective-permute-done.4 = bf16[256,1024]{1,0:T(8,128)(2,1)S(1)} collective-permute-done((bf16[256,1024]{1,0:T(8,128)(2,1)S(1)}, bf16[256,1024]{1,0:T(8,128)(2,1)S(1)}, u32[]{:S(2)}, u32[]{:S(2)}) %collective-permute-start.4) | collective-permute-done | bytes 524320 | tf_op jit(solution)/shard_map/ppermute | solution.py:238
  46.1 0.1 broadcast_select_fusion.1
  46.2 0.0 collective-permute-done.7.mate_ref
  46.2 1.6 %collective-permute-done.5.heavy_ref = bf16[256,1024]{1,0:T(8,128)(2,1)S(1)} collective-permute-done((bf16[256,1024]{1,0:T(8,128)(2,1)S(1)}, bf16[256,1024]{1,0:T(8,128)(2,1)S(1)}, u32[]{:S(2)}, u32[]{:S(2)}) %collective-permute-start.5) | collective-permute-done | bytes 524320 | tf_op jit(solution)/shard_map/ppermute | solution.py:242
  47.8 2.8 %shard_map.59 = (bf16[2,256,512]{2,1,0:T(8,128)(2,1)S(1)}, bf16[2,256,512]{2,1,0:T(8,128)(2,1)S(1)}) custom-call(s32[1]{0:T(128)} %bitcast.core_ref, bf16[256,1024]{1,0:T(8,128)(2,1)S(1)} %get-tuple-element.18.light_ref, bf16[256,1024]{1,0:T(8,128)(2,1)S(1)} %collective-permute-done.5.heavy_ref, bf16[1024,512]{1,0:T(8,128)(2,1)} %own_ref.3, ...), custom_call_target="tpu_custom_call" | custom-call | flops 1073741824 | bytes 4194304 | tf_op jit(solution)/shard_map/pallas_call | solution.py:276
  50.6 11.2 %collective-permute-start.9 = (bf16[2,256,512]{2,1,0:T(8,128)(2,1)S(1)}, bf16[2,256,512]{2,1,0:T(8,128)(2,1)S(1)}, u32[]{:S(2)}, u32[]{:S(2)}) collective-permute-start(bf16[2,256,512]{2,1,0:T(8,128)(2,1)S(1)} %get-tuple-element.16), channel_id=1, source_target_pairs={{0,1},{1,0},{2,3},{3,2},{4,5},{5,4},{6,7},{7,6},{8,9},{9,8},{10,11... | collective-permute-start | bytes 1572872 | tf_op jit(solution)/shard_map/ppermute | solution.py:242
  61.8 0.1 collective-permute-start.6
  61.9 1.5 %collective-permute-done.9 = bf16[2,256,512]{2,1,0:T(8,128)(2,1)S(1)} collective-permute-done((bf16[2,256,512]{2,1,0:T(8,128)(2,1)S(1)}, bf16[2,256,512]{2,1,0:T(8,128)(2,1)S(1)}, u32[]{:S(2)}, u32[]{:S(2)}) %collective-permute-start.9) | collective-permute-done | bytes 524320 | tf_op jit(solution)/shard_map/ppermute | solution.py:242
  63.3 0.1 add_convert_fusion.1
  63.5 1.1 %collective-permute-start.10 = (bf16[2,256,512]{2,1,0:T(8,128)(2,1)S(1)}, bf16[2,256,512]{2,1,0:T(8,128)(2,1)S(1)}, u32[]{:S(2)}, u32[]{:S(2)}) collective-permute-start(bf16[2,256,512]{2,1,0:T(8,128)(2,1)S(1)} %add_convert_fusion.1), channel_id=1, source_target_pairs={{0,2},{1,3},{2,0},{3,1},{4,6},{5,7},{6,4},{7,5},{8,10},{9,11},{10,... | collective-permute-start | bytes 1572872 | tf_op jit(solution)/shard_map/ppermute | solution.py:242
  64.5 10.8 %collective-permute-done.6.heavy_ref = bf16[256,1024]{1,0:T(8,128)(2,1)S(1)} collective-permute-done((bf16[256,1024]{1,0:T(8,128)(2,1)S(1)}, bf16[256,1024]{1,0:T(8,128)(2,1)S(1)}, u32[]{:S(2)}, u32[]{:S(2)}) %collective-permute-start.6) | collective-permute-done | bytes 524320 | tf_op jit(solution)/shard_map/ppermute | solution.py:238
  75.3 2.8 %shard_map.58 = (bf16[2,256,512]{2,1,0:T(8,128)(2,1)S(1)}, bf16[2,256,512]{2,1,0:T(8,128)(2,1)S(1)}) custom-call(s32[1]{0:T(128)} %bitcast.core_ref, bf16[256,1024]{1,0:T(8,128)(2,1)S(1)} %get-tuple-element.17.light_ref, bf16[256,1024]{1,0:T(8,128)(2,1)S(1)} %collective-permute-done.6.heavy_ref, bf16[1024,512]{1,0:T(8,128)(2,1)} %own_ref.3, ...), custom_call_target="tpu_custom_call" | custom-call | flops 1073741824 | bytes 4194304 | tf_op jit(solution)/shard_map/pallas_call | solution.py:276
  78.2 0.9 collective-permute-start.8
  79.1 0.0 collective-permute-done.10
  79.1 1.5 %collective-permute-done.8 = bf16[2,256,512]{2,1,0:T(8,128)(2,1)S(1)} collective-permute-done((bf16[2,256,512]{2,1,0:T(8,128)(2,1)S(1)}, bf16[2,256,512]{2,1,0:T(8,128)(2,1)S(1)}, u32[]{:S(2)}, u32[]{:S(2)}) %collective-permute-start.8) | collective-permute-done | bytes 524320 | tf_op jit(solution)/shard_map/ppermute | solution.py:242
  80.6 0.2 add_convert_fusion
  80.8 4.3 %collective-permute-start.11 = (bf16[2,256,512]{2,1,0:T(8,128)(2,1)S(1)}, bf16[2,256,512]{2,1,0:T(8,128)(2,1)S(1)}, u32[]{:S(2)}, u32[]{:S(2)}) collective-permute-start(bf16[2,256,512]{2,1,0:T(8,128)(2,1)S(1)} %add_convert_fusion), channel_id=1, source_target_pairs={{0,0},{1,24},{2,8},{3,16},{4,4},{5,28},{6,12},{7,20},{8,9},{9,17},... | collective-permute-start | bytes 1572872 | tf_op jit(solution)/shard_map/ppermute | solution.py:242
  85.2 11.5 %collective-permute-done.11 = bf16[2,256,512]{2,1,0:T(8,128)(2,1)S(1)} collective-permute-done((bf16[2,256,512]{2,1,0:T(8,128)(2,1)S(1)}, bf16[2,256,512]{2,1,0:T(8,128)(2,1)S(1)}, u32[]{:S(2)}, u32[]{:S(2)}) %collective-permute-start.11) | collective-permute-done | bytes 524320 | tf_op jit(solution)/shard_map/ppermute | solution.py:242
  96.7 0.9 pad_maximum_fusion
  (1 shorter events, 0.0 us)
Async XLA Ops:
  0.0 1.0 %copy-start = (bf16[256,1024]{1,0:T(8,128)(2,1)S(1)}, bf16[256,1024]{1,0:T(8,128)(2,1)}, u32[]{:S(2)}) copy-start(bf16[256,1024]{1,0:T(8,128)(2,1)} %k_ref.3) | copy-start | bytes 1572868
  1.0 1.0 %copy-start.2 = (bf16[256,1024]{1,0:T(8,128)(2,1)S(1)}, bf16[256,1024]{1,0:T(8,128)(2,1)}, u32[]{:S(2)}) copy-start(bf16[256,1024]{1,0:T(8,128)(2,1)} %v_ref.3) | copy-start | bytes 1572868
  2.4 8.2 %collective-permute-start = (bf16[8,128,128]{2,1,0:T(8,128)(2,1)S(1)}, bf16[8,128,128]{2,1,0:T(8,128)(2,1)S(1)}, u32[]{:S(2)}, u32[]{:S(2)}) collective-permute-start(bf16[8,128,128]{2,1,0:T(8,128)(2,1)S(1)} %get-tuple-element.11), channel_id=1, source_target_pairs={{0,4},{4,0},{8,12},{12,8},{16,20},{20,16},{24,28},{28,24},{1,5},{5... | collective-permute-start | bytes 786440 | tf_op jit(solution)/shard_map/ppermute | solution.py:238
  10.7 7.1 %collective-permute-start.1 = (bf16[8,128,128]{2,1,0:T(8,128)(2,1)S(1)}, bf16[8,128,128]{2,1,0:T(8,128)(2,1)S(1)}, u32[]{:S(2)}, u32[]{:S(2)}) collective-permute-start(bf16[8,128,128]{2,1,0:T(8,128)(2,1)S(1)} %fusion), channel_id=1, source_target_pairs={{0,8},{4,12},{1,9},{5,13},{2,10},{6,14},{3,11},{7,15}} | collective-permute-start | bytes 786440 | tf_op jit(solution)/shard_map/ppermute | solution.py:263
  17.9 3.0 %copy-start.1 = (bf16[256,1024]{1,0:T(8,128)(2,1)S(1)}, bf16[256,1024]{1,0:T(8,128)(2,1)}, u32[]{:S(2)}) copy-start(bf16[256,1024]{1,0:T(8,128)(2,1)} %k_ref.3) | copy-start | bytes 1572868
  17.9 3.0 %copy-start.3 = (bf16[256,1024]{1,0:T(8,128)(2,1)S(1)}, bf16[256,1024]{1,0:T(8,128)(2,1)}, u32[]{:S(2)}) copy-start(bf16[256,1024]{1,0:T(8,128)(2,1)} %v_ref.3) | copy-start | bytes 1572868
  17.9 3.0 %copy-start.4 = (bf16[256,1024]{1,0:T(8,128)(2,1)S(1)}, bf16[256,1024]{1,0:T(8,128)(2,1)}, u32[]{:S(2)}) copy-start(bf16[256,1024]{1,0:T(8,128)(2,1)} %q_ref.3) | copy-start | bytes 1572868
  17.9 0.8 collective-permute-start.2
  18.9 2.9 %collective-permute-start.3 = (bf16[8,128,128]{2,1,0:T(8,128)(2,1)S(1)}, bf16[8,128,128]{2,1,0:T(8,128)(2,1)S(1)}, u32[]{:S(2)}, u32[]{:S(2)}) collective-permute-start(bf16[8,128,128]{2,1,0:T(8,128)(2,1)S(1)} %add_convert_fusion.2), channel_id=1, source_target_pairs={{16,24},{20,28},{17,25},{21,29},{18,26},{22,30},{19,27},{23,31}} | collective-permute-start | bytes 786440 | tf_op jit(solution)/shard_map/ppermute | solution.py:263
  19.6 26.6 %collective-permute-start.7 = (bf16[1024,512]{1,0:T(8,128)(2,1)}, bf16[1024,512]{1,0:T(8,128)(2,1)}, u32[]{:S(2)}, u32[]{:S(2)}) collective-permute-start(bf16[1024,512]{1,0:T(8,128)(2,1)} %own_ref.3), channel_id=1, source_target_pairs={{0,4},{4,0},{8,12},{12,8},{16,20},{20,16},{24,28},{28,24},{1,5},{5... | collective-permute-start | bytes 3145736 | tf_op jit(solution)/shard_map/ppermute | solution.py:238
  20.9 1.0 copy-start.5
  22.6 23.5 %collective-permute-start.4 = (bf16[256,1024]{1,0:T(8,128)(2,1)S(1)}, bf16[256,1024]{1,0:T(8,128)(2,1)S(1)}, u32[]{:S(2)}, u32[]{:S(2)}) collective-permute-start(bf16[256,1024]{1,0:T(8,128)(2,1)S(1)} %shard_map.57), channel_id=1, source_target_pairs={{0,8},{4,12},{8,0},{12,4},{16,24},{20,28},{24,16},{28,20},{1,9},{5... | collective-permute-start | bytes 1572872 | tf_op jit(solution)/shard_map/ppermute | solution.py:238
  28.8 19.0 %collective-permute-start.5 = (bf16[256,1024]{1,0:T(8,128)(2,1)S(1)}, bf16[256,1024]{1,0:T(8,128)(2,1)S(1)}, u32[]{:S(2)}, u32[]{:S(2)}) collective-permute-start(bf16[256,1024]{1,0:T(8,128)(2,1)S(1)} %shard_map.57), channel_id=1, source_target_pairs={{0,16},{1,17},{2,26},{3,27},{4,20},{5,21},{6,30},{7,31},{8,24},{9,... | collective-permute-start | bytes 1572872 | tf_op jit(solution)/shard_map/ppermute | solution.py:242
  50.6 12.7 %collective-permute-start.9 = (bf16[2,256,512]{2,1,0:T(8,128)(2,1)S(1)}, bf16[2,256,512]{2,1,0:T(8,128)(2,1)S(1)}, u32[]{:S(2)}, u32[]{:S(2)}) collective-permute-start(bf16[2,256,512]{2,1,0:T(8,128)(2,1)S(1)} %get-tuple-element.16), channel_id=1, source_target_pairs={{0,1},{1,0},{2,3},{3,2},{4,5},{5,4},{6,7},{7,6},{8,9},{9,8},{10,11... | collective-permute-start | bytes 1572872 | tf_op jit(solution)/shard_map/ppermute | solution.py:242
  61.8 13.5 %collective-permute-start.6 = (bf16[256,1024]{1,0:T(8,128)(2,1)S(1)}, bf16[256,1024]{1,0:T(8,128)(2,1)S(1)}, u32[]{:S(2)}, u32[]{:S(2)}) collective-permute-start(bf16[256,1024]{1,0:T(8,128)(2,1)S(1)} %collective-permute-done.5.heavy_ref), channel_id=1, source_target_pairs={{0,8},{4,12},{8,0},{12,4},{16,24},{20,28},{24,16},{28,20},{1,9},{5... | collective-permute-start | bytes 1572872 | tf_op jit(solution)/shard_map/ppermute | solution.py:238
  63.5 15.6 %collective-permute-start.10 = (bf16[2,256,512]{2,1,0:T(8,128)(2,1)S(1)}, bf16[2,256,512]{2,1,0:T(8,128)(2,1)S(1)}, u32[]{:S(2)}, u32[]{:S(2)}) collective-permute-start(bf16[2,256,512]{2,1,0:T(8,128)(2,1)S(1)} %add_convert_fusion.1), channel_id=1, source_target_pairs={{0,2},{1,3},{2,0},{3,1},{4,6},{5,7},{6,4},{7,5},{8,10},{9,11},{10,... | collective-permute-start | bytes 1572872 | tf_op jit(solution)/shard_map/ppermute | solution.py:242
  78.2 2.5 %collective-permute-start.8 = (bf16[2,256,512]{2,1,0:T(8,128)(2,1)S(1)}, bf16[2,256,512]{2,1,0:T(8,128)(2,1)S(1)}, u32[]{:S(2)}, u32[]{:S(2)}) collective-permute-start(bf16[2,256,512]{2,1,0:T(8,128)(2,1)S(1)} %get-tuple-element.14), channel_id=1, source_target_pairs={{0,1},{1,0},{2,3},{3,2},{4,5},{5,4},{6,7},{7,6},{8,9},{9,8},{10,11... | collective-permute-start | bytes 1572872 | tf_op jit(solution)/shard_map/ppermute | solution.py:242
  80.8 15.9 %collective-permute-start.11 = (bf16[2,256,512]{2,1,0:T(8,128)(2,1)S(1)}, bf16[2,256,512]{2,1,0:T(8,128)(2,1)S(1)}, u32[]{:S(2)}, u32[]{:S(2)}) collective-permute-start(bf16[2,256,512]{2,1,0:T(8,128)(2,1)S(1)} %add_convert_fusion), channel_id=1, source_target_pairs={{0,0},{1,24},{2,8},{3,16},{4,4},{5,28},{6,12},{7,20},{8,9},{9,17},... | collective-permute-start | bytes 1572872 | tf_op jit(solution)/shard_map/ppermute | solution.py:242

commit v13 on v12

--- a/solution.py
+++ b/solution.py
@@ -1,3 +1,5 @@
+import functools
+
 import jax
 import jax.numpy as jnp
 from jax import lax
@@ -51,14 +53,47 @@
     return slice(head * HD, (head + 1) * HD)
 
 
-def state_kernel(k_ref, v_ref, wide_ref, narrow_ref):
-    for head in range(wide_ref.shape[0]):
-        cols = head_slice(head)
-        state = lax.dot_general(
-            k_ref[:, cols], v_ref[:, cols], (((0,), (0,)), ((), ())), preferred_element_type=F32
-        )
-        wide_ref[head] = state
-        narrow_ref[head] = state.astype(BF16)
+def state_kernel(k_hbm, v_hbm, wide_ref, narrow_ref, k_ref, v_ref, done):
+    width = k_ref.shape[1] // done.shape[0]
+
+    def copies(group):
+        cols = slice(group * width, (group + 1) * width)
+        return [
+            pltpu.make_async_copy(hbm.at[:, cols], ref.at[:, cols], done.at[group, index])
+            for index, (hbm, ref) in enumerate(((k_hbm, k_ref), (v_hbm, v_ref)))
+        ]
+
+    for group in range(done.shape[0]):
+        for copy in copies(group):
+            copy.start()
+    for group in range(done.shape[0]):
+        for copy in copies(group):
+            copy.wait()
+        for head in range(group * width // HD, (group + 1) * width // HD):
+            cols = head_slice(head)
+            state = lax.dot_general(
+                k_ref[:, cols], v_ref[:, cols], (((0,), (0,)), ((), ())), preferred_element_type=F32
+            )
+            wide_ref[head] = state
+            narrow_ref[head] = state.astype(BF16)
+
+
+def block_states(keys, values):
+    rows, features = keys.shape
+    heads, groups = features // HD, 4
+    hbm, vmem = (pl.BlockSpec(memory_space=space) for space in (pltpu.HBM, pltpu.VMEM))
+    held = pltpu.VMEM((rows, features), BF16)
+    return pl.pallas_call(
+        state_kernel,
+        out_shape=[jax.ShapeDtypeStruct((heads, HD, HD), kind) for kind in (F32, BF16)],
+        in_specs=[hbm, hbm],
+        out_specs=[vmem, vmem],
+        scratch_shapes=[held, held, pltpu.SemaphoreType.DMA((groups, 2))],
+        compiler_params=pltpu.CompilerParams(vmem_limit_bytes=56 * 1024 * 1024),
+        cost_estimate=pl.CostEstimate(
+            flops=2 * rows * features * HD, bytes_accessed=4 * rows * features, transcendentals=0
+        ),
+    )(keys, values)
 
 
 def within_kernel(q_ref, k_ref, v_ref, out_ref):
@@ -161,15 +196,7 @@
         heads = features // HD
         size = rows * features
         weight = gather_weight(out_weight)
-        wide, narrow = call(
-            state_kernel,
-            (
-                jax.ShapeDtypeStruct((heads, HD, HD), F32),
-                jax.ShapeDtypeStruct((heads, HD, HD), BF16),
-            ),
-            2 * size * HD,
-            4 * size + 6 * heads * HD * HD,
-        )(key_vectors, value_vectors)
+        wide, narrow = block_states(key_vectors, value_vectors)
         within = call(
             within_kernel, jax.ShapeDtypeStruct((rows, features), F32), 4 * size * BLOCK, 10 * size
         )(queries, key_vectors, value_vectors)
@@ -206,19 +233,24 @@
         out_ref[half] = product.astype(BF16)
 
 
-def project_pair_kernel(core_ref, light_ref, heavy_ref, own_ref, mate_ref, keep_ref, send_ref):
-    def multiply(out_ref, tokens_ref):
-        project_kernel(tokens_ref, own_ref, mate_ref, out_ref)
-
+def project_light_kernel(chip_ref, own_ref, beside_ref, weight_ref, mate_ref, out_ref):
+    chip = chip_ref[0]
+    project_kernel(own_ref, weight_ref, mate_ref, out_ref.at[1 - chip])
+    project_kernel(beside_ref, weight_ref, mate_ref, out_ref.at[chip])
+
+
+def project_heavy_kernel(
+    which, core_ref, light_ref, heavy_ref, own_ref, mate_ref, keep_ref, send_ref
+):
     @pl.when(core_ref[0] == 0)
     def _():
-        multiply(send_ref, heavy_ref)
-        multiply(keep_ref, light_ref)
+        project_kernel(heavy_ref, own_ref, mate_ref, send_ref)
+        keep_ref[...] = light_ref[which]
 
     @pl.when(core_ref[0] != 0)
     def _():
-        multiply(send_ref, light_ref)
-        multiply(keep_ref, heavy_ref)
+        project_kernel(heavy_ref, own_ref, mate_ref, keep_ref)
+        send_ref[...] = light_ref[which]
 
 
 def pairs_body(queries, key_vectors, value_vectors, norm_gain, out_weight):
@@ -241,53 +273,47 @@
         pairs = [(at(*d), at(*place_of(*d))) for d in devices if chosen(*d)]
         return lax.ppermute(value, both, pairs)
 
-    wide, narrow = call(
-        state_kernel,
-        (
-            jax.ShapeDtypeStruct((heads, HD, HD), F32),
-            jax.ShapeDtypeStruct((heads, HD, HD), BF16),
-        ),
-        2 * size * HD,
-        4 * size + 6 * heads * HD * HD,
-    )(key_vectors, value_vectors)
+    wide, narrow = block_states(key_vectors, value_vectors)
     within = call(
         within_kernel, jax.ShapeDtypeStruct((rows, features), F32), 4 * size * BLOCK, 10 * size
     )(queries, key_vectors, value_vectors)
-    mate_weight = swap(out_weight, 1)
-
     mate = swap(narrow, 1)
-    onward = wide + mate.astype(F32)
-    earlier = []
-    for plane in range(3):
+    earlier = [lax.ppermute(narrow, "seq", [(i, 2 + (i ^ flip)) for i in range(2)]) for flip in (0, 1)]
+    onward = wide + sum(state.astype(F32) for state in [mate] + earlier)
+    for plane in (1, 2):
         pairs = [(2 * plane + i, 2 * plane + 2 + i) for i in range(2)]
         earlier.append(lax.ppermute(onward.astype(BF16), "seq", pairs))
         onward += earlier[-1].astype(F32)
+    weight, _ = lax.optimization_barrier((out_weight, earlier[1]))
+    mate_weight = swap(weight, 1)
     attended = attend(y, queries, within, norm_gain, mate, *earlier)
 
     straight = move(attended, lambda z, y, x, c: (z ^ (2 + x), y, x, c))
     beside = swap(attended, 2)
     onward = swap(straight, 2)
 
-    tile = jax.ShapeDtypeStruct((2, rows, half_cols), BF16)
-    flops, moved = 4 * size * half_cols, 8 * size
-    vmem = pl.BlockSpec(memory_space=pltpu.VMEM)
-
-    def projected(light, heavy):
-        keep, send = pl.pallas_call(
-            project_pair_kernel,
-            out_shape=(tile, tile),
-            in_specs=[pl.BlockSpec(memory_space=pltpu.SMEM)] + [vmem] * 4,
-            out_specs=(vmem, vmem),
+    def project(kernel, tiles, scalar, *operands):
+        vmem = pl.BlockSpec(memory_space=pltpu.VMEM)
+        return pl.pallas_call(
+            kernel,
+            out_shape=[jax.ShapeDtypeStruct(shape + (rows, half_cols), BF16) for shape in tiles],
+            in_specs=[pl.BlockSpec(memory_space=pltpu.SMEM)] + [vmem] * (len(operands) + 2),
+            out_specs=[vmem] * len(tiles),
             compiler_params=pltpu.CompilerParams(vmem_limit_bytes=24 * 1024 * 1024),
             cost_estimate=pl.CostEstimate(
-                flops=2 * flops, bytes_accessed=2 * moved, transcendentals=0
+                flops=8 * size * half_cols, bytes_accessed=16 * size, transcendentals=0
             ),
-        )(core.astype(jnp.int32)[None], light, heavy, out_weight, mate_weight)
+        )(scalar.astype(jnp.int32)[None], *operands, out_weight, mate_weight)
+
+    def projected(which, heavy):
+        kernel = functools.partial(project_heavy_kernel, which)
+        keep, send = project(kernel, [(2,), (2,)], core, light, heavy)
         return keep.astype(F32) + move(send, lambda z, y, x, c: (z, y, x, 1 - c)).astype(F32)
 
-    far = projected(jnp.where(x == 0, beside, attended), straight).astype(BF16)
+    (light,) = project(project_light_kernel, [(2, 2)], x, attended, beside)
+    far = projected(0, straight).astype(BF16)
     crossed = move(far, lambda z, y, x, c: (z, y, 1 - x, c))
-    near = projected(jnp.where(x == 0, attended, beside), onward) + crossed.astype(F32)
+    near = projected(1, onward) + crossed.astype(F32)
     result = move(near.astype(BF16), lambda z, y, x, c: (z ^ 3 * c ^ x, y, z // 2, z % 2))
     first = jnp.where(y == 0, result[0], result[1])
     return jnp.concatenate([first, jnp.where(y == 0, result[1], result[0])], axis=1)

time: 97.9 us -> 103 us (1.052)
  Pallas kernels: 7.7 us -> 12 us
  local copies, waits for them, and re-layouts: 2.1 us -> 0.04 us
  other arithmetic: 1.6 us -> 3.35 us
  starting transfers between devices: 37.7 us -> 39.1 us
    ppermute x0 -> x2, waiting for transfers between devices: none -> 7.53 us  [pairs_body(): lax.ppermute(narrow, 'seq', [(i, 2 + (i ^ flip)) for i in range(2)])]
    ppermute x0 -> x2, starting transfers between devices: none -> 4.57 us  [pairs_body(): lax.ppermute(narrow, 'seq', [(i, 2 + (i ^ flip)) for i in range(2)])]
    ppermute x3 -> x2, waiting for transfers between devices: 4.02 us -> 0.01 us  [pairs_body(): earlier.append(lax.ppermute(onward.astype(BF16), 'seq', pairs))]
    pallas_call x3 -> x4, Pallas kernels: 6 us -> 9.36 us  [the longest x3 6.5 us: project(): pl.pallas_call(kernel, out_shape=[jax.ShapeDtypeStruct(shape + (rows, hal...]
    ppermute x4, waiting for transfers between devices: 28.2 us -> 24.8 us  [swap(): return lax.ppermute(value, 'seq', [(s, s ^ mask) for s in range(8)])]
    ppermute x3 -> x2, starting transfers between devices: 4.6 us -> 2.16 us  [pairs_body(): earlier.append(lax.ppermute(onward.astype(BF16), 'seq', pairs))]
    unnamed x12 -> x16, local copies, waits for them, and re-layouts: 2.1 us -> 0.04 us
    convert_element_type x3 -> x2, other arithmetic: 0.28 us -> 2.1 us  [pairs_body(): earlier.append(lax.ppermute(onward.astype(BF16), 'seq', pairs))]
  transfers between devices with their start and end apart: 12 -> 13, of which waited for: 8 -> 8; matrix products, arithmetic and copies ran while one was open for 0% -> 1% of each run, Pallas kernels for 5% -> 7%
where the time goes in v13:
time: 103 us
  waiting for transfers between devices  48 us (47%)
  starting transfers between devices  39.1 us (38%)
  Pallas kernels  12 us (12%)
  other arithmetic  3.35 us (3%)
    ppermute x4, waiting for transfers between devices, swap(): return lax.ppermute(value, 'seq', [(s, s ^ mask) for s in range(8)])  24.8 us
    ppermute x5, starting transfers between devices, move(): return lax.ppermute(value, both, pairs)  23.1 us
    ppermute x5, waiting for transfers between devices, move(): return lax.ppermute(value, both, pairs)  15.7 us
    ppermute x4, starting transfers between devices, swap(): return lax.ppermute(value, 'seq', [(s, s ^ mask) for s in range(8)])  9.33 us
    ppermute x2, waiting for transfers between devices, pairs_body(): lax.ppermute(narrow, 'seq', [(i, 2 + (i ^ flip)) for i in range(2)])  7.53 us
    pallas_call x3, Pallas kernels, project(): pl.pallas_call(kernel, out_shape=[jax.ShapeDtypeStruct(shape + (rows, hal...  6.5 us
    ppermute x2, starting transfers between devices, pairs_body(): lax.ppermute(narrow, 'seq', [(i, 2 + (i ^ flip)) for i in range(2)])  4.57 us
    pallas_call x1, Pallas kernels, block_states(): pl.pallas_call(state_kernel, out_shape=[jax.ShapeDtypeStruct((heads, HD,...  2.87 us
  transfers between devices with their start and end apart: 13, of which 8 were waited for; matrix products, arithmetic and copies ran while one was open for 1% of the time, Pallas kernels for 7%

profile of v13, /device:TPU:1, one launch (start us, length us, event | category | flops | bytes accessed | tf_op | source)
XLA Modules:
  0.0 102.8 jit_solution(3976253333206470881)
XLA Ops:
  0.0 2.9 %shard_map.56 = (f32[8,128,128]{2,1,0:T(8,128)}, bf16[8,128,128]{2,1,0:T(8,128)(2,1)}) custom-call(bf16[256,1024]{1,0:T(8,128)(2,1)} %k_hbm.1, bf16[256,1024]{1,0:T(8,128)(2,1)} %v_hbm.1), custom_call_target="tpu_custom_call" | custom-call | flops 67108864 | bytes 1048576 | tf_op jit(solution)/shard_map/pallas_call | solution.py:86
  2.9 0.0 copy-start.3
  2.9 2.1 %collective-permute-start = (bf16[8,128,128]{2,1,0:T(8,128)(2,1)}, bf16[8,128,128]{2,1,0:T(8,128)(2,1)S(1)}, u32[]{:S(2)}, u32[]{:S(2)}) collective-permute-start(bf16[8,128,128]{2,1,0:T(8,128)(2,1)} %get-tuple-element.12), channel_id=1, source_target_pairs={{0,4},{4,0},{8,12},{12,8},{16,20},{20,16},{24,28},{28,24},{1,5},{5... | collective-permute-start | bytes 786440 | tf_op jit(solution)/shard_map/ppermute | solution.py:270
  5.0 3.2 %collective-permute-start.1 = (bf16[8,128,128]{2,1,0:T(8,128)(2,1)}, bf16[8,128,128]{2,1,0:T(8,128)(2,1)S(1)}, u32[]{:S(2)}, u32[]{:S(2)}) collective-permute-start(bf16[8,128,128]{2,1,0:T(8,128)(2,1)} %get-tuple-element.12), channel_id=1, source_target_pairs={{0,8},{4,12},{1,9},{5,13},{2,10},{6,14},{3,11},{7,15}} | collective-permute-start | bytes 786440 | tf_op jit(solution)/shard_map/ppermute | solution.py:281
  8.2 1.4 %collective-permute-start.2 = (bf16[8,128,128]{2,1,0:T(8,128)(2,1)}, bf16[8,128,128]{2,1,0:T(8,128)(2,1)S(1)}, u32[]{:S(2)}, u32[]{:S(2)}) collective-permute-start(bf16[8,128,128]{2,1,0:T(8,128)(2,1)} %get-tuple-element.12), channel_id=1, source_target_pairs={{0,12},{4,8},{1,13},{5,9},{2,14},{6,10},{3,15},{7,11}} | collective-permute-start | bytes 786440 | tf_op jit(solution)/shard_map/ppermute | solution.py:281
  9.6 1.6 %collective-permute-done.mate_ref = bf16[8,128,128]{2,1,0:T(8,128)(2,1)S(1)} collective-permute-done((bf16[8,128,128]{2,1,0:T(8,128)(2,1)}, bf16[8,128,128]{2,1,0:T(8,128)(2,1)S(1)}, u32[]{:S(2)}, u32[]{:S(2)}) %collective-permute-start) | collective-permute-done | bytes 262176 | tf_op jit(solution)/shard_map/ppermute | solution.py:270
  11.3 1.9 %collective-permute-done.1.refs_0_ = bf16[8,128,128]{2,1,0:T(8,128)(2,1)S(1)} collective-permute-done((bf16[8,128,128]{2,1,0:T(8,128)(2,1)}, bf16[8,128,128]{2,1,0:T(8,128)(2,1)S(1)}, u32[]{:S(2)}, u32[]{:S(2)}) %collective-permute-start.1) | collective-permute-done | bytes 262176 | tf_op jit(solution)/shard_map/ppermute | solution.py:281
  13.2 5.6 %collective-permute-done.2.refs_1_ = bf16[8,128,128]{2,1,0:T(8,128)(2,1)S(1)} collective-permute-done((bf16[8,128,128]{2,1,0:T(8,128)(2,1)}, bf16[8,128,128]{2,1,0:T(8,128)(2,1)S(1)}, u32[]{:S(2)}, u32[]{:S(2)}) %collective-permute-start.2) | collective-permute-done | bytes 262176 | tf_op jit(solution)/shard_map/ppermute | solution.py:281
  18.8 0.0 copy-start.7
  18.8 1.2 %fusion = bf16[8,128,128]{2,1,0:T(8,128)(2,1)S(1)} fusion(f32[8,128,128]{2,1,0:T(8,128)} %get-tuple-element.13, bf16[8,128,128]{2,1,0:T(8,128)(2,1)S(1)} %collective-permute-done.2.refs_1_, bf16[8,128,128]{2,1,0:T(8,128)(2,1)S(1)} %collective-permute-done.1.refs_0_, bf16[8,128,128]{2,1,0:T(8,128)(2,1)S(1)} %collective-permute-done.mate_ref), kind=kLoop, calls=%fused_computation.7 | loop fusion | flops 917504 | bytes 1572864 | tf_op jit(solution)/shard_map/convert_element_type | solution.py:285
  20.0 0.0 copy-start
  20.0 0.0 copy-start.1
  20.0 0.0 copy-start.2
  20.1 0.8 collective-permute-start.3
  20.9 0.0 copy-done.3
  20.9 0.6 collective-permute-start.6
  21.5 0.0 collective-permute-done.3.refs_2_
  21.5 0.0 copy-done.7
  21.5 0.0 copy-start.4
  21.5 0.9 add_convert_fusion.2
  22.3 0.0 copy-done.4
  22.3 1.3 %collective-permute-start.4 = (bf16[8,128,128]{2,1,0:T(8,128)(2,1)}, bf16[8,128,128]{2,1,0:T(8,128)(2,1)}, u32[]{:S(2)}, u32[]{:S(2)}) collective-permute-start(bf16[8,128,128]{2,1,0:T(8,128)(2,1)} %add_convert_fusion.2), channel_id=1, source_target_pairs={{16,24},{20,28},{17,25},{21,29},{18,26},{22,30},{19,27},{23,31}} | collective-permute-start | bytes 786440 | tf_op jit(solution)/shard_map/ppermute | solution.py:285
  23.7 0.0 copy-done
  23.7 0.0 copy-done.1
  23.7 0.0 copy-done.2
  23.7 0.0 copy-start.5
  23.7 0.0 copy-start.6
  23.7 0.9 shard_map.55.within_ref
  24.7 0.0 collective-permute-done.4.refs_3_
  24.7 0.0 copy-done.5
  24.7 0.0 copy-done.6
  24.7 1.7 %shard_map.57.own_ref = bf16[256,1024]{1,0:T(8,128)(2,1)S(1)} custom-call(s32[1]{0:T(128)} %bitcast.2.second_ref, bf16[256,1024]{1,0:T(8,128)(2,1)S(1)} %copy-done.2, f32[256,1024]{1,0:T(8,128)S(1)} %shard_map.55.within_ref, f32[1,1024]{1,0:T(1,128)S(1)} %bitcast.8, bf16[8,128,128]{2,1,0:T(8,128)(2,1)S(1)} %collective-permute-done.mate_ref, ...), custom_call_target="tpu_custom_call" | custom-call | flops 67108864 | bytes 2097152 | tf_op jit(solution)/shard_map/pallas_call | solution.py:140
  26.4 6.6 %collective-permute-start.5 = (bf16[256,1024]{1,0:T(8,128)(2,1)S(1)}, bf16[256,1024]{1,0:T(8,128)(2,1)S(1)}, u32[]{:S(2)}, u32[]{:S(2)}) collective-permute-start(bf16[256,1024]{1,0:T(8,128)(2,1)S(1)} %shard_map.57.own_ref), channel_id=1, source_target_pairs={{0,8},{4,12},{8,0},{12,4},{16,24},{20,28},{24,16},{28,20},{1,9},{5... | collective-permute-start | bytes 1572872 | tf_op jit(solution)/shard_map/ppermute | solution.py:270
  33.0 7.1 %collective-permute-start.7 = (bf16[256,1024]{1,0:T(8,128)(2,1)S(1)}, bf16[256,1024]{1,0:T(8,128)(2,1)}, u32[]{:S(2)}, u32[]{:S(2)}) collective-permute-start(bf16[256,1024]{1,0:T(8,128)(2,1)S(1)} %shard_map.57.own_ref), channel_id=1, source_target_pairs={{0,16},{1,17},{2,26},{3,27},{4,20},{5,21},{6,30},{7,31},{8,24},{9,... | collective-permute-start | bytes 1572872 | tf_op jit(solution)/shard_map/ppermute | solution.py:274
  40.1 12.2 %collective-permute-done.5.beside_ref = bf16[256,1024]{1,0:T(8,128)(2,1)S(1)} collective-permute-done((bf16[256,1024]{1,0:T(8,128)(2,1)S(1)}, bf16[256,1024]{1,0:T(8,128)(2,1)S(1)}, u32[]{:S(2)}, u32[]{:S(2)}) %collective-permute-start.5) | collective-permute-done | bytes 524320 | tf_op jit(solution)/shard_map/ppermute | solution.py:270
  52.2 0.0 collective-permute-done.6.mate_ref
  52.2 2.5 %shard_map.58.light_ref = bf16[2,2,256,512]{3,2,1,0:T(8,128)(2,1)S(1)} custom-call(s32[1]{0:T(128)} %bitcast.1.chip_ref, bf16[256,1024]{1,0:T(8,128)(2,1)S(1)} %shard_map.57.own_ref, bf16[256,1024]{1,0:T(8,128)(2,1)S(1)} %collective-permute-done.5.beside_ref, bf16[1024,512]{1,0:T(8,128)(2,1)S(1)} %copy-done.3, bf16[1024,512]{1,0:T(8,128)(2,1)} %collective-permute-done.6.mate_ref), custom_call_target="tpu_custom_call" | custom-call | flops 1073741824 | bytes 4194304 | tf_op jit(solution)/shard_map/pallas_call | solution.py:297
  54.7 0.0 collective-permute-done.7.heavy_ref
  54.7 2.1 %shard_map.60 = (bf16[2,256,512]{2,1,0:T(8,128)(2,1)S(1)}, bf16[2,256,512]{2,1,0:T(8,128)(2,1)S(1)}) custom-call(s32[1]{0:T(128)} %bitcast.core_ref, bf16[2,2,256,512]{3,2,1,0:T(8,128)(2,1)S(1)} %shard_map.58.light_ref, bf16[256,1024]{1,0:T(8,128)(2,1)} %collective-permute-done.7.heavy_ref, bf16[1024,512]{1,0:T(8,128)(2,1)S(1)} %copy-done.3, ...), custom_call_target="tpu_custom_call" | custom-call | flops 1073741824 | bytes 4194304 | tf_op jit(solution)/shard_map/pallas_call | solution.py:297
  56.8 9.7 %collective-permute-start.10 = (bf16[2,256,512]{2,1,0:T(8,128)(2,1)S(1)}, bf16[2,256,512]{2,1,0:T(8,128)(2,1)S(1)}, u32[]{:S(2)}, u32[]{:S(2)}) collective-permute-start(bf16[2,256,512]{2,1,0:T(8,128)(2,1)S(1)} %get-tuple-element.18), channel_id=1, source_target_pairs={{0,1},{1,0},{2,3},{3,2},{4,5},{5,4},{6,7},{7,6},{8,9},{9,8},{10,11... | collective-permute-start | bytes 1572872 | tf_op jit(solution)/shard_map/ppermute | solution.py:274
  66.5 0.1 collective-permute-start.8
  66.6 1.5 %collective-permute-done.10 = bf16[2,256,512]{2,1,0:T(8,128)(2,1)S(1)} collective-permute-done((bf16[2,256,512]{2,1,0:T(8,128)(2,1)S(1)}, bf16[2,256,512]{2,1,0:T(8,128)(2,1)S(1)}, u32[]{:S(2)}, u32[]{:S(2)}) %collective-permute-start.10) | collective-permute-done | bytes 524320 | tf_op jit(solution)/shard_map/ppermute | solution.py:274
  68.0 0.1 add_convert_fusion.1
  68.2 1.0 %collective-permute-start.11 = (bf16[2,256,512]{2,1,0:T(8,128)(2,1)S(1)}, bf16[2,256,512]{2,1,0:T(8,128)(2,1)S(1)}, u32[]{:S(2)}, u32[]{:S(2)}) collective-permute-start(bf16[2,256,512]{2,1,0:T(8,128)(2,1)S(1)} %add_convert_fusion.1), channel_id=1, source_target_pairs={{0,2},{1,3},{2,0},{3,1},{4,6},{5,7},{6,4},{7,5},{8,10},{9,11},{10,... | collective-permute-start | bytes 1572872 | tf_op jit(solution)/shard_map/ppermute | solution.py:274
  69.2 11.0 %collective-permute-done.8.heavy_ref = bf16[256,1024]{1,0:T(8,128)(2,1)S(1)} collective-permute-done((bf16[256,1024]{1,0:T(8,128)(2,1)}, bf16[256,1024]{1,0:T(8,128)(2,1)S(1)}, u32[]{:S(2)}, u32[]{:S(2)}) %collective-permute-start.8) | collective-permute-done | bytes 524320 | tf_op jit(solution)/shard_map/ppermute | solution.py:270
  80.2 1.9 %shard_map.59 = (bf16[2,256,512]{2,1,0:T(8,128)(2,1)S(1)}, bf16[2,256,512]{2,1,0:T(8,128)(2,1)S(1)}) custom-call(s32[1]{0:T(128)} %bitcast.core_ref, bf16[2,2,256,512]{3,2,1,0:T(8,128)(2,1)S(1)} %shard_map.58.light_ref, bf16[256,1024]{1,0:T(8,128)(2,1)S(1)} %collective-permute-done.8.heavy_ref, bf16[1024,512]{1,0:T(8,128)(2,1)S(1)} %copy-done.3, ...), custom_call_target="tpu_custom_call" | custom-call | flops 1073741824 | bytes 4194304 | tf_op jit(solution)/shard_map/pallas_call | solution.py:297
  82.2 0.9 collective-permute-start.9
  83.1 0.0 collective-permute-done.11
  83.1 1.5 %collective-permute-done.9 = bf16[2,256,512]{2,1,0:T(8,128)(2,1)S(1)} collective-permute-done((bf16[2,256,512]{2,1,0:T(8,128)(2,1)S(1)}, bf16[2,256,512]{2,1,0:T(8,128)(2,1)S(1)}, u32[]{:S(2)}, u32[]{:S(2)}) %collective-permute-start.9) | collective-permute-done | bytes 524320 | tf_op jit(solution)/shard_map/ppermute | solution.py:274
  84.6 0.2 add_convert_fusion
  84.8 4.3 %collective-permute-start.12 = (bf16[2,256,512]{2,1,0:T(8,128)(2,1)S(1)}, bf16[2,256,512]{2,1,0:T(8,128)(2,1)S(1)}, u32[]{:S(2)}, u32[]{:S(2)}) collective-permute-start(bf16[2,256,512]{2,1,0:T(8,128)(2,1)S(1)} %add_convert_fusion), channel_id=1, source_target_pairs={{0,0},{1,24},{2,8},{3,16},{4,4},{5,28},{6,12},{7,20},{8,9},{9,17},... | collective-permute-start | bytes 1572872 | tf_op jit(solution)/shard_map/ppermute | solution.py:274
  89.2 12.7 %collective-permute-done.12 = bf16[2,256,512]{2,1,0:T(8,128)(2,1)S(1)} collective-permute-done((bf16[2,256,512]{2,1,0:T(8,128)(2,1)S(1)}, bf16[2,256,512]{2,1,0:T(8,128)(2,1)S(1)}, u32[]{:S(2)}, u32[]{:S(2)}) %collective-permute-start.12) | collective-permute-done | bytes 524320 | tf_op jit(solution)/shard_map/ppermute | solution.py:274
  101.9 0.9 pad_maximum_fusion
  (1 shorter events, 0.0 us)
Async XLA Ops:
  2.9 18.0 %copy-start.3 = (bf16[1024,512]{1,0:T(8,128)(2,1)S(1)}, bf16[1024,512]{1,0:T(8,128)(2,1)}, u32[]{:S(2)}) copy-start(bf16[1024,512]{1,0:T(8,128)(2,1)} %own_ref.3) | copy-start | bytes 3145732
  2.9 8.4 %collective-permute-start = (bf16[8,128,128]{2,1,0:T(8,128)(2,1)}, bf16[8,128,128]{2,1,0:T(8,128)(2,1)S(1)}, u32[]{:S(2)}, u32[]{:S(2)}) collective-permute-start(bf16[8,128,128]{2,1,0:T(8,128)(2,1)} %get-tuple-element.12), channel_id=1, source_target_pairs={{0,4},{4,0},{8,12},{12,8},{16,20},{20,16},{24,28},{28,24},{1,5},{5... | collective-permute-start | bytes 786440 | tf_op jit(solution)/shard_map/ppermute | solution.py:270
  5.0 8.1 %collective-permute-start.1 = (bf16[8,128,128]{2,1,0:T(8,128)(2,1)}, bf16[8,128,128]{2,1,0:T(8,128)(2,1)S(1)}, u32[]{:S(2)}, u32[]{:S(2)}) collective-permute-start(bf16[8,128,128]{2,1,0:T(8,128)(2,1)} %get-tuple-element.12), channel_id=1, source_target_pairs={{0,8},{4,12},{1,9},{5,13},{2,10},{6,14},{3,11},{7,15}} | collective-permute-start | bytes 786440 | tf_op jit(solution)/shard_map/ppermute | solution.py:281
  8.2 10.6 %collective-permute-start.2 = (bf16[8,128,128]{2,1,0:T(8,128)(2,1)}, bf16[8,128,128]{2,1,0:T(8,128)(2,1)S(1)}, u32[]{:S(2)}, u32[]{:S(2)}) collective-permute-start(bf16[8,128,128]{2,1,0:T(8,128)(2,1)} %get-tuple-element.12), channel_id=1, source_target_pairs={{0,12},{4,8},{1,13},{5,9},{2,14},{6,10},{3,15},{7,11}} | collective-permute-start | bytes 786440 | tf_op jit(solution)/shard_map/ppermute | solution.py:281
  18.8 2.7 %copy-start.7 = (f32[8,128,128]{2,1,0:T(8,128)S(1)}, f32[8,128,128]{2,1,0:T(8,128)}, u32[]{:S(2)}) copy-start(f32[8,128,128]{2,1,0:T(8,128)} %get-tuple-element.13) | copy-start | bytes 1572868
  20.0 3.7 %copy-start = (bf16[256,1024]{1,0:T(8,128)(2,1)S(1)}, bf16[256,1024]{1,0:T(8,128)(2,1)}, u32[]{:S(2)}) copy-start(bf16[256,1024]{1,0:T(8,128)(2,1)} %k_hbm.1) | copy-start | bytes 1572868
  20.0 3.7 %copy-start.1 = (bf16[256,1024]{1,0:T(8,128)(2,1)S(1)}, bf16[256,1024]{1,0:T(8,128)(2,1)}, u32[]{:S(2)}) copy-start(bf16[256,1024]{1,0:T(8,128)(2,1)} %v_hbm.1) | copy-start | bytes 1572868
  20.0 3.6 %copy-start.2 = (bf16[256,1024]{1,0:T(8,128)(2,1)S(1)}, bf16[256,1024]{1,0:T(8,128)(2,1)}, u32[]{:S(2)}) copy-start(bf16[256,1024]{1,0:T(8,128)(2,1)} %q_ref.3) | copy-start | bytes 1572868
  20.1 1.4 %collective-permute-start.3 = (bf16[8,128,128]{2,1,0:T(8,128)(2,1)S(1)}, bf16[8,128,128]{2,1,0:T(8,128)(2,1)S(1)}, u32[]{:S(2)}, u32[]{:S(2)}) collective-permute-start(bf16[8,128,128]{2,1,0:T(8,128)(2,1)S(1)} %fusion), channel_id=1, source_target_pairs={{8,16},{12,20},{9,17},{13,21},{10,18},{14,22},{11,19},{15,23}} | collective-permute-start | bytes 786440 | tf_op jit(solution)/shard_map/ppermute | solution.py:285
  20.9 31.3 %collective-permute-start.6 = (bf16[1024,512]{1,0:T(8,128)(2,1)S(1)}, bf16[1024,512]{1,0:T(8,128)(2,1)}, u32[]{:S(2)}, u32[]{:S(2)}) collective-permute-start(bf16[1024,512]{1,0:T(8,128)(2,1)S(1)} %copy-done.3), channel_id=1, source_target_pairs={{0,4},{4,0},{8,12},{12,8},{16,20},{20,16},{24,28},{28,24},{1,5},{5... | collective-permute-start | bytes 3145736 | tf_op jit(solution)/shard_map/ppermute | solution.py:270
  21.5 0.9 copy-start.4
  22.3 2.3 %collective-permute-start.4 = (bf16[8,128,128]{2,1,0:T(8,128)(2,1)}, bf16[8,128,128]{2,1,0:T(8,128)(2,1)}, u32[]{:S(2)}, u32[]{:S(2)}) collective-permute-start(bf16[8,128,128]{2,1,0:T(8,128)(2,1)} %add_convert_fusion.2), channel_id=1, source_target_pairs={{16,24},{20,28},{17,25},{21,29},{18,26},{22,30},{19,27},{23,31}} | collective-permute-start | bytes 786440 | tf_op jit(solution)/shard_map/ppermute | solution.py:285
  23.7 1.0 copy-start.5
  23.7 1.0 copy-start.6
  26.4 25.8 %collective-permute-start.5 = (bf16[256,1024]{1,0:T(8,128)(2,1)S(1)}, bf16[256,1024]{1,0:T(8,128)(2,1)S(1)}, u32[]{:S(2)}, u32[]{:S(2)}) collective-permute-start(bf16[256,1024]{1,0:T(8,128)(2,1)S(1)} %shard_map.57.own_ref), channel_id=1, source_target_pairs={{0,8},{4,12},{8,0},{12,4},{16,24},{20,28},{24,16},{28,20},{1,9},{5... | collective-permute-start | bytes 1572872 | tf_op jit(solution)/shard_map/ppermute | solution.py:270
  33.0 21.7 %collective-permute-start.7 = (bf16[256,1024]{1,0:T(8,128)(2,1)S(1)}, bf16[256,1024]{1,0:T(8,128)(2,1)}, u32[]{:S(2)}, u32[]{:S(2)}) collective-permute-start(bf16[256,1024]{1,0:T(8,128)(2,1)S(1)} %shard_map.57.own_ref), channel_id=1, source_target_pairs={{0,16},{1,17},{2,26},{3,27},{4,20},{5,21},{6,30},{7,31},{8,24},{9,... | collective-permute-start | bytes 1572872 | tf_op jit(solution)/shard_map/ppermute | solution.py:274
  56.8 11.2 %collective-permute-start.10 = (bf16[2,256,512]{2,1,0:T(8,128)(2,1)S(1)}, bf16[2,256,512]{2,1,0:T(8,128)(2,1)S(1)}, u32[]{:S(2)}, u32[]{:S(2)}) collective-permute-start(bf16[2,256,512]{2,1,0:T(8,128)(2,1)S(1)} %get-tuple-element.18), channel_id=1, source_target_pairs={{0,1},{1,0},{2,3},{3,2},{4,5},{5,4},{6,7},{7,6},{8,9},{9,8},{10,11... | collective-permute-start | bytes 1572872 | tf_op jit(solution)/shard_map/ppermute | solution.py:274
  66.5 13.7 %collective-permute-start.8 = (bf16[256,1024]{1,0:T(8,128)(2,1)}, bf16[256,1024]{1,0:T(8,128)(2,1)S(1)}, u32[]{:S(2)}, u32[]{:S(2)}) collective-permute-start(bf16[256,1024]{1,0:T(8,128)(2,1)} %collective-permute-done.7.heavy_ref), channel_id=1, source_target_pairs={{0,8},{4,12},{8,0},{12,4},{16,24},{20,28},{24,16},{28,20},{1,9},{5... | collective-permute-start | bytes 1572872 | tf_op jit(solution)/shard_map/ppermute | solution.py:270
  68.2 14.9 %collective-permute-start.11 = (bf16[2,256,512]{2,1,0:T(8,128)(2,1)S(1)}, bf16[2,256,512]{2,1,0:T(8,128)(2,1)S(1)}, u32[]{:S(2)}, u32[]{:S(2)}) collective-permute-start(bf16[2,256,512]{2,1,0:T(8,128)(2,1)S(1)} %add_convert_fusion.1), channel_id=1, source_target_pairs={{0,2},{1,3},{2,0},{3,1},{4,6},{5,7},{6,4},{7,5},{8,10},{9,11},{10,... | collective-permute-start | bytes 1572872 | tf_op jit(solution)/shard_map/ppermute | solution.py:274
  82.2 2.5 %collective-permute-start.9 = (bf16[2,256,512]{2,1,0:T(8,128)(2,1)S(1)}, bf16[2,256,512]{2,1,0:T(8,128)(2,1)S(1)}, u32[]{:S(2)}, u32[]{:S(2)}) collective-permute-start(bf16[2,256,512]{2,1,0:T(8,128)(2,1)S(1)} %get-tuple-element.16), channel_id=1, source_target_pairs={{0,1},{1,0},{2,3},{3,2},{4,5},{5,4},{6,7},{7,6},{8,9},{9,8},{10,11... | collective-permute-start | bytes 1572872 | tf_op jit(solution)/shard_map/ppermute | solution.py:274
  84.8 17.0 %collective-permute-start.12 = (bf16[2,256,512]{2,1,0:T(8,128)(2,1)S(1)}, bf16[2,256,512]{2,1,0:T(8,128)(2,1)S(1)}, u32[]{:S(2)}, u32[]{:S(2)}) collective-permute-start(bf16[2,256,512]{2,1,0:T(8,128)(2,1)S(1)} %add_convert_fusion), channel_id=1, source_target_pairs={{0,0},{1,24},{2,8},{3,16},{4,4},{5,28},{6,12},{7,20},{8,9},{9,17},... | collective-permute-start | bytes 1572872 | tf_op jit(solution)/shard_map/ppermute | solution.py:274

commit v14 on v12

--- a/solution.py
+++ b/solution.py
@@ -200,25 +200,19 @@
     return body
 
 
-def project_kernel(tokens_ref, own_ref, mate_ref, out_ref):
-    for half, weight_ref in enumerate((own_ref, mate_ref)):
-        product = jnp.dot(tokens_ref[...], weight_ref[...], preferred_element_type=F32)
-        out_ref[half] = product.astype(BF16)
-
-
-def project_pair_kernel(core_ref, light_ref, heavy_ref, own_ref, mate_ref, keep_ref, send_ref):
-    def multiply(out_ref, tokens_ref):
-        project_kernel(tokens_ref, own_ref, mate_ref, out_ref)
-
-    @pl.when(core_ref[0] == 0)
-    def _():
-        multiply(send_ref, heavy_ref)
-        multiply(keep_ref, light_ref)
-
-    @pl.when(core_ref[0] != 0)
-    def _():
-        multiply(send_ref, light_ref)
-        multiply(keep_ref, heavy_ref)
+def project_kernel(choice_ref, *refs):
+    *token_refs, own_ref, mate_ref, other_own_ref, other_mate_ref, out_ref = refs
+    weights = ((own_ref, other_own_ref), (mate_ref, other_mate_ref))
+    for choice in range(len(token_refs) // 2):
+
+        @pl.when(choice_ref[0] == choice)
+        def _():
+            for half, pair in enumerate(weights):
+                products = [
+                    jnp.dot(tokens[...], weight[...], preferred_element_type=F32)
+                    for tokens, weight in zip(token_refs[2 * choice : 2 * choice + 2], pair)
+                ]
+                out_ref[half] = (products[0] + products[1]).astype(BF16)
 
 
 def pairs_body(queries, key_vectors, value_vectors, norm_gain, out_weight):
@@ -253,7 +247,15 @@
     within = call(
         within_kernel, jax.ShapeDtypeStruct((rows, features), F32), 4 * size * BLOCK, 10 * size
     )(queries, key_vectors, value_vectors)
-    mate_weight = swap(out_weight, 1)
+    def to_other_core(value, chosen=lambda z, y, x, c: True):
+        return move(value, lambda z, y, x, c: (z, y, x, 1 - c), chosen)
+
+    weights = (
+        out_weight,
+        swap(out_weight, 1),
+        to_other_core(out_weight),
+        move(out_weight, lambda z, y, x, c: (z, 1 - y, x, 1 - c)),
+    )
 
     mate = swap(narrow, 1)
     onward = wide + mate.astype(F32)
@@ -264,30 +266,34 @@
         onward += earlier[-1].astype(F32)
     attended = attend(y, queries, within, norm_gain, mate, *earlier)
 
-    straight = move(attended, lambda z, y, x, c: (z ^ (2 + x), y, x, c))
-    beside = swap(attended, 2)
-    onward = swap(straight, 2)
-
-    tile = jax.ShapeDtypeStruct((2, rows, half_cols), BF16)
-    flops, moved = 4 * size * half_cols, 8 * size
-    vmem = pl.BlockSpec(memory_space=pltpu.VMEM)
-
-    def projected(light, heavy):
-        keep, send = pl.pallas_call(
-            project_pair_kernel,
-            out_shape=(tile, tile),
-            in_specs=[pl.BlockSpec(memory_space=pltpu.SMEM)] + [vmem] * 4,
-            out_specs=(vmem, vmem),
+    def sent(z, x, heavy):
+        return z ^ (2 + x) if heavy else z ^ 1
+
+    same = move(attended, lambda z, y, x, c: (sent(z, x, c == 1), y, x, c))
+    other = move(attended, lambda z, y, x, c: (sent(z, x, c == 0), y, x, 1 - c))
+    beside = to_other_core(attended, lambda z, y, x, c: c == 1)
+    passed = [
+        move(value, lambda z, y, x, c: (z ^ 1, y, x, c), lambda z, y, x, c: c == 1)
+        for value in (same, other)
+    ]
+
+    def project(choice, *tokens):
+        vmem = pl.BlockSpec(memory_space=pltpu.VMEM)
+        return pl.pallas_call(
+            project_kernel,
+            out_shape=jax.ShapeDtypeStruct((2, rows, half_cols), BF16),
+            in_specs=[pl.BlockSpec(memory_space=pltpu.SMEM)] + [vmem] * (len(tokens) + 4),
+            out_specs=vmem,
             compiler_params=pltpu.CompilerParams(vmem_limit_bytes=24 * 1024 * 1024),
             cost_estimate=pl.CostEstimate(
-                flops=2 * flops, bytes_accessed=2 * moved, transcendentals=0
+                flops=8 * size * half_cols, bytes_accessed=14 * size, transcendentals=0
             ),
-        )(core.astype(jnp.int32)[None], light, heavy, out_weight, mate_weight)
-        return keep.astype(F32) + move(send, lambda z, y, x, c: (z, y, x, 1 - c)).astype(F32)
-
-    far = projected(jnp.where(x == 0, beside, attended), straight).astype(BF16)
+        )(choice.astype(jnp.int32)[None], *tokens, *weights)
+
+    far = project((1 - core) * x, same, other, attended, beside)
     crossed = move(far, lambda z, y, x, c: (z, y, 1 - x, c))
-    near = projected(jnp.where(x == 0, attended, beside), onward) + crossed.astype(F32)
+    near = project((1 - core) * (1 + x), *passed, attended, beside, same, other)
+    near = near.astype(F32) + crossed.astype(F32)
     result = move(near.astype(BF16), lambda z, y, x, c: (z ^ 3 * c ^ x, y, z // 2, z % 2))
     first = jnp.where(y == 0, result[0], result[1])
     return jnp.concatenate([first, jnp.where(y == 0, result[1], result[0])], axis=1)

time: 97.9 us -> 101 us (1.032); the launches traced: 97.6 us -> 99.2 us
  waiting for transfers between devices: 48.3 us -> 42.8 us
  Pallas kernels: 7.7 us -> 10.3 us
  local copies, waits for them, and re-layouts: 2.1 us -> 4.27 us
  other arithmetic: 1.6 us -> 3.05 us
    ppermute x4 -> x2, waiting for transfers between devices: 28.2 us -> 6.03 us  [swap(): return lax.ppermute(value, 'seq', [(s, s ^ mask) for s in range(8)])]
    ppermute x5 -> x9, waiting for transfers between devices: 16.1 us -> 35.8 us  [move(): return lax.ppermute(value, both, pairs)]
    ppermute x5 -> x9, starting transfers between devices: 23.5 us -> 29.9 us  [move(): return lax.ppermute(value, both, pairs)]
    ppermute x4 -> x2, starting transfers between devices: 9.66 us -> 3.39 us  [swap(): return lax.ppermute(value, 'seq', [(s, s ^ mask) for s in range(8)])]
    ppermute x3, waiting for transfers between devices: 4.02 us -> 1 us  [pairs_body(): earlier.append(lax.ppermute(onward.astype(BF16), 'seq', pairs))]
    unnamed x12 -> x14, local copies, waits for them, and re-layouts: 2.1 us -> 4.27 us
    pallas_call x2, Pallas kernels: 5.65 us -> 7.34 us  [project(): pl.pallas_call(project_kernel, out_shape=jax.ShapeDtypeStruct((2, rows, h...]
  transfers between devices with their start and end apart: 12 -> 14, of which waited for: 8 -> 8; matrix products, arithmetic and copies ran while one was open for 0% -> 1% of each run, Pallas kernels for 5% -> 10%
where the time goes in v14:
time: 101 us; the launch traced here: 99.2 us
  waiting for transfers between devices  42.8 us (42%)
  starting transfers between devices  38.6 us (38%)
  Pallas kernels  10.3 us (10%)
  local copies, waits for them, and re-layouts  4.27 us (4%)
  other arithmetic  3.05 us (3%)
    ppermute x9, waiting for transfers between devices, move(): return lax.ppermute(value, both, pairs)  35.8 us
    ppermute x9, starting transfers between devices, move(): return lax.ppermute(value, both, pairs)  29.9 us
    pallas_call x2, Pallas kernels, project(): pl.pallas_call(project_kernel, out_shape=jax.ShapeDtypeStruct((2, rows, h...  7.34 us
    ppermute x2, waiting for transfers between devices, swap(): return lax.ppermute(value, 'seq', [(s, s ^ mask) for s in range(8)])  6.03 us
    ppermute x3, starting transfers between devices, pairs_body(): earlier.append(lax.ppermute(onward.astype(BF16), 'seq', pairs))  5.3 us
    unnamed x14, local copies, waits for them, and re-layouts  4.27 us
    ppermute x2, starting transfers between devices, swap(): return lax.ppermute(value, 'seq', [(s, s ^ mask) for s in range(8)])  3.39 us
  transfers between devices with their start and end apart: 14, of which 8 were waited for; matrix products, arithmetic and copies ran while one was open for 1% of the time, Pallas kernels for 10%

profile of v14, /device:TPU:1, one launch (start us, length us, event | category | flops | bytes accessed | tf_op | source)
XLA Modules:
  0.0 99.2 jit_solution(159388777562288177)
XLA Ops:
  0.0 0.0 copy-start
  0.0 0.0 copy-start.1
  0.0 1.1 %copy-done.1 = bf16[256,1024]{1,0:T(8,128)(2,1)S(1)} copy-done((bf16[256,1024]{1,0:T(8,128)(2,1)S(1)}, bf16[256,1024]{1,0:T(8,128)(2,1)}, u32[]{:S(2)}) %copy-start.1) | copy-done | bytes 524312
  1.1 0.0 copy-start.3
  1.1 1.0 %copy-done.3 = bf16[256,1024]{1,0:T(8,128)(2,1)S(1)} copy-done((bf16[256,1024]{1,0:T(8,128)(2,1)S(1)}, bf16[256,1024]{1,0:T(8,128)(2,1)}, u32[]{:S(2)}) %copy-start.3) | copy-done | bytes 524312
  2.2 0.4 shard_map.56
  2.5 2.1 %collective-permute-start = (bf16[8,128,128]{2,1,0:T(8,128)(2,1)S(1)}, bf16[8,128,128]{2,1,0:T(8,128)(2,1)S(1)}, u32[]{:S(2)}, u32[]{:S(2)}) collective-permute-start(bf16[8,128,128]{2,1,0:T(8,128)(2,1)S(1)} %get-tuple-element.7), channel_id=1, source_target_pairs={{0,4},{4,0},{8,12},{12,8},{16,20},{20,16},{24,28},{28,24},{1,5},{5... | collective-permute-start | bytes 786440 | tf_op jit(solution)/shard_map/ppermute | solution.py:232
  4.7 6.0 %collective-permute-done.mate_ref = bf16[8,128,128]{2,1,0:T(8,128)(2,1)S(1)} collective-permute-done((bf16[8,128,128]{2,1,0:T(8,128)(2,1)S(1)}, bf16[8,128,128]{2,1,0:T(8,128)(2,1)S(1)}, u32[]{:S(2)}, u32[]{:S(2)}) %collective-permute-start) | collective-permute-done | bytes 262176 | tf_op jit(solution)/shard_map/ppermute | solution.py:232
  10.7 0.1 fusion
  10.8 3.1 %collective-permute-start.1 = (bf16[8,128,128]{2,1,0:T(8,128)(2,1)S(1)}, bf16[8,128,128]{2,1,0:T(8,128)(2,1)S(1)}, u32[]{:S(2)}, u32[]{:S(2)}) collective-permute-start(bf16[8,128,128]{2,1,0:T(8,128)(2,1)S(1)} %fusion), channel_id=1, source_target_pairs={{0,8},{4,12},{1,9},{5,13},{2,10},{6,14},{3,11},{7,15}} | collective-permute-start | bytes 786440 | tf_op jit(solution)/shard_map/ppermute | solution.py:265
  13.9 0.0 copy-done
  13.9 3.0 %collective-permute-start.11 = (bf16[1024,512]{1,0:T(8,128)(2,1)S(1)}, bf16[1024,512]{1,0:T(8,128)(2,1)S(1)}, u32[]{:S(2)}, u32[]{:S(2)}) collective-permute-start(bf16[1024,512]{1,0:T(8,128)(2,1)S(1)} %copy-done), channel_id=1, source_target_pairs={{0,5},{1,4},{2,7},{3,6},{4,1},{5,0},{6,3},{7,2},{8,13},{9,12},{10,... | collective-permute-start | bytes 3145736 | tf_op jit(solution)/shard_map/ppermute | solution.py:236
  16.9 1.0 collective-permute-done.1.refs_0_
  17.9 0.1 fusion.1
  18.0 0.0 copy-start.2
  18.0 0.8 collective-permute-start.2
  18.8 2.5 %collective-permute-start.10 = (bf16[1024,512]{1,0:T(8,128)(2,1)S(1)}, bf16[1024,512]{1,0:T(8,128)(2,1)}, u32[]{:S(2)}, u32[]{:S(2)}) collective-permute-start(bf16[1024,512]{1,0:T(8,128)(2,1)S(1)} %copy-done), channel_id=1, source_target_pairs={{0,1},{1,0},{2,3},{3,2},{4,5},{5,4},{6,7},{7,6},{8,9},{9,8},{10,11... | collective-permute-start | bytes 3145736 | tf_op jit(solution)/shard_map/ppermute | solution.py:236
  21.4 1.3 %collective-permute-start.9 = (bf16[1024,512]{1,0:T(8,128)(2,1)S(1)}, bf16[1024,512]{1,0:T(8,128)(2,1)}, u32[]{:S(2)}, u32[]{:S(2)}) collective-permute-start(bf16[1024,512]{1,0:T(8,128)(2,1)S(1)} %copy-done), channel_id=1, source_target_pairs={{0,4},{4,0},{8,12},{12,8},{16,20},{20,16},{24,28},{28,24},{1,5},{5... | collective-permute-start | bytes 3145736 | tf_op jit(solution)/shard_map/ppermute | solution.py:232
  22.6 0.0 collective-permute-done.2.refs_1_
  22.6 0.8 add_convert_fusion.1
  23.5 1.4 %collective-permute-start.3 = (bf16[8,128,128]{2,1,0:T(8,128)(2,1)}, bf16[8,128,128]{2,1,0:T(8,128)(2,1)}, u32[]{:S(2)}, u32[]{:S(2)}) collective-permute-start(bf16[8,128,128]{2,1,0:T(8,128)(2,1)} %add_convert_fusion.1), channel_id=1, source_target_pairs={{16,24},{20,28},{17,25},{21,29},{18,26},{22,30},{19,27},{23,31}} | collective-permute-start | bytes 786440 | tf_op jit(solution)/shard_map/ppermute | solution.py:265
  24.8 0.0 copy-done.2
  24.8 0.0 copy-start.4
  24.8 1.0 %copy-done.4 = bf16[256,1024]{1,0:T(8,128)(2,1)S(1)} copy-done((bf16[256,1024]{1,0:T(8,128)(2,1)S(1)}, bf16[256,1024]{1,0:T(8,128)(2,1)}, u32[]{:S(2)}) %copy-start.4) | copy-done | bytes 524312
  25.9 0.0 copy-start.5
  25.9 1.0 %copy-done.5 = bf16[256,1024]{1,0:T(8,128)(2,1)S(1)} copy-done((bf16[256,1024]{1,0:T(8,128)(2,1)S(1)}, bf16[256,1024]{1,0:T(8,128)(2,1)}, u32[]{:S(2)}) %copy-start.5) | copy-done | bytes 524312
  26.9 0.0 copy-start.6
  26.9 0.9 shard_map.55.within_ref
  27.8 0.0 collective-permute-done.3.refs_2_
  27.9 0.0 copy-done.6
  27.9 1.7 %shard_map.57.refs_2_ = bf16[256,1024]{1,0:T(8,128)(2,1)S(1)} custom-call(s32[1]{0:T(128)} %bitcast.1.second_ref, bf16[256,1024]{1,0:T(8,128)(2,1)S(1)} %copy-done.5, f32[256,1024]{1,0:T(8,128)S(1)} %shard_map.55.within_ref, f32[1,1024]{1,0:T(1,128)S(1)} %bitcast.8, bf16[8,128,128]{2,1,0:T(8,128)(2,1)S(1)} %collective-permute-done.mate_ref, ...), custom_call_target="tpu_custom_call" | custom-call | flops 67108864 | bytes 2097152 | tf_op jit(solution)/shard_map/pallas_call | solution.py:105
  29.6 5.5 %collective-permute-start.6 = (bf16[256,1024]{1,0:T(8,128)(2,1)S(1)}, bf16[256,1024]{1,0:T(8,128)(2,1)S(1)}, u32[]{:S(2)}, u32[]{:S(2)}) collective-permute-start(bf16[256,1024]{1,0:T(8,128)(2,1)S(1)} %shard_map.57.refs_2_), channel_id=1, source_target_pairs={{0,17},{1,8},{2,27},{3,10},{4,21},{5,12},{6,31},{7,14},{8,25},{9,0... | collective-permute-start | bytes 1572872 | tf_op jit(solution)/shard_map/ppermute | solution.py:236
  35.1 5.2 %collective-permute-start.4 = (bf16[256,1024]{1,0:T(8,128)(2,1)S(1)}, bf16[256,1024]{1,0:T(8,128)(2,1)}, u32[]{:S(2)}, u32[]{:S(2)}) collective-permute-start(bf16[256,1024]{1,0:T(8,128)(2,1)S(1)} %shard_map.57.refs_2_), channel_id=1, source_target_pairs={{0,8},{1,17},{2,10},{3,27},{4,12},{5,21},{6,14},{7,31},{8,0},{9,25... | collective-permute-start | bytes 1572872 | tf_op jit(solution)/shard_map/ppermute | solution.py:236
  40.2 0.8 collective-permute-done.11.refs_9_.refs_7_
  41.0 2.8 %collective-permute-start.8 = (bf16[256,1024]{1,0:T(8,128)(2,1)S(1)}, bf16[256,1024]{1,0:T(8,128)(2,1)}, u32[]{:S(2)}, u32[]{:S(2)}) collective-permute-start(bf16[256,1024]{1,0:T(8,128)(2,1)S(1)} %shard_map.57.refs_2_), channel_id=1, source_target_pairs={{1,0},{3,2},{5,4},{7,6},{9,8},{11,10},{13,12},{15,14},{17,16},{19,... | collective-permute-start | bytes 1572872 | tf_op jit(solution)/shard_map/ppermute | solution.py:236
  43.9 14.2 %collective-permute-done.6.refs_5_.refs_1_ = bf16[256,1024]{1,0:T(8,128)(2,1)S(1)} collective-permute-done((bf16[256,1024]{1,0:T(8,128)(2,1)S(1)}, bf16[256,1024]{1,0:T(8,128)(2,1)S(1)}, u32[]{:S(2)}, u32[]{:S(2)}) %collective-permute-start.6) | collective-permute-done | bytes 524320 | tf_op jit(solution)/shard_map/ppermute | solution.py:236
  58.1 1.9 %collective-permute-start.7 = (bf16[256,1024]{1,0:T(8,128)(2,1)S(1)}, bf16[256,1024]{1,0:T(8,128)(2,1)}, u32[]{:S(2)}, u32[]{:S(2)}) collective-permute-start(bf16[256,1024]{1,0:T(8,128)(2,1)S(1)} %collective-permute-done.6.refs_5_.refs_1_), channel_id=1, source_target_pairs={{1,9},{3,11},{5,13},{7,15},{9,1},{11,3},{13,5},{15,7},{17,25},{19,... | collective-permute-start | bytes 1572872 | tf_op jit(solution)/shard_map/ppermute | solution.py:236
  60.0 1.9 %collective-permute-done.4.refs_4_.refs_0_ = bf16[256,1024]{1,0:T(8,128)(2,1)} collective-permute-done((bf16[256,1024]{1,0:T(8,128)(2,1)S(1)}, bf16[256,1024]{1,0:T(8,128)(2,1)}, u32[]{:S(2)}, u32[]{:S(2)}) %collective-permute-start.4) | collective-permute-done | bytes 524320 | tf_op jit(solution)/shard_map/ppermute | solution.py:236
  61.9 2.0 %collective-permute-start.5 = (bf16[256,1024]{1,0:T(8,128)(2,1)}, bf16[256,1024]{1,0:T(8,128)(2,1)}, u32[]{:S(2)}, u32[]{:S(2)}) collective-permute-start(bf16[256,1024]{1,0:T(8,128)(2,1)} %collective-permute-done.4.refs_4_.refs_0_), channel_id=1, source_target_pairs={{1,9},{3,11},{5,13},{7,15},{9,1},{11,3},{13,5},{15,7},{17,25},{19,... | collective-permute-start | bytes 1572872 | tf_op jit(solution)/shard_map/ppermute | solution.py:236
  63.9 0.0 collective-permute-done.10.refs_8_.refs_6_
  63.9 0.0 collective-permute-done.9.refs_7_.refs_5_
  63.9 0.0 collective-permute-done.8.refs_3_
  64.0 3.9 %shard_map.59 = bf16[2,256,512]{2,1,0:T(8,128)(2,1)} custom-call(s32[1]{0:T(128)} %bitcast.3.choice_ref, bf16[256,1024]{1,0:T(8,128)(2,1)} %collective-permute-done.4.refs_4_.refs_0_, bf16[256,1024]{1,0:T(8,128)(2,1)S(1)} %collective-permute-done.6.refs_5_.refs_1_, bf16[256,1024]{1,0:T(8,128)(2,1)S(1)} %shard_map.57.refs_2_, ...), custom_call_target="tpu_custom_call" | custom-call | flops 1073741824 | bytes 3670016 | tf_op jit(solution)/shard_map/pallas_call | solution.py:282
  67.9 1.6 %collective-permute-start.12 = (bf16[2,256,512]{2,1,0:T(8,128)(2,1)}, bf16[2,256,512]{2,1,0:T(8,128)(2,1)}, u32[]{:S(2)}, u32[]{:S(2)}) collective-permute-start(bf16[2,256,512]{2,1,0:T(8,128)(2,1)} %shard_map.59), channel_id=1, source_target_pairs={{0,2},{1,3},{2,0},{3,1},{4,6},{5,7},{6,4},{7,5},{8,10},{9,11},{10,... | collective-permute-start | bytes 1572872 | tf_op jit(solution)/shard_map/ppermute | solution.py:236
  69.5 0.0 collective-permute-done.7.refs_1_
  69.5 4.5 %collective-permute-done.5.refs_0_ = bf16[256,1024]{1,0:T(8,128)(2,1)} collective-permute-done((bf16[256,1024]{1,0:T(8,128)(2,1)}, bf16[256,1024]{1,0:T(8,128)(2,1)}, u32[]{:S(2)}, u32[]{:S(2)}) %collective-permute-start.5) | collective-permute-done | bytes 524320 | tf_op jit(solution)/shard_map/ppermute | solution.py:236
  74.0 3.4 %shard_map.58 = bf16[2,256,512]{2,1,0:T(8,128)(2,1)S(1)} custom-call(s32[1]{0:T(128)} %bitcast.choice_ref, bf16[256,1024]{1,0:T(8,128)(2,1)} %collective-permute-done.5.refs_0_, bf16[256,1024]{1,0:T(8,128)(2,1)} %collective-permute-done.7.refs_1_, bf16[256,1024]{1,0:T(8,128)(2,1)S(1)} %shard_map.57.refs_2_, ...), custom_call_target="tpu_custom_call" | custom-call | flops 1073741824 | bytes 3670016 | tf_op jit(solution)/shard_map/pallas_call | solution.py:282
  77.5 4.6 %collective-permute-done.12 = bf16[2,256,512]{2,1,0:T(8,128)(2,1)} collective-permute-done((bf16[2,256,512]{2,1,0:T(8,128)(2,1)}, bf16[2,256,512]{2,1,0:T(8,128)(2,1)}, u32[]{:S(2)}, u32[]{:S(2)}) %collective-permute-start.12) | collective-permute-done | bytes 524320 | tf_op jit(solution)/shard_map/ppermute | solution.py:236
  82.1 1.2 %add_convert_fusion = bf16[2,256,512]{2,1,0:T(8,128)(2,1)S(1)} fusion(bf16[2,256,512]{2,1,0:T(8,128)(2,1)} %collective-permute-done.12, bf16[2,256,512]{2,1,0:T(8,128)(2,1)S(1)} %shard_map.58), kind=kLoop, calls=%fused_computation | loop fusion | flops 1048576 | bytes 1572864 | tf_op jit(solution)/shard_map/convert_element_type | solution.py:297
  83.3 5.3 %collective-permute-start.13 = (bf16[2,256,512]{2,1,0:T(8,128)(2,1)S(1)}, bf16[2,256,512]{2,1,0:T(8,128)(2,1)S(1)}, u32[]{:S(2)}, u32[]{:S(2)}) collective-permute-start(bf16[2,256,512]{2,1,0:T(8,128)(2,1)S(1)} %add_convert_fusion), channel_id=1, source_target_pairs={{0,0},{1,24},{2,8},{3,16},{4,4},{5,28},{6,12},{7,20},{8,9},{9,17},... | collective-permute-start | bytes 1572872 | tf_op jit(solution)/shard_map/ppermute | solution.py:236
  88.6 9.7 %collective-permute-done.13 = bf16[2,256,512]{2,1,0:T(8,128)(2,1)S(1)} collective-permute-done((bf16[2,256,512]{2,1,0:T(8,128)(2,1)S(1)}, bf16[2,256,512]{2,1,0:T(8,128)(2,1)S(1)}, u32[]{:S(2)}, u32[]{:S(2)}) %collective-permute-start.13) | collective-permute-done | bytes 524320 | tf_op jit(solution)/shard_map/ppermute | solution.py:236
  98.4 0.9 pad_maximum_fusion
  (1 shorter events, 0.0 us)
Async XLA Ops:
  0.0 13.9 %copy-start = (bf16[1024,512]{1,0:T(8,128)(2,1)S(1)}, bf16[1024,512]{1,0:T(8,128)(2,1)}, u32[]{:S(2)}) copy-start(bf16[1024,512]{1,0:T(8,128)(2,1)} %refs_4_.1) | copy-start | bytes 3145732
  0.0 1.1 %copy-start.1 = (bf16[256,1024]{1,0:T(8,128)(2,1)S(1)}, bf16[256,1024]{1,0:T(8,128)(2,1)}, u32[]{:S(2)}) copy-start(bf16[256,1024]{1,0:T(8,128)(2,1)} %k_ref.3) | copy-start | bytes 1572868
  1.1 1.0 %copy-start.3 = (bf16[256,1024]{1,0:T(8,128)(2,1)S(1)}, bf16[256,1024]{1,0:T(8,128)(2,1)}, u32[]{:S(2)}) copy-start(bf16[256,1024]{1,0:T(8,128)(2,1)} %v_ref.3) | copy-start | bytes 1572868
  2.5 8.2 %collective-permute-start = (bf16[8,128,128]{2,1,0:T(8,128)(2,1)S(1)}, bf16[8,128,128]{2,1,0:T(8,128)(2,1)S(1)}, u32[]{:S(2)}, u32[]{:S(2)}) collective-permute-start(bf16[8,128,128]{2,1,0:T(8,128)(2,1)S(1)} %get-tuple-element.7), channel_id=1, source_target_pairs={{0,4},{4,0},{8,12},{12,8},{16,20},{20,16},{24,28},{28,24},{1,5},{5... | collective-permute-start | bytes 786440 | tf_op jit(solution)/shard_map/ppermute | solution.py:232
  10.8 7.2 %collective-permute-start.1 = (bf16[8,128,128]{2,1,0:T(8,128)(2,1)S(1)}, bf16[8,128,128]{2,1,0:T(8,128)(2,1)S(1)}, u32[]{:S(2)}, u32[]{:S(2)}) collective-permute-start(bf16[8,128,128]{2,1,0:T(8,128)(2,1)S(1)} %fusion), channel_id=1, source_target_pairs={{0,8},{4,12},{1,9},{5,13},{2,10},{6,14},{3,11},{7,15}} | collective-permute-start | bytes 786440 | tf_op jit(solution)/shard_map/ppermute | solution.py:265
  13.9 27.1 %collective-permute-start.11 = (bf16[1024,512]{1,0:T(8,128)(2,1)S(1)}, bf16[1024,512]{1,0:T(8,128)(2,1)S(1)}, u32[]{:S(2)}, u32[]{:S(2)}) collective-permute-start(bf16[1024,512]{1,0:T(8,128)(2,1)S(1)} %copy-done), channel_id=1, source_target_pairs={{0,5},{1,4},{2,7},{3,6},{4,1},{5,0},{6,3},{7,2},{8,13},{9,12},{10,... | collective-permute-start | bytes 3145736 | tf_op jit(solution)/shard_map/ppermute | solution.py:236
  18.0 6.8 %copy-start.2 = (bf16[256,1024]{1,0:T(8,128)(2,1)S(1)}, bf16[256,1024]{1,0:T(8,128)(2,1)}, u32[]{:S(2)}) copy-start(bf16[256,1024]{1,0:T(8,128)(2,1)} %k_ref.3) | copy-start | bytes 1572868
  18.0 4.6 %collective-permute-start.2 = (bf16[8,128,128]{2,1,0:T(8,128)(2,1)S(1)}, bf16[8,128,128]{2,1,0:T(8,128)(2,1)S(1)}, u32[]{:S(2)}, u32[]{:S(2)}) collective-permute-start(bf16[8,128,128]{2,1,0:T(8,128)(2,1)S(1)} %fusion.1), channel_id=1, source_target_pairs={{8,16},{12,20},{9,17},{13,21},{10,18},{14,22},{11,19},{15,23}} | collective-permute-start | bytes 786440 | tf_op jit(solution)/shard_map/ppermute | solution.py:265
  18.8 45.1 %collective-permute-start.10 = (bf16[1024,512]{1,0:T(8,128)(2,1)S(1)}, bf16[1024,512]{1,0:T(8,128)(2,1)}, u32[]{:S(2)}, u32[]{:S(2)}) collective-permute-start(bf16[1024,512]{1,0:T(8,128)(2,1)S(1)} %copy-done), channel_id=1, source_target_pairs={{0,1},{1,0},{2,3},{3,2},{4,5},{5,4},{6,7},{7,6},{8,9},{9,8},{10,11... | collective-permute-start | bytes 3145736 | tf_op jit(solution)/shard_map/ppermute | solution.py:236
  21.4 42.6 %collective-permute-start.9 = (bf16[1024,512]{1,0:T(8,128)(2,1)S(1)}, bf16[1024,512]{1,0:T(8,128)(2,1)}, u32[]{:S(2)}, u32[]{:S(2)}) collective-permute-start(bf16[1024,512]{1,0:T(8,128)(2,1)S(1)} %copy-done), channel_id=1, source_target_pairs={{0,4},{4,0},{8,12},{12,8},{16,20},{20,16},{24,28},{28,24},{1,5},{5... | collective-permute-start | bytes 3145736 | tf_op jit(solution)/shard_map/ppermute | solution.py:232
  23.5 4.4 %collective-permute-start.3 = (bf16[8,128,128]{2,1,0:T(8,128)(2,1)}, bf16[8,128,128]{2,1,0:T(8,128)(2,1)}, u32[]{:S(2)}, u32[]{:S(2)}) collective-permute-start(bf16[8,128,128]{2,1,0:T(8,128)(2,1)} %add_convert_fusion.1), channel_id=1, source_target_pairs={{16,24},{20,28},{17,25},{21,29},{18,26},{22,30},{19,27},{23,31}} | collective-permute-start | bytes 786440 | tf_op jit(solution)/shard_map/ppermute | solution.py:265
  24.8 1.0 %copy-start.4 = (bf16[256,1024]{1,0:T(8,128)(2,1)S(1)}, bf16[256,1024]{1,0:T(8,128)(2,1)}, u32[]{:S(2)}) copy-start(bf16[256,1024]{1,0:T(8,128)(2,1)} %v_ref.3) | copy-start | bytes 1572868
  25.9 1.0 %copy-start.5 = (bf16[256,1024]{1,0:T(8,128)(2,1)S(1)}, bf16[256,1024]{1,0:T(8,128)(2,1)}, u32[]{:S(2)}) copy-start(bf16[256,1024]{1,0:T(8,128)(2,1)} %q_ref.3) | copy-start | bytes 1572868
  26.9 0.9 copy-start.6
  29.6 28.5 %collective-permute-start.6 = (bf16[256,1024]{1,0:T(8,128)(2,1)S(1)}, bf16[256,1024]{1,0:T(8,128)(2,1)S(1)}, u32[]{:S(2)}, u32[]{:S(2)}) collective-permute-start(bf16[256,1024]{1,0:T(8,128)(2,1)S(1)} %shard_map.57.refs_2_), channel_id=1, source_target_pairs={{0,17},{1,8},{2,27},{3,10},{4,21},{5,12},{6,31},{7,14},{8,25},{9,0... | collective-permute-start | bytes 1572872 | tf_op jit(solution)/shard_map/ppermute | solution.py:236
  35.1 26.8 %collective-permute-start.4 = (bf16[256,1024]{1,0:T(8,128)(2,1)S(1)}, bf16[256,1024]{1,0:T(8,128)(2,1)}, u32[]{:S(2)}, u32[]{:S(2)}) collective-permute-start(bf16[256,1024]{1,0:T(8,128)(2,1)S(1)} %shard_map.57.refs_2_), channel_id=1, source_target_pairs={{0,8},{1,17},{2,10},{3,27},{4,12},{5,21},{6,14},{7,31},{8,0},{9,25... | collective-permute-start | bytes 1572872 | tf_op jit(solution)/shard_map/ppermute | solution.py:236
  41.0 22.9 %collective-permute-start.8 = (bf16[256,1024]{1,0:T(8,128)(2,1)S(1)}, bf16[256,1024]{1,0:T(8,128)(2,1)}, u32[]{:S(2)}, u32[]{:S(2)}) collective-permute-start(bf16[256,1024]{1,0:T(8,128)(2,1)S(1)} %shard_map.57.refs_2_), channel_id=1, source_target_pairs={{1,0},{3,2},{5,4},{7,6},{9,8},{11,10},{13,12},{15,14},{17,16},{19,... | collective-permute-start | bytes 1572872 | tf_op jit(solution)/shard_map/ppermute | solution.py:236
  58.1 11.4 %collective-permute-start.7 = (bf16[256,1024]{1,0:T(8,128)(2,1)S(1)}, bf16[256,1024]{1,0:T(8,128)(2,1)}, u32[]{:S(2)}, u32[]{:S(2)}) collective-permute-start(bf16[256,1024]{1,0:T(8,128)(2,1)S(1)} %collective-permute-done.6.refs_5_.refs_1_), channel_id=1, source_target_pairs={{1,9},{3,11},{5,13},{7,15},{9,1},{11,3},{13,5},{15,7},{17,25},{19,... | collective-permute-start | bytes 1572872 | tf_op jit(solution)/shard_map/ppermute | solution.py:236
  61.9 12.1 %collective-permute-start.5 = (bf16[256,1024]{1,0:T(8,128)(2,1)}, bf16[256,1024]{1,0:T(8,128)(2,1)}, u32[]{:S(2)}, u32[]{:S(2)}) collective-permute-start(bf16[256,1024]{1,0:T(8,128)(2,1)} %collective-permute-done.4.refs_4_.refs_0_), channel_id=1, source_target_pairs={{1,9},{3,11},{5,13},{7,15},{9,1},{11,3},{13,5},{15,7},{17,25},{19,... | collective-permute-start | bytes 1572872 | tf_op jit(solution)/shard_map/ppermute | solution.py:236
  67.9 14.2 %collective-permute-start.12 = (bf16[2,256,512]{2,1,0:T(8,128)(2,1)}, bf16[2,256,512]{2,1,0:T(8,128)(2,1)}, u32[]{:S(2)}, u32[]{:S(2)}) collective-permute-start(bf16[2,256,512]{2,1,0:T(8,128)(2,1)} %shard_map.59), channel_id=1, source_target_pairs={{0,2},{1,3},{2,0},{3,1},{4,6},{5,7},{6,4},{7,5},{8,10},{9,11},{10,... | collective-permute-start | bytes 1572872 | tf_op jit(solution)/shard_map/ppermute | solution.py:236
  83.3 15.0 %collective-permute-start.13 = (bf16[2,256,512]{2,1,0:T(8,128)(2,1)S(1)}, bf16[2,256,512]{2,1,0:T(8,128)(2,1)S(1)}, u32[]{:S(2)}, u32[]{:S(2)}) collective-permute-start(bf16[2,256,512]{2,1,0:T(8,128)(2,1)S(1)} %add_convert_fusion), channel_id=1, source_target_pairs={{0,0},{1,24},{2,8},{3,16},{4,4},{5,28},{6,12},{7,20},{8,9},{9,17},... | collective-permute-start | bytes 1572872 | tf_op jit(solution)/shard_map/ppermute | solution.py:236

commit v15 on v12

--- a/solution.py
+++ b/solution.py
@@ -200,15 +200,20 @@
     return body
 
 
-def project_kernel(tokens_ref, own_ref, mate_ref, out_ref):
-    for half, weight_ref in enumerate((own_ref, mate_ref)):
-        product = jnp.dot(tokens_ref[...], weight_ref[...], preferred_element_type=F32)
+def join_kernel(own_ref, mate_ref, out_ref):
+    out_ref[0] = own_ref[...]
+    out_ref[1] = mate_ref[...]
+
+
+def project_kernel(tokens_ref, weight_ref, out_ref):
+    for half in range(2):
+        product = jnp.dot(tokens_ref[...], weight_ref[half], preferred_element_type=F32)
         out_ref[half] = product.astype(BF16)
 
 
-def project_pair_kernel(core_ref, light_ref, heavy_ref, own_ref, mate_ref, keep_ref, send_ref):
+def project_pair_kernel(core_ref, light_ref, heavy_ref, weight_ref, keep_ref, send_ref):
     def multiply(out_ref, tokens_ref):
-        project_kernel(tokens_ref, own_ref, mate_ref, out_ref)
+        project_kernel(tokens_ref, weight_ref, out_ref)
 
     @pl.when(core_ref[0] == 0)
     def _():
@@ -264,6 +269,11 @@
         onward += earlier[-1].astype(F32)
     attended = attend(y, queries, within, norm_gain, mate, *earlier)
 
+    mate_weight, _ = lax.optimization_barrier((mate_weight, attended))
+    weight = call(
+        join_kernel, jax.ShapeDtypeStruct((2,) + out_weight.shape, BF16), 0, 8 * out_weight.size
+    )(out_weight, mate_weight)
+
     straight = move(attended, lambda z, y, x, c: (z ^ (2 + x), y, x, c))
     beside = swap(attended, 2)
     onward = swap(straight, 2)
@@ -276,13 +286,13 @@
         keep, send = pl.pallas_call(
             project_pair_kernel,
             out_shape=(tile, tile),
-            in_specs=[pl.BlockSpec(memory_space=pltpu.SMEM)] + [vmem] * 4,
+            in_specs=[pl.BlockSpec(memory_space=pltpu.SMEM)] + [vmem] * 3,
             out_specs=(vmem, vmem),
             compiler_params=pltpu.CompilerParams(vmem_limit_bytes=24 * 1024 * 1024),
             cost_estimate=pl.CostEstimate(
                 flops=2 * flops, bytes_accessed=2 * moved, transcendentals=0
             ),
-        )(core.astype(jnp.int32)[None], light, heavy, out_weight, mate_weight)
+        )(core.astype(jnp.int32)[None], light, heavy, weight)
         return keep.astype(F32) + move(send, lambda z, y, x, c: (z, y, x, 1 - c)).astype(F32)
 
     far = projected(jnp.where(x == 0, beside, attended), straight).astype(BF16)

time: 97.9 us -> 96.7 us (0.988)
  waiting for transfers between devices: 48.3 us -> 46.3 us
    pallas_call x2, Pallas kernels: 5.65 us -> 2.56 us  [projected(): pl.pallas_call(project_pair_kernel, out_shape=(tile, tile), in_specs=[pl....]
    ppermute x4, waiting for transfers between devices: 28.2 us -> 25.5 us  [swap(): return lax.ppermute(value, 'seq', [(s, s ^ mask) for s in range(8)])]
    ppermute x5, starting transfers between devices: 23.5 us -> 25.1 us  [move(): return lax.ppermute(value, both, pairs)]
    pallas_call x0 -> x1, Pallas kernels: none -> 1.36 us  [pairs_body(): call(join_kernel, jax.ShapeDtypeStruct((2,) + out_weight.shape, BF16), 0,...]
    ppermute x4, starting transfers between devices: 9.66 us -> 8.37 us  [swap(): return lax.ppermute(value, 'seq', [(s, s ^ mask) for s in range(8)])]
    unnamed x12 -> x14, local copies, waits for them, and re-layouts: 2.1 us -> 2.11 us
  transfers between devices with their start and end apart: 12 -> 12, of which waited for: 8 -> 9; matrix products, arithmetic and copies ran while one was open for 0% -> 1% of each run, Pallas kernels for 5% -> 5%
where the time goes in v15:
time: 96.7 us; the launch traced here: 96.4 us
  waiting for transfers between devices  46.3 us (48%)
  starting transfers between devices  38.6 us (40%)
  Pallas kernels  6.92 us (7%)
  other arithmetic  2.3 us (2%)
  local copies, waits for them, and re-layouts  2.11 us (2%)
    ppermute x4, waiting for transfers between devices, swap(): return lax.ppermute(value, 'seq', [(s, s ^ mask) for s in range(8)])  25.5 us
    ppermute x5, starting transfers between devices, move(): return lax.ppermute(value, both, pairs)  25.1 us
    ppermute x5, waiting for transfers between devices, move(): return lax.ppermute(value, both, pairs)  16.8 us
    ppermute x4, starting transfers between devices, swap(): return lax.ppermute(value, 'seq', [(s, s ^ mask) for s in range(8)])  8.37 us
    ppermute x3, starting transfers between devices, pairs_body(): earlier.append(lax.ppermute(onward.astype(BF16), 'seq', pairs))  5.15 us
    ppermute x3, waiting for transfers between devices, pairs_body(): earlier.append(lax.ppermute(onward.astype(BF16), 'seq', pairs))  4.02 us
    pallas_call x2, Pallas kernels, projected(): pl.pallas_call(project_pair_kernel, out_shape=(tile, tile), in_specs=[pl....  2.56 us
    unnamed x14, local copies, waits for them, and re-layouts  2.11 us
  transfers between devices with their start and end apart: 12, of which 9 were waited for; matrix products, arithmetic and copies ran while one was open for 1% of the time, Pallas kernels for 5%

profile of v15, /device:TPU:1, one launch (start us, length us, event | category | flops | bytes accessed | tf_op | source)
XLA Modules:
  0.0 96.4 jit_solution(17360890750739651660)
XLA Ops:
  0.0 0.0 copy-start
  0.0 1.0 %copy-done = bf16[256,1024]{1,0:T(8,128)(2,1)S(1)} copy-done((bf16[256,1024]{1,0:T(8,128)(2,1)S(1)}, bf16[256,1024]{1,0:T(8,128)(2,1)}, u32[]{:S(2)}) %copy-start) | copy-done | bytes 524312
  1.0 0.0 copy-start.2
  1.0 1.0 %copy-done.2 = bf16[256,1024]{1,0:T(8,128)(2,1)S(1)} copy-done((bf16[256,1024]{1,0:T(8,128)(2,1)S(1)}, bf16[256,1024]{1,0:T(8,128)(2,1)}, u32[]{:S(2)}) %copy-start.2) | copy-done | bytes 524312
  2.1 0.0 copy-start.5
  2.1 0.4 shard_map.56
  2.4 0.0 copy-start.1
  2.5 0.0 copy-start.3
  2.5 0.0 copy-start.4
  2.5 2.1 %collective-permute-start = (bf16[8,128,128]{2,1,0:T(8,128)(2,1)S(1)}, bf16[8,128,128]{2,1,0:T(8,128)(2,1)S(1)}, u32[]{:S(2)}, u32[]{:S(2)}) collective-permute-start(bf16[8,128,128]{2,1,0:T(8,128)(2,1)S(1)} %get-tuple-element.12), channel_id=1, source_target_pairs={{0,4},{4,0},{8,12},{12,8},{16,20},{20,16},{24,28},{28,24},{1,5},{5... | collective-permute-start | bytes 786440 | tf_op jit(solution)/shard_map/ppermute | solution.py:243
  4.6 6.0 %collective-permute-done.mate_ref = bf16[8,128,128]{2,1,0:T(8,128)(2,1)S(1)} collective-permute-done((bf16[8,128,128]{2,1,0:T(8,128)(2,1)S(1)}, bf16[8,128,128]{2,1,0:T(8,128)(2,1)S(1)}, u32[]{:S(2)}, u32[]{:S(2)}) %collective-permute-start) | collective-permute-done | bytes 262176 | tf_op jit(solution)/shard_map/ppermute | solution.py:243
  10.6 0.1 fusion
  10.7 3.1 %collective-permute-start.1 = (bf16[8,128,128]{2,1,0:T(8,128)(2,1)S(1)}, bf16[8,128,128]{2,1,0:T(8,128)(2,1)S(1)}, u32[]{:S(2)}, u32[]{:S(2)}) collective-permute-start(bf16[8,128,128]{2,1,0:T(8,128)(2,1)S(1)} %fusion), channel_id=1, source_target_pairs={{0,8},{4,12},{1,9},{5,13},{2,10},{6,14},{3,11},{7,15}} | collective-permute-start | bytes 786440 | tf_op jit(solution)/shard_map/ppermute | solution.py:268
  13.8 4.0 %collective-permute-done.1.refs_0_ = bf16[8,128,128]{2,1,0:T(8,128)(2,1)S(1)} collective-permute-done((bf16[8,128,128]{2,1,0:T(8,128)(2,1)S(1)}, bf16[8,128,128]{2,1,0:T(8,128)(2,1)S(1)}, u32[]{:S(2)}, u32[]{:S(2)}) %collective-permute-start.1) | collective-permute-done | bytes 262176 | tf_op jit(solution)/shard_map/ppermute | solution.py:268
  17.9 0.1 fusion.1
  18.0 0.0 copy-start.6
  18.0 0.7 collective-permute-start.2
  18.7 0.0 copy-done.5
  18.7 1.3 %collective-permute-start.7 = (bf16[1024,512]{1,0:T(8,128)(2,1)S(1)}, bf16[1024,512]{1,0:T(8,128)(2,1)}, u32[]{:S(2)}, u32[]{:S(2)}) collective-permute-start(bf16[1024,512]{1,0:T(8,128)(2,1)S(1)} %copy-done.5), channel_id=1, source_target_pairs={{0,4},{4,0},{8,12},{12,8},{16,20},{20,16},{24,28},{28,24},{1,5},{5... | collective-permute-start | bytes 3145736 | tf_op jit(solution)/shard_map/ppermute | solution.py:243
  20.0 0.0 collective-permute-done.2.refs_1_
  20.0 0.8 add_convert_fusion.2
  20.8 1.3 %collective-permute-start.3 = (bf16[8,128,128]{2,1,0:T(8,128)(2,1)}, bf16[8,128,128]{2,1,0:T(8,128)(2,1)}, u32[]{:S(2)}, u32[]{:S(2)}) collective-permute-start(bf16[8,128,128]{2,1,0:T(8,128)(2,1)} %add_convert_fusion.2), channel_id=1, source_target_pairs={{16,24},{20,28},{17,25},{21,29},{18,26},{22,30},{19,27},{23,31}} | collective-permute-start | bytes 786440 | tf_op jit(solution)/shard_map/ppermute | solution.py:268
  22.1 0.0 copy-done.1
  22.1 0.0 copy-done.3
  22.2 0.0 copy-done.4
  22.2 0.9 shard_map.55.within_ref
  23.1 0.0 collective-permute-done.3.refs_2_
  23.1 0.0 copy-done.6
  23.1 1.7 %shard_map.57 = bf16[256,1024]{1,0:T(8,128)(2,1)S(1)} custom-call(s32[1]{0:T(128)} %bitcast.1.second_ref, bf16[256,1024]{1,0:T(8,128)(2,1)S(1)} %copy-done.4, f32[256,1024]{1,0:T(8,128)S(1)} %shard_map.55.within_ref, f32[1,1024]{1,0:T(1,128)S(1)} %bitcast.7, bf16[8,128,128]{2,1,0:T(8,128)(2,1)S(1)} %collective-permute-done.mate_ref, ...), custom_call_target="tpu_custom_call" | custom-call | flops 67108864 | bytes 2097152 | tf_op jit(solution)/shard_map/pallas_call | solution.py:105
  24.8 4.9 %collective-permute-start.4 = (bf16[256,1024]{1,0:T(8,128)(2,1)S(1)}, bf16[256,1024]{1,0:T(8,128)(2,1)S(1)}, u32[]{:S(2)}, u32[]{:S(2)}) collective-permute-start(bf16[256,1024]{1,0:T(8,128)(2,1)S(1)} %shard_map.57), channel_id=1, source_target_pairs={{0,8},{4,12},{8,0},{12,4},{16,24},{20,28},{24,16},{28,20},{1,9},{5... | collective-permute-start | bytes 1572872 | tf_op jit(solution)/shard_map/ppermute | solution.py:243
  29.7 6.9 %collective-permute-start.5 = (bf16[256,1024]{1,0:T(8,128)(2,1)S(1)}, bf16[256,1024]{1,0:T(8,128)(2,1)S(1)}, u32[]{:S(2)}, u32[]{:S(2)}) collective-permute-start(bf16[256,1024]{1,0:T(8,128)(2,1)S(1)} %shard_map.57), channel_id=1, source_target_pairs={{0,16},{1,17},{2,26},{3,27},{4,20},{5,21},{6,30},{7,31},{8,24},{9,... | collective-permute-start | bytes 1572872 | tf_op jit(solution)/shard_map/ppermute | solution.py:247
  36.6 4.4 %collective-permute-done.7.mate_ref = bf16[1024,512]{1,0:T(8,128)(2,1)} collective-permute-done((bf16[1024,512]{1,0:T(8,128)(2,1)S(1)}, bf16[1024,512]{1,0:T(8,128)(2,1)}, u32[]{:S(2)}, u32[]{:S(2)}) %collective-permute-start.7) | collective-permute-done | bytes 1048608 | tf_op jit(solution)/shard_map/ppermute | solution.py:243
  41.0 1.4 %shard_map.58.weight_ref = bf16[2,1024,512]{2,1,0:T(8,128)(2,1)S(1)} custom-call(bf16[1024,512]{1,0:T(8,128)(2,1)S(1)} %copy-done.5, bf16[1024,512]{1,0:T(8,128)(2,1)} %collective-permute-done.7.mate_ref), custom_call_target="tpu_custom_call" | custom-call | bytes 4194304 | tf_op jit(solution)/shard_map/pallas_call | solution.py:273
  42.4 4.2 %collective-permute-done.4 = bf16[256,1024]{1,0:T(8,128)(2,1)S(1)} collective-permute-done((bf16[256,1024]{1,0:T(8,128)(2,1)S(1)}, bf16[256,1024]{1,0:T(8,128)(2,1)S(1)}, u32[]{:S(2)}, u32[]{:S(2)}) %collective-permute-start.4) | collective-permute-done | bytes 524320 | tf_op jit(solution)/shard_map/ppermute | solution.py:243
  46.6 0.1 broadcast_select_fusion.1
  46.7 2.3 %collective-permute-done.5.heavy_ref = bf16[256,1024]{1,0:T(8,128)(2,1)S(1)} collective-permute-done((bf16[256,1024]{1,0:T(8,128)(2,1)S(1)}, bf16[256,1024]{1,0:T(8,128)(2,1)S(1)}, u32[]{:S(2)}, u32[]{:S(2)}) %collective-permute-start.5) | collective-permute-done | bytes 524320 | tf_op jit(solution)/shard_map/ppermute | solution.py:247
  49.0 1.3 %shard_map.60 = (bf16[2,256,512]{2,1,0:T(8,128)(2,1)S(1)}, bf16[2,256,512]{2,1,0:T(8,128)(2,1)S(1)}) custom-call(s32[1]{0:T(128)} %bitcast.core_ref, bf16[256,1024]{1,0:T(8,128)(2,1)S(1)} %get-tuple-element.20.light_ref, bf16[256,1024]{1,0:T(8,128)(2,1)S(1)} %collective-permute-done.5.heavy_ref, bf16[2,1024,512]{2,1,0:T(8,128)(2,1)S(1)} %shard_map.58.weight_ref), custom_call_target="tpu_custom_call" | custom-call | flops 1073741824 | bytes 4194304 | tf_op jit(solution)/shard_map/pallas_call | solution.py:286
  50.3 11.8 %collective-permute-start.9 = (bf16[2,256,512]{2,1,0:T(8,128)(2,1)S(1)}, bf16[2,256,512]{2,1,0:T(8,128)(2,1)S(1)}, u32[]{:S(2)}, u32[]{:S(2)}) collective-permute-start(bf16[2,256,512]{2,1,0:T(8,128)(2,1)S(1)} %get-tuple-element.18), channel_id=1, source_target_pairs={{0,1},{1,0},{2,3},{3,2},{4,5},{5,4},{6,7},{7,6},{8,9},{9,8},{10,11... | collective-permute-start | bytes 1572872 | tf_op jit(solution)/shard_map/ppermute | solution.py:247
  62.1 0.1 collective-permute-start.6
  62.2 1.5 %collective-permute-done.9 = bf16[2,256,512]{2,1,0:T(8,128)(2,1)S(1)} collective-permute-done((bf16[2,256,512]{2,1,0:T(8,128)(2,1)S(1)}, bf16[2,256,512]{2,1,0:T(8,128)(2,1)S(1)}, u32[]{:S(2)}, u32[]{:S(2)}) %collective-permute-start.9) | collective-permute-done | bytes 524320 | tf_op jit(solution)/shard_map/ppermute | solution.py:247
  63.6 0.1 add_convert_fusion.1
  63.8 1.1 %collective-permute-start.10 = (bf16[2,256,512]{2,1,0:T(8,128)(2,1)S(1)}, bf16[2,256,512]{2,1,0:T(8,128)(2,1)S(1)}, u32[]{:S(2)}, u32[]{:S(2)}) collective-permute-start(bf16[2,256,512]{2,1,0:T(8,128)(2,1)S(1)} %add_convert_fusion.1), channel_id=1, source_target_pairs={{0,2},{1,3},{2,0},{3,1},{4,6},{5,7},{6,4},{7,5},{8,10},{9,11},{10,... | collective-permute-start | bytes 1572872 | tf_op jit(solution)/shard_map/ppermute | solution.py:247
  64.8 10.8 %collective-permute-done.6.heavy_ref = bf16[256,1024]{1,0:T(8,128)(2,1)S(1)} collective-permute-done((bf16[256,1024]{1,0:T(8,128)(2,1)S(1)}, bf16[256,1024]{1,0:T(8,128)(2,1)S(1)}, u32[]{:S(2)}, u32[]{:S(2)}) %collective-permute-start.6) | collective-permute-done | bytes 524320 | tf_op jit(solution)/shard_map/ppermute | solution.py:243
  75.6 1.3 %shard_map.59 = (bf16[2,256,512]{2,1,0:T(8,128)(2,1)S(1)}, bf16[2,256,512]{2,1,0:T(8,128)(2,1)S(1)}) custom-call(s32[1]{0:T(128)} %bitcast.core_ref, bf16[256,1024]{1,0:T(8,128)(2,1)S(1)} %get-tuple-element.19.light_ref, bf16[256,1024]{1,0:T(8,128)(2,1)S(1)} %collective-permute-done.6.heavy_ref, bf16[2,1024,512]{2,1,0:T(8,128)(2,1)S(1)} %shard_map.58.weight_ref), custom_call_target="tpu_custom_call" | custom-call | flops 1073741824 | bytes 4194304 | tf_op jit(solution)/shard_map/pallas_call | solution.py:286
  76.9 0.9 collective-permute-start.8
  77.8 0.0 collective-permute-done.10
  77.8 1.5 %collective-permute-done.8 = bf16[2,256,512]{2,1,0:T(8,128)(2,1)S(1)} collective-permute-done((bf16[2,256,512]{2,1,0:T(8,128)(2,1)S(1)}, bf16[2,256,512]{2,1,0:T(8,128)(2,1)S(1)}, u32[]{:S(2)}, u32[]{:S(2)}) %collective-permute-start.8) | collective-permute-done | bytes 524320 | tf_op jit(solution)/shard_map/ppermute | solution.py:247
  79.4 0.2 add_convert_fusion
  79.6 4.3 %collective-permute-start.11 = (bf16[2,256,512]{2,1,0:T(8,128)(2,1)S(1)}, bf16[2,256,512]{2,1,0:T(8,128)(2,1)S(1)}, u32[]{:S(2)}, u32[]{:S(2)}) collective-permute-start(bf16[2,256,512]{2,1,0:T(8,128)(2,1)S(1)} %add_convert_fusion), channel_id=1, source_target_pairs={{0,0},{1,24},{2,8},{3,16},{4,4},{5,28},{6,12},{7,20},{8,9},{9,17},... | collective-permute-start | bytes 1572872 | tf_op jit(solution)/shard_map/ppermute | solution.py:247
  83.9 11.5 %collective-permute-done.11 = bf16[2,256,512]{2,1,0:T(8,128)(2,1)S(1)} collective-permute-done((bf16[2,256,512]{2,1,0:T(8,128)(2,1)S(1)}, bf16[2,256,512]{2,1,0:T(8,128)(2,1)S(1)}, u32[]{:S(2)}, u32[]{:S(2)}) %collective-permute-start.11) | collective-permute-done | bytes 524320 | tf_op jit(solution)/shard_map/ppermute | solution.py:247
  95.5 0.9 pad_maximum_fusion
  (1 shorter events, 0.0 us)
Async XLA Ops:
  0.0 1.0 %copy-start = (bf16[256,1024]{1,0:T(8,128)(2,1)S(1)}, bf16[256,1024]{1,0:T(8,128)(2,1)}, u32[]{:S(2)}) copy-start(bf16[256,1024]{1,0:T(8,128)(2,1)} %k_ref.3) | copy-start | bytes 1572868
  1.0 1.0 %copy-start.2 = (bf16[256,1024]{1,0:T(8,128)(2,1)S(1)}, bf16[256,1024]{1,0:T(8,128)(2,1)}, u32[]{:S(2)}) copy-start(bf16[256,1024]{1,0:T(8,128)(2,1)} %v_ref.3) | copy-start | bytes 1572868
  2.1 16.6 %copy-start.5 = (bf16[1024,512]{1,0:T(8,128)(2,1)S(1)}, bf16[1024,512]{1,0:T(8,128)(2,1)}, u32[]{:S(2)}) copy-start(bf16[1024,512]{1,0:T(8,128)(2,1)} %own_ref.1) | copy-start | bytes 3145732
  2.4 19.7 %copy-start.1 = (bf16[256,1024]{1,0:T(8,128)(2,1)S(1)}, bf16[256,1024]{1,0:T(8,128)(2,1)}, u32[]{:S(2)}) copy-start(bf16[256,1024]{1,0:T(8,128)(2,1)} %k_ref.3) | copy-start | bytes 1572868
  2.5 19.7 %copy-start.3 = (bf16[256,1024]{1,0:T(8,128)(2,1)S(1)}, bf16[256,1024]{1,0:T(8,128)(2,1)}, u32[]{:S(2)}) copy-start(bf16[256,1024]{1,0:T(8,128)(2,1)} %v_ref.3) | copy-start | bytes 1572868
  2.5 19.7 %copy-start.4 = (bf16[256,1024]{1,0:T(8,128)(2,1)S(1)}, bf16[256,1024]{1,0:T(8,128)(2,1)}, u32[]{:S(2)}) copy-start(bf16[256,1024]{1,0:T(8,128)(2,1)} %q_ref.3) | copy-start | bytes 1572868
  2.5 8.2 %collective-permute-start = (bf16[8,128,128]{2,1,0:T(8,128)(2,1)S(1)}, bf16[8,128,128]{2,1,0:T(8,128)(2,1)S(1)}, u32[]{:S(2)}, u32[]{:S(2)}) collective-permute-start(bf16[8,128,128]{2,1,0:T(8,128)(2,1)S(1)} %get-tuple-element.12), channel_id=1, source_target_pairs={{0,4},{4,0},{8,12},{12,8},{16,20},{20,16},{24,28},{28,24},{1,5},{5... | collective-permute-start | bytes 786440 | tf_op jit(solution)/shard_map/ppermute | solution.py:243
  10.7 7.1 %collective-permute-start.1 = (bf16[8,128,128]{2,1,0:T(8,128)(2,1)S(1)}, bf16[8,128,128]{2,1,0:T(8,128)(2,1)S(1)}, u32[]{:S(2)}, u32[]{:S(2)}) collective-permute-start(bf16[8,128,128]{2,1,0:T(8,128)(2,1)S(1)} %fusion), channel_id=1, source_target_pairs={{0,8},{4,12},{1,9},{5,13},{2,10},{6,14},{3,11},{7,15}} | collective-permute-start | bytes 786440 | tf_op jit(solution)/shard_map/ppermute | solution.py:268
  18.0 5.1 %copy-start.6 = (f32[1024]{0:T(1024)S(1)}, f32[1024]{0:T(1024)}, u32[]{:S(2)}) copy-start(f32[1024]{0:T(1024)} %param.8) | copy-start | bytes 12292
  18.0 2.0 %collective-permute-start.2 = (bf16[8,128,128]{2,1,0:T(8,128)(2,1)S(1)}, bf16[8,128,128]{2,1,0:T(8,128)(2,1)S(1)}, u32[]{:S(2)}, u32[]{:S(2)}) collective-permute-start(bf16[8,128,128]{2,1,0:T(8,128)(2,1)S(1)} %fusion.1), channel_id=1, source_target_pairs={{8,16},{12,20},{9,17},{13,21},{10,18},{14,22},{11,19},{15,23}} | collective-permute-start | bytes 786440 | tf_op jit(solution)/shard_map/ppermute | solution.py:268
  18.7 22.4 %collective-permute-start.7 = (bf16[1024,512]{1,0:T(8,128)(2,1)S(1)}, bf16[1024,512]{1,0:T(8,128)(2,1)}, u32[]{:S(2)}, u32[]{:S(2)}) collective-permute-start(bf16[1024,512]{1,0:T(8,128)(2,1)S(1)} %copy-done.5), channel_id=1, source_target_pairs={{0,4},{4,0},{8,12},{12,8},{16,20},{20,16},{24,28},{28,24},{1,5},{5... | collective-permute-start | bytes 3145736 | tf_op jit(solution)/shard_map/ppermute | solution.py:243
  20.8 2.3 %collective-permute-start.3 = (bf16[8,128,128]{2,1,0:T(8,128)(2,1)}, bf16[8,128,128]{2,1,0:T(8,128)(2,1)}, u32[]{:S(2)}, u32[]{:S(2)}) collective-permute-start(bf16[8,128,128]{2,1,0:T(8,128)(2,1)} %add_convert_fusion.2), channel_id=1, source_target_pairs={{16,24},{20,28},{17,25},{21,29},{18,26},{22,30},{19,27},{23,31}} | collective-permute-start | bytes 786440 | tf_op jit(solution)/shard_map/ppermute | solution.py:268
  24.8 21.8 %collective-permute-start.4 = (bf16[256,1024]{1,0:T(8,128)(2,1)S(1)}, bf16[256,1024]{1,0:T(8,128)(2,1)S(1)}, u32[]{:S(2)}, u32[]{:S(2)}) collective-permute-start(bf16[256,1024]{1,0:T(8,128)(2,1)S(1)} %shard_map.57), channel_id=1, source_target_pairs={{0,8},{4,12},{8,0},{12,4},{16,24},{20,28},{24,16},{28,20},{1,9},{5... | collective-permute-start | bytes 1572872 | tf_op jit(solution)/shard_map/ppermute | solution.py:243
  29.7 19.3 %collective-permute-start.5 = (bf16[256,1024]{1,0:T(8,128)(2,1)S(1)}, bf16[256,1024]{1,0:T(8,128)(2,1)S(1)}, u32[]{:S(2)}, u32[]{:S(2)}) collective-permute-start(bf16[256,1024]{1,0:T(8,128)(2,1)S(1)} %shard_map.57), channel_id=1, source_target_pairs={{0,16},{1,17},{2,26},{3,27},{4,20},{5,21},{6,30},{7,31},{8,24},{9,... | collective-permute-start | bytes 1572872 | tf_op jit(solution)/shard_map/ppermute | solution.py:247
  50.3 13.4 %collective-permute-start.9 = (bf16[2,256,512]{2,1,0:T(8,128)(2,1)S(1)}, bf16[2,256,512]{2,1,0:T(8,128)(2,1)S(1)}, u32[]{:S(2)}, u32[]{:S(2)}) collective-permute-start(bf16[2,256,512]{2,1,0:T(8,128)(2,1)S(1)} %get-tuple-element.18), channel_id=1, source_target_pairs={{0,1},{1,0},{2,3},{3,2},{4,5},{5,4},{6,7},{7,6},{8,9},{9,8},{10,11... | collective-permute-start | bytes 1572872 | tf_op jit(solution)/shard_map/ppermute | solution.py:247
  62.1 13.5 %collective-permute-start.6 = (bf16[256,1024]{1,0:T(8,128)(2,1)S(1)}, bf16[256,1024]{1,0:T(8,128)(2,1)S(1)}, u32[]{:S(2)}, u32[]{:S(2)}) collective-permute-start(bf16[256,1024]{1,0:T(8,128)(2,1)S(1)} %collective-permute-done.5.heavy_ref), channel_id=1, source_target_pairs={{0,8},{4,12},{8,0},{12,4},{16,24},{20,28},{24,16},{28,20},{1,9},{5... | collective-permute-start | bytes 1572872 | tf_op jit(solution)/shard_map/ppermute | solution.py:243
  63.8 14.1 %collective-permute-start.10 = (bf16[2,256,512]{2,1,0:T(8,128)(2,1)S(1)}, bf16[2,256,512]{2,1,0:T(8,128)(2,1)S(1)}, u32[]{:S(2)}, u32[]{:S(2)}) collective-permute-start(bf16[2,256,512]{2,1,0:T(8,128)(2,1)S(1)} %add_convert_fusion.1), channel_id=1, source_target_pairs={{0,2},{1,3},{2,0},{3,1},{4,6},{5,7},{6,4},{7,5},{8,10},{9,11},{10,... | collective-permute-start | bytes 1572872 | tf_op jit(solution)/shard_map/ppermute | solution.py:247
  76.9 2.5 %collective-permute-start.8 = (bf16[2,256,512]{2,1,0:T(8,128)(2,1)S(1)}, bf16[2,256,512]{2,1,0:T(8,128)(2,1)S(1)}, u32[]{:S(2)}, u32[]{:S(2)}) collective-permute-start(bf16[2,256,512]{2,1,0:T(8,128)(2,1)S(1)} %get-tuple-element.16), channel_id=1, source_target_pairs={{0,1},{1,0},{2,3},{3,2},{4,5},{5,4},{6,7},{7,6},{8,9},{9,8},{10,11... | collective-permute-start | bytes 1572872 | tf_op jit(solution)/shard_map/ppermute | solution.py:247
  79.6 15.9 %collective-permute-start.11 = (bf16[2,256,512]{2,1,0:T(8,128)(2,1)S(1)}, bf16[2,256,512]{2,1,0:T(8,128)(2,1)S(1)}, u32[]{:S(2)}, u32[]{:S(2)}) collective-permute-start(bf16[2,256,512]{2,1,0:T(8,128)(2,1)S(1)} %add_convert_fusion), channel_id=1, source_target_pairs={{0,0},{1,24},{2,8},{3,16},{4,4},{5,28},{6,12},{7,20},{8,9},{9,17},... | collective-permute-start | bytes 1572872 | tf_op jit(solution)/shard_map/ppermute | solution.py:247

commit v16 on v15

--- a/solution.py
+++ b/solution.py
@@ -261,6 +261,7 @@
     mate_weight = swap(out_weight, 1)
 
     mate = swap(narrow, 1)
+    mate, within = lax.optimization_barrier((mate, within))
     onward = wide + mate.astype(F32)
     earlier = []
     for plane in range(3):

time: 96.7 us -> 94.8 us (0.980)
  waiting for transfers between devices: 46.3 us -> 42.4 us
  local copies, waits for them, and re-layouts: 2.11 us -> 4.18 us
  starting transfers between devices: 38.6 us -> 39.8 us
    ppermute x4, waiting for transfers between devices: 25.5 us -> 20.2 us  [swap(): return lax.ppermute(value, 'seq', [(s, s ^ mask) for s in range(8)])]
    unnamed x14 -> x12, local copies, waits for them, and re-layouts: 2.11 us -> 4.18 us
    ppermute x5, starting transfers between devices: 25.1 us -> 27 us  [move(): return lax.ppermute(value, both, pairs)]
    ppermute x5, waiting for transfers between devices: 16.8 us -> 18.1 us  [move(): return lax.ppermute(value, both, pairs)]
  transfers between devices with their start and end apart: 12 -> 12, of which waited for: 9 -> 8; matrix products, arithmetic and copies ran while one was open for 1% -> 0% of each run, Pallas kernels for 5% -> 5%
where the time goes in v16:
time: 94.8 us; the launch traced here: 94.5 us
  waiting for transfers between devices  42.4 us (45%)
  starting transfers between devices  39.8 us (42%)
  Pallas kernels  6.28 us (7%)
  local copies, waits for them, and re-layouts  4.18 us (4%)
  other arithmetic  1.6 us (2%)
    ppermute x5, starting transfers between devices, move(): return lax.ppermute(value, both, pairs)  27 us
    ppermute x4, waiting for transfers between devices, swap(): return lax.ppermute(value, 'seq', [(s, s ^ mask) for s in range(8)])  20.2 us
    ppermute x5, waiting for transfers between devices, move(): return lax.ppermute(value, both, pairs)  18.1 us
    ppermute x4, starting transfers between devices, swap(): return lax.ppermute(value, 'seq', [(s, s ^ mask) for s in range(8)])  8.38 us
    ppermute x3, starting transfers between devices, pairs_body(): earlier.append(lax.ppermute(onward.astype(BF16), 'seq', pairs))  4.47 us
    unnamed x12, local copies, waits for them, and re-layouts  4.18 us
    ppermute x3, waiting for transfers between devices, pairs_body(): earlier.append(lax.ppermute(onward.astype(BF16), 'seq', pairs))  4.02 us
    pallas_call x2, Pallas kernels, projected(): pl.pallas_call(project_pair_kernel, out_shape=(tile, tile), in_specs=[pl....  2.57 us
  transfers between devices with their start and end apart: 12, of which 8 were waited for; matrix products, arithmetic and copies ran while one was open for 0% of the time, Pallas kernels for 5%

profile of v16, /device:TPU:1, one launch (start us, length us, event | category | flops | bytes accessed | tf_op | source)
XLA Modules:
  0.0 94.5 jit_solution(3200095161311639197)
XLA Ops:
  0.0 0.0 copy-start
  0.0 1.0 %copy-done = bf16[256,1024]{1,0:T(8,128)(2,1)S(1)} copy-done((bf16[256,1024]{1,0:T(8,128)(2,1)S(1)}, bf16[256,1024]{1,0:T(8,128)(2,1)}, u32[]{:S(2)}) %copy-start) | copy-done | bytes 524312
  1.0 0.0 copy-start.2
  1.0 1.0 %copy-done.2 = bf16[256,1024]{1,0:T(8,128)(2,1)S(1)} copy-done((bf16[256,1024]{1,0:T(8,128)(2,1)S(1)}, bf16[256,1024]{1,0:T(8,128)(2,1)}, u32[]{:S(2)}) %copy-start.2) | copy-done | bytes 524312
  2.1 0.4 shard_map.55
  2.4 2.1 %collective-permute-start = (bf16[8,128,128]{2,1,0:T(8,128)(2,1)S(1)}, bf16[8,128,128]{2,1,0:T(8,128)(2,1)S(1)}, u32[]{:S(2)}, u32[]{:S(2)}) collective-permute-start(bf16[8,128,128]{2,1,0:T(8,128)(2,1)S(1)} %get-tuple-element.14), channel_id=1, source_target_pairs={{0,4},{4,0},{8,12},{12,8},{16,20},{20,16},{24,28},{28,24},{1,5},{5... | collective-permute-start | bytes 786440 | tf_op jit(solution)/shard_map/ppermute | solution.py:243
  4.6 0.0 copy-start.1
  4.6 1.0 %copy-done.1 = bf16[256,1024]{1,0:T(8,128)(2,1)S(1)} copy-done((bf16[256,1024]{1,0:T(8,128)(2,1)S(1)}, bf16[256,1024]{1,0:T(8,128)(2,1)}, u32[]{:S(2)}) %copy-start.1) | copy-done | bytes 524312
  5.6 0.0 copy-start.3
  5.6 1.0 %copy-done.3 = bf16[256,1024]{1,0:T(8,128)(2,1)S(1)} copy-done((bf16[256,1024]{1,0:T(8,128)(2,1)S(1)}, bf16[256,1024]{1,0:T(8,128)(2,1)}, u32[]{:S(2)}) %copy-start.3) | copy-done | bytes 524312
  6.7 0.9 shard_map.56.within_ref
  7.6 0.0 copy-start.4
  7.6 0.0 copy-start.5
  7.6 3.0 %collective-permute-done.mate_ref = bf16[8,128,128]{2,1,0:T(8,128)(2,1)S(1)} collective-permute-done((bf16[8,128,128]{2,1,0:T(8,128)(2,1)S(1)}, bf16[8,128,128]{2,1,0:T(8,128)(2,1)S(1)}, u32[]{:S(2)}, u32[]{:S(2)}) %collective-permute-start) | collective-permute-done | bytes 262176 | tf_op jit(solution)/shard_map/ppermute | solution.py:243
  10.6 0.1 fusion
  10.7 3.1 %collective-permute-start.1 = (bf16[8,128,128]{2,1,0:T(8,128)(2,1)S(1)}, bf16[8,128,128]{2,1,0:T(8,128)(2,1)S(1)}, u32[]{:S(2)}, u32[]{:S(2)}) collective-permute-start(bf16[8,128,128]{2,1,0:T(8,128)(2,1)S(1)} %fusion), channel_id=1, source_target_pairs={{0,8},{4,12},{1,9},{5,13},{2,10},{6,14},{3,11},{7,15}} | collective-permute-start | bytes 786440 | tf_op jit(solution)/shard_map/ppermute | solution.py:269
  13.8 4.0 %collective-permute-done.1.refs_0_ = bf16[8,128,128]{2,1,0:T(8,128)(2,1)S(1)} collective-permute-done((bf16[8,128,128]{2,1,0:T(8,128)(2,1)S(1)}, bf16[8,128,128]{2,1,0:T(8,128)(2,1)S(1)}, u32[]{:S(2)}, u32[]{:S(2)}) %collective-permute-start.1) | collective-permute-done | bytes 262176 | tf_op jit(solution)/shard_map/ppermute | solution.py:269
  17.8 0.1 fusion.1
  17.9 0.7 collective-permute-start.2
  18.6 1.3 %collective-permute-start.7 = (bf16[1024,512]{1,0:T(8,128)(2,1)}, bf16[1024,512]{1,0:T(8,128)(2,1)}, u32[]{:S(2)}, u32[]{:S(2)}) collective-permute-start(bf16[1024,512]{1,0:T(8,128)(2,1)} %own_ref.1), channel_id=1, source_target_pairs={{0,4},{4,0},{8,12},{12,8},{16,20},{20,16},{24,28},{28,24},{1,5},{5... | collective-permute-start | bytes 3145736 | tf_op jit(solution)/shard_map/ppermute | solution.py:243
  19.9 0.0 collective-permute-done.2.refs_1_
  19.9 0.1 add_convert_fusion.2
  20.0 0.7 collective-permute-start.3
  20.7 0.0 collective-permute-done.3.refs_2_
  20.7 0.0 copy-done.4
  20.7 0.0 copy-done.5
  20.8 0.8 shard_map.57
  21.5 4.9 %collective-permute-start.4 = (bf16[256,1024]{1,0:T(8,128)(2,1)S(1)}, bf16[256,1024]{1,0:T(8,128)(2,1)S(1)}, u32[]{:S(2)}, u32[]{:S(2)}) collective-permute-start(bf16[256,1024]{1,0:T(8,128)(2,1)S(1)} %shard_map.57), channel_id=1, source_target_pairs={{0,8},{4,12},{8,0},{12,4},{16,24},{20,28},{24,16},{28,20},{1,9},{5... | collective-permute-start | bytes 1572872 | tf_op jit(solution)/shard_map/ppermute | solution.py:243
  26.4 8.3 %collective-permute-start.5 = (bf16[256,1024]{1,0:T(8,128)(2,1)S(1)}, bf16[256,1024]{1,0:T(8,128)(2,1)S(1)}, u32[]{:S(2)}, u32[]{:S(2)}) collective-permute-start(bf16[256,1024]{1,0:T(8,128)(2,1)S(1)} %shard_map.57), channel_id=1, source_target_pairs={{0,16},{1,17},{2,26},{3,27},{4,20},{5,21},{6,30},{7,31},{8,24},{9,... | collective-permute-start | bytes 1572872 | tf_op jit(solution)/shard_map/ppermute | solution.py:247
  34.7 6.5 %collective-permute-done.7.mate_ref = bf16[1024,512]{1,0:T(8,128)(2,1)} collective-permute-done((bf16[1024,512]{1,0:T(8,128)(2,1)}, bf16[1024,512]{1,0:T(8,128)(2,1)}, u32[]{:S(2)}, u32[]{:S(2)}) %collective-permute-start.7) | collective-permute-done | bytes 1048608 | tf_op jit(solution)/shard_map/ppermute | solution.py:243
  41.2 1.7 %shard_map.58.weight_ref = bf16[2,1024,512]{2,1,0:T(8,128)(2,1)S(1)} custom-call(bf16[1024,512]{1,0:T(8,128)(2,1)} %own_ref.1, bf16[1024,512]{1,0:T(8,128)(2,1)} %collective-permute-done.7.mate_ref), custom_call_target="tpu_custom_call" | custom-call | bytes 4194304 | tf_op jit(solution)/shard_map/pallas_call | solution.py:274
  42.8 0.0 collective-permute-done.4
  42.9 0.1 broadcast_select_fusion.1
  42.9 3.6 %collective-permute-done.5.heavy_ref = bf16[256,1024]{1,0:T(8,128)(2,1)S(1)} collective-permute-done((bf16[256,1024]{1,0:T(8,128)(2,1)S(1)}, bf16[256,1024]{1,0:T(8,128)(2,1)S(1)}, u32[]{:S(2)}, u32[]{:S(2)}) %collective-permute-start.5) | collective-permute-done | bytes 524320 | tf_op jit(solution)/shard_map/ppermute | solution.py:247
  46.5 1.3 %shard_map.60 = (bf16[2,256,512]{2,1,0:T(8,128)(2,1)S(1)}, bf16[2,256,512]{2,1,0:T(8,128)(2,1)S(1)}) custom-call(s32[1]{0:T(128)} %bitcast.core_ref, bf16[256,1024]{1,0:T(8,128)(2,1)S(1)} %get-tuple-element.24.light_ref, bf16[256,1024]{1,0:T(8,128)(2,1)S(1)} %collective-permute-done.5.heavy_ref, bf16[2,1024,512]{2,1,0:T(8,128)(2,1)S(1)} %shard_map.58.weight_ref), custom_call_target="tpu_custom_call" | custom-call | flops 1073741824 | bytes 4194304 | tf_op jit(solution)/shard_map/pallas_call | solution.py:287
  47.8 12.4 %collective-permute-start.9 = (bf16[2,256,512]{2,1,0:T(8,128)(2,1)S(1)}, bf16[2,256,512]{2,1,0:T(8,128)(2,1)S(1)}, u32[]{:S(2)}, u32[]{:S(2)}) collective-permute-start(bf16[2,256,512]{2,1,0:T(8,128)(2,1)S(1)} %get-tuple-element.22), channel_id=1, source_target_pairs={{0,1},{1,0},{2,3},{3,2},{4,5},{5,4},{6,7},{7,6},{8,9},{9,8},{10,11... | collective-permute-start | bytes 1572872 | tf_op jit(solution)/shard_map/ppermute | solution.py:247
  60.2 0.1 collective-permute-start.6
  60.3 1.5 %collective-permute-done.9 = bf16[2,256,512]{2,1,0:T(8,128)(2,1)S(1)} collective-permute-done((bf16[2,256,512]{2,1,0:T(8,128)(2,1)S(1)}, bf16[2,256,512]{2,1,0:T(8,128)(2,1)S(1)}, u32[]{:S(2)}, u32[]{:S(2)}) %collective-permute-start.9) | collective-permute-done | bytes 524320 | tf_op jit(solution)/shard_map/ppermute | solution.py:247
  61.7 0.1 add_convert_fusion.1
  61.9 1.1 %collective-permute-start.10 = (bf16[2,256,512]{2,1,0:T(8,128)(2,1)S(1)}, bf16[2,256,512]{2,1,0:T(8,128)(2,1)S(1)}, u32[]{:S(2)}, u32[]{:S(2)}) collective-permute-start(bf16[2,256,512]{2,1,0:T(8,128)(2,1)S(1)} %add_convert_fusion.1), channel_id=1, source_target_pairs={{0,2},{1,3},{2,0},{3,1},{4,6},{5,7},{6,4},{7,5},{8,10},{9,11},{10,... | collective-permute-start | bytes 1572872 | tf_op jit(solution)/shard_map/ppermute | solution.py:247
  62.9 10.8 %collective-permute-done.6.heavy_ref = bf16[256,1024]{1,0:T(8,128)(2,1)S(1)} collective-permute-done((bf16[256,1024]{1,0:T(8,128)(2,1)S(1)}, bf16[256,1024]{1,0:T(8,128)(2,1)S(1)}, u32[]{:S(2)}, u32[]{:S(2)}) %collective-permute-start.6) | collective-permute-done | bytes 524320 | tf_op jit(solution)/shard_map/ppermute | solution.py:243
  73.7 1.3 %shard_map.59 = (bf16[2,256,512]{2,1,0:T(8,128)(2,1)S(1)}, bf16[2,256,512]{2,1,0:T(8,128)(2,1)S(1)}) custom-call(s32[1]{0:T(128)} %bitcast.core_ref, bf16[256,1024]{1,0:T(8,128)(2,1)S(1)} %get-tuple-element.23.light_ref, bf16[256,1024]{1,0:T(8,128)(2,1)S(1)} %collective-permute-done.6.heavy_ref, bf16[2,1024,512]{2,1,0:T(8,128)(2,1)S(1)} %shard_map.58.weight_ref), custom_call_target="tpu_custom_call" | custom-call | flops 1073741824 | bytes 4194304 | tf_op jit(solution)/shard_map/pallas_call | solution.py:287
  75.0 0.9 collective-permute-start.8
  75.9 0.0 collective-permute-done.10
  75.9 1.5 %collective-permute-done.8 = bf16[2,256,512]{2,1,0:T(8,128)(2,1)S(1)} collective-permute-done((bf16[2,256,512]{2,1,0:T(8,128)(2,1)S(1)}, bf16[2,256,512]{2,1,0:T(8,128)(2,1)S(1)}, u32[]{:S(2)}, u32[]{:S(2)}) %collective-permute-start.8) | collective-permute-done | bytes 524320 | tf_op jit(solution)/shard_map/ppermute | solution.py:247
  77.5 0.2 add_convert_fusion
  77.7 4.3 %collective-permute-start.11 = (bf16[2,256,512]{2,1,0:T(8,128)(2,1)S(1)}, bf16[2,256,512]{2,1,0:T(8,128)(2,1)S(1)}, u32[]{:S(2)}, u32[]{:S(2)}) collective-permute-start(bf16[2,256,512]{2,1,0:T(8,128)(2,1)S(1)} %add_convert_fusion), channel_id=1, source_target_pairs={{0,0},{1,24},{2,8},{3,16},{4,4},{5,28},{6,12},{7,20},{8,9},{9,17},... | collective-permute-start | bytes 1572872 | tf_op jit(solution)/shard_map/ppermute | solution.py:247
  82.0 11.5 %collective-permute-done.11 = bf16[2,256,512]{2,1,0:T(8,128)(2,1)S(1)} collective-permute-done((bf16[2,256,512]{2,1,0:T(8,128)(2,1)S(1)}, bf16[2,256,512]{2,1,0:T(8,128)(2,1)S(1)}, u32[]{:S(2)}, u32[]{:S(2)}) %collective-permute-start.11) | collective-permute-done | bytes 524320 | tf_op jit(solution)/shard_map/ppermute | solution.py:247
  93.6 0.9 pad_maximum_fusion
  (1 shorter events, 0.0 us)
Async XLA Ops:
  0.0 1.0 %copy-start = (bf16[256,1024]{1,0:T(8,128)(2,1)S(1)}, bf16[256,1024]{1,0:T(8,128)(2,1)}, u32[]{:S(2)}) copy-start(bf16[256,1024]{1,0:T(8,128)(2,1)} %k_ref.3) | copy-start | bytes 1572868
  1.0 1.0 %copy-start.2 = (bf16[256,1024]{1,0:T(8,128)(2,1)S(1)}, bf16[256,1024]{1,0:T(8,128)(2,1)}, u32[]{:S(2)}) copy-start(bf16[256,1024]{1,0:T(8,128)(2,1)} %v_ref.3) | copy-start | bytes 1572868
  2.4 8.2 %collective-permute-start = (bf16[8,128,128]{2,1,0:T(8,128)(2,1)S(1)}, bf16[8,128,128]{2,1,0:T(8,128)(2,1)S(1)}, u32[]{:S(2)}, u32[]{:S(2)}) collective-permute-start(bf16[8,128,128]{2,1,0:T(8,128)(2,1)S(1)} %get-tuple-element.14), channel_id=1, source_target_pairs={{0,4},{4,0},{8,12},{12,8},{16,20},{20,16},{24,28},{28,24},{1,5},{5... | collective-permute-start | bytes 786440 | tf_op jit(solution)/shard_map/ppermute | solution.py:243
  4.6 1.0 %copy-start.1 = (bf16[256,1024]{1,0:T(8,128)(2,1)S(1)}, bf16[256,1024]{1,0:T(8,128)(2,1)}, u32[]{:S(2)}) copy-start(bf16[256,1024]{1,0:T(8,128)(2,1)} %k_ref.3) | copy-start | bytes 1572868
  5.6 1.0 %copy-start.3 = (bf16[256,1024]{1,0:T(8,128)(2,1)S(1)}, bf16[256,1024]{1,0:T(8,128)(2,1)}, u32[]{:S(2)}) copy-start(bf16[256,1024]{1,0:T(8,128)(2,1)} %q_ref.3) | copy-start | bytes 1572868
  7.6 13.1 %copy-start.4 = (bf16[256,1024]{1,0:T(8,128)(2,1)S(1)}, bf16[256,1024]{1,0:T(8,128)(2,1)}, u32[]{:S(2)}) copy-start(bf16[256,1024]{1,0:T(8,128)(2,1)} %q_ref.3) | copy-start | bytes 1572868
  7.6 13.1 %copy-start.5 = (f32[1024]{0:T(1024)S(1)}, f32[1024]{0:T(1024)}, u32[]{:S(2)}) copy-start(f32[1024]{0:T(1024)} %param.8) | copy-start | bytes 12292
  10.7 7.1 %collective-permute-start.1 = (bf16[8,128,128]{2,1,0:T(8,128)(2,1)S(1)}, bf16[8,128,128]{2,1,0:T(8,128)(2,1)S(1)}, u32[]{:S(2)}, u32[]{:S(2)}) collective-permute-start(bf16[8,128,128]{2,1,0:T(8,128)(2,1)S(1)} %fusion), channel_id=1, source_target_pairs={{0,8},{4,12},{1,9},{5,13},{2,10},{6,14},{3,11},{7,15}} | collective-permute-start | bytes 786440 | tf_op jit(solution)/shard_map/ppermute | solution.py:269
  17.9 2.0 %collective-permute-start.2 = (bf16[8,128,128]{2,1,0:T(8,128)(2,1)S(1)}, bf16[8,128,128]{2,1,0:T(8,128)(2,1)S(1)}, u32[]{:S(2)}, u32[]{:S(2)}) collective-permute-start(bf16[8,128,128]{2,1,0:T(8,128)(2,1)S(1)} %fusion.1), channel_id=1, source_target_pairs={{8,16},{12,20},{9,17},{13,21},{10,18},{14,22},{11,19},{15,23}} | collective-permute-start | bytes 786440 | tf_op jit(solution)/shard_map/ppermute | solution.py:269
  18.6 22.6 %collective-permute-start.7 = (bf16[1024,512]{1,0:T(8,128)(2,1)}, bf16[1024,512]{1,0:T(8,128)(2,1)}, u32[]{:S(2)}, u32[]{:S(2)}) collective-permute-start(bf16[1024,512]{1,0:T(8,128)(2,1)} %own_ref.1), channel_id=1, source_target_pairs={{0,4},{4,0},{8,12},{12,8},{16,20},{20,16},{24,28},{28,24},{1,5},{5... | collective-permute-start | bytes 3145736 | tf_op jit(solution)/shard_map/ppermute | solution.py:243
  20.0 0.7 collective-permute-start.3
  21.5 21.3 %collective-permute-start.4 = (bf16[256,1024]{1,0:T(8,128)(2,1)S(1)}, bf16[256,1024]{1,0:T(8,128)(2,1)S(1)}, u32[]{:S(2)}, u32[]{:S(2)}) collective-permute-start(bf16[256,1024]{1,0:T(8,128)(2,1)S(1)} %shard_map.57), channel_id=1, source_target_pairs={{0,8},{4,12},{8,0},{12,4},{16,24},{20,28},{24,16},{28,20},{1,9},{5... | collective-permute-start | bytes 1572872 | tf_op jit(solution)/shard_map/ppermute | solution.py:243
  26.4 20.1 %collective-permute-start.5 = (bf16[256,1024]{1,0:T(8,128)(2,1)S(1)}, bf16[256,1024]{1,0:T(8,128)(2,1)S(1)}, u32[]{:S(2)}, u32[]{:S(2)}) collective-permute-start(bf16[256,1024]{1,0:T(8,128)(2,1)S(1)} %shard_map.57), channel_id=1, source_target_pairs={{0,16},{1,17},{2,26},{3,27},{4,20},{5,21},{6,30},{7,31},{8,24},{9,... | collective-permute-start | bytes 1572872 | tf_op jit(solution)/shard_map/ppermute | solution.py:247
  47.8 13.9 %collective-permute-start.9 = (bf16[2,256,512]{2,1,0:T(8,128)(2,1)S(1)}, bf16[2,256,512]{2,1,0:T(8,128)(2,1)S(1)}, u32[]{:S(2)}, u32[]{:S(2)}) collective-permute-start(bf16[2,256,512]{2,1,0:T(8,128)(2,1)S(1)} %get-tuple-element.22), channel_id=1, source_target_pairs={{0,1},{1,0},{2,3},{3,2},{4,5},{5,4},{6,7},{7,6},{8,9},{9,8},{10,11... | collective-permute-start | bytes 1572872 | tf_op jit(solution)/shard_map/ppermute | solution.py:247
  60.2 13.5 %collective-permute-start.6 = (bf16[256,1024]{1,0:T(8,128)(2,1)S(1)}, bf16[256,1024]{1,0:T(8,128)(2,1)S(1)}, u32[]{:S(2)}, u32[]{:S(2)}) collective-permute-start(bf16[256,1024]{1,0:T(8,128)(2,1)S(1)} %collective-permute-done.5.heavy_ref), channel_id=1, source_target_pairs={{0,8},{4,12},{8,0},{12,4},{16,24},{20,28},{24,16},{28,20},{1,9},{5... | collective-permute-start | bytes 1572872 | tf_op jit(solution)/shard_map/ppermute | solution.py:243
  61.9 14.1 %collective-permute-start.10 = (bf16[2,256,512]{2,1,0:T(8,128)(2,1)S(1)}, bf16[2,256,512]{2,1,0:T(8,128)(2,1)S(1)}, u32[]{:S(2)}, u32[]{:S(2)}) collective-permute-start(bf16[2,256,512]{2,1,0:T(8,128)(2,1)S(1)} %add_convert_fusion.1), channel_id=1, source_target_pairs={{0,2},{1,3},{2,0},{3,1},{4,6},{5,7},{6,4},{7,5},{8,10},{9,11},{10,... | collective-permute-start | bytes 1572872 | tf_op jit(solution)/shard_map/ppermute | solution.py:247
  75.0 2.5 %collective-permute-start.8 = (bf16[2,256,512]{2,1,0:T(8,128)(2,1)S(1)}, bf16[2,256,512]{2,1,0:T(8,128)(2,1)S(1)}, u32[]{:S(2)}, u32[]{:S(2)}) collective-permute-start(bf16[2,256,512]{2,1,0:T(8,128)(2,1)S(1)} %get-tuple-element.20), channel_id=1, source_target_pairs={{0,1},{1,0},{2,3},{3,2},{4,5},{5,4},{6,7},{7,6},{8,9},{9,8},{10,11... | collective-permute-start | bytes 1572872 | tf_op jit(solution)/shard_map/ppermute | solution.py:247
  77.7 15.9 %collective-permute-start.11 = (bf16[2,256,512]{2,1,0:T(8,128)(2,1)S(1)}, bf16[2,256,512]{2,1,0:T(8,128)(2,1)S(1)}, u32[]{:S(2)}, u32[]{:S(2)}) collective-permute-start(bf16[2,256,512]{2,1,0:T(8,128)(2,1)S(1)} %add_convert_fusion), channel_id=1, source_target_pairs={{0,0},{1,24},{2,8},{3,16},{4,4},{5,28},{6,12},{7,20},{8,9},{9,17},... | collective-permute-start | bytes 1572872 | tf_op jit(solution)/shard_map/ppermute | solution.py:247

commit v17 on v16

--- a/solution.py
+++ b/solution.py
@@ -205,25 +205,42 @@
     out_ref[1] = mate_ref[...]
 
 
+def multiply(tokens, weight_ref, out_ref):
+    for half in range(2):
+        product = jnp.dot(tokens, weight_ref[half], preferred_element_type=F32)
+        out_ref[half] = product.astype(BF16)
+
+
 def project_kernel(tokens_ref, weight_ref, out_ref):
-    for half in range(2):
-        product = jnp.dot(tokens_ref[...], weight_ref[half], preferred_element_type=F32)
-        out_ref[half] = product.astype(BF16)
-
-
-def project_pair_kernel(core_ref, light_ref, heavy_ref, weight_ref, keep_ref, send_ref):
-    def multiply(out_ref, tokens_ref):
-        project_kernel(tokens_ref, weight_ref, out_ref)
-
-    @pl.when(core_ref[0] == 0)
+    multiply(tokens_ref[...], weight_ref, out_ref)
+
+
+def project_light_kernel(place_ref, first_ref, second_ref, heavy_ref, weight_ref, keep_ref, send_ref):
+    light = jnp.where(place_ref[1] == 1, first_ref[...], second_ref[...])
+
+    @pl.when(place_ref[0] == 0)
     def _():
-        multiply(send_ref, heavy_ref)
-        multiply(keep_ref, light_ref)
-
-    @pl.when(core_ref[0] != 0)
+        multiply(light, weight_ref, keep_ref)
+        send_ref[...] = heavy_ref[...]
+
+    @pl.when(place_ref[0] != 0)
     def _():
-        multiply(send_ref, light_ref)
-        multiply(keep_ref, heavy_ref)
+        multiply(light, weight_ref, send_ref)
+        keep_ref[...] = heavy_ref[...]
+
+
+def project_pair_kernel(place_ref, first_ref, second_ref, heavy_ref, weight_ref, keep_ref, send_ref):
+    light = jnp.where(place_ref[1] == 1, first_ref[...], second_ref[...])
+
+    @pl.when(place_ref[0] == 0)
+    def _():
+        multiply(heavy_ref[...], weight_ref, send_ref)
+        multiply(light, weight_ref, keep_ref)
+
+    @pl.when(place_ref[0] != 0)
+    def _():
+        multiply(light, weight_ref, send_ref)
+        multiply(heavy_ref[...], weight_ref, keep_ref)
 
 
 def pairs_body(queries, key_vectors, value_vectors, norm_gain, out_weight):
@@ -283,22 +300,24 @@
     flops, moved = 4 * size * half_cols, 8 * size
     vmem = pl.BlockSpec(memory_space=pltpu.VMEM)
 
-    def projected(light, heavy):
+    def projected(kernel, own, heavy):
         keep, send = pl.pallas_call(
-            project_pair_kernel,
+            kernel,
             out_shape=(tile, tile),
-            in_specs=[pl.BlockSpec(memory_space=pltpu.SMEM)] + [vmem] * 3,
+            in_specs=[pl.BlockSpec(memory_space=pltpu.SMEM)] + [vmem] * 4,
             out_specs=(vmem, vmem),
             compiler_params=pltpu.CompilerParams(vmem_limit_bytes=24 * 1024 * 1024),
             cost_estimate=pl.CostEstimate(
                 flops=2 * flops, bytes_accessed=2 * moved, transcendentals=0
             ),
-        )(core.astype(jnp.int32)[None], light, heavy, weight)
+        )(jnp.stack([core, own.astype(core.dtype)]).astype(jnp.int32), attended, beside, heavy, weight)
         return keep.astype(F32) + move(send, lambda z, y, x, c: (z, y, x, 1 - c)).astype(F32)
 
-    far = projected(jnp.where(x == 0, beside, attended), straight).astype(BF16)
+    product = call(project_kernel, tile, flops, moved)(straight, weight)
+    product, beside = lax.optimization_barrier((product, beside))
+    far = projected(project_light_kernel, x == 1, product).astype(BF16)
     crossed = move(far, lambda z, y, x, c: (z, y, 1 - x, c))
-    near = projected(jnp.where(x == 0, attended, beside), onward) + crossed.astype(F32)
+    near = projected(project_pair_kernel, x == 0, onward) + crossed.astype(F32)
     result = move(near.astype(BF16), lambda z, y, x, c: (z ^ 3 * c ^ x, y, z // 2, z % 2))
     first = jnp.where(y == 0, result[0], result[1])
     return jnp.concatenate([first, jnp.where(y == 0, result[1], result[0])], axis=1)

time: 94.8 us -> 102 us (1.076)
  starting transfers between devices: 39.8 us -> 31.9 us
  waiting for transfers between devices: 42.4 us -> 49.3 us
  Pallas kernels: 6.28 us -> 12.2 us
  other arithmetic: 1.6 us -> 3.41 us
    ppermute x5, waiting for transfers between devices: 18.1 us -> 29.4 us  [move(): return lax.ppermute(value, both, pairs)]
    ppermute x5, starting transfers between devices: 27 us -> 20.7 us  [move(): return lax.ppermute(value, both, pairs)]
    pallas_call x2 -> x3, Pallas kernels: 2.57 us -> 7.04 us  [the longest x2 5.3 us: projected(): pl.pallas_call(kernel, out_shape=(tile, tile), in_specs=[pl.BlockSpec(mem...]
    ppermute x4, waiting for transfers between devices: 20.2 us -> 15.9 us  [swap(): return lax.ppermute(value, 'seq', [(s, s ^ mask) for s in range(8)])]
    ppermute x4, starting transfers between devices: 8.38 us -> 6.01 us  [swap(): return lax.ppermute(value, 'seq', [(s, s ^ mask) for s in range(8)])]
    pallas_call x1, Pallas kernels: 0.75 us -> 2.5 us  [attend(): pl.pallas_call(attend_kernel, out_shape=jax.ShapeDtypeStruct((rows, featu...]
    convert_element_type x1, other arithmetic: 0.14 us -> 1.17 us  [pairs_body(): far = projected(project_light_kernel, x == 1, product).astype(BF16)]
    unnamed x12 -> x14, local copies, waits for them, and re-layouts: 4.18 us -> 4.18 us
  transfers between devices with their start and end apart: 12 -> 12, of which waited for: 8 -> 8; matrix products, arithmetic and copies ran while one was open for 0% -> 2% of each run, Pallas kernels for 5% -> 9%
where the time goes in v17:
time: 102 us; the launch traced here: 101 us
  waiting for transfers between devices  49.3 us (48%)
  starting transfers between devices  31.9 us (31%)
  Pallas kernels  12.2 us (12%)
  local copies, waits for them, and re-layouts  4.18 us (4%)
  other arithmetic  3.41 us (3%)
    ppermute x5, waiting for transfers between devices, move(): return lax.ppermute(value, both, pairs)  29.4 us
    ppermute x5, starting transfers between devices, move(): return lax.ppermute(value, both, pairs)  20.7 us
    ppermute x4, waiting for transfers between devices, swap(): return lax.ppermute(value, 'seq', [(s, s ^ mask) for s in range(8)])  15.9 us
    ppermute x4, starting transfers between devices, swap(): return lax.ppermute(value, 'seq', [(s, s ^ mask) for s in range(8)])  6.01 us
    pallas_call x2, Pallas kernels, projected(): pl.pallas_call(kernel, out_shape=(tile, tile), in_specs=[pl.BlockSpec(mem...  5.3 us
    ppermute x3, starting transfers between devices, pairs_body(): earlier.append(lax.ppermute(onward.astype(BF16), 'seq', pairs))  5.15 us
    unnamed x14, local copies, waits for them, and re-layouts  4.18 us
    ppermute x3, waiting for transfers between devices, pairs_body(): earlier.append(lax.ppermute(onward.astype(BF16), 'seq', pairs))  4.02 us
  transfers between devices with their start and end apart: 12, of which 8 were waited for; matrix products, arithmetic and copies ran while one was open for 2% of the time, Pallas kernels for 9%

profile of v17, /device:TPU:1, one launch (start us, length us, event | category | flops | bytes accessed | tf_op | source)
XLA Modules:
  0.0 101.1 jit_solution(10458928553066956018)
XLA Ops:
  0.0 0.0 copy-start
  0.0 1.0 %copy-done = bf16[256,1024]{1,0:T(8,128)(2,1)S(1)} copy-done((bf16[256,1024]{1,0:T(8,128)(2,1)S(1)}, bf16[256,1024]{1,0:T(8,128)(2,1)}, u32[]{:S(2)}) %copy-start) | copy-done | bytes 524312
  1.0 0.0 copy-start.2
  1.0 1.0 %copy-done.2 = bf16[256,1024]{1,0:T(8,128)(2,1)S(1)} copy-done((bf16[256,1024]{1,0:T(8,128)(2,1)S(1)}, bf16[256,1024]{1,0:T(8,128)(2,1)}, u32[]{:S(2)}) %copy-start.2) | copy-done | bytes 524312
  2.1 0.4 shard_map.55
  2.4 2.1 %collective-permute-start = (bf16[8,128,128]{2,1,0:T(8,128)(2,1)S(1)}, bf16[8,128,128]{2,1,0:T(8,128)(2,1)S(1)}, u32[]{:S(2)}, u32[]{:S(2)}) collective-permute-start(bf16[8,128,128]{2,1,0:T(8,128)(2,1)S(1)} %get-tuple-element.16), channel_id=1, source_target_pairs={{0,4},{4,0},{8,12},{12,8},{16,20},{20,16},{24,28},{28,24},{1,5},{5... | collective-permute-start | bytes 786440 | tf_op jit(solution)/shard_map/ppermute | solution.py:260
  4.6 0.0 copy-start.1
  4.6 1.0 %copy-done.1 = bf16[256,1024]{1,0:T(8,128)(2,1)S(1)} copy-done((bf16[256,1024]{1,0:T(8,128)(2,1)S(1)}, bf16[256,1024]{1,0:T(8,128)(2,1)}, u32[]{:S(2)}) %copy-start.1) | copy-done | bytes 524312
  5.6 0.0 copy-start.3
  5.6 1.0 %copy-done.3 = bf16[256,1024]{1,0:T(8,128)(2,1)S(1)} copy-done((bf16[256,1024]{1,0:T(8,128)(2,1)S(1)}, bf16[256,1024]{1,0:T(8,128)(2,1)}, u32[]{:S(2)}) %copy-start.3) | copy-done | bytes 524312
  6.7 0.0 copy-start.5
  6.7 0.9 shard_map.56.within_ref
  7.6 0.0 copy-start.4
  7.6 0.0 copy-start.6
  7.6 3.0 %collective-permute-done.mate_ref = bf16[8,128,128]{2,1,0:T(8,128)(2,1)S(1)} collective-permute-done((bf16[8,128,128]{2,1,0:T(8,128)(2,1)S(1)}, bf16[8,128,128]{2,1,0:T(8,128)(2,1)S(1)}, u32[]{:S(2)}, u32[]{:S(2)}) %collective-permute-start) | collective-permute-done | bytes 262176 | tf_op jit(solution)/shard_map/ppermute | solution.py:260
  10.6 0.1 fusion
  10.7 3.1 %collective-permute-start.1 = (bf16[8,128,128]{2,1,0:T(8,128)(2,1)S(1)}, bf16[8,128,128]{2,1,0:T(8,128)(2,1)S(1)}, u32[]{:S(2)}, u32[]{:S(2)}) collective-permute-start(bf16[8,128,128]{2,1,0:T(8,128)(2,1)S(1)} %fusion), channel_id=1, source_target_pairs={{0,8},{4,12},{1,9},{5,13},{2,10},{6,14},{3,11},{7,15}} | collective-permute-start | bytes 786440 | tf_op jit(solution)/shard_map/ppermute | solution.py:286
  13.8 4.0 %collective-permute-done.1.refs_0_ = bf16[8,128,128]{2,1,0:T(8,128)(2,1)S(1)} collective-permute-done((bf16[8,128,128]{2,1,0:T(8,128)(2,1)S(1)}, bf16[8,128,128]{2,1,0:T(8,128)(2,1)S(1)}, u32[]{:S(2)}, u32[]{:S(2)}) %collective-permute-start.1) | collective-permute-done | bytes 262176 | tf_op jit(solution)/shard_map/ppermute | solution.py:286
  17.8 0.1 fusion.1
  17.9 0.7 collective-permute-start.2
  18.6 0.0 copy-done.5
  18.6 1.3 %collective-permute-start.5 = (bf16[1024,512]{1,0:T(8,128)(2,1)S(1)}, bf16[1024,512]{1,0:T(8,128)(2,1)}, u32[]{:S(2)}, u32[]{:S(2)}) collective-permute-start(bf16[1024,512]{1,0:T(8,128)(2,1)S(1)} %copy-done.5), channel_id=1, source_target_pairs={{0,4},{4,0},{8,12},{12,8},{16,20},{20,16},{24,28},{28,24},{1,5},{5... | collective-permute-start | bytes 3145736 | tf_op jit(solution)/shard_map/ppermute | solution.py:260
  19.9 0.0 collective-permute-done.2.refs_1_
  19.9 0.8 add_convert_fusion.2
  20.7 1.4 %collective-permute-start.3 = (bf16[8,128,128]{2,1,0:T(8,128)(2,1)}, bf16[8,128,128]{2,1,0:T(8,128)(2,1)}, u32[]{:S(2)}, u32[]{:S(2)}) collective-permute-start(bf16[8,128,128]{2,1,0:T(8,128)(2,1)} %add_convert_fusion.2), channel_id=1, source_target_pairs={{16,24},{20,28},{17,25},{21,29},{18,26},{22,30},{19,27},{23,31}} | collective-permute-start | bytes 786440 | tf_op jit(solution)/shard_map/ppermute | solution.py:286
  22.1 0.0 collective-permute-done.3.refs_2_
  22.1 0.0 copy-done.4
  22.1 0.0 copy-done.6
  22.1 2.5 %shard_map.57.first_ref = bf16[256,1024]{1,0:T(8,128)(2,1)} custom-call(s32[1]{0:T(128)} %bitcast.2.second_ref, bf16[256,1024]{1,0:T(8,128)(2,1)S(1)} %copy-done.4, f32[256,1024]{1,0:T(8,128)S(1)} %shard_map.56.within_ref, f32[1,1024]{1,0:T(1,128)S(1)} %bitcast.9, bf16[8,128,128]{2,1,0:T(8,128)(2,1)S(1)} %collective-permute-done.mate_ref, ...), custom_call_target="tpu_custom_call" | custom-call | flops 67108864 | bytes 2097152 | tf_op jit(solution)/shard_map/pallas_call | solution.py:105
  24.6 10.5 %collective-permute-start.4 = (bf16[256,1024]{1,0:T(8,128)(2,1)}, bf16[256,1024]{1,0:T(8,128)(2,1)}, u32[]{:S(2)}, u32[]{:S(2)}) collective-permute-start(bf16[256,1024]{1,0:T(8,128)(2,1)} %shard_map.57.first_ref), channel_id=1, source_target_pairs={{0,16},{1,17},{2,26},{3,27},{4,20},{5,21},{6,30},{7,31},{8,24},{9,... | collective-permute-start | bytes 1572872 | tf_op jit(solution)/shard_map/ppermute | solution.py:264
  35.1 2.2 %collective-permute-start.6 = (bf16[256,1024]{1,0:T(8,128)(2,1)}, bf16[256,1024]{1,0:T(8,128)(2,1)}, u32[]{:S(2)}, u32[]{:S(2)}) collective-permute-start(bf16[256,1024]{1,0:T(8,128)(2,1)} %shard_map.57.first_ref), channel_id=1, source_target_pairs={{0,8},{4,12},{8,0},{12,4},{16,24},{20,28},{24,16},{28,20},{1,9},{5... | collective-permute-start | bytes 1572872 | tf_op jit(solution)/shard_map/ppermute | solution.py:260
  37.3 0.1 pad_add_fusion.1.place_ref
  37.3 3.6 %collective-permute-done.5.mate_ref = bf16[1024,512]{1,0:T(8,128)(2,1)} collective-permute-done((bf16[1024,512]{1,0:T(8,128)(2,1)S(1)}, bf16[1024,512]{1,0:T(8,128)(2,1)}, u32[]{:S(2)}, u32[]{:S(2)}) %collective-permute-start.5) | collective-permute-done | bytes 1048608 | tf_op jit(solution)/shard_map/ppermute | solution.py:260
  41.0 1.4 %shard_map.58.weight_ref = bf16[2,1024,512]{2,1,0:T(8,128)(2,1)S(1)} custom-call(bf16[1024,512]{1,0:T(8,128)(2,1)S(1)} %copy-done.5, bf16[1024,512]{1,0:T(8,128)(2,1)} %collective-permute-done.5.mate_ref), custom_call_target="tpu_custom_call" | custom-call | bytes 4194304 | tf_op jit(solution)/shard_map/pallas_call | solution.py:291
  42.3 14.7 %collective-permute-done.4.tokens_ref = bf16[256,1024]{1,0:T(8,128)(2,1)} collective-permute-done((bf16[256,1024]{1,0:T(8,128)(2,1)}, bf16[256,1024]{1,0:T(8,128)(2,1)}, u32[]{:S(2)}, u32[]{:S(2)}) %collective-permute-start.4) | collective-permute-done | bytes 524320 | tf_op jit(solution)/shard_map/ppermute | solution.py:264
  57.1 1.7 %shard_map.59.heavy_ref = bf16[2,256,512]{2,1,0:T(8,128)(2,1)S(1)} custom-call(bf16[256,1024]{1,0:T(8,128)(2,1)} %collective-permute-done.4.tokens_ref, bf16[2,1024,512]{2,1,0:T(8,128)(2,1)S(1)} %shard_map.58.weight_ref), custom_call_target="tpu_custom_call" | custom-call | flops 536870912 | bytes 2097152 | tf_op jit(solution)/shard_map/pallas_call | solution.py:316
  58.8 0.0 collective-permute-done.6.second_ref
  58.8 2.8 %shard_map.61 = (bf16[2,256,512]{2,1,0:T(8,128)(2,1)S(1)}, bf16[2,256,512]{2,1,0:T(8,128)(2,1)}) custom-call(s32[2]{0:T(128)S(1)} %pad_add_fusion.1.place_ref, bf16[256,1024]{1,0:T(8,128)(2,1)} %shard_map.57.first_ref, bf16[256,1024]{1,0:T(8,128)(2,1)} %collective-permute-done.6.second_ref, bf16[2,256,512]{2,1,0:T(8,128)(2,1)S(1)} %shard_map.59.heavy_ref, ...), custom_call_target="tpu_custom_call" | custom-call | flops 1073741824 | bytes 4194304 | tf_op jit(solution)/shard_map/pallas_call | solution.py:304
  61.6 2.5 %collective-permute-start.9 = (bf16[2,256,512]{2,1,0:T(8,128)(2,1)}, bf16[2,256,512]{2,1,0:T(8,128)(2,1)}, u32[]{:S(2)}, u32[]{:S(2)}) collective-permute-start(bf16[2,256,512]{2,1,0:T(8,128)(2,1)} %get-tuple-element.26), channel_id=1, source_target_pairs={{0,1},{1,0},{2,3},{3,2},{4,5},{5,4},{6,7},{7,6},{8,9},{9,8},{10,11... | collective-permute-start | bytes 1572872 | tf_op jit(solution)/shard_map/ppermute | solution.py:264
  64.1 0.4 collective-permute-start.7
  64.5 0.1 pad_add_fusion.place_ref
  64.6 1.4 %collective-permute-done.9 = bf16[2,256,512]{2,1,0:T(8,128)(2,1)} collective-permute-done((bf16[2,256,512]{2,1,0:T(8,128)(2,1)}, bf16[2,256,512]{2,1,0:T(8,128)(2,1)}, u32[]{:S(2)}, u32[]{:S(2)}) %collective-permute-start.9) | collective-permute-done | bytes 524320 | tf_op jit(solution)/shard_map/ppermute | solution.py:264
  66.0 1.2 %add_convert_fusion.1 = bf16[2,256,512]{2,1,0:T(8,128)(2,1)S(1)} fusion(bf16[2,256,512]{2,1,0:T(8,128)(2,1)} %collective-permute-done.9, bf16[2,256,512]{2,1,0:T(8,128)(2,1)S(1)} %get-tuple-element.25), kind=kLoop, calls=%fused_computation.1 | loop fusion | flops 1048576 | bytes 1572864 | tf_op jit(solution)/shard_map/convert_element_type | solution.py:318
  67.2 1.4 %collective-permute-start.10 = (bf16[2,256,512]{2,1,0:T(8,128)(2,1)S(1)}, bf16[2,256,512]{2,1,0:T(8,128)(2,1)S(1)}, u32[]{:S(2)}, u32[]{:S(2)}) collective-permute-start(bf16[2,256,512]{2,1,0:T(8,128)(2,1)S(1)} %add_convert_fusion.1), channel_id=1, source_target_pairs={{0,2},{1,3},{2,0},{3,1},{4,6},{5,7},{6,4},{7,5},{8,10},{9,11},{10,... | collective-permute-start | bytes 1572872 | tf_op jit(solution)/shard_map/ppermute | solution.py:264
  68.6 9.3 %collective-permute-done.7.heavy_ref = bf16[256,1024]{1,0:T(8,128)(2,1)S(1)} collective-permute-done((bf16[256,1024]{1,0:T(8,128)(2,1)}, bf16[256,1024]{1,0:T(8,128)(2,1)S(1)}, u32[]{:S(2)}, u32[]{:S(2)}) %collective-permute-start.7) | collective-permute-done | bytes 524320 | tf_op jit(solution)/shard_map/ppermute | solution.py:260
  77.9 2.5 %shard_map.60 = (bf16[2,256,512]{2,1,0:T(8,128)(2,1)S(1)}, bf16[2,256,512]{2,1,0:T(8,128)(2,1)S(1)}) custom-call(s32[2]{0:T(128)S(1)} %pad_add_fusion.place_ref, bf16[256,1024]{1,0:T(8,128)(2,1)} %shard_map.57.first_ref, bf16[256,1024]{1,0:T(8,128)(2,1)} %collective-permute-done.6.second_ref, bf16[256,1024]{1,0:T(8,128)(2,1)S(1)} %collective-permute-done.7.heavy_ref, ...), custom_call_target="tpu_custom_call" | custom-call | flops 1073741824 | bytes 4194304 | tf_op jit(solution)/shard_map/pallas_call | solution.py:304
  80.4 0.9 collective-permute-start.8
  81.3 0.0 collective-permute-done.10
  81.3 1.5 %collective-permute-done.8 = bf16[2,256,512]{2,1,0:T(8,128)(2,1)S(1)} collective-permute-done((bf16[2,256,512]{2,1,0:T(8,128)(2,1)S(1)}, bf16[2,256,512]{2,1,0:T(8,128)(2,1)S(1)}, u32[]{:S(2)}, u32[]{:S(2)}) %collective-permute-start.8) | collective-permute-done | bytes 524320 | tf_op jit(solution)/shard_map/ppermute | solution.py:264
  82.8 0.2 add_convert_fusion
  83.0 5.4 %collective-permute-start.11 = (bf16[2,256,512]{2,1,0:T(8,128)(2,1)S(1)}, bf16[2,256,512]{2,1,0:T(8,128)(2,1)S(1)}, u32[]{:S(2)}, u32[]{:S(2)}) collective-permute-start(bf16[2,256,512]{2,1,0:T(8,128)(2,1)S(1)} %add_convert_fusion), channel_id=1, source_target_pairs={{0,0},{1,24},{2,8},{3,16},{4,4},{5,28},{6,12},{7,20},{8,9},{9,17},... | collective-permute-start | bytes 1572872 | tf_op jit(solution)/shard_map/ppermute | solution.py:264
  88.5 11.7 %collective-permute-done.11 = bf16[2,256,512]{2,1,0:T(8,128)(2,1)S(1)} collective-permute-done((bf16[2,256,512]{2,1,0:T(8,128)(2,1)S(1)}, bf16[2,256,512]{2,1,0:T(8,128)(2,1)S(1)}, u32[]{:S(2)}, u32[]{:S(2)}) %collective-permute-start.11) | collective-permute-done | bytes 524320 | tf_op jit(solution)/shard_map/ppermute | solution.py:264
  100.2 0.9 pad_maximum_fusion
  (1 shorter events, 0.0 us)
Async XLA Ops:
  0.0 1.0 %copy-start = (bf16[256,1024]{1,0:T(8,128)(2,1)S(1)}, bf16[256,1024]{1,0:T(8,128)(2,1)}, u32[]{:S(2)}) copy-start(bf16[256,1024]{1,0:T(8,128)(2,1)} %k_ref.3) | copy-start | bytes 1572868
  1.0 1.0 %copy-start.2 = (bf16[256,1024]{1,0:T(8,128)(2,1)S(1)}, bf16[256,1024]{1,0:T(8,128)(2,1)}, u32[]{:S(2)}) copy-start(bf16[256,1024]{1,0:T(8,128)(2,1)} %v_ref.3) | copy-start | bytes 1572868
  2.4 8.2 %collective-permute-start = (bf16[8,128,128]{2,1,0:T(8,128)(2,1)S(1)}, bf16[8,128,128]{2,1,0:T(8,128)(2,1)S(1)}, u32[]{:S(2)}, u32[]{:S(2)}) collective-permute-start(bf16[8,128,128]{2,1,0:T(8,128)(2,1)S(1)} %get-tuple-element.16), channel_id=1, source_target_pairs={{0,4},{4,0},{8,12},{12,8},{16,20},{20,16},{24,28},{28,24},{1,5},{5... | collective-permute-start | bytes 786440 | tf_op jit(solution)/shard_map/ppermute | solution.py:260
  4.6 1.0 %copy-start.1 = (bf16[256,1024]{1,0:T(8,128)(2,1)S(1)}, bf16[256,1024]{1,0:T(8,128)(2,1)}, u32[]{:S(2)}) copy-start(bf16[256,1024]{1,0:T(8,128)(2,1)} %k_ref.3) | copy-start | bytes 1572868
  5.6 1.0 %copy-start.3 = (bf16[256,1024]{1,0:T(8,128)(2,1)S(1)}, bf16[256,1024]{1,0:T(8,128)(2,1)}, u32[]{:S(2)}) copy-start(bf16[256,1024]{1,0:T(8,128)(2,1)} %q_ref.3) | copy-start | bytes 1572868
  6.7 11.9 %copy-start.5 = (bf16[1024,512]{1,0:T(8,128)(2,1)S(1)}, bf16[1024,512]{1,0:T(8,128)(2,1)}, u32[]{:S(2)}) copy-start(bf16[1024,512]{1,0:T(8,128)(2,1)} %own_ref.1) | copy-start | bytes 3145732
  7.6 14.5 %copy-start.4 = (bf16[256,1024]{1,0:T(8,128)(2,1)S(1)}, bf16[256,1024]{1,0:T(8,128)(2,1)}, u32[]{:S(2)}) copy-start(bf16[256,1024]{1,0:T(8,128)(2,1)} %q_ref.3) | copy-start | bytes 1572868
  7.6 14.5 %copy-start.6 = (f32[1024]{0:T(1024)S(1)}, f32[1024]{0:T(1024)}, u32[]{:S(2)}) copy-start(f32[1024]{0:T(1024)} %param.8) | copy-start | bytes 12292
  10.7 7.1 %collective-permute-start.1 = (bf16[8,128,128]{2,1,0:T(8,128)(2,1)S(1)}, bf16[8,128,128]{2,1,0:T(8,128)(2,1)S(1)}, u32[]{:S(2)}, u32[]{:S(2)}) collective-permute-start(bf16[8,128,128]{2,1,0:T(8,128)(2,1)S(1)} %fusion), channel_id=1, source_target_pairs={{0,8},{4,12},{1,9},{5,13},{2,10},{6,14},{3,11},{7,15}} | collective-permute-start | bytes 786440 | tf_op jit(solution)/shard_map/ppermute | solution.py:286
  17.9 2.0 %collective-permute-start.2 = (bf16[8,128,128]{2,1,0:T(8,128)(2,1)S(1)}, bf16[8,128,128]{2,1,0:T(8,128)(2,1)S(1)}, u32[]{:S(2)}, u32[]{:S(2)}) collective-permute-start(bf16[8,128,128]{2,1,0:T(8,128)(2,1)S(1)} %fusion.1), channel_id=1, source_target_pairs={{8,16},{12,20},{9,17},{13,21},{10,18},{14,22},{11,19},{15,23}} | collective-permute-start | bytes 786440 | tf_op jit(solution)/shard_map/ppermute | solution.py:286
  18.6 22.4 %collective-permute-start.5 = (bf16[1024,512]{1,0:T(8,128)(2,1)S(1)}, bf16[1024,512]{1,0:T(8,128)(2,1)}, u32[]{:S(2)}, u32[]{:S(2)}) collective-permute-start(bf16[1024,512]{1,0:T(8,128)(2,1)S(1)} %copy-done.5), channel_id=1, source_target_pairs={{0,4},{4,0},{8,12},{12,8},{16,20},{20,16},{24,28},{28,24},{1,5},{5... | collective-permute-start | bytes 3145736 | tf_op jit(solution)/shard_map/ppermute | solution.py:260
  20.7 1.4 %collective-permute-start.3 = (bf16[8,128,128]{2,1,0:T(8,128)(2,1)}, bf16[8,128,128]{2,1,0:T(8,128)(2,1)}, u32[]{:S(2)}, u32[]{:S(2)}) collective-permute-start(bf16[8,128,128]{2,1,0:T(8,128)(2,1)} %add_convert_fusion.2), channel_id=1, source_target_pairs={{16,24},{20,28},{17,25},{21,29},{18,26},{22,30},{19,27},{23,31}} | collective-permute-start | bytes 786440 | tf_op jit(solution)/shard_map/ppermute | solution.py:286
  24.6 32.5 %collective-permute-start.4 = (bf16[256,1024]{1,0:T(8,128)(2,1)}, bf16[256,1024]{1,0:T(8,128)(2,1)}, u32[]{:S(2)}, u32[]{:S(2)}) collective-permute-start(bf16[256,1024]{1,0:T(8,128)(2,1)} %shard_map.57.first_ref), channel_id=1, source_target_pairs={{0,16},{1,17},{2,26},{3,27},{4,20},{5,21},{6,30},{7,31},{8,24},{9,... | collective-permute-start | bytes 1572872 | tf_op jit(solution)/shard_map/ppermute | solution.py:264
  35.1 23.7 %collective-permute-start.6 = (bf16[256,1024]{1,0:T(8,128)(2,1)}, bf16[256,1024]{1,0:T(8,128)(2,1)}, u32[]{:S(2)}, u32[]{:S(2)}) collective-permute-start(bf16[256,1024]{1,0:T(8,128)(2,1)} %shard_map.57.first_ref), channel_id=1, source_target_pairs={{0,8},{4,12},{8,0},{12,4},{16,24},{20,28},{24,16},{28,20},{1,9},{5... | collective-permute-start | bytes 1572872 | tf_op jit(solution)/shard_map/ppermute | solution.py:260
  61.6 4.4 %collective-permute-start.9 = (bf16[2,256,512]{2,1,0:T(8,128)(2,1)}, bf16[2,256,512]{2,1,0:T(8,128)(2,1)}, u32[]{:S(2)}, u32[]{:S(2)}) collective-permute-start(bf16[2,256,512]{2,1,0:T(8,128)(2,1)} %get-tuple-element.26), channel_id=1, source_target_pairs={{0,1},{1,0},{2,3},{3,2},{4,5},{5,4},{6,7},{7,6},{8,9},{9,8},{10,11... | collective-permute-start | bytes 1572872 | tf_op jit(solution)/shard_map/ppermute | solution.py:264
  64.1 13.8 %collective-permute-start.7 = (bf16[256,1024]{1,0:T(8,128)(2,1)}, bf16[256,1024]{1,0:T(8,128)(2,1)S(1)}, u32[]{:S(2)}, u32[]{:S(2)}) collective-permute-start(bf16[256,1024]{1,0:T(8,128)(2,1)} %collective-permute-done.4.tokens_ref), channel_id=1, source_target_pairs={{0,8},{4,12},{8,0},{12,4},{16,24},{20,28},{24,16},{28,20},{1,9},{5... | collective-permute-start | bytes 1572872 | tf_op jit(solution)/shard_map/ppermute | solution.py:260
  67.2 14.1 %collective-permute-start.10 = (bf16[2,256,512]{2,1,0:T(8,128)(2,1)S(1)}, bf16[2,256,512]{2,1,0:T(8,128)(2,1)S(1)}, u32[]{:S(2)}, u32[]{:S(2)}) collective-permute-start(bf16[2,256,512]{2,1,0:T(8,128)(2,1)S(1)} %add_convert_fusion.1), channel_id=1, source_target_pairs={{0,2},{1,3},{2,0},{3,1},{4,6},{5,7},{6,4},{7,5},{8,10},{9,11},{10,... | collective-permute-start | bytes 1572872 | tf_op jit(solution)/shard_map/ppermute | solution.py:264
  80.4 2.4 %collective-permute-start.8 = (bf16[2,256,512]{2,1,0:T(8,128)(2,1)S(1)}, bf16[2,256,512]{2,1,0:T(8,128)(2,1)S(1)}, u32[]{:S(2)}, u32[]{:S(2)}) collective-permute-start(bf16[2,256,512]{2,1,0:T(8,128)(2,1)S(1)} %get-tuple-element.23), channel_id=1, source_target_pairs={{0,1},{1,0},{2,3},{3,2},{4,5},{5,4},{6,7},{7,6},{8,9},{9,8},{10,11... | collective-permute-start | bytes 1572872 | tf_op jit(solution)/shard_map/ppermute | solution.py:264
  83.0 17.1 %collective-permute-start.11 = (bf16[2,256,512]{2,1,0:T(8,128)(2,1)S(1)}, bf16[2,256,512]{2,1,0:T(8,128)(2,1)S(1)}, u32[]{:S(2)}, u32[]{:S(2)}) collective-permute-start(bf16[2,256,512]{2,1,0:T(8,128)(2,1)S(1)} %add_convert_fusion), channel_id=1, source_target_pairs={{0,0},{1,24},{2,8},{3,16},{4,4},{5,28},{6,12},{7,20},{8,9},{9,17},... | collective-permute-start | bytes 1572872 | tf_op jit(solution)/shard_map/ppermute | solution.py:264

commit v18 on v16

--- a/solution.py
+++ b/solution.py
@@ -226,6 +226,18 @@
         multiply(keep_ref, heavy_ref)
 
 
+def project_light_kernel(core_ref, light_ref, heavy_ref, weight_ref, keep_ref, send_ref):
+    @pl.when(core_ref[0] == 0)
+    def _():
+        project_kernel(light_ref, weight_ref, keep_ref)
+        send_ref[...] = heavy_ref[...]
+
+    @pl.when(core_ref[0] != 0)
+    def _():
+        project_kernel(light_ref, weight_ref, send_ref)
+        keep_ref[...] = heavy_ref[...]
+
+
 def pairs_body(queries, key_vectors, value_vectors, norm_gain, out_weight):
     rows, features = queries.shape
     heads = features // HD
@@ -283,9 +295,9 @@
     flops, moved = 4 * size * half_cols, 8 * size
     vmem = pl.BlockSpec(memory_space=pltpu.VMEM)
 
-    def projected(light, heavy):
+    def projected(kernel, light, heavy):
         keep, send = pl.pallas_call(
-            project_pair_kernel,
+            kernel,
             out_shape=(tile, tile),
             in_specs=[pl.BlockSpec(memory_space=pltpu.SMEM)] + [vmem] * 3,
             out_specs=(vmem, vmem),
@@ -296,9 +308,11 @@
         )(core.astype(jnp.int32)[None], light, heavy, weight)
         return keep.astype(F32) + move(send, lambda z, y, x, c: (z, y, x, 1 - c)).astype(F32)
 
-    far = projected(jnp.where(x == 0, beside, attended), straight).astype(BF16)
+    product = call(project_kernel, tile, flops, moved)(straight, weight)
+    product, beside = lax.optimization_barrier((product, beside))
+    far = projected(project_light_kernel, jnp.where(x == 0, beside, attended), product).astype(BF16)
     crossed = move(far, lambda z, y, x, c: (z, y, 1 - x, c))
-    near = projected(jnp.where(x == 0, attended, beside), onward) + crossed.astype(F32)
+    near = projected(project_pair_kernel, jnp.where(x == 0, attended, beside), onward) + crossed.astype(F32)
     result = move(near.astype(BF16), lambda z, y, x, c: (z ^ 3 * c ^ x, y, z // 2, z % 2))
     first = jnp.where(y == 0, result[0], result[1])
     return jnp.concatenate([first, jnp.where(y == 0, result[1], result[0])], axis=1)

time: 94.8 us -> 94.7 us (level)
  starting transfers between devices: 39.8 us -> 33.3 us
  waiting for transfers between devices: 42.4 us -> 48.6 us
    ppermute x5, waiting for transfers between devices: 18.1 us -> 25.8 us  [move(): return lax.ppermute(value, both, pairs)]
    ppermute x5, starting transfers between devices: 27 us -> 22.5 us  [move(): return lax.ppermute(value, both, pairs)]
    ppermute x4, starting transfers between devices: 8.38 us -> 6.39 us  [swap(): return lax.ppermute(value, 'seq', [(s, s ^ mask) for s in range(8)])]
    ppermute x4, waiting for transfers between devices: 20.2 us -> 18.7 us  [swap(): return lax.ppermute(value, 'seq', [(s, s ^ mask) for s in range(8)])]
    pallas_call x2 -> x3, Pallas kernels: 2.57 us -> 2.74 us  [the longest x2 2.02 us: projected(): pl.pallas_call(kernel, out_shape=(tile, tile), in_specs=[pl.BlockSpec(mem...]
  transfers between devices with their start and end apart: 12 -> 12, of which waited for: 8 -> 9; matrix products, arithmetic and copies ran while one was open for 0% -> 0% of each run, Pallas kernels for 5% -> 6%
where the time goes in v18:
time: 94.7 us; the launch traced here: 94.3 us
  waiting for transfers between devices  48.6 us (51%)
  starting transfers between devices  33.3 us (35%)
  Pallas kernels  6.45 us (7%)
  local copies, waits for them, and re-layouts  4.18 us (4%)
  other arithmetic  1.6 us (2%)
    ppermute x5, waiting for transfers between devices, move(): return lax.ppermute(value, both, pairs)  25.8 us
    ppermute x5, starting transfers between devices, move(): return lax.ppermute(value, both, pairs)  22.5 us
    ppermute x4, waiting for transfers between devices, swap(): return lax.ppermute(value, 'seq', [(s, s ^ mask) for s in range(8)])  18.7 us
    ppermute x4, starting transfers between devices, swap(): return lax.ppermute(value, 'seq', [(s, s ^ mask) for s in range(8)])  6.39 us
    ppermute x3, starting transfers between devices, pairs_body(): earlier.append(lax.ppermute(onward.astype(BF16), 'seq', pairs))  4.47 us
    unnamed x12, local copies, waits for them, and re-layouts  4.18 us
    ppermute x3, waiting for transfers between devices, pairs_body(): earlier.append(lax.ppermute(onward.astype(BF16), 'seq', pairs))  4.02 us
    pallas_call x2, Pallas kernels, projected(): pl.pallas_call(kernel, out_shape=(tile, tile), in_specs=[pl.BlockSpec(mem...  2.02 us
  transfers between devices with their start and end apart: 12, of which 9 were waited for; matrix products, arithmetic and copies ran while one was open for 0% of the time, Pallas kernels for 6%

profile of v18, /device:TPU:1, one launch (start us, length us, event | category | flops | bytes accessed | tf_op | source)
XLA Modules:
  0.0 94.3 jit_solution(2462512058232474603)
XLA Ops:
  0.0 0.0 copy-start
  0.0 1.0 %copy-done = bf16[256,1024]{1,0:T(8,128)(2,1)S(1)} copy-done((bf16[256,1024]{1,0:T(8,128)(2,1)S(1)}, bf16[256,1024]{1,0:T(8,128)(2,1)}, u32[]{:S(2)}) %copy-start) | copy-done | bytes 524312
  1.0 0.0 copy-start.2
  1.0 1.0 %copy-done.2 = bf16[256,1024]{1,0:T(8,128)(2,1)S(1)} copy-done((bf16[256,1024]{1,0:T(8,128)(2,1)S(1)}, bf16[256,1024]{1,0:T(8,128)(2,1)}, u32[]{:S(2)}) %copy-start.2) | copy-done | bytes 524312
  2.1 0.4 shard_map.55
  2.4 2.1 %collective-permute-start = (bf16[8,128,128]{2,1,0:T(8,128)(2,1)S(1)}, bf16[8,128,128]{2,1,0:T(8,128)(2,1)S(1)}, u32[]{:S(2)}, u32[]{:S(2)}) collective-permute-start(bf16[8,128,128]{2,1,0:T(8,128)(2,1)S(1)} %get-tuple-element.16), channel_id=1, source_target_pairs={{0,4},{4,0},{8,12},{12,8},{16,20},{20,16},{24,28},{28,24},{1,5},{5... | collective-permute-start | bytes 786440 | tf_op jit(solution)/shard_map/ppermute | solution.py:255
  4.6 0.0 copy-start.1
  4.6 1.0 %copy-done.1 = bf16[256,1024]{1,0:T(8,128)(2,1)S(1)} copy-done((bf16[256,1024]{1,0:T(8,128)(2,1)S(1)}, bf16[256,1024]{1,0:T(8,128)(2,1)}, u32[]{:S(2)}) %copy-start.1) | copy-done | bytes 524312
  5.6 0.0 copy-start.3
  5.6 1.0 %copy-done.3 = bf16[256,1024]{1,0:T(8,128)(2,1)S(1)} copy-done((bf16[256,1024]{1,0:T(8,128)(2,1)S(1)}, bf16[256,1024]{1,0:T(8,128)(2,1)}, u32[]{:S(2)}) %copy-start.3) | copy-done | bytes 524312
  6.7 0.9 shard_map.56.within_ref
  7.6 0.0 copy-start.4
  7.6 0.0 copy-start.5
  7.6 3.0 %collective-permute-done.mate_ref = bf16[8,128,128]{2,1,0:T(8,128)(2,1)S(1)} collective-permute-done((bf16[8,128,128]{2,1,0:T(8,128)(2,1)S(1)}, bf16[8,128,128]{2,1,0:T(8,128)(2,1)S(1)}, u32[]{:S(2)}, u32[]{:S(2)}) %collective-permute-start) | collective-permute-done | bytes 262176 | tf_op jit(solution)/shard_map/ppermute | solution.py:255
  10.6 0.1 fusion
  10.7 3.1 %collective-permute-start.1 = (bf16[8,128,128]{2,1,0:T(8,128)(2,1)S(1)}, bf16[8,128,128]{2,1,0:T(8,128)(2,1)S(1)}, u32[]{:S(2)}, u32[]{:S(2)}) collective-permute-start(bf16[8,128,128]{2,1,0:T(8,128)(2,1)S(1)} %fusion), channel_id=1, source_target_pairs={{0,8},{4,12},{1,9},{5,13},{2,10},{6,14},{3,11},{7,15}} | collective-permute-start | bytes 786440 | tf_op jit(solution)/shard_map/ppermute | solution.py:281
  13.8 4.0 %collective-permute-done.1.refs_0_ = bf16[8,128,128]{2,1,0:T(8,128)(2,1)S(1)} collective-permute-done((bf16[8,128,128]{2,1,0:T(8,128)(2,1)S(1)}, bf16[8,128,128]{2,1,0:T(8,128)(2,1)S(1)}, u32[]{:S(2)}, u32[]{:S(2)}) %collective-permute-start.1) | collective-permute-done | bytes 262176 | tf_op jit(solution)/shard_map/ppermute | solution.py:281
  17.8 0.1 fusion.1
  17.9 0.7 collective-permute-start.2
  18.6 1.3 %collective-permute-start.5 = (bf16[1024,512]{1,0:T(8,128)(2,1)}, bf16[1024,512]{1,0:T(8,128)(2,1)}, u32[]{:S(2)}, u32[]{:S(2)}) collective-permute-start(bf16[1024,512]{1,0:T(8,128)(2,1)} %own_ref.1), channel_id=1, source_target_pairs={{0,4},{4,0},{8,12},{12,8},{16,20},{20,16},{24,28},{28,24},{1,5},{5... | collective-permute-start | bytes 3145736 | tf_op jit(solution)/shard_map/ppermute | solution.py:255
  19.9 0.0 collective-permute-done.2.refs_1_
  19.9 0.1 add_convert_fusion.2
  20.0 0.7 collective-permute-start.3
  20.7 0.0 collective-permute-done.3.refs_2_
  20.7 0.0 copy-done.4
  20.7 0.0 copy-done.5
  20.8 0.8 shard_map.57
  21.5 10.9 %collective-permute-start.4 = (bf16[256,1024]{1,0:T(8,128)(2,1)S(1)}, bf16[256,1024]{1,0:T(8,128)(2,1)S(1)}, u32[]{:S(2)}, u32[]{:S(2)}) collective-permute-start(bf16[256,1024]{1,0:T(8,128)(2,1)S(1)} %shard_map.57), channel_id=1, source_target_pairs={{0,16},{1,17},{2,26},{3,27},{4,20},{5,21},{6,30},{7,31},{8,24},{9,... | collective-permute-start | bytes 1572872 | tf_op jit(solution)/shard_map/ppermute | solution.py:259
  32.4 2.3 %collective-permute-start.6 = (bf16[256,1024]{1,0:T(8,128)(2,1)S(1)}, bf16[256,1024]{1,0:T(8,128)(2,1)S(1)}, u32[]{:S(2)}, u32[]{:S(2)}) collective-permute-start(bf16[256,1024]{1,0:T(8,128)(2,1)S(1)} %shard_map.57), channel_id=1, source_target_pairs={{0,8},{4,12},{8,0},{12,4},{16,24},{20,28},{24,16},{28,20},{1,9},{5... | collective-permute-start | bytes 1572872 | tf_op jit(solution)/shard_map/ppermute | solution.py:255
  34.7 6.5 %collective-permute-done.5.mate_ref = bf16[1024,512]{1,0:T(8,128)(2,1)} collective-permute-done((bf16[1024,512]{1,0:T(8,128)(2,1)}, bf16[1024,512]{1,0:T(8,128)(2,1)}, u32[]{:S(2)}, u32[]{:S(2)}) %collective-permute-start.5) | collective-permute-done | bytes 1048608 | tf_op jit(solution)/shard_map/ppermute | solution.py:255
  41.2 1.7 %shard_map.58.weight_ref = bf16[2,1024,512]{2,1,0:T(8,128)(2,1)S(1)} custom-call(bf16[1024,512]{1,0:T(8,128)(2,1)} %own_ref.1, bf16[1024,512]{1,0:T(8,128)(2,1)} %collective-permute-done.5.mate_ref), custom_call_target="tpu_custom_call" | custom-call | bytes 4194304 | tf_op jit(solution)/shard_map/pallas_call | solution.py:286
  42.8 11.1 %collective-permute-done.4.tokens_ref = bf16[256,1024]{1,0:T(8,128)(2,1)S(1)} collective-permute-done((bf16[256,1024]{1,0:T(8,128)(2,1)S(1)}, bf16[256,1024]{1,0:T(8,128)(2,1)S(1)}, u32[]{:S(2)}, u32[]{:S(2)}) %collective-permute-start.4) | collective-permute-done | bytes 524320 | tf_op jit(solution)/shard_map/ppermute | solution.py:259
  54.0 0.7 shard_map.59.heavy_ref
  54.7 0.0 collective-permute-done.6
  54.7 0.1 broadcast_select_fusion.1
  54.8 0.7 shard_map.61
  55.5 2.7 %collective-permute-start.9 = (bf16[2,256,512]{2,1,0:T(8,128)(2,1)S(1)}, bf16[2,256,512]{2,1,0:T(8,128)(2,1)S(1)}, u32[]{:S(2)}, u32[]{:S(2)}) collective-permute-start(bf16[2,256,512]{2,1,0:T(8,128)(2,1)S(1)} %get-tuple-element.26), channel_id=1, source_target_pairs={{0,1},{1,0},{2,3},{3,2},{4,5},{5,4},{6,7},{7,6},{8,9},{9,8},{10,11... | collective-permute-start | bytes 1572872 | tf_op jit(solution)/shard_map/ppermute | solution.py:259
  58.2 0.7 collective-permute-start.7
  58.9 0.9 collective-permute-done.9
  59.8 0.1 add_convert_fusion.1
  59.9 2.5 %collective-permute-start.10 = (bf16[2,256,512]{2,1,0:T(8,128)(2,1)S(1)}, bf16[2,256,512]{2,1,0:T(8,128)(2,1)S(1)}, u32[]{:S(2)}, u32[]{:S(2)}) collective-permute-start(bf16[2,256,512]{2,1,0:T(8,128)(2,1)S(1)} %add_convert_fusion.1), channel_id=1, source_target_pairs={{0,2},{1,3},{2,0},{3,1},{4,6},{5,7},{6,4},{7,5},{8,10},{9,11},{10,... | collective-permute-start | bytes 1572872 | tf_op jit(solution)/shard_map/ppermute | solution.py:259
  62.4 9.3 %collective-permute-done.7.heavy_ref = bf16[256,1024]{1,0:T(8,128)(2,1)S(1)} collective-permute-done((bf16[256,1024]{1,0:T(8,128)(2,1)S(1)}, bf16[256,1024]{1,0:T(8,128)(2,1)S(1)}, u32[]{:S(2)}, u32[]{:S(2)}) %collective-permute-start.7) | collective-permute-done | bytes 524320 | tf_op jit(solution)/shard_map/ppermute | solution.py:255
  71.7 1.3 %shard_map.60 = (bf16[2,256,512]{2,1,0:T(8,128)(2,1)S(1)}, bf16[2,256,512]{2,1,0:T(8,128)(2,1)S(1)}) custom-call(s32[1]{0:T(128)} %bitcast.core_ref, bf16[256,1024]{1,0:T(8,128)(2,1)S(1)} %get-tuple-element.27.light_ref, bf16[256,1024]{1,0:T(8,128)(2,1)S(1)} %collective-permute-done.7.heavy_ref, bf16[2,1024,512]{2,1,0:T(8,128)(2,1)S(1)} %shard_map.58.weight_ref), custom_call_target="tpu_custom_call" | custom-call | flops 1073741824 | bytes 4194304 | tf_op jit(solution)/shard_map/pallas_call | solution.py:299
  73.0 0.9 collective-permute-start.8
  73.9 0.5 collective-permute-done.10
  74.4 1.0 %collective-permute-done.8 = bf16[2,256,512]{2,1,0:T(8,128)(2,1)S(1)} collective-permute-done((bf16[2,256,512]{2,1,0:T(8,128)(2,1)S(1)}, bf16[2,256,512]{2,1,0:T(8,128)(2,1)S(1)}, u32[]{:S(2)}, u32[]{:S(2)}) %collective-permute-start.8) | collective-permute-done | bytes 524320 | tf_op jit(solution)/shard_map/ppermute | solution.py:259
  75.5 0.2 add_convert_fusion
  75.7 5.4 %collective-permute-start.11 = (bf16[2,256,512]{2,1,0:T(8,128)(2,1)S(1)}, bf16[2,256,512]{2,1,0:T(8,128)(2,1)S(1)}, u32[]{:S(2)}, u32[]{:S(2)}) collective-permute-start(bf16[2,256,512]{2,1,0:T(8,128)(2,1)S(1)} %add_convert_fusion), channel_id=1, source_target_pairs={{0,0},{1,24},{2,8},{3,16},{4,4},{5,28},{6,12},{7,20},{8,9},{9,17},... | collective-permute-start | bytes 1572872 | tf_op jit(solution)/shard_map/ppermute | solution.py:259
  81.1 12.3 %collective-permute-done.11 = bf16[2,256,512]{2,1,0:T(8,128)(2,1)S(1)} collective-permute-done((bf16[2,256,512]{2,1,0:T(8,128)(2,1)S(1)}, bf16[2,256,512]{2,1,0:T(8,128)(2,1)S(1)}, u32[]{:S(2)}, u32[]{:S(2)}) %collective-permute-start.11) | collective-permute-done | bytes 524320 | tf_op jit(solution)/shard_map/ppermute | solution.py:259
  93.5 0.9 pad_maximum_fusion
  (1 shorter events, 0.0 us)
Async XLA Ops:
  0.0 1.0 %copy-start = (bf16[256,1024]{1,0:T(8,128)(2,1)S(1)}, bf16[256,1024]{1,0:T(8,128)(2,1)}, u32[]{:S(2)}) copy-start(bf16[256,1024]{1,0:T(8,128)(2,1)} %k_ref.3) | copy-start | bytes 1572868
  1.0 1.0 %copy-start.2 = (bf16[256,1024]{1,0:T(8,128)(2,1)S(1)}, bf16[256,1024]{1,0:T(8,128)(2,1)}, u32[]{:S(2)}) copy-start(bf16[256,1024]{1,0:T(8,128)(2,1)} %v_ref.3) | copy-start | bytes 1572868
  2.4 8.2 %collective-permute-start = (bf16[8,128,128]{2,1,0:T(8,128)(2,1)S(1)}, bf16[8,128,128]{2,1,0:T(8,128)(2,1)S(1)}, u32[]{:S(2)}, u32[]{:S(2)}) collective-permute-start(bf16[8,128,128]{2,1,0:T(8,128)(2,1)S(1)} %get-tuple-element.16), channel_id=1, source_target_pairs={{0,4},{4,0},{8,12},{12,8},{16,20},{20,16},{24,28},{28,24},{1,5},{5... | collective-permute-start | bytes 786440 | tf_op jit(solution)/shard_map/ppermute | solution.py:255
  4.6 1.0 %copy-start.1 = (bf16[256,1024]{1,0:T(8,128)(2,1)S(1)}, bf16[256,1024]{1,0:T(8,128)(2,1)}, u32[]{:S(2)}) copy-start(bf16[256,1024]{1,0:T(8,128)(2,1)} %k_ref.3) | copy-start | bytes 1572868
  5.6 1.0 %copy-start.3 = (bf16[256,1024]{1,0:T(8,128)(2,1)S(1)}, bf16[256,1024]{1,0:T(8,128)(2,1)}, u32[]{:S(2)}) copy-start(bf16[256,1024]{1,0:T(8,128)(2,1)} %q_ref.3) | copy-start | bytes 1572868
  7.6 13.1 %copy-start.4 = (bf16[256,1024]{1,0:T(8,128)(2,1)S(1)}, bf16[256,1024]{1,0:T(8,128)(2,1)}, u32[]{:S(2)}) copy-start(bf16[256,1024]{1,0:T(8,128)(2,1)} %q_ref.3) | copy-start | bytes 1572868
  7.6 13.1 %copy-start.5 = (f32[1024]{0:T(1024)S(1)}, f32[1024]{0:T(1024)}, u32[]{:S(2)}) copy-start(f32[1024]{0:T(1024)} %param.8) | copy-start | bytes 12292
  10.7 7.1 %collective-permute-start.1 = (bf16[8,128,128]{2,1,0:T(8,128)(2,1)S(1)}, bf16[8,128,128]{2,1,0:T(8,128)(2,1)S(1)}, u32[]{:S(2)}, u32[]{:S(2)}) collective-permute-start(bf16[8,128,128]{2,1,0:T(8,128)(2,1)S(1)} %fusion), channel_id=1, source_target_pairs={{0,8},{4,12},{1,9},{5,13},{2,10},{6,14},{3,11},{7,15}} | collective-permute-start | bytes 786440 | tf_op jit(solution)/shard_map/ppermute | solution.py:281
  17.9 2.0 %collective-permute-start.2 = (bf16[8,128,128]{2,1,0:T(8,128)(2,1)S(1)}, bf16[8,128,128]{2,1,0:T(8,128)(2,1)S(1)}, u32[]{:S(2)}, u32[]{:S(2)}) collective-permute-start(bf16[8,128,128]{2,1,0:T(8,128)(2,1)S(1)} %fusion.1), channel_id=1, source_target_pairs={{8,16},{12,20},{9,17},{13,21},{10,18},{14,22},{11,19},{15,23}} | collective-permute-start | bytes 786440 | tf_op jit(solution)/shard_map/ppermute | solution.py:281
  18.6 22.6 %collective-permute-start.5 = (bf16[1024,512]{1,0:T(8,128)(2,1)}, bf16[1024,512]{1,0:T(8,128)(2,1)}, u32[]{:S(2)}, u32[]{:S(2)}) collective-permute-start(bf16[1024,512]{1,0:T(8,128)(2,1)} %own_ref.1), channel_id=1, source_target_pairs={{0,4},{4,0},{8,12},{12,8},{16,20},{20,16},{24,28},{28,24},{1,5},{5... | collective-permute-start | bytes 3145736 | tf_op jit(solution)/shard_map/ppermute | solution.py:255
  20.0 0.7 collective-permute-start.3
  21.5 32.4 %collective-permute-start.4 = (bf16[256,1024]{1,0:T(8,128)(2,1)S(1)}, bf16[256,1024]{1,0:T(8,128)(2,1)S(1)}, u32[]{:S(2)}, u32[]{:S(2)}) collective-permute-start(bf16[256,1024]{1,0:T(8,128)(2,1)S(1)} %shard_map.57), channel_id=1, source_target_pairs={{0,16},{1,17},{2,26},{3,27},{4,20},{5,21},{6,30},{7,31},{8,24},{9,... | collective-permute-start | bytes 1572872 | tf_op jit(solution)/shard_map/ppermute | solution.py:259
  32.4 22.3 %collective-permute-start.6 = (bf16[256,1024]{1,0:T(8,128)(2,1)S(1)}, bf16[256,1024]{1,0:T(8,128)(2,1)S(1)}, u32[]{:S(2)}, u32[]{:S(2)}) collective-permute-start(bf16[256,1024]{1,0:T(8,128)(2,1)S(1)} %shard_map.57), channel_id=1, source_target_pairs={{0,8},{4,12},{8,0},{12,4},{16,24},{20,28},{24,16},{28,20},{1,9},{5... | collective-permute-start | bytes 1572872 | tf_op jit(solution)/shard_map/ppermute | solution.py:255
  55.5 4.2 %collective-permute-start.9 = (bf16[2,256,512]{2,1,0:T(8,128)(2,1)S(1)}, bf16[2,256,512]{2,1,0:T(8,128)(2,1)S(1)}, u32[]{:S(2)}, u32[]{:S(2)}) collective-permute-start(bf16[2,256,512]{2,1,0:T(8,128)(2,1)S(1)} %get-tuple-element.26), channel_id=1, source_target_pairs={{0,1},{1,0},{2,3},{3,2},{4,5},{5,4},{6,7},{7,6},{8,9},{9,8},{10,11... | collective-permute-start | bytes 1572872 | tf_op jit(solution)/shard_map/ppermute | solution.py:259
  58.2 13.5 %collective-permute-start.7 = (bf16[256,1024]{1,0:T(8,128)(2,1)S(1)}, bf16[256,1024]{1,0:T(8,128)(2,1)S(1)}, u32[]{:S(2)}, u32[]{:S(2)}) collective-permute-start(bf16[256,1024]{1,0:T(8,128)(2,1)S(1)} %collective-permute-done.4.tokens_ref), channel_id=1, source_target_pairs={{0,8},{4,12},{8,0},{12,4},{16,24},{20,28},{24,16},{28,20},{1,9},{5... | collective-permute-start | bytes 1572872 | tf_op jit(solution)/shard_map/ppermute | solution.py:255
  59.9 14.5 %collective-permute-start.10 = (bf16[2,256,512]{2,1,0:T(8,128)(2,1)S(1)}, bf16[2,256,512]{2,1,0:T(8,128)(2,1)S(1)}, u32[]{:S(2)}, u32[]{:S(2)}) collective-permute-start(bf16[2,256,512]{2,1,0:T(8,128)(2,1)S(1)} %add_convert_fusion.1), channel_id=1, source_target_pairs={{0,2},{1,3},{2,0},{3,1},{4,6},{5,7},{6,4},{7,5},{8,10},{9,11},{10,... | collective-permute-start | bytes 1572872 | tf_op jit(solution)/shard_map/ppermute | solution.py:259
  73.0 2.5 %collective-permute-start.8 = (bf16[2,256,512]{2,1,0:T(8,128)(2,1)S(1)}, bf16[2,256,512]{2,1,0:T(8,128)(2,1)S(1)}, u32[]{:S(2)}, u32[]{:S(2)}) collective-permute-start(bf16[2,256,512]{2,1,0:T(8,128)(2,1)S(1)} %get-tuple-element.23), channel_id=1, source_target_pairs={{0,1},{1,0},{2,3},{3,2},{4,5},{5,4},{6,7},{7,6},{8,9},{9,8},{10,11... | collective-permute-start | bytes 1572872 | tf_op jit(solution)/shard_map/ppermute | solution.py:259
  75.7 17.7 %collective-permute-start.11 = (bf16[2,256,512]{2,1,0:T(8,128)(2,1)S(1)}, bf16[2,256,512]{2,1,0:T(8,128)(2,1)S(1)}, u32[]{:S(2)}, u32[]{:S(2)}) collective-permute-start(bf16[2,256,512]{2,1,0:T(8,128)(2,1)S(1)} %add_convert_fusion), channel_id=1, source_target_pairs={{0,0},{1,24},{2,8},{3,16},{4,4},{5,28},{6,12},{7,20},{8,9},{9,17},... | collective-permute-start | bytes 1572872 | tf_op jit(solution)/shard_map/ppermute | solution.py:259

commit v19 on v18

--- a/solution.py
+++ b/solution.py
@@ -51,7 +51,22 @@
     return slice(head * HD, (head + 1) * HD)
 
 
-def state_kernel(k_ref, v_ref, wide_ref, narrow_ref):
+def state_kernel(k_hbm, v_hbm, wide_ref, narrow_ref, k_ref, v_ref, done):
+    blocks = done.shape[1]
+    step = k_ref.shape[0] // blocks
+    copies = [
+        pltpu.make_async_copy(
+            hbm.at[block * step : (block + 1) * step],
+            ref.at[block * step : (block + 1) * step],
+            done.at[index, block],
+        )
+        for block in range(blocks)
+        for index, (hbm, ref) in enumerate(((k_hbm, k_ref), (v_hbm, v_ref)))
+    ]
+    for copy in copies:
+        copy.start()
+    for copy in copies:
+        copy.wait()
     for head in range(wide_ref.shape[0]):
         cols = head_slice(head)
         state = lax.dot_general(
@@ -59,6 +74,24 @@
         )
         wide_ref[head] = state
         narrow_ref[head] = state.astype(BF16)
+
+
+def block_states(keys, values):
+    rows, features = keys.shape
+    heads, blocks = features // HD, 4
+    hbm, vmem = (pl.BlockSpec(memory_space=space) for space in (pltpu.HBM, pltpu.VMEM))
+    held = pltpu.VMEM((rows, features), BF16)
+    return pl.pallas_call(
+        state_kernel,
+        out_shape=[jax.ShapeDtypeStruct((heads, HD, HD), kind) for kind in (F32, BF16)],
+        in_specs=[hbm, hbm],
+        out_specs=[vmem, vmem],
+        scratch_shapes=[held, held, pltpu.SemaphoreType.DMA((2, blocks))],
+        compiler_params=pltpu.CompilerParams(vmem_limit_bytes=56 * 1024 * 1024),
+        cost_estimate=pl.CostEstimate(
+            flops=2 * rows * features * HD, bytes_accessed=4 * rows * features, transcendentals=0
+        ),
+    )(keys, values)
 
 
 def within_kernel(q_ref, k_ref, v_ref, out_ref):
@@ -161,15 +194,7 @@
         heads = features // HD
         size = rows * features
         weight = gather_weight(out_weight)
-        wide, narrow = call(
-            state_kernel,
-            (
-                jax.ShapeDtypeStruct((heads, HD, HD), F32),
-                jax.ShapeDtypeStruct((heads, HD, HD), BF16),
-            ),
-            2 * size * HD,
-            4 * size + 6 * heads * HD * HD,
-        )(key_vectors, value_vectors)
+        wide, narrow = block_states(key_vectors, value_vectors)
         within = call(
             within_kernel, jax.ShapeDtypeStruct((rows, features), F32), 4 * size * BLOCK, 10 * size
         )(queries, key_vectors, value_vectors)
@@ -258,15 +283,7 @@
         pairs = [(at(*d), at(*place_of(*d))) for d in devices if chosen(*d)]
         return lax.ppermute(value, both, pairs)
 
-    wide, narrow = call(
-        state_kernel,
-        (
-            jax.ShapeDtypeStruct((heads, HD, HD), F32),
-            jax.ShapeDtypeStruct((heads, HD, HD), BF16),
-        ),
-        2 * size * HD,
-        4 * size + 6 * heads * HD * HD,
-    )(key_vectors, value_vectors)
+    wide, narrow = block_states(key_vectors, value_vectors)
     within = call(
         within_kernel, jax.ShapeDtypeStruct((rows, features), F32), 4 * size * BLOCK, 10 * size
     )(queries, key_vectors, value_vectors)

time: 94.7 us -> 95.1 us (level)
  Pallas kernels: 6.45 us -> 8.68 us
  local copies, waits for them, and re-layouts: 4.18 us -> 3.14 us
    pallas_call x1, Pallas kernels: 0.35 us -> 2.57 us  [block_states(): pl.pallas_call(state_kernel, out_shape=[jax.ShapeDtypeStruct((heads, HD,...]
    unnamed x12, local copies, waits for them, and re-layouts: 4.18 us -> 3.14 us
where the time goes in v19:
time: 95.1 us; the launch traced here: 94.7 us
  waiting for transfers between devices  47.8 us (50%)
  starting transfers between devices  33.3 us (35%)
  Pallas kernels  8.68 us (9%)
  local copies, waits for them, and re-layouts  3.14 us (3%)
  other arithmetic  1.6 us (2%)
    ppermute x5, waiting for transfers between devices, move(): return lax.ppermute(value, both, pairs)  25.8 us
    ppermute x5, starting transfers between devices, move(): return lax.ppermute(value, both, pairs)  22.5 us
    ppermute x4, waiting for transfers between devices, swap(): return lax.ppermute(value, 'seq', [(s, s ^ mask) for s in range(8)])  17.9 us
    ppermute x4, starting transfers between devices, swap(): return lax.ppermute(value, 'seq', [(s, s ^ mask) for s in range(8)])  6.42 us
    ppermute x3, starting transfers between devices, pairs_body(): earlier.append(lax.ppermute(onward.astype(BF16), 'seq', pairs))  4.47 us
    ppermute x3, waiting for transfers between devices, pairs_body(): earlier.append(lax.ppermute(onward.astype(BF16), 'seq', pairs))  4.02 us
    unnamed x12, local copies, waits for them, and re-layouts  3.14 us
    pallas_call x1, Pallas kernels, block_states(): pl.pallas_call(state_kernel, out_shape=[jax.ShapeDtypeStruct((heads, HD,...  2.57 us
  transfers between devices with their start and end apart: 12, of which 9 were waited for; matrix products, arithmetic and copies ran while one was open for 0% of the time, Pallas kernels for 6%

profile of v19, /device:TPU:1, one launch (start us, length us, event | category | flops | bytes accessed | tf_op | source)
XLA Modules:
  0.0 94.7 jit_solution(15542422702855084894)
XLA Ops:
  0.0 2.6 %shard_map.55 = (f32[8,128,128]{2,1,0:T(8,128)}, bf16[8,128,128]{2,1,0:T(8,128)(2,1)}) custom-call(bf16[256,1024]{1,0:T(8,128)(2,1)} %k_ref.1, bf16[256,1024]{1,0:T(8,128)(2,1)} %v_ref.1), custom_call_target="tpu_custom_call" | custom-call | flops 67108864 | bytes 1048576 | tf_op jit(solution)/shard_map/pallas_call | solution.py:84
  2.6 2.1 %collective-permute-start = (bf16[8,128,128]{2,1,0:T(8,128)(2,1)}, bf16[8,128,128]{2,1,0:T(8,128)(2,1)S(1)}, u32[]{:S(2)}, u32[]{:S(2)}) collective-permute-start(bf16[8,128,128]{2,1,0:T(8,128)(2,1)} %get-tuple-element.16), channel_id=1, source_target_pairs={{0,4},{4,0},{8,12},{12,8},{16,20},{20,16},{24,28},{28,24},{1,5},{5... | collective-permute-start | bytes 786440 | tf_op jit(solution)/shard_map/ppermute | solution.py:280
  4.7 0.0 copy-start
  4.7 1.0 %copy-done = bf16[256,1024]{1,0:T(8,128)(2,1)S(1)} copy-done((bf16[256,1024]{1,0:T(8,128)(2,1)S(1)}, bf16[256,1024]{1,0:T(8,128)(2,1)}, u32[]{:S(2)}) %copy-start) | copy-done | bytes 524312
  5.8 0.0 copy-start.1
  5.8 1.0 %copy-done.1 = bf16[256,1024]{1,0:T(8,128)(2,1)S(1)} copy-done((bf16[256,1024]{1,0:T(8,128)(2,1)S(1)}, bf16[256,1024]{1,0:T(8,128)(2,1)}, u32[]{:S(2)}) %copy-start.1) | copy-done | bytes 524312
  6.8 0.0 copy-start.2
  6.8 1.0 %copy-done.2 = bf16[256,1024]{1,0:T(8,128)(2,1)S(1)} copy-done((bf16[256,1024]{1,0:T(8,128)(2,1)S(1)}, bf16[256,1024]{1,0:T(8,128)(2,1)}, u32[]{:S(2)}) %copy-start.2) | copy-done | bytes 524312
  7.8 0.0 copy-start.5
  7.8 0.9 shard_map.56.within_ref
  8.8 0.0 copy-start.3
  8.8 0.0 copy-start.4
  8.8 2.2 %collective-permute-done.mate_ref = bf16[8,128,128]{2,1,0:T(8,128)(2,1)S(1)} collective-permute-done((bf16[8,128,128]{2,1,0:T(8,128)(2,1)}, bf16[8,128,128]{2,1,0:T(8,128)(2,1)S(1)}, u32[]{:S(2)}, u32[]{:S(2)}) %collective-permute-start) | collective-permute-done | bytes 262176 | tf_op jit(solution)/shard_map/ppermute | solution.py:280
  11.0 0.0 copy-done.5
  11.0 0.1 fusion
  11.0 3.1 %collective-permute-start.1 = (bf16[8,128,128]{2,1,0:T(8,128)(2,1)S(1)}, bf16[8,128,128]{2,1,0:T(8,128)(2,1)S(1)}, u32[]{:S(2)}, u32[]{:S(2)}) collective-permute-start(bf16[8,128,128]{2,1,0:T(8,128)(2,1)S(1)} %fusion), channel_id=1, source_target_pairs={{0,8},{4,12},{1,9},{5,13},{2,10},{6,14},{3,11},{7,15}} | collective-permute-start | bytes 786440 | tf_op jit(solution)/shard_map/ppermute | solution.py:298
  14.1 4.0 %collective-permute-done.1.refs_0_ = bf16[8,128,128]{2,1,0:T(8,128)(2,1)S(1)} collective-permute-done((bf16[8,128,128]{2,1,0:T(8,128)(2,1)S(1)}, bf16[8,128,128]{2,1,0:T(8,128)(2,1)S(1)}, u32[]{:S(2)}, u32[]{:S(2)}) %collective-permute-start.1) | collective-permute-done | bytes 262176 | tf_op jit(solution)/shard_map/ppermute | solution.py:298
  18.2 0.1 fusion.1
  18.3 0.7 collective-permute-start.2
  18.9 1.3 %collective-permute-start.5 = (bf16[1024,512]{1,0:T(8,128)(2,1)}, bf16[1024,512]{1,0:T(8,128)(2,1)}, u32[]{:S(2)}, u32[]{:S(2)}) collective-permute-start(bf16[1024,512]{1,0:T(8,128)(2,1)} %own_ref.1), channel_id=1, source_target_pairs={{0,4},{4,0},{8,12},{12,8},{16,20},{20,16},{24,28},{28,24},{1,5},{5... | collective-permute-start | bytes 3145736 | tf_op jit(solution)/shard_map/ppermute | solution.py:280
  20.3 0.0 collective-permute-done.2.refs_1_
  20.3 0.1 add_convert_fusion.2
  20.4 0.7 collective-permute-start.3
  21.1 0.0 collective-permute-done.3.refs_2_
  21.1 0.0 copy-done.3
  21.1 0.0 copy-done.4
  21.1 0.8 shard_map.57
  21.9 10.8 %collective-permute-start.4 = (bf16[256,1024]{1,0:T(8,128)(2,1)S(1)}, bf16[256,1024]{1,0:T(8,128)(2,1)S(1)}, u32[]{:S(2)}, u32[]{:S(2)}) collective-permute-start(bf16[256,1024]{1,0:T(8,128)(2,1)S(1)} %shard_map.57), channel_id=1, source_target_pairs={{0,16},{1,17},{2,26},{3,27},{4,20},{5,21},{6,30},{7,31},{8,24},{9,... | collective-permute-start | bytes 1572872 | tf_op jit(solution)/shard_map/ppermute | solution.py:284
  32.7 2.3 %collective-permute-start.6 = (bf16[256,1024]{1,0:T(8,128)(2,1)S(1)}, bf16[256,1024]{1,0:T(8,128)(2,1)S(1)}, u32[]{:S(2)}, u32[]{:S(2)}) collective-permute-start(bf16[256,1024]{1,0:T(8,128)(2,1)S(1)} %shard_map.57), channel_id=1, source_target_pairs={{0,8},{4,12},{8,0},{12,4},{16,24},{20,28},{24,16},{28,20},{1,9},{5... | collective-permute-start | bytes 1572872 | tf_op jit(solution)/shard_map/ppermute | solution.py:280
  35.0 6.5 %collective-permute-done.5.mate_ref = bf16[1024,512]{1,0:T(8,128)(2,1)} collective-permute-done((bf16[1024,512]{1,0:T(8,128)(2,1)}, bf16[1024,512]{1,0:T(8,128)(2,1)}, u32[]{:S(2)}, u32[]{:S(2)}) %collective-permute-start.5) | collective-permute-done | bytes 1048608 | tf_op jit(solution)/shard_map/ppermute | solution.py:280
  41.5 1.7 %shard_map.58.weight_ref = bf16[2,1024,512]{2,1,0:T(8,128)(2,1)S(1)} custom-call(bf16[1024,512]{1,0:T(8,128)(2,1)} %own_ref.1, bf16[1024,512]{1,0:T(8,128)(2,1)} %collective-permute-done.5.mate_ref), custom_call_target="tpu_custom_call" | custom-call | bytes 4194304 | tf_op jit(solution)/shard_map/pallas_call | solution.py:303
  43.2 11.1 %collective-permute-done.4.tokens_ref = bf16[256,1024]{1,0:T(8,128)(2,1)S(1)} collective-permute-done((bf16[256,1024]{1,0:T(8,128)(2,1)S(1)}, bf16[256,1024]{1,0:T(8,128)(2,1)S(1)}, u32[]{:S(2)}, u32[]{:S(2)}) %collective-permute-start.4) | collective-permute-done | bytes 524320 | tf_op jit(solution)/shard_map/ppermute | solution.py:284
  54.3 0.7 shard_map.59.heavy_ref
  55.0 0.0 collective-permute-done.6
  55.0 0.1 broadcast_select_fusion.1
  55.1 0.7 shard_map.61
  55.8 2.7 %collective-permute-start.9 = (bf16[2,256,512]{2,1,0:T(8,128)(2,1)S(1)}, bf16[2,256,512]{2,1,0:T(8,128)(2,1)S(1)}, u32[]{:S(2)}, u32[]{:S(2)}) collective-permute-start(bf16[2,256,512]{2,1,0:T(8,128)(2,1)S(1)} %get-tuple-element.26), channel_id=1, source_target_pairs={{0,1},{1,0},{2,3},{3,2},{4,5},{5,4},{6,7},{7,6},{8,9},{9,8},{10,11... | collective-permute-start | bytes 1572872 | tf_op jit(solution)/shard_map/ppermute | solution.py:284
  58.6 0.7 collective-permute-start.7
  59.2 0.9 collective-permute-done.9
  60.1 0.1 add_convert_fusion.1
  60.2 2.6 %collective-permute-start.10 = (bf16[2,256,512]{2,1,0:T(8,128)(2,1)S(1)}, bf16[2,256,512]{2,1,0:T(8,128)(2,1)S(1)}, u32[]{:S(2)}, u32[]{:S(2)}) collective-permute-start(bf16[2,256,512]{2,1,0:T(8,128)(2,1)S(1)} %add_convert_fusion.1), channel_id=1, source_target_pairs={{0,2},{1,3},{2,0},{3,1},{4,6},{5,7},{6,4},{7,5},{8,10},{9,11},{10,... | collective-permute-start | bytes 1572872 | tf_op jit(solution)/shard_map/ppermute | solution.py:284
  62.8 9.3 %collective-permute-done.7.heavy_ref = bf16[256,1024]{1,0:T(8,128)(2,1)S(1)} collective-permute-done((bf16[256,1024]{1,0:T(8,128)(2,1)S(1)}, bf16[256,1024]{1,0:T(8,128)(2,1)S(1)}, u32[]{:S(2)}, u32[]{:S(2)}) %collective-permute-start.7) | collective-permute-done | bytes 524320 | tf_op jit(solution)/shard_map/ppermute | solution.py:280
  72.1 1.3 %shard_map.60 = (bf16[2,256,512]{2,1,0:T(8,128)(2,1)S(1)}, bf16[2,256,512]{2,1,0:T(8,128)(2,1)S(1)}) custom-call(s32[1]{0:T(128)} %bitcast.core_ref, bf16[256,1024]{1,0:T(8,128)(2,1)S(1)} %get-tuple-element.27.light_ref, bf16[256,1024]{1,0:T(8,128)(2,1)S(1)} %collective-permute-done.7.heavy_ref, bf16[2,1024,512]{2,1,0:T(8,128)(2,1)S(1)} %shard_map.58.weight_ref), custom_call_target="tpu_custom_call" | custom-call | flops 1073741824 | bytes 4194304 | tf_op jit(solution)/shard_map/pallas_call | solution.py:316
  73.4 0.9 collective-permute-start.8
  74.3 0.5 collective-permute-done.10
  74.8 1.0 %collective-permute-done.8 = bf16[2,256,512]{2,1,0:T(8,128)(2,1)S(1)} collective-permute-done((bf16[2,256,512]{2,1,0:T(8,128)(2,1)S(1)}, bf16[2,256,512]{2,1,0:T(8,128)(2,1)S(1)}, u32[]{:S(2)}, u32[]{:S(2)}) %collective-permute-start.8) | collective-permute-done | bytes 524320 | tf_op jit(solution)/shard_map/ppermute | solution.py:284
  75.8 0.2 add_convert_fusion
  76.0 5.4 %collective-permute-start.11 = (bf16[2,256,512]{2,1,0:T(8,128)(2,1)S(1)}, bf16[2,256,512]{2,1,0:T(8,128)(2,1)S(1)}, u32[]{:S(2)}, u32[]{:S(2)}) collective-permute-start(bf16[2,256,512]{2,1,0:T(8,128)(2,1)S(1)} %add_convert_fusion), channel_id=1, source_target_pairs={{0,0},{1,24},{2,8},{3,16},{4,4},{5,28},{6,12},{7,20},{8,9},{9,17},... | collective-permute-start | bytes 1572872 | tf_op jit(solution)/shard_map/ppermute | solution.py:284
  81.5 12.3 %collective-permute-done.11 = bf16[2,256,512]{2,1,0:T(8,128)(2,1)S(1)} collective-permute-done((bf16[2,256,512]{2,1,0:T(8,128)(2,1)S(1)}, bf16[2,256,512]{2,1,0:T(8,128)(2,1)S(1)}, u32[]{:S(2)}, u32[]{:S(2)}) %collective-permute-start.11) | collective-permute-done | bytes 524320 | tf_op jit(solution)/shard_map/ppermute | solution.py:284
  93.8 0.9 pad_maximum_fusion
  (1 shorter events, 0.0 us)
Async XLA Ops:
  2.6 8.4 %collective-permute-start = (bf16[8,128,128]{2,1,0:T(8,128)(2,1)}, bf16[8,128,128]{2,1,0:T(8,128)(2,1)S(1)}, u32[]{:S(2)}, u32[]{:S(2)}) collective-permute-start(bf16[8,128,128]{2,1,0:T(8,128)(2,1)} %get-tuple-element.16), channel_id=1, source_target_pairs={{0,4},{4,0},{8,12},{12,8},{16,20},{20,16},{24,28},{28,24},{1,5},{5... | collective-permute-start | bytes 786440 | tf_op jit(solution)/shard_map/ppermute | solution.py:280
  4.7 1.0 %copy-start = (bf16[256,1024]{1,0:T(8,128)(2,1)S(1)}, bf16[256,1024]{1,0:T(8,128)(2,1)}, u32[]{:S(2)}) copy-start(bf16[256,1024]{1,0:T(8,128)(2,1)} %k_ref.1) | copy-start | bytes 1572868
  5.8 1.0 %copy-start.1 = (bf16[256,1024]{1,0:T(8,128)(2,1)S(1)}, bf16[256,1024]{1,0:T(8,128)(2,1)}, u32[]{:S(2)}) copy-start(bf16[256,1024]{1,0:T(8,128)(2,1)} %v_ref.1) | copy-start | bytes 1572868
  6.8 1.0 %copy-start.2 = (bf16[256,1024]{1,0:T(8,128)(2,1)S(1)}, bf16[256,1024]{1,0:T(8,128)(2,1)}, u32[]{:S(2)}) copy-start(bf16[256,1024]{1,0:T(8,128)(2,1)} %q_ref.3) | copy-start | bytes 1572868
  7.8 3.1 %copy-start.5 = (f32[8,128,128]{2,1,0:T(8,128)S(1)}, f32[8,128,128]{2,1,0:T(8,128)}, u32[]{:S(2)}) copy-start(f32[8,128,128]{2,1,0:T(8,128)} %get-tuple-element.19) | copy-start | bytes 1572868
  8.8 12.3 %copy-start.3 = (bf16[256,1024]{1,0:T(8,128)(2,1)S(1)}, bf16[256,1024]{1,0:T(8,128)(2,1)}, u32[]{:S(2)}) copy-start(bf16[256,1024]{1,0:T(8,128)(2,1)} %q_ref.3) | copy-start | bytes 1572868
  8.8 12.3 %copy-start.4 = (f32[1024]{0:T(1024)S(1)}, f32[1024]{0:T(1024)}, u32[]{:S(2)}) copy-start(f32[1024]{0:T(1024)} %param.8) | copy-start | bytes 12292
  11.0 7.1 %collective-permute-start.1 = (bf16[8,128,128]{2,1,0:T(8,128)(2,1)S(1)}, bf16[8,128,128]{2,1,0:T(8,128)(2,1)S(1)}, u32[]{:S(2)}, u32[]{:S(2)}) collective-permute-start(bf16[8,128,128]{2,1,0:T(8,128)(2,1)S(1)} %fusion), channel_id=1, source_target_pairs={{0,8},{4,12},{1,9},{5,13},{2,10},{6,14},{3,11},{7,15}} | collective-permute-start | bytes 786440 | tf_op jit(solution)/shard_map/ppermute | solution.py:298
  18.3 2.0 %collective-permute-start.2 = (bf16[8,128,128]{2,1,0:T(8,128)(2,1)S(1)}, bf16[8,128,128]{2,1,0:T(8,128)(2,1)S(1)}, u32[]{:S(2)}, u32[]{:S(2)}) collective-permute-start(bf16[8,128,128]{2,1,0:T(8,128)(2,1)S(1)} %fusion.1), channel_id=1, source_target_pairs={{8,16},{12,20},{9,17},{13,21},{10,18},{14,22},{11,19},{15,23}} | collective-permute-start | bytes 786440 | tf_op jit(solution)/shard_map/ppermute | solution.py:298
  18.9 22.6 %collective-permute-start.5 = (bf16[1024,512]{1,0:T(8,128)(2,1)}, bf16[1024,512]{1,0:T(8,128)(2,1)}, u32[]{:S(2)}, u32[]{:S(2)}) collective-permute-start(bf16[1024,512]{1,0:T(8,128)(2,1)} %own_ref.1), channel_id=1, source_target_pairs={{0,4},{4,0},{8,12},{12,8},{16,20},{20,16},{24,28},{28,24},{1,5},{5... | collective-permute-start | bytes 3145736 | tf_op jit(solution)/shard_map/ppermute | solution.py:280
  20.4 0.7 collective-permute-start.3
  21.9 32.4 %collective-permute-start.4 = (bf16[256,1024]{1,0:T(8,128)(2,1)S(1)}, bf16[256,1024]{1,0:T(8,128)(2,1)S(1)}, u32[]{:S(2)}, u32[]{:S(2)}) collective-permute-start(bf16[256,1024]{1,0:T(8,128)(2,1)S(1)} %shard_map.57), channel_id=1, source_target_pairs={{0,16},{1,17},{2,26},{3,27},{4,20},{5,21},{6,30},{7,31},{8,24},{9,... | collective-permute-start | bytes 1572872 | tf_op jit(solution)/shard_map/ppermute | solution.py:284
  32.7 22.3 %collective-permute-start.6 = (bf16[256,1024]{1,0:T(8,128)(2,1)S(1)}, bf16[256,1024]{1,0:T(8,128)(2,1)S(1)}, u32[]{:S(2)}, u32[]{:S(2)}) collective-permute-start(bf16[256,1024]{1,0:T(8,128)(2,1)S(1)} %shard_map.57), channel_id=1, source_target_pairs={{0,8},{4,12},{8,0},{12,4},{16,24},{20,28},{24,16},{28,20},{1,9},{5... | collective-permute-start | bytes 1572872 | tf_op jit(solution)/shard_map/ppermute | solution.py:280
  55.8 4.2 %collective-permute-start.9 = (bf16[2,256,512]{2,1,0:T(8,128)(2,1)S(1)}, bf16[2,256,512]{2,1,0:T(8,128)(2,1)S(1)}, u32[]{:S(2)}, u32[]{:S(2)}) collective-permute-start(bf16[2,256,512]{2,1,0:T(8,128)(2,1)S(1)} %get-tuple-element.26), channel_id=1, source_target_pairs={{0,1},{1,0},{2,3},{3,2},{4,5},{5,4},{6,7},{7,6},{8,9},{9,8},{10,11... | collective-permute-start | bytes 1572872 | tf_op jit(solution)/shard_map/ppermute | solution.py:284
  58.6 13.5 %collective-permute-start.7 = (bf16[256,1024]{1,0:T(8,128)(2,1)S(1)}, bf16[256,1024]{1,0:T(8,128)(2,1)S(1)}, u32[]{:S(2)}, u32[]{:S(2)}) collective-permute-start(bf16[256,1024]{1,0:T(8,128)(2,1)S(1)} %collective-permute-done.4.tokens_ref), channel_id=1, source_target_pairs={{0,8},{4,12},{8,0},{12,4},{16,24},{20,28},{24,16},{28,20},{1,9},{5... | collective-permute-start | bytes 1572872 | tf_op jit(solution)/shard_map/ppermute | solution.py:280
  60.2 14.6 %collective-permute-start.10 = (bf16[2,256,512]{2,1,0:T(8,128)(2,1)S(1)}, bf16[2,256,512]{2,1,0:T(8,128)(2,1)S(1)}, u32[]{:S(2)}, u32[]{:S(2)}) collective-permute-start(bf16[2,256,512]{2,1,0:T(8,128)(2,1)S(1)} %add_convert_fusion.1), channel_id=1, source_target_pairs={{0,2},{1,3},{2,0},{3,1},{4,6},{5,7},{6,4},{7,5},{8,10},{9,11},{10,... | collective-permute-start | bytes 1572872 | tf_op jit(solution)/shard_map/ppermute | solution.py:284
  73.4 2.5 %collective-permute-start.8 = (bf16[2,256,512]{2,1,0:T(8,128)(2,1)S(1)}, bf16[2,256,512]{2,1,0:T(8,128)(2,1)S(1)}, u32[]{:S(2)}, u32[]{:S(2)}) collective-permute-start(bf16[2,256,512]{2,1,0:T(8,128)(2,1)S(1)} %get-tuple-element.23), channel_id=1, source_target_pairs={{0,1},{1,0},{2,3},{3,2},{4,5},{5,4},{6,7},{7,6},{8,9},{9,8},{10,11... | collective-permute-start | bytes 1572872 | tf_op jit(solution)/shard_map/ppermute | solution.py:284
  76.0 17.8 %collective-permute-start.11 = (bf16[2,256,512]{2,1,0:T(8,128)(2,1)S(1)}, bf16[2,256,512]{2,1,0:T(8,128)(2,1)S(1)}, u32[]{:S(2)}, u32[]{:S(2)}) collective-permute-start(bf16[2,256,512]{2,1,0:T(8,128)(2,1)S(1)} %add_convert_fusion), channel_id=1, source_target_pairs={{0,0},{1,24},{2,8},{3,16},{4,4},{5,28},{6,12},{7,20},{8,9},{9,17},... | collective-permute-start | bytes 1572872 | tf_op jit(solution)/shard_map/ppermute | solution.py:284

commit v20 on v16

--- a/solution.py
+++ b/solution.py
@@ -211,19 +211,16 @@
         out_ref[half] = product.astype(BF16)
 
 
-def project_pair_kernel(core_ref, light_ref, heavy_ref, weight_ref, keep_ref, send_ref):
-    def multiply(out_ref, tokens_ref):
-        project_kernel(tokens_ref, weight_ref, out_ref)
-
+def project_heavy_kernel(core_ref, light_ref, heavy_ref, weight_ref, keep_ref, send_ref):
     @pl.when(core_ref[0] == 0)
     def _():
-        multiply(send_ref, heavy_ref)
-        multiply(keep_ref, light_ref)
+        project_kernel(heavy_ref, weight_ref, send_ref)
+        keep_ref[...] = light_ref[...]
 
     @pl.when(core_ref[0] != 0)
     def _():
-        multiply(send_ref, light_ref)
-        multiply(keep_ref, heavy_ref)
+        project_kernel(heavy_ref, weight_ref, keep_ref)
+        send_ref[...] = light_ref[...]
 
 
 def pairs_body(queries, key_vectors, value_vectors, norm_gain, out_weight):
@@ -285,7 +282,7 @@
 
     def projected(light, heavy):
         keep, send = pl.pallas_call(
-            project_pair_kernel,
+            project_heavy_kernel,
             out_shape=(tile, tile),
             in_specs=[pl.BlockSpec(memory_space=pltpu.SMEM)] + [vmem] * 3,
             out_specs=(vmem, vmem),
@@ -296,9 +293,14 @@
         )(core.astype(jnp.int32)[None], light, heavy, weight)
         return keep.astype(F32) + move(send, lambda z, y, x, c: (z, y, x, 1 - c)).astype(F32)
 
-    far = projected(jnp.where(x == 0, beside, attended), straight).astype(BF16)
+    def product(tokens):
+        return call(project_kernel, tile, flops, moved)(tokens, weight)
+
+    far_light = product(jnp.where(x == 0, beside, attended))
+    far = projected(far_light, straight).astype(BF16)
     crossed = move(far, lambda z, y, x, c: (z, y, 1 - x, c))
-    near = projected(jnp.where(x == 0, attended, beside), onward) + crossed.astype(F32)
+    near_light = product(jnp.where(x == 0, attended, beside))
+    near = projected(near_light, onward) + crossed.astype(F32)
     result = move(near.astype(BF16), lambda z, y, x, c: (z ^ 3 * c ^ x, y, z // 2, z % 2))
     first = jnp.where(y == 0, result[0], result[1])
     return jnp.concatenate([first, jnp.where(y == 0, result[1], result[0])], axis=1)

time: 94.8 us -> 93.7 us (0.988)
  waiting for transfers between devices: 42.4 us -> 40.9 us
    ppermute x5, waiting for transfers between devices: 18.1 us -> 16.7 us  [move(): return lax.ppermute(value, both, pairs)]
    pallas_call x2 -> x4, Pallas kernels: 2.57 us -> 2.9 us  [the longest x2 1.45 us: projected(): pl.pallas_call(project_heavy_kernel, out_shape=(tile, tile), in_specs=[pl...]
  transfers between devices with their start and end apart: 12 -> 12, of which waited for: 8 -> 8; matrix products, arithmetic and copies ran while one was open for 0% -> 0% of each run, Pallas kernels for 5% -> 6%
where the time goes in v20:
time: 93.7 us; the launch traced here: 93.3 us
  waiting for transfers between devices  40.9 us (44%)
  starting transfers between devices  39.8 us (42%)
  Pallas kernels  6.61 us (7%)
  local copies, waits for them, and re-layouts  4.18 us (4%)
  other arithmetic  1.6 us (2%)
    ppermute x5, starting transfers between devices, move(): return lax.ppermute(value, both, pairs)  27 us
    ppermute x4, waiting for transfers between devices, swap(): return lax.ppermute(value, 'seq', [(s, s ^ mask) for s in range(8)])  20.2 us
    ppermute x5, waiting for transfers between devices, move(): return lax.ppermute(value, both, pairs)  16.7 us
    ppermute x4, starting transfers between devices, swap(): return lax.ppermute(value, 'seq', [(s, s ^ mask) for s in range(8)])  8.38 us
    ppermute x3, starting transfers between devices, pairs_body(): earlier.append(lax.ppermute(onward.astype(BF16), 'seq', pairs))  4.47 us
    unnamed x12, local copies, waits for them, and re-layouts  4.18 us
    ppermute x3, waiting for transfers between devices, pairs_body(): earlier.append(lax.ppermute(onward.astype(BF16), 'seq', pairs))  4.02 us
  transfers between devices with their start and end apart: 12, of which 8 were waited for; matrix products, arithmetic and copies ran while one was open for 0% of the time, Pallas kernels for 6%

profile of v20, /device:TPU:1, one launch (start us, length us, event | category | flops | bytes accessed | tf_op | source)
XLA Modules:
  0.0 93.3 jit_solution(6821683415272195264)
XLA Ops:
  0.0 0.0 copy-start
  0.0 1.0 %copy-done = bf16[256,1024]{1,0:T(8,128)(2,1)S(1)} copy-done((bf16[256,1024]{1,0:T(8,128)(2,1)S(1)}, bf16[256,1024]{1,0:T(8,128)(2,1)}, u32[]{:S(2)}) %copy-start) | copy-done | bytes 524312
  1.0 0.0 copy-start.2
  1.0 1.0 %copy-done.2 = bf16[256,1024]{1,0:T(8,128)(2,1)S(1)} copy-done((bf16[256,1024]{1,0:T(8,128)(2,1)S(1)}, bf16[256,1024]{1,0:T(8,128)(2,1)}, u32[]{:S(2)}) %copy-start.2) | copy-done | bytes 524312
  2.1 0.4 shard_map.55
  2.4 2.1 %collective-permute-start = (bf16[8,128,128]{2,1,0:T(8,128)(2,1)S(1)}, bf16[8,128,128]{2,1,0:T(8,128)(2,1)S(1)}, u32[]{:S(2)}, u32[]{:S(2)}) collective-permute-start(bf16[8,128,128]{2,1,0:T(8,128)(2,1)S(1)} %get-tuple-element.14), channel_id=1, source_target_pairs={{0,4},{4,0},{8,12},{12,8},{16,20},{20,16},{24,28},{28,24},{1,5},{5... | collective-permute-start | bytes 786440 | tf_op jit(solution)/shard_map/ppermute | solution.py:240
  4.6 0.0 copy-start.1
  4.6 1.0 %copy-done.1 = bf16[256,1024]{1,0:T(8,128)(2,1)S(1)} copy-done((bf16[256,1024]{1,0:T(8,128)(2,1)S(1)}, bf16[256,1024]{1,0:T(8,128)(2,1)}, u32[]{:S(2)}) %copy-start.1) | copy-done | bytes 524312
  5.6 0.0 copy-start.3
  5.6 1.0 %copy-done.3 = bf16[256,1024]{1,0:T(8,128)(2,1)S(1)} copy-done((bf16[256,1024]{1,0:T(8,128)(2,1)S(1)}, bf16[256,1024]{1,0:T(8,128)(2,1)}, u32[]{:S(2)}) %copy-start.3) | copy-done | bytes 524312
  6.7 0.9 shard_map.56.within_ref
  7.6 0.0 copy-start.4
  7.6 0.0 copy-start.5
  7.6 3.0 %collective-permute-done.mate_ref = bf16[8,128,128]{2,1,0:T(8,128)(2,1)S(1)} collective-permute-done((bf16[8,128,128]{2,1,0:T(8,128)(2,1)S(1)}, bf16[8,128,128]{2,1,0:T(8,128)(2,1)S(1)}, u32[]{:S(2)}, u32[]{:S(2)}) %collective-permute-start) | collective-permute-done | bytes 262176 | tf_op jit(solution)/shard_map/ppermute | solution.py:240
  10.6 0.1 fusion
  10.7 3.1 %collective-permute-start.1 = (bf16[8,128,128]{2,1,0:T(8,128)(2,1)S(1)}, bf16[8,128,128]{2,1,0:T(8,128)(2,1)S(1)}, u32[]{:S(2)}, u32[]{:S(2)}) collective-permute-start(bf16[8,128,128]{2,1,0:T(8,128)(2,1)S(1)} %fusion), channel_id=1, source_target_pairs={{0,8},{4,12},{1,9},{5,13},{2,10},{6,14},{3,11},{7,15}} | collective-permute-start | bytes 786440 | tf_op jit(solution)/shard_map/ppermute | solution.py:266
  13.8 4.0 %collective-permute-done.1.refs_0_ = bf16[8,128,128]{2,1,0:T(8,128)(2,1)S(1)} collective-permute-done((bf16[8,128,128]{2,1,0:T(8,128)(2,1)S(1)}, bf16[8,128,128]{2,1,0:T(8,128)(2,1)S(1)}, u32[]{:S(2)}, u32[]{:S(2)}) %collective-permute-start.1) | collective-permute-done | bytes 262176 | tf_op jit(solution)/shard_map/ppermute | solution.py:266
  17.8 0.1 fusion.1
  17.9 0.7 collective-permute-start.2
  18.6 1.3 %collective-permute-start.5 = (bf16[1024,512]{1,0:T(8,128)(2,1)}, bf16[1024,512]{1,0:T(8,128)(2,1)}, u32[]{:S(2)}, u32[]{:S(2)}) collective-permute-start(bf16[1024,512]{1,0:T(8,128)(2,1)} %own_ref.1), channel_id=1, source_target_pairs={{0,4},{4,0},{8,12},{12,8},{16,20},{20,16},{24,28},{28,24},{1,5},{5... | collective-permute-start | bytes 3145736 | tf_op jit(solution)/shard_map/ppermute | solution.py:240
  19.9 0.0 collective-permute-done.2.refs_1_
  19.9 0.1 add_convert_fusion.2
  20.0 0.7 collective-permute-start.3
  20.7 0.0 collective-permute-done.3.refs_2_
  20.7 0.0 copy-done.4
  20.7 0.0 copy-done.5
  20.8 0.8 shard_map.57
  21.5 4.9 %collective-permute-start.4 = (bf16[256,1024]{1,0:T(8,128)(2,1)S(1)}, bf16[256,1024]{1,0:T(8,128)(2,1)S(1)}, u32[]{:S(2)}, u32[]{:S(2)}) collective-permute-start(bf16[256,1024]{1,0:T(8,128)(2,1)S(1)} %shard_map.57), channel_id=1, source_target_pairs={{0,8},{4,12},{8,0},{12,4},{16,24},{20,28},{24,16},{28,20},{1,9},{5... | collective-permute-start | bytes 1572872 | tf_op jit(solution)/shard_map/ppermute | solution.py:240
  26.4 8.3 %collective-permute-start.6 = (bf16[256,1024]{1,0:T(8,128)(2,1)S(1)}, bf16[256,1024]{1,0:T(8,128)(2,1)S(1)}, u32[]{:S(2)}, u32[]{:S(2)}) collective-permute-start(bf16[256,1024]{1,0:T(8,128)(2,1)S(1)} %shard_map.57), channel_id=1, source_target_pairs={{0,16},{1,17},{2,26},{3,27},{4,20},{5,21},{6,30},{7,31},{8,24},{9,... | collective-permute-start | bytes 1572872 | tf_op jit(solution)/shard_map/ppermute | solution.py:244
  34.7 6.5 %collective-permute-done.5.mate_ref = bf16[1024,512]{1,0:T(8,128)(2,1)} collective-permute-done((bf16[1024,512]{1,0:T(8,128)(2,1)}, bf16[1024,512]{1,0:T(8,128)(2,1)}, u32[]{:S(2)}, u32[]{:S(2)}) %collective-permute-start.5) | collective-permute-done | bytes 1048608 | tf_op jit(solution)/shard_map/ppermute | solution.py:240
  41.2 1.7 %shard_map.58.weight_ref = bf16[2,1024,512]{2,1,0:T(8,128)(2,1)S(1)} custom-call(bf16[1024,512]{1,0:T(8,128)(2,1)} %own_ref.1, bf16[1024,512]{1,0:T(8,128)(2,1)} %collective-permute-done.5.mate_ref), custom_call_target="tpu_custom_call" | custom-call | bytes 4194304 | tf_op jit(solution)/shard_map/pallas_call | solution.py:271
  42.8 0.0 collective-permute-done.4
  42.9 0.1 broadcast_select_fusion.1
  42.9 0.7 shard_map.61.light_ref
  43.7 2.9 %collective-permute-done.6.heavy_ref = bf16[256,1024]{1,0:T(8,128)(2,1)S(1)} collective-permute-done((bf16[256,1024]{1,0:T(8,128)(2,1)S(1)}, bf16[256,1024]{1,0:T(8,128)(2,1)S(1)}, u32[]{:S(2)}, u32[]{:S(2)}) %collective-permute-start.6) | collective-permute-done | bytes 524320 | tf_op jit(solution)/shard_map/ppermute | solution.py:244
  46.5 0.7 shard_map.62
  47.3 12.4 %collective-permute-start.9 = (bf16[2,256,512]{2,1,0:T(8,128)(2,1)S(1)}, bf16[2,256,512]{2,1,0:T(8,128)(2,1)S(1)}, u32[]{:S(2)}, u32[]{:S(2)}) collective-permute-start(bf16[2,256,512]{2,1,0:T(8,128)(2,1)S(1)} %get-tuple-element.22), channel_id=1, source_target_pairs={{0,1},{1,0},{2,3},{3,2},{4,5},{5,4},{6,7},{7,6},{8,9},{9,8},{10,11... | collective-permute-start | bytes 1572872 | tf_op jit(solution)/shard_map/ppermute | solution.py:244
  59.6 0.1 collective-permute-start.7
  59.7 0.7 shard_map.59.light_ref
  60.5 0.7 collective-permute-done.9
  61.2 0.1 add_convert_fusion.1
  61.3 1.1 %collective-permute-start.10 = (bf16[2,256,512]{2,1,0:T(8,128)(2,1)S(1)}, bf16[2,256,512]{2,1,0:T(8,128)(2,1)S(1)}, u32[]{:S(2)}, u32[]{:S(2)}) collective-permute-start(bf16[2,256,512]{2,1,0:T(8,128)(2,1)S(1)} %add_convert_fusion.1), channel_id=1, source_target_pairs={{0,2},{1,3},{2,0},{3,1},{4,6},{5,7},{6,4},{7,5},{8,10},{9,11},{10,... | collective-permute-start | bytes 1572872 | tf_op jit(solution)/shard_map/ppermute | solution.py:244
  62.4 10.8 %collective-permute-done.7.heavy_ref = bf16[256,1024]{1,0:T(8,128)(2,1)S(1)} collective-permute-done((bf16[256,1024]{1,0:T(8,128)(2,1)S(1)}, bf16[256,1024]{1,0:T(8,128)(2,1)S(1)}, u32[]{:S(2)}, u32[]{:S(2)}) %collective-permute-start.7) | collective-permute-done | bytes 524320 | tf_op jit(solution)/shard_map/ppermute | solution.py:240
  73.1 0.7 shard_map.60
  73.9 0.9 collective-permute-start.8
  74.8 0.0 collective-permute-done.10
  74.8 1.5 %collective-permute-done.8 = bf16[2,256,512]{2,1,0:T(8,128)(2,1)S(1)} collective-permute-done((bf16[2,256,512]{2,1,0:T(8,128)(2,1)S(1)}, bf16[2,256,512]{2,1,0:T(8,128)(2,1)S(1)}, u32[]{:S(2)}, u32[]{:S(2)}) %collective-permute-start.8) | collective-permute-done | bytes 524320 | tf_op jit(solution)/shard_map/ppermute | solution.py:244
  76.3 0.2 add_convert_fusion
  76.6 4.3 %collective-permute-start.11 = (bf16[2,256,512]{2,1,0:T(8,128)(2,1)S(1)}, bf16[2,256,512]{2,1,0:T(8,128)(2,1)S(1)}, u32[]{:S(2)}, u32[]{:S(2)}) collective-permute-start(bf16[2,256,512]{2,1,0:T(8,128)(2,1)S(1)} %add_convert_fusion), channel_id=1, source_target_pairs={{0,0},{1,24},{2,8},{3,16},{4,4},{5,28},{6,12},{7,20},{8,9},{9,17},... | collective-permute-start | bytes 1572872 | tf_op jit(solution)/shard_map/ppermute | solution.py:244
  80.9 11.5 %collective-permute-done.11 = bf16[2,256,512]{2,1,0:T(8,128)(2,1)S(1)} collective-permute-done((bf16[2,256,512]{2,1,0:T(8,128)(2,1)S(1)}, bf16[2,256,512]{2,1,0:T(8,128)(2,1)S(1)}, u32[]{:S(2)}, u32[]{:S(2)}) %collective-permute-start.11) | collective-permute-done | bytes 524320 | tf_op jit(solution)/shard_map/ppermute | solution.py:244
  92.5 0.9 pad_maximum_fusion
  (1 shorter events, 0.0 us)
Async XLA Ops:
  0.0 1.0 %copy-start = (bf16[256,1024]{1,0:T(8,128)(2,1)S(1)}, bf16[256,1024]{1,0:T(8,128)(2,1)}, u32[]{:S(2)}) copy-start(bf16[256,1024]{1,0:T(8,128)(2,1)} %k_ref.3) | copy-start | bytes 1572868
  1.0 1.0 %copy-start.2 = (bf16[256,1024]{1,0:T(8,128)(2,1)S(1)}, bf16[256,1024]{1,0:T(8,128)(2,1)}, u32[]{:S(2)}) copy-start(bf16[256,1024]{1,0:T(8,128)(2,1)} %v_ref.3) | copy-start | bytes 1572868
  2.4 8.2 %collective-permute-start = (bf16[8,128,128]{2,1,0:T(8,128)(2,1)S(1)}, bf16[8,128,128]{2,1,0:T(8,128)(2,1)S(1)}, u32[]{:S(2)}, u32[]{:S(2)}) collective-permute-start(bf16[8,128,128]{2,1,0:T(8,128)(2,1)S(1)} %get-tuple-element.14), channel_id=1, source_target_pairs={{0,4},{4,0},{8,12},{12,8},{16,20},{20,16},{24,28},{28,24},{1,5},{5... | collective-permute-start | bytes 786440 | tf_op jit(solution)/shard_map/ppermute | solution.py:240
  4.6 1.0 %copy-start.1 = (bf16[256,1024]{1,0:T(8,128)(2,1)S(1)}, bf16[256,1024]{1,0:T(8,128)(2,1)}, u32[]{:S(2)}) copy-start(bf16[256,1024]{1,0:T(8,128)(2,1)} %k_ref.3) | copy-start | bytes 1572868
  5.6 1.0 %copy-start.3 = (bf16[256,1024]{1,0:T(8,128)(2,1)S(1)}, bf16[256,1024]{1,0:T(8,128)(2,1)}, u32[]{:S(2)}) copy-start(bf16[256,1024]{1,0:T(8,128)(2,1)} %q_ref.3) | copy-start | bytes 1572868
  7.6 13.1 %copy-start.4 = (bf16[256,1024]{1,0:T(8,128)(2,1)S(1)}, bf16[256,1024]{1,0:T(8,128)(2,1)}, u32[]{:S(2)}) copy-start(bf16[256,1024]{1,0:T(8,128)(2,1)} %q_ref.3) | copy-start | bytes 1572868
  7.6 13.1 %copy-start.5 = (f32[1024]{0:T(1024)S(1)}, f32[1024]{0:T(1024)}, u32[]{:S(2)}) copy-start(f32[1024]{0:T(1024)} %param.8) | copy-start | bytes 12292
  10.7 7.1 %collective-permute-start.1 = (bf16[8,128,128]{2,1,0:T(8,128)(2,1)S(1)}, bf16[8,128,128]{2,1,0:T(8,128)(2,1)S(1)}, u32[]{:S(2)}, u32[]{:S(2)}) collective-permute-start(bf16[8,128,128]{2,1,0:T(8,128)(2,1)S(1)} %fusion), channel_id=1, source_target_pairs={{0,8},{4,12},{1,9},{5,13},{2,10},{6,14},{3,11},{7,15}} | collective-permute-start | bytes 786440 | tf_op jit(solution)/shard_map/ppermute | solution.py:266
  17.9 2.0 %collective-permute-start.2 = (bf16[8,128,128]{2,1,0:T(8,128)(2,1)S(1)}, bf16[8,128,128]{2,1,0:T(8,128)(2,1)S(1)}, u32[]{:S(2)}, u32[]{:S(2)}) collective-permute-start(bf16[8,128,128]{2,1,0:T(8,128)(2,1)S(1)} %fusion.1), channel_id=1, source_target_pairs={{8,16},{12,20},{9,17},{13,21},{10,18},{14,22},{11,19},{15,23}} | collective-permute-start | bytes 786440 | tf_op jit(solution)/shard_map/ppermute | solution.py:266
  18.6 22.6 %collective-permute-start.5 = (bf16[1024,512]{1,0:T(8,128)(2,1)}, bf16[1024,512]{1,0:T(8,128)(2,1)}, u32[]{:S(2)}, u32[]{:S(2)}) collective-permute-start(bf16[1024,512]{1,0:T(8,128)(2,1)} %own_ref.1), channel_id=1, source_target_pairs={{0,4},{4,0},{8,12},{12,8},{16,20},{20,16},{24,28},{28,24},{1,5},{5... | collective-permute-start | bytes 3145736 | tf_op jit(solution)/shard_map/ppermute | solution.py:240
  20.0 0.7 collective-permute-start.3
  21.5 21.3 %collective-permute-start.4 = (bf16[256,1024]{1,0:T(8,128)(2,1)S(1)}, bf16[256,1024]{1,0:T(8,128)(2,1)S(1)}, u32[]{:S(2)}, u32[]{:S(2)}) collective-permute-start(bf16[256,1024]{1,0:T(8,128)(2,1)S(1)} %shard_map.57), channel_id=1, source_target_pairs={{0,8},{4,12},{8,0},{12,4},{16,24},{20,28},{24,16},{28,20},{1,9},{5... | collective-permute-start | bytes 1572872 | tf_op jit(solution)/shard_map/ppermute | solution.py:240
  26.4 20.1 %collective-permute-start.6 = (bf16[256,1024]{1,0:T(8,128)(2,1)S(1)}, bf16[256,1024]{1,0:T(8,128)(2,1)S(1)}, u32[]{:S(2)}, u32[]{:S(2)}) collective-permute-start(bf16[256,1024]{1,0:T(8,128)(2,1)S(1)} %shard_map.57), channel_id=1, source_target_pairs={{0,16},{1,17},{2,26},{3,27},{4,20},{5,21},{6,30},{7,31},{8,24},{9,... | collective-permute-start | bytes 1572872 | tf_op jit(solution)/shard_map/ppermute | solution.py:244
  47.3 13.9 %collective-permute-start.9 = (bf16[2,256,512]{2,1,0:T(8,128)(2,1)S(1)}, bf16[2,256,512]{2,1,0:T(8,128)(2,1)S(1)}, u32[]{:S(2)}, u32[]{:S(2)}) collective-permute-start(bf16[2,256,512]{2,1,0:T(8,128)(2,1)S(1)} %get-tuple-element.22), channel_id=1, source_target_pairs={{0,1},{1,0},{2,3},{3,2},{4,5},{5,4},{6,7},{7,6},{8,9},{9,8},{10,11... | collective-permute-start | bytes 1572872 | tf_op jit(solution)/shard_map/ppermute | solution.py:244
  59.6 13.5 %collective-permute-start.7 = (bf16[256,1024]{1,0:T(8,128)(2,1)S(1)}, bf16[256,1024]{1,0:T(8,128)(2,1)S(1)}, u32[]{:S(2)}, u32[]{:S(2)}) collective-permute-start(bf16[256,1024]{1,0:T(8,128)(2,1)S(1)} %collective-permute-done.6.heavy_ref), channel_id=1, source_target_pairs={{0,8},{4,12},{8,0},{12,4},{16,24},{20,28},{24,16},{28,20},{1,9},{5... | collective-permute-start | bytes 1572872 | tf_op jit(solution)/shard_map/ppermute | solution.py:240
  61.3 13.5 %collective-permute-start.10 = (bf16[2,256,512]{2,1,0:T(8,128)(2,1)S(1)}, bf16[2,256,512]{2,1,0:T(8,128)(2,1)S(1)}, u32[]{:S(2)}, u32[]{:S(2)}) collective-permute-start(bf16[2,256,512]{2,1,0:T(8,128)(2,1)S(1)} %add_convert_fusion.1), channel_id=1, source_target_pairs={{0,2},{1,3},{2,0},{3,1},{4,6},{5,7},{6,4},{7,5},{8,10},{9,11},{10,... | collective-permute-start | bytes 1572872 | tf_op jit(solution)/shard_map/ppermute | solution.py:244
  73.9 2.5 %collective-permute-start.8 = (bf16[2,256,512]{2,1,0:T(8,128)(2,1)S(1)}, bf16[2,256,512]{2,1,0:T(8,128)(2,1)S(1)}, u32[]{:S(2)}, u32[]{:S(2)}) collective-permute-start(bf16[2,256,512]{2,1,0:T(8,128)(2,1)S(1)} %get-tuple-element.20), channel_id=1, source_target_pairs={{0,1},{1,0},{2,3},{3,2},{4,5},{5,4},{6,7},{7,6},{8,9},{9,8},{10,11... | collective-permute-start | bytes 1572872 | tf_op jit(solution)/shard_map/ppermute | solution.py:244
  76.6 15.9 %collective-permute-start.11 = (bf16[2,256,512]{2,1,0:T(8,128)(2,1)S(1)}, bf16[2,256,512]{2,1,0:T(8,128)(2,1)S(1)}, u32[]{:S(2)}, u32[]{:S(2)}) collective-permute-start(bf16[2,256,512]{2,1,0:T(8,128)(2,1)S(1)} %add_convert_fusion), channel_id=1, source_target_pairs={{0,0},{1,24},{2,8},{3,16},{4,4},{5,28},{6,12},{7,20},{8,9},{9,17},... | collective-permute-start | bytes 1572872 | tf_op jit(solution)/shard_map/ppermute | solution.py:244

commit v21 on v20

--- a/solution.py
+++ b/solution.py
@@ -1,3 +1,5 @@
+import functools
+
 import jax
 import jax.numpy as jnp
 from jax import lax
@@ -74,14 +76,13 @@
         out_ref[:, cols] = jnp.dot(scores, v_ref[:, cols], preferred_element_type=F32)
 
 
-def attend_kernel(second_ref, q_ref, within_ref, gain_ref, mate_ref, *refs):
-    *earlier_refs, out_ref = refs
+def attend_kernel(mates, second_ref, q_ref, within_ref, gain_ref, *refs):
+    *state_refs, out_ref = refs
     second = second_ref[0] == 1
     for head in range(q_ref.shape[1] // HD):
         cols = head_slice(head)
-        state = jnp.where(second, mate_ref[head].astype(F32), 0.0)
-        for earlier_ref in earlier_refs:
-            state += earlier_ref[head].astype(F32)
+        states = [state_ref[head].astype(F32) for state_ref in state_refs]
+        state = jnp.where(second, sum(states[:mates]), 0.0) + sum(states[mates:])
         carried = jnp.dot(q_ref[:, cols], state.astype(BF16), preferred_element_type=F32)
         combined = within_ref[:, cols] + carried
         mean_square = jnp.mean(combined * combined, axis=-1, keepdims=True)
@@ -98,20 +99,20 @@
     )
 
 
-def attend(second, queries, within, norm_gain, mate, *earlier):
+def attend(second, queries, within, norm_gain, mates, *earlier):
     rows, features = queries.shape
     size = rows * features
     vmem = pl.BlockSpec(memory_space=pltpu.VMEM)
     return pl.pallas_call(
-        attend_kernel,
+        functools.partial(attend_kernel, len(mates)),
         out_shape=jax.ShapeDtypeStruct((rows, features), BF16),
-        in_specs=[pl.BlockSpec(memory_space=pltpu.SMEM)] + [vmem] * (4 + len(earlier)),
+        in_specs=[pl.BlockSpec(memory_space=pltpu.SMEM)] + [vmem] * (3 + len(mates) + len(earlier)),
         out_specs=vmem,
         compiler_params=pltpu.CompilerParams(vmem_limit_bytes=24 * 1024 * 1024),
         cost_estimate=pl.CostEstimate(
             flops=2 * size * HD, bytes_accessed=8 * size, transcendentals=0
         ),
-    )(second.astype(jnp.int32)[None], queries, within, norm_gain[None], mate, *earlier)
+    )(second.astype(jnp.int32)[None], queries, within, norm_gain[None], *mates, *earlier)
 
 
 def planes_body(seq_count, head_groups):
@@ -176,7 +177,7 @@
         prefix = prefix_over_planes if inner == 2 else prefix_over_seq
         mate, earlier = prefix(wide, narrow)
         second = lax.axis_index("seq") % 2
-        attended = attend(second, queries, within, norm_gain, mate, *earlier)
+        attended = attend(second, queries, within, norm_gain, (mate,), *earlier)
 
         parts = [None] * head_groups
         for j in (3, 2, 1, 0):
@@ -257,15 +258,17 @@
     )(queries, key_vectors, value_vectors)
     mate_weight = swap(out_weight, 1)
 
-    mate = swap(narrow, 1)
-    mate, within = lax.optimization_barrier((mate, within))
-    onward = wide + mate.astype(F32)
+    pairs = [(s, s ^ 1) for s in range(8)]
+    mate_first = lax.ppermute(narrow, "seq", pairs[:2])
+    mate = lax.ppermute(narrow, "seq", pairs[2:])
+    mate_first, within = lax.optimization_barrier((mate_first, within))
+    onward = wide + mate_first.astype(F32)
     earlier = []
     for plane in range(3):
         pairs = [(2 * plane + i, 2 * plane + 2 + i) for i in range(2)]
         earlier.append(lax.ppermute(onward.astype(BF16), "seq", pairs))
-        onward += earlier[-1].astype(F32)
-    attended = attend(y, queries, within, norm_gain, mate, *earlier)
+        onward = wide + sum(state.astype(F32) for state in [mate] + earlier)
+    attended = attend(y, queries, within, norm_gain, (mate_first, mate), *earlier)
 
     mate_weight, _ = lax.optimization_barrier((mate_weight, attended))
     weight = call(

time: 93.7 us -> 96.3 us (1.028)
  waiting for transfers between devices: 40.9 us -> 42.9 us
    ppermute x0 -> x2, starting transfers between devices: none -> 4.66 us  [the longest x1 3.98 us: pairs_body(): mate_first = lax.ppermute(narrow, 'seq', pairs[:2])]
    ppermute x0 -> x2, waiting for transfers between devices: none -> 2.29 us  [the longest x1 2.29 us: pairs_body(): mate_first = lax.ppermute(narrow, 'seq', pairs[:2])]
    ppermute x3, starting transfers between devices: 4.47 us -> 2.66 us  [pairs_body(): earlier.append(lax.ppermute(onward.astype(BF16), 'seq', pairs))]
    ppermute x4 -> x3, starting transfers between devices: 8.38 us -> 6.94 us  [swap(): return lax.ppermute(value, 'seq', [(s, s ^ mask) for s in range(8)])]
    ppermute x4 -> x3, waiting for transfers between devices: 20.2 us -> 19.2 us  [swap(): return lax.ppermute(value, 'seq', [(s, s ^ mask) for s in range(8)])]
  transfers between devices with their start and end apart: 12 -> 13, of which waited for: 8 -> 9; matrix products, arithmetic and copies ran while one was open for 0% -> 0% of each run, Pallas kernels for 6% -> 6%
where the time goes in v21:
time: 96.3 us; the launch traced here: 95.9 us
  waiting for transfers between devices  42.9 us (45%)
  starting transfers between devices  40.4 us (42%)
  Pallas kernels  6.63 us (7%)
  local copies, waits for them, and re-layouts  4.17 us (4%)
  other arithmetic  1.6 us (2%)
    ppermute x5, starting transfers between devices, move(): return lax.ppermute(value, both, pairs)  26.1 us
    ppermute x3, waiting for transfers between devices, swap(): return lax.ppermute(value, 'seq', [(s, s ^ mask) for s in range(8)])  19.2 us
    ppermute x5, waiting for transfers between devices, move(): return lax.ppermute(value, both, pairs)  16.8 us
    ppermute x3, starting transfers between devices, swap(): return lax.ppermute(value, 'seq', [(s, s ^ mask) for s in range(8)])  6.94 us
    ppermute x3, waiting for transfers between devices, pairs_body(): earlier.append(lax.ppermute(onward.astype(BF16), 'seq', pairs))  4.62 us
    unnamed x12, local copies, waits for them, and re-layouts  4.17 us
    ppermute x1, starting transfers between devices, pairs_body(): mate_first = lax.ppermute(narrow, 'seq', pairs[:2])  3.98 us
    ppermute x3, starting transfers between devices, pairs_body(): earlier.append(lax.ppermute(onward.astype(BF16), 'seq', pairs))  2.66 us
  transfers between devices with their start and end apart: 13, of which 9 were waited for; matrix products, arithmetic and copies ran while one was open for 0% of the time, Pallas kernels for 6%

profile of v21, /device:TPU:1, one launch (start us, length us, event | category | flops | bytes accessed | tf_op | source)
XLA Modules:
  0.0 95.9 jit_solution(3271126969452117735)
XLA Ops:
  0.0 0.0 copy-start
  0.0 1.0 %copy-done = bf16[256,1024]{1,0:T(8,128)(2,1)S(1)} copy-done((bf16[256,1024]{1,0:T(8,128)(2,1)S(1)}, bf16[256,1024]{1,0:T(8,128)(2,1)}, u32[]{:S(2)}) %copy-start) | copy-done | bytes 524312
  1.0 0.0 copy-start.2
  1.0 1.0 %copy-done.2 = bf16[256,1024]{1,0:T(8,128)(2,1)S(1)} copy-done((bf16[256,1024]{1,0:T(8,128)(2,1)S(1)}, bf16[256,1024]{1,0:T(8,128)(2,1)}, u32[]{:S(2)}) %copy-start.2) | copy-done | bytes 524312
  2.1 0.4 shard_map.55
  2.4 4.0 %collective-permute-start = (bf16[8,128,128]{2,1,0:T(8,128)(2,1)S(1)}, bf16[8,128,128]{2,1,0:T(8,128)(2,1)S(1)}, u32[]{:S(2)}, u32[]{:S(2)}) collective-permute-start(bf16[8,128,128]{2,1,0:T(8,128)(2,1)S(1)} %get-tuple-element.14), channel_id=1, source_target_pairs={{0,4},{4,0},{1,5},{5,1},{2,6},{6,2},{3,7},{7,3}} | collective-permute-start | bytes 786440 | tf_op jit(solution)/shard_map/ppermute | solution.py:262
  6.4 0.7 collective-permute-start.1
  7.1 0.0 copy-start.1
  7.1 1.0 %copy-done.1 = bf16[256,1024]{1,0:T(8,128)(2,1)S(1)} copy-done((bf16[256,1024]{1,0:T(8,128)(2,1)S(1)}, bf16[256,1024]{1,0:T(8,128)(2,1)}, u32[]{:S(2)}) %copy-start.1) | copy-done | bytes 524312
  8.2 0.0 copy-start.3
  8.2 1.0 %copy-done.3 = bf16[256,1024]{1,0:T(8,128)(2,1)S(1)} copy-done((bf16[256,1024]{1,0:T(8,128)(2,1)S(1)}, bf16[256,1024]{1,0:T(8,128)(2,1)}, u32[]{:S(2)}) %copy-start.3) | copy-done | bytes 524312
  9.2 0.9 shard_map.56.within_ref
  10.1 0.0 copy-start.4
  10.1 0.0 copy-start.5
  10.2 2.3 %collective-permute-done.refs_0_ = bf16[8,128,128]{2,1,0:T(8,128)(2,1)S(1)} collective-permute-done((bf16[8,128,128]{2,1,0:T(8,128)(2,1)S(1)}, bf16[8,128,128]{2,1,0:T(8,128)(2,1)S(1)}, u32[]{:S(2)}, u32[]{:S(2)}) %collective-permute-start) | collective-permute-done | bytes 262176 | tf_op jit(solution)/shard_map/ppermute | solution.py:262
  12.4 0.1 add_convert_fusion.4
  12.5 1.3 %collective-permute-start.2 = (bf16[8,128,128]{2,1,0:T(8,128)(2,1)S(1)}, bf16[8,128,128]{2,1,0:T(8,128)(2,1)S(1)}, u32[]{:S(2)}, u32[]{:S(2)}) collective-permute-start(bf16[8,128,128]{2,1,0:T(8,128)(2,1)S(1)} %add_convert_fusion.4), channel_id=1, source_target_pairs={{0,8},{4,12},{1,9},{5,13},{2,10},{6,14},{3,11},{7,15}} | collective-permute-start | bytes 786440 | tf_op jit(solution)/shard_map/ppermute | solution.py:269
  13.8 0.0 collective-permute-done.1.refs_1_
  13.8 4.6 %collective-permute-done.2.refs_2_ = bf16[8,128,128]{2,1,0:T(8,128)(2,1)S(1)} collective-permute-done((bf16[8,128,128]{2,1,0:T(8,128)(2,1)S(1)}, bf16[8,128,128]{2,1,0:T(8,128)(2,1)S(1)}, u32[]{:S(2)}, u32[]{:S(2)}) %collective-permute-start.2) | collective-permute-done | bytes 262176 | tf_op jit(solution)/shard_map/ppermute | solution.py:269
  18.4 0.1 add_convert_fusion.3
  18.5 0.7 collective-permute-start.3
  19.2 0.9 collective-permute-start.6
  20.1 0.0 collective-permute-done.3.refs_3_
  20.1 0.1 add_convert_fusion.2
  20.2 0.7 collective-permute-start.4
  20.9 0.0 collective-permute-done.4.refs_4_
  20.9 0.0 copy-done.4
  21.0 0.0 copy-done.5
  21.0 0.8 shard_map.57
  21.7 6.0 %collective-permute-start.5 = (bf16[256,1024]{1,0:T(8,128)(2,1)S(1)}, bf16[256,1024]{1,0:T(8,128)(2,1)S(1)}, u32[]{:S(2)}, u32[]{:S(2)}) collective-permute-start(bf16[256,1024]{1,0:T(8,128)(2,1)S(1)} %shard_map.57), channel_id=1, source_target_pairs={{0,8},{4,12},{8,0},{12,4},{16,24},{20,28},{24,16},{28,20},{1,9},{5... | collective-permute-start | bytes 1572872 | tf_op jit(solution)/shard_map/ppermute | solution.py:241
  27.7 8.4 %collective-permute-start.7 = (bf16[256,1024]{1,0:T(8,128)(2,1)S(1)}, bf16[256,1024]{1,0:T(8,128)(2,1)S(1)}, u32[]{:S(2)}, u32[]{:S(2)}) collective-permute-start(bf16[256,1024]{1,0:T(8,128)(2,1)S(1)} %shard_map.57), channel_id=1, source_target_pairs={{0,16},{1,17},{2,26},{3,27},{4,20},{5,21},{6,30},{7,31},{8,24},{9,... | collective-permute-start | bytes 1572872 | tf_op jit(solution)/shard_map/ppermute | solution.py:245
  36.1 6.3 %collective-permute-done.6.mate_ref = bf16[1024,512]{1,0:T(8,128)(2,1)} collective-permute-done((bf16[1024,512]{1,0:T(8,128)(2,1)}, bf16[1024,512]{1,0:T(8,128)(2,1)}, u32[]{:S(2)}, u32[]{:S(2)}) %collective-permute-start.6) | collective-permute-done | bytes 1048608 | tf_op jit(solution)/shard_map/ppermute | solution.py:241
  42.4 1.7 %shard_map.58.weight_ref = bf16[2,1024,512]{2,1,0:T(8,128)(2,1)S(1)} custom-call(bf16[1024,512]{1,0:T(8,128)(2,1)} %own_ref.1, bf16[1024,512]{1,0:T(8,128)(2,1)} %collective-permute-done.6.mate_ref), custom_call_target="tpu_custom_call" | custom-call | bytes 4194304 | tf_op jit(solution)/shard_map/pallas_call | solution.py:274
  44.1 1.2 %collective-permute-done.5 = bf16[256,1024]{1,0:T(8,128)(2,1)S(1)} collective-permute-done((bf16[256,1024]{1,0:T(8,128)(2,1)S(1)}, bf16[256,1024]{1,0:T(8,128)(2,1)S(1)}, u32[]{:S(2)}, u32[]{:S(2)}) %collective-permute-start.5) | collective-permute-done | bytes 524320 | tf_op jit(solution)/shard_map/ppermute | solution.py:241
  45.3 0.1 broadcast_select_fusion.1
  45.4 0.7 shard_map.61.light_ref
  46.1 1.9 %collective-permute-done.7.heavy_ref = bf16[256,1024]{1,0:T(8,128)(2,1)S(1)} collective-permute-done((bf16[256,1024]{1,0:T(8,128)(2,1)S(1)}, bf16[256,1024]{1,0:T(8,128)(2,1)S(1)}, u32[]{:S(2)}, u32[]{:S(2)}) %collective-permute-start.7) | collective-permute-done | bytes 524320 | tf_op jit(solution)/shard_map/ppermute | solution.py:245
  48.0 0.7 shard_map.62
  48.7 12.4 %collective-permute-start.10 = (bf16[2,256,512]{2,1,0:T(8,128)(2,1)S(1)}, bf16[2,256,512]{2,1,0:T(8,128)(2,1)S(1)}, u32[]{:S(2)}, u32[]{:S(2)}) collective-permute-start(bf16[2,256,512]{2,1,0:T(8,128)(2,1)S(1)} %get-tuple-element.22), channel_id=1, source_target_pairs={{0,1},{1,0},{2,3},{3,2},{4,5},{5,4},{6,7},{7,6},{8,9},{9,8},{10,11... | collective-permute-start | bytes 1572872 | tf_op jit(solution)/shard_map/ppermute | solution.py:245
  61.1 0.1 collective-permute-start.8
  61.1 0.7 shard_map.59.light_ref
  61.9 0.7 collective-permute-done.10
  62.6 0.1 add_convert_fusion.1
  62.7 0.1 collective-permute-start.11
  62.9 11.7 %collective-permute-done.8.heavy_ref = bf16[256,1024]{1,0:T(8,128)(2,1)S(1)} collective-permute-done((bf16[256,1024]{1,0:T(8,128)(2,1)S(1)}, bf16[256,1024]{1,0:T(8,128)(2,1)S(1)}, u32[]{:S(2)}, u32[]{:S(2)}) %collective-permute-start.8) | collective-permute-done | bytes 524320 | tf_op jit(solution)/shard_map/ppermute | solution.py:241
  74.6 0.7 shard_map.60
  75.3 0.9 collective-permute-start.9
  76.2 0.0 collective-permute-done.11
  76.2 1.5 %collective-permute-done.9 = bf16[2,256,512]{2,1,0:T(8,128)(2,1)S(1)} collective-permute-done((bf16[2,256,512]{2,1,0:T(8,128)(2,1)S(1)}, bf16[2,256,512]{2,1,0:T(8,128)(2,1)S(1)}, u32[]{:S(2)}, u32[]{:S(2)}) %collective-permute-start.9) | collective-permute-done | bytes 524320 | tf_op jit(solution)/shard_map/ppermute | solution.py:245
  77.8 0.2 add_convert_fusion
  78.0 4.3 %collective-permute-start.12 = (bf16[2,256,512]{2,1,0:T(8,128)(2,1)S(1)}, bf16[2,256,512]{2,1,0:T(8,128)(2,1)S(1)}, u32[]{:S(2)}, u32[]{:S(2)}) collective-permute-start(bf16[2,256,512]{2,1,0:T(8,128)(2,1)S(1)} %add_convert_fusion), channel_id=1, source_target_pairs={{0,0},{1,24},{2,8},{3,16},{4,4},{5,28},{6,12},{7,20},{8,9},{9,17},... | collective-permute-start | bytes 1572872 | tf_op jit(solution)/shard_map/ppermute | solution.py:245
  82.3 12.6 %collective-permute-done.12 = bf16[2,256,512]{2,1,0:T(8,128)(2,1)S(1)} collective-permute-done((bf16[2,256,512]{2,1,0:T(8,128)(2,1)S(1)}, bf16[2,256,512]{2,1,0:T(8,128)(2,1)S(1)}, u32[]{:S(2)}, u32[]{:S(2)}) %collective-permute-start.12) | collective-permute-done | bytes 524320 | tf_op jit(solution)/shard_map/ppermute | solution.py:245
  95.0 0.9 pad_maximum_fusion
  (1 shorter events, 0.0 us)
Async XLA Ops:
  0.0 1.0 %copy-start = (bf16[256,1024]{1,0:T(8,128)(2,1)S(1)}, bf16[256,1024]{1,0:T(8,128)(2,1)}, u32[]{:S(2)}) copy-start(bf16[256,1024]{1,0:T(8,128)(2,1)} %k_ref.3) | copy-start | bytes 1572868
  1.0 1.0 %copy-start.2 = (bf16[256,1024]{1,0:T(8,128)(2,1)S(1)}, bf16[256,1024]{1,0:T(8,128)(2,1)}, u32[]{:S(2)}) copy-start(bf16[256,1024]{1,0:T(8,128)(2,1)} %v_ref.3) | copy-start | bytes 1572868
  2.4 10.0 %collective-permute-start = (bf16[8,128,128]{2,1,0:T(8,128)(2,1)S(1)}, bf16[8,128,128]{2,1,0:T(8,128)(2,1)S(1)}, u32[]{:S(2)}, u32[]{:S(2)}) collective-permute-start(bf16[8,128,128]{2,1,0:T(8,128)(2,1)S(1)} %get-tuple-element.14), channel_id=1, source_target_pairs={{0,4},{4,0},{1,5},{5,1},{2,6},{6,2},{3,7},{7,3}} | collective-permute-start | bytes 786440 | tf_op jit(solution)/shard_map/ppermute | solution.py:262
  6.4 7.4 %collective-permute-start.1 = (bf16[8,128,128]{2,1,0:T(8,128)(2,1)S(1)}, bf16[8,128,128]{2,1,0:T(8,128)(2,1)S(1)}, u32[]{:S(2)}, u32[]{:S(2)}) collective-permute-start(bf16[8,128,128]{2,1,0:T(8,128)(2,1)S(1)} %get-tuple-element.14), channel_id=1, source_target_pairs={{8,12},{12,8},{16,20},{20,16},{24,28},{28,24},{9,13},{13,9},{17,21... | collective-permute-start | bytes 786440 | tf_op jit(solution)/shard_map/ppermute | solution.py:263
  7.1 1.0 %copy-start.1 = (bf16[256,1024]{1,0:T(8,128)(2,1)S(1)}, bf16[256,1024]{1,0:T(8,128)(2,1)}, u32[]{:S(2)}) copy-start(bf16[256,1024]{1,0:T(8,128)(2,1)} %k_ref.3) | copy-start | bytes 1572868
  8.2 1.0 %copy-start.3 = (bf16[256,1024]{1,0:T(8,128)(2,1)S(1)}, bf16[256,1024]{1,0:T(8,128)(2,1)}, u32[]{:S(2)}) copy-start(bf16[256,1024]{1,0:T(8,128)(2,1)} %q_ref.3) | copy-start | bytes 1572868
  10.1 10.8 %copy-start.4 = (bf16[256,1024]{1,0:T(8,128)(2,1)S(1)}, bf16[256,1024]{1,0:T(8,128)(2,1)}, u32[]{:S(2)}) copy-start(bf16[256,1024]{1,0:T(8,128)(2,1)} %q_ref.3) | copy-start | bytes 1572868
  10.1 10.8 %copy-start.5 = (f32[1024]{0:T(1024)S(1)}, f32[1024]{0:T(1024)}, u32[]{:S(2)}) copy-start(f32[1024]{0:T(1024)} %param.8) | copy-start | bytes 12292
  12.5 5.9 %collective-permute-start.2 = (bf16[8,128,128]{2,1,0:T(8,128)(2,1)S(1)}, bf16[8,128,128]{2,1,0:T(8,128)(2,1)S(1)}, u32[]{:S(2)}, u32[]{:S(2)}) collective-permute-start(bf16[8,128,128]{2,1,0:T(8,128)(2,1)S(1)} %add_convert_fusion.4), channel_id=1, source_target_pairs={{0,8},{4,12},{1,9},{5,13},{2,10},{6,14},{3,11},{7,15}} | collective-permute-start | bytes 786440 | tf_op jit(solution)/shard_map/ppermute | solution.py:269
  18.5 1.6 %collective-permute-start.3 = (bf16[8,128,128]{2,1,0:T(8,128)(2,1)S(1)}, bf16[8,128,128]{2,1,0:T(8,128)(2,1)S(1)}, u32[]{:S(2)}, u32[]{:S(2)}) collective-permute-start(bf16[8,128,128]{2,1,0:T(8,128)(2,1)S(1)} %add_convert_fusion.3), channel_id=1, source_target_pairs={{8,16},{12,20},{9,17},{13,21},{10,18},{14,22},{11,19},{15,23}} | collective-permute-start | bytes 786440 | tf_op jit(solution)/shard_map/ppermute | solution.py:269
  19.2 23.2 %collective-permute-start.6 = (bf16[1024,512]{1,0:T(8,128)(2,1)}, bf16[1024,512]{1,0:T(8,128)(2,1)}, u32[]{:S(2)}, u32[]{:S(2)}) collective-permute-start(bf16[1024,512]{1,0:T(8,128)(2,1)} %own_ref.1), channel_id=1, source_target_pairs={{0,4},{4,0},{8,12},{12,8},{16,20},{20,16},{24,28},{28,24},{1,5},{5... | collective-permute-start | bytes 3145736 | tf_op jit(solution)/shard_map/ppermute | solution.py:241
  20.2 0.7 collective-permute-start.4
  21.7 23.5 %collective-permute-start.5 = (bf16[256,1024]{1,0:T(8,128)(2,1)S(1)}, bf16[256,1024]{1,0:T(8,128)(2,1)S(1)}, u32[]{:S(2)}, u32[]{:S(2)}) collective-permute-start(bf16[256,1024]{1,0:T(8,128)(2,1)S(1)} %shard_map.57), channel_id=1, source_target_pairs={{0,8},{4,12},{8,0},{12,4},{16,24},{20,28},{24,16},{28,20},{1,9},{5... | collective-permute-start | bytes 1572872 | tf_op jit(solution)/shard_map/ppermute | solution.py:241
  27.7 20.2 %collective-permute-start.7 = (bf16[256,1024]{1,0:T(8,128)(2,1)S(1)}, bf16[256,1024]{1,0:T(8,128)(2,1)S(1)}, u32[]{:S(2)}, u32[]{:S(2)}) collective-permute-start(bf16[256,1024]{1,0:T(8,128)(2,1)S(1)} %shard_map.57), channel_id=1, source_target_pairs={{0,16},{1,17},{2,26},{3,27},{4,20},{5,21},{6,30},{7,31},{8,24},{9,... | collective-permute-start | bytes 1572872 | tf_op jit(solution)/shard_map/ppermute | solution.py:245
  48.7 13.9 %collective-permute-start.10 = (bf16[2,256,512]{2,1,0:T(8,128)(2,1)S(1)}, bf16[2,256,512]{2,1,0:T(8,128)(2,1)S(1)}, u32[]{:S(2)}, u32[]{:S(2)}) collective-permute-start(bf16[2,256,512]{2,1,0:T(8,128)(2,1)S(1)} %get-tuple-element.22), channel_id=1, source_target_pairs={{0,1},{1,0},{2,3},{3,2},{4,5},{5,4},{6,7},{7,6},{8,9},{9,8},{10,11... | collective-permute-start | bytes 1572872 | tf_op jit(solution)/shard_map/ppermute | solution.py:245
  61.1 13.5 %collective-permute-start.8 = (bf16[256,1024]{1,0:T(8,128)(2,1)S(1)}, bf16[256,1024]{1,0:T(8,128)(2,1)S(1)}, u32[]{:S(2)}, u32[]{:S(2)}) collective-permute-start(bf16[256,1024]{1,0:T(8,128)(2,1)S(1)} %collective-permute-done.7.heavy_ref), channel_id=1, source_target_pairs={{0,8},{4,12},{8,0},{12,4},{16,24},{20,28},{24,16},{28,20},{1,9},{5... | collective-permute-start | bytes 1572872 | tf_op jit(solution)/shard_map/ppermute | solution.py:241
  62.7 13.5 %collective-permute-start.11 = (bf16[2,256,512]{2,1,0:T(8,128)(2,1)S(1)}, bf16[2,256,512]{2,1,0:T(8,128)(2,1)S(1)}, u32[]{:S(2)}, u32[]{:S(2)}) collective-permute-start(bf16[2,256,512]{2,1,0:T(8,128)(2,1)S(1)} %add_convert_fusion.1), channel_id=1, source_target_pairs={{0,2},{1,3},{2,0},{3,1},{4,6},{5,7},{6,4},{7,5},{8,10},{9,11},{10,... | collective-permute-start | bytes 1572872 | tf_op jit(solution)/shard_map/ppermute | solution.py:245
  75.3 2.5 %collective-permute-start.9 = (bf16[2,256,512]{2,1,0:T(8,128)(2,1)S(1)}, bf16[2,256,512]{2,1,0:T(8,128)(2,1)S(1)}, u32[]{:S(2)}, u32[]{:S(2)}) collective-permute-start(bf16[2,256,512]{2,1,0:T(8,128)(2,1)S(1)} %get-tuple-element.20), channel_id=1, source_target_pairs={{0,1},{1,0},{2,3},{3,2},{4,5},{5,4},{6,7},{7,6},{8,9},{9,8},{10,11... | collective-permute-start | bytes 1572872 | tf_op jit(solution)/shard_map/ppermute | solution.py:245
  78.0 17.0 %collective-permute-start.12 = (bf16[2,256,512]{2,1,0:T(8,128)(2,1)S(1)}, bf16[2,256,512]{2,1,0:T(8,128)(2,1)S(1)}, u32[]{:S(2)}, u32[]{:S(2)}) collective-permute-start(bf16[2,256,512]{2,1,0:T(8,128)(2,1)S(1)} %add_convert_fusion), channel_id=1, source_target_pairs={{0,0},{1,24},{2,8},{3,16},{4,4},{5,28},{6,12},{7,20},{8,9},{9,17},... | collective-permute-start | bytes 1572872 | tf_op jit(solution)/shard_map/ppermute | solution.py:245

commit v22 on v21

--- a/solution.py
+++ b/solution.py
@@ -53,14 +53,25 @@
     return slice(head * HD, (head + 1) * HD)
 
 
-def state_kernel(k_ref, v_ref, wide_ref, narrow_ref):
-    for head in range(wide_ref.shape[0]):
-        cols = head_slice(head)
-        state = lax.dot_general(
-            k_ref[:, cols], v_ref[:, cols], (((0,), (0,)), ((), ())), preferred_element_type=F32
-        )
-        wide_ref[head] = state
-        narrow_ref[head] = state.astype(BF16)
+def state_kernel(k_ref, v_ref, *out_refs):
+    half = len(out_refs) // 2
+    count = out_refs[0].shape[0]
+    for part in range(half):
+        for index in range(count):
+            cols = head_slice(part * count + index)
+            state = lax.dot_general(
+                k_ref[:, cols], v_ref[:, cols], (((0,), (0,)), ((), ())), preferred_element_type=F32
+            )
+            out_refs[part][index] = state
+            out_refs[half + part][index] = state.astype(BF16)
+
+
+def sum_kernel(*refs):
+    *value_refs, out_ref = refs
+    total = value_refs[0][...].astype(F32)
+    for value_ref in value_refs[1:]:
+        total += value_ref[...].astype(F32)
+    out_ref[...] = total.astype(out_ref.dtype)
 
 
 def within_kernel(q_ref, k_ref, v_ref, out_ref):
@@ -76,13 +87,17 @@
         out_ref[:, cols] = jnp.dot(scores, v_ref[:, cols], preferred_element_type=F32)
 
 
-def attend_kernel(mates, second_ref, q_ref, within_ref, gain_ref, *refs):
+def attend_kernel(parts, second_ref, q_ref, within_ref, gain_ref, *refs):
     *state_refs, out_ref = refs
     second = second_ref[0] == 1
-    for head in range(q_ref.shape[1] // HD):
+    each, heads = len(state_refs) // parts, q_ref.shape[1] // HD
+    for head in range(heads):
         cols = head_slice(head)
-        states = [state_ref[head].astype(F32) for state_ref in state_refs]
-        state = jnp.where(second, sum(states[:mates]), 0.0) + sum(states[mates:])
+        part, index = divmod(head, heads // parts)
+        mate_ref, *earlier_refs = state_refs[part * each : (part + 1) * each]
+        state = jnp.where(second, mate_ref[index].astype(F32), 0.0)
+        for earlier_ref in earlier_refs:
+            state += earlier_ref[index].astype(F32)
         carried = jnp.dot(q_ref[:, cols], state.astype(BF16), preferred_element_type=F32)
         combined = within_ref[:, cols] + carried
         mean_square = jnp.mean(combined * combined, axis=-1, keepdims=True)
@@ -99,20 +114,29 @@
     )
 
 
-def attend(second, queries, within, norm_gain, mates, *earlier):
+def block_states(keys, values, parts):
+    rows, features = keys.shape
+    shape = (features // HD // parts, HD, HD)
+    outs = [jax.ShapeDtypeStruct(shape, kind) for kind in (F32, BF16) for _ in range(parts)]
+    states = call(state_kernel, outs, 2 * keys.size * HD, 4 * keys.size)(keys, values)
+    return states[:parts], states[parts:]
+
+
+def attend(second, queries, within, norm_gain, states):
     rows, features = queries.shape
     size = rows * features
     vmem = pl.BlockSpec(memory_space=pltpu.VMEM)
+    flat = [state for part in states for state in part]
     return pl.pallas_call(
-        functools.partial(attend_kernel, len(mates)),
+        functools.partial(attend_kernel, len(states)),
         out_shape=jax.ShapeDtypeStruct((rows, features), BF16),
-        in_specs=[pl.BlockSpec(memory_space=pltpu.SMEM)] + [vmem] * (3 + len(mates) + len(earlier)),
+        in_specs=[pl.BlockSpec(memory_space=pltpu.SMEM)] + [vmem] * (3 + len(flat)),
         out_specs=vmem,
         compiler_params=pltpu.CompilerParams(vmem_limit_bytes=24 * 1024 * 1024),
         cost_estimate=pl.CostEstimate(
             flops=2 * size * HD, bytes_accessed=8 * size, transcendentals=0
         ),
-    )(second.astype(jnp.int32)[None], queries, within, norm_gain[None], *mates, *earlier)
+    )(second.astype(jnp.int32)[None], queries, within, norm_gain[None], *flat)
 
 
 def planes_body(seq_count, head_groups):
@@ -162,22 +186,14 @@
         heads = features // HD
         size = rows * features
         weight = gather_weight(out_weight)
-        wide, narrow = call(
-            state_kernel,
-            (
-                jax.ShapeDtypeStruct((heads, HD, HD), F32),
-                jax.ShapeDtypeStruct((heads, HD, HD), BF16),
-            ),
-            2 * size * HD,
-            4 * size + 6 * heads * HD * HD,
-        )(key_vectors, value_vectors)
+        (wide,), (narrow,) = block_states(key_vectors, value_vectors, 1)
         within = call(
             within_kernel, jax.ShapeDtypeStruct((rows, features), F32), 4 * size * BLOCK, 10 * size
         )(queries, key_vectors, value_vectors)
         prefix = prefix_over_planes if inner == 2 else prefix_over_seq
         mate, earlier = prefix(wide, narrow)
         second = lax.axis_index("seq") % 2
-        attended = attend(second, queries, within, norm_gain, (mate,), *earlier)
+        attended = attend(second, queries, within, norm_gain, [(mate, *earlier)])
 
         parts = [None] * head_groups
         for j in (3, 2, 1, 0):
@@ -244,31 +260,26 @@
         pairs = [(at(*d), at(*place_of(*d))) for d in devices if chosen(*d)]
         return lax.ppermute(value, both, pairs)
 
-    wide, narrow = call(
-        state_kernel,
-        (
-            jax.ShapeDtypeStruct((heads, HD, HD), F32),
-            jax.ShapeDtypeStruct((heads, HD, HD), BF16),
-        ),
-        2 * size * HD,
-        4 * size + 6 * heads * HD * HD,
-    )(key_vectors, value_vectors)
+    parts = 2
+    wide, narrow = block_states(key_vectors, value_vectors, parts)
     within = call(
         within_kernel, jax.ShapeDtypeStruct((rows, features), F32), 4 * size * BLOCK, 10 * size
     )(queries, key_vectors, value_vectors)
     mate_weight = swap(out_weight, 1)
 
-    pairs = [(s, s ^ 1) for s in range(8)]
-    mate_first = lax.ppermute(narrow, "seq", pairs[:2])
-    mate = lax.ppermute(narrow, "seq", pairs[2:])
-    mate_first, within = lax.optimization_barrier((mate_first, within))
-    onward = wide + mate_first.astype(F32)
-    earlier = []
+    def add(*values):
+        return call(
+            sum_kernel, jax.ShapeDtypeStruct(values[0].shape, BF16), size, 4 * values[0].size
+        )(*values)
+
+    states = [[swap(part, 1)] for part in narrow]
+    states[0][0], within = lax.optimization_barrier((states[0][0], within))
     for plane in range(3):
         pairs = [(2 * plane + i, 2 * plane + 2 + i) for i in range(2)]
-        earlier.append(lax.ppermute(onward.astype(BF16), "seq", pairs))
-        onward = wide + sum(state.astype(F32) for state in [mate] + earlier)
-    attended = attend(y, queries, within, norm_gain, (mate_first, mate), *earlier)
+        onward = [add(wide[part], *states[part]) for part in range(parts)]
+        for part in range(parts):
+            states[part].append(lax.ppermute(onward[part], "seq", pairs))
+    attended = attend(y, queries, within, norm_gain, states)
 
     mate_weight, _ = lax.optimization_barrier((mate_weight, attended))
     weight = call(

time: 96.3 us -> 91 us (0.945)
  waiting for transfers between devices: 42.9 us -> 35.9 us
  local copies, waits for them, and re-layouts: 4.17 us -> 6.44 us
    ppermute x5 -> x6, waiting for transfers between devices: 6.91 us -> 1.99 us  [pairs_body(): states[part].append(lax.ppermute(onward[part], 'seq', pairs))]
    unnamed x12 -> x16, local copies, waits for them, and re-layouts: 4.17 us -> 6.44 us
    ppermute x5, waiting for transfers between devices: 16.8 us -> 14.6 us  [move(): return lax.ppermute(value, both, pairs)]
    ppermute x5, starting transfers between devices: 26.1 us -> 24.6 us  [move(): return lax.ppermute(value, both, pairs)]
    ppermute x3 -> x5, starting transfers between devices: 6.94 us -> 8.07 us  [swap(): return lax.ppermute(value, 'seq', [(s, s ^ mask) for s in range(8)])]
    ppermute x3 -> x5, waiting for transfers between devices: 19.2 us -> 19.3 us  [swap(): return lax.ppermute(value, 'seq', [(s, s ^ mask) for s in range(8)])]
    ppermute x5 -> x6, starting transfers between devices: 7.32 us -> 7.31 us  [pairs_body(): states[part].append(lax.ppermute(onward[part], 'seq', pairs))]
  transfers between devices with their start and end apart: 13 -> 16, of which waited for: 9 -> 9; matrix products, arithmetic and copies ran while one was open for 0% -> 0% of each run, Pallas kernels for 6% -> 6%
where the time goes in v22:
time: 91 us; the launch traced here: 90.4 us
  starting transfers between devices  39.9 us (44%)
  waiting for transfers between devices  35.9 us (39%)
  Pallas kernels  6.54 us (7%)
  local copies, waits for them, and re-layouts  6.44 us (7%)
  other arithmetic  1.33 us (1%)
    ppermute x5, starting transfers between devices, move(): return lax.ppermute(value, both, pairs)  24.6 us
    ppermute x5, waiting for transfers between devices, swap(): return lax.ppermute(value, 'seq', [(s, s ^ mask) for s in range(8)])  19.3 us
    ppermute x5, waiting for transfers between devices, move(): return lax.ppermute(value, both, pairs)  14.6 us
    ppermute x5, starting transfers between devices, swap(): return lax.ppermute(value, 'seq', [(s, s ^ mask) for s in range(8)])  8.07 us
    ppermute x6, starting transfers between devices, pairs_body(): states[part].append(lax.ppermute(onward[part], 'seq', pairs))  7.31 us
    unnamed x16, local copies, waits for them, and re-layouts  6.44 us
    ppermute x6, waiting for transfers between devices, pairs_body(): states[part].append(lax.ppermute(onward[part], 'seq', pairs))  1.99 us
  transfers between devices with their start and end apart: 16, of which 9 were waited for; matrix products, arithmetic and copies ran while one was open for 0% of the time, Pallas kernels for 6%

profile of v22, /device:TPU:1, one launch (start us, length us, event | category | flops | bytes accessed | tf_op | source)
XLA Modules:
  0.0 90.4 jit_solution(11999896208228142095)
XLA Ops:
  0.0 0.0 copy-start
  0.0 1.0 %copy-done = bf16[256,1024]{1,0:T(8,128)(2,1)S(1)} copy-done((bf16[256,1024]{1,0:T(8,128)(2,1)S(1)}, bf16[256,1024]{1,0:T(8,128)(2,1)}, u32[]{:S(2)}) %copy-start) | copy-done | bytes 524312
  1.0 0.0 copy-start.2
  1.0 1.0 %copy-done.2 = bf16[256,1024]{1,0:T(8,128)(2,1)S(1)} copy-done((bf16[256,1024]{1,0:T(8,128)(2,1)S(1)}, bf16[256,1024]{1,0:T(8,128)(2,1)}, u32[]{:S(2)}) %copy-start.2) | copy-done | bytes 524312
  2.1 0.4 shard_map.55
  2.4 2.1 %collective-permute-start = (bf16[4,128,128]{2,1,0:T(8,128)(2,1)S(1)}, bf16[4,128,128]{2,1,0:T(8,128)(2,1)S(1)}, u32[]{:S(2)}, u32[]{:S(2)}) collective-permute-start(bf16[4,128,128]{2,1,0:T(8,128)(2,1)S(1)} %get-tuple-element.16), channel_id=1, source_target_pairs={{0,4},{4,0},{8,12},{12,8},{16,20},{20,16},{24,28},{28,24},{1,5},{5... | collective-permute-start | bytes 393224 | tf_op jit(solution)/shard_map/ppermute | solution.py:257
  4.6 0.1 collective-permute-start.4
  4.7 1.4 %collective-permute-start.9 = (bf16[1024,512]{1,0:T(8,128)(2,1)}, bf16[1024,512]{1,0:T(8,128)(2,1)}, u32[]{:S(2)}, u32[]{:S(2)}) collective-permute-start(bf16[1024,512]{1,0:T(8,128)(2,1)} %own_ref.1), channel_id=1, source_target_pairs={{0,4},{4,0},{8,12},{12,8},{16,20},{20,16},{24,28},{28,24},{1,5},{5... | collective-permute-start | bytes 3145736 | tf_op jit(solution)/shard_map/ppermute | solution.py:257
  6.0 0.0 copy-start.1
  6.0 1.0 %copy-done.1 = bf16[256,1024]{1,0:T(8,128)(2,1)S(1)} copy-done((bf16[256,1024]{1,0:T(8,128)(2,1)S(1)}, bf16[256,1024]{1,0:T(8,128)(2,1)}, u32[]{:S(2)}) %copy-start.1) | copy-done | bytes 524312
  7.1 0.0 copy-start.3
  7.1 1.0 %copy-done.3 = bf16[256,1024]{1,0:T(8,128)(2,1)S(1)} copy-done((bf16[256,1024]{1,0:T(8,128)(2,1)S(1)}, bf16[256,1024]{1,0:T(8,128)(2,1)}, u32[]{:S(2)}) %copy-start.3) | copy-done | bytes 524312
  8.1 0.0 copy-start.4
  8.1 1.0 %copy-done.4 = bf16[256,1024]{1,0:T(8,128)(2,1)S(1)} copy-done((bf16[256,1024]{1,0:T(8,128)(2,1)S(1)}, bf16[256,1024]{1,0:T(8,128)(2,1)}, u32[]{:S(2)}) %copy-start.4) | copy-done | bytes 524312
  9.2 0.9 %shard_map.56.within_ref = f32[256,1024]{1,0:T(8,128)S(1)} custom-call(bf16[256,1024]{1,0:T(8,128)(2,1)S(1)} %copy-done.4, bf16[256,1024]{1,0:T(8,128)(2,1)S(1)} %copy-done.1, bf16[256,1024]{1,0:T(8,128)(2,1)S(1)} %copy-done.3), custom_call_target="tpu_custom_call" | custom-call | flops 268435456 | bytes 2621440 | tf_op jit(solution)/shard_map/pallas_call | solution.py:265
  10.1 0.0 copy-start.5
  10.1 0.0 copy-start.7
  10.1 0.0 collective-permute-done.refs_1_.refs_0_
  10.2 3.3 %collective-permute-start.1 = (bf16[4,128,128]{2,1,0:T(8,128)(2,1)S(1)}, bf16[4,128,128]{2,1,0:T(8,128)(2,1)S(1)}, u32[]{:S(2)}, u32[]{:S(2)}) collective-permute-start(bf16[4,128,128]{2,1,0:T(8,128)(2,1)S(1)} %shard_map.57), channel_id=1, source_target_pairs={{0,8},{4,12},{1,9},{5,13},{2,10},{6,14},{3,11},{7,15}} | collective-permute-start | bytes 393224 | tf_op jit(solution)/shard_map/ppermute | solution.py:281
  13.5 0.0 collective-permute-done.4.refs_1_.refs_4_
  13.6 1.3 %collective-permute-start.5 = (bf16[4,128,128]{2,1,0:T(8,128)(2,1)S(1)}, bf16[4,128,128]{2,1,0:T(8,128)(2,1)S(1)}, u32[]{:S(2)}, u32[]{:S(2)}) collective-permute-start(bf16[4,128,128]{2,1,0:T(8,128)(2,1)S(1)} %shard_map.60), channel_id=1, source_target_pairs={{0,8},{4,12},{1,9},{5,13},{2,10},{6,14},{3,11},{7,15}} | collective-permute-start | bytes 393224 | tf_op jit(solution)/shard_map/ppermute | solution.py:281
  14.9 0.6 collective-permute-done.1.refs_2_.refs_1_
  15.5 0.7 collective-permute-start.2
  16.2 1.4 %collective-permute-done.5.refs_2_.refs_5_ = bf16[4,128,128]{2,1,0:T(8,128)(2,1)S(1)} collective-permute-done((bf16[4,128,128]{2,1,0:T(8,128)(2,1)S(1)}, bf16[4,128,128]{2,1,0:T(8,128)(2,1)S(1)}, u32[]{:S(2)}, u32[]{:S(2)}) %collective-permute-start.5) | collective-permute-done | bytes 131104 | tf_op jit(solution)/shard_map/ppermute | solution.py:281
  17.6 0.7 collective-permute-start.6
  18.3 0.0 collective-permute-done.2.refs_3_.refs_2_
  18.3 0.1 shard_map.59
  18.4 0.7 collective-permute-start.3
  19.1 0.0 collective-permute-done.6.refs_3_.refs_6_
  19.1 0.1 shard_map.62
  19.1 0.7 collective-permute-start.7
  19.8 0.0 collective-permute-done.3.refs_3_
  19.8 0.0 collective-permute-done.7.refs_7_
  19.8 0.0 copy-done.5
  19.9 0.0 copy-done.7
  19.9 0.8 shard_map.63
  20.6 4.4 %collective-permute-start.8 = (bf16[256,1024]{1,0:T(8,128)(2,1)S(1)}, bf16[256,1024]{1,0:T(8,128)(2,1)S(1)}, u32[]{:S(2)}, u32[]{:S(2)}) collective-permute-start(bf16[256,1024]{1,0:T(8,128)(2,1)S(1)} %shard_map.63), channel_id=1, source_target_pairs={{0,8},{4,12},{8,0},{12,4},{16,24},{20,28},{24,16},{28,20},{1,9},{5... | collective-permute-start | bytes 1572872 | tf_op jit(solution)/shard_map/ppermute | solution.py:257
  25.0 6.8 %collective-permute-start.10 = (bf16[256,1024]{1,0:T(8,128)(2,1)S(1)}, bf16[256,1024]{1,0:T(8,128)(2,1)S(1)}, u32[]{:S(2)}, u32[]{:S(2)}) collective-permute-start(bf16[256,1024]{1,0:T(8,128)(2,1)S(1)} %shard_map.63), channel_id=1, source_target_pairs={{0,16},{1,17},{2,26},{3,27},{4,20},{5,21},{6,30},{7,31},{8,24},{9,... | collective-permute-start | bytes 1572872 | tf_op jit(solution)/shard_map/ppermute | solution.py:261
  31.8 1.4 %collective-permute-done.9.mate_ref = bf16[1024,512]{1,0:T(8,128)(2,1)} collective-permute-done((bf16[1024,512]{1,0:T(8,128)(2,1)}, bf16[1024,512]{1,0:T(8,128)(2,1)}, u32[]{:S(2)}, u32[]{:S(2)}) %collective-permute-start.9) | collective-permute-done | bytes 1048608 | tf_op jit(solution)/shard_map/ppermute | solution.py:257
  33.2 0.0 copy-start.6
  33.2 1.2 %copy-done.6 = bf16[1024,512]{1,0:T(8,128)(2,1)S(1)} copy-done((bf16[1024,512]{1,0:T(8,128)(2,1)S(1)}, bf16[1024,512]{1,0:T(8,128)(2,1)}, u32[]{:S(2)}) %copy-start.6) | copy-done | bytes 1048600
  34.4 1.4 %shard_map.64.weight_ref = bf16[2,1024,512]{2,1,0:T(8,128)(2,1)S(1)} custom-call(bf16[1024,512]{1,0:T(8,128)(2,1)S(1)} %copy-done.6, bf16[1024,512]{1,0:T(8,128)(2,1)} %collective-permute-done.9.mate_ref), custom_call_target="tpu_custom_call" | custom-call | bytes 4194304 | tf_op jit(solution)/shard_map/pallas_call | solution.py:285
  35.8 7.2 %collective-permute-done.8 = bf16[256,1024]{1,0:T(8,128)(2,1)S(1)} collective-permute-done((bf16[256,1024]{1,0:T(8,128)(2,1)S(1)}, bf16[256,1024]{1,0:T(8,128)(2,1)S(1)}, u32[]{:S(2)}, u32[]{:S(2)}) %collective-permute-start.8) | collective-permute-done | bytes 524320 | tf_op jit(solution)/shard_map/ppermute | solution.py:257
  42.9 0.1 broadcast_select_fusion.1
  43.0 0.7 shard_map.67.light_ref
  43.7 0.9 collective-permute-done.10.heavy_ref
  44.6 0.7 shard_map.68
  45.3 11.5 %collective-permute-start.13 = (bf16[2,256,512]{2,1,0:T(8,128)(2,1)S(1)}, bf16[2,256,512]{2,1,0:T(8,128)(2,1)S(1)}, u32[]{:S(2)}, u32[]{:S(2)}) collective-permute-start(bf16[2,256,512]{2,1,0:T(8,128)(2,1)S(1)} %get-tuple-element.26), channel_id=1, source_target_pairs={{0,1},{1,0},{2,3},{3,2},{4,5},{5,4},{6,7},{7,6},{8,9},{9,8},{10,11... | collective-permute-start | bytes 1572872 | tf_op jit(solution)/shard_map/ppermute | solution.py:261
  56.8 0.1 collective-permute-start.11
  56.8 0.7 shard_map.65.light_ref
  57.6 0.7 collective-permute-done.13
  58.3 0.1 add_convert_fusion.1
  58.5 1.1 %collective-permute-start.14 = (bf16[2,256,512]{2,1,0:T(8,128)(2,1)S(1)}, bf16[2,256,512]{2,1,0:T(8,128)(2,1)S(1)}, u32[]{:S(2)}, u32[]{:S(2)}) collective-permute-start(bf16[2,256,512]{2,1,0:T(8,128)(2,1)S(1)} %add_convert_fusion.1), channel_id=1, source_target_pairs={{0,2},{1,3},{2,0},{3,1},{4,6},{5,7},{6,4},{7,5},{8,10},{9,11},{10,... | collective-permute-start | bytes 1572872 | tf_op jit(solution)/shard_map/ppermute | solution.py:261
  59.5 10.8 %collective-permute-done.11.heavy_ref = bf16[256,1024]{1,0:T(8,128)(2,1)S(1)} collective-permute-done((bf16[256,1024]{1,0:T(8,128)(2,1)S(1)}, bf16[256,1024]{1,0:T(8,128)(2,1)S(1)}, u32[]{:S(2)}, u32[]{:S(2)}) %collective-permute-start.11) | collective-permute-done | bytes 524320 | tf_op jit(solution)/shard_map/ppermute | solution.py:257
  70.3 0.7 shard_map.66
  71.0 0.9 %collective-permute-start.12 = (bf16[2,256,512]{2,1,0:T(8,128)(2,1)S(1)}, bf16[2,256,512]{2,1,0:T(8,128)(2,1)S(1)}, u32[]{:S(2)}, u32[]{:S(2)}) collective-permute-start(bf16[2,256,512]{2,1,0:T(8,128)(2,1)S(1)} %get-tuple-element.24), channel_id=1, source_target_pairs={{0,1},{1,0},{2,3},{3,2},{4,5},{5,4},{6,7},{7,6},{8,9},{9,8},{10,11... | collective-permute-start | bytes 1572872 | tf_op jit(solution)/shard_map/ppermute | solution.py:261
  71.9 0.0 collective-permute-done.14
  71.9 1.5 %collective-permute-done.12 = bf16[2,256,512]{2,1,0:T(8,128)(2,1)S(1)} collective-permute-done((bf16[2,256,512]{2,1,0:T(8,128)(2,1)S(1)}, bf16[2,256,512]{2,1,0:T(8,128)(2,1)S(1)}, u32[]{:S(2)}, u32[]{:S(2)}) %collective-permute-start.12) | collective-permute-done | bytes 524320 | tf_op jit(solution)/shard_map/ppermute | solution.py:261
  73.5 0.2 add_convert_fusion
  73.7 4.3 %collective-permute-start.15 = (bf16[2,256,512]{2,1,0:T(8,128)(2,1)S(1)}, bf16[2,256,512]{2,1,0:T(8,128)(2,1)S(1)}, u32[]{:S(2)}, u32[]{:S(2)}) collective-permute-start(bf16[2,256,512]{2,1,0:T(8,128)(2,1)S(1)} %add_convert_fusion), channel_id=1, source_target_pairs={{0,0},{1,24},{2,8},{3,16},{4,4},{5,28},{6,12},{7,20},{8,9},{9,17},... | collective-permute-start | bytes 1572872 | tf_op jit(solution)/shard_map/ppermute | solution.py:261
  78.0 11.5 %collective-permute-done.15 = bf16[2,256,512]{2,1,0:T(8,128)(2,1)S(1)} collective-permute-done((bf16[2,256,512]{2,1,0:T(8,128)(2,1)S(1)}, bf16[2,256,512]{2,1,0:T(8,128)(2,1)S(1)}, u32[]{:S(2)}, u32[]{:S(2)}) %collective-permute-start.15) | collective-permute-done | bytes 524320 | tf_op jit(solution)/shard_map/ppermute | solution.py:261
  89.6 0.9 pad_maximum_fusion
  (5 shorter events, 0.2 us)
Async XLA Ops:
  0.0 1.0 %copy-start = (bf16[256,1024]{1,0:T(8,128)(2,1)S(1)}, bf16[256,1024]{1,0:T(8,128)(2,1)}, u32[]{:S(2)}) copy-start(bf16[256,1024]{1,0:T(8,128)(2,1)} %k_ref.3) | copy-start | bytes 1572868
  1.0 1.0 %copy-start.2 = (bf16[256,1024]{1,0:T(8,128)(2,1)S(1)}, bf16[256,1024]{1,0:T(8,128)(2,1)}, u32[]{:S(2)}) copy-start(bf16[256,1024]{1,0:T(8,128)(2,1)} %v_ref.3) | copy-start | bytes 1572868
  2.4 7.7 %collective-permute-start = (bf16[4,128,128]{2,1,0:T(8,128)(2,1)S(1)}, bf16[4,128,128]{2,1,0:T(8,128)(2,1)S(1)}, u32[]{:S(2)}, u32[]{:S(2)}) collective-permute-start(bf16[4,128,128]{2,1,0:T(8,128)(2,1)S(1)} %get-tuple-element.16), channel_id=1, source_target_pairs={{0,4},{4,0},{8,12},{12,8},{16,20},{20,16},{24,28},{28,24},{1,5},{5... | collective-permute-start | bytes 393224 | tf_op jit(solution)/shard_map/ppermute | solution.py:257
  4.6 8.9 %collective-permute-start.4 = (bf16[4,128,128]{2,1,0:T(8,128)(2,1)S(1)}, bf16[4,128,128]{2,1,0:T(8,128)(2,1)S(1)}, u32[]{:S(2)}, u32[]{:S(2)}) collective-permute-start(bf16[4,128,128]{2,1,0:T(8,128)(2,1)S(1)} %get-tuple-element.20), channel_id=1, source_target_pairs={{0,4},{4,0},{8,12},{12,8},{16,20},{20,16},{24,28},{28,24},{1,5},{5... | collective-permute-start | bytes 393224 | tf_op jit(solution)/shard_map/ppermute | solution.py:257
  4.7 28.5 %collective-permute-start.9 = (bf16[1024,512]{1,0:T(8,128)(2,1)}, bf16[1024,512]{1,0:T(8,128)(2,1)}, u32[]{:S(2)}, u32[]{:S(2)}) collective-permute-start(bf16[1024,512]{1,0:T(8,128)(2,1)} %own_ref.1), channel_id=1, source_target_pairs={{0,4},{4,0},{8,12},{12,8},{16,20},{20,16},{24,28},{28,24},{1,5},{5... | collective-permute-start | bytes 3145736 | tf_op jit(solution)/shard_map/ppermute | solution.py:257
  6.0 1.0 %copy-start.1 = (bf16[256,1024]{1,0:T(8,128)(2,1)S(1)}, bf16[256,1024]{1,0:T(8,128)(2,1)}, u32[]{:S(2)}) copy-start(bf16[256,1024]{1,0:T(8,128)(2,1)} %k_ref.3) | copy-start | bytes 1572868
  7.1 1.0 %copy-start.3 = (bf16[256,1024]{1,0:T(8,128)(2,1)S(1)}, bf16[256,1024]{1,0:T(8,128)(2,1)}, u32[]{:S(2)}) copy-start(bf16[256,1024]{1,0:T(8,128)(2,1)} %v_ref.3) | copy-start | bytes 1572868
  8.1 1.0 %copy-start.4 = (bf16[256,1024]{1,0:T(8,128)(2,1)S(1)}, bf16[256,1024]{1,0:T(8,128)(2,1)}, u32[]{:S(2)}) copy-start(bf16[256,1024]{1,0:T(8,128)(2,1)} %q_ref.3) | copy-start | bytes 1572868
  10.1 9.7 %copy-start.5 = (bf16[256,1024]{1,0:T(8,128)(2,1)S(1)}, bf16[256,1024]{1,0:T(8,128)(2,1)}, u32[]{:S(2)}) copy-start(bf16[256,1024]{1,0:T(8,128)(2,1)} %q_ref.3) | copy-start | bytes 1572868
  10.1 9.7 %copy-start.7 = (f32[1024]{0:T(1024)S(1)}, f32[1024]{0:T(1024)}, u32[]{:S(2)}) copy-start(f32[1024]{0:T(1024)} %param.8) | copy-start | bytes 12292
  10.2 5.3 %collective-permute-start.1 = (bf16[4,128,128]{2,1,0:T(8,128)(2,1)S(1)}, bf16[4,128,128]{2,1,0:T(8,128)(2,1)S(1)}, u32[]{:S(2)}, u32[]{:S(2)}) collective-permute-start(bf16[4,128,128]{2,1,0:T(8,128)(2,1)S(1)} %shard_map.57), channel_id=1, source_target_pairs={{0,8},{4,12},{1,9},{5,13},{2,10},{6,14},{3,11},{7,15}} | collective-permute-start | bytes 393224 | tf_op jit(solution)/shard_map/ppermute | solution.py:281
  13.6 4.0 %collective-permute-start.5 = (bf16[4,128,128]{2,1,0:T(8,128)(2,1)S(1)}, bf16[4,128,128]{2,1,0:T(8,128)(2,1)S(1)}, u32[]{:S(2)}, u32[]{:S(2)}) collective-permute-start(bf16[4,128,128]{2,1,0:T(8,128)(2,1)S(1)} %shard_map.60), channel_id=1, source_target_pairs={{0,8},{4,12},{1,9},{5,13},{2,10},{6,14},{3,11},{7,15}} | collective-permute-start | bytes 393224 | tf_op jit(solution)/shard_map/ppermute | solution.py:281
  15.5 2.8 %collective-permute-start.2 = (bf16[4,128,128]{2,1,0:T(8,128)(2,1)S(1)}, bf16[4,128,128]{2,1,0:T(8,128)(2,1)S(1)}, u32[]{:S(2)}, u32[]{:S(2)}) collective-permute-start(bf16[4,128,128]{2,1,0:T(8,128)(2,1)S(1)} %shard_map.58), channel_id=1, source_target_pairs={{8,16},{12,20},{9,17},{13,21},{10,18},{14,22},{11,19},{15,23}} | collective-permute-start | bytes 393224 | tf_op jit(solution)/shard_map/ppermute | solution.py:281
  17.6 1.4 %collective-permute-start.6 = (bf16[4,128,128]{2,1,0:T(8,128)(2,1)S(1)}, bf16[4,128,128]{2,1,0:T(8,128)(2,1)S(1)}, u32[]{:S(2)}, u32[]{:S(2)}) collective-permute-start(bf16[4,128,128]{2,1,0:T(8,128)(2,1)S(1)} %shard_map.61), channel_id=1, source_target_pairs={{8,16},{12,20},{9,17},{13,21},{10,18},{14,22},{11,19},{15,23}} | collective-permute-start | bytes 393224 | tf_op jit(solution)/shard_map/ppermute | solution.py:281
  18.4 1.4 %collective-permute-start.3 = (bf16[4,128,128]{2,1,0:T(8,128)(2,1)S(1)}, bf16[4,128,128]{2,1,0:T(8,128)(2,1)S(1)}, u32[]{:S(2)}, u32[]{:S(2)}) collective-permute-start(bf16[4,128,128]{2,1,0:T(8,128)(2,1)S(1)} %shard_map.59), channel_id=1, source_target_pairs={{16,24},{20,28},{17,25},{21,29},{18,26},{22,30},{19,27},{23,31}} | collective-permute-start | bytes 393224 | tf_op jit(solution)/shard_map/ppermute | solution.py:281
  19.1 0.7 collective-permute-start.7
  20.6 22.3 %collective-permute-start.8 = (bf16[256,1024]{1,0:T(8,128)(2,1)S(1)}, bf16[256,1024]{1,0:T(8,128)(2,1)S(1)}, u32[]{:S(2)}, u32[]{:S(2)}) collective-permute-start(bf16[256,1024]{1,0:T(8,128)(2,1)S(1)} %shard_map.63), channel_id=1, source_target_pairs={{0,8},{4,12},{8,0},{12,4},{16,24},{20,28},{24,16},{28,20},{1,9},{5... | collective-permute-start | bytes 1572872 | tf_op jit(solution)/shard_map/ppermute | solution.py:257
  25.0 19.6 %collective-permute-start.10 = (bf16[256,1024]{1,0:T(8,128)(2,1)S(1)}, bf16[256,1024]{1,0:T(8,128)(2,1)S(1)}, u32[]{:S(2)}, u32[]{:S(2)}) collective-permute-start(bf16[256,1024]{1,0:T(8,128)(2,1)S(1)} %shard_map.63), channel_id=1, source_target_pairs={{0,16},{1,17},{2,26},{3,27},{4,20},{5,21},{6,30},{7,31},{8,24},{9,... | collective-permute-start | bytes 1572872 | tf_op jit(solution)/shard_map/ppermute | solution.py:261
  33.2 1.2 %copy-start.6 = (bf16[1024,512]{1,0:T(8,128)(2,1)S(1)}, bf16[1024,512]{1,0:T(8,128)(2,1)}, u32[]{:S(2)}) copy-start(bf16[1024,512]{1,0:T(8,128)(2,1)} %own_ref.1) | copy-start | bytes 3145732
  45.3 13.0 %collective-permute-start.13 = (bf16[2,256,512]{2,1,0:T(8,128)(2,1)S(1)}, bf16[2,256,512]{2,1,0:T(8,128)(2,1)S(1)}, u32[]{:S(2)}, u32[]{:S(2)}) collective-permute-start(bf16[2,256,512]{2,1,0:T(8,128)(2,1)S(1)} %get-tuple-element.26), channel_id=1, source_target_pairs={{0,1},{1,0},{2,3},{3,2},{4,5},{5,4},{6,7},{7,6},{8,9},{9,8},{10,11... | collective-permute-start | bytes 1572872 | tf_op jit(solution)/shard_map/ppermute | solution.py:261
  56.8 13.5 %collective-permute-start.11 = (bf16[256,1024]{1,0:T(8,128)(2,1)S(1)}, bf16[256,1024]{1,0:T(8,128)(2,1)S(1)}, u32[]{:S(2)}, u32[]{:S(2)}) collective-permute-start(bf16[256,1024]{1,0:T(8,128)(2,1)S(1)} %collective-permute-done.10.heavy_ref), channel_id=1, source_target_pairs={{0,8},{4,12},{8,0},{12,4},{16,24},{20,28},{24,16},{28,20},{1,9},{5... | collective-permute-start | bytes 1572872 | tf_op jit(solution)/shard_map/ppermute | solution.py:257
  58.5 13.5 %collective-permute-start.14 = (bf16[2,256,512]{2,1,0:T(8,128)(2,1)S(1)}, bf16[2,256,512]{2,1,0:T(8,128)(2,1)S(1)}, u32[]{:S(2)}, u32[]{:S(2)}) collective-permute-start(bf16[2,256,512]{2,1,0:T(8,128)(2,1)S(1)} %add_convert_fusion.1), channel_id=1, source_target_pairs={{0,2},{1,3},{2,0},{3,1},{4,6},{5,7},{6,4},{7,5},{8,10},{9,11},{10,... | collective-permute-start | bytes 1572872 | tf_op jit(solution)/shard_map/ppermute | solution.py:261
  71.0 2.5 %collective-permute-start.12 = (bf16[2,256,512]{2,1,0:T(8,128)(2,1)S(1)}, bf16[2,256,512]{2,1,0:T(8,128)(2,1)S(1)}, u32[]{:S(2)}, u32[]{:S(2)}) collective-permute-start(bf16[2,256,512]{2,1,0:T(8,128)(2,1)S(1)} %get-tuple-element.24), channel_id=1, source_target_pairs={{0,1},{1,0},{2,3},{3,2},{4,5},{5,4},{6,7},{7,6},{8,9},{9,8},{10,11... | collective-permute-start | bytes 1572872 | tf_op jit(solution)/shard_map/ppermute | solution.py:261
  73.7 15.9 %collective-permute-start.15 = (bf16[2,256,512]{2,1,0:T(8,128)(2,1)S(1)}, bf16[2,256,512]{2,1,0:T(8,128)(2,1)S(1)}, u32[]{:S(2)}, u32[]{:S(2)}) collective-permute-start(bf16[2,256,512]{2,1,0:T(8,128)(2,1)S(1)} %add_convert_fusion), channel_id=1, source_target_pairs={{0,0},{1,24},{2,8},{3,16},{4,4},{5,28},{6,12},{7,20},{8,9},{9,17},... | collective-permute-start | bytes 1572872 | tf_op jit(solution)/shard_map/ppermute | solution.py:261

commit v23 on v22

--- a/solution.py
+++ b/solution.py
@@ -260,7 +260,7 @@
         pairs = [(at(*d), at(*place_of(*d))) for d in devices if chosen(*d)]
         return lax.ppermute(value, both, pairs)
 
-    parts = 2
+    parts = 2 if heads % 2 == 0 else 1
     wide, narrow = block_states(key_vectors, value_vectors, parts)
     within = call(
         within_kernel, jax.ShapeDtypeStruct((rows, features), F32), 4 * size * BLOCK, 10 * size
@@ -269,7 +269,7 @@
 
     def add(*values):
         return call(
-            sum_kernel, jax.ShapeDtypeStruct(values[0].shape, BF16), size, 4 * values[0].size
+            sum_kernel, jax.ShapeDtypeStruct(values[0].shape, BF16), size * 3072, 4 * values[0].size
         )(*values)
 
     states = [[swap(part, 1)] for part in narrow]

time: 91 us -> 96.4 us (1.059)
  local copies, waits for them, and re-layouts: 6.44 us -> 11.1 us
  Pallas kernels: 6.54 us -> 7.88 us
  starting transfers between devices: 39.9 us -> 38.7 us
    unnamed x16 -> x36, local copies, waits for them, and re-layouts: 6.44 us -> 11.1 us
    ppermute x5, waiting for transfers between devices: 19.3 us -> 21 us  [swap(): return lax.ppermute(value, 'seq', [(s, s ^ mask) for s in range(8)])]
    pallas_call x6, Pallas kernels: 0.26 us -> 1.6 us  [add(): call(sum_kernel, jax.ShapeDtypeStruct(values[0].shape, BF16), size * 3072...]
    ppermute x6, waiting for transfers between devices: 1.99 us -> 0.85 us  [pairs_body(): states[part].append(lax.ppermute(onward[part], 'seq', pairs))]
  transfers between devices with their start and end apart: 16 -> 16, of which waited for: 9 -> 7; matrix products, arithmetic and copies ran while one was open for 0% -> 0% of each run, Pallas kernels for 6% -> 7%
where the time goes in v23:
time: 96.4 us; the launch traced here: 95.8 us
  starting transfers between devices  38.7 us (40%)
  waiting for transfers between devices  36.5 us (38%)
  local copies, waits for them, and re-layouts  11.1 us (12%)
  Pallas kernels  7.88 us (8%)
  other arithmetic  1.33 us (1%)
    ppermute x5, starting transfers between devices, move(): return lax.ppermute(value, both, pairs)  23.6 us
    ppermute x5, waiting for transfers between devices, swap(): return lax.ppermute(value, 'seq', [(s, s ^ mask) for s in range(8)])  21 us
    ppermute x5, waiting for transfers between devices, move(): return lax.ppermute(value, both, pairs)  14.7 us
    unnamed x36, local copies, waits for them, and re-layouts  11.1 us
    ppermute x6, starting transfers between devices, pairs_body(): states[part].append(lax.ppermute(onward[part], 'seq', pairs))  7.7 us
    ppermute x5, starting transfers between devices, swap(): return lax.ppermute(value, 'seq', [(s, s ^ mask) for s in range(8)])  7.41 us
  transfers between devices with their start and end apart: 16, of which 7 were waited for; matrix products, arithmetic and copies ran while one was open for 0% of the time, Pallas kernels for 7%

profile of v23, /device:TPU:1, one launch (start us, length us, event | category | flops | bytes accessed | tf_op | source)
XLA Modules:
  0.0 95.8 jit_solution(14829885482641958122)
XLA Ops:
  0.0 1.0 %copy-done = bf16[256,1024]{1,0:T(8,128)(2,1)S(1)} copy-done((bf16[256,1024]{1,0:T(8,128)(2,1)S(1)}, bf16[256,1024]{1,0:T(8,128)(2,1)}, u32[]{:S(2)}) %copy-start) | copy-done | bytes 524312
  1.0 1.0 %copy-done.2 = bf16[256,1024]{1,0:T(8,128)(2,1)S(1)} copy-done((bf16[256,1024]{1,0:T(8,128)(2,1)S(1)}, bf16[256,1024]{1,0:T(8,128)(2,1)}, u32[]{:S(2)}) %copy-start.2) | copy-done | bytes 524312
  2.1 0.4 shard_map.55
  2.4 2.1 %collective-permute-start = (bf16[4,128,128]{2,1,0:T(8,128)(2,1)S(1)}, bf16[4,128,128]{2,1,0:T(8,128)(2,1)S(1)}, u32[]{:S(2)}, u32[]{:S(2)}) collective-permute-start(bf16[4,128,128]{2,1,0:T(8,128)(2,1)S(1)} %get-tuple-element.16), channel_id=1, source_target_pairs={{0,4},{4,0},{8,12},{12,8},{16,20},{20,16},{24,28},{28,24},{1,5},{5... | collective-permute-start | bytes 393224 | tf_op jit(solution)/shard_map/ppermute | solution.py:257
  4.6 0.1 collective-permute-start.4
  4.7 1.0 %copy-done.1 = bf16[256,1024]{1,0:T(8,128)(2,1)S(1)} copy-done((bf16[256,1024]{1,0:T(8,128)(2,1)S(1)}, bf16[256,1024]{1,0:T(8,128)(2,1)}, u32[]{:S(2)}) %copy-start.1) | copy-done | bytes 524312
  5.7 1.0 %copy-done.3 = bf16[256,1024]{1,0:T(8,128)(2,1)S(1)} copy-done((bf16[256,1024]{1,0:T(8,128)(2,1)S(1)}, bf16[256,1024]{1,0:T(8,128)(2,1)}, u32[]{:S(2)}) %copy-start.3) | copy-done | bytes 524312
  6.7 1.0 %copy-done.4 = bf16[256,1024]{1,0:T(8,128)(2,1)S(1)} copy-done((bf16[256,1024]{1,0:T(8,128)(2,1)S(1)}, bf16[256,1024]{1,0:T(8,128)(2,1)}, u32[]{:S(2)}) %copy-start.4) | copy-done | bytes 524312
  7.8 0.9 shard_map.56.within_ref
  8.7 0.0 collective-permute-done.refs_1_.refs_0_
  8.8 0.0 copy-start.6
  8.8 3.5 %collective-permute-start.1 = (bf16[4,128,128]{2,1,0:T(8,128)(2,1)S(1)}, bf16[4,128,128]{2,1,0:T(8,128)(2,1)S(1)}, u32[]{:S(2)}, u32[]{:S(2)}) collective-permute-start(bf16[4,128,128]{2,1,0:T(8,128)(2,1)S(1)} %shard_map.57), channel_id=1, source_target_pairs={{0,8},{4,12},{1,9},{5,13},{2,10},{6,14},{3,11},{7,15}} | collective-permute-start | bytes 393224 | tf_op jit(solution)/shard_map/ppermute | solution.py:281
  12.3 0.0 collective-permute-done.4.refs_1_.refs_4_
  12.3 1.4 %collective-permute-start.5 = (bf16[4,128,128]{2,1,0:T(8,128)(2,1)S(1)}, bf16[4,128,128]{2,1,0:T(8,128)(2,1)S(1)}, u32[]{:S(2)}, u32[]{:S(2)}) collective-permute-start(bf16[4,128,128]{2,1,0:T(8,128)(2,1)S(1)} %shard_map.60), channel_id=1, source_target_pairs={{0,8},{4,12},{1,9},{5,13},{2,10},{6,14},{3,11},{7,15}} | collective-permute-start | bytes 393224 | tf_op jit(solution)/shard_map/ppermute | solution.py:281
  13.8 0.0 copy-done.6
  13.8 1.3 %collective-permute-start.9 = (bf16[1024,512]{1,0:T(8,128)(2,1)S(1)}, bf16[1024,512]{1,0:T(8,128)(2,1)}, u32[]{:S(2)}, u32[]{:S(2)}) collective-permute-start(bf16[1024,512]{1,0:T(8,128)(2,1)S(1)} %copy-done.6), channel_id=1, source_target_pairs={{0,4},{4,0},{8,12},{12,8},{16,20},{20,16},{24,28},{28,24},{1,5},{5... | collective-permute-start | bytes 3145736 | tf_op jit(solution)/shard_map/ppermute | solution.py:257
  15.1 0.0 collective-permute-done.1.refs_2_.refs_1_
  15.1 0.7 collective-permute-start.2
  15.8 0.8 collective-permute-done.5.refs_2_.refs_5_
  16.7 0.7 collective-permute-start.6
  17.4 0.0 collective-permute-done.2.refs_3_.refs_2_
  17.4 0.0 copy-start.9
  17.4 0.7 shard_map.59
  18.1 0.8 collective-permute-start.3
  18.9 0.0 collective-permute-done.6.refs_3_.refs_6_
  18.9 0.0 copy-done.7
  18.9 0.0 copy-start.11
  18.9 0.7 shard_map.62
  19.7 0.7 collective-permute-start.7
  20.4 0.0 collective-permute-done.3.refs_3_
  20.4 0.7 copy-done.13
  21.0 0.0 collective-permute-done.7.refs_7_
  21.0 0.7 copy-done.15
  21.7 0.0 copy-done.11
  21.7 0.9 copy-done.8
  22.6 0.9 copy-done.10
  23.5 0.9 copy-done.12
  24.4 0.9 copy-done.14
  25.3 0.9 copy-done.16
  26.2 0.7 shard_map.63
  27.0 3.8 %collective-permute-start.8 = (bf16[256,1024]{1,0:T(8,128)(2,1)S(1)}, bf16[256,1024]{1,0:T(8,128)(2,1)S(1)}, u32[]{:S(2)}, u32[]{:S(2)}) collective-permute-start(bf16[256,1024]{1,0:T(8,128)(2,1)S(1)} %shard_map.63), channel_id=1, source_target_pairs={{0,8},{4,12},{8,0},{12,4},{16,24},{20,28},{24,16},{28,20},{1,9},{5... | collective-permute-start | bytes 1572872 | tf_op jit(solution)/shard_map/ppermute | solution.py:257
  30.8 6.4 %collective-permute-start.10 = (bf16[256,1024]{1,0:T(8,128)(2,1)S(1)}, bf16[256,1024]{1,0:T(8,128)(2,1)S(1)}, u32[]{:S(2)}, u32[]{:S(2)}) collective-permute-start(bf16[256,1024]{1,0:T(8,128)(2,1)S(1)} %shard_map.63), channel_id=1, source_target_pairs={{0,16},{1,17},{2,26},{3,27},{4,20},{5,21},{6,30},{7,31},{8,24},{9,... | collective-permute-start | bytes 1572872 | tf_op jit(solution)/shard_map/ppermute | solution.py:261
  37.2 0.0 collective-permute-done.9.mate_ref
  37.2 1.4 %shard_map.64.weight_ref = bf16[2,1024,512]{2,1,0:T(8,128)(2,1)S(1)} custom-call(bf16[1024,512]{1,0:T(8,128)(2,1)S(1)} %copy-done.6, bf16[1024,512]{1,0:T(8,128)(2,1)} %collective-permute-done.9.mate_ref), custom_call_target="tpu_custom_call" | custom-call | bytes 4194304 | tf_op jit(solution)/shard_map/pallas_call | solution.py:285
  38.5 10.2 %collective-permute-done.8 = bf16[256,1024]{1,0:T(8,128)(2,1)S(1)} collective-permute-done((bf16[256,1024]{1,0:T(8,128)(2,1)S(1)}, bf16[256,1024]{1,0:T(8,128)(2,1)S(1)}, u32[]{:S(2)}, u32[]{:S(2)}) %collective-permute-start.8) | collective-permute-done | bytes 524320 | tf_op jit(solution)/shard_map/ppermute | solution.py:257
  48.8 0.1 broadcast_select_fusion.1
  48.9 0.7 shard_map.67.light_ref
  49.6 0.9 collective-permute-done.10.heavy_ref
  50.5 0.7 shard_map.68
  51.2 10.9 %collective-permute-start.13 = (bf16[2,256,512]{2,1,0:T(8,128)(2,1)S(1)}, bf16[2,256,512]{2,1,0:T(8,128)(2,1)S(1)}, u32[]{:S(2)}, u32[]{:S(2)}) collective-permute-start(bf16[2,256,512]{2,1,0:T(8,128)(2,1)S(1)} %get-tuple-element.26), channel_id=1, source_target_pairs={{0,1},{1,0},{2,3},{3,2},{4,5},{5,4},{6,7},{7,6},{8,9},{9,8},{10,11... | collective-permute-start | bytes 1572872 | tf_op jit(solution)/shard_map/ppermute | solution.py:261
  62.1 0.1 collective-permute-start.11
  62.2 0.7 shard_map.65.light_ref
  62.9 0.7 collective-permute-done.13
  63.7 0.1 add_convert_fusion.1
  63.8 1.1 %collective-permute-start.14 = (bf16[2,256,512]{2,1,0:T(8,128)(2,1)S(1)}, bf16[2,256,512]{2,1,0:T(8,128)(2,1)S(1)}, u32[]{:S(2)}, u32[]{:S(2)}) collective-permute-start(bf16[2,256,512]{2,1,0:T(8,128)(2,1)S(1)} %add_convert_fusion.1), channel_id=1, source_target_pairs={{0,2},{1,3},{2,0},{3,1},{4,6},{5,7},{6,4},{7,5},{8,10},{9,11},{10,... | collective-permute-start | bytes 1572872 | tf_op jit(solution)/shard_map/ppermute | solution.py:261
  64.9 10.8 %collective-permute-done.11.heavy_ref = bf16[256,1024]{1,0:T(8,128)(2,1)S(1)} collective-permute-done((bf16[256,1024]{1,0:T(8,128)(2,1)S(1)}, bf16[256,1024]{1,0:T(8,128)(2,1)S(1)}, u32[]{:S(2)}, u32[]{:S(2)}) %collective-permute-start.11) | collective-permute-done | bytes 524320 | tf_op jit(solution)/shard_map/ppermute | solution.py:257
  75.6 0.7 shard_map.66
  76.4 0.9 collective-permute-start.12
  77.3 0.0 collective-permute-done.14
  77.3 1.5 %collective-permute-done.12 = bf16[2,256,512]{2,1,0:T(8,128)(2,1)S(1)} collective-permute-done((bf16[2,256,512]{2,1,0:T(8,128)(2,1)S(1)}, bf16[2,256,512]{2,1,0:T(8,128)(2,1)S(1)}, u32[]{:S(2)}, u32[]{:S(2)}) %collective-permute-start.12) | collective-permute-done | bytes 524320 | tf_op jit(solution)/shard_map/ppermute | solution.py:261
  78.8 0.2 add_convert_fusion
  79.0 4.3 %collective-permute-start.15 = (bf16[2,256,512]{2,1,0:T(8,128)(2,1)S(1)}, bf16[2,256,512]{2,1,0:T(8,128)(2,1)S(1)}, u32[]{:S(2)}, u32[]{:S(2)}) collective-permute-start(bf16[2,256,512]{2,1,0:T(8,128)(2,1)S(1)} %add_convert_fusion), channel_id=1, source_target_pairs={{0,0},{1,24},{2,8},{3,16},{4,4},{5,28},{6,12},{7,20},{8,9},{9,17},... | collective-permute-start | bytes 1572872 | tf_op jit(solution)/shard_map/ppermute | solution.py:261
  83.4 11.5 %collective-permute-done.15 = bf16[2,256,512]{2,1,0:T(8,128)(2,1)S(1)} collective-permute-done((bf16[2,256,512]{2,1,0:T(8,128)(2,1)S(1)}, bf16[2,256,512]{2,1,0:T(8,128)(2,1)S(1)}, u32[]{:S(2)}, u32[]{:S(2)}) %collective-permute-start.15) | collective-permute-done | bytes 524320 | tf_op jit(solution)/shard_map/ppermute | solution.py:261
  94.9 0.9 pad_maximum_fusion
  (23 shorter events, 0.2 us)
Async XLA Ops:
  0.0 1.0 %copy-start = (bf16[256,1024]{1,0:T(8,128)(2,1)S(1)}, bf16[256,1024]{1,0:T(8,128)(2,1)}, u32[]{:S(2)}) copy-start(bf16[256,1024]{1,0:T(8,128)(2,1)} %k_ref.3) | copy-start | bytes 1572868
  1.0 1.0 %copy-start.2 = (bf16[256,1024]{1,0:T(8,128)(2,1)S(1)}, bf16[256,1024]{1,0:T(8,128)(2,1)}, u32[]{:S(2)}) copy-start(bf16[256,1024]{1,0:T(8,128)(2,1)} %v_ref.3) | copy-start | bytes 1572868
  2.4 6.3 %collective-permute-start = (bf16[4,128,128]{2,1,0:T(8,128)(2,1)S(1)}, bf16[4,128,128]{2,1,0:T(8,128)(2,1)S(1)}, u32[]{:S(2)}, u32[]{:S(2)}) collective-permute-start(bf16[4,128,128]{2,1,0:T(8,128)(2,1)S(1)} %get-tuple-element.16), channel_id=1, source_target_pairs={{0,4},{4,0},{8,12},{12,8},{16,20},{20,16},{24,28},{28,24},{1,5},{5... | collective-permute-start | bytes 393224 | tf_op jit(solution)/shard_map/ppermute | solution.py:257
  4.6 7.7 %collective-permute-start.4 = (bf16[4,128,128]{2,1,0:T(8,128)(2,1)S(1)}, bf16[4,128,128]{2,1,0:T(8,128)(2,1)S(1)}, u32[]{:S(2)}, u32[]{:S(2)}) collective-permute-start(bf16[4,128,128]{2,1,0:T(8,128)(2,1)S(1)} %get-tuple-element.20), channel_id=1, source_target_pairs={{0,4},{4,0},{8,12},{12,8},{16,20},{20,16},{24,28},{28,24},{1,5},{5... | collective-permute-start | bytes 393224 | tf_op jit(solution)/shard_map/ppermute | solution.py:257
  4.7 1.0 %copy-start.1 = (bf16[256,1024]{1,0:T(8,128)(2,1)S(1)}, bf16[256,1024]{1,0:T(8,128)(2,1)}, u32[]{:S(2)}) copy-start(bf16[256,1024]{1,0:T(8,128)(2,1)} %k_ref.3) | copy-start | bytes 1572868
  5.7 1.0 %copy-start.3 = (bf16[256,1024]{1,0:T(8,128)(2,1)S(1)}, bf16[256,1024]{1,0:T(8,128)(2,1)}, u32[]{:S(2)}) copy-start(bf16[256,1024]{1,0:T(8,128)(2,1)} %v_ref.3) | copy-start | bytes 1572868
  6.7 1.0 %copy-start.4 = (bf16[256,1024]{1,0:T(8,128)(2,1)S(1)}, bf16[256,1024]{1,0:T(8,128)(2,1)}, u32[]{:S(2)}) copy-start(bf16[256,1024]{1,0:T(8,128)(2,1)} %q_ref.3) | copy-start | bytes 1572868
  8.8 5.0 %copy-start.6 = (bf16[1024,512]{1,0:T(8,128)(2,1)S(1)}, bf16[1024,512]{1,0:T(8,128)(2,1)}, u32[]{:S(2)}) copy-start(bf16[1024,512]{1,0:T(8,128)(2,1)} %own_ref.1) | copy-start | bytes 3145732
  8.8 6.3 %collective-permute-start.1 = (bf16[4,128,128]{2,1,0:T(8,128)(2,1)S(1)}, bf16[4,128,128]{2,1,0:T(8,128)(2,1)S(1)}, u32[]{:S(2)}, u32[]{:S(2)}) collective-permute-start(bf16[4,128,128]{2,1,0:T(8,128)(2,1)S(1)} %shard_map.57), channel_id=1, source_target_pairs={{0,8},{4,12},{1,9},{5,13},{2,10},{6,14},{3,11},{7,15}} | collective-permute-start | bytes 393224 | tf_op jit(solution)/shard_map/ppermute | solution.py:281
  12.3 4.3 %collective-permute-start.5 = (bf16[4,128,128]{2,1,0:T(8,128)(2,1)S(1)}, bf16[4,128,128]{2,1,0:T(8,128)(2,1)S(1)}, u32[]{:S(2)}, u32[]{:S(2)}) collective-permute-start(bf16[4,128,128]{2,1,0:T(8,128)(2,1)S(1)} %shard_map.60), channel_id=1, source_target_pairs={{0,8},{4,12},{1,9},{5,13},{2,10},{6,14},{3,11},{7,15}} | collective-permute-start | bytes 393224 | tf_op jit(solution)/shard_map/ppermute | solution.py:281
  13.8 23.4 %collective-permute-start.9 = (bf16[1024,512]{1,0:T(8,128)(2,1)S(1)}, bf16[1024,512]{1,0:T(8,128)(2,1)}, u32[]{:S(2)}, u32[]{:S(2)}) collective-permute-start(bf16[1024,512]{1,0:T(8,128)(2,1)S(1)} %copy-done.6), channel_id=1, source_target_pairs={{0,4},{4,0},{8,12},{12,8},{16,20},{20,16},{24,28},{28,24},{1,5},{5... | collective-permute-start | bytes 3145736 | tf_op jit(solution)/shard_map/ppermute | solution.py:257
  15.1 2.2 %collective-permute-start.2 = (bf16[4,128,128]{2,1,0:T(8,128)(2,1)S(1)}, bf16[4,128,128]{2,1,0:T(8,128)(2,1)S(1)}, u32[]{:S(2)}, u32[]{:S(2)}) collective-permute-start(bf16[4,128,128]{2,1,0:T(8,128)(2,1)S(1)} %shard_map.58), channel_id=1, source_target_pairs={{8,16},{12,20},{9,17},{13,21},{10,18},{14,22},{11,19},{15,23}} | collective-permute-start | bytes 393224 | tf_op jit(solution)/shard_map/ppermute | solution.py:281
  16.6 2.3 %copy-start.7 = (bf16[4,128,128]{2,1,0:T(8,128)(2,1)}, bf16[4,128,128]{2,1,0:T(8,128)(2,1)S(1)}, u32[]{:S(2)}) copy-start(bf16[4,128,128]{2,1,0:T(8,128)(2,1)S(1)} %collective-permute-done.5.refs_2_.refs_5_) | copy-start | bytes 393220
  16.7 2.2 %collective-permute-start.6 = (bf16[4,128,128]{2,1,0:T(8,128)(2,1)S(1)}, bf16[4,128,128]{2,1,0:T(8,128)(2,1)S(1)}, u32[]{:S(2)}, u32[]{:S(2)}) collective-permute-start(bf16[4,128,128]{2,1,0:T(8,128)(2,1)S(1)} %shard_map.61), channel_id=1, source_target_pairs={{8,16},{12,20},{9,17},{13,21},{10,18},{14,22},{11,19},{15,23}} | collective-permute-start | bytes 393224 | tf_op jit(solution)/shard_map/ppermute | solution.py:281
  17.4 2.3 %copy-start.9 = (bf16[4,128,128]{2,1,0:T(8,128)(2,1)}, bf16[4,128,128]{2,1,0:T(8,128)(2,1)S(1)}, u32[]{:S(2)}) copy-start(bf16[4,128,128]{2,1,0:T(8,128)(2,1)S(1)} %collective-permute-done.2.refs_3_.refs_2_) | copy-start | bytes 393220
  18.1 3.6 %copy-start.5 = (bf16[256,1024]{1,0:T(8,128)(2,1)S(1)}, bf16[256,1024]{1,0:T(8,128)(2,1)}, u32[]{:S(2)}) copy-start(bf16[256,1024]{1,0:T(8,128)(2,1)} %q_ref.3) | copy-start | bytes 1572868
  18.1 3.6 %copy-start.17 = (f32[1024]{0:T(1024)S(1)}, f32[1024]{0:T(1024)}, u32[]{:S(2)}) copy-start(f32[1024]{0:T(1024)} %param.8) | copy-start | bytes 12292
  18.1 2.2 %collective-permute-start.3 = (bf16[4,128,128]{2,1,0:T(8,128)(2,1)}, bf16[4,128,128]{2,1,0:T(8,128)(2,1)S(1)}, u32[]{:S(2)}, u32[]{:S(2)}) collective-permute-start(bf16[4,128,128]{2,1,0:T(8,128)(2,1)} %shard_map.59), channel_id=1, source_target_pairs={{16,24},{20,28},{17,25},{21,29},{18,26},{22,30},{19,27},{23,31}} | collective-permute-start | bytes 393224 | tf_op jit(solution)/shard_map/ppermute | solution.py:281
  18.9 2.8 %copy-start.11 = (bf16[4,128,128]{2,1,0:T(8,128)(2,1)}, bf16[4,128,128]{2,1,0:T(8,128)(2,1)S(1)}, u32[]{:S(2)}) copy-start(bf16[4,128,128]{2,1,0:T(8,128)(2,1)S(1)} %collective-permute-done.6.refs_3_.refs_6_) | copy-start | bytes 393220
  19.7 1.4 %collective-permute-start.7 = (bf16[4,128,128]{2,1,0:T(8,128)(2,1)}, bf16[4,128,128]{2,1,0:T(8,128)(2,1)S(1)}, u32[]{:S(2)}, u32[]{:S(2)}) collective-permute-start(bf16[4,128,128]{2,1,0:T(8,128)(2,1)} %shard_map.62), channel_id=1, source_target_pairs={{16,24},{20,28},{17,25},{21,29},{18,26},{22,30},{19,27},{23,31}} | collective-permute-start | bytes 393224 | tf_op jit(solution)/shard_map/ppermute | solution.py:281
  20.4 0.7 copy-start.13
  21.0 0.7 copy-start.15
  21.7 0.9 copy-start.8
  22.6 0.9 copy-start.10
  23.5 0.9 copy-start.12
  24.4 0.9 copy-start.14
  25.3 0.9 copy-start.16
  27.0 21.8 %collective-permute-start.8 = (bf16[256,1024]{1,0:T(8,128)(2,1)S(1)}, bf16[256,1024]{1,0:T(8,128)(2,1)S(1)}, u32[]{:S(2)}, u32[]{:S(2)}) collective-permute-start(bf16[256,1024]{1,0:T(8,128)(2,1)S(1)} %shard_map.63), channel_id=1, source_target_pairs={{0,8},{4,12},{8,0},{12,4},{16,24},{20,28},{24,16},{28,20},{1,9},{5... | collective-permute-start | bytes 1572872 | tf_op jit(solution)/shard_map/ppermute | solution.py:257
  30.8 19.7 %collective-permute-start.10 = (bf16[256,1024]{1,0:T(8,128)(2,1)S(1)}, bf16[256,1024]{1,0:T(8,128)(2,1)S(1)}, u32[]{:S(2)}, u32[]{:S(2)}) collective-permute-start(bf16[256,1024]{1,0:T(8,128)(2,1)S(1)} %shard_map.63), channel_id=1, source_target_pairs={{0,16},{1,17},{2,26},{3,27},{4,20},{5,21},{6,30},{7,31},{8,24},{9,... | collective-permute-start | bytes 1572872 | tf_op jit(solution)/shard_map/ppermute | solution.py:261
  51.2 12.5 %collective-permute-start.13 = (bf16[2,256,512]{2,1,0:T(8,128)(2,1)S(1)}, bf16[2,256,512]{2,1,0:T(8,128)(2,1)S(1)}, u32[]{:S(2)}, u32[]{:S(2)}) collective-permute-start(bf16[2,256,512]{2,1,0:T(8,128)(2,1)S(1)} %get-tuple-element.26), channel_id=1, source_target_pairs={{0,1},{1,0},{2,3},{3,2},{4,5},{5,4},{6,7},{7,6},{8,9},{9,8},{10,11... | collective-permute-start | bytes 1572872 | tf_op jit(solution)/shard_map/ppermute | solution.py:261
  62.1 13.5 %collective-permute-start.11 = (bf16[256,1024]{1,0:T(8,128)(2,1)S(1)}, bf16[256,1024]{1,0:T(8,128)(2,1)S(1)}, u32[]{:S(2)}, u32[]{:S(2)}) collective-permute-start(bf16[256,1024]{1,0:T(8,128)(2,1)S(1)} %collective-permute-done.10.heavy_ref), channel_id=1, source_target_pairs={{0,8},{4,12},{8,0},{12,4},{16,24},{20,28},{24,16},{28,20},{1,9},{5... | collective-permute-start | bytes 1572872 | tf_op jit(solution)/shard_map/ppermute | solution.py:257
  63.8 13.5 %collective-permute-start.14 = (bf16[2,256,512]{2,1,0:T(8,128)(2,1)S(1)}, bf16[2,256,512]{2,1,0:T(8,128)(2,1)S(1)}, u32[]{:S(2)}, u32[]{:S(2)}) collective-permute-start(bf16[2,256,512]{2,1,0:T(8,128)(2,1)S(1)} %add_convert_fusion.1), channel_id=1, source_target_pairs={{0,2},{1,3},{2,0},{3,1},{4,6},{5,7},{6,4},{7,5},{8,10},{9,11},{10,... | collective-permute-start | bytes 1572872 | tf_op jit(solution)/shard_map/ppermute | solution.py:261
  76.4 2.5 %collective-permute-start.12 = (bf16[2,256,512]{2,1,0:T(8,128)(2,1)S(1)}, bf16[2,256,512]{2,1,0:T(8,128)(2,1)S(1)}, u32[]{:S(2)}, u32[]{:S(2)}) collective-permute-start(bf16[2,256,512]{2,1,0:T(8,128)(2,1)S(1)} %get-tuple-element.24), channel_id=1, source_target_pairs={{0,1},{1,0},{2,3},{3,2},{4,5},{5,4},{6,7},{7,6},{8,9},{9,8},{10,11... | collective-permute-start | bytes 1572872 | tf_op jit(solution)/shard_map/ppermute | solution.py:261
  79.0 15.9 %collective-permute-start.15 = (bf16[2,256,512]{2,1,0:T(8,128)(2,1)S(1)}, bf16[2,256,512]{2,1,0:T(8,128)(2,1)S(1)}, u32[]{:S(2)}, u32[]{:S(2)}) collective-permute-start(bf16[2,256,512]{2,1,0:T(8,128)(2,1)S(1)} %add_convert_fusion), channel_id=1, source_target_pairs={{0,0},{1,24},{2,8},{3,16},{4,4},{5,28},{6,12},{7,20},{8,9},{9,17},... | collective-permute-start | bytes 1572872 | tf_op jit(solution)/shard_map/ppermute | solution.py:261

commit v24 on v23

--- a/solution.py
+++ b/solution.py
@@ -265,18 +265,18 @@
     within = call(
         within_kernel, jax.ShapeDtypeStruct((rows, features), F32), 4 * size * BLOCK, 10 * size
     )(queries, key_vectors, value_vectors)
-    mate_weight = swap(out_weight, 1)
-
-    def add(*values):
-        return call(
-            sum_kernel, jax.ShapeDtypeStruct(values[0].shape, BF16), size * 3072, 4 * values[0].size
-        )(*values)
+
+    def add(cost, *values):
+        out = jax.ShapeDtypeStruct(values[0].shape, BF16)
+        return call(sum_kernel, out, cost, 4 * values[0].size)(*values)
 
     states = [[swap(part, 1)] for part in narrow]
     states[0][0], within = lax.optimization_barrier((states[0][0], within))
+    weight, _ = lax.optimization_barrier((out_weight, states[1][0]))
+    mate_weight = swap(weight, 1)
     for plane in range(3):
         pairs = [(2 * plane + i, 2 * plane + 2 + i) for i in range(2)]
-        onward = [add(wide[part], *states[part]) for part in range(parts)]
+        onward = [add(size, wide[part], *states[part]) for part in range(parts)]
         for part in range(parts):
             states[part].append(lax.ppermute(onward[part], "seq", pairs))
     attended = attend(y, queries, within, norm_gain, states)
@@ -288,7 +288,6 @@
 
     straight = move(attended, lambda z, y, x, c: (z ^ (2 + x), y, x, c))
     beside = swap(attended, 2)
-    onward = swap(straight, 2)
 
     tile = jax.ShapeDtypeStruct((2, rows, half_cols), BF16)
     flops, moved = 4 * size * half_cols, 8 * size
@@ -311,6 +310,8 @@
         return call(project_kernel, tile, flops, moved)(tokens, weight)
 
     far_light = product(jnp.where(x == 0, beside, attended))
+    straight, far_light = lax.optimization_barrier((straight, far_light))
+    onward = swap(straight, 2)
     far = projected(far_light, straight).astype(BF16)
     crossed = move(far, lambda z, y, x, c: (z, y, 1 - x, c))
     near_light = product(jnp.where(x == 0, attended, beside))

time: 96.4 us -> 91.3 us (0.947)
  local copies, waits for them, and re-layouts: 11.1 us -> 5.22 us
  waiting for transfers between devices: 36.5 us -> 39.6 us
  starting transfers between devices: 38.7 us -> 37.6 us
  Pallas kernels: 7.88 us -> 6.86 us
    unnamed x36 -> x14, local copies, waits for them, and re-layouts: 11.1 us -> 5.22 us
    ppermute x5, waiting for transfers between devices: 21 us -> 22.6 us  [swap(): return lax.ppermute(value, 'seq', [(s, s ^ mask) for s in range(8)])]
    ppermute x6, waiting for transfers between devices: 0.85 us -> 2.23 us  [pairs_body(): states[part].append(lax.ppermute(onward[part], 'seq', pairs))]
    pallas_call x6, Pallas kernels: 1.6 us -> 0.26 us  [add(): return call(sum_kernel, out, cost, 4 * values[0].size)(*values)]
  transfers between devices with their start and end apart: 16 -> 16, of which waited for: 7 -> 7; matrix products, arithmetic and copies ran while one was open for 0% -> 0% of each run, Pallas kernels for 7% -> 6%
where the time goes in v24:
time: 91.3 us; the launch traced here: 90.8 us
  waiting for transfers between devices  39.6 us (43%)
  starting transfers between devices  37.6 us (41%)
  Pallas kernels  6.86 us (8%)
  local copies, waits for them, and re-layouts  5.22 us (6%)
  other arithmetic  1.32 us (1%)
    ppermute x5, starting transfers between devices, move(): return lax.ppermute(value, both, pairs)  23.2 us
    ppermute x5, waiting for transfers between devices, swap(): return lax.ppermute(value, 'seq', [(s, s ^ mask) for s in range(8)])  22.6 us
    ppermute x5, waiting for transfers between devices, move(): return lax.ppermute(value, both, pairs)  14.7 us
    ppermute x6, starting transfers between devices, pairs_body(): states[part].append(lax.ppermute(onward[part], 'seq', pairs))  7.58 us
    ppermute x5, starting transfers between devices, swap(): return lax.ppermute(value, 'seq', [(s, s ^ mask) for s in range(8)])  6.81 us
    unnamed x14, local copies, waits for them, and re-layouts  5.22 us
    ppermute x6, waiting for transfers between devices, pairs_body(): states[part].append(lax.ppermute(onward[part], 'seq', pairs))  2.23 us
  transfers between devices with their start and end apart: 16, of which 7 were waited for; matrix products, arithmetic and copies ran while one was open for 0% of the time, Pallas kernels for 6%

profile of v24, /device:TPU:1, one launch (start us, length us, event | category | flops | bytes accessed | tf_op | source)
XLA Modules:
  0.0 90.8 jit_solution(14103599464428797087)
XLA Ops:
  0.0 0.0 copy-start
  0.0 1.0 %copy-done = bf16[256,1024]{1,0:T(8,128)(2,1)S(1)} copy-done((bf16[256,1024]{1,0:T(8,128)(2,1)S(1)}, bf16[256,1024]{1,0:T(8,128)(2,1)}, u32[]{:S(2)}) %copy-start) | copy-done | bytes 524312
  1.0 0.0 copy-start.2
  1.0 1.0 %copy-done.2 = bf16[256,1024]{1,0:T(8,128)(2,1)S(1)} copy-done((bf16[256,1024]{1,0:T(8,128)(2,1)S(1)}, bf16[256,1024]{1,0:T(8,128)(2,1)}, u32[]{:S(2)}) %copy-start.2) | copy-done | bytes 524312
  2.1 0.4 shard_map.55
  2.4 2.1 %collective-permute-start.4 = (bf16[4,128,128]{2,1,0:T(8,128)(2,1)S(1)}, bf16[4,128,128]{2,1,0:T(8,128)(2,1)S(1)}, u32[]{:S(2)}, u32[]{:S(2)}) collective-permute-start(bf16[4,128,128]{2,1,0:T(8,128)(2,1)S(1)} %get-tuple-element.23), channel_id=1, source_target_pairs={{0,4},{4,0},{8,12},{12,8},{16,20},{20,16},{24,28},{28,24},{1,5},{5... | collective-permute-start | bytes 393224 | tf_op jit(solution)/shard_map/ppermute | solution.py:257
  4.6 0.1 collective-permute-start
  4.7 0.0 copy-start.1
  4.7 1.0 %copy-done.1 = bf16[256,1024]{1,0:T(8,128)(2,1)S(1)} copy-done((bf16[256,1024]{1,0:T(8,128)(2,1)S(1)}, bf16[256,1024]{1,0:T(8,128)(2,1)}, u32[]{:S(2)}) %copy-start.1) | copy-done | bytes 524312
  5.7 0.0 copy-start.3
  5.7 1.0 %copy-done.3 = bf16[256,1024]{1,0:T(8,128)(2,1)S(1)} copy-done((bf16[256,1024]{1,0:T(8,128)(2,1)S(1)}, bf16[256,1024]{1,0:T(8,128)(2,1)}, u32[]{:S(2)}) %copy-start.3) | copy-done | bytes 524312
  6.7 0.0 copy-start.4
  6.7 1.0 %copy-done.4 = bf16[256,1024]{1,0:T(8,128)(2,1)S(1)} copy-done((bf16[256,1024]{1,0:T(8,128)(2,1)S(1)}, bf16[256,1024]{1,0:T(8,128)(2,1)}, u32[]{:S(2)}) %copy-start.4) | copy-done | bytes 524312
  7.8 0.9 %shard_map.56.within_ref = f32[256,1024]{1,0:T(8,128)S(1)} custom-call(bf16[256,1024]{1,0:T(8,128)(2,1)S(1)} %copy-done.4, bf16[256,1024]{1,0:T(8,128)(2,1)S(1)} %copy-done.1, bf16[256,1024]{1,0:T(8,128)(2,1)S(1)} %copy-done.3), custom_call_target="tpu_custom_call" | custom-call | flops 268435456 | bytes 2621440 | tf_op jit(solution)/shard_map/pallas_call | solution.py:265
  8.7 0.0 copy-start.5
  8.7 0.0 copy-start.6
  8.7 0.0 collective-permute-done.4.refs_1_.refs_4_
  8.8 3.5 %collective-permute-start.5 = (bf16[4,128,128]{2,1,0:T(8,128)(2,1)S(1)}, bf16[4,128,128]{2,1,0:T(8,128)(2,1)S(1)}, u32[]{:S(2)}, u32[]{:S(2)}) collective-permute-start(bf16[4,128,128]{2,1,0:T(8,128)(2,1)S(1)} %shard_map.60), channel_id=1, source_target_pairs={{0,8},{4,12},{1,9},{5,13},{2,10},{6,14},{3,11},{7,15}} | collective-permute-start | bytes 393224 | tf_op jit(solution)/shard_map/ppermute | solution.py:281
  12.3 0.0 collective-permute-done.refs_1_.refs_0_
  12.3 1.4 %collective-permute-start.1 = (bf16[4,128,128]{2,1,0:T(8,128)(2,1)S(1)}, bf16[4,128,128]{2,1,0:T(8,128)(2,1)S(1)}, u32[]{:S(2)}, u32[]{:S(2)}) collective-permute-start(bf16[4,128,128]{2,1,0:T(8,128)(2,1)S(1)} %shard_map.57), channel_id=1, source_target_pairs={{0,8},{4,12},{1,9},{5,13},{2,10},{6,14},{3,11},{7,15}} | collective-permute-start | bytes 393224 | tf_op jit(solution)/shard_map/ppermute | solution.py:281
  13.8 0.4 collective-permute-done.5.refs_2_.refs_5_
  14.3 0.7 collective-permute-start.6
  14.9 1.8 %collective-permute-done.1.refs_2_.refs_1_ = bf16[4,128,128]{2,1,0:T(8,128)(2,1)S(1)} collective-permute-done((bf16[4,128,128]{2,1,0:T(8,128)(2,1)S(1)}, bf16[4,128,128]{2,1,0:T(8,128)(2,1)S(1)}, u32[]{:S(2)}, u32[]{:S(2)}) %collective-permute-start.1) | collective-permute-done | bytes 131104 | tf_op jit(solution)/shard_map/ppermute | solution.py:281
  16.8 0.7 collective-permute-start.2
  17.4 1.4 %collective-permute-start.9 = (bf16[1024,512]{1,0:T(8,128)(2,1)}, bf16[1024,512]{1,0:T(8,128)(2,1)}, u32[]{:S(2)}, u32[]{:S(2)}) collective-permute-start(bf16[1024,512]{1,0:T(8,128)(2,1)} %own_ref.1), channel_id=1, source_target_pairs={{0,4},{4,0},{8,12},{12,8},{16,20},{20,16},{24,28},{28,24},{1,5},{5... | collective-permute-start | bytes 3145736 | tf_op jit(solution)/shard_map/ppermute | solution.py:257
  18.8 0.0 collective-permute-done.6.refs_3_.refs_6_
  18.8 0.1 shard_map.62
  18.9 0.7 collective-permute-start.7
  19.6 0.0 collective-permute-done.2.refs_3_.refs_2_
  19.6 0.1 shard_map.59
  19.6 0.7 collective-permute-start.3
  20.3 0.0 collective-permute-done.7.refs_7_
  20.3 0.0 collective-permute-done.3.refs_3_
  20.3 0.0 copy-done.5
  20.4 0.0 copy-done.6
  20.4 0.8 shard_map.63
  21.1 3.1 %collective-permute-start.8 = (bf16[256,1024]{1,0:T(8,128)(2,1)S(1)}, bf16[256,1024]{1,0:T(8,128)(2,1)S(1)}, u32[]{:S(2)}, u32[]{:S(2)}) collective-permute-start(bf16[256,1024]{1,0:T(8,128)(2,1)S(1)} %shard_map.63), channel_id=1, source_target_pairs={{0,8},{4,12},{8,0},{12,4},{16,24},{20,28},{24,16},{28,20},{1,9},{5... | collective-permute-start | bytes 1572872 | tf_op jit(solution)/shard_map/ppermute | solution.py:257
  24.3 6.8 %collective-permute-start.10 = (bf16[256,1024]{1,0:T(8,128)(2,1)S(1)}, bf16[256,1024]{1,0:T(8,128)(2,1)S(1)}, u32[]{:S(2)}, u32[]{:S(2)}) collective-permute-start(bf16[256,1024]{1,0:T(8,128)(2,1)S(1)} %shard_map.63), channel_id=1, source_target_pairs={{0,16},{1,17},{2,26},{3,27},{4,20},{5,21},{6,30},{7,31},{8,24},{9,... | collective-permute-start | bytes 1572872 | tf_op jit(solution)/shard_map/ppermute | solution.py:261
  31.1 11.8 %collective-permute-done.8 = bf16[256,1024]{1,0:T(8,128)(2,1)S(1)} collective-permute-done((bf16[256,1024]{1,0:T(8,128)(2,1)S(1)}, bf16[256,1024]{1,0:T(8,128)(2,1)S(1)}, u32[]{:S(2)}, u32[]{:S(2)}) %collective-permute-start.8) | collective-permute-done | bytes 524320 | tf_op jit(solution)/shard_map/ppermute | solution.py:257
  42.9 0.1 broadcast_select_fusion.1
  43.0 0.0 collective-permute-done.9.mate_ref
  43.0 1.7 %shard_map.64.weight_ref = bf16[2,1024,512]{2,1,0:T(8,128)(2,1)S(1)} custom-call(bf16[1024,512]{1,0:T(8,128)(2,1)} %own_ref.1, bf16[1024,512]{1,0:T(8,128)(2,1)} %collective-permute-done.9.mate_ref), custom_call_target="tpu_custom_call" | custom-call | bytes 4194304 | tf_op jit(solution)/shard_map/pallas_call | solution.py:285
  44.7 0.7 shard_map.66.light_ref
  45.4 0.0 collective-permute-done.10.heavy_ref
  45.4 0.7 shard_map.68
  46.2 9.9 %collective-permute-start.13 = (bf16[2,256,512]{2,1,0:T(8,128)(2,1)S(1)}, bf16[2,256,512]{2,1,0:T(8,128)(2,1)S(1)}, u32[]{:S(2)}, u32[]{:S(2)}) collective-permute-start(bf16[2,256,512]{2,1,0:T(8,128)(2,1)S(1)} %get-tuple-element.32), channel_id=1, source_target_pairs={{0,1},{1,0},{2,3},{3,2},{4,5},{5,4},{6,7},{7,6},{8,9},{9,8},{10,11... | collective-permute-start | bytes 1572872 | tf_op jit(solution)/shard_map/ppermute | solution.py:261
  56.0 0.1 collective-permute-start.11
  56.1 0.7 shard_map.65.light_ref
  56.8 0.8 collective-permute-done.13
  57.6 0.1 add_convert_fusion.1
  57.7 1.1 %collective-permute-start.14 = (bf16[2,256,512]{2,1,0:T(8,128)(2,1)S(1)}, bf16[2,256,512]{2,1,0:T(8,128)(2,1)S(1)}, u32[]{:S(2)}, u32[]{:S(2)}) collective-permute-start(bf16[2,256,512]{2,1,0:T(8,128)(2,1)S(1)} %add_convert_fusion.1), channel_id=1, source_target_pairs={{0,2},{1,3},{2,0},{3,1},{4,6},{5,7},{6,4},{7,5},{8,10},{9,11},{10,... | collective-permute-start | bytes 1572872 | tf_op jit(solution)/shard_map/ppermute | solution.py:261
  58.7 10.8 %collective-permute-done.11.heavy_ref = bf16[256,1024]{1,0:T(8,128)(2,1)S(1)} collective-permute-done((bf16[256,1024]{1,0:T(8,128)(2,1)S(1)}, bf16[256,1024]{1,0:T(8,128)(2,1)S(1)}, u32[]{:S(2)}, u32[]{:S(2)}) %collective-permute-start.11) | collective-permute-done | bytes 524320 | tf_op jit(solution)/shard_map/ppermute | solution.py:257
  69.5 0.7 shard_map.67
  70.3 0.9 %collective-permute-start.12 = (bf16[2,256,512]{2,1,0:T(8,128)(2,1)S(1)}, bf16[2,256,512]{2,1,0:T(8,128)(2,1)S(1)}, u32[]{:S(2)}, u32[]{:S(2)}) collective-permute-start(bf16[2,256,512]{2,1,0:T(8,128)(2,1)S(1)} %get-tuple-element.29), channel_id=1, source_target_pairs={{0,1},{1,0},{2,3},{3,2},{4,5},{5,4},{6,7},{7,6},{8,9},{9,8},{10,11... | collective-permute-start | bytes 1572872 | tf_op jit(solution)/shard_map/ppermute | solution.py:261
  71.2 0.0 collective-permute-done.14
  71.2 1.5 %collective-permute-done.12 = bf16[2,256,512]{2,1,0:T(8,128)(2,1)S(1)} collective-permute-done((bf16[2,256,512]{2,1,0:T(8,128)(2,1)S(1)}, bf16[2,256,512]{2,1,0:T(8,128)(2,1)S(1)}, u32[]{:S(2)}, u32[]{:S(2)}) %collective-permute-start.12) | collective-permute-done | bytes 524320 | tf_op jit(solution)/shard_map/ppermute | solution.py:261
  72.7 0.2 add_convert_fusion
  72.9 4.6 %collective-permute-start.15 = (bf16[2,256,512]{2,1,0:T(8,128)(2,1)S(1)}, bf16[2,256,512]{2,1,0:T(8,128)(2,1)S(1)}, u32[]{:S(2)}, u32[]{:S(2)}) collective-permute-start(bf16[2,256,512]{2,1,0:T(8,128)(2,1)S(1)} %add_convert_fusion), channel_id=1, source_target_pairs={{0,0},{1,24},{2,8},{3,16},{4,4},{5,28},{6,12},{7,20},{8,9},{9,17},... | collective-permute-start | bytes 1572872 | tf_op jit(solution)/shard_map/ppermute | solution.py:261
  77.5 12.4 %collective-permute-done.15 = bf16[2,256,512]{2,1,0:T(8,128)(2,1)S(1)} collective-permute-done((bf16[2,256,512]{2,1,0:T(8,128)(2,1)S(1)}, bf16[2,256,512]{2,1,0:T(8,128)(2,1)S(1)}, u32[]{:S(2)}, u32[]{:S(2)}) %collective-permute-start.15) | collective-permute-done | bytes 524320 | tf_op jit(solution)/shard_map/ppermute | solution.py:261
  90.0 0.9 pad_maximum_fusion
  (5 shorter events, 0.2 us)
Async XLA Ops:
  0.0 1.0 %copy-start = (bf16[256,1024]{1,0:T(8,128)(2,1)S(1)}, bf16[256,1024]{1,0:T(8,128)(2,1)}, u32[]{:S(2)}) copy-start(bf16[256,1024]{1,0:T(8,128)(2,1)} %k_ref.3) | copy-start | bytes 1572868
  1.0 1.0 %copy-start.2 = (bf16[256,1024]{1,0:T(8,128)(2,1)S(1)}, bf16[256,1024]{1,0:T(8,128)(2,1)}, u32[]{:S(2)}) copy-start(bf16[256,1024]{1,0:T(8,128)(2,1)} %v_ref.3) | copy-start | bytes 1572868
  2.4 6.3 %collective-permute-start.4 = (bf16[4,128,128]{2,1,0:T(8,128)(2,1)S(1)}, bf16[4,128,128]{2,1,0:T(8,128)(2,1)S(1)}, u32[]{:S(2)}, u32[]{:S(2)}) collective-permute-start(bf16[4,128,128]{2,1,0:T(8,128)(2,1)S(1)} %get-tuple-element.23), channel_id=1, source_target_pairs={{0,4},{4,0},{8,12},{12,8},{16,20},{20,16},{24,28},{28,24},{1,5},{5... | collective-permute-start | bytes 393224 | tf_op jit(solution)/shard_map/ppermute | solution.py:257
  4.6 7.7 %collective-permute-start = (bf16[4,128,128]{2,1,0:T(8,128)(2,1)S(1)}, bf16[4,128,128]{2,1,0:T(8,128)(2,1)S(1)}, u32[]{:S(2)}, u32[]{:S(2)}) collective-permute-start(bf16[4,128,128]{2,1,0:T(8,128)(2,1)S(1)} %get-tuple-element.19), channel_id=1, source_target_pairs={{0,4},{4,0},{8,12},{12,8},{16,20},{20,16},{24,28},{28,24},{1,5},{5... | collective-permute-start | bytes 393224 | tf_op jit(solution)/shard_map/ppermute | solution.py:257
  4.7 1.0 %copy-start.1 = (bf16[256,1024]{1,0:T(8,128)(2,1)S(1)}, bf16[256,1024]{1,0:T(8,128)(2,1)}, u32[]{:S(2)}) copy-start(bf16[256,1024]{1,0:T(8,128)(2,1)} %k_ref.3) | copy-start | bytes 1572868
  5.7 1.0 %copy-start.3 = (bf16[256,1024]{1,0:T(8,128)(2,1)S(1)}, bf16[256,1024]{1,0:T(8,128)(2,1)}, u32[]{:S(2)}) copy-start(bf16[256,1024]{1,0:T(8,128)(2,1)} %v_ref.3) | copy-start | bytes 1572868
  6.7 1.0 %copy-start.4 = (bf16[256,1024]{1,0:T(8,128)(2,1)S(1)}, bf16[256,1024]{1,0:T(8,128)(2,1)}, u32[]{:S(2)}) copy-start(bf16[256,1024]{1,0:T(8,128)(2,1)} %q_ref.3) | copy-start | bytes 1572868
  8.7 11.6 %copy-start.5 = (bf16[256,1024]{1,0:T(8,128)(2,1)S(1)}, bf16[256,1024]{1,0:T(8,128)(2,1)}, u32[]{:S(2)}) copy-start(bf16[256,1024]{1,0:T(8,128)(2,1)} %q_ref.3) | copy-start | bytes 1572868
  8.7 11.6 %copy-start.6 = (f32[1024]{0:T(1024)S(1)}, f32[1024]{0:T(1024)}, u32[]{:S(2)}) copy-start(f32[1024]{0:T(1024)} %param.8) | copy-start | bytes 12292
  8.8 5.4 %collective-permute-start.5 = (bf16[4,128,128]{2,1,0:T(8,128)(2,1)S(1)}, bf16[4,128,128]{2,1,0:T(8,128)(2,1)S(1)}, u32[]{:S(2)}, u32[]{:S(2)}) collective-permute-start(bf16[4,128,128]{2,1,0:T(8,128)(2,1)S(1)} %shard_map.60), channel_id=1, source_target_pairs={{0,8},{4,12},{1,9},{5,13},{2,10},{6,14},{3,11},{7,15}} | collective-permute-start | bytes 393224 | tf_op jit(solution)/shard_map/ppermute | solution.py:281
  12.3 4.4 %collective-permute-start.1 = (bf16[4,128,128]{2,1,0:T(8,128)(2,1)S(1)}, bf16[4,128,128]{2,1,0:T(8,128)(2,1)S(1)}, u32[]{:S(2)}, u32[]{:S(2)}) collective-permute-start(bf16[4,128,128]{2,1,0:T(8,128)(2,1)S(1)} %shard_map.57), channel_id=1, source_target_pairs={{0,8},{4,12},{1,9},{5,13},{2,10},{6,14},{3,11},{7,15}} | collective-permute-start | bytes 393224 | tf_op jit(solution)/shard_map/ppermute | solution.py:281
  14.3 4.6 %collective-permute-start.6 = (bf16[4,128,128]{2,1,0:T(8,128)(2,1)S(1)}, bf16[4,128,128]{2,1,0:T(8,128)(2,1)S(1)}, u32[]{:S(2)}, u32[]{:S(2)}) collective-permute-start(bf16[4,128,128]{2,1,0:T(8,128)(2,1)S(1)} %shard_map.61), channel_id=1, source_target_pairs={{8,16},{12,20},{9,17},{13,21},{10,18},{14,22},{11,19},{15,23}} | collective-permute-start | bytes 393224 | tf_op jit(solution)/shard_map/ppermute | solution.py:281
  16.8 2.8 %collective-permute-start.2 = (bf16[4,128,128]{2,1,0:T(8,128)(2,1)S(1)}, bf16[4,128,128]{2,1,0:T(8,128)(2,1)S(1)}, u32[]{:S(2)}, u32[]{:S(2)}) collective-permute-start(bf16[4,128,128]{2,1,0:T(8,128)(2,1)S(1)} %shard_map.58), channel_id=1, source_target_pairs={{8,16},{12,20},{9,17},{13,21},{10,18},{14,22},{11,19},{15,23}} | collective-permute-start | bytes 393224 | tf_op jit(solution)/shard_map/ppermute | solution.py:281
  17.4 25.6 %collective-permute-start.9 = (bf16[1024,512]{1,0:T(8,128)(2,1)}, bf16[1024,512]{1,0:T(8,128)(2,1)}, u32[]{:S(2)}, u32[]{:S(2)}) collective-permute-start(bf16[1024,512]{1,0:T(8,128)(2,1)} %own_ref.1), channel_id=1, source_target_pairs={{0,4},{4,0},{8,12},{12,8},{16,20},{20,16},{24,28},{28,24},{1,5},{5... | collective-permute-start | bytes 3145736 | tf_op jit(solution)/shard_map/ppermute | solution.py:257
  18.9 1.4 %collective-permute-start.7 = (bf16[4,128,128]{2,1,0:T(8,128)(2,1)S(1)}, bf16[4,128,128]{2,1,0:T(8,128)(2,1)S(1)}, u32[]{:S(2)}, u32[]{:S(2)}) collective-permute-start(bf16[4,128,128]{2,1,0:T(8,128)(2,1)S(1)} %shard_map.62), channel_id=1, source_target_pairs={{16,24},{20,28},{17,25},{21,29},{18,26},{22,30},{19,27},{23,31}} | collective-permute-start | bytes 393224 | tf_op jit(solution)/shard_map/ppermute | solution.py:281
  19.6 0.7 collective-permute-start.3
  21.1 21.8 %collective-permute-start.8 = (bf16[256,1024]{1,0:T(8,128)(2,1)S(1)}, bf16[256,1024]{1,0:T(8,128)(2,1)S(1)}, u32[]{:S(2)}, u32[]{:S(2)}) collective-permute-start(bf16[256,1024]{1,0:T(8,128)(2,1)S(1)} %shard_map.63), channel_id=1, source_target_pairs={{0,8},{4,12},{8,0},{12,4},{16,24},{20,28},{24,16},{28,20},{1,9},{5... | collective-permute-start | bytes 1572872 | tf_op jit(solution)/shard_map/ppermute | solution.py:257
  24.3 21.1 %collective-permute-start.10 = (bf16[256,1024]{1,0:T(8,128)(2,1)S(1)}, bf16[256,1024]{1,0:T(8,128)(2,1)S(1)}, u32[]{:S(2)}, u32[]{:S(2)}) collective-permute-start(bf16[256,1024]{1,0:T(8,128)(2,1)S(1)} %shard_map.63), channel_id=1, source_target_pairs={{0,16},{1,17},{2,26},{3,27},{4,20},{5,21},{6,30},{7,31},{8,24},{9,... | collective-permute-start | bytes 1572872 | tf_op jit(solution)/shard_map/ppermute | solution.py:261
  46.2 11.4 %collective-permute-start.13 = (bf16[2,256,512]{2,1,0:T(8,128)(2,1)S(1)}, bf16[2,256,512]{2,1,0:T(8,128)(2,1)S(1)}, u32[]{:S(2)}, u32[]{:S(2)}) collective-permute-start(bf16[2,256,512]{2,1,0:T(8,128)(2,1)S(1)} %get-tuple-element.32), channel_id=1, source_target_pairs={{0,1},{1,0},{2,3},{3,2},{4,5},{5,4},{6,7},{7,6},{8,9},{9,8},{10,11... | collective-permute-start | bytes 1572872 | tf_op jit(solution)/shard_map/ppermute | solution.py:261
  56.0 13.5 %collective-permute-start.11 = (bf16[256,1024]{1,0:T(8,128)(2,1)S(1)}, bf16[256,1024]{1,0:T(8,128)(2,1)S(1)}, u32[]{:S(2)}, u32[]{:S(2)}) collective-permute-start(bf16[256,1024]{1,0:T(8,128)(2,1)S(1)} %collective-permute-done.10.heavy_ref), channel_id=1, source_target_pairs={{0,8},{4,12},{8,0},{12,4},{16,24},{20,28},{24,16},{28,20},{1,9},{5... | collective-permute-start | bytes 1572872 | tf_op jit(solution)/shard_map/ppermute | solution.py:257
  57.7 13.5 %collective-permute-start.14 = (bf16[2,256,512]{2,1,0:T(8,128)(2,1)S(1)}, bf16[2,256,512]{2,1,0:T(8,128)(2,1)S(1)}, u32[]{:S(2)}, u32[]{:S(2)}) collective-permute-start(bf16[2,256,512]{2,1,0:T(8,128)(2,1)S(1)} %add_convert_fusion.1), channel_id=1, source_target_pairs={{0,2},{1,3},{2,0},{3,1},{4,6},{5,7},{6,4},{7,5},{8,10},{9,11},{10,... | collective-permute-start | bytes 1572872 | tf_op jit(solution)/shard_map/ppermute | solution.py:261
  70.3 2.5 %collective-permute-start.12 = (bf16[2,256,512]{2,1,0:T(8,128)(2,1)S(1)}, bf16[2,256,512]{2,1,0:T(8,128)(2,1)S(1)}, u32[]{:S(2)}, u32[]{:S(2)}) collective-permute-start(bf16[2,256,512]{2,1,0:T(8,128)(2,1)S(1)} %get-tuple-element.29), channel_id=1, source_target_pairs={{0,1},{1,0},{2,3},{3,2},{4,5},{5,4},{6,7},{7,6},{8,9},{9,8},{10,11... | collective-permute-start | bytes 1572872 | tf_op jit(solution)/shard_map/ppermute | solution.py:261
  72.9 17.0 %collective-permute-start.15 = (bf16[2,256,512]{2,1,0:T(8,128)(2,1)S(1)}, bf16[2,256,512]{2,1,0:T(8,128)(2,1)S(1)}, u32[]{:S(2)}, u32[]{:S(2)}) collective-permute-start(bf16[2,256,512]{2,1,0:T(8,128)(2,1)S(1)} %add_convert_fusion), channel_id=1, source_target_pairs={{0,0},{1,24},{2,8},{3,16},{4,4},{5,28},{6,12},{7,20},{8,9},{9,17},... | collective-permute-start | bytes 1572872 | tf_op jit(solution)/shard_map/ppermute | solution.py:261

commit v25 on v24

--- a/solution.py
+++ b/solution.py
@@ -53,17 +53,14 @@
     return slice(head * HD, (head + 1) * HD)
 
 
-def state_kernel(k_ref, v_ref, *out_refs):
-    half = len(out_refs) // 2
-    count = out_refs[0].shape[0]
-    for part in range(half):
-        for index in range(count):
-            cols = head_slice(part * count + index)
-            state = lax.dot_general(
-                k_ref[:, cols], v_ref[:, cols], (((0,), (0,)), ((), ())), preferred_element_type=F32
-            )
-            out_refs[part][index] = state
-            out_refs[half + part][index] = state.astype(BF16)
+def state_kernel(k_ref, v_ref, wide_ref, narrow_ref):
+    for head in range(wide_ref.shape[0]):
+        cols = head_slice(head)
+        state = lax.dot_general(
+            k_ref[:, cols], v_ref[:, cols], (((0,), (0,)), ((), ())), preferred_element_type=F32
+        )
+        wide_ref[head] = state
+        narrow_ref[head] = state.astype(BF16)
 
 
 def sum_kernel(*refs):
@@ -115,11 +112,15 @@
 
 
 def block_states(keys, values, parts):
-    rows, features = keys.shape
-    shape = (features // HD // parts, HD, HD)
-    outs = [jax.ShapeDtypeStruct(shape, kind) for kind in (F32, BF16) for _ in range(parts)]
-    states = call(state_kernel, outs, 2 * keys.size * HD, 4 * keys.size)(keys, values)
-    return states[:parts], states[parts:]
+    width = keys.shape[1] // parts
+    outs = [jax.ShapeDtypeStruct((width // HD, HD, HD), kind) for kind in (F32, BF16)]
+    states = []
+    for part in range(parts):
+        cols = slice(part * width, (part + 1) * width)
+        operands = keys[:, cols], values[:, cols]
+        size = operands[0].size
+        states.append(call(state_kernel, outs, 2 * size * HD, 4 * size)(*operands))
+    return tuple(zip(*states))
 
 
 def attend(second, queries, within, norm_gain, states):

time: 91.3 us -> 90.3 us (0.989)
  local copies, waits for them, and re-layouts: 5.22 us -> 1.41 us
  waiting for transfers between devices: 39.6 us -> 41.4 us
  starting transfers between devices: 37.6 us -> 38.6 us
    unnamed x14 -> x8, local copies, waits for them, and re-layouts: 5.22 us -> 0.02 us
    ppermute x5, waiting for transfers between devices: 22.6 us -> 24.5 us  [swap(): return lax.ppermute(value, 'seq', [(s, s ^ mask) for s in range(8)])]
    slice x0 -> x1, local copies, waits for them, and re-layouts: none -> 1.39 us  [block_states(): operands = (keys[:, cols], values[:, cols])]
    ppermute x6, starting transfers between devices: 7.58 us -> 8.54 us  [pairs_body(): states[part].append(lax.ppermute(onward[part], 'seq', pairs))]
  transfers between devices with their start and end apart: 16 -> 16, of which waited for: 7 -> 7; matrix products, arithmetic and copies ran while one was open for 0% -> 0% of each run, Pallas kernels for 6% -> 7%
where the time goes in v25:
time: 90.3 us; the launch traced here: 90.1 us
  waiting for transfers between devices  41.4 us (46%)
  starting transfers between devices  38.6 us (43%)
  Pallas kernels  7.04 us (8%)
  local copies, waits for them, and re-layouts  1.41 us (2%)
  other arithmetic  1.32 us (1%)
    ppermute x5, waiting for transfers between devices, swap(): return lax.ppermute(value, 'seq', [(s, s ^ mask) for s in range(8)])  24.5 us
    ppermute x5, starting transfers between devices, move(): return lax.ppermute(value, both, pairs)  23.2 us
    ppermute x5, waiting for transfers between devices, move(): return lax.ppermute(value, both, pairs)  14.7 us
    ppermute x6, starting transfers between devices, pairs_body(): states[part].append(lax.ppermute(onward[part], 'seq', pairs))  8.54 us
    ppermute x5, starting transfers between devices, swap(): return lax.ppermute(value, 'seq', [(s, s ^ mask) for s in range(8)])  6.8 us
    ppermute x6, waiting for transfers between devices, pairs_body(): states[part].append(lax.ppermute(onward[part], 'seq', pairs))  2.22 us
  transfers between devices with their start and end apart: 16, of which 7 were waited for; matrix products, arithmetic and copies ran while one was open for 0% of the time, Pallas kernels for 7%

profile of v25, /device:TPU:1, one launch (start us, length us, event | category | flops | bytes accessed | tf_op | source)
XLA Modules:
  0.0 90.1 jit_solution(18021620935182400089)
XLA Ops:
  0.0 0.0 copy-start.1
  0.0 0.0 copy-start
  0.0 0.0 copy-start.2
  0.0 1.4 %fusion = (bf16[256,512]{1,0:T(8,128)(2,1)S(1)}, bf16[256,512]{1,0:T(8,128)(2,1)S(1)}, bf16[256,512]{1,0:T(8,128)(2,1)S(1)}, bf16[256,512]{1,0:T(8,128)(2,1)S(1)}) fusion(bf16[256,1024]{1,0:T(8,128)(2,1)} %v_ref.1, bf16[256,1024]{1,0:T(8,128)(2,1)} %k_ref.1), kind=kLoop, calls=%fused_computation.7 | loop fusion | bytes 2097152 | tf_op jit(solution)/shard_map/slice | solution.py:120
  1.4 0.3 shard_map.60
  1.7 2.1 %collective-permute-start.4 = (bf16[4,128,128]{2,1,0:T(8,128)(2,1)S(1)}, bf16[4,128,128]{2,1,0:T(8,128)(2,1)S(1)}, u32[]{:S(2)}, u32[]{:S(2)}) collective-permute-start(bf16[4,128,128]{2,1,0:T(8,128)(2,1)S(1)} %get-tuple-element.23), channel_id=1, source_target_pairs={{0,4},{4,0},{8,12},{12,8},{16,20},{20,16},{24,28},{28,24},{1,5},{5... | collective-permute-start | bytes 393224 | tf_op jit(solution)/shard_map/ppermute | solution.py:258
  3.8 0.3 shard_map.55
  4.1 0.1 collective-permute-start
  4.2 0.0 copy-done.1
  4.2 0.0 copy-done
  4.2 0.0 copy-done.2
  4.2 0.9 %shard_map.56.within_ref = f32[256,1024]{1,0:T(8,128)S(1)} custom-call(bf16[256,1024]{1,0:T(8,128)(2,1)S(1)} %copy-done.2, bf16[256,1024]{1,0:T(8,128)(2,1)S(1)} %copy-done, bf16[256,1024]{1,0:T(8,128)(2,1)S(1)} %copy-done.1), custom_call_target="tpu_custom_call" | custom-call | flops 268435456 | bytes 2621440 | tf_op jit(solution)/shard_map/pallas_call | solution.py:266
  5.1 0.0 copy-start.3
  5.1 1.9 %collective-permute-done.4.refs_1_.refs_4_ = bf16[4,128,128]{2,1,0:T(8,128)(2,1)S(1)} collective-permute-done((bf16[4,128,128]{2,1,0:T(8,128)(2,1)S(1)}, bf16[4,128,128]{2,1,0:T(8,128)(2,1)S(1)}, u32[]{:S(2)}, u32[]{:S(2)}) %collective-permute-start.4) | collective-permute-done | bytes 131104 | tf_op jit(solution)/shard_map/ppermute | solution.py:258
  7.1 3.1 %collective-permute-start.5 = (bf16[4,128,128]{2,1,0:T(8,128)(2,1)S(1)}, bf16[4,128,128]{2,1,0:T(8,128)(2,1)S(1)}, u32[]{:S(2)}, u32[]{:S(2)}) collective-permute-start(bf16[4,128,128]{2,1,0:T(8,128)(2,1)S(1)} %shard_map.61), channel_id=1, source_target_pairs={{0,8},{4,12},{1,9},{5,13},{2,10},{6,14},{3,11},{7,15}} | collective-permute-start | bytes 393224 | tf_op jit(solution)/shard_map/ppermute | solution.py:282
  10.2 0.0 collective-permute-done.refs_1_.refs_0_
  10.2 2.8 %collective-permute-start.1 = (bf16[4,128,128]{2,1,0:T(8,128)(2,1)S(1)}, bf16[4,128,128]{2,1,0:T(8,128)(2,1)S(1)}, u32[]{:S(2)}, u32[]{:S(2)}) collective-permute-start(bf16[4,128,128]{2,1,0:T(8,128)(2,1)S(1)} %shard_map.57), channel_id=1, source_target_pairs={{0,8},{4,12},{1,9},{5,13},{2,10},{6,14},{3,11},{7,15}} | collective-permute-start | bytes 393224 | tf_op jit(solution)/shard_map/ppermute | solution.py:282
  13.0 0.0 collective-permute-done.5.refs_2_.refs_5_
  13.1 0.7 collective-permute-start.6
  13.7 2.2 %collective-permute-done.1.refs_2_.refs_1_ = bf16[4,128,128]{2,1,0:T(8,128)(2,1)S(1)} collective-permute-done((bf16[4,128,128]{2,1,0:T(8,128)(2,1)S(1)}, bf16[4,128,128]{2,1,0:T(8,128)(2,1)S(1)}, u32[]{:S(2)}, u32[]{:S(2)}) %collective-permute-start.1) | collective-permute-done | bytes 131104 | tf_op jit(solution)/shard_map/ppermute | solution.py:282
  16.0 0.7 collective-permute-start.2
  16.7 1.3 %collective-permute-start.9 = (bf16[1024,512]{1,0:T(8,128)(2,1)}, bf16[1024,512]{1,0:T(8,128)(2,1)}, u32[]{:S(2)}, u32[]{:S(2)}) collective-permute-start(bf16[1024,512]{1,0:T(8,128)(2,1)} %own_ref.1), channel_id=1, source_target_pairs={{0,4},{4,0},{8,12},{12,8},{16,20},{20,16},{24,28},{28,24},{1,5},{5... | collective-permute-start | bytes 3145736 | tf_op jit(solution)/shard_map/ppermute | solution.py:258
  18.0 0.0 collective-permute-done.6.refs_3_.refs_6_
  18.0 0.1 shard_map.63
  18.0 0.7 collective-permute-start.7
  18.7 0.0 collective-permute-done.2.refs_3_.refs_2_
  18.7 0.1 shard_map.59
  18.8 0.7 collective-permute-start.3
  19.5 0.0 collective-permute-done.7.refs_7_
  19.5 0.0 collective-permute-done.3.refs_3_
  19.5 0.0 copy-done.3
  19.5 0.8 shard_map.64
  20.3 3.2 %collective-permute-start.8 = (bf16[256,1024]{1,0:T(8,128)(2,1)S(1)}, bf16[256,1024]{1,0:T(8,128)(2,1)S(1)}, u32[]{:S(2)}, u32[]{:S(2)}) collective-permute-start(bf16[256,1024]{1,0:T(8,128)(2,1)S(1)} %shard_map.64), channel_id=1, source_target_pairs={{0,8},{4,12},{8,0},{12,4},{16,24},{20,28},{24,16},{28,20},{1,9},{5... | collective-permute-start | bytes 1572872 | tf_op jit(solution)/shard_map/ppermute | solution.py:258
  23.5 6.8 %collective-permute-start.10 = (bf16[256,1024]{1,0:T(8,128)(2,1)S(1)}, bf16[256,1024]{1,0:T(8,128)(2,1)S(1)}, u32[]{:S(2)}, u32[]{:S(2)}) collective-permute-start(bf16[256,1024]{1,0:T(8,128)(2,1)S(1)} %shard_map.64), channel_id=1, source_target_pairs={{0,16},{1,17},{2,26},{3,27},{4,20},{5,21},{6,30},{7,31},{8,24},{9,... | collective-permute-start | bytes 1572872 | tf_op jit(solution)/shard_map/ppermute | solution.py:262
  30.3 11.8 %collective-permute-done.8 = bf16[256,1024]{1,0:T(8,128)(2,1)S(1)} collective-permute-done((bf16[256,1024]{1,0:T(8,128)(2,1)S(1)}, bf16[256,1024]{1,0:T(8,128)(2,1)S(1)}, u32[]{:S(2)}, u32[]{:S(2)}) %collective-permute-start.8) | collective-permute-done | bytes 524320 | tf_op jit(solution)/shard_map/ppermute | solution.py:258
  42.1 0.1 broadcast_select_fusion.1
  42.2 0.0 collective-permute-done.9.mate_ref
  42.2 1.7 %shard_map.65.weight_ref = bf16[2,1024,512]{2,1,0:T(8,128)(2,1)S(1)} custom-call(bf16[1024,512]{1,0:T(8,128)(2,1)} %own_ref.1, bf16[1024,512]{1,0:T(8,128)(2,1)} %collective-permute-done.9.mate_ref), custom_call_target="tpu_custom_call" | custom-call | bytes 4194304 | tf_op jit(solution)/shard_map/pallas_call | solution.py:286
  43.9 0.7 shard_map.67.light_ref
  44.6 0.0 collective-permute-done.10.heavy_ref
  44.6 0.7 shard_map.69
  45.4 9.9 %collective-permute-start.13 = (bf16[2,256,512]{2,1,0:T(8,128)(2,1)S(1)}, bf16[2,256,512]{2,1,0:T(8,128)(2,1)S(1)}, u32[]{:S(2)}, u32[]{:S(2)}) collective-permute-start(bf16[2,256,512]{2,1,0:T(8,128)(2,1)S(1)} %get-tuple-element.32), channel_id=1, source_target_pairs={{0,1},{1,0},{2,3},{3,2},{4,5},{5,4},{6,7},{7,6},{8,9},{9,8},{10,11... | collective-permute-start | bytes 1572872 | tf_op jit(solution)/shard_map/ppermute | solution.py:262
  55.2 0.1 collective-permute-start.11
  55.3 0.7 shard_map.66.light_ref
  56.0 0.8 collective-permute-done.13
  56.8 0.1 add_convert_fusion.1
  56.9 1.1 %collective-permute-start.14 = (bf16[2,256,512]{2,1,0:T(8,128)(2,1)S(1)}, bf16[2,256,512]{2,1,0:T(8,128)(2,1)S(1)}, u32[]{:S(2)}, u32[]{:S(2)}) collective-permute-start(bf16[2,256,512]{2,1,0:T(8,128)(2,1)S(1)} %add_convert_fusion.1), channel_id=1, source_target_pairs={{0,2},{1,3},{2,0},{3,1},{4,6},{5,7},{6,4},{7,5},{8,10},{9,11},{10,... | collective-permute-start | bytes 1572872 | tf_op jit(solution)/shard_map/ppermute | solution.py:262
  58.0 10.8 %collective-permute-done.11.heavy_ref = bf16[256,1024]{1,0:T(8,128)(2,1)S(1)} collective-permute-done((bf16[256,1024]{1,0:T(8,128)(2,1)S(1)}, bf16[256,1024]{1,0:T(8,128)(2,1)S(1)}, u32[]{:S(2)}, u32[]{:S(2)}) %collective-permute-start.11) | collective-permute-done | bytes 524320 | tf_op jit(solution)/shard_map/ppermute | solution.py:258
  68.7 0.7 shard_map.68
  69.5 0.9 %collective-permute-start.12 = (bf16[2,256,512]{2,1,0:T(8,128)(2,1)S(1)}, bf16[2,256,512]{2,1,0:T(8,128)(2,1)S(1)}, u32[]{:S(2)}, u32[]{:S(2)}) collective-permute-start(bf16[2,256,512]{2,1,0:T(8,128)(2,1)S(1)} %get-tuple-element.29), channel_id=1, source_target_pairs={{0,1},{1,0},{2,3},{3,2},{4,5},{5,4},{6,7},{7,6},{8,9},{9,8},{10,11... | collective-permute-start | bytes 1572872 | tf_op jit(solution)/shard_map/ppermute | solution.py:262
  70.4 0.0 collective-permute-done.14
  70.4 1.5 %collective-permute-done.12 = bf16[2,256,512]{2,1,0:T(8,128)(2,1)S(1)} collective-permute-done((bf16[2,256,512]{2,1,0:T(8,128)(2,1)S(1)}, bf16[2,256,512]{2,1,0:T(8,128)(2,1)S(1)}, u32[]{:S(2)}, u32[]{:S(2)}) %collective-permute-start.12) | collective-permute-done | bytes 524320 | tf_op jit(solution)/shard_map/ppermute | solution.py:262
  71.9 0.2 add_convert_fusion
  72.1 4.6 %collective-permute-start.15 = (bf16[2,256,512]{2,1,0:T(8,128)(2,1)S(1)}, bf16[2,256,512]{2,1,0:T(8,128)(2,1)S(1)}, u32[]{:S(2)}, u32[]{:S(2)}) collective-permute-start(bf16[2,256,512]{2,1,0:T(8,128)(2,1)S(1)} %add_convert_fusion), channel_id=1, source_target_pairs={{0,0},{1,24},{2,8},{3,16},{4,4},{5,28},{6,12},{7,20},{8,9},{9,17},... | collective-permute-start | bytes 1572872 | tf_op jit(solution)/shard_map/ppermute | solution.py:262
  76.7 12.4 %collective-permute-done.15 = bf16[2,256,512]{2,1,0:T(8,128)(2,1)S(1)} collective-permute-done((bf16[2,256,512]{2,1,0:T(8,128)(2,1)S(1)}, bf16[2,256,512]{2,1,0:T(8,128)(2,1)S(1)}, u32[]{:S(2)}, u32[]{:S(2)}) %collective-permute-start.15) | collective-permute-done | bytes 524320 | tf_op jit(solution)/shard_map/ppermute | solution.py:262
  89.2 0.9 pad_maximum_fusion
  (5 shorter events, 0.2 us)
Async XLA Ops:
  0.0 4.2 %copy-start.1 = (bf16[256,1024]{1,0:T(8,128)(2,1)S(1)}, bf16[256,1024]{1,0:T(8,128)(2,1)}, u32[]{:S(2)}) copy-start(bf16[256,1024]{1,0:T(8,128)(2,1)} %v_ref.1) | copy-start | bytes 1572868
  0.0 4.2 %copy-start = (bf16[256,1024]{1,0:T(8,128)(2,1)S(1)}, bf16[256,1024]{1,0:T(8,128)(2,1)}, u32[]{:S(2)}) copy-start(bf16[256,1024]{1,0:T(8,128)(2,1)} %k_ref.1) | copy-start | bytes 1572868
  0.0 4.2 %copy-start.2 = (bf16[256,1024]{1,0:T(8,128)(2,1)S(1)}, bf16[256,1024]{1,0:T(8,128)(2,1)}, u32[]{:S(2)}) copy-start(bf16[256,1024]{1,0:T(8,128)(2,1)} %q_ref.3) | copy-start | bytes 1572868
  1.7 5.4 %collective-permute-start.4 = (bf16[4,128,128]{2,1,0:T(8,128)(2,1)S(1)}, bf16[4,128,128]{2,1,0:T(8,128)(2,1)S(1)}, u32[]{:S(2)}, u32[]{:S(2)}) collective-permute-start(bf16[4,128,128]{2,1,0:T(8,128)(2,1)S(1)} %get-tuple-element.23), channel_id=1, source_target_pairs={{0,4},{4,0},{8,12},{12,8},{16,20},{20,16},{24,28},{28,24},{1,5},{5... | collective-permute-start | bytes 393224 | tf_op jit(solution)/shard_map/ppermute | solution.py:258
  4.1 6.1 %collective-permute-start = (bf16[4,128,128]{2,1,0:T(8,128)(2,1)S(1)}, bf16[4,128,128]{2,1,0:T(8,128)(2,1)S(1)}, u32[]{:S(2)}, u32[]{:S(2)}) collective-permute-start(bf16[4,128,128]{2,1,0:T(8,128)(2,1)S(1)} %get-tuple-element.19), channel_id=1, source_target_pairs={{0,4},{4,0},{8,12},{12,8},{16,20},{20,16},{24,28},{28,24},{1,5},{5... | collective-permute-start | bytes 393224 | tf_op jit(solution)/shard_map/ppermute | solution.py:258
  5.1 14.4 %copy-start.3 = (f32[1024]{0:T(1024)S(1)}, f32[1024]{0:T(1024)}, u32[]{:S(2)}) copy-start(f32[1024]{0:T(1024)} %param.8) | copy-start | bytes 12292
  7.1 5.9 %collective-permute-start.5 = (bf16[4,128,128]{2,1,0:T(8,128)(2,1)S(1)}, bf16[4,128,128]{2,1,0:T(8,128)(2,1)S(1)}, u32[]{:S(2)}, u32[]{:S(2)}) collective-permute-start(bf16[4,128,128]{2,1,0:T(8,128)(2,1)S(1)} %shard_map.61), channel_id=1, source_target_pairs={{0,8},{4,12},{1,9},{5,13},{2,10},{6,14},{3,11},{7,15}} | collective-permute-start | bytes 393224 | tf_op jit(solution)/shard_map/ppermute | solution.py:282
  10.2 5.7 %collective-permute-start.1 = (bf16[4,128,128]{2,1,0:T(8,128)(2,1)S(1)}, bf16[4,128,128]{2,1,0:T(8,128)(2,1)S(1)}, u32[]{:S(2)}, u32[]{:S(2)}) collective-permute-start(bf16[4,128,128]{2,1,0:T(8,128)(2,1)S(1)} %shard_map.57), channel_id=1, source_target_pairs={{0,8},{4,12},{1,9},{5,13},{2,10},{6,14},{3,11},{7,15}} | collective-permute-start | bytes 393224 | tf_op jit(solution)/shard_map/ppermute | solution.py:282
  13.1 4.9 %collective-permute-start.6 = (bf16[4,128,128]{2,1,0:T(8,128)(2,1)S(1)}, bf16[4,128,128]{2,1,0:T(8,128)(2,1)S(1)}, u32[]{:S(2)}, u32[]{:S(2)}) collective-permute-start(bf16[4,128,128]{2,1,0:T(8,128)(2,1)S(1)} %shard_map.62), channel_id=1, source_target_pairs={{8,16},{12,20},{9,17},{13,21},{10,18},{14,22},{11,19},{15,23}} | collective-permute-start | bytes 393224 | tf_op jit(solution)/shard_map/ppermute | solution.py:282
  16.0 2.7 %collective-permute-start.2 = (bf16[4,128,128]{2,1,0:T(8,128)(2,1)S(1)}, bf16[4,128,128]{2,1,0:T(8,128)(2,1)S(1)}, u32[]{:S(2)}, u32[]{:S(2)}) collective-permute-start(bf16[4,128,128]{2,1,0:T(8,128)(2,1)S(1)} %shard_map.58), channel_id=1, source_target_pairs={{8,16},{12,20},{9,17},{13,21},{10,18},{14,22},{11,19},{15,23}} | collective-permute-start | bytes 393224 | tf_op jit(solution)/shard_map/ppermute | solution.py:282
  16.7 25.5 %collective-permute-start.9 = (bf16[1024,512]{1,0:T(8,128)(2,1)}, bf16[1024,512]{1,0:T(8,128)(2,1)}, u32[]{:S(2)}, u32[]{:S(2)}) collective-permute-start(bf16[1024,512]{1,0:T(8,128)(2,1)} %own_ref.1), channel_id=1, source_target_pairs={{0,4},{4,0},{8,12},{12,8},{16,20},{20,16},{24,28},{28,24},{1,5},{5... | collective-permute-start | bytes 3145736 | tf_op jit(solution)/shard_map/ppermute | solution.py:258
  18.0 1.4 %collective-permute-start.7 = (bf16[4,128,128]{2,1,0:T(8,128)(2,1)S(1)}, bf16[4,128,128]{2,1,0:T(8,128)(2,1)S(1)}, u32[]{:S(2)}, u32[]{:S(2)}) collective-permute-start(bf16[4,128,128]{2,1,0:T(8,128)(2,1)S(1)} %shard_map.63), channel_id=1, source_target_pairs={{16,24},{20,28},{17,25},{21,29},{18,26},{22,30},{19,27},{23,31}} | collective-permute-start | bytes 393224 | tf_op jit(solution)/shard_map/ppermute | solution.py:282
  18.8 0.7 collective-permute-start.3
  20.3 21.8 %collective-permute-start.8 = (bf16[256,1024]{1,0:T(8,128)(2,1)S(1)}, bf16[256,1024]{1,0:T(8,128)(2,1)S(1)}, u32[]{:S(2)}, u32[]{:S(2)}) collective-permute-start(bf16[256,1024]{1,0:T(8,128)(2,1)S(1)} %shard_map.64), channel_id=1, source_target_pairs={{0,8},{4,12},{8,0},{12,4},{16,24},{20,28},{24,16},{28,20},{1,9},{5... | collective-permute-start | bytes 1572872 | tf_op jit(solution)/shard_map/ppermute | solution.py:258
  23.5 21.1 %collective-permute-start.10 = (bf16[256,1024]{1,0:T(8,128)(2,1)S(1)}, bf16[256,1024]{1,0:T(8,128)(2,1)S(1)}, u32[]{:S(2)}, u32[]{:S(2)}) collective-permute-start(bf16[256,1024]{1,0:T(8,128)(2,1)S(1)} %shard_map.64), channel_id=1, source_target_pairs={{0,16},{1,17},{2,26},{3,27},{4,20},{5,21},{6,30},{7,31},{8,24},{9,... | collective-permute-start | bytes 1572872 | tf_op jit(solution)/shard_map/ppermute | solution.py:262
  45.4 11.4 %collective-permute-start.13 = (bf16[2,256,512]{2,1,0:T(8,128)(2,1)S(1)}, bf16[2,256,512]{2,1,0:T(8,128)(2,1)S(1)}, u32[]{:S(2)}, u32[]{:S(2)}) collective-permute-start(bf16[2,256,512]{2,1,0:T(8,128)(2,1)S(1)} %get-tuple-element.32), channel_id=1, source_target_pairs={{0,1},{1,0},{2,3},{3,2},{4,5},{5,4},{6,7},{7,6},{8,9},{9,8},{10,11... | collective-permute-start | bytes 1572872 | tf_op jit(solution)/shard_map/ppermute | solution.py:262
  55.2 13.5 %collective-permute-start.11 = (bf16[256,1024]{1,0:T(8,128)(2,1)S(1)}, bf16[256,1024]{1,0:T(8,128)(2,1)S(1)}, u32[]{:S(2)}, u32[]{:S(2)}) collective-permute-start(bf16[256,1024]{1,0:T(8,128)(2,1)S(1)} %collective-permute-done.10.heavy_ref), channel_id=1, source_target_pairs={{0,8},{4,12},{8,0},{12,4},{16,24},{20,28},{24,16},{28,20},{1,9},{5... | collective-permute-start | bytes 1572872 | tf_op jit(solution)/shard_map/ppermute | solution.py:258
  56.9 13.5 %collective-permute-start.14 = (bf16[2,256,512]{2,1,0:T(8,128)(2,1)S(1)}, bf16[2,256,512]{2,1,0:T(8,128)(2,1)S(1)}, u32[]{:S(2)}, u32[]{:S(2)}) collective-permute-start(bf16[2,256,512]{2,1,0:T(8,128)(2,1)S(1)} %add_convert_fusion.1), channel_id=1, source_target_pairs={{0,2},{1,3},{2,0},{3,1},{4,6},{5,7},{6,4},{7,5},{8,10},{9,11},{10,... | collective-permute-start | bytes 1572872 | tf_op jit(solution)/shard_map/ppermute | solution.py:262
  69.5 2.5 %collective-permute-start.12 = (bf16[2,256,512]{2,1,0:T(8,128)(2,1)S(1)}, bf16[2,256,512]{2,1,0:T(8,128)(2,1)S(1)}, u32[]{:S(2)}, u32[]{:S(2)}) collective-permute-start(bf16[2,256,512]{2,1,0:T(8,128)(2,1)S(1)} %get-tuple-element.29), channel_id=1, source_target_pairs={{0,1},{1,0},{2,3},{3,2},{4,5},{5,4},{6,7},{7,6},{8,9},{9,8},{10,11... | collective-permute-start | bytes 1572872 | tf_op jit(solution)/shard_map/ppermute | solution.py:262
  72.1 17.0 %collective-permute-start.15 = (bf16[2,256,512]{2,1,0:T(8,128)(2,1)S(1)}, bf16[2,256,512]{2,1,0:T(8,128)(2,1)S(1)}, u32[]{:S(2)}, u32[]{:S(2)}) collective-permute-start(bf16[2,256,512]{2,1,0:T(8,128)(2,1)S(1)} %add_convert_fusion), channel_id=1, source_target_pairs={{0,0},{1,24},{2,8},{3,16},{4,4},{5,28},{6,12},{7,20},{8,9},{9,17},... | collective-permute-start | bytes 1572872 | tf_op jit(solution)/shard_map/ppermute | solution.py:262

commit v26 on v25

--- a/solution.py
+++ b/solution.py
@@ -275,7 +275,11 @@
     states[0][0], within = lax.optimization_barrier((states[0][0], within))
     weight, _ = lax.optimization_barrier((out_weight, states[1][0]))
     mate_weight = swap(weight, 1)
-    for plane in range(3):
+    for part in range(parts):
+        for flip in (0, 1):
+            pairs = [(i, 2 + (i ^ flip)) for i in range(2)]
+            states[part].append(lax.ppermute(narrow[part], "seq", pairs))
+    for plane in (1, 2):
         pairs = [(2 * plane + i, 2 * plane + 2 + i) for i in range(2)]
         onward = [add(size, wide[part], *states[part]) for part in range(parts)]
         for part in range(parts):

time: 90.3 us -> 92.3 us (1.022)
  waiting for transfers between devices: 41.4 us -> 43.2 us
    ppermute x0 -> x4, starting transfers between devices: none -> 9.38 us  [pairs_body(): states[part].append(lax.ppermute(narrow[part], 'seq', pairs))]
    ppermute x6 -> x4, starting transfers between devices: 8.54 us -> 2.68 us  [pairs_body(): states[part].append(lax.ppermute(onward[part], 'seq', pairs))]
    ppermute x5, starting transfers between devices: 23.2 us -> 20 us  [move(): return lax.ppermute(value, both, pairs)]
    ppermute x0 -> x4, waiting for transfers between devices: none -> 2.43 us  [pairs_body(): states[part].append(lax.ppermute(narrow[part], 'seq', pairs))]
    ppermute x6 -> x4, waiting for transfers between devices: 2.22 us -> 0.01 us  [pairs_body(): states[part].append(lax.ppermute(onward[part], 'seq', pairs))]
    ppermute x5, waiting for transfers between devices: 24.5 us -> 26 us  [swap(): return lax.ppermute(value, 'seq', [(s, s ^ mask) for s in range(8)])]
  transfers between devices with their start and end apart: 16 -> 18, of which waited for: 7 -> 7; matrix products, arithmetic and copies ran while one was open for 0% -> 0% of each run, Pallas kernels for 7% -> 7%
where the time goes in v26:
time: 92.3 us; the launch traced here: 92 us
  waiting for transfers between devices  43.2 us (47%)
  starting transfers between devices  38.8 us (42%)
  Pallas kernels  7.07 us (8%)
  local copies, waits for them, and re-layouts  1.39 us (2%)
  other arithmetic  1.32 us (1%)
    ppermute x5, waiting for transfers between devices, swap(): return lax.ppermute(value, 'seq', [(s, s ^ mask) for s in range(8)])  26 us
    ppermute x5, starting transfers between devices, move(): return lax.ppermute(value, both, pairs)  20 us
    ppermute x5, waiting for transfers between devices, move(): return lax.ppermute(value, both, pairs)  14.7 us
    ppermute x4, starting transfers between devices, pairs_body(): states[part].append(lax.ppermute(narrow[part], 'seq', pairs))  9.38 us
    ppermute x5, starting transfers between devices, swap(): return lax.ppermute(value, 'seq', [(s, s ^ mask) for s in range(8)])  6.68 us
    ppermute x4, starting transfers between devices, pairs_body(): states[part].append(lax.ppermute(onward[part], 'seq', pairs))  2.68 us
    ppermute x4, waiting for transfers between devices, pairs_body(): states[part].append(lax.ppermute(narrow[part], 'seq', pairs))  2.43 us
  transfers between devices with their start and end apart: 18, of which 7 were waited for; matrix products, arithmetic and copies ran while one was open for 0% of the time, Pallas kernels for 7%

profile of v26, /device:TPU:1, one launch (start us, length us, event | category | flops | bytes accessed | tf_op | source)
XLA Modules:
  0.0 92.0 jit_solution(17951452512175912165)
XLA Ops:
  0.0 0.0 copy-start.1
  0.0 0.0 copy-start
  0.0 0.0 copy-start.2
  0.0 1.4 %fusion = (bf16[256,512]{1,0:T(8,128)(2,1)S(1)}, bf16[256,512]{1,0:T(8,128)(2,1)S(1)}, bf16[256,512]{1,0:T(8,128)(2,1)S(1)}, bf16[256,512]{1,0:T(8,128)(2,1)S(1)}) fusion(bf16[256,1024]{1,0:T(8,128)(2,1)} %v_ref.1, bf16[256,1024]{1,0:T(8,128)(2,1)} %k_ref.1), kind=kLoop, calls=%fused_computation.7 | loop fusion | bytes 2097152 | tf_op jit(solution)/shard_map/slice | solution.py:120
  1.4 0.3 shard_map.59
  1.7 5.0 %collective-permute-start.7 = (bf16[4,128,128]{2,1,0:T(8,128)(2,1)S(1)}, bf16[4,128,128]{2,1,0:T(8,128)(2,1)S(1)}, u32[]{:S(2)}, u32[]{:S(2)}) collective-permute-start(bf16[4,128,128]{2,1,0:T(8,128)(2,1)S(1)} %get-tuple-element.23), channel_id=1, source_target_pairs={{0,12},{4,8},{1,13},{5,9},{2,14},{6,10},{3,15},{7,11}} | collective-permute-start | bytes 393224 | tf_op jit(solution)/shard_map/ppermute | solution.py:281
  6.7 1.3 %collective-permute-start.6 = (bf16[4,128,128]{2,1,0:T(8,128)(2,1)S(1)}, bf16[4,128,128]{2,1,0:T(8,128)(2,1)S(1)}, u32[]{:S(2)}, u32[]{:S(2)}) collective-permute-start(bf16[4,128,128]{2,1,0:T(8,128)(2,1)S(1)} %get-tuple-element.23), channel_id=1, source_target_pairs={{0,8},{4,12},{1,9},{5,13},{2,10},{6,14},{3,11},{7,15}} | collective-permute-start | bytes 393224 | tf_op jit(solution)/shard_map/ppermute | solution.py:281
  8.0 0.3 collective-permute-start.5
  8.3 0.3 shard_map.55
  8.6 1.3 %collective-permute-start = (bf16[4,128,128]{2,1,0:T(8,128)(2,1)S(1)}, bf16[4,128,128]{2,1,0:T(8,128)(2,1)S(1)}, u32[]{:S(2)}, u32[]{:S(2)}) collective-permute-start(bf16[4,128,128]{2,1,0:T(8,128)(2,1)S(1)} %get-tuple-element.19), channel_id=1, source_target_pairs={{0,4},{4,0},{8,12},{12,8},{16,20},{20,16},{24,28},{28,24},{1,5},{5... | collective-permute-start | bytes 393224 | tf_op jit(solution)/shard_map/ppermute | solution.py:258
  9.8 1.3 %collective-permute-start.2 = (bf16[4,128,128]{2,1,0:T(8,128)(2,1)S(1)}, bf16[4,128,128]{2,1,0:T(8,128)(2,1)S(1)}, u32[]{:S(2)}, u32[]{:S(2)}) collective-permute-start(bf16[4,128,128]{2,1,0:T(8,128)(2,1)S(1)} %get-tuple-element.19), channel_id=1, source_target_pairs={{0,12},{4,8},{1,13},{5,9},{2,14},{6,10},{3,15},{7,11}} | collective-permute-start | bytes 393224 | tf_op jit(solution)/shard_map/ppermute | solution.py:281
  11.1 0.0 collective-permute-done.7.refs_3_.refs_7_
  11.1 1.8 %collective-permute-start.1 = (bf16[4,128,128]{2,1,0:T(8,128)(2,1)S(1)}, bf16[4,128,128]{2,1,0:T(8,128)(2,1)S(1)}, u32[]{:S(2)}, u32[]{:S(2)}) collective-permute-start(bf16[4,128,128]{2,1,0:T(8,128)(2,1)S(1)} %get-tuple-element.19), channel_id=1, source_target_pairs={{0,8},{4,12},{1,9},{5,13},{2,10},{6,14},{3,11},{7,15}} | collective-permute-start | bytes 393224 | tf_op jit(solution)/shard_map/ppermute | solution.py:281
  12.9 0.0 copy-done.1
  13.0 0.0 copy-done
  13.0 0.0 copy-done.2
  13.0 0.9 %shard_map.56.within_ref = f32[256,1024]{1,0:T(8,128)S(1)} custom-call(bf16[256,1024]{1,0:T(8,128)(2,1)S(1)} %copy-done.2, bf16[256,1024]{1,0:T(8,128)(2,1)S(1)} %copy-done, bf16[256,1024]{1,0:T(8,128)(2,1)S(1)} %copy-done.1), custom_call_target="tpu_custom_call" | custom-call | flops 268435456 | bytes 2621440 | tf_op jit(solution)/shard_map/pallas_call | solution.py:266
  13.9 0.0 copy-start.3
  13.9 0.0 collective-permute-done.6.refs_2_.refs_6_
  13.9 0.0 collective-permute-done.5.refs_1_.refs_5_
  13.9 0.1 shard_map.60
  14.0 0.7 collective-permute-start.8
  14.7 0.2 collective-permute-done.refs_1_.refs_0_
  14.9 0.0 collective-permute-done.2.refs_3_.refs_2_
  14.9 2.4 %collective-permute-done.1.refs_2_.refs_1_ = bf16[4,128,128]{2,1,0:T(8,128)(2,1)S(1)} collective-permute-done((bf16[4,128,128]{2,1,0:T(8,128)(2,1)S(1)}, bf16[4,128,128]{2,1,0:T(8,128)(2,1)S(1)}, u32[]{:S(2)}, u32[]{:S(2)}) %collective-permute-start.1) | collective-permute-done | bytes 131104 | tf_op jit(solution)/shard_map/ppermute | solution.py:281
  17.3 0.1 shard_map.57
  17.4 0.7 collective-permute-start.3
  18.1 0.1 collective-permute-start.11
  18.1 0.0 collective-permute-done.8.refs_4_.refs_8_
  18.2 0.1 shard_map.61
  18.2 0.7 collective-permute-start.9
  18.9 0.0 collective-permute-done.3.refs_4_.refs_3_
  18.9 0.1 shard_map.58
  19.0 0.7 collective-permute-start.4
  19.7 0.0 collective-permute-done.9.refs_9_
  19.7 0.0 collective-permute-done.4.refs_4_
  19.7 0.0 copy-done.3
  19.7 0.8 shard_map.62
  20.5 4.9 %collective-permute-start.10 = (bf16[256,1024]{1,0:T(8,128)(2,1)S(1)}, bf16[256,1024]{1,0:T(8,128)(2,1)S(1)}, u32[]{:S(2)}, u32[]{:S(2)}) collective-permute-start(bf16[256,1024]{1,0:T(8,128)(2,1)S(1)} %shard_map.62), channel_id=1, source_target_pairs={{0,8},{4,12},{8,0},{12,4},{16,24},{20,28},{24,16},{28,20},{1,9},{5... | collective-permute-start | bytes 1572872 | tf_op jit(solution)/shard_map/ppermute | solution.py:258
  25.4 6.8 %collective-permute-start.12 = (bf16[256,1024]{1,0:T(8,128)(2,1)S(1)}, bf16[256,1024]{1,0:T(8,128)(2,1)S(1)}, u32[]{:S(2)}, u32[]{:S(2)}) collective-permute-start(bf16[256,1024]{1,0:T(8,128)(2,1)S(1)} %shard_map.62), channel_id=1, source_target_pairs={{0,16},{1,17},{2,26},{3,27},{4,20},{5,21},{6,30},{7,31},{8,24},{9,... | collective-permute-start | bytes 1572872 | tf_op jit(solution)/shard_map/ppermute | solution.py:262
  32.2 15.0 %collective-permute-done.10 = bf16[256,1024]{1,0:T(8,128)(2,1)S(1)} collective-permute-done((bf16[256,1024]{1,0:T(8,128)(2,1)S(1)}, bf16[256,1024]{1,0:T(8,128)(2,1)S(1)}, u32[]{:S(2)}, u32[]{:S(2)}) %collective-permute-start.10) | collective-permute-done | bytes 524320 | tf_op jit(solution)/shard_map/ppermute | solution.py:258
  47.3 0.1 broadcast_select_fusion.1
  47.3 0.0 collective-permute-done.11.mate_ref
  47.4 1.7 %shard_map.63.weight_ref = bf16[2,1024,512]{2,1,0:T(8,128)(2,1)S(1)} custom-call(bf16[1024,512]{1,0:T(8,128)(2,1)} %own_ref.1, bf16[1024,512]{1,0:T(8,128)(2,1)} %collective-permute-done.11.mate_ref), custom_call_target="tpu_custom_call" | custom-call | bytes 4194304 | tf_op jit(solution)/shard_map/pallas_call | solution.py:290
  49.0 0.7 shard_map.65.light_ref
  49.8 0.0 collective-permute-done.12.heavy_ref
  49.8 0.7 shard_map.67
  50.5 6.7 %collective-permute-start.15 = (bf16[2,256,512]{2,1,0:T(8,128)(2,1)S(1)}, bf16[2,256,512]{2,1,0:T(8,128)(2,1)S(1)}, u32[]{:S(2)}, u32[]{:S(2)}) collective-permute-start(bf16[2,256,512]{2,1,0:T(8,128)(2,1)S(1)} %get-tuple-element.32), channel_id=1, source_target_pairs={{0,1},{1,0},{2,3},{3,2},{4,5},{5,4},{6,7},{7,6},{8,9},{9,8},{10,11... | collective-permute-start | bytes 1572872 | tf_op jit(solution)/shard_map/ppermute | solution.py:262
  57.2 0.1 collective-permute-start.13
  57.3 0.7 shard_map.64.light_ref
  58.0 0.8 collective-permute-done.15
  58.7 0.1 add_convert_fusion.1
  58.9 1.1 %collective-permute-start.16 = (bf16[2,256,512]{2,1,0:T(8,128)(2,1)S(1)}, bf16[2,256,512]{2,1,0:T(8,128)(2,1)S(1)}, u32[]{:S(2)}, u32[]{:S(2)}) collective-permute-start(bf16[2,256,512]{2,1,0:T(8,128)(2,1)S(1)} %add_convert_fusion.1), channel_id=1, source_target_pairs={{0,2},{1,3},{2,0},{3,1},{4,6},{5,7},{6,4},{7,5},{8,10},{9,11},{10,... | collective-permute-start | bytes 1572872 | tf_op jit(solution)/shard_map/ppermute | solution.py:262
  59.9 10.8 %collective-permute-done.13.heavy_ref = bf16[256,1024]{1,0:T(8,128)(2,1)S(1)} collective-permute-done((bf16[256,1024]{1,0:T(8,128)(2,1)S(1)}, bf16[256,1024]{1,0:T(8,128)(2,1)S(1)}, u32[]{:S(2)}, u32[]{:S(2)}) %collective-permute-start.13) | collective-permute-done | bytes 524320 | tf_op jit(solution)/shard_map/ppermute | solution.py:258
  70.7 0.7 shard_map.66
  71.4 0.9 %collective-permute-start.14 = (bf16[2,256,512]{2,1,0:T(8,128)(2,1)S(1)}, bf16[2,256,512]{2,1,0:T(8,128)(2,1)S(1)}, u32[]{:S(2)}, u32[]{:S(2)}) collective-permute-start(bf16[2,256,512]{2,1,0:T(8,128)(2,1)S(1)} %get-tuple-element.29), channel_id=1, source_target_pairs={{0,1},{1,0},{2,3},{3,2},{4,5},{5,4},{6,7},{7,6},{8,9},{9,8},{10,11... | collective-permute-start | bytes 1572872 | tf_op jit(solution)/shard_map/ppermute | solution.py:262
  72.4 0.0 collective-permute-done.16
  72.4 1.5 %collective-permute-done.14 = bf16[2,256,512]{2,1,0:T(8,128)(2,1)S(1)} collective-permute-done((bf16[2,256,512]{2,1,0:T(8,128)(2,1)S(1)}, bf16[2,256,512]{2,1,0:T(8,128)(2,1)S(1)}, u32[]{:S(2)}, u32[]{:S(2)}) %collective-permute-start.14) | collective-permute-done | bytes 524320 | tf_op jit(solution)/shard_map/ppermute | solution.py:262
  73.9 0.2 add_convert_fusion
  74.1 4.6 %collective-permute-start.17 = (bf16[2,256,512]{2,1,0:T(8,128)(2,1)S(1)}, bf16[2,256,512]{2,1,0:T(8,128)(2,1)S(1)}, u32[]{:S(2)}, u32[]{:S(2)}) collective-permute-start(bf16[2,256,512]{2,1,0:T(8,128)(2,1)S(1)} %add_convert_fusion), channel_id=1, source_target_pairs={{0,0},{1,24},{2,8},{3,16},{4,4},{5,28},{6,12},{7,20},{8,9},{9,17},... | collective-permute-start | bytes 1572872 | tf_op jit(solution)/shard_map/ppermute | solution.py:262
  78.7 12.4 %collective-permute-done.17 = bf16[2,256,512]{2,1,0:T(8,128)(2,1)S(1)} collective-permute-done((bf16[2,256,512]{2,1,0:T(8,128)(2,1)S(1)}, bf16[2,256,512]{2,1,0:T(8,128)(2,1)S(1)}, u32[]{:S(2)}, u32[]{:S(2)}) %collective-permute-start.17) | collective-permute-done | bytes 524320 | tf_op jit(solution)/shard_map/ppermute | solution.py:262
  91.2 0.9 pad_maximum_fusion
  (1 shorter events, 0.0 us)
Async XLA Ops:
  0.0 12.9 %copy-start.1 = (bf16[256,1024]{1,0:T(8,128)(2,1)S(1)}, bf16[256,1024]{1,0:T(8,128)(2,1)}, u32[]{:S(2)}) copy-start(bf16[256,1024]{1,0:T(8,128)(2,1)} %v_ref.1) | copy-start | bytes 1572868
  0.0 13.0 %copy-start = (bf16[256,1024]{1,0:T(8,128)(2,1)S(1)}, bf16[256,1024]{1,0:T(8,128)(2,1)}, u32[]{:S(2)}) copy-start(bf16[256,1024]{1,0:T(8,128)(2,1)} %k_ref.1) | copy-start | bytes 1572868
  0.0 13.0 %copy-start.2 = (bf16[256,1024]{1,0:T(8,128)(2,1)S(1)}, bf16[256,1024]{1,0:T(8,128)(2,1)}, u32[]{:S(2)}) copy-start(bf16[256,1024]{1,0:T(8,128)(2,1)} %q_ref.3) | copy-start | bytes 1572868
  1.7 9.5 %collective-permute-start.7 = (bf16[4,128,128]{2,1,0:T(8,128)(2,1)S(1)}, bf16[4,128,128]{2,1,0:T(8,128)(2,1)S(1)}, u32[]{:S(2)}, u32[]{:S(2)}) collective-permute-start(bf16[4,128,128]{2,1,0:T(8,128)(2,1)S(1)} %get-tuple-element.23), channel_id=1, source_target_pairs={{0,12},{4,8},{1,13},{5,9},{2,14},{6,10},{3,15},{7,11}} | collective-permute-start | bytes 393224 | tf_op jit(solution)/shard_map/ppermute | solution.py:281
  6.7 7.3 %collective-permute-start.6 = (bf16[4,128,128]{2,1,0:T(8,128)(2,1)S(1)}, bf16[4,128,128]{2,1,0:T(8,128)(2,1)S(1)}, u32[]{:S(2)}, u32[]{:S(2)}) collective-permute-start(bf16[4,128,128]{2,1,0:T(8,128)(2,1)S(1)} %get-tuple-element.23), channel_id=1, source_target_pairs={{0,8},{4,12},{1,9},{5,13},{2,10},{6,14},{3,11},{7,15}} | collective-permute-start | bytes 393224 | tf_op jit(solution)/shard_map/ppermute | solution.py:281
  8.0 6.0 %collective-permute-start.5 = (bf16[4,128,128]{2,1,0:T(8,128)(2,1)S(1)}, bf16[4,128,128]{2,1,0:T(8,128)(2,1)S(1)}, u32[]{:S(2)}, u32[]{:S(2)}) collective-permute-start(bf16[4,128,128]{2,1,0:T(8,128)(2,1)S(1)} %get-tuple-element.23), channel_id=1, source_target_pairs={{0,4},{4,0},{8,12},{12,8},{16,20},{20,16},{24,28},{28,24},{1,5},{5... | collective-permute-start | bytes 393224 | tf_op jit(solution)/shard_map/ppermute | solution.py:258
  8.6 6.3 %collective-permute-start = (bf16[4,128,128]{2,1,0:T(8,128)(2,1)S(1)}, bf16[4,128,128]{2,1,0:T(8,128)(2,1)S(1)}, u32[]{:S(2)}, u32[]{:S(2)}) collective-permute-start(bf16[4,128,128]{2,1,0:T(8,128)(2,1)S(1)} %get-tuple-element.19), channel_id=1, source_target_pairs={{0,4},{4,0},{8,12},{12,8},{16,20},{20,16},{24,28},{28,24},{1,5},{5... | collective-permute-start | bytes 393224 | tf_op jit(solution)/shard_map/ppermute | solution.py:258
  9.8 5.1 %collective-permute-start.2 = (bf16[4,128,128]{2,1,0:T(8,128)(2,1)S(1)}, bf16[4,128,128]{2,1,0:T(8,128)(2,1)S(1)}, u32[]{:S(2)}, u32[]{:S(2)}) collective-permute-start(bf16[4,128,128]{2,1,0:T(8,128)(2,1)S(1)} %get-tuple-element.19), channel_id=1, source_target_pairs={{0,12},{4,8},{1,13},{5,9},{2,14},{6,10},{3,15},{7,11}} | collective-permute-start | bytes 393224 | tf_op jit(solution)/shard_map/ppermute | solution.py:281
  11.1 6.2 %collective-permute-start.1 = (bf16[4,128,128]{2,1,0:T(8,128)(2,1)S(1)}, bf16[4,128,128]{2,1,0:T(8,128)(2,1)S(1)}, u32[]{:S(2)}, u32[]{:S(2)}) collective-permute-start(bf16[4,128,128]{2,1,0:T(8,128)(2,1)S(1)} %get-tuple-element.19), channel_id=1, source_target_pairs={{0,8},{4,12},{1,9},{5,13},{2,10},{6,14},{3,11},{7,15}} | collective-permute-start | bytes 393224 | tf_op jit(solution)/shard_map/ppermute | solution.py:281
  13.9 5.8 %copy-start.3 = (f32[1024]{0:T(1024)S(1)}, f32[1024]{0:T(1024)}, u32[]{:S(2)}) copy-start(f32[1024]{0:T(1024)} %param.8) | copy-start | bytes 12292
  14.0 4.1 %collective-permute-start.8 = (bf16[4,128,128]{2,1,0:T(8,128)(2,1)S(1)}, bf16[4,128,128]{2,1,0:T(8,128)(2,1)S(1)}, u32[]{:S(2)}, u32[]{:S(2)}) collective-permute-start(bf16[4,128,128]{2,1,0:T(8,128)(2,1)S(1)} %shard_map.60), channel_id=1, source_target_pairs={{8,16},{12,20},{9,17},{13,21},{10,18},{14,22},{11,19},{15,23}} | collective-permute-start | bytes 393224 | tf_op jit(solution)/shard_map/ppermute | solution.py:286
  17.4 1.5 %collective-permute-start.3 = (bf16[4,128,128]{2,1,0:T(8,128)(2,1)S(1)}, bf16[4,128,128]{2,1,0:T(8,128)(2,1)S(1)}, u32[]{:S(2)}, u32[]{:S(2)}) collective-permute-start(bf16[4,128,128]{2,1,0:T(8,128)(2,1)S(1)} %shard_map.57), channel_id=1, source_target_pairs={{8,16},{12,20},{9,17},{13,21},{10,18},{14,22},{11,19},{15,23}} | collective-permute-start | bytes 393224 | tf_op jit(solution)/shard_map/ppermute | solution.py:286
  18.1 29.3 %collective-permute-start.11 = (bf16[1024,512]{1,0:T(8,128)(2,1)}, bf16[1024,512]{1,0:T(8,128)(2,1)}, u32[]{:S(2)}, u32[]{:S(2)}) collective-permute-start(bf16[1024,512]{1,0:T(8,128)(2,1)} %own_ref.1), channel_id=1, source_target_pairs={{0,4},{4,0},{8,12},{12,8},{16,20},{20,16},{24,28},{28,24},{1,5},{5... | collective-permute-start | bytes 3145736 | tf_op jit(solution)/shard_map/ppermute | solution.py:258
  18.2 1.5 %collective-permute-start.9 = (bf16[4,128,128]{2,1,0:T(8,128)(2,1)S(1)}, bf16[4,128,128]{2,1,0:T(8,128)(2,1)S(1)}, u32[]{:S(2)}, u32[]{:S(2)}) collective-permute-start(bf16[4,128,128]{2,1,0:T(8,128)(2,1)S(1)} %shard_map.61), channel_id=1, source_target_pairs={{16,24},{20,28},{17,25},{21,29},{18,26},{22,30},{19,27},{23,31}} | collective-permute-start | bytes 393224 | tf_op jit(solution)/shard_map/ppermute | solution.py:286
  19.0 0.7 collective-permute-start.4
  20.5 26.8 %collective-permute-start.10 = (bf16[256,1024]{1,0:T(8,128)(2,1)S(1)}, bf16[256,1024]{1,0:T(8,128)(2,1)S(1)}, u32[]{:S(2)}, u32[]{:S(2)}) collective-permute-start(bf16[256,1024]{1,0:T(8,128)(2,1)S(1)} %shard_map.62), channel_id=1, source_target_pairs={{0,8},{4,12},{8,0},{12,4},{16,24},{20,28},{24,16},{28,20},{1,9},{5... | collective-permute-start | bytes 1572872 | tf_op jit(solution)/shard_map/ppermute | solution.py:258
  25.4 24.3 %collective-permute-start.12 = (bf16[256,1024]{1,0:T(8,128)(2,1)S(1)}, bf16[256,1024]{1,0:T(8,128)(2,1)S(1)}, u32[]{:S(2)}, u32[]{:S(2)}) collective-permute-start(bf16[256,1024]{1,0:T(8,128)(2,1)S(1)} %shard_map.62), channel_id=1, source_target_pairs={{0,16},{1,17},{2,26},{3,27},{4,20},{5,21},{6,30},{7,31},{8,24},{9,... | collective-permute-start | bytes 1572872 | tf_op jit(solution)/shard_map/ppermute | solution.py:262
  50.5 8.2 %collective-permute-start.15 = (bf16[2,256,512]{2,1,0:T(8,128)(2,1)S(1)}, bf16[2,256,512]{2,1,0:T(8,128)(2,1)S(1)}, u32[]{:S(2)}, u32[]{:S(2)}) collective-permute-start(bf16[2,256,512]{2,1,0:T(8,128)(2,1)S(1)} %get-tuple-element.32), channel_id=1, source_target_pairs={{0,1},{1,0},{2,3},{3,2},{4,5},{5,4},{6,7},{7,6},{8,9},{9,8},{10,11... | collective-permute-start | bytes 1572872 | tf_op jit(solution)/shard_map/ppermute | solution.py:262
  57.2 13.5 %collective-permute-start.13 = (bf16[256,1024]{1,0:T(8,128)(2,1)S(1)}, bf16[256,1024]{1,0:T(8,128)(2,1)S(1)}, u32[]{:S(2)}, u32[]{:S(2)}) collective-permute-start(bf16[256,1024]{1,0:T(8,128)(2,1)S(1)} %collective-permute-done.12.heavy_ref), channel_id=1, source_target_pairs={{0,8},{4,12},{8,0},{12,4},{16,24},{20,28},{24,16},{28,20},{1,9},{5... | collective-permute-start | bytes 1572872 | tf_op jit(solution)/shard_map/ppermute | solution.py:258
  58.9 13.5 %collective-permute-start.16 = (bf16[2,256,512]{2,1,0:T(8,128)(2,1)S(1)}, bf16[2,256,512]{2,1,0:T(8,128)(2,1)S(1)}, u32[]{:S(2)}, u32[]{:S(2)}) collective-permute-start(bf16[2,256,512]{2,1,0:T(8,128)(2,1)S(1)} %add_convert_fusion.1), channel_id=1, source_target_pairs={{0,2},{1,3},{2,0},{3,1},{4,6},{5,7},{6,4},{7,5},{8,10},{9,11},{10,... | collective-permute-start | bytes 1572872 | tf_op jit(solution)/shard_map/ppermute | solution.py:262
  71.4 2.5 %collective-permute-start.14 = (bf16[2,256,512]{2,1,0:T(8,128)(2,1)S(1)}, bf16[2,256,512]{2,1,0:T(8,128)(2,1)S(1)}, u32[]{:S(2)}, u32[]{:S(2)}) collective-permute-start(bf16[2,256,512]{2,1,0:T(8,128)(2,1)S(1)} %get-tuple-element.29), channel_id=1, source_target_pairs={{0,1},{1,0},{2,3},{3,2},{4,5},{5,4},{6,7},{7,6},{8,9},{9,8},{10,11... | collective-permute-start | bytes 1572872 | tf_op jit(solution)/shard_map/ppermute | solution.py:262
  74.1 17.0 %collective-permute-start.17 = (bf16[2,256,512]{2,1,0:T(8,128)(2,1)S(1)}, bf16[2,256,512]{2,1,0:T(8,128)(2,1)S(1)}, u32[]{:S(2)}, u32[]{:S(2)}) collective-permute-start(bf16[2,256,512]{2,1,0:T(8,128)(2,1)S(1)} %add_convert_fusion), channel_id=1, source_target_pairs={{0,0},{1,24},{2,8},{3,16},{4,4},{5,28},{6,12},{7,20},{8,9},{9,17},... | collective-permute-start | bytes 1572872 | tf_op jit(solution)/shard_map/ppermute | solution.py:262

commit v27 on v25

--- a/solution.py
+++ b/solution.py
@@ -98,7 +98,7 @@
         carried = jnp.dot(q_ref[:, cols], state.astype(BF16), preferred_element_type=F32)
         combined = within_ref[:, cols] + carried
         mean_square = jnp.mean(combined * combined, axis=-1, keepdims=True)
-        scaled = combined / jnp.sqrt(mean_square + epsilon) * gain_ref[:, cols]
+        scaled = combined * (lax.rsqrt(mean_square + epsilon) * gain_ref[:, cols])
         out_ref[:, cols] = scaled.astype(BF16)
 
 

time: 90.3 us -> 90.1 us (level)
  transfers between devices with their start and end apart: 16 -> 16, of which waited for: 7 -> 7; matrix products, arithmetic and copies ran while one was open for 0% -> 0% of each run, Pallas kernels for 7% -> 6%
where the time goes in v27:
time: 90.1 us; the launch traced here: 89.9 us
  waiting for transfers between devices  41.4 us (46%)
  starting transfers between devices  38.6 us (43%)
  Pallas kernels  6.83 us (8%)
  local copies, waits for them, and re-layouts  1.41 us (2%)
  other arithmetic  1.32 us (1%)
    ppermute x5, waiting for transfers between devices, swap(): return lax.ppermute(value, 'seq', [(s, s ^ mask) for s in range(8)])  24.5 us
    ppermute x5, starting transfers between devices, move(): return lax.ppermute(value, both, pairs)  23.2 us
    ppermute x5, waiting for transfers between devices, move(): return lax.ppermute(value, both, pairs)  14.7 us
    ppermute x6, starting transfers between devices, pairs_body(): states[part].append(lax.ppermute(onward[part], 'seq', pairs))  8.54 us
    ppermute x5, starting transfers between devices, swap(): return lax.ppermute(value, 'seq', [(s, s ^ mask) for s in range(8)])  6.8 us
    ppermute x6, waiting for transfers between devices, pairs_body(): states[part].append(lax.ppermute(onward[part], 'seq', pairs))  2.22 us
  transfers between devices with their start and end apart: 16, of which 7 were waited for; matrix products, arithmetic and copies ran while one was open for 0% of the time, Pallas kernels for 6%

profile of v27, /device:TPU:1, one launch (start us, length us, event | category | flops | bytes accessed | tf_op | source)
XLA Modules:
  0.0 89.9 jit_solution(9471793743751330474)
XLA Ops:
  0.0 0.0 copy-start.1
  0.0 0.0 copy-start
  0.0 0.0 copy-start.2
  0.0 1.4 %fusion = (bf16[256,512]{1,0:T(8,128)(2,1)S(1)}, bf16[256,512]{1,0:T(8,128)(2,1)S(1)}, bf16[256,512]{1,0:T(8,128)(2,1)S(1)}, bf16[256,512]{1,0:T(8,128)(2,1)S(1)}) fusion(bf16[256,1024]{1,0:T(8,128)(2,1)} %v_ref.1, bf16[256,1024]{1,0:T(8,128)(2,1)} %k_ref.1), kind=kLoop, calls=%fused_computation.7 | loop fusion | bytes 2097152 | tf_op jit(solution)/shard_map/slice | solution.py:120
  1.4 0.3 shard_map.60
  1.7 2.1 %collective-permute-start.4 = (bf16[4,128,128]{2,1,0:T(8,128)(2,1)S(1)}, bf16[4,128,128]{2,1,0:T(8,128)(2,1)S(1)}, u32[]{:S(2)}, u32[]{:S(2)}) collective-permute-start(bf16[4,128,128]{2,1,0:T(8,128)(2,1)S(1)} %get-tuple-element.23), channel_id=1, source_target_pairs={{0,4},{4,0},{8,12},{12,8},{16,20},{20,16},{24,28},{28,24},{1,5},{5... | collective-permute-start | bytes 393224 | tf_op jit(solution)/shard_map/ppermute | solution.py:258
  3.8 0.3 shard_map.55
  4.1 0.1 collective-permute-start
  4.2 0.0 copy-done.1
  4.2 0.0 copy-done
  4.2 0.0 copy-done.2
  4.2 0.9 %shard_map.56.within_ref = f32[256,1024]{1,0:T(8,128)S(1)} custom-call(bf16[256,1024]{1,0:T(8,128)(2,1)S(1)} %copy-done.2, bf16[256,1024]{1,0:T(8,128)(2,1)S(1)} %copy-done, bf16[256,1024]{1,0:T(8,128)(2,1)S(1)} %copy-done.1), custom_call_target="tpu_custom_call" | custom-call | flops 268435456 | bytes 2621440 | tf_op jit(solution)/shard_map/pallas_call | solution.py:266
  5.1 0.0 copy-start.3
  5.1 1.9 %collective-permute-done.4.refs_1_.refs_4_ = bf16[4,128,128]{2,1,0:T(8,128)(2,1)S(1)} collective-permute-done((bf16[4,128,128]{2,1,0:T(8,128)(2,1)S(1)}, bf16[4,128,128]{2,1,0:T(8,128)(2,1)S(1)}, u32[]{:S(2)}, u32[]{:S(2)}) %collective-permute-start.4) | collective-permute-done | bytes 131104 | tf_op jit(solution)/shard_map/ppermute | solution.py:258
  7.1 3.1 %collective-permute-start.5 = (bf16[4,128,128]{2,1,0:T(8,128)(2,1)S(1)}, bf16[4,128,128]{2,1,0:T(8,128)(2,1)S(1)}, u32[]{:S(2)}, u32[]{:S(2)}) collective-permute-start(bf16[4,128,128]{2,1,0:T(8,128)(2,1)S(1)} %shard_map.61), channel_id=1, source_target_pairs={{0,8},{4,12},{1,9},{5,13},{2,10},{6,14},{3,11},{7,15}} | collective-permute-start | bytes 393224 | tf_op jit(solution)/shard_map/ppermute | solution.py:282
  10.2 0.0 collective-permute-done.refs_1_.refs_0_
  10.2 2.8 %collective-permute-start.1 = (bf16[4,128,128]{2,1,0:T(8,128)(2,1)S(1)}, bf16[4,128,128]{2,1,0:T(8,128)(2,1)S(1)}, u32[]{:S(2)}, u32[]{:S(2)}) collective-permute-start(bf16[4,128,128]{2,1,0:T(8,128)(2,1)S(1)} %shard_map.57), channel_id=1, source_target_pairs={{0,8},{4,12},{1,9},{5,13},{2,10},{6,14},{3,11},{7,15}} | collective-permute-start | bytes 393224 | tf_op jit(solution)/shard_map/ppermute | solution.py:282
  13.0 0.0 collective-permute-done.5.refs_2_.refs_5_
  13.1 0.7 collective-permute-start.6
  13.7 2.2 %collective-permute-done.1.refs_2_.refs_1_ = bf16[4,128,128]{2,1,0:T(8,128)(2,1)S(1)} collective-permute-done((bf16[4,128,128]{2,1,0:T(8,128)(2,1)S(1)}, bf16[4,128,128]{2,1,0:T(8,128)(2,1)S(1)}, u32[]{:S(2)}, u32[]{:S(2)}) %collective-permute-start.1) | collective-permute-done | bytes 131104 | tf_op jit(solution)/shard_map/ppermute | solution.py:282
  16.0 0.7 collective-permute-start.2
  16.7 1.3 %collective-permute-start.9 = (bf16[1024,512]{1,0:T(8,128)(2,1)}, bf16[1024,512]{1,0:T(8,128)(2,1)}, u32[]{:S(2)}, u32[]{:S(2)}) collective-permute-start(bf16[1024,512]{1,0:T(8,128)(2,1)} %own_ref.1), channel_id=1, source_target_pairs={{0,4},{4,0},{8,12},{12,8},{16,20},{20,16},{24,28},{28,24},{1,5},{5... | collective-permute-start | bytes 3145736 | tf_op jit(solution)/shard_map/ppermute | solution.py:258
  18.0 0.0 collective-permute-done.6.refs_3_.refs_6_
  18.0 0.1 shard_map.63
  18.0 0.7 collective-permute-start.7
  18.7 0.0 collective-permute-done.2.refs_3_.refs_2_
  18.7 0.1 shard_map.59
  18.8 0.7 collective-permute-start.3
  19.5 0.0 collective-permute-done.7.refs_7_
  19.5 0.0 collective-permute-done.3.refs_3_
  19.5 0.0 copy-done.3
  19.5 0.5 shard_map.64
  20.1 3.2 %collective-permute-start.8 = (bf16[256,1024]{1,0:T(8,128)(2,1)S(1)}, bf16[256,1024]{1,0:T(8,128)(2,1)S(1)}, u32[]{:S(2)}, u32[]{:S(2)}) collective-permute-start(bf16[256,1024]{1,0:T(8,128)(2,1)S(1)} %shard_map.64), channel_id=1, source_target_pairs={{0,8},{4,12},{8,0},{12,4},{16,24},{20,28},{24,16},{28,20},{1,9},{5... | collective-permute-start | bytes 1572872 | tf_op jit(solution)/shard_map/ppermute | solution.py:258
  23.3 6.8 %collective-permute-start.10 = (bf16[256,1024]{1,0:T(8,128)(2,1)S(1)}, bf16[256,1024]{1,0:T(8,128)(2,1)S(1)}, u32[]{:S(2)}, u32[]{:S(2)}) collective-permute-start(bf16[256,1024]{1,0:T(8,128)(2,1)S(1)} %shard_map.64), channel_id=1, source_target_pairs={{0,16},{1,17},{2,26},{3,27},{4,20},{5,21},{6,30},{7,31},{8,24},{9,... | collective-permute-start | bytes 1572872 | tf_op jit(solution)/shard_map/ppermute | solution.py:262
  30.1 11.8 %collective-permute-done.8 = bf16[256,1024]{1,0:T(8,128)(2,1)S(1)} collective-permute-done((bf16[256,1024]{1,0:T(8,128)(2,1)S(1)}, bf16[256,1024]{1,0:T(8,128)(2,1)S(1)}, u32[]{:S(2)}, u32[]{:S(2)}) %collective-permute-start.8) | collective-permute-done | bytes 524320 | tf_op jit(solution)/shard_map/ppermute | solution.py:258
  41.9 0.1 broadcast_select_fusion.1
  42.0 0.0 collective-permute-done.9.mate_ref
  42.0 1.7 %shard_map.65.weight_ref = bf16[2,1024,512]{2,1,0:T(8,128)(2,1)S(1)} custom-call(bf16[1024,512]{1,0:T(8,128)(2,1)} %own_ref.1, bf16[1024,512]{1,0:T(8,128)(2,1)} %collective-permute-done.9.mate_ref), custom_call_target="tpu_custom_call" | custom-call | bytes 4194304 | tf_op jit(solution)/shard_map/pallas_call | solution.py:286
  43.7 0.7 shard_map.67.light_ref
  44.4 0.0 collective-permute-done.10.heavy_ref
  44.4 0.7 shard_map.69
  45.2 9.9 %collective-permute-start.13 = (bf16[2,256,512]{2,1,0:T(8,128)(2,1)S(1)}, bf16[2,256,512]{2,1,0:T(8,128)(2,1)S(1)}, u32[]{:S(2)}, u32[]{:S(2)}) collective-permute-start(bf16[2,256,512]{2,1,0:T(8,128)(2,1)S(1)} %get-tuple-element.32), channel_id=1, source_target_pairs={{0,1},{1,0},{2,3},{3,2},{4,5},{5,4},{6,7},{7,6},{8,9},{9,8},{10,11... | collective-permute-start | bytes 1572872 | tf_op jit(solution)/shard_map/ppermute | solution.py:262
  55.0 0.1 collective-permute-start.11
  55.1 0.7 shard_map.66.light_ref
  55.8 0.8 collective-permute-done.13
  56.6 0.1 add_convert_fusion.1
  56.7 1.1 %collective-permute-start.14 = (bf16[2,256,512]{2,1,0:T(8,128)(2,1)S(1)}, bf16[2,256,512]{2,1,0:T(8,128)(2,1)S(1)}, u32[]{:S(2)}, u32[]{:S(2)}) collective-permute-start(bf16[2,256,512]{2,1,0:T(8,128)(2,1)S(1)} %add_convert_fusion.1), channel_id=1, source_target_pairs={{0,2},{1,3},{2,0},{3,1},{4,6},{5,7},{6,4},{7,5},{8,10},{9,11},{10,... | collective-permute-start | bytes 1572872 | tf_op jit(solution)/shard_map/ppermute | solution.py:262
  57.8 10.8 %collective-permute-done.11.heavy_ref = bf16[256,1024]{1,0:T(8,128)(2,1)S(1)} collective-permute-done((bf16[256,1024]{1,0:T(8,128)(2,1)S(1)}, bf16[256,1024]{1,0:T(8,128)(2,1)S(1)}, u32[]{:S(2)}, u32[]{:S(2)}) %collective-permute-start.11) | collective-permute-done | bytes 524320 | tf_op jit(solution)/shard_map/ppermute | solution.py:258
  68.5 0.7 shard_map.68
  69.3 0.9 %collective-permute-start.12 = (bf16[2,256,512]{2,1,0:T(8,128)(2,1)S(1)}, bf16[2,256,512]{2,1,0:T(8,128)(2,1)S(1)}, u32[]{:S(2)}, u32[]{:S(2)}) collective-permute-start(bf16[2,256,512]{2,1,0:T(8,128)(2,1)S(1)} %get-tuple-element.29), channel_id=1, source_target_pairs={{0,1},{1,0},{2,3},{3,2},{4,5},{5,4},{6,7},{7,6},{8,9},{9,8},{10,11... | collective-permute-start | bytes 1572872 | tf_op jit(solution)/shard_map/ppermute | solution.py:262
  70.2 0.0 collective-permute-done.14
  70.2 1.5 %collective-permute-done.12 = bf16[2,256,512]{2,1,0:T(8,128)(2,1)S(1)} collective-permute-done((bf16[2,256,512]{2,1,0:T(8,128)(2,1)S(1)}, bf16[2,256,512]{2,1,0:T(8,128)(2,1)S(1)}, u32[]{:S(2)}, u32[]{:S(2)}) %collective-permute-start.12) | collective-permute-done | bytes 524320 | tf_op jit(solution)/shard_map/ppermute | solution.py:262
  71.7 0.2 add_convert_fusion
  71.9 4.6 %collective-permute-start.15 = (bf16[2,256,512]{2,1,0:T(8,128)(2,1)S(1)}, bf16[2,256,512]{2,1,0:T(8,128)(2,1)S(1)}, u32[]{:S(2)}, u32[]{:S(2)}) collective-permute-start(bf16[2,256,512]{2,1,0:T(8,128)(2,1)S(1)} %add_convert_fusion), channel_id=1, source_target_pairs={{0,0},{1,24},{2,8},{3,16},{4,4},{5,28},{6,12},{7,20},{8,9},{9,17},... | collective-permute-start | bytes 1572872 | tf_op jit(solution)/shard_map/ppermute | solution.py:262
  76.5 12.4 %collective-permute-done.15 = bf16[2,256,512]{2,1,0:T(8,128)(2,1)S(1)} collective-permute-done((bf16[2,256,512]{2,1,0:T(8,128)(2,1)S(1)}, bf16[2,256,512]{2,1,0:T(8,128)(2,1)S(1)}, u32[]{:S(2)}, u32[]{:S(2)}) %collective-permute-start.15) | collective-permute-done | bytes 524320 | tf_op jit(solution)/shard_map/ppermute | solution.py:262
  89.0 0.9 pad_maximum_fusion
  (5 shorter events, 0.2 us)
Async XLA Ops:
  0.0 4.2 %copy-start.1 = (bf16[256,1024]{1,0:T(8,128)(2,1)S(1)}, bf16[256,1024]{1,0:T(8,128)(2,1)}, u32[]{:S(2)}) copy-start(bf16[256,1024]{1,0:T(8,128)(2,1)} %v_ref.1) | copy-start | bytes 1572868
  0.0 4.2 %copy-start = (bf16[256,1024]{1,0:T(8,128)(2,1)S(1)}, bf16[256,1024]{1,0:T(8,128)(2,1)}, u32[]{:S(2)}) copy-start(bf16[256,1024]{1,0:T(8,128)(2,1)} %k_ref.1) | copy-start | bytes 1572868
  0.0 4.2 %copy-start.2 = (bf16[256,1024]{1,0:T(8,128)(2,1)S(1)}, bf16[256,1024]{1,0:T(8,128)(2,1)}, u32[]{:S(2)}) copy-start(bf16[256,1024]{1,0:T(8,128)(2,1)} %q_ref.3) | copy-start | bytes 1572868
  1.7 5.4 %collective-permute-start.4 = (bf16[4,128,128]{2,1,0:T(8,128)(2,1)S(1)}, bf16[4,128,128]{2,1,0:T(8,128)(2,1)S(1)}, u32[]{:S(2)}, u32[]{:S(2)}) collective-permute-start(bf16[4,128,128]{2,1,0:T(8,128)(2,1)S(1)} %get-tuple-element.23), channel_id=1, source_target_pairs={{0,4},{4,0},{8,12},{12,8},{16,20},{20,16},{24,28},{28,24},{1,5},{5... | collective-permute-start | bytes 393224 | tf_op jit(solution)/shard_map/ppermute | solution.py:258
  4.1 6.1 %collective-permute-start = (bf16[4,128,128]{2,1,0:T(8,128)(2,1)S(1)}, bf16[4,128,128]{2,1,0:T(8,128)(2,1)S(1)}, u32[]{:S(2)}, u32[]{:S(2)}) collective-permute-start(bf16[4,128,128]{2,1,0:T(8,128)(2,1)S(1)} %get-tuple-element.19), channel_id=1, source_target_pairs={{0,4},{4,0},{8,12},{12,8},{16,20},{20,16},{24,28},{28,24},{1,5},{5... | collective-permute-start | bytes 393224 | tf_op jit(solution)/shard_map/ppermute | solution.py:258
  5.1 14.4 %copy-start.3 = (f32[1024]{0:T(1024)S(1)}, f32[1024]{0:T(1024)}, u32[]{:S(2)}) copy-start(f32[1024]{0:T(1024)} %param.8) | copy-start | bytes 12292
  7.1 5.9 %collective-permute-start.5 = (bf16[4,128,128]{2,1,0:T(8,128)(2,1)S(1)}, bf16[4,128,128]{2,1,0:T(8,128)(2,1)S(1)}, u32[]{:S(2)}, u32[]{:S(2)}) collective-permute-start(bf16[4,128,128]{2,1,0:T(8,128)(2,1)S(1)} %shard_map.61), channel_id=1, source_target_pairs={{0,8},{4,12},{1,9},{5,13},{2,10},{6,14},{3,11},{7,15}} | collective-permute-start | bytes 393224 | tf_op jit(solution)/shard_map/ppermute | solution.py:282
  10.2 5.7 %collective-permute-start.1 = (bf16[4,128,128]{2,1,0:T(8,128)(2,1)S(1)}, bf16[4,128,128]{2,1,0:T(8,128)(2,1)S(1)}, u32[]{:S(2)}, u32[]{:S(2)}) collective-permute-start(bf16[4,128,128]{2,1,0:T(8,128)(2,1)S(1)} %shard_map.57), channel_id=1, source_target_pairs={{0,8},{4,12},{1,9},{5,13},{2,10},{6,14},{3,11},{7,15}} | collective-permute-start | bytes 393224 | tf_op jit(solution)/shard_map/ppermute | solution.py:282
  13.1 4.9 %collective-permute-start.6 = (bf16[4,128,128]{2,1,0:T(8,128)(2,1)S(1)}, bf16[4,128,128]{2,1,0:T(8,128)(2,1)S(1)}, u32[]{:S(2)}, u32[]{:S(2)}) collective-permute-start(bf16[4,128,128]{2,1,0:T(8,128)(2,1)S(1)} %shard_map.62), channel_id=1, source_target_pairs={{8,16},{12,20},{9,17},{13,21},{10,18},{14,22},{11,19},{15,23}} | collective-permute-start | bytes 393224 | tf_op jit(solution)/shard_map/ppermute | solution.py:282
  16.0 2.7 %collective-permute-start.2 = (bf16[4,128,128]{2,1,0:T(8,128)(2,1)S(1)}, bf16[4,128,128]{2,1,0:T(8,128)(2,1)S(1)}, u32[]{:S(2)}, u32[]{:S(2)}) collective-permute-start(bf16[4,128,128]{2,1,0:T(8,128)(2,1)S(1)} %shard_map.58), channel_id=1, source_target_pairs={{8,16},{12,20},{9,17},{13,21},{10,18},{14,22},{11,19},{15,23}} | collective-permute-start | bytes 393224 | tf_op jit(solution)/shard_map/ppermute | solution.py:282
  16.7 25.3 %collective-permute-start.9 = (bf16[1024,512]{1,0:T(8,128)(2,1)}, bf16[1024,512]{1,0:T(8,128)(2,1)}, u32[]{:S(2)}, u32[]{:S(2)}) collective-permute-start(bf16[1024,512]{1,0:T(8,128)(2,1)} %own_ref.1), channel_id=1, source_target_pairs={{0,4},{4,0},{8,12},{12,8},{16,20},{20,16},{24,28},{28,24},{1,5},{5... | collective-permute-start | bytes 3145736 | tf_op jit(solution)/shard_map/ppermute | solution.py:258
  18.0 1.4 %collective-permute-start.7 = (bf16[4,128,128]{2,1,0:T(8,128)(2,1)S(1)}, bf16[4,128,128]{2,1,0:T(8,128)(2,1)S(1)}, u32[]{:S(2)}, u32[]{:S(2)}) collective-permute-start(bf16[4,128,128]{2,1,0:T(8,128)(2,1)S(1)} %shard_map.63), channel_id=1, source_target_pairs={{16,24},{20,28},{17,25},{21,29},{18,26},{22,30},{19,27},{23,31}} | collective-permute-start | bytes 393224 | tf_op jit(solution)/shard_map/ppermute | solution.py:282
  18.8 0.7 collective-permute-start.3
  20.1 21.8 %collective-permute-start.8 = (bf16[256,1024]{1,0:T(8,128)(2,1)S(1)}, bf16[256,1024]{1,0:T(8,128)(2,1)S(1)}, u32[]{:S(2)}, u32[]{:S(2)}) collective-permute-start(bf16[256,1024]{1,0:T(8,128)(2,1)S(1)} %shard_map.64), channel_id=1, source_target_pairs={{0,8},{4,12},{8,0},{12,4},{16,24},{20,28},{24,16},{28,20},{1,9},{5... | collective-permute-start | bytes 1572872 | tf_op jit(solution)/shard_map/ppermute | solution.py:258
  23.3 21.1 %collective-permute-start.10 = (bf16[256,1024]{1,0:T(8,128)(2,1)S(1)}, bf16[256,1024]{1,0:T(8,128)(2,1)S(1)}, u32[]{:S(2)}, u32[]{:S(2)}) collective-permute-start(bf16[256,1024]{1,0:T(8,128)(2,1)S(1)} %shard_map.64), channel_id=1, source_target_pairs={{0,16},{1,17},{2,26},{3,27},{4,20},{5,21},{6,30},{7,31},{8,24},{9,... | collective-permute-start | bytes 1572872 | tf_op jit(solution)/shard_map/ppermute | solution.py:262
  45.2 11.4 %collective-permute-start.13 = (bf16[2,256,512]{2,1,0:T(8,128)(2,1)S(1)}, bf16[2,256,512]{2,1,0:T(8,128)(2,1)S(1)}, u32[]{:S(2)}, u32[]{:S(2)}) collective-permute-start(bf16[2,256,512]{2,1,0:T(8,128)(2,1)S(1)} %get-tuple-element.32), channel_id=1, source_target_pairs={{0,1},{1,0},{2,3},{3,2},{4,5},{5,4},{6,7},{7,6},{8,9},{9,8},{10,11... | collective-permute-start | bytes 1572872 | tf_op jit(solution)/shard_map/ppermute | solution.py:262
  55.0 13.5 %collective-permute-start.11 = (bf16[256,1024]{1,0:T(8,128)(2,1)S(1)}, bf16[256,1024]{1,0:T(8,128)(2,1)S(1)}, u32[]{:S(2)}, u32[]{:S(2)}) collective-permute-start(bf16[256,1024]{1,0:T(8,128)(2,1)S(1)} %collective-permute-done.10.heavy_ref), channel_id=1, source_target_pairs={{0,8},{4,12},{8,0},{12,4},{16,24},{20,28},{24,16},{28,20},{1,9},{5... | collective-permute-start | bytes 1572872 | tf_op jit(solution)/shard_map/ppermute | solution.py:258
  56.7 13.5 %collective-permute-start.14 = (bf16[2,256,512]{2,1,0:T(8,128)(2,1)S(1)}, bf16[2,256,512]{2,1,0:T(8,128)(2,1)S(1)}, u32[]{:S(2)}, u32[]{:S(2)}) collective-permute-start(bf16[2,256,512]{2,1,0:T(8,128)(2,1)S(1)} %add_convert_fusion.1), channel_id=1, source_target_pairs={{0,2},{1,3},{2,0},{3,1},{4,6},{5,7},{6,4},{7,5},{8,10},{9,11},{10,... | collective-permute-start | bytes 1572872 | tf_op jit(solution)/shard_map/ppermute | solution.py:262
  69.3 2.5 %collective-permute-start.12 = (bf16[2,256,512]{2,1,0:T(8,128)(2,1)S(1)}, bf16[2,256,512]{2,1,0:T(8,128)(2,1)S(1)}, u32[]{:S(2)}, u32[]{:S(2)}) collective-permute-start(bf16[2,256,512]{2,1,0:T(8,128)(2,1)S(1)} %get-tuple-element.29), channel_id=1, source_target_pairs={{0,1},{1,0},{2,3},{3,2},{4,5},{5,4},{6,7},{7,6},{8,9},{9,8},{10,11... | collective-permute-start | bytes 1572872 | tf_op jit(solution)/shard_map/ppermute | solution.py:262
  71.9 17.0 %collective-permute-start.15 = (bf16[2,256,512]{2,1,0:T(8,128)(2,1)S(1)}, bf16[2,256,512]{2,1,0:T(8,128)(2,1)S(1)}, u32[]{:S(2)}, u32[]{:S(2)}) collective-permute-start(bf16[2,256,512]{2,1,0:T(8,128)(2,1)S(1)} %add_convert_fusion), channel_id=1, source_target_pairs={{0,0},{1,24},{2,8},{3,16},{4,4},{5,28},{6,12},{7,20},{8,9},{9,17},... | collective-permute-start | bytes 1572872 | tf_op jit(solution)/shard_map/ppermute | solution.py:262

commit v28 on v27

--- a/solution.py
+++ b/solution.py
@@ -84,14 +84,15 @@
         out_ref[:, cols] = jnp.dot(scores, v_ref[:, cols], preferred_element_type=F32)
 
 
-def attend_kernel(parts, second_ref, q_ref, within_ref, gain_ref, *refs):
+def attend_kernel(counts, second_ref, q_ref, within_ref, gain_ref, *refs):
     *state_refs, out_ref = refs
     second = second_ref[0] == 1
-    each, heads = len(state_refs) // parts, q_ref.shape[1] // HD
+    heads, parts = q_ref.shape[1] // HD, len(counts)
     for head in range(heads):
         cols = head_slice(head)
         part, index = divmod(head, heads // parts)
-        mate_ref, *earlier_refs = state_refs[part * each : (part + 1) * each]
+        first = sum(counts[:part])
+        mate_ref, *earlier_refs = state_refs[first : first + counts[part]]
         state = jnp.where(second, mate_ref[index].astype(F32), 0.0)
         for earlier_ref in earlier_refs:
             state += earlier_ref[index].astype(F32)
@@ -129,7 +130,7 @@
     vmem = pl.BlockSpec(memory_space=pltpu.VMEM)
     flat = [state for part in states for state in part]
     return pl.pallas_call(
-        functools.partial(attend_kernel, len(states)),
+        functools.partial(attend_kernel, tuple(len(part) for part in states)),
         out_shape=jax.ShapeDtypeStruct((rows, features), BF16),
         in_specs=[pl.BlockSpec(memory_space=pltpu.SMEM)] + [vmem] * (3 + len(flat)),
         out_specs=vmem,
@@ -275,11 +276,16 @@
     states[0][0], within = lax.optimization_barrier((states[0][0], within))
     weight, _ = lax.optimization_barrier((out_weight, states[1][0]))
     mate_weight = swap(weight, 1)
+    ahead = parts - 1
+    for flip in (0, 1):
+        pairs = [(i, 2 + (i ^ flip)) for i in range(2)]
+        states[ahead].append(lax.ppermute(narrow[ahead], "seq", pairs))
     for plane in range(3):
         pairs = [(2 * plane + i, 2 * plane + 2 + i) for i in range(2)]
-        onward = [add(size, wide[part], *states[part]) for part in range(parts)]
-        for part in range(parts):
-            states[part].append(lax.ppermute(onward[part], "seq", pairs))
+        chosen = [part for part in range(parts) if plane or part != ahead]
+        onward = [add(size, wide[part], *states[part]) for part in chosen]
+        for part, value in zip(chosen, onward):
+            states[part].append(lax.ppermute(value, "seq", pairs))
     attended = attend(y, queries, within, norm_gain, states)
 
     mate_weight, _ = lax.optimization_barrier((mate_weight, attended))

time: 90.1 us -> 92.5 us (1.027)
  starting transfers between devices: 38.6 us -> 40.7 us
    ppermute x5, starting transfers between devices: 6.8 us -> 9.67 us  [swap(): return lax.ppermute(value, 'seq', [(s, s ^ mask) for s in range(8)])]
    ppermute x6 -> x7, waiting for transfers between devices: 2.22 us -> 1.98 us  [the longest x5 1.97 us: pairs_body(): states[part].append(lax.ppermute(value, 'seq', pairs))]
    ppermute x6 -> x7, starting transfers between devices: 8.54 us -> 8.47 us  [the longest x2 4.5 us: pairs_body(): states[ahead].append(lax.ppermute(narrow[ahead], 'seq', pairs))]
  transfers between devices with their start and end apart: 16 -> 17, of which waited for: 7 -> 7; matrix products, arithmetic and copies ran while one was open for 0% -> 0% of each run, Pallas kernels for 6% -> 6%
where the time goes in v28:
time: 92.5 us; the launch traced here: 92.2 us
  waiting for transfers between devices  41.7 us (45%)
  starting transfers between devices  40.7 us (44%)
  Pallas kernels  6.85 us (7%)
  local copies, waits for them, and re-layouts  1.4 us (2%)
  other arithmetic  1.32 us (1%)
    ppermute x5, waiting for transfers between devices, swap(): return lax.ppermute(value, 'seq', [(s, s ^ mask) for s in range(8)])  25 us
    ppermute x5, starting transfers between devices, move(): return lax.ppermute(value, both, pairs)  22.5 us
    ppermute x5, waiting for transfers between devices, move(): return lax.ppermute(value, both, pairs)  14.7 us
    ppermute x5, starting transfers between devices, swap(): return lax.ppermute(value, 'seq', [(s, s ^ mask) for s in range(8)])  9.67 us
    ppermute x2, starting transfers between devices, pairs_body(): states[ahead].append(lax.ppermute(narrow[ahead], 'seq', pairs))  4.5 us
    ppermute x5, starting transfers between devices, pairs_body(): states[part].append(lax.ppermute(value, 'seq', pairs))  3.97 us
    ppermute x5, waiting for transfers between devices, pairs_body(): states[part].append(lax.ppermute(value, 'seq', pairs))  1.97 us
  transfers between devices with their start and end apart: 17, of which 7 were waited for; matrix products, arithmetic and copies ran while one was open for 0% of the time, Pallas kernels for 6%

profile of v28, /device:TPU:1, one launch (start us, length us, event | category | flops | bytes accessed | tf_op | source)
XLA Modules:
  0.0 92.2 jit_solution(1527740556899255820)
XLA Ops:
  0.0 0.0 copy-start.1
  0.0 0.0 copy-start
  0.0 0.0 copy-start.2
  0.0 1.4 %fusion = (bf16[256,512]{1,0:T(8,128)(2,1)S(1)}, bf16[256,512]{1,0:T(8,128)(2,1)S(1)}, bf16[256,512]{1,0:T(8,128)(2,1)S(1)}, bf16[256,512]{1,0:T(8,128)(2,1)S(1)}) fusion(bf16[256,1024]{1,0:T(8,128)(2,1)} %v_ref.1, bf16[256,1024]{1,0:T(8,128)(2,1)} %k_ref.1), kind=kLoop, calls=%fused_computation.7 | loop fusion | bytes 2097152 | tf_op jit(solution)/shard_map/slice | solution.py:121
  1.4 0.3 shard_map.55
  1.7 2.1 %collective-permute-start = (bf16[4,128,128]{2,1,0:T(8,128)(2,1)S(1)}, bf16[4,128,128]{2,1,0:T(8,128)(2,1)S(1)}, u32[]{:S(2)}, u32[]{:S(2)}) collective-permute-start(bf16[4,128,128]{2,1,0:T(8,128)(2,1)S(1)} %get-tuple-element.19), channel_id=1, source_target_pairs={{0,4},{4,0},{8,12},{12,8},{16,20},{20,16},{24,28},{28,24},{1,5},{5... | collective-permute-start | bytes 393224 | tf_op jit(solution)/shard_map/ppermute | solution.py:259
  3.8 0.3 shard_map.60
  4.1 3.2 %collective-permute-start.6 = (bf16[4,128,128]{2,1,0:T(8,128)(2,1)S(1)}, bf16[4,128,128]{2,1,0:T(8,128)(2,1)S(1)}, u32[]{:S(2)}, u32[]{:S(2)}) collective-permute-start(bf16[4,128,128]{2,1,0:T(8,128)(2,1)S(1)} %get-tuple-element.23), channel_id=1, source_target_pairs={{0,12},{4,8},{1,13},{5,9},{2,14},{6,10},{3,15},{7,11}} | collective-permute-start | bytes 393224 | tf_op jit(solution)/shard_map/ppermute | solution.py:282
  7.2 1.3 %collective-permute-start.5 = (bf16[4,128,128]{2,1,0:T(8,128)(2,1)S(1)}, bf16[4,128,128]{2,1,0:T(8,128)(2,1)S(1)}, u32[]{:S(2)}, u32[]{:S(2)}) collective-permute-start(bf16[4,128,128]{2,1,0:T(8,128)(2,1)S(1)} %get-tuple-element.23), channel_id=1, source_target_pairs={{0,8},{4,12},{1,9},{5,13},{2,10},{6,14},{3,11},{7,15}} | collective-permute-start | bytes 393224 | tf_op jit(solution)/shard_map/ppermute | solution.py:282
  8.6 1.3 %collective-permute-start.4 = (bf16[4,128,128]{2,1,0:T(8,128)(2,1)S(1)}, bf16[4,128,128]{2,1,0:T(8,128)(2,1)S(1)}, u32[]{:S(2)}, u32[]{:S(2)}) collective-permute-start(bf16[4,128,128]{2,1,0:T(8,128)(2,1)S(1)} %get-tuple-element.23), channel_id=1, source_target_pairs={{0,4},{4,0},{8,12},{12,8},{16,20},{20,16},{24,28},{28,24},{1,5},{5... | collective-permute-start | bytes 393224 | tf_op jit(solution)/shard_map/ppermute | solution.py:259
  9.8 0.0 copy-done.1
  9.8 0.0 copy-done
  9.9 0.0 copy-done.2
  9.9 0.9 %shard_map.56.within_ref = f32[256,1024]{1,0:T(8,128)S(1)} custom-call(bf16[256,1024]{1,0:T(8,128)(2,1)S(1)} %copy-done.2, bf16[256,1024]{1,0:T(8,128)(2,1)S(1)} %copy-done, bf16[256,1024]{1,0:T(8,128)(2,1)S(1)} %copy-done.1), custom_call_target="tpu_custom_call" | custom-call | flops 268435456 | bytes 2621440 | tf_op jit(solution)/shard_map/pallas_call | solution.py:267
  10.8 0.0 copy-start.3
  10.8 0.0 collective-permute-done.refs_1_.refs_0_
  10.8 1.3 %collective-permute-start.1 = (bf16[4,128,128]{2,1,0:T(8,128)(2,1)S(1)}, bf16[4,128,128]{2,1,0:T(8,128)(2,1)S(1)}, u32[]{:S(2)}, u32[]{:S(2)}) collective-permute-start(bf16[4,128,128]{2,1,0:T(8,128)(2,1)S(1)} %shard_map.57), channel_id=1, source_target_pairs={{0,8},{4,12},{1,9},{5,13},{2,10},{6,14},{3,11},{7,15}} | collective-permute-start | bytes 393224 | tf_op jit(solution)/shard_map/ppermute | solution.py:288
  12.2 0.0 collective-permute-done.6.refs_3_.refs_6_
  12.2 0.0 collective-permute-done.5.refs_2_.refs_5_
  12.2 0.3 collective-permute-done.4.refs_1_.refs_4_
  12.5 0.1 shard_map.61
  12.5 0.7 collective-permute-start.7
  13.2 2.0 %collective-permute-done.1.refs_2_.refs_1_ = bf16[4,128,128]{2,1,0:T(8,128)(2,1)S(1)} collective-permute-done((bf16[4,128,128]{2,1,0:T(8,128)(2,1)S(1)}, bf16[4,128,128]{2,1,0:T(8,128)(2,1)S(1)}, u32[]{:S(2)}, u32[]{:S(2)}) %collective-permute-start.1) | collective-permute-done | bytes 131104 | tf_op jit(solution)/shard_map/ppermute | solution.py:288
  15.2 0.7 collective-permute-start.2
  15.9 0.9 collective-permute-start.10
  16.8 0.0 collective-permute-done.7.refs_4_.refs_7_
  16.8 0.1 shard_map.62
  16.9 0.7 collective-permute-start.8
  17.6 0.0 collective-permute-done.2.refs_3_.refs_2_
  17.6 0.1 shard_map.59
  17.6 0.7 collective-permute-start.3
  18.3 0.0 collective-permute-done.8.refs_8_
  18.3 0.0 collective-permute-done.3.refs_3_
  18.3 0.0 copy-done.3
  18.4 0.6 shard_map.63
  18.9 5.3 %collective-permute-start.9 = (bf16[256,1024]{1,0:T(8,128)(2,1)S(1)}, bf16[256,1024]{1,0:T(8,128)(2,1)S(1)}, u32[]{:S(2)}, u32[]{:S(2)}) collective-permute-start(bf16[256,1024]{1,0:T(8,128)(2,1)S(1)} %shard_map.63), channel_id=1, source_target_pairs={{0,8},{4,12},{8,0},{12,4},{16,24},{20,28},{24,16},{28,20},{1,9},{5... | collective-permute-start | bytes 1572872 | tf_op jit(solution)/shard_map/ppermute | solution.py:259
  24.2 8.2 %collective-permute-start.11 = (bf16[256,1024]{1,0:T(8,128)(2,1)S(1)}, bf16[256,1024]{1,0:T(8,128)(2,1)S(1)}, u32[]{:S(2)}, u32[]{:S(2)}) collective-permute-start(bf16[256,1024]{1,0:T(8,128)(2,1)S(1)} %shard_map.63), channel_id=1, source_target_pairs={{0,16},{1,17},{2,26},{3,27},{4,20},{5,21},{6,30},{7,31},{8,24},{9,... | collective-permute-start | bytes 1572872 | tf_op jit(solution)/shard_map/ppermute | solution.py:263
  32.4 13.9 %collective-permute-done.9 = bf16[256,1024]{1,0:T(8,128)(2,1)S(1)} collective-permute-done((bf16[256,1024]{1,0:T(8,128)(2,1)S(1)}, bf16[256,1024]{1,0:T(8,128)(2,1)S(1)}, u32[]{:S(2)}, u32[]{:S(2)}) %collective-permute-start.9) | collective-permute-done | bytes 524320 | tf_op jit(solution)/shard_map/ppermute | solution.py:259
  46.3 0.1 broadcast_select_fusion.1
  46.4 0.0 collective-permute-done.10.mate_ref
  46.4 1.7 %shard_map.64.weight_ref = bf16[2,1024,512]{2,1,0:T(8,128)(2,1)S(1)} custom-call(bf16[1024,512]{1,0:T(8,128)(2,1)} %own_ref.1, bf16[1024,512]{1,0:T(8,128)(2,1)} %collective-permute-done.10.mate_ref), custom_call_target="tpu_custom_call" | custom-call | bytes 4194304 | tf_op jit(solution)/shard_map/pallas_call | solution.py:292
  48.1 0.7 shard_map.66.light_ref
  48.8 0.0 collective-permute-done.11.heavy_ref
  48.8 0.7 shard_map.68
  49.6 7.8 %collective-permute-start.14 = (bf16[2,256,512]{2,1,0:T(8,128)(2,1)S(1)}, bf16[2,256,512]{2,1,0:T(8,128)(2,1)S(1)}, u32[]{:S(2)}, u32[]{:S(2)}) collective-permute-start(bf16[2,256,512]{2,1,0:T(8,128)(2,1)S(1)} %get-tuple-element.32), channel_id=1, source_target_pairs={{0,1},{1,0},{2,3},{3,2},{4,5},{5,4},{6,7},{7,6},{8,9},{9,8},{10,11... | collective-permute-start | bytes 1572872 | tf_op jit(solution)/shard_map/ppermute | solution.py:263
  57.4 0.1 collective-permute-start.12
  57.4 0.7 shard_map.65.light_ref
  58.2 0.8 collective-permute-done.14
  58.9 0.1 add_convert_fusion.1
  59.0 1.1 %collective-permute-start.15 = (bf16[2,256,512]{2,1,0:T(8,128)(2,1)S(1)}, bf16[2,256,512]{2,1,0:T(8,128)(2,1)S(1)}, u32[]{:S(2)}, u32[]{:S(2)}) collective-permute-start(bf16[2,256,512]{2,1,0:T(8,128)(2,1)S(1)} %add_convert_fusion.1), channel_id=1, source_target_pairs={{0,2},{1,3},{2,0},{3,1},{4,6},{5,7},{6,4},{7,5},{8,10},{9,11},{10,... | collective-permute-start | bytes 1572872 | tf_op jit(solution)/shard_map/ppermute | solution.py:263
  60.1 10.8 %collective-permute-done.12.heavy_ref = bf16[256,1024]{1,0:T(8,128)(2,1)S(1)} collective-permute-done((bf16[256,1024]{1,0:T(8,128)(2,1)S(1)}, bf16[256,1024]{1,0:T(8,128)(2,1)S(1)}, u32[]{:S(2)}, u32[]{:S(2)}) %collective-permute-start.12) | collective-permute-done | bytes 524320 | tf_op jit(solution)/shard_map/ppermute | solution.py:259
  70.9 0.7 shard_map.67
  71.6 0.9 %collective-permute-start.13 = (bf16[2,256,512]{2,1,0:T(8,128)(2,1)S(1)}, bf16[2,256,512]{2,1,0:T(8,128)(2,1)S(1)}, u32[]{:S(2)}, u32[]{:S(2)}) collective-permute-start(bf16[2,256,512]{2,1,0:T(8,128)(2,1)S(1)} %get-tuple-element.29), channel_id=1, source_target_pairs={{0,1},{1,0},{2,3},{3,2},{4,5},{5,4},{6,7},{7,6},{8,9},{9,8},{10,11... | collective-permute-start | bytes 1572872 | tf_op jit(solution)/shard_map/ppermute | solution.py:263
  72.5 0.0 collective-permute-done.15
  72.5 1.5 %collective-permute-done.13 = bf16[2,256,512]{2,1,0:T(8,128)(2,1)S(1)} collective-permute-done((bf16[2,256,512]{2,1,0:T(8,128)(2,1)S(1)}, bf16[2,256,512]{2,1,0:T(8,128)(2,1)S(1)}, u32[]{:S(2)}, u32[]{:S(2)}) %collective-permute-start.13) | collective-permute-done | bytes 524320 | tf_op jit(solution)/shard_map/ppermute | solution.py:263
  74.1 0.2 add_convert_fusion
  74.3 4.6 %collective-permute-start.16 = (bf16[2,256,512]{2,1,0:T(8,128)(2,1)S(1)}, bf16[2,256,512]{2,1,0:T(8,128)(2,1)S(1)}, u32[]{:S(2)}, u32[]{:S(2)}) collective-permute-start(bf16[2,256,512]{2,1,0:T(8,128)(2,1)S(1)} %add_convert_fusion), channel_id=1, source_target_pairs={{0,0},{1,24},{2,8},{3,16},{4,4},{5,28},{6,12},{7,20},{8,9},{9,17},... | collective-permute-start | bytes 1572872 | tf_op jit(solution)/shard_map/ppermute | solution.py:263
  78.9 12.4 %collective-permute-done.16 = bf16[2,256,512]{2,1,0:T(8,128)(2,1)S(1)} collective-permute-done((bf16[2,256,512]{2,1,0:T(8,128)(2,1)S(1)}, bf16[2,256,512]{2,1,0:T(8,128)(2,1)S(1)}, u32[]{:S(2)}, u32[]{:S(2)}) %collective-permute-start.16) | collective-permute-done | bytes 524320 | tf_op jit(solution)/shard_map/ppermute | solution.py:263
  91.3 0.9 pad_maximum_fusion
  (3 shorter events, 0.1 us)
Async XLA Ops:
  0.0 9.8 %copy-start.1 = (bf16[256,1024]{1,0:T(8,128)(2,1)S(1)}, bf16[256,1024]{1,0:T(8,128)(2,1)}, u32[]{:S(2)}) copy-start(bf16[256,1024]{1,0:T(8,128)(2,1)} %v_ref.1) | copy-start | bytes 1572868
  0.0 9.8 %copy-start = (bf16[256,1024]{1,0:T(8,128)(2,1)S(1)}, bf16[256,1024]{1,0:T(8,128)(2,1)}, u32[]{:S(2)}) copy-start(bf16[256,1024]{1,0:T(8,128)(2,1)} %k_ref.1) | copy-start | bytes 1572868
  0.0 9.8 %copy-start.2 = (bf16[256,1024]{1,0:T(8,128)(2,1)S(1)}, bf16[256,1024]{1,0:T(8,128)(2,1)}, u32[]{:S(2)}) copy-start(bf16[256,1024]{1,0:T(8,128)(2,1)} %q_ref.3) | copy-start | bytes 1572868
  1.7 9.1 %collective-permute-start = (bf16[4,128,128]{2,1,0:T(8,128)(2,1)S(1)}, bf16[4,128,128]{2,1,0:T(8,128)(2,1)S(1)}, u32[]{:S(2)}, u32[]{:S(2)}) collective-permute-start(bf16[4,128,128]{2,1,0:T(8,128)(2,1)S(1)} %get-tuple-element.19), channel_id=1, source_target_pairs={{0,4},{4,0},{8,12},{12,8},{16,20},{20,16},{24,28},{28,24},{1,5},{5... | collective-permute-start | bytes 393224 | tf_op jit(solution)/shard_map/ppermute | solution.py:259
  4.1 8.1 %collective-permute-start.6 = (bf16[4,128,128]{2,1,0:T(8,128)(2,1)S(1)}, bf16[4,128,128]{2,1,0:T(8,128)(2,1)S(1)}, u32[]{:S(2)}, u32[]{:S(2)}) collective-permute-start(bf16[4,128,128]{2,1,0:T(8,128)(2,1)S(1)} %get-tuple-element.23), channel_id=1, source_target_pairs={{0,12},{4,8},{1,13},{5,9},{2,14},{6,10},{3,15},{7,11}} | collective-permute-start | bytes 393224 | tf_op jit(solution)/shard_map/ppermute | solution.py:282
  7.2 4.9 %collective-permute-start.5 = (bf16[4,128,128]{2,1,0:T(8,128)(2,1)S(1)}, bf16[4,128,128]{2,1,0:T(8,128)(2,1)S(1)}, u32[]{:S(2)}, u32[]{:S(2)}) collective-permute-start(bf16[4,128,128]{2,1,0:T(8,128)(2,1)S(1)} %get-tuple-element.23), channel_id=1, source_target_pairs={{0,8},{4,12},{1,9},{5,13},{2,10},{6,14},{3,11},{7,15}} | collective-permute-start | bytes 393224 | tf_op jit(solution)/shard_map/ppermute | solution.py:282
  8.6 3.9 %collective-permute-start.4 = (bf16[4,128,128]{2,1,0:T(8,128)(2,1)S(1)}, bf16[4,128,128]{2,1,0:T(8,128)(2,1)S(1)}, u32[]{:S(2)}, u32[]{:S(2)}) collective-permute-start(bf16[4,128,128]{2,1,0:T(8,128)(2,1)S(1)} %get-tuple-element.23), channel_id=1, source_target_pairs={{0,4},{4,0},{8,12},{12,8},{16,20},{20,16},{24,28},{28,24},{1,5},{5... | collective-permute-start | bytes 393224 | tf_op jit(solution)/shard_map/ppermute | solution.py:259
  10.8 7.6 %copy-start.3 = (f32[1024]{0:T(1024)S(1)}, f32[1024]{0:T(1024)}, u32[]{:S(2)}) copy-start(f32[1024]{0:T(1024)} %param.8) | copy-start | bytes 12292
  10.8 4.3 %collective-permute-start.1 = (bf16[4,128,128]{2,1,0:T(8,128)(2,1)S(1)}, bf16[4,128,128]{2,1,0:T(8,128)(2,1)S(1)}, u32[]{:S(2)}, u32[]{:S(2)}) collective-permute-start(bf16[4,128,128]{2,1,0:T(8,128)(2,1)S(1)} %shard_map.57), channel_id=1, source_target_pairs={{0,8},{4,12},{1,9},{5,13},{2,10},{6,14},{3,11},{7,15}} | collective-permute-start | bytes 393224 | tf_op jit(solution)/shard_map/ppermute | solution.py:288
  12.5 4.3 %collective-permute-start.7 = (bf16[4,128,128]{2,1,0:T(8,128)(2,1)S(1)}, bf16[4,128,128]{2,1,0:T(8,128)(2,1)S(1)}, u32[]{:S(2)}, u32[]{:S(2)}) collective-permute-start(bf16[4,128,128]{2,1,0:T(8,128)(2,1)S(1)} %shard_map.61), channel_id=1, source_target_pairs={{8,16},{12,20},{9,17},{13,21},{10,18},{14,22},{11,19},{15,23}} | collective-permute-start | bytes 393224 | tf_op jit(solution)/shard_map/ppermute | solution.py:288
  15.2 2.3 %collective-permute-start.2 = (bf16[4,128,128]{2,1,0:T(8,128)(2,1)S(1)}, bf16[4,128,128]{2,1,0:T(8,128)(2,1)S(1)}, u32[]{:S(2)}, u32[]{:S(2)}) collective-permute-start(bf16[4,128,128]{2,1,0:T(8,128)(2,1)S(1)} %shard_map.58), channel_id=1, source_target_pairs={{8,16},{12,20},{9,17},{13,21},{10,18},{14,22},{11,19},{15,23}} | collective-permute-start | bytes 393224 | tf_op jit(solution)/shard_map/ppermute | solution.py:288
  15.9 30.5 %collective-permute-start.10 = (bf16[1024,512]{1,0:T(8,128)(2,1)}, bf16[1024,512]{1,0:T(8,128)(2,1)}, u32[]{:S(2)}, u32[]{:S(2)}) collective-permute-start(bf16[1024,512]{1,0:T(8,128)(2,1)} %own_ref.1), channel_id=1, source_target_pairs={{0,4},{4,0},{8,12},{12,8},{16,20},{20,16},{24,28},{28,24},{1,5},{5... | collective-permute-start | bytes 3145736 | tf_op jit(solution)/shard_map/ppermute | solution.py:259
  16.9 1.4 %collective-permute-start.8 = (bf16[4,128,128]{2,1,0:T(8,128)(2,1)S(1)}, bf16[4,128,128]{2,1,0:T(8,128)(2,1)S(1)}, u32[]{:S(2)}, u32[]{:S(2)}) collective-permute-start(bf16[4,128,128]{2,1,0:T(8,128)(2,1)S(1)} %shard_map.62), channel_id=1, source_target_pairs={{16,24},{20,28},{17,25},{21,29},{18,26},{22,30},{19,27},{23,31}} | collective-permute-start | bytes 393224 | tf_op jit(solution)/shard_map/ppermute | solution.py:288
  17.6 0.7 collective-permute-start.3
  18.9 27.4 %collective-permute-start.9 = (bf16[256,1024]{1,0:T(8,128)(2,1)S(1)}, bf16[256,1024]{1,0:T(8,128)(2,1)S(1)}, u32[]{:S(2)}, u32[]{:S(2)}) collective-permute-start(bf16[256,1024]{1,0:T(8,128)(2,1)S(1)} %shard_map.63), channel_id=1, source_target_pairs={{0,8},{4,12},{8,0},{12,4},{16,24},{20,28},{24,16},{28,20},{1,9},{5... | collective-permute-start | bytes 1572872 | tf_op jit(solution)/shard_map/ppermute | solution.py:259
  24.2 24.6 %collective-permute-start.11 = (bf16[256,1024]{1,0:T(8,128)(2,1)S(1)}, bf16[256,1024]{1,0:T(8,128)(2,1)S(1)}, u32[]{:S(2)}, u32[]{:S(2)}) collective-permute-start(bf16[256,1024]{1,0:T(8,128)(2,1)S(1)} %shard_map.63), channel_id=1, source_target_pairs={{0,16},{1,17},{2,26},{3,27},{4,20},{5,21},{6,30},{7,31},{8,24},{9,... | collective-permute-start | bytes 1572872 | tf_op jit(solution)/shard_map/ppermute | solution.py:263
  49.6 9.3 %collective-permute-start.14 = (bf16[2,256,512]{2,1,0:T(8,128)(2,1)S(1)}, bf16[2,256,512]{2,1,0:T(8,128)(2,1)S(1)}, u32[]{:S(2)}, u32[]{:S(2)}) collective-permute-start(bf16[2,256,512]{2,1,0:T(8,128)(2,1)S(1)} %get-tuple-element.32), channel_id=1, source_target_pairs={{0,1},{1,0},{2,3},{3,2},{4,5},{5,4},{6,7},{7,6},{8,9},{9,8},{10,11... | collective-permute-start | bytes 1572872 | tf_op jit(solution)/shard_map/ppermute | solution.py:263
  57.4 13.5 %collective-permute-start.12 = (bf16[256,1024]{1,0:T(8,128)(2,1)S(1)}, bf16[256,1024]{1,0:T(8,128)(2,1)S(1)}, u32[]{:S(2)}, u32[]{:S(2)}) collective-permute-start(bf16[256,1024]{1,0:T(8,128)(2,1)S(1)} %collective-permute-done.11.heavy_ref), channel_id=1, source_target_pairs={{0,8},{4,12},{8,0},{12,4},{16,24},{20,28},{24,16},{28,20},{1,9},{5... | collective-permute-start | bytes 1572872 | tf_op jit(solution)/shard_map/ppermute | solution.py:259
  59.0 13.5 %collective-permute-start.15 = (bf16[2,256,512]{2,1,0:T(8,128)(2,1)S(1)}, bf16[2,256,512]{2,1,0:T(8,128)(2,1)S(1)}, u32[]{:S(2)}, u32[]{:S(2)}) collective-permute-start(bf16[2,256,512]{2,1,0:T(8,128)(2,1)S(1)} %add_convert_fusion.1), channel_id=1, source_target_pairs={{0,2},{1,3},{2,0},{3,1},{4,6},{5,7},{6,4},{7,5},{8,10},{9,11},{10,... | collective-permute-start | bytes 1572872 | tf_op jit(solution)/shard_map/ppermute | solution.py:263
  71.6 2.5 %collective-permute-start.13 = (bf16[2,256,512]{2,1,0:T(8,128)(2,1)S(1)}, bf16[2,256,512]{2,1,0:T(8,128)(2,1)S(1)}, u32[]{:S(2)}, u32[]{:S(2)}) collective-permute-start(bf16[2,256,512]{2,1,0:T(8,128)(2,1)S(1)} %get-tuple-element.29), channel_id=1, source_target_pairs={{0,1},{1,0},{2,3},{3,2},{4,5},{5,4},{6,7},{7,6},{8,9},{9,8},{10,11... | collective-permute-start | bytes 1572872 | tf_op jit(solution)/shard_map/ppermute | solution.py:263
  74.3 17.0 %collective-permute-start.16 = (bf16[2,256,512]{2,1,0:T(8,128)(2,1)S(1)}, bf16[2,256,512]{2,1,0:T(8,128)(2,1)S(1)}, u32[]{:S(2)}, u32[]{:S(2)}) collective-permute-start(bf16[2,256,512]{2,1,0:T(8,128)(2,1)S(1)} %add_convert_fusion), channel_id=1, source_target_pairs={{0,0},{1,24},{2,8},{3,16},{4,4},{5,28},{6,12},{7,20},{8,9},{9,17},... | collective-permute-start | bytes 1572872 | tf_op jit(solution)/shard_map/ppermute | solution.py:263

commit v29 on v27

--- a/solution.py
+++ b/solution.py
@@ -287,7 +287,7 @@
         join_kernel, jax.ShapeDtypeStruct((2,) + out_weight.shape, BF16), 0, 8 * out_weight.size
     )(out_weight, mate_weight)
 
-    straight = move(attended, lambda z, y, x, c: (z ^ (2 + x), y, x, c))
+    straight = move(attended, lambda z, y, x, c: (z ^ (3 - x), y, x, c))
     beside = swap(attended, 2)
 
     tile = jax.ShapeDtypeStruct((2, rows, half_cols), BF16)
@@ -317,7 +317,7 @@
     crossed = move(far, lambda z, y, x, c: (z, y, 1 - x, c))
     near_light = product(jnp.where(x == 0, attended, beside))
     near = projected(near_light, onward) + crossed.astype(F32)
-    result = move(near.astype(BF16), lambda z, y, x, c: (z ^ 3 * c ^ x, y, z // 2, z % 2))
+    result = move(near.astype(BF16), lambda z, y, x, c: (z ^ (2 * c + x), y, z // 2, z % 2))
     first = jnp.where(y == 0, result[0], result[1])
     return jnp.concatenate([first, jnp.where(y == 0, result[1], result[0])], axis=1)
 

time: 90.1 us -> 90 us (level); the launches traced: 89.9 us -> 88.2 us
  starting transfers between devices: 38.6 us -> 33.5 us
  waiting for transfers between devices: 41.4 us -> 45 us
    ppermute x5, waiting for transfers between devices: 14.7 us -> 20.9 us  [move(): return lax.ppermute(value, both, pairs)]
    ppermute x5, starting transfers between devices: 23.2 us -> 17.7 us  [move(): return lax.ppermute(value, both, pairs)]
    ppermute x5, waiting for transfers between devices: 24.5 us -> 21.8 us  [swap(): return lax.ppermute(value, 'seq', [(s, s ^ mask) for s in range(8)])]
  transfers between devices with their start and end apart: 16 -> 16, of which waited for: 7 -> 9; matrix products, arithmetic and copies ran while one was open for 0% -> 0% of each run, Pallas kernels for 6% -> 7%
where the time goes in v29:
time: 90 us; the launch traced here: 88.2 us
  waiting for transfers between devices  45 us (50%)
  starting transfers between devices  33.5 us (37%)
  Pallas kernels  6.82 us (8%)
  local copies, waits for them, and re-layouts  1.41 us (2%)
  other arithmetic  1.32 us (1%)
    ppermute x5, waiting for transfers between devices, swap(): return lax.ppermute(value, 'seq', [(s, s ^ mask) for s in range(8)])  21.8 us
    ppermute x5, waiting for transfers between devices, move(): return lax.ppermute(value, both, pairs)  20.9 us
    ppermute x5, starting transfers between devices, move(): return lax.ppermute(value, both, pairs)  17.7 us
    ppermute x6, starting transfers between devices, pairs_body(): states[part].append(lax.ppermute(onward[part], 'seq', pairs))  8.54 us
    ppermute x5, starting transfers between devices, swap(): return lax.ppermute(value, 'seq', [(s, s ^ mask) for s in range(8)])  7.2 us
    ppermute x6, waiting for transfers between devices, pairs_body(): states[part].append(lax.ppermute(onward[part], 'seq', pairs))  2.22 us
  transfers between devices with their start and end apart: 16, of which 9 were waited for; matrix products, arithmetic and copies ran while one was open for 0% of the time, Pallas kernels for 7%

profile of v29, /device:TPU:1, one launch (start us, length us, event | category | flops | bytes accessed | tf_op | source)
XLA Modules:
  0.0 88.2 jit_solution(15888536801234250273)
XLA Ops:
  0.0 0.0 copy-start.1
  0.0 0.0 copy-start
  0.0 0.0 copy-start.2
  0.0 1.4 %fusion = (bf16[256,512]{1,0:T(8,128)(2,1)S(1)}, bf16[256,512]{1,0:T(8,128)(2,1)S(1)}, bf16[256,512]{1,0:T(8,128)(2,1)S(1)}, bf16[256,512]{1,0:T(8,128)(2,1)S(1)}) fusion(bf16[256,1024]{1,0:T(8,128)(2,1)} %v_ref.1, bf16[256,1024]{1,0:T(8,128)(2,1)} %k_ref.1), kind=kLoop, calls=%fused_computation.7 | loop fusion | bytes 2097152 | tf_op jit(solution)/shard_map/slice | solution.py:120
  1.4 0.3 shard_map.60
  1.7 2.1 %collective-permute-start.4 = (bf16[4,128,128]{2,1,0:T(8,128)(2,1)S(1)}, bf16[4,128,128]{2,1,0:T(8,128)(2,1)S(1)}, u32[]{:S(2)}, u32[]{:S(2)}) collective-permute-start(bf16[4,128,128]{2,1,0:T(8,128)(2,1)S(1)} %get-tuple-element.23), channel_id=1, source_target_pairs={{0,4},{4,0},{8,12},{12,8},{16,20},{20,16},{24,28},{28,24},{1,5},{5... | collective-permute-start | bytes 393224 | tf_op jit(solution)/shard_map/ppermute | solution.py:258
  3.8 0.3 shard_map.55
  4.1 0.1 collective-permute-start
  4.2 0.0 copy-done.1
  4.2 0.0 copy-done
  4.2 0.0 copy-done.2
  4.2 0.9 %shard_map.56.within_ref = f32[256,1024]{1,0:T(8,128)S(1)} custom-call(bf16[256,1024]{1,0:T(8,128)(2,1)S(1)} %copy-done.2, bf16[256,1024]{1,0:T(8,128)(2,1)S(1)} %copy-done, bf16[256,1024]{1,0:T(8,128)(2,1)S(1)} %copy-done.1), custom_call_target="tpu_custom_call" | custom-call | flops 268435456 | bytes 2621440 | tf_op jit(solution)/shard_map/pallas_call | solution.py:266
  5.1 0.0 copy-start.3
  5.1 1.9 %collective-permute-done.4.refs_1_.refs_4_ = bf16[4,128,128]{2,1,0:T(8,128)(2,1)S(1)} collective-permute-done((bf16[4,128,128]{2,1,0:T(8,128)(2,1)S(1)}, bf16[4,128,128]{2,1,0:T(8,128)(2,1)S(1)}, u32[]{:S(2)}, u32[]{:S(2)}) %collective-permute-start.4) | collective-permute-done | bytes 131104 | tf_op jit(solution)/shard_map/ppermute | solution.py:258
  7.1 3.1 %collective-permute-start.5 = (bf16[4,128,128]{2,1,0:T(8,128)(2,1)S(1)}, bf16[4,128,128]{2,1,0:T(8,128)(2,1)S(1)}, u32[]{:S(2)}, u32[]{:S(2)}) collective-permute-start(bf16[4,128,128]{2,1,0:T(8,128)(2,1)S(1)} %shard_map.61), channel_id=1, source_target_pairs={{0,8},{4,12},{1,9},{5,13},{2,10},{6,14},{3,11},{7,15}} | collective-permute-start | bytes 393224 | tf_op jit(solution)/shard_map/ppermute | solution.py:282
  10.2 0.0 collective-permute-done.refs_1_.refs_0_
  10.2 2.8 %collective-permute-start.1 = (bf16[4,128,128]{2,1,0:T(8,128)(2,1)S(1)}, bf16[4,128,128]{2,1,0:T(8,128)(2,1)S(1)}, u32[]{:S(2)}, u32[]{:S(2)}) collective-permute-start(bf16[4,128,128]{2,1,0:T(8,128)(2,1)S(1)} %shard_map.57), channel_id=1, source_target_pairs={{0,8},{4,12},{1,9},{5,13},{2,10},{6,14},{3,11},{7,15}} | collective-permute-start | bytes 393224 | tf_op jit(solution)/shard_map/ppermute | solution.py:282
  13.0 0.0 collective-permute-done.5.refs_2_.refs_5_
  13.1 0.7 collective-permute-start.6
  13.7 2.2 %collective-permute-done.1.refs_2_.refs_1_ = bf16[4,128,128]{2,1,0:T(8,128)(2,1)S(1)} collective-permute-done((bf16[4,128,128]{2,1,0:T(8,128)(2,1)S(1)}, bf16[4,128,128]{2,1,0:T(8,128)(2,1)S(1)}, u32[]{:S(2)}, u32[]{:S(2)}) %collective-permute-start.1) | collective-permute-done | bytes 131104 | tf_op jit(solution)/shard_map/ppermute | solution.py:282
  16.0 0.7 collective-permute-start.2
  16.7 1.3 %collective-permute-start.9 = (bf16[1024,512]{1,0:T(8,128)(2,1)}, bf16[1024,512]{1,0:T(8,128)(2,1)}, u32[]{:S(2)}, u32[]{:S(2)}) collective-permute-start(bf16[1024,512]{1,0:T(8,128)(2,1)} %own_ref.1), channel_id=1, source_target_pairs={{0,4},{4,0},{8,12},{12,8},{16,20},{20,16},{24,28},{28,24},{1,5},{5... | collective-permute-start | bytes 3145736 | tf_op jit(solution)/shard_map/ppermute | solution.py:258
  18.0 0.0 collective-permute-done.6.refs_3_.refs_6_
  18.0 0.1 shard_map.63
  18.0 0.7 collective-permute-start.7
  18.7 0.0 collective-permute-done.2.refs_3_.refs_2_
  18.7 0.1 shard_map.59
  18.8 0.7 collective-permute-start.3
  19.5 0.0 collective-permute-done.7.refs_7_
  19.5 0.0 collective-permute-done.3.refs_3_
  19.5 0.0 copy-done.3
  19.5 0.5 shard_map.64
  20.1 3.2 %collective-permute-start.8 = (bf16[256,1024]{1,0:T(8,128)(2,1)S(1)}, bf16[256,1024]{1,0:T(8,128)(2,1)S(1)}, u32[]{:S(2)}, u32[]{:S(2)}) collective-permute-start(bf16[256,1024]{1,0:T(8,128)(2,1)S(1)} %shard_map.64), channel_id=1, source_target_pairs={{0,8},{4,12},{8,0},{12,4},{16,24},{20,28},{24,16},{28,20},{1,9},{5... | collective-permute-start | bytes 1572872 | tf_op jit(solution)/shard_map/ppermute | solution.py:258
  23.3 6.6 %collective-permute-start.10 = (bf16[256,1024]{1,0:T(8,128)(2,1)S(1)}, bf16[256,1024]{1,0:T(8,128)(2,1)S(1)}, u32[]{:S(2)}, u32[]{:S(2)}) collective-permute-start(bf16[256,1024]{1,0:T(8,128)(2,1)S(1)} %shard_map.64), channel_id=1, source_target_pairs={{0,24},{1,25},{2,18},{3,19},{4,28},{5,29},{6,22},{7,23},{8,16},{9,... | collective-permute-start | bytes 1572872 | tf_op jit(solution)/shard_map/ppermute | solution.py:262
  29.9 3.0 %collective-permute-done.8 = bf16[256,1024]{1,0:T(8,128)(2,1)S(1)} collective-permute-done((bf16[256,1024]{1,0:T(8,128)(2,1)S(1)}, bf16[256,1024]{1,0:T(8,128)(2,1)S(1)}, u32[]{:S(2)}, u32[]{:S(2)}) %collective-permute-start.8) | collective-permute-done | bytes 524320 | tf_op jit(solution)/shard_map/ppermute | solution.py:258
  32.9 0.1 broadcast_select_fusion.1
  33.0 6.6 %collective-permute-done.9.mate_ref = bf16[1024,512]{1,0:T(8,128)(2,1)} collective-permute-done((bf16[1024,512]{1,0:T(8,128)(2,1)}, bf16[1024,512]{1,0:T(8,128)(2,1)}, u32[]{:S(2)}, u32[]{:S(2)}) %collective-permute-start.9) | collective-permute-done | bytes 1048608 | tf_op jit(solution)/shard_map/ppermute | solution.py:258
  39.6 1.7 %shard_map.65.weight_ref = bf16[2,1024,512]{2,1,0:T(8,128)(2,1)S(1)} custom-call(bf16[1024,512]{1,0:T(8,128)(2,1)} %own_ref.1, bf16[1024,512]{1,0:T(8,128)(2,1)} %collective-permute-done.9.mate_ref), custom_call_target="tpu_custom_call" | custom-call | bytes 4194304 | tf_op jit(solution)/shard_map/pallas_call | solution.py:286
  41.2 0.7 shard_map.67.light_ref
  42.0 8.2 %collective-permute-done.10.heavy_ref = bf16[256,1024]{1,0:T(8,128)(2,1)S(1)} collective-permute-done((bf16[256,1024]{1,0:T(8,128)(2,1)S(1)}, bf16[256,1024]{1,0:T(8,128)(2,1)S(1)}, u32[]{:S(2)}, u32[]{:S(2)}) %collective-permute-start.10) | collective-permute-done | bytes 524320 | tf_op jit(solution)/shard_map/ppermute | solution.py:262
  50.2 0.7 shard_map.69
  50.9 3.9 %collective-permute-start.13 = (bf16[2,256,512]{2,1,0:T(8,128)(2,1)S(1)}, bf16[2,256,512]{2,1,0:T(8,128)(2,1)S(1)}, u32[]{:S(2)}, u32[]{:S(2)}) collective-permute-start(bf16[2,256,512]{2,1,0:T(8,128)(2,1)S(1)} %get-tuple-element.32), channel_id=1, source_target_pairs={{0,1},{1,0},{2,3},{3,2},{4,5},{5,4},{6,7},{7,6},{8,9},{9,8},{10,11... | collective-permute-start | bytes 1572872 | tf_op jit(solution)/shard_map/ppermute | solution.py:262
  54.8 0.5 collective-permute-start.11
  55.3 0.7 shard_map.66.light_ref
  56.0 0.4 collective-permute-done.13
  56.4 0.1 add_convert_fusion.1
  56.5 1.5 %collective-permute-start.14 = (bf16[2,256,512]{2,1,0:T(8,128)(2,1)S(1)}, bf16[2,256,512]{2,1,0:T(8,128)(2,1)S(1)}, u32[]{:S(2)}, u32[]{:S(2)}) collective-permute-start(bf16[2,256,512]{2,1,0:T(8,128)(2,1)S(1)} %add_convert_fusion.1), channel_id=1, source_target_pairs={{0,2},{1,3},{2,0},{3,1},{4,6},{5,7},{6,4},{7,5},{8,10},{9,11},{10,... | collective-permute-start | bytes 1572872 | tf_op jit(solution)/shard_map/ppermute | solution.py:262
  58.0 10.3 %collective-permute-done.11.heavy_ref = bf16[256,1024]{1,0:T(8,128)(2,1)S(1)} collective-permute-done((bf16[256,1024]{1,0:T(8,128)(2,1)S(1)}, bf16[256,1024]{1,0:T(8,128)(2,1)S(1)}, u32[]{:S(2)}, u32[]{:S(2)}) %collective-permute-start.11) | collective-permute-done | bytes 524320 | tf_op jit(solution)/shard_map/ppermute | solution.py:258
  68.3 0.7 shard_map.68
  69.0 0.9 %collective-permute-start.12 = (bf16[2,256,512]{2,1,0:T(8,128)(2,1)S(1)}, bf16[2,256,512]{2,1,0:T(8,128)(2,1)S(1)}, u32[]{:S(2)}, u32[]{:S(2)}) collective-permute-start(bf16[2,256,512]{2,1,0:T(8,128)(2,1)S(1)} %get-tuple-element.29), channel_id=1, source_target_pairs={{0,1},{1,0},{2,3},{3,2},{4,5},{5,4},{6,7},{7,6},{8,9},{9,8},{10,11... | collective-permute-start | bytes 1572872 | tf_op jit(solution)/shard_map/ppermute | solution.py:262
  70.0 0.0 collective-permute-done.14
  70.0 1.5 %collective-permute-done.12 = bf16[2,256,512]{2,1,0:T(8,128)(2,1)S(1)} collective-permute-done((bf16[2,256,512]{2,1,0:T(8,128)(2,1)S(1)}, bf16[2,256,512]{2,1,0:T(8,128)(2,1)S(1)}, u32[]{:S(2)}, u32[]{:S(2)}) %collective-permute-start.12) | collective-permute-done | bytes 524320 | tf_op jit(solution)/shard_map/ppermute | solution.py:262
  71.5 0.2 add_convert_fusion
  71.7 4.8 %collective-permute-start.15 = (bf16[2,256,512]{2,1,0:T(8,128)(2,1)S(1)}, bf16[2,256,512]{2,1,0:T(8,128)(2,1)S(1)}, u32[]{:S(2)}, u32[]{:S(2)}) collective-permute-start(bf16[2,256,512]{2,1,0:T(8,128)(2,1)S(1)} %add_convert_fusion), channel_id=1, source_target_pairs={{0,0},{1,16},{2,8},{3,24},{4,4},{5,20},{6,12},{7,28},{8,9},{9,25},... | collective-permute-start | bytes 1572872 | tf_op jit(solution)/shard_map/ppermute | solution.py:262
  76.6 10.8 %collective-permute-done.15 = bf16[2,256,512]{2,1,0:T(8,128)(2,1)S(1)} collective-permute-done((bf16[2,256,512]{2,1,0:T(8,128)(2,1)S(1)}, bf16[2,256,512]{2,1,0:T(8,128)(2,1)S(1)}, u32[]{:S(2)}, u32[]{:S(2)}) %collective-permute-start.15) | collective-permute-done | bytes 524320 | tf_op jit(solution)/shard_map/ppermute | solution.py:262
  87.4 0.9 pad_maximum_fusion
  (5 shorter events, 0.2 us)
Async XLA Ops:
  0.0 4.2 %copy-start.1 = (bf16[256,1024]{1,0:T(8,128)(2,1)S(1)}, bf16[256,1024]{1,0:T(8,128)(2,1)}, u32[]{:S(2)}) copy-start(bf16[256,1024]{1,0:T(8,128)(2,1)} %v_ref.1) | copy-start | bytes 1572868
  0.0 4.2 %copy-start = (bf16[256,1024]{1,0:T(8,128)(2,1)S(1)}, bf16[256,1024]{1,0:T(8,128)(2,1)}, u32[]{:S(2)}) copy-start(bf16[256,1024]{1,0:T(8,128)(2,1)} %k_ref.1) | copy-start | bytes 1572868
  0.0 4.2 %copy-start.2 = (bf16[256,1024]{1,0:T(8,128)(2,1)S(1)}, bf16[256,1024]{1,0:T(8,128)(2,1)}, u32[]{:S(2)}) copy-start(bf16[256,1024]{1,0:T(8,128)(2,1)} %q_ref.3) | copy-start | bytes 1572868
  1.7 5.4 %collective-permute-start.4 = (bf16[4,128,128]{2,1,0:T(8,128)(2,1)S(1)}, bf16[4,128,128]{2,1,0:T(8,128)(2,1)S(1)}, u32[]{:S(2)}, u32[]{:S(2)}) collective-permute-start(bf16[4,128,128]{2,1,0:T(8,128)(2,1)S(1)} %get-tuple-element.23), channel_id=1, source_target_pairs={{0,4},{4,0},{8,12},{12,8},{16,20},{20,16},{24,28},{28,24},{1,5},{5... | collective-permute-start | bytes 393224 | tf_op jit(solution)/shard_map/ppermute | solution.py:258
  4.1 6.1 %collective-permute-start = (bf16[4,128,128]{2,1,0:T(8,128)(2,1)S(1)}, bf16[4,128,128]{2,1,0:T(8,128)(2,1)S(1)}, u32[]{:S(2)}, u32[]{:S(2)}) collective-permute-start(bf16[4,128,128]{2,1,0:T(8,128)(2,1)S(1)} %get-tuple-element.19), channel_id=1, source_target_pairs={{0,4},{4,0},{8,12},{12,8},{16,20},{20,16},{24,28},{28,24},{1,5},{5... | collective-permute-start | bytes 393224 | tf_op jit(solution)/shard_map/ppermute | solution.py:258
  5.1 14.4 %copy-start.3 = (f32[1024]{0:T(1024)S(1)}, f32[1024]{0:T(1024)}, u32[]{:S(2)}) copy-start(f32[1024]{0:T(1024)} %param.8) | copy-start | bytes 12292
  7.1 5.9 %collective-permute-start.5 = (bf16[4,128,128]{2,1,0:T(8,128)(2,1)S(1)}, bf16[4,128,128]{2,1,0:T(8,128)(2,1)S(1)}, u32[]{:S(2)}, u32[]{:S(2)}) collective-permute-start(bf16[4,128,128]{2,1,0:T(8,128)(2,1)S(1)} %shard_map.61), channel_id=1, source_target_pairs={{0,8},{4,12},{1,9},{5,13},{2,10},{6,14},{3,11},{7,15}} | collective-permute-start | bytes 393224 | tf_op jit(solution)/shard_map/ppermute | solution.py:282
  10.2 5.7 %collective-permute-start.1 = (bf16[4,128,128]{2,1,0:T(8,128)(2,1)S(1)}, bf16[4,128,128]{2,1,0:T(8,128)(2,1)S(1)}, u32[]{:S(2)}, u32[]{:S(2)}) collective-permute-start(bf16[4,128,128]{2,1,0:T(8,128)(2,1)S(1)} %shard_map.57), channel_id=1, source_target_pairs={{0,8},{4,12},{1,9},{5,13},{2,10},{6,14},{3,11},{7,15}} | collective-permute-start | bytes 393224 | tf_op jit(solution)/shard_map/ppermute | solution.py:282
  13.1 4.9 %collective-permute-start.6 = (bf16[4,128,128]{2,1,0:T(8,128)(2,1)S(1)}, bf16[4,128,128]{2,1,0:T(8,128)(2,1)S(1)}, u32[]{:S(2)}, u32[]{:S(2)}) collective-permute-start(bf16[4,128,128]{2,1,0:T(8,128)(2,1)S(1)} %shard_map.62), channel_id=1, source_target_pairs={{8,16},{12,20},{9,17},{13,21},{10,18},{14,22},{11,19},{15,23}} | collective-permute-start | bytes 393224 | tf_op jit(solution)/shard_map/ppermute | solution.py:282
  16.0 2.7 %collective-permute-start.2 = (bf16[4,128,128]{2,1,0:T(8,128)(2,1)S(1)}, bf16[4,128,128]{2,1,0:T(8,128)(2,1)S(1)}, u32[]{:S(2)}, u32[]{:S(2)}) collective-permute-start(bf16[4,128,128]{2,1,0:T(8,128)(2,1)S(1)} %shard_map.58), channel_id=1, source_target_pairs={{8,16},{12,20},{9,17},{13,21},{10,18},{14,22},{11,19},{15,23}} | collective-permute-start | bytes 393224 | tf_op jit(solution)/shard_map/ppermute | solution.py:282
  16.7 22.9 %collective-permute-start.9 = (bf16[1024,512]{1,0:T(8,128)(2,1)}, bf16[1024,512]{1,0:T(8,128)(2,1)}, u32[]{:S(2)}, u32[]{:S(2)}) collective-permute-start(bf16[1024,512]{1,0:T(8,128)(2,1)} %own_ref.1), channel_id=1, source_target_pairs={{0,4},{4,0},{8,12},{12,8},{16,20},{20,16},{24,28},{28,24},{1,5},{5... | collective-permute-start | bytes 3145736 | tf_op jit(solution)/shard_map/ppermute | solution.py:258
  18.0 1.4 %collective-permute-start.7 = (bf16[4,128,128]{2,1,0:T(8,128)(2,1)S(1)}, bf16[4,128,128]{2,1,0:T(8,128)(2,1)S(1)}, u32[]{:S(2)}, u32[]{:S(2)}) collective-permute-start(bf16[4,128,128]{2,1,0:T(8,128)(2,1)S(1)} %shard_map.63), channel_id=1, source_target_pairs={{16,24},{20,28},{17,25},{21,29},{18,26},{22,30},{19,27},{23,31}} | collective-permute-start | bytes 393224 | tf_op jit(solution)/shard_map/ppermute | solution.py:282
  18.8 0.7 collective-permute-start.3
  20.1 12.8 %collective-permute-start.8 = (bf16[256,1024]{1,0:T(8,128)(2,1)S(1)}, bf16[256,1024]{1,0:T(8,128)(2,1)S(1)}, u32[]{:S(2)}, u32[]{:S(2)}) collective-permute-start(bf16[256,1024]{1,0:T(8,128)(2,1)S(1)} %shard_map.64), channel_id=1, source_target_pairs={{0,8},{4,12},{8,0},{12,4},{16,24},{20,28},{24,16},{28,20},{1,9},{5... | collective-permute-start | bytes 1572872 | tf_op jit(solution)/shard_map/ppermute | solution.py:258
  23.3 26.9 %collective-permute-start.10 = (bf16[256,1024]{1,0:T(8,128)(2,1)S(1)}, bf16[256,1024]{1,0:T(8,128)(2,1)S(1)}, u32[]{:S(2)}, u32[]{:S(2)}) collective-permute-start(bf16[256,1024]{1,0:T(8,128)(2,1)S(1)} %shard_map.64), channel_id=1, source_target_pairs={{0,24},{1,25},{2,18},{3,19},{4,28},{5,29},{6,22},{7,23},{8,16},{9,... | collective-permute-start | bytes 1572872 | tf_op jit(solution)/shard_map/ppermute | solution.py:262
  50.9 5.4 %collective-permute-start.13 = (bf16[2,256,512]{2,1,0:T(8,128)(2,1)S(1)}, bf16[2,256,512]{2,1,0:T(8,128)(2,1)S(1)}, u32[]{:S(2)}, u32[]{:S(2)}) collective-permute-start(bf16[2,256,512]{2,1,0:T(8,128)(2,1)S(1)} %get-tuple-element.32), channel_id=1, source_target_pairs={{0,1},{1,0},{2,3},{3,2},{4,5},{5,4},{6,7},{7,6},{8,9},{9,8},{10,11... | collective-permute-start | bytes 1572872 | tf_op jit(solution)/shard_map/ppermute | solution.py:262
  54.8 13.5 %collective-permute-start.11 = (bf16[256,1024]{1,0:T(8,128)(2,1)S(1)}, bf16[256,1024]{1,0:T(8,128)(2,1)S(1)}, u32[]{:S(2)}, u32[]{:S(2)}) collective-permute-start(bf16[256,1024]{1,0:T(8,128)(2,1)S(1)} %collective-permute-done.10.heavy_ref), channel_id=1, source_target_pairs={{0,8},{4,12},{8,0},{12,4},{16,24},{20,28},{24,16},{28,20},{1,9},{5... | collective-permute-start | bytes 1572872 | tf_op jit(solution)/shard_map/ppermute | solution.py:258
  56.5 13.5 %collective-permute-start.14 = (bf16[2,256,512]{2,1,0:T(8,128)(2,1)S(1)}, bf16[2,256,512]{2,1,0:T(8,128)(2,1)S(1)}, u32[]{:S(2)}, u32[]{:S(2)}) collective-permute-start(bf16[2,256,512]{2,1,0:T(8,128)(2,1)S(1)} %add_convert_fusion.1), channel_id=1, source_target_pairs={{0,2},{1,3},{2,0},{3,1},{4,6},{5,7},{6,4},{7,5},{8,10},{9,11},{10,... | collective-permute-start | bytes 1572872 | tf_op jit(solution)/shard_map/ppermute | solution.py:262
  69.0 2.5 %collective-permute-start.12 = (bf16[2,256,512]{2,1,0:T(8,128)(2,1)S(1)}, bf16[2,256,512]{2,1,0:T(8,128)(2,1)S(1)}, u32[]{:S(2)}, u32[]{:S(2)}) collective-permute-start(bf16[2,256,512]{2,1,0:T(8,128)(2,1)S(1)} %get-tuple-element.29), channel_id=1, source_target_pairs={{0,1},{1,0},{2,3},{3,2},{4,5},{5,4},{6,7},{7,6},{8,9},{9,8},{10,11... | collective-permute-start | bytes 1572872 | tf_op jit(solution)/shard_map/ppermute | solution.py:262
  71.7 15.6 %collective-permute-start.15 = (bf16[2,256,512]{2,1,0:T(8,128)(2,1)S(1)}, bf16[2,256,512]{2,1,0:T(8,128)(2,1)S(1)}, u32[]{:S(2)}, u32[]{:S(2)}) collective-permute-start(bf16[2,256,512]{2,1,0:T(8,128)(2,1)S(1)} %add_convert_fusion), channel_id=1, source_target_pairs={{0,0},{1,16},{2,8},{3,24},{4,4},{5,20},{6,12},{7,28},{8,9},{9,25},... | collective-permute-start | bytes 1572872 | tf_op jit(solution)/shard_map/ppermute | solution.py:262

commit v30 on v27

--- a/solution.py
+++ b/solution.py
@@ -93,8 +93,7 @@
         part, index = divmod(head, heads // parts)
         mate_ref, *earlier_refs = state_refs[part * each : (part + 1) * each]
         state = jnp.where(second, mate_ref[index].astype(F32), 0.0)
-        for earlier_ref in earlier_refs:
-            state += earlier_ref[index].astype(F32)
+        state += sum(earlier_ref[index] for earlier_ref in earlier_refs).astype(F32)
         carried = jnp.dot(q_ref[:, cols], state.astype(BF16), preferred_element_type=F32)
         combined = within_ref[:, cols] + carried
         mean_square = jnp.mean(combined * combined, axis=-1, keepdims=True)

time: 90.1 us -> 90.1 us (level)
  no operation moved by 1% of the time
where the time goes in v30:
time: 90.1 us; the launch traced here: 89.9 us
  waiting for transfers between devices  41.5 us (46%)
  starting transfers between devices  38.6 us (43%)
  Pallas kernels  6.83 us (8%)
  local copies, waits for them, and re-layouts  1.41 us (2%)
  other arithmetic  1.32 us (1%)
    ppermute x5, waiting for transfers between devices, swap(): return lax.ppermute(value, 'seq', [(s, s ^ mask) for s in range(8)])  24.5 us
    ppermute x5, starting transfers between devices, move(): return lax.ppermute(value, both, pairs)  23.2 us
    ppermute x5, waiting for transfers between devices, move(): return lax.ppermute(value, both, pairs)  14.7 us
    ppermute x6, starting transfers between devices, pairs_body(): states[part].append(lax.ppermute(onward[part], 'seq', pairs))  8.54 us
    ppermute x5, starting transfers between devices, swap(): return lax.ppermute(value, 'seq', [(s, s ^ mask) for s in range(8)])  6.79 us
    ppermute x6, waiting for transfers between devices, pairs_body(): states[part].append(lax.ppermute(onward[part], 'seq', pairs))  2.22 us
  transfers between devices with their start and end apart: 16, of which 7 were waited for; matrix products, arithmetic and copies ran while one was open for 0% of the time, Pallas kernels for 6%

profile of v30, /device:TPU:1, one launch (start us, length us, event | category | flops | bytes accessed | tf_op | source)
XLA Modules:
  0.0 89.9 jit_solution(6473700716310668690)
XLA Ops:
  0.0 0.0 copy-start.1
  0.0 0.0 copy-start
  0.0 0.0 copy-start.2
  0.0 1.4 %fusion = (bf16[256,512]{1,0:T(8,128)(2,1)S(1)}, bf16[256,512]{1,0:T(8,128)(2,1)S(1)}, bf16[256,512]{1,0:T(8,128)(2,1)S(1)}, bf16[256,512]{1,0:T(8,128)(2,1)S(1)}) fusion(bf16[256,1024]{1,0:T(8,128)(2,1)} %v_ref.1, bf16[256,1024]{1,0:T(8,128)(2,1)} %k_ref.1), kind=kLoop, calls=%fused_computation.7 | loop fusion | bytes 2097152 | tf_op jit(solution)/shard_map/slice | solution.py:119
  1.4 0.3 shard_map.60
  1.7 2.1 %collective-permute-start.4 = (bf16[4,128,128]{2,1,0:T(8,128)(2,1)S(1)}, bf16[4,128,128]{2,1,0:T(8,128)(2,1)S(1)}, u32[]{:S(2)}, u32[]{:S(2)}) collective-permute-start(bf16[4,128,128]{2,1,0:T(8,128)(2,1)S(1)} %get-tuple-element.23), channel_id=1, source_target_pairs={{0,4},{4,0},{8,12},{12,8},{16,20},{20,16},{24,28},{28,24},{1,5},{5... | collective-permute-start | bytes 393224 | tf_op jit(solution)/shard_map/ppermute | solution.py:257
  3.8 0.3 shard_map.55
  4.1 0.1 collective-permute-start
  4.2 0.0 copy-done.1
  4.2 0.0 copy-done
  4.2 0.0 copy-done.2
  4.2 0.9 %shard_map.56.within_ref = f32[256,1024]{1,0:T(8,128)S(1)} custom-call(bf16[256,1024]{1,0:T(8,128)(2,1)S(1)} %copy-done.2, bf16[256,1024]{1,0:T(8,128)(2,1)S(1)} %copy-done, bf16[256,1024]{1,0:T(8,128)(2,1)S(1)} %copy-done.1), custom_call_target="tpu_custom_call" | custom-call | flops 268435456 | bytes 2621440 | tf_op jit(solution)/shard_map/pallas_call | solution.py:265
  5.1 0.0 copy-start.3
  5.1 1.9 %collective-permute-done.4.refs_1_.refs_4_ = bf16[4,128,128]{2,1,0:T(8,128)(2,1)S(1)} collective-permute-done((bf16[4,128,128]{2,1,0:T(8,128)(2,1)S(1)}, bf16[4,128,128]{2,1,0:T(8,128)(2,1)S(1)}, u32[]{:S(2)}, u32[]{:S(2)}) %collective-permute-start.4) | collective-permute-done | bytes 131104 | tf_op jit(solution)/shard_map/ppermute | solution.py:257
  7.1 3.1 %collective-permute-start.5 = (bf16[4,128,128]{2,1,0:T(8,128)(2,1)S(1)}, bf16[4,128,128]{2,1,0:T(8,128)(2,1)S(1)}, u32[]{:S(2)}, u32[]{:S(2)}) collective-permute-start(bf16[4,128,128]{2,1,0:T(8,128)(2,1)S(1)} %shard_map.61), channel_id=1, source_target_pairs={{0,8},{4,12},{1,9},{5,13},{2,10},{6,14},{3,11},{7,15}} | collective-permute-start | bytes 393224 | tf_op jit(solution)/shard_map/ppermute | solution.py:281
  10.2 0.0 collective-permute-done.refs_1_.refs_0_
  10.2 2.8 %collective-permute-start.1 = (bf16[4,128,128]{2,1,0:T(8,128)(2,1)S(1)}, bf16[4,128,128]{2,1,0:T(8,128)(2,1)S(1)}, u32[]{:S(2)}, u32[]{:S(2)}) collective-permute-start(bf16[4,128,128]{2,1,0:T(8,128)(2,1)S(1)} %shard_map.57), channel_id=1, source_target_pairs={{0,8},{4,12},{1,9},{5,13},{2,10},{6,14},{3,11},{7,15}} | collective-permute-start | bytes 393224 | tf_op jit(solution)/shard_map/ppermute | solution.py:281
  13.0 0.0 collective-permute-done.5.refs_2_.refs_5_
  13.1 0.7 collective-permute-start.6
  13.7 2.2 %collective-permute-done.1.refs_2_.refs_1_ = bf16[4,128,128]{2,1,0:T(8,128)(2,1)S(1)} collective-permute-done((bf16[4,128,128]{2,1,0:T(8,128)(2,1)S(1)}, bf16[4,128,128]{2,1,0:T(8,128)(2,1)S(1)}, u32[]{:S(2)}, u32[]{:S(2)}) %collective-permute-start.1) | collective-permute-done | bytes 131104 | tf_op jit(solution)/shard_map/ppermute | solution.py:281
  16.0 0.7 collective-permute-start.2
  16.7 1.3 %collective-permute-start.9 = (bf16[1024,512]{1,0:T(8,128)(2,1)}, bf16[1024,512]{1,0:T(8,128)(2,1)}, u32[]{:S(2)}, u32[]{:S(2)}) collective-permute-start(bf16[1024,512]{1,0:T(8,128)(2,1)} %own_ref.1), channel_id=1, source_target_pairs={{0,4},{4,0},{8,12},{12,8},{16,20},{20,16},{24,28},{28,24},{1,5},{5... | collective-permute-start | bytes 3145736 | tf_op jit(solution)/shard_map/ppermute | solution.py:257
  18.0 0.0 collective-permute-done.6.refs_3_.refs_6_
  18.0 0.1 shard_map.63
  18.0 0.7 collective-permute-start.7
  18.7 0.0 collective-permute-done.2.refs_3_.refs_2_
  18.7 0.1 shard_map.59
  18.8 0.7 collective-permute-start.3
  19.5 0.0 collective-permute-done.7.refs_7_
  19.5 0.0 collective-permute-done.3.refs_3_
  19.5 0.0 copy-done.3
  19.5 0.6 shard_map.64
  20.1 3.2 %collective-permute-start.8 = (bf16[256,1024]{1,0:T(8,128)(2,1)S(1)}, bf16[256,1024]{1,0:T(8,128)(2,1)S(1)}, u32[]{:S(2)}, u32[]{:S(2)}) collective-permute-start(bf16[256,1024]{1,0:T(8,128)(2,1)S(1)} %shard_map.64), channel_id=1, source_target_pairs={{0,8},{4,12},{8,0},{12,4},{16,24},{20,28},{24,16},{28,20},{1,9},{5... | collective-permute-start | bytes 1572872 | tf_op jit(solution)/shard_map/ppermute | solution.py:257
  23.3 6.8 %collective-permute-start.10 = (bf16[256,1024]{1,0:T(8,128)(2,1)S(1)}, bf16[256,1024]{1,0:T(8,128)(2,1)S(1)}, u32[]{:S(2)}, u32[]{:S(2)}) collective-permute-start(bf16[256,1024]{1,0:T(8,128)(2,1)S(1)} %shard_map.64), channel_id=1, source_target_pairs={{0,16},{1,17},{2,26},{3,27},{4,20},{5,21},{6,30},{7,31},{8,24},{9,... | collective-permute-start | bytes 1572872 | tf_op jit(solution)/shard_map/ppermute | solution.py:261
  30.1 11.8 %collective-permute-done.8 = bf16[256,1024]{1,0:T(8,128)(2,1)S(1)} collective-permute-done((bf16[256,1024]{1,0:T(8,128)(2,1)S(1)}, bf16[256,1024]{1,0:T(8,128)(2,1)S(1)}, u32[]{:S(2)}, u32[]{:S(2)}) %collective-permute-start.8) | collective-permute-done | bytes 524320 | tf_op jit(solution)/shard_map/ppermute | solution.py:257
  41.9 0.1 broadcast_select_fusion.1
  42.0 0.0 collective-permute-done.9.mate_ref
  42.0 1.7 %shard_map.65.weight_ref = bf16[2,1024,512]{2,1,0:T(8,128)(2,1)S(1)} custom-call(bf16[1024,512]{1,0:T(8,128)(2,1)} %own_ref.1, bf16[1024,512]{1,0:T(8,128)(2,1)} %collective-permute-done.9.mate_ref), custom_call_target="tpu_custom_call" | custom-call | bytes 4194304 | tf_op jit(solution)/shard_map/pallas_call | solution.py:285
  43.7 0.7 shard_map.67.light_ref
  44.4 0.0 collective-permute-done.10.heavy_ref
  44.4 0.7 shard_map.69
  45.2 9.9 %collective-permute-start.13 = (bf16[2,256,512]{2,1,0:T(8,128)(2,1)S(1)}, bf16[2,256,512]{2,1,0:T(8,128)(2,1)S(1)}, u32[]{:S(2)}, u32[]{:S(2)}) collective-permute-start(bf16[2,256,512]{2,1,0:T(8,128)(2,1)S(1)} %get-tuple-element.32), channel_id=1, source_target_pairs={{0,1},{1,0},{2,3},{3,2},{4,5},{5,4},{6,7},{7,6},{8,9},{9,8},{10,11... | collective-permute-start | bytes 1572872 | tf_op jit(solution)/shard_map/ppermute | solution.py:261
  55.0 0.1 collective-permute-start.11
  55.1 0.7 shard_map.66.light_ref
  55.8 0.8 collective-permute-done.13
  56.6 0.1 add_convert_fusion.1
  56.7 1.1 %collective-permute-start.14 = (bf16[2,256,512]{2,1,0:T(8,128)(2,1)S(1)}, bf16[2,256,512]{2,1,0:T(8,128)(2,1)S(1)}, u32[]{:S(2)}, u32[]{:S(2)}) collective-permute-start(bf16[2,256,512]{2,1,0:T(8,128)(2,1)S(1)} %add_convert_fusion.1), channel_id=1, source_target_pairs={{0,2},{1,3},{2,0},{3,1},{4,6},{5,7},{6,4},{7,5},{8,10},{9,11},{10,... | collective-permute-start | bytes 1572872 | tf_op jit(solution)/shard_map/ppermute | solution.py:261
  57.8 10.8 %collective-permute-done.11.heavy_ref = bf16[256,1024]{1,0:T(8,128)(2,1)S(1)} collective-permute-done((bf16[256,1024]{1,0:T(8,128)(2,1)S(1)}, bf16[256,1024]{1,0:T(8,128)(2,1)S(1)}, u32[]{:S(2)}, u32[]{:S(2)}) %collective-permute-start.11) | collective-permute-done | bytes 524320 | tf_op jit(solution)/shard_map/ppermute | solution.py:257
  68.5 0.7 shard_map.68
  69.3 0.9 %collective-permute-start.12 = (bf16[2,256,512]{2,1,0:T(8,128)(2,1)S(1)}, bf16[2,256,512]{2,1,0:T(8,128)(2,1)S(1)}, u32[]{:S(2)}, u32[]{:S(2)}) collective-permute-start(bf16[2,256,512]{2,1,0:T(8,128)(2,1)S(1)} %get-tuple-element.29), channel_id=1, source_target_pairs={{0,1},{1,0},{2,3},{3,2},{4,5},{5,4},{6,7},{7,6},{8,9},{9,8},{10,11... | collective-permute-start | bytes 1572872 | tf_op jit(solution)/shard_map/ppermute | solution.py:261
  70.2 0.0 collective-permute-done.14
  70.2 1.5 %collective-permute-done.12 = bf16[2,256,512]{2,1,0:T(8,128)(2,1)S(1)} collective-permute-done((bf16[2,256,512]{2,1,0:T(8,128)(2,1)S(1)}, bf16[2,256,512]{2,1,0:T(8,128)(2,1)S(1)}, u32[]{:S(2)}, u32[]{:S(2)}) %collective-permute-start.12) | collective-permute-done | bytes 524320 | tf_op jit(solution)/shard_map/ppermute | solution.py:261
  71.7 0.2 add_convert_fusion
  71.9 4.6 %collective-permute-start.15 = (bf16[2,256,512]{2,1,0:T(8,128)(2,1)S(1)}, bf16[2,256,512]{2,1,0:T(8,128)(2,1)S(1)}, u32[]{:S(2)}, u32[]{:S(2)}) collective-permute-start(bf16[2,256,512]{2,1,0:T(8,128)(2,1)S(1)} %add_convert_fusion), channel_id=1, source_target_pairs={{0,0},{1,24},{2,8},{3,16},{4,4},{5,28},{6,12},{7,20},{8,9},{9,17},... | collective-permute-start | bytes 1572872 | tf_op jit(solution)/shard_map/ppermute | solution.py:261
  76.5 12.4 %collective-permute-done.15 = bf16[2,256,512]{2,1,0:T(8,128)(2,1)S(1)} collective-permute-done((bf16[2,256,512]{2,1,0:T(8,128)(2,1)S(1)}, bf16[2,256,512]{2,1,0:T(8,128)(2,1)S(1)}, u32[]{:S(2)}, u32[]{:S(2)}) %collective-permute-start.15) | collective-permute-done | bytes 524320 | tf_op jit(solution)/shard_map/ppermute | solution.py:261
  89.0 0.9 pad_maximum_fusion
  (5 shorter events, 0.2 us)
Async XLA Ops:
  0.0 4.2 %copy-start.1 = (bf16[256,1024]{1,0:T(8,128)(2,1)S(1)}, bf16[256,1024]{1,0:T(8,128)(2,1)}, u32[]{:S(2)}) copy-start(bf16[256,1024]{1,0:T(8,128)(2,1)} %v_ref.1) | copy-start | bytes 1572868
  0.0 4.2 %copy-start = (bf16[256,1024]{1,0:T(8,128)(2,1)S(1)}, bf16[256,1024]{1,0:T(8,128)(2,1)}, u32[]{:S(2)}) copy-start(bf16[256,1024]{1,0:T(8,128)(2,1)} %k_ref.1) | copy-start | bytes 1572868
  0.0 4.2 %copy-start.2 = (bf16[256,1024]{1,0:T(8,128)(2,1)S(1)}, bf16[256,1024]{1,0:T(8,128)(2,1)}, u32[]{:S(2)}) copy-start(bf16[256,1024]{1,0:T(8,128)(2,1)} %q_ref.3) | copy-start | bytes 1572868
  1.7 5.4 %collective-permute-start.4 = (bf16[4,128,128]{2,1,0:T(8,128)(2,1)S(1)}, bf16[4,128,128]{2,1,0:T(8,128)(2,1)S(1)}, u32[]{:S(2)}, u32[]{:S(2)}) collective-permute-start(bf16[4,128,128]{2,1,0:T(8,128)(2,1)S(1)} %get-tuple-element.23), channel_id=1, source_target_pairs={{0,4},{4,0},{8,12},{12,8},{16,20},{20,16},{24,28},{28,24},{1,5},{5... | collective-permute-start | bytes 393224 | tf_op jit(solution)/shard_map/ppermute | solution.py:257
  4.1 6.1 %collective-permute-start = (bf16[4,128,128]{2,1,0:T(8,128)(2,1)S(1)}, bf16[4,128,128]{2,1,0:T(8,128)(2,1)S(1)}, u32[]{:S(2)}, u32[]{:S(2)}) collective-permute-start(bf16[4,128,128]{2,1,0:T(8,128)(2,1)S(1)} %get-tuple-element.19), channel_id=1, source_target_pairs={{0,4},{4,0},{8,12},{12,8},{16,20},{20,16},{24,28},{28,24},{1,5},{5... | collective-permute-start | bytes 393224 | tf_op jit(solution)/shard_map/ppermute | solution.py:257
  5.1 14.4 %copy-start.3 = (f32[1024]{0:T(1024)S(1)}, f32[1024]{0:T(1024)}, u32[]{:S(2)}) copy-start(f32[1024]{0:T(1024)} %param.8) | copy-start | bytes 12292
  7.1 5.9 %collective-permute-start.5 = (bf16[4,128,128]{2,1,0:T(8,128)(2,1)S(1)}, bf16[4,128,128]{2,1,0:T(8,128)(2,1)S(1)}, u32[]{:S(2)}, u32[]{:S(2)}) collective-permute-start(bf16[4,128,128]{2,1,0:T(8,128)(2,1)S(1)} %shard_map.61), channel_id=1, source_target_pairs={{0,8},{4,12},{1,9},{5,13},{2,10},{6,14},{3,11},{7,15}} | collective-permute-start | bytes 393224 | tf_op jit(solution)/shard_map/ppermute | solution.py:281
  10.2 5.7 %collective-permute-start.1 = (bf16[4,128,128]{2,1,0:T(8,128)(2,1)S(1)}, bf16[4,128,128]{2,1,0:T(8,128)(2,1)S(1)}, u32[]{:S(2)}, u32[]{:S(2)}) collective-permute-start(bf16[4,128,128]{2,1,0:T(8,128)(2,1)S(1)} %shard_map.57), channel_id=1, source_target_pairs={{0,8},{4,12},{1,9},{5,13},{2,10},{6,14},{3,11},{7,15}} | collective-permute-start | bytes 393224 | tf_op jit(solution)/shard_map/ppermute | solution.py:281
  13.1 4.9 %collective-permute-start.6 = (bf16[4,128,128]{2,1,0:T(8,128)(2,1)S(1)}, bf16[4,128,128]{2,1,0:T(8,128)(2,1)S(1)}, u32[]{:S(2)}, u32[]{:S(2)}) collective-permute-start(bf16[4,128,128]{2,1,0:T(8,128)(2,1)S(1)} %shard_map.62), channel_id=1, source_target_pairs={{8,16},{12,20},{9,17},{13,21},{10,18},{14,22},{11,19},{15,23}} | collective-permute-start | bytes 393224 | tf_op jit(solution)/shard_map/ppermute | solution.py:281
  16.0 2.7 %collective-permute-start.2 = (bf16[4,128,128]{2,1,0:T(8,128)(2,1)S(1)}, bf16[4,128,128]{2,1,0:T(8,128)(2,1)S(1)}, u32[]{:S(2)}, u32[]{:S(2)}) collective-permute-start(bf16[4,128,128]{2,1,0:T(8,128)(2,1)S(1)} %shard_map.58), channel_id=1, source_target_pairs={{8,16},{12,20},{9,17},{13,21},{10,18},{14,22},{11,19},{15,23}} | collective-permute-start | bytes 393224 | tf_op jit(solution)/shard_map/ppermute | solution.py:281
  16.7 25.3 %collective-permute-start.9 = (bf16[1024,512]{1,0:T(8,128)(2,1)}, bf16[1024,512]{1,0:T(8,128)(2,1)}, u32[]{:S(2)}, u32[]{:S(2)}) collective-permute-start(bf16[1024,512]{1,0:T(8,128)(2,1)} %own_ref.1), channel_id=1, source_target_pairs={{0,4},{4,0},{8,12},{12,8},{16,20},{20,16},{24,28},{28,24},{1,5},{5... | collective-permute-start | bytes 3145736 | tf_op jit(solution)/shard_map/ppermute | solution.py:257
  18.0 1.4 %collective-permute-start.7 = (bf16[4,128,128]{2,1,0:T(8,128)(2,1)S(1)}, bf16[4,128,128]{2,1,0:T(8,128)(2,1)S(1)}, u32[]{:S(2)}, u32[]{:S(2)}) collective-permute-start(bf16[4,128,128]{2,1,0:T(8,128)(2,1)S(1)} %shard_map.63), channel_id=1, source_target_pairs={{16,24},{20,28},{17,25},{21,29},{18,26},{22,30},{19,27},{23,31}} | collective-permute-start | bytes 393224 | tf_op jit(solution)/shard_map/ppermute | solution.py:281
  18.8 0.7 collective-permute-start.3
  20.1 21.8 %collective-permute-start.8 = (bf16[256,1024]{1,0:T(8,128)(2,1)S(1)}, bf16[256,1024]{1,0:T(8,128)(2,1)S(1)}, u32[]{:S(2)}, u32[]{:S(2)}) collective-permute-start(bf16[256,1024]{1,0:T(8,128)(2,1)S(1)} %shard_map.64), channel_id=1, source_target_pairs={{0,8},{4,12},{8,0},{12,4},{16,24},{20,28},{24,16},{28,20},{1,9},{5... | collective-permute-start | bytes 1572872 | tf_op jit(solution)/shard_map/ppermute | solution.py:257
  23.3 21.1 %collective-permute-start.10 = (bf16[256,1024]{1,0:T(8,128)(2,1)S(1)}, bf16[256,1024]{1,0:T(8,128)(2,1)S(1)}, u32[]{:S(2)}, u32[]{:S(2)}) collective-permute-start(bf16[256,1024]{1,0:T(8,128)(2,1)S(1)} %shard_map.64), channel_id=1, source_target_pairs={{0,16},{1,17},{2,26},{3,27},{4,20},{5,21},{6,30},{7,31},{8,24},{9,... | collective-permute-start | bytes 1572872 | tf_op jit(solution)/shard_map/ppermute | solution.py:261
  45.2 11.4 %collective-permute-start.13 = (bf16[2,256,512]{2,1,0:T(8,128)(2,1)S(1)}, bf16[2,256,512]{2,1,0:T(8,128)(2,1)S(1)}, u32[]{:S(2)}, u32[]{:S(2)}) collective-permute-start(bf16[2,256,512]{2,1,0:T(8,128)(2,1)S(1)} %get-tuple-element.32), channel_id=1, source_target_pairs={{0,1},{1,0},{2,3},{3,2},{4,5},{5,4},{6,7},{7,6},{8,9},{9,8},{10,11... | collective-permute-start | bytes 1572872 | tf_op jit(solution)/shard_map/ppermute | solution.py:261
  55.0 13.5 %collective-permute-start.11 = (bf16[256,1024]{1,0:T(8,128)(2,1)S(1)}, bf16[256,1024]{1,0:T(8,128)(2,1)S(1)}, u32[]{:S(2)}, u32[]{:S(2)}) collective-permute-start(bf16[256,1024]{1,0:T(8,128)(2,1)S(1)} %collective-permute-done.10.heavy_ref), channel_id=1, source_target_pairs={{0,8},{4,12},{8,0},{12,4},{16,24},{20,28},{24,16},{28,20},{1,9},{5... | collective-permute-start | bytes 1572872 | tf_op jit(solution)/shard_map/ppermute | solution.py:257
  56.7 13.5 %collective-permute-start.14 = (bf16[2,256,512]{2,1,0:T(8,128)(2,1)S(1)}, bf16[2,256,512]{2,1,0:T(8,128)(2,1)S(1)}, u32[]{:S(2)}, u32[]{:S(2)}) collective-permute-start(bf16[2,256,512]{2,1,0:T(8,128)(2,1)S(1)} %add_convert_fusion.1), channel_id=1, source_target_pairs={{0,2},{1,3},{2,0},{3,1},{4,6},{5,7},{6,4},{7,5},{8,10},{9,11},{10,... | collective-permute-start | bytes 1572872 | tf_op jit(solution)/shard_map/ppermute | solution.py:261
  69.3 2.5 %collective-permute-start.12 = (bf16[2,256,512]{2,1,0:T(8,128)(2,1)S(1)}, bf16[2,256,512]{2,1,0:T(8,128)(2,1)S(1)}, u32[]{:S(2)}, u32[]{:S(2)}) collective-permute-start(bf16[2,256,512]{2,1,0:T(8,128)(2,1)S(1)} %get-tuple-element.29), channel_id=1, source_target_pairs={{0,1},{1,0},{2,3},{3,2},{4,5},{5,4},{6,7},{7,6},{8,9},{9,8},{10,11... | collective-permute-start | bytes 1572872 | tf_op jit(solution)/shard_map/ppermute | solution.py:261
  71.9 17.0 %collective-permute-start.15 = (bf16[2,256,512]{2,1,0:T(8,128)(2,1)S(1)}, bf16[2,256,512]{2,1,0:T(8,128)(2,1)S(1)}, u32[]{:S(2)}, u32[]{:S(2)}) collective-permute-start(bf16[2,256,512]{2,1,0:T(8,128)(2,1)S(1)} %add_convert_fusion), channel_id=1, source_target_pairs={{0,0},{1,24},{2,8},{3,16},{4,4},{5,28},{6,12},{7,20},{8,9},{9,17},... | collective-permute-start | bytes 1572872 | tf_op jit(solution)/shard_map/ppermute | solution.py:261

commit v31 on v27

--- a/solution.py
+++ b/solution.py
@@ -317,9 +317,10 @@
     crossed = move(far, lambda z, y, x, c: (z, y, 1 - x, c))
     near_light = product(jnp.where(x == 0, attended, beside))
     near = projected(near_light, onward) + crossed.astype(F32)
-    result = move(near.astype(BF16), lambda z, y, x, c: (z ^ 3 * c ^ x, y, z // 2, z % 2))
-    first = jnp.where(y == 0, result[0], result[1])
-    return jnp.concatenate([first, jnp.where(y == 0, result[1], result[0])], axis=1)
+    near = near.astype(BF16)
+    first = jnp.where(y == 0, near[0], near[1])
+    near = jnp.concatenate([first, jnp.where(y == 0, near[1], near[0])], axis=1)
+    return move(near, lambda z, y, x, c: (z ^ 3 * c ^ x, y, z // 2, z % 2))
 
 
 def solution(mesh):

time: 90.1 us -> 90.1 us (level)
  no operation moved by 1% of the time
where the time goes in v31:
time: 90.1 us; the launch traced here: 89.9 us
  waiting for transfers between devices  41.4 us (46%)
  starting transfers between devices  38.6 us (43%)
  Pallas kernels  6.83 us (8%)
  local copies, waits for them, and re-layouts  2.2 us (2%)
    ppermute x5, waiting for transfers between devices, swap(): return lax.ppermute(value, 'seq', [(s, s ^ mask) for s in range(8)])  24.5 us
    ppermute x5, starting transfers between devices, move(): return lax.ppermute(value, both, pairs)  23.3 us
    ppermute x5, waiting for transfers between devices, move(): return lax.ppermute(value, both, pairs)  14.7 us
    ppermute x6, starting transfers between devices, pairs_body(): states[part].append(lax.ppermute(onward[part], 'seq', pairs))  8.54 us
    ppermute x5, starting transfers between devices, swap(): return lax.ppermute(value, 'seq', [(s, s ^ mask) for s in range(8)])  6.8 us
    ppermute x6, waiting for transfers between devices, pairs_body(): states[part].append(lax.ppermute(onward[part], 'seq', pairs))  2.22 us
  transfers between devices with their start and end apart: 16, of which 7 were waited for; matrix products, arithmetic and copies ran while one was open for 0% of the time, Pallas kernels for 6%

profile of v31, /device:TPU:1, one launch (start us, length us, event | category | flops | bytes accessed | tf_op | source)
XLA Modules:
  0.0 89.9 jit_solution(2401925312308453389)
XLA Ops:
  0.0 0.0 copy-start.1
  0.0 0.0 copy-start
  0.0 0.0 copy-start.2
  0.0 1.4 %fusion = (bf16[256,512]{1,0:T(8,128)(2,1)S(1)}, bf16[256,512]{1,0:T(8,128)(2,1)S(1)}, bf16[256,512]{1,0:T(8,128)(2,1)S(1)}, bf16[256,512]{1,0:T(8,128)(2,1)S(1)}) fusion(bf16[256,1024]{1,0:T(8,128)(2,1)} %v_ref.1, bf16[256,1024]{1,0:T(8,128)(2,1)} %k_ref.1), kind=kLoop, calls=%fused_computation.7 | loop fusion | bytes 2097152 | tf_op jit(solution)/shard_map/slice | solution.py:120
  1.4 0.3 shard_map.60
  1.7 2.1 %collective-permute-start.4 = (bf16[4,128,128]{2,1,0:T(8,128)(2,1)S(1)}, bf16[4,128,128]{2,1,0:T(8,128)(2,1)S(1)}, u32[]{:S(2)}, u32[]{:S(2)}) collective-permute-start(bf16[4,128,128]{2,1,0:T(8,128)(2,1)S(1)} %get-tuple-element.23), channel_id=1, source_target_pairs={{0,4},{4,0},{8,12},{12,8},{16,20},{20,16},{24,28},{28,24},{1,5},{5... | collective-permute-start | bytes 393224 | tf_op jit(solution)/shard_map/ppermute | solution.py:258
  3.8 0.3 shard_map.55
  4.1 0.1 collective-permute-start
  4.2 0.0 copy-done.1
  4.2 0.0 copy-done
  4.2 0.0 copy-done.2
  4.2 0.9 %shard_map.56.within_ref = f32[256,1024]{1,0:T(8,128)S(1)} custom-call(bf16[256,1024]{1,0:T(8,128)(2,1)S(1)} %copy-done.2, bf16[256,1024]{1,0:T(8,128)(2,1)S(1)} %copy-done, bf16[256,1024]{1,0:T(8,128)(2,1)S(1)} %copy-done.1), custom_call_target="tpu_custom_call" | custom-call | flops 268435456 | bytes 2621440 | tf_op jit(solution)/shard_map/pallas_call | solution.py:266
  5.1 0.0 copy-start.3
  5.1 1.9 %collective-permute-done.4.refs_1_.refs_4_ = bf16[4,128,128]{2,1,0:T(8,128)(2,1)S(1)} collective-permute-done((bf16[4,128,128]{2,1,0:T(8,128)(2,1)S(1)}, bf16[4,128,128]{2,1,0:T(8,128)(2,1)S(1)}, u32[]{:S(2)}, u32[]{:S(2)}) %collective-permute-start.4) | collective-permute-done | bytes 131104 | tf_op jit(solution)/shard_map/ppermute | solution.py:258
  7.1 3.1 %collective-permute-start.5 = (bf16[4,128,128]{2,1,0:T(8,128)(2,1)S(1)}, bf16[4,128,128]{2,1,0:T(8,128)(2,1)S(1)}, u32[]{:S(2)}, u32[]{:S(2)}) collective-permute-start(bf16[4,128,128]{2,1,0:T(8,128)(2,1)S(1)} %shard_map.61), channel_id=1, source_target_pairs={{0,8},{4,12},{1,9},{5,13},{2,10},{6,14},{3,11},{7,15}} | collective-permute-start | bytes 393224 | tf_op jit(solution)/shard_map/ppermute | solution.py:282
  10.2 0.0 collective-permute-done.refs_1_.refs_0_
  10.2 2.8 %collective-permute-start.1 = (bf16[4,128,128]{2,1,0:T(8,128)(2,1)S(1)}, bf16[4,128,128]{2,1,0:T(8,128)(2,1)S(1)}, u32[]{:S(2)}, u32[]{:S(2)}) collective-permute-start(bf16[4,128,128]{2,1,0:T(8,128)(2,1)S(1)} %shard_map.57), channel_id=1, source_target_pairs={{0,8},{4,12},{1,9},{5,13},{2,10},{6,14},{3,11},{7,15}} | collective-permute-start | bytes 393224 | tf_op jit(solution)/shard_map/ppermute | solution.py:282
  13.0 0.0 collective-permute-done.5.refs_2_.refs_5_
  13.1 0.7 collective-permute-start.6
  13.7 2.2 %collective-permute-done.1.refs_2_.refs_1_ = bf16[4,128,128]{2,1,0:T(8,128)(2,1)S(1)} collective-permute-done((bf16[4,128,128]{2,1,0:T(8,128)(2,1)S(1)}, bf16[4,128,128]{2,1,0:T(8,128)(2,1)S(1)}, u32[]{:S(2)}, u32[]{:S(2)}) %collective-permute-start.1) | collective-permute-done | bytes 131104 | tf_op jit(solution)/shard_map/ppermute | solution.py:282
  16.0 0.7 collective-permute-start.2
  16.7 1.3 %collective-permute-start.9 = (bf16[1024,512]{1,0:T(8,128)(2,1)}, bf16[1024,512]{1,0:T(8,128)(2,1)}, u32[]{:S(2)}, u32[]{:S(2)}) collective-permute-start(bf16[1024,512]{1,0:T(8,128)(2,1)} %own_ref.1), channel_id=1, source_target_pairs={{0,4},{4,0},{8,12},{12,8},{16,20},{20,16},{24,28},{28,24},{1,5},{5... | collective-permute-start | bytes 3145736 | tf_op jit(solution)/shard_map/ppermute | solution.py:258
  18.0 0.0 collective-permute-done.6.refs_3_.refs_6_
  18.0 0.1 shard_map.63
  18.0 0.7 collective-permute-start.7
  18.7 0.0 collective-permute-done.2.refs_3_.refs_2_
  18.7 0.1 shard_map.59
  18.8 0.7 collective-permute-start.3
  19.5 0.0 collective-permute-done.7.refs_7_
  19.5 0.0 collective-permute-done.3.refs_3_
  19.5 0.0 copy-done.3
  19.5 0.5 shard_map.64
  20.1 3.2 %collective-permute-start.8 = (bf16[256,1024]{1,0:T(8,128)(2,1)S(1)}, bf16[256,1024]{1,0:T(8,128)(2,1)S(1)}, u32[]{:S(2)}, u32[]{:S(2)}) collective-permute-start(bf16[256,1024]{1,0:T(8,128)(2,1)S(1)} %shard_map.64), channel_id=1, source_target_pairs={{0,8},{4,12},{8,0},{12,4},{16,24},{20,28},{24,16},{28,20},{1,9},{5... | collective-permute-start | bytes 1572872 | tf_op jit(solution)/shard_map/ppermute | solution.py:258
  23.3 6.8 %collective-permute-start.10 = (bf16[256,1024]{1,0:T(8,128)(2,1)S(1)}, bf16[256,1024]{1,0:T(8,128)(2,1)S(1)}, u32[]{:S(2)}, u32[]{:S(2)}) collective-permute-start(bf16[256,1024]{1,0:T(8,128)(2,1)S(1)} %shard_map.64), channel_id=1, source_target_pairs={{0,16},{1,17},{2,26},{3,27},{4,20},{5,21},{6,30},{7,31},{8,24},{9,... | collective-permute-start | bytes 1572872 | tf_op jit(solution)/shard_map/ppermute | solution.py:262
  30.1 11.8 %collective-permute-done.8 = bf16[256,1024]{1,0:T(8,128)(2,1)S(1)} collective-permute-done((bf16[256,1024]{1,0:T(8,128)(2,1)S(1)}, bf16[256,1024]{1,0:T(8,128)(2,1)S(1)}, u32[]{:S(2)}, u32[]{:S(2)}) %collective-permute-start.8) | collective-permute-done | bytes 524320 | tf_op jit(solution)/shard_map/ppermute | solution.py:258
  41.9 0.1 broadcast_select_fusion.1
  42.0 0.0 collective-permute-done.9.mate_ref
  42.0 1.7 %shard_map.65.weight_ref = bf16[2,1024,512]{2,1,0:T(8,128)(2,1)S(1)} custom-call(bf16[1024,512]{1,0:T(8,128)(2,1)} %own_ref.1, bf16[1024,512]{1,0:T(8,128)(2,1)} %collective-permute-done.9.mate_ref), custom_call_target="tpu_custom_call" | custom-call | bytes 4194304 | tf_op jit(solution)/shard_map/pallas_call | solution.py:286
  43.7 0.7 shard_map.67.light_ref
  44.4 0.0 collective-permute-done.10.heavy_ref
  44.4 0.7 shard_map.69
  45.2 9.9 %collective-permute-start.13 = (bf16[2,256,512]{2,1,0:T(8,128)(2,1)S(1)}, bf16[2,256,512]{2,1,0:T(8,128)(2,1)S(1)}, u32[]{:S(2)}, u32[]{:S(2)}) collective-permute-start(bf16[2,256,512]{2,1,0:T(8,128)(2,1)S(1)} %get-tuple-element.32), channel_id=1, source_target_pairs={{0,1},{1,0},{2,3},{3,2},{4,5},{5,4},{6,7},{7,6},{8,9},{9,8},{10,11... | collective-permute-start | bytes 1572872 | tf_op jit(solution)/shard_map/ppermute | solution.py:262
  55.0 0.1 collective-permute-start.11
  55.1 0.7 shard_map.66.light_ref
  55.8 0.8 collective-permute-done.13
  56.6 0.1 add_convert_fusion.1
  56.7 1.1 %collective-permute-start.14 = (bf16[2,256,512]{2,1,0:T(8,128)(2,1)S(1)}, bf16[2,256,512]{2,1,0:T(8,128)(2,1)S(1)}, u32[]{:S(2)}, u32[]{:S(2)}) collective-permute-start(bf16[2,256,512]{2,1,0:T(8,128)(2,1)S(1)} %add_convert_fusion.1), channel_id=1, source_target_pairs={{0,2},{1,3},{2,0},{3,1},{4,6},{5,7},{6,4},{7,5},{8,10},{9,11},{10,... | collective-permute-start | bytes 1572872 | tf_op jit(solution)/shard_map/ppermute | solution.py:262
  57.8 10.8 %collective-permute-done.11.heavy_ref = bf16[256,1024]{1,0:T(8,128)(2,1)S(1)} collective-permute-done((bf16[256,1024]{1,0:T(8,128)(2,1)S(1)}, bf16[256,1024]{1,0:T(8,128)(2,1)S(1)}, u32[]{:S(2)}, u32[]{:S(2)}) %collective-permute-start.11) | collective-permute-done | bytes 524320 | tf_op jit(solution)/shard_map/ppermute | solution.py:258
  68.5 0.7 shard_map.68
  69.3 0.9 %collective-permute-start.12 = (bf16[2,256,512]{2,1,0:T(8,128)(2,1)S(1)}, bf16[2,256,512]{2,1,0:T(8,128)(2,1)S(1)}, u32[]{:S(2)}, u32[]{:S(2)}) collective-permute-start(bf16[2,256,512]{2,1,0:T(8,128)(2,1)S(1)} %get-tuple-element.29), channel_id=1, source_target_pairs={{0,1},{1,0},{2,3},{3,2},{4,5},{5,4},{6,7},{7,6},{8,9},{9,8},{10,11... | collective-permute-start | bytes 1572872 | tf_op jit(solution)/shard_map/ppermute | solution.py:262
  70.2 0.0 collective-permute-done.14
  70.2 1.5 %collective-permute-done.12 = bf16[2,256,512]{2,1,0:T(8,128)(2,1)S(1)} collective-permute-done((bf16[2,256,512]{2,1,0:T(8,128)(2,1)S(1)}, bf16[2,256,512]{2,1,0:T(8,128)(2,1)S(1)}, u32[]{:S(2)}, u32[]{:S(2)}) %collective-permute-start.12) | collective-permute-done | bytes 524320 | tf_op jit(solution)/shard_map/ppermute | solution.py:262
  71.7 0.2 add_convert_fusion
  72.0 0.1 pad_maximum_fusion
  72.0 4.6 %collective-permute-start.15 = (bf16[256,1024]{1,0:T(8,128)(2,1)S(1)}, bf16[256,1024]{1,0:T(8,128)(2,1)S(1)}, u32[]{:S(2)}, u32[]{:S(2)}) collective-permute-start(bf16[256,1024]{1,0:T(8,128)(2,1)S(1)} %pad_maximum_fusion), channel_id=1, source_target_pairs={{0,0},{1,24},{2,8},{3,16},{4,4},{5,28},{6,12},{7,20},{8,9},{9,17},... | collective-permute-start | bytes 1572872 | tf_op jit(solution)/shard_map/ppermute | solution.py:262
  76.7 12.4 %collective-permute-done.15 = bf16[256,1024]{1,0:T(8,128)(2,1)S(1)} collective-permute-done((bf16[256,1024]{1,0:T(8,128)(2,1)S(1)}, bf16[256,1024]{1,0:T(8,128)(2,1)S(1)}, u32[]{:S(2)}, u32[]{:S(2)}) %collective-permute-start.15) | collective-permute-done | bytes 524320 | tf_op jit(solution)/shard_map/ppermute | solution.py:262
  89.1 0.8 copy.7
  (5 shorter events, 0.2 us)
Async XLA Ops:
  0.0 4.2 %copy-start.1 = (bf16[256,1024]{1,0:T(8,128)(2,1)S(1)}, bf16[256,1024]{1,0:T(8,128)(2,1)}, u32[]{:S(2)}) copy-start(bf16[256,1024]{1,0:T(8,128)(2,1)} %v_ref.1) | copy-start | bytes 1572868
  0.0 4.2 %copy-start = (bf16[256,1024]{1,0:T(8,128)(2,1)S(1)}, bf16[256,1024]{1,0:T(8,128)(2,1)}, u32[]{:S(2)}) copy-start(bf16[256,1024]{1,0:T(8,128)(2,1)} %k_ref.1) | copy-start | bytes 1572868
  0.0 4.2 %copy-start.2 = (bf16[256,1024]{1,0:T(8,128)(2,1)S(1)}, bf16[256,1024]{1,0:T(8,128)(2,1)}, u32[]{:S(2)}) copy-start(bf16[256,1024]{1,0:T(8,128)(2,1)} %q_ref.3) | copy-start | bytes 1572868
  1.7 5.4 %collective-permute-start.4 = (bf16[4,128,128]{2,1,0:T(8,128)(2,1)S(1)}, bf16[4,128,128]{2,1,0:T(8,128)(2,1)S(1)}, u32[]{:S(2)}, u32[]{:S(2)}) collective-permute-start(bf16[4,128,128]{2,1,0:T(8,128)(2,1)S(1)} %get-tuple-element.23), channel_id=1, source_target_pairs={{0,4},{4,0},{8,12},{12,8},{16,20},{20,16},{24,28},{28,24},{1,5},{5... | collective-permute-start | bytes 393224 | tf_op jit(solution)/shard_map/ppermute | solution.py:258
  4.1 6.1 %collective-permute-start = (bf16[4,128,128]{2,1,0:T(8,128)(2,1)S(1)}, bf16[4,128,128]{2,1,0:T(8,128)(2,1)S(1)}, u32[]{:S(2)}, u32[]{:S(2)}) collective-permute-start(bf16[4,128,128]{2,1,0:T(8,128)(2,1)S(1)} %get-tuple-element.19), channel_id=1, source_target_pairs={{0,4},{4,0},{8,12},{12,8},{16,20},{20,16},{24,28},{28,24},{1,5},{5... | collective-permute-start | bytes 393224 | tf_op jit(solution)/shard_map/ppermute | solution.py:258
  5.1 14.4 %copy-start.3 = (f32[1024]{0:T(1024)S(1)}, f32[1024]{0:T(1024)}, u32[]{:S(2)}) copy-start(f32[1024]{0:T(1024)} %param.8) | copy-start | bytes 12292
  7.1 5.9 %collective-permute-start.5 = (bf16[4,128,128]{2,1,0:T(8,128)(2,1)S(1)}, bf16[4,128,128]{2,1,0:T(8,128)(2,1)S(1)}, u32[]{:S(2)}, u32[]{:S(2)}) collective-permute-start(bf16[4,128,128]{2,1,0:T(8,128)(2,1)S(1)} %shard_map.61), channel_id=1, source_target_pairs={{0,8},{4,12},{1,9},{5,13},{2,10},{6,14},{3,11},{7,15}} | collective-permute-start | bytes 393224 | tf_op jit(solution)/shard_map/ppermute | solution.py:282
  10.2 5.7 %collective-permute-start.1 = (bf16[4,128,128]{2,1,0:T(8,128)(2,1)S(1)}, bf16[4,128,128]{2,1,0:T(8,128)(2,1)S(1)}, u32[]{:S(2)}, u32[]{:S(2)}) collective-permute-start(bf16[4,128,128]{2,1,0:T(8,128)(2,1)S(1)} %shard_map.57), channel_id=1, source_target_pairs={{0,8},{4,12},{1,9},{5,13},{2,10},{6,14},{3,11},{7,15}} | collective-permute-start | bytes 393224 | tf_op jit(solution)/shard_map/ppermute | solution.py:282
  13.1 4.9 %collective-permute-start.6 = (bf16[4,128,128]{2,1,0:T(8,128)(2,1)S(1)}, bf16[4,128,128]{2,1,0:T(8,128)(2,1)S(1)}, u32[]{:S(2)}, u32[]{:S(2)}) collective-permute-start(bf16[4,128,128]{2,1,0:T(8,128)(2,1)S(1)} %shard_map.62), channel_id=1, source_target_pairs={{8,16},{12,20},{9,17},{13,21},{10,18},{14,22},{11,19},{15,23}} | collective-permute-start | bytes 393224 | tf_op jit(solution)/shard_map/ppermute | solution.py:282
  16.0 2.7 %collective-permute-start.2 = (bf16[4,128,128]{2,1,0:T(8,128)(2,1)S(1)}, bf16[4,128,128]{2,1,0:T(8,128)(2,1)S(1)}, u32[]{:S(2)}, u32[]{:S(2)}) collective-permute-start(bf16[4,128,128]{2,1,0:T(8,128)(2,1)S(1)} %shard_map.58), channel_id=1, source_target_pairs={{8,16},{12,20},{9,17},{13,21},{10,18},{14,22},{11,19},{15,23}} | collective-permute-start | bytes 393224 | tf_op jit(solution)/shard_map/ppermute | solution.py:282
  16.7 25.3 %collective-permute-start.9 = (bf16[1024,512]{1,0:T(8,128)(2,1)}, bf16[1024,512]{1,0:T(8,128)(2,1)}, u32[]{:S(2)}, u32[]{:S(2)}) collective-permute-start(bf16[1024,512]{1,0:T(8,128)(2,1)} %own_ref.1), channel_id=1, source_target_pairs={{0,4},{4,0},{8,12},{12,8},{16,20},{20,16},{24,28},{28,24},{1,5},{5... | collective-permute-start | bytes 3145736 | tf_op jit(solution)/shard_map/ppermute | solution.py:258
  18.0 1.4 %collective-permute-start.7 = (bf16[4,128,128]{2,1,0:T(8,128)(2,1)S(1)}, bf16[4,128,128]{2,1,0:T(8,128)(2,1)S(1)}, u32[]{:S(2)}, u32[]{:S(2)}) collective-permute-start(bf16[4,128,128]{2,1,0:T(8,128)(2,1)S(1)} %shard_map.63), channel_id=1, source_target_pairs={{16,24},{20,28},{17,25},{21,29},{18,26},{22,30},{19,27},{23,31}} | collective-permute-start | bytes 393224 | tf_op jit(solution)/shard_map/ppermute | solution.py:282
  18.8 0.7 collective-permute-start.3
  20.1 21.8 %collective-permute-start.8 = (bf16[256,1024]{1,0:T(8,128)(2,1)S(1)}, bf16[256,1024]{1,0:T(8,128)(2,1)S(1)}, u32[]{:S(2)}, u32[]{:S(2)}) collective-permute-start(bf16[256,1024]{1,0:T(8,128)(2,1)S(1)} %shard_map.64), channel_id=1, source_target_pairs={{0,8},{4,12},{8,0},{12,4},{16,24},{20,28},{24,16},{28,20},{1,9},{5... | collective-permute-start | bytes 1572872 | tf_op jit(solution)/shard_map/ppermute | solution.py:258
  23.3 21.1 %collective-permute-start.10 = (bf16[256,1024]{1,0:T(8,128)(2,1)S(1)}, bf16[256,1024]{1,0:T(8,128)(2,1)S(1)}, u32[]{:S(2)}, u32[]{:S(2)}) collective-permute-start(bf16[256,1024]{1,0:T(8,128)(2,1)S(1)} %shard_map.64), channel_id=1, source_target_pairs={{0,16},{1,17},{2,26},{3,27},{4,20},{5,21},{6,30},{7,31},{8,24},{9,... | collective-permute-start | bytes 1572872 | tf_op jit(solution)/shard_map/ppermute | solution.py:262
  45.2 11.4 %collective-permute-start.13 = (bf16[2,256,512]{2,1,0:T(8,128)(2,1)S(1)}, bf16[2,256,512]{2,1,0:T(8,128)(2,1)S(1)}, u32[]{:S(2)}, u32[]{:S(2)}) collective-permute-start(bf16[2,256,512]{2,1,0:T(8,128)(2,1)S(1)} %get-tuple-element.32), channel_id=1, source_target_pairs={{0,1},{1,0},{2,3},{3,2},{4,5},{5,4},{6,7},{7,6},{8,9},{9,8},{10,11... | collective-permute-start | bytes 1572872 | tf_op jit(solution)/shard_map/ppermute | solution.py:262
  55.0 13.5 %collective-permute-start.11 = (bf16[256,1024]{1,0:T(8,128)(2,1)S(1)}, bf16[256,1024]{1,0:T(8,128)(2,1)S(1)}, u32[]{:S(2)}, u32[]{:S(2)}) collective-permute-start(bf16[256,1024]{1,0:T(8,128)(2,1)S(1)} %collective-permute-done.10.heavy_ref), channel_id=1, source_target_pairs={{0,8},{4,12},{8,0},{12,4},{16,24},{20,28},{24,16},{28,20},{1,9},{5... | collective-permute-start | bytes 1572872 | tf_op jit(solution)/shard_map/ppermute | solution.py:258
  56.7 13.5 %collective-permute-start.14 = (bf16[2,256,512]{2,1,0:T(8,128)(2,1)S(1)}, bf16[2,256,512]{2,1,0:T(8,128)(2,1)S(1)}, u32[]{:S(2)}, u32[]{:S(2)}) collective-permute-start(bf16[2,256,512]{2,1,0:T(8,128)(2,1)S(1)} %add_convert_fusion.1), channel_id=1, source_target_pairs={{0,2},{1,3},{2,0},{3,1},{4,6},{5,7},{6,4},{7,5},{8,10},{9,11},{10,... | collective-permute-start | bytes 1572872 | tf_op jit(solution)/shard_map/ppermute | solution.py:262
  69.3 2.5 %collective-permute-start.12 = (bf16[2,256,512]{2,1,0:T(8,128)(2,1)S(1)}, bf16[2,256,512]{2,1,0:T(8,128)(2,1)S(1)}, u32[]{:S(2)}, u32[]{:S(2)}) collective-permute-start(bf16[2,256,512]{2,1,0:T(8,128)(2,1)S(1)} %get-tuple-element.29), channel_id=1, source_target_pairs={{0,1},{1,0},{2,3},{3,2},{4,5},{5,4},{6,7},{7,6},{8,9},{9,8},{10,11... | collective-permute-start | bytes 1572872 | tf_op jit(solution)/shard_map/ppermute | solution.py:262
  72.0 17.0 %collective-permute-start.15 = (bf16[256,1024]{1,0:T(8,128)(2,1)S(1)}, bf16[256,1024]{1,0:T(8,128)(2,1)S(1)}, u32[]{:S(2)}, u32[]{:S(2)}) collective-permute-start(bf16[256,1024]{1,0:T(8,128)(2,1)S(1)} %pad_maximum_fusion), channel_id=1, source_target_pairs={{0,0},{1,24},{2,8},{3,16},{4,4},{5,28},{6,12},{7,20},{8,9},{9,17},... | collective-permute-start | bytes 1572872 | tf_op jit(solution)/shard_map/ppermute | solution.py:262

commit v32 on v31

--- a/solution.py
+++ b/solution.py
@@ -93,8 +93,7 @@
         part, index = divmod(head, heads // parts)
         mate_ref, *earlier_refs = state_refs[part * each : (part + 1) * each]
         state = jnp.where(second, mate_ref[index].astype(F32), 0.0)
-        for earlier_ref in earlier_refs:
-            state += earlier_ref[index].astype(F32)
+        state += sum(earlier_ref[index] for earlier_ref in earlier_refs).astype(F32)
         carried = jnp.dot(q_ref[:, cols], state.astype(BF16), preferred_element_type=F32)
         combined = within_ref[:, cols] + carried
         mean_square = jnp.mean(combined * combined, axis=-1, keepdims=True)

time: 90.1 us -> 90.1 us (level)
  no operation moved by 1% of the time
where the time goes in v32:
time: 90.1 us; the launch traced here: 89.9 us
  waiting for transfers between devices  41.4 us (46%)
  starting transfers between devices  38.6 us (43%)
  Pallas kernels  6.83 us (8%)
  local copies, waits for them, and re-layouts  2.2 us (2%)
    ppermute x5, waiting for transfers between devices, swap(): return lax.ppermute(value, 'seq', [(s, s ^ mask) for s in range(8)])  24.5 us
    ppermute x5, starting transfers between devices, move(): return lax.ppermute(value, both, pairs)  23.2 us
    ppermute x5, waiting for transfers between devices, move(): return lax.ppermute(value, both, pairs)  14.7 us
    ppermute x6, starting transfers between devices, pairs_body(): states[part].append(lax.ppermute(onward[part], 'seq', pairs))  8.54 us
    ppermute x5, starting transfers between devices, swap(): return lax.ppermute(value, 'seq', [(s, s ^ mask) for s in range(8)])  6.79 us
    ppermute x6, waiting for transfers between devices, pairs_body(): states[part].append(lax.ppermute(onward[part], 'seq', pairs))  2.22 us
  transfers between devices with their start and end apart: 16, of which 7 were waited for; matrix products, arithmetic and copies ran while one was open for 0% of the time, Pallas kernels for 6%

profile of v32, /device:TPU:1, one launch (start us, length us, event | category | flops | bytes accessed | tf_op | source)
XLA Modules:
  0.0 89.9 jit_solution(7649450532640356674)
XLA Ops:
  0.0 0.0 copy-start.1
  0.0 0.0 copy-start
  0.0 0.0 copy-start.2
  0.0 1.4 %fusion = (bf16[256,512]{1,0:T(8,128)(2,1)S(1)}, bf16[256,512]{1,0:T(8,128)(2,1)S(1)}, bf16[256,512]{1,0:T(8,128)(2,1)S(1)}, bf16[256,512]{1,0:T(8,128)(2,1)S(1)}) fusion(bf16[256,1024]{1,0:T(8,128)(2,1)} %v_ref.1, bf16[256,1024]{1,0:T(8,128)(2,1)} %k_ref.1), kind=kLoop, calls=%fused_computation.7 | loop fusion | bytes 2097152 | tf_op jit(solution)/shard_map/slice | solution.py:119
  1.4 0.3 shard_map.60
  1.7 2.1 %collective-permute-start.4 = (bf16[4,128,128]{2,1,0:T(8,128)(2,1)S(1)}, bf16[4,128,128]{2,1,0:T(8,128)(2,1)S(1)}, u32[]{:S(2)}, u32[]{:S(2)}) collective-permute-start(bf16[4,128,128]{2,1,0:T(8,128)(2,1)S(1)} %get-tuple-element.23), channel_id=1, source_target_pairs={{0,4},{4,0},{8,12},{12,8},{16,20},{20,16},{24,28},{28,24},{1,5},{5... | collective-permute-start | bytes 393224 | tf_op jit(solution)/shard_map/ppermute | solution.py:257
  3.8 0.3 shard_map.55
  4.1 0.1 collective-permute-start
  4.2 0.0 copy-done.1
  4.2 0.0 copy-done
  4.2 0.0 copy-done.2
  4.2 0.9 %shard_map.56.within_ref = f32[256,1024]{1,0:T(8,128)S(1)} custom-call(bf16[256,1024]{1,0:T(8,128)(2,1)S(1)} %copy-done.2, bf16[256,1024]{1,0:T(8,128)(2,1)S(1)} %copy-done, bf16[256,1024]{1,0:T(8,128)(2,1)S(1)} %copy-done.1), custom_call_target="tpu_custom_call" | custom-call | flops 268435456 | bytes 2621440 | tf_op jit(solution)/shard_map/pallas_call | solution.py:265
  5.1 0.0 copy-start.3
  5.1 1.9 %collective-permute-done.4.refs_1_.refs_4_ = bf16[4,128,128]{2,1,0:T(8,128)(2,1)S(1)} collective-permute-done((bf16[4,128,128]{2,1,0:T(8,128)(2,1)S(1)}, bf16[4,128,128]{2,1,0:T(8,128)(2,1)S(1)}, u32[]{:S(2)}, u32[]{:S(2)}) %collective-permute-start.4) | collective-permute-done | bytes 131104 | tf_op jit(solution)/shard_map/ppermute | solution.py:257
  7.1 3.1 %collective-permute-start.5 = (bf16[4,128,128]{2,1,0:T(8,128)(2,1)S(1)}, bf16[4,128,128]{2,1,0:T(8,128)(2,1)S(1)}, u32[]{:S(2)}, u32[]{:S(2)}) collective-permute-start(bf16[4,128,128]{2,1,0:T(8,128)(2,1)S(1)} %shard_map.61), channel_id=1, source_target_pairs={{0,8},{4,12},{1,9},{5,13},{2,10},{6,14},{3,11},{7,15}} | collective-permute-start | bytes 393224 | tf_op jit(solution)/shard_map/ppermute | solution.py:281
  10.2 0.0 collective-permute-done.refs_1_.refs_0_
  10.2 2.8 %collective-permute-start.1 = (bf16[4,128,128]{2,1,0:T(8,128)(2,1)S(1)}, bf16[4,128,128]{2,1,0:T(8,128)(2,1)S(1)}, u32[]{:S(2)}, u32[]{:S(2)}) collective-permute-start(bf16[4,128,128]{2,1,0:T(8,128)(2,1)S(1)} %shard_map.57), channel_id=1, source_target_pairs={{0,8},{4,12},{1,9},{5,13},{2,10},{6,14},{3,11},{7,15}} | collective-permute-start | bytes 393224 | tf_op jit(solution)/shard_map/ppermute | solution.py:281
  13.0 0.0 collective-permute-done.5.refs_2_.refs_5_
  13.1 0.7 collective-permute-start.6
  13.7 2.2 %collective-permute-done.1.refs_2_.refs_1_ = bf16[4,128,128]{2,1,0:T(8,128)(2,1)S(1)} collective-permute-done((bf16[4,128,128]{2,1,0:T(8,128)(2,1)S(1)}, bf16[4,128,128]{2,1,0:T(8,128)(2,1)S(1)}, u32[]{:S(2)}, u32[]{:S(2)}) %collective-permute-start.1) | collective-permute-done | bytes 131104 | tf_op jit(solution)/shard_map/ppermute | solution.py:281
  16.0 0.7 collective-permute-start.2
  16.7 1.3 %collective-permute-start.9 = (bf16[1024,512]{1,0:T(8,128)(2,1)}, bf16[1024,512]{1,0:T(8,128)(2,1)}, u32[]{:S(2)}, u32[]{:S(2)}) collective-permute-start(bf16[1024,512]{1,0:T(8,128)(2,1)} %own_ref.1), channel_id=1, source_target_pairs={{0,4},{4,0},{8,12},{12,8},{16,20},{20,16},{24,28},{28,24},{1,5},{5... | collective-permute-start | bytes 3145736 | tf_op jit(solution)/shard_map/ppermute | solution.py:257
  18.0 0.0 collective-permute-done.6.refs_3_.refs_6_
  18.0 0.1 shard_map.63
  18.0 0.7 collective-permute-start.7
  18.7 0.0 collective-permute-done.2.refs_3_.refs_2_
  18.7 0.1 shard_map.59
  18.8 0.7 collective-permute-start.3
  19.5 0.0 collective-permute-done.7.refs_7_
  19.5 0.0 collective-permute-done.3.refs_3_
  19.5 0.0 copy-done.3
  19.5 0.6 shard_map.64
  20.1 3.2 %collective-permute-start.8 = (bf16[256,1024]{1,0:T(8,128)(2,1)S(1)}, bf16[256,1024]{1,0:T(8,128)(2,1)S(1)}, u32[]{:S(2)}, u32[]{:S(2)}) collective-permute-start(bf16[256,1024]{1,0:T(8,128)(2,1)S(1)} %shard_map.64), channel_id=1, source_target_pairs={{0,8},{4,12},{8,0},{12,4},{16,24},{20,28},{24,16},{28,20},{1,9},{5... | collective-permute-start | bytes 1572872 | tf_op jit(solution)/shard_map/ppermute | solution.py:257
  23.3 6.8 %collective-permute-start.10 = (bf16[256,1024]{1,0:T(8,128)(2,1)S(1)}, bf16[256,1024]{1,0:T(8,128)(2,1)S(1)}, u32[]{:S(2)}, u32[]{:S(2)}) collective-permute-start(bf16[256,1024]{1,0:T(8,128)(2,1)S(1)} %shard_map.64), channel_id=1, source_target_pairs={{0,16},{1,17},{2,26},{3,27},{4,20},{5,21},{6,30},{7,31},{8,24},{9,... | collective-permute-start | bytes 1572872 | tf_op jit(solution)/shard_map/ppermute | solution.py:261
  30.1 11.8 %collective-permute-done.8 = bf16[256,1024]{1,0:T(8,128)(2,1)S(1)} collective-permute-done((bf16[256,1024]{1,0:T(8,128)(2,1)S(1)}, bf16[256,1024]{1,0:T(8,128)(2,1)S(1)}, u32[]{:S(2)}, u32[]{:S(2)}) %collective-permute-start.8) | collective-permute-done | bytes 524320 | tf_op jit(solution)/shard_map/ppermute | solution.py:257
  41.9 0.1 broadcast_select_fusion.1
  42.0 0.0 collective-permute-done.9.mate_ref
  42.0 1.7 %shard_map.65.weight_ref = bf16[2,1024,512]{2,1,0:T(8,128)(2,1)S(1)} custom-call(bf16[1024,512]{1,0:T(8,128)(2,1)} %own_ref.1, bf16[1024,512]{1,0:T(8,128)(2,1)} %collective-permute-done.9.mate_ref), custom_call_target="tpu_custom_call" | custom-call | bytes 4194304 | tf_op jit(solution)/shard_map/pallas_call | solution.py:285
  43.7 0.7 shard_map.67.light_ref
  44.4 0.0 collective-permute-done.10.heavy_ref
  44.4 0.7 shard_map.69
  45.2 9.9 %collective-permute-start.13 = (bf16[2,256,512]{2,1,0:T(8,128)(2,1)S(1)}, bf16[2,256,512]{2,1,0:T(8,128)(2,1)S(1)}, u32[]{:S(2)}, u32[]{:S(2)}) collective-permute-start(bf16[2,256,512]{2,1,0:T(8,128)(2,1)S(1)} %get-tuple-element.32), channel_id=1, source_target_pairs={{0,1},{1,0},{2,3},{3,2},{4,5},{5,4},{6,7},{7,6},{8,9},{9,8},{10,11... | collective-permute-start | bytes 1572872 | tf_op jit(solution)/shard_map/ppermute | solution.py:261
  55.0 0.1 collective-permute-start.11
  55.1 0.7 shard_map.66.light_ref
  55.8 0.8 collective-permute-done.13
  56.6 0.1 add_convert_fusion.1
  56.7 1.1 %collective-permute-start.14 = (bf16[2,256,512]{2,1,0:T(8,128)(2,1)S(1)}, bf16[2,256,512]{2,1,0:T(8,128)(2,1)S(1)}, u32[]{:S(2)}, u32[]{:S(2)}) collective-permute-start(bf16[2,256,512]{2,1,0:T(8,128)(2,1)S(1)} %add_convert_fusion.1), channel_id=1, source_target_pairs={{0,2},{1,3},{2,0},{3,1},{4,6},{5,7},{6,4},{7,5},{8,10},{9,11},{10,... | collective-permute-start | bytes 1572872 | tf_op jit(solution)/shard_map/ppermute | solution.py:261
  57.8 10.8 %collective-permute-done.11.heavy_ref = bf16[256,1024]{1,0:T(8,128)(2,1)S(1)} collective-permute-done((bf16[256,1024]{1,0:T(8,128)(2,1)S(1)}, bf16[256,1024]{1,0:T(8,128)(2,1)S(1)}, u32[]{:S(2)}, u32[]{:S(2)}) %collective-permute-start.11) | collective-permute-done | bytes 524320 | tf_op jit(solution)/shard_map/ppermute | solution.py:257
  68.5 0.7 shard_map.68
  69.3 0.9 %collective-permute-start.12 = (bf16[2,256,512]{2,1,0:T(8,128)(2,1)S(1)}, bf16[2,256,512]{2,1,0:T(8,128)(2,1)S(1)}, u32[]{:S(2)}, u32[]{:S(2)}) collective-permute-start(bf16[2,256,512]{2,1,0:T(8,128)(2,1)S(1)} %get-tuple-element.29), channel_id=1, source_target_pairs={{0,1},{1,0},{2,3},{3,2},{4,5},{5,4},{6,7},{7,6},{8,9},{9,8},{10,11... | collective-permute-start | bytes 1572872 | tf_op jit(solution)/shard_map/ppermute | solution.py:261
  70.2 0.0 collective-permute-done.14
  70.2 1.5 %collective-permute-done.12 = bf16[2,256,512]{2,1,0:T(8,128)(2,1)S(1)} collective-permute-done((bf16[2,256,512]{2,1,0:T(8,128)(2,1)S(1)}, bf16[2,256,512]{2,1,0:T(8,128)(2,1)S(1)}, u32[]{:S(2)}, u32[]{:S(2)}) %collective-permute-start.12) | collective-permute-done | bytes 524320 | tf_op jit(solution)/shard_map/ppermute | solution.py:261
  71.7 0.2 add_convert_fusion
  72.0 0.1 pad_maximum_fusion
  72.1 4.6 %collective-permute-start.15 = (bf16[256,1024]{1,0:T(8,128)(2,1)S(1)}, bf16[256,1024]{1,0:T(8,128)(2,1)S(1)}, u32[]{:S(2)}, u32[]{:S(2)}) collective-permute-start(bf16[256,1024]{1,0:T(8,128)(2,1)S(1)} %pad_maximum_fusion), channel_id=1, source_target_pairs={{0,0},{1,24},{2,8},{3,16},{4,4},{5,28},{6,12},{7,20},{8,9},{9,17},... | collective-permute-start | bytes 1572872 | tf_op jit(solution)/shard_map/ppermute | solution.py:261
  76.6 12.4 %collective-permute-done.15 = bf16[256,1024]{1,0:T(8,128)(2,1)S(1)} collective-permute-done((bf16[256,1024]{1,0:T(8,128)(2,1)S(1)}, bf16[256,1024]{1,0:T(8,128)(2,1)S(1)}, u32[]{:S(2)}, u32[]{:S(2)}) %collective-permute-start.15) | collective-permute-done | bytes 524320 | tf_op jit(solution)/shard_map/ppermute | solution.py:261
  89.1 0.8 copy.7
  (5 shorter events, 0.2 us)
Async XLA Ops:
  0.0 4.2 %copy-start.1 = (bf16[256,1024]{1,0:T(8,128)(2,1)S(1)}, bf16[256,1024]{1,0:T(8,128)(2,1)}, u32[]{:S(2)}) copy-start(bf16[256,1024]{1,0:T(8,128)(2,1)} %v_ref.1) | copy-start | bytes 1572868
  0.0 4.2 %copy-start = (bf16[256,1024]{1,0:T(8,128)(2,1)S(1)}, bf16[256,1024]{1,0:T(8,128)(2,1)}, u32[]{:S(2)}) copy-start(bf16[256,1024]{1,0:T(8,128)(2,1)} %k_ref.1) | copy-start | bytes 1572868
  0.0 4.2 %copy-start.2 = (bf16[256,1024]{1,0:T(8,128)(2,1)S(1)}, bf16[256,1024]{1,0:T(8,128)(2,1)}, u32[]{:S(2)}) copy-start(bf16[256,1024]{1,0:T(8,128)(2,1)} %q_ref.3) | copy-start | bytes 1572868
  1.7 5.4 %collective-permute-start.4 = (bf16[4,128,128]{2,1,0:T(8,128)(2,1)S(1)}, bf16[4,128,128]{2,1,0:T(8,128)(2,1)S(1)}, u32[]{:S(2)}, u32[]{:S(2)}) collective-permute-start(bf16[4,128,128]{2,1,0:T(8,128)(2,1)S(1)} %get-tuple-element.23), channel_id=1, source_target_pairs={{0,4},{4,0},{8,12},{12,8},{16,20},{20,16},{24,28},{28,24},{1,5},{5... | collective-permute-start | bytes 393224 | tf_op jit(solution)/shard_map/ppermute | solution.py:257
  4.1 6.1 %collective-permute-start = (bf16[4,128,128]{2,1,0:T(8,128)(2,1)S(1)}, bf16[4,128,128]{2,1,0:T(8,128)(2,1)S(1)}, u32[]{:S(2)}, u32[]{:S(2)}) collective-permute-start(bf16[4,128,128]{2,1,0:T(8,128)(2,1)S(1)} %get-tuple-element.19), channel_id=1, source_target_pairs={{0,4},{4,0},{8,12},{12,8},{16,20},{20,16},{24,28},{28,24},{1,5},{5... | collective-permute-start | bytes 393224 | tf_op jit(solution)/shard_map/ppermute | solution.py:257
  5.1 14.4 %copy-start.3 = (f32[1024]{0:T(1024)S(1)}, f32[1024]{0:T(1024)}, u32[]{:S(2)}) copy-start(f32[1024]{0:T(1024)} %param.8) | copy-start | bytes 12292
  7.1 5.9 %collective-permute-start.5 = (bf16[4,128,128]{2,1,0:T(8,128)(2,1)S(1)}, bf16[4,128,128]{2,1,0:T(8,128)(2,1)S(1)}, u32[]{:S(2)}, u32[]{:S(2)}) collective-permute-start(bf16[4,128,128]{2,1,0:T(8,128)(2,1)S(1)} %shard_map.61), channel_id=1, source_target_pairs={{0,8},{4,12},{1,9},{5,13},{2,10},{6,14},{3,11},{7,15}} | collective-permute-start | bytes 393224 | tf_op jit(solution)/shard_map/ppermute | solution.py:281
  10.2 5.7 %collective-permute-start.1 = (bf16[4,128,128]{2,1,0:T(8,128)(2,1)S(1)}, bf16[4,128,128]{2,1,0:T(8,128)(2,1)S(1)}, u32[]{:S(2)}, u32[]{:S(2)}) collective-permute-start(bf16[4,128,128]{2,1,0:T(8,128)(2,1)S(1)} %shard_map.57), channel_id=1, source_target_pairs={{0,8},{4,12},{1,9},{5,13},{2,10},{6,14},{3,11},{7,15}} | collective-permute-start | bytes 393224 | tf_op jit(solution)/shard_map/ppermute | solution.py:281
  13.1 4.9 %collective-permute-start.6 = (bf16[4,128,128]{2,1,0:T(8,128)(2,1)S(1)}, bf16[4,128,128]{2,1,0:T(8,128)(2,1)S(1)}, u32[]{:S(2)}, u32[]{:S(2)}) collective-permute-start(bf16[4,128,128]{2,1,0:T(8,128)(2,1)S(1)} %shard_map.62), channel_id=1, source_target_pairs={{8,16},{12,20},{9,17},{13,21},{10,18},{14,22},{11,19},{15,23}} | collective-permute-start | bytes 393224 | tf_op jit(solution)/shard_map/ppermute | solution.py:281
  16.0 2.7 %collective-permute-start.2 = (bf16[4,128,128]{2,1,0:T(8,128)(2,1)S(1)}, bf16[4,128,128]{2,1,0:T(8,128)(2,1)S(1)}, u32[]{:S(2)}, u32[]{:S(2)}) collective-permute-start(bf16[4,128,128]{2,1,0:T(8,128)(2,1)S(1)} %shard_map.58), channel_id=1, source_target_pairs={{8,16},{12,20},{9,17},{13,21},{10,18},{14,22},{11,19},{15,23}} | collective-permute-start | bytes 393224 | tf_op jit(solution)/shard_map/ppermute | solution.py:281
  16.7 25.3 %collective-permute-start.9 = (bf16[1024,512]{1,0:T(8,128)(2,1)}, bf16[1024,512]{1,0:T(8,128)(2,1)}, u32[]{:S(2)}, u32[]{:S(2)}) collective-permute-start(bf16[1024,512]{1,0:T(8,128)(2,1)} %own_ref.1), channel_id=1, source_target_pairs={{0,4},{4,0},{8,12},{12,8},{16,20},{20,16},{24,28},{28,24},{1,5},{5... | collective-permute-start | bytes 3145736 | tf_op jit(solution)/shard_map/ppermute | solution.py:257
  18.0 1.4 %collective-permute-start.7 = (bf16[4,128,128]{2,1,0:T(8,128)(2,1)S(1)}, bf16[4,128,128]{2,1,0:T(8,128)(2,1)S(1)}, u32[]{:S(2)}, u32[]{:S(2)}) collective-permute-start(bf16[4,128,128]{2,1,0:T(8,128)(2,1)S(1)} %shard_map.63), channel_id=1, source_target_pairs={{16,24},{20,28},{17,25},{21,29},{18,26},{22,30},{19,27},{23,31}} | collective-permute-start | bytes 393224 | tf_op jit(solution)/shard_map/ppermute | solution.py:281
  18.8 0.7 collective-permute-start.3
  20.1 21.8 %collective-permute-start.8 = (bf16[256,1024]{1,0:T(8,128)(2,1)S(1)}, bf16[256,1024]{1,0:T(8,128)(2,1)S(1)}, u32[]{:S(2)}, u32[]{:S(2)}) collective-permute-start(bf16[256,1024]{1,0:T(8,128)(2,1)S(1)} %shard_map.64), channel_id=1, source_target_pairs={{0,8},{4,12},{8,0},{12,4},{16,24},{20,28},{24,16},{28,20},{1,9},{5... | collective-permute-start | bytes 1572872 | tf_op jit(solution)/shard_map/ppermute | solution.py:257
  23.3 21.1 %collective-permute-start.10 = (bf16[256,1024]{1,0:T(8,128)(2,1)S(1)}, bf16[256,1024]{1,0:T(8,128)(2,1)S(1)}, u32[]{:S(2)}, u32[]{:S(2)}) collective-permute-start(bf16[256,1024]{1,0:T(8,128)(2,1)S(1)} %shard_map.64), channel_id=1, source_target_pairs={{0,16},{1,17},{2,26},{3,27},{4,20},{5,21},{6,30},{7,31},{8,24},{9,... | collective-permute-start | bytes 1572872 | tf_op jit(solution)/shard_map/ppermute | solution.py:261
  45.2 11.4 %collective-permute-start.13 = (bf16[2,256,512]{2,1,0:T(8,128)(2,1)S(1)}, bf16[2,256,512]{2,1,0:T(8,128)(2,1)S(1)}, u32[]{:S(2)}, u32[]{:S(2)}) collective-permute-start(bf16[2,256,512]{2,1,0:T(8,128)(2,1)S(1)} %get-tuple-element.32), channel_id=1, source_target_pairs={{0,1},{1,0},{2,3},{3,2},{4,5},{5,4},{6,7},{7,6},{8,9},{9,8},{10,11... | collective-permute-start | bytes 1572872 | tf_op jit(solution)/shard_map/ppermute | solution.py:261
  55.0 13.5 %collective-permute-start.11 = (bf16[256,1024]{1,0:T(8,128)(2,1)S(1)}, bf16[256,1024]{1,0:T(8,128)(2,1)S(1)}, u32[]{:S(2)}, u32[]{:S(2)}) collective-permute-start(bf16[256,1024]{1,0:T(8,128)(2,1)S(1)} %collective-permute-done.10.heavy_ref), channel_id=1, source_target_pairs={{0,8},{4,12},{8,0},{12,4},{16,24},{20,28},{24,16},{28,20},{1,9},{5... | collective-permute-start | bytes 1572872 | tf_op jit(solution)/shard_map/ppermute | solution.py:257
  56.7 13.5 %collective-permute-start.14 = (bf16[2,256,512]{2,1,0:T(8,128)(2,1)S(1)}, bf16[2,256,512]{2,1,0:T(8,128)(2,1)S(1)}, u32[]{:S(2)}, u32[]{:S(2)}) collective-permute-start(bf16[2,256,512]{2,1,0:T(8,128)(2,1)S(1)} %add_convert_fusion.1), channel_id=1, source_target_pairs={{0,2},{1,3},{2,0},{3,1},{4,6},{5,7},{6,4},{7,5},{8,10},{9,11},{10,... | collective-permute-start | bytes 1572872 | tf_op jit(solution)/shard_map/ppermute | solution.py:261
  69.3 2.5 %collective-permute-start.12 = (bf16[2,256,512]{2,1,0:T(8,128)(2,1)S(1)}, bf16[2,256,512]{2,1,0:T(8,128)(2,1)S(1)}, u32[]{:S(2)}, u32[]{:S(2)}) collective-permute-start(bf16[2,256,512]{2,1,0:T(8,128)(2,1)S(1)} %get-tuple-element.29), channel_id=1, source_target_pairs={{0,1},{1,0},{2,3},{3,2},{4,5},{5,4},{6,7},{7,6},{8,9},{9,8},{10,11... | collective-permute-start | bytes 1572872 | tf_op jit(solution)/shard_map/ppermute | solution.py:261
  72.1 17.0 %collective-permute-start.15 = (bf16[256,1024]{1,0:T(8,128)(2,1)S(1)}, bf16[256,1024]{1,0:T(8,128)(2,1)S(1)}, u32[]{:S(2)}, u32[]{:S(2)}) collective-permute-start(bf16[256,1024]{1,0:T(8,128)(2,1)S(1)} %pad_maximum_fusion), channel_id=1, source_target_pairs={{0,0},{1,24},{2,8},{3,16},{4,4},{5,28},{6,12},{7,20},{8,9},{9,17},... | collective-permute-start | bytes 1572872 | tf_op jit(solution)/shard_map/ppermute | solution.py:261
